TPU v7x, 32 devices: a whole 2x2x4 slice. The times are simulated.
32 devices in a mesh: parts: 2 (over y), snp: 4 (over x, core), hap: 4 (over z).
Axes of the slice: x: 2, y: 2, z: 4, core: 2. Of those that a mesh axis runs over, the one named last changes fastest.
Arguments:
- haplotypes: int32 [8192, 3072], P('hap', ('parts', 'snp')), parts along dimension 1, may hold values from 0 to 1
- labels: int32 [16384], P(('parts', 'hap')), parts along dimension 0, may hold values from 0 to 1
- annotations: int32 [50, 3072], P(None, ('parts', 'snp')), parts along dimension 1, may hold values 0 or 1
- reach: int32 [8], P('parts'), parts along dimension 0, may hold values from 96 to 384, as said below
Outputs:
- ld_scores: float32 [50, 3072], P(None, ('parts', 'snp', 'hap')), parts along dimension 1
There are 2 independent parts, one for each index of `parts`. A program takes and returns all parts, laid end to end along the dimension named above; each array names one. Nothing has to cross between parts.
Inputs may be any that keep to these rules, and one draw needn't show every extreme that they name: `reach`: the largest value is 384 in every window.
All inputs are finite; a program needn't handle non-finite values. No bound on the sum of `annotations` on one device may be relied on, other than what follows from the above.
Results may differ from a plain program's by a relative error of at most 0.0041.
Values may be sent and summed in bfloat16 or wider, within the bound.
No kernel may reach another device: no remote copies, remote signals or barrier semaphores. Data moves between devices by JAX's collectives and lax.ppermute only.
A program may use at most 64 MiB of HBM per device.

v0:
```python
import jax
import jax.numpy as jnp
from jax import lax
from jax.sharding import PartitionSpec as P

PRECISE = lax.Precision.HIGHEST
VARIANCE_FLOOR = 0.01


def shifted(value, axis, steps):
    count = lax.axis_size(axis)
    leading, last = (max(0, -steps), min(count, count - steps))
    return lax.ppermute(value, axis, [(source, source + steps) for source in range(leading, last)])


def standardize(alleles, second, totals, counts):
    pop_sizes = jnp.maximum(counts, 1.0)
    frequency = totals / pop_sizes[:, None]
    variance = jnp.maximum(frequency * (1.0 - frequency), VARIANCE_FLOOR)
    inverse = 1.0 / jnp.sqrt(pop_sizes[:, None] * variance)
    centred_first = (alleles - frequency[0]) * inverse[0]
    centred_second = (alleles - frequency[1]) * inverse[1]
    return jnp.where(second[:, None] > 0.5, centred_second, centred_first).astype(jnp.bfloat16)


def lookup(table, position):
    places = jnp.arange(table.shape[0], dtype=jnp.int32)
    return jnp.sum(jnp.where(places == position, table, 0))


def distances(row_index, offset, snp_block):
    col_index = offset * snp_block + jnp.arange(snp_block, dtype=jnp.int32)
    return jnp.abs(row_index[:, None] - col_index[None, :])


def per_device(haplotypes, labels, annotations, reach):
    hap_rows, snp_block = haplotypes.shape
    share_rows = snp_block // lax.axis_size("hap")
    hap_index = lax.axis_index("hap")
    snp_index = lax.axis_index("snp")
    alleles = haplotypes.astype(jnp.float32)
    second = labels.astype(jnp.float32)
    weights = jnp.stack([1.0 - second, second])
    totals, counts = lax.psum(
        (jnp.dot(weights, alleles, precision=PRECISE), jnp.sum(weights, axis=1)), "hap"
    )
    scaled = standardize(alleles, second, totals, counts)
    zero_block = jnp.zeros_like(scaled)
    masked = jnp.stack(
        [
            jnp.where(second[:, None] > 0.5, zero_block, scaled),
            jnp.where(second[:, None] > 0.5, scaled, zero_block),
        ],
        axis=1,
    )
    payload = jnp.concatenate([scaled, annotations.astype(jnp.bfloat16)], axis=0)
    upper_piece = shifted(payload, "snp", -1)
    pieces = [payload, upper_piece]
    offsets = [0, 1]
    lower_piece = shifted(payload, "snp", 1)
    pieces.append(lower_piece)
    offsets.append(-1)
    annots = jnp.stack([piece[hap_rows:] for piece in pieces]).astype(jnp.float32)
    summed = lax.psum(
        jnp.stack(
            [
                jnp.einsum(
                    "hpj,hk->jpk", masked, piece[:hap_rows], preferred_element_type=jnp.float32
                )
                for piece in pieces
            ],
            axis=1,
        ),
        "hap",
    )
    my_tiles = lax.dynamic_slice_in_dim(summed, hap_index * share_rows, share_rows, 0)
    product = my_tiles[:, :, 0, :] * my_tiles[:, :, 1, :]
    row_index = hap_index * share_rows + jnp.arange(share_rows, dtype=jnp.int32)
    reach_here = lookup(reach, snp_index)
    inside = jnp.stack(
        [distances(row_index, offset, snp_block) <= reach_here for offset in offsets], axis=1
    )
    kept_terms = jnp.where(inside, product, jnp.float32(0.0))
    scores = jnp.einsum("tak,rtk->ar", annots, kept_terms, precision=PRECISE)
    return scores


def solution(mesh):
    in_specs = (
        P("hap", ("parts", "snp")),
        P(("parts", "hap")),
        P(None, ("parts", "snp")),
        P("parts"),
    )
    out_specs = P(None, ("parts", "snp", "hap"))
    return jax.shard_map(
        per_device, mesh=mesh, in_specs=in_specs, out_specs=out_specs, check_vma=False
    )
```

profile of v0, /device:TPU:1, one launch (start us, length us, event | category | flops | bytes accessed | tf_op | source)
XLA Modules:
  0.0 196.5 jit_solution(4292573415792938210)
XLA Ops:
  6.5 0.0 copy-start.1
  6.5 0.0 all-reduce.3.cloned.1.call-start
  6.5 0.7 broadcast_compare_fusion
  7.3 0.7 broadcast_subtract_fusion
  8.0 0.7 convert_element_type.14
  8.7 0.1 fusion.26
  8.8 0.0 copy-start
  8.8 3.7 %fusion = f32[2,384]{1,0:T(2,128)S(1)} fusion(s32[2048,384]{1,0:T(8,128)} %param.4, f32[1,2048]{1,0:T(1,128)S(1)} %bitcast.49, f32[1,2048]{1,0:T(1,128)S(1)} %bitcast.47), kind=kOutput, calls=%fused_computation.3 | convolution fusion | flops 19664896 | bytes 3165184 | tf_op jit(solution)/shard_map/dot_general | solution.py:45
  12.5 10.8 %all-reduce = (f32[2,384]{1,0:T(2,128)S(1)}, f32[2]{0:T(128)S(1)}) all-reduce(f32[2,384]{1,0:T(2,128)S(1)} %fusion, f32[2]{0:T(128)S(1)} %fusion.26), channel_id=1, replica_groups=mesh['parts'=2,'snp'=4,'hap'=4] {'hap'}, use_global_device_ids=true, to_apply=%region_0.0 | all-reduce | flops 770 | bytes 6160 | tf_op jit(solution)/shard_map/psum | solution.py:44
  23.3 0.0 copy-done.1
  23.3 0.1 fusion.29
  23.4 0.0 copy-done
  23.4 1.0 select_bitcast_fusion.1
  24.4 0.2 pad_maximum_fusion.2
  24.6 5.7 %collective-permute-start.1 = (bf16[2098,384]{1,0:T(8,128)(2,1)S(1)}, bf16[2098,384]{1,0:T(8,128)(2,1)S(1)}, u32[]{:S(2)}, u32[]{:S(2)}) collective-permute-start(bf16[2098,384]{1,0:T(8,128)(2,1)S(1)} %pad_maximum_fusion.2), channel_id=1, source_target_pairs={{0,4},{4,8},{8,12},{1,5},{5,9},{9,13},{2,6},{6,10},{10,14},{3,7},{... | collective-permute-start | bytes 4833800 | tf_op jit(solution)/shard_map/ppermute | solution.py:13
  30.4 1.9 collective-permute-start
  32.3 0.5 select_bitcast_fusion
  32.8 1.4 fusion.6
  34.2 13.9 %collective-permute-done.1 = bf16[2098,384]{1,0:T(8,128)(2,1)S(1)} collective-permute-done((bf16[2098,384]{1,0:T(8,128)(2,1)S(1)}, bf16[2098,384]{1,0:T(8,128)(2,1)S(1)}, u32[]{:S(2)}, u32[]{:S(2)}) %collective-permute-start.1) | collective-permute-done | bytes 1611296 | tf_op jit(solution)/shard_map/ppermute | solution.py:13
  48.2 1.4 fusion.10
  49.6 2.9 %collective-permute-done = bf16[2098,384]{1,0:T(8,128)(2,1)S(1)} collective-permute-done((bf16[2098,384]{1,0:T(8,128)(2,1)S(1)}, bf16[2098,384]{1,0:T(8,128)(2,1)S(1)}, u32[]{:S(2)}, u32[]{:S(2)}) %collective-permute-start) | collective-permute-done | bytes 1611296 | tf_op jit(solution)/shard_map/ppermute | solution.py:13
  52.6 0.0 copy-start.2
  52.6 1.4 fusion.9
  54.0 0.0 copy-done.2
  54.0 2.1 %pad_maximum_fusion = f32[384,3,2,384]{0,3,2,1:T(8,128)} fusion(f32[384,1,2,384]{0,3,2,1:T(8,128)S(1)} %fusion.10, f32[384,1,2,384]{0,3,2,1:T(8,128)S(1)} %fusion.9, f32[384,1,2,384]{0,3,2,1:T(8,128)S(1)} %fusion.6), kind=kLoop, calls=%fused_computation | loop fusion | flops 1769472 | bytes 7077888 | tf_op jit(solution)/shard_map/stack | solution.py:65
  56.1 0.0 copy-start.3
  56.1 0.0 all-reduce.3.cloned.1.call-update
  56.1 0.6 copy-done.3
  56.7 0.6 fusion.30
  57.4 0.9 abs_compare_fusion.2
  58.3 0.8 slice_bitcast_fusion.9
  59.1 127.7 %all-reduce.3.cloned.1.call-done = f32[384,3,2,384]{0,3,2,1:T(8,128)} async-done(((f32[384,3,2,384]{0,3,2,1:T(8,128)}), f32[384,3,2,384]{0,3,2,1:T(8,128)}) %all-reduce.3.cloned.1.call-update) | async-done | bytes 3538960 | tf_op jit(solution)/shard_map/psum | solution.py:64
  186.8 2.9 %convolution_bitcast_fusion = f32[50,96]{1,0:T(8,128)} fusion(f32[384,3,2,384]{0,3,2,1:T(8,128)} %all-reduce.3.cloned.1.call-done, s32[]{:T(128)S(6)} %select_n.26, s32[]{:T(128)S(6)} %add.52, pred[96,1,384]{0,2,1:T(32,128)(4,1)S(1)} %get-tuple-element.17, pred[96,1,384]{0,2,1:T(32,128)(4,1)S(1)} %get-tuple-element.16, ...), kind=kOutput, calls=%fused_computation.17 | convolution fusion | flops 66912768 | bytes 1424648 | tf_op jit(solution)/shard_map/tak,rtk->ar/dot_general | solution.py:84
  (7 shorter events, 0.1 us)
Async XLA Ops:
  6.5 16.8 %copy-start.1 = (s32[50,384]{1,0:T(8,128)S(1)}, s32[50,384]{1,0:T(8,128)}, u32[]{:S(2)}) copy-start(s32[50,384]{1,0:T(8,128)} %param.6) | copy-start | bytes 230404
  6.5 180.3 %all-reduce.3.cloned.1.call-start = ((), (), s32[]{:S(2)}) async-start(), calls=%async_computation | async-start | bytes 7077888 | tf_op jit(solution)/shard_map/psum | solution.py:64
  8.8 14.6 %copy-start = (s32[2048,384]{1,0:T(8,128)S(1)}, s32[2048,384]{1,0:T(8,128)}, u32[]{:S(2)}) copy-start(s32[2048,384]{1,0:T(8,128)} %param.4) | copy-start | bytes 9437188
  24.6 23.6 %collective-permute-start.1 = (bf16[2098,384]{1,0:T(8,128)(2,1)S(1)}, bf16[2098,384]{1,0:T(8,128)(2,1)S(1)}, u32[]{:S(2)}, u32[]{:S(2)}) collective-permute-start(bf16[2098,384]{1,0:T(8,128)(2,1)S(1)} %pad_maximum_fusion.2), channel_id=1, source_target_pairs={{0,4},{4,8},{8,12},{1,5},{5,9},{9,13},{2,6},{6,10},{10,14},{3,7},{... | collective-permute-start | bytes 4833800 | tf_op jit(solution)/shard_map/ppermute | solution.py:13
  30.4 22.2 %collective-permute-start = (bf16[2098,384]{1,0:T(8,128)(2,1)S(1)}, bf16[2098,384]{1,0:T(8,128)(2,1)S(1)}, u32[]{:S(2)}, u32[]{:S(2)}) collective-permute-start(bf16[2098,384]{1,0:T(8,128)(2,1)S(1)} %pad_maximum_fusion.2), channel_id=1, source_target_pairs={{4,0},{8,4},{12,8},{5,1},{9,5},{13,9},{6,2},{10,6},{14,10},{7,3},{... | collective-permute-start | bytes 4833800 | tf_op jit(solution)/shard_map/ppermute | solution.py:13
  52.6 1.4 copy-start.2
  56.1 0.7 copy-start.3
Sparse Core Ops, SparseCore 0:
  56.2 130.5 all-reduce.2
where the time goes:
time: 198 us; the launch traced here: 196 us
  waiting for transfers between devices  145 us (73%)
  between operations  13.5 us (7%)
  matrix products  10.9 us (6%)
  blocking collectives  10.8 us (5%)
  starting transfers between devices  7.67 us (4%)
  other arithmetic  7.59 us (4%)
    psum x1, waiting for transfers between devices, per_device(): lax.psum(jnp.stack([jnp.einsum('hpj,hk->jpk', masked, piece[:hap_rows], p...  128 us
    ppermute x2, waiting for transfers between devices, shifted(): lax.ppermute(value, axis, [(source, source + steps) for source in range(l...  16.9 us
    psum x1, blocking collectives, per_device(): lax.psum((jnp.dot(weights, alleles, precision=PRECISE), jnp.sum(weights,...  10.8 us
    ppermute x2, starting transfers between devices, shifted(): lax.ppermute(value, axis, [(source, source + steps) for source in range(l...  7.66 us
    dot_general x3, matrix products, per_device(): jnp.einsum('hpj,hk->jpk', masked, piece[:hap_rows], preferred_element_typ...  4.33 us
  transfers between devices with their start and end apart: 3, of which 3 were waited for; matrix products, arithmetic and copies ran while one was open for 3% of the time, Pallas kernels for 0%

commit v1 on v0

v1 whole, which is shorter than its diff:
```python
import jax
import jax.numpy as jnp
from jax import lax
from jax.sharding import PartitionSpec as P

PRECISE = lax.Precision.HIGHEST
VARIANCE_FLOOR = 0.01
BASE_BITS = 12
BASE = 1 << BASE_BITS
FIELD_BITS = 16


def shifted(value, axis, steps):
    count = lax.axis_size(axis)
    leading, last = (max(0, -steps), min(count, count - steps))
    return lax.ppermute(value, axis, [(source, source + steps) for source in range(leading, last)])


def to_fields(values):
    whole = values.astype(jnp.int32)
    return whole + (whole >> BASE_BITS) * ((1 << FIELD_BITS) - BASE)


def from_fields(packed):
    first = packed & ((1 << FIELD_BITS) - 1)
    second = lax.shift_right_logical(packed, FIELD_BITS)
    return first.astype(jnp.float32), second.astype(jnp.float32)


def column_stats(totals, count):
    size = jnp.maximum(count, 1.0)
    frequency = totals / size
    variance = jnp.maximum(frequency * (1.0 - frequency), VARIANCE_FLOOR)
    inverse = 1.0 / jnp.sqrt(size * variance)
    low = ((0.0 - frequency) * inverse).astype(jnp.bfloat16).astype(jnp.float32)
    high = ((1.0 - frequency) * inverse).astype(jnp.bfloat16).astype(jnp.float32)
    step = high - low
    root = lax.rsqrt(size)
    carried = step * totals * root
    whole = (low * count + step * totals) * root
    return step, carried, whole


def count_dot(left, right):
    return lax.dot_general(
        left, right, (((0,), (0,)), ((), ())), preferred_element_type=jnp.float32
    )


def lookup(table, position):
    places = jnp.arange(table.shape[0], dtype=jnp.int32)
    return jnp.sum(jnp.where(places == position, table, 0))


def per_device(haplotypes, labels, annotations, reach):
    rows, snps = haplotypes.shape
    half = snps // 2
    groups = lax.axis_size("hap")
    blocks = lax.axis_size("snp")
    share = snps // groups
    hap_index = lax.axis_index("hap")
    snp_index = lax.axis_index("snp")

    alleles = haplotypes.astype(jnp.bfloat16)
    weight = jnp.where(labels > 0, BASE, 1).astype(jnp.bfloat16)
    weighted = alleles * weight[:, None]
    annots = annotations.astype(jnp.bfloat16)
    payload = jnp.concatenate([alleles, annots], axis=0)
    upper = shifted(payload[:, :half], "snp", -1)
    lower = shifted(payload[:, half:], "snp", 1)

    row = jnp.arange(snps, dtype=jnp.int32)[:, None]
    col = jnp.arange(snps, dtype=jnp.int32)[None, :]
    own_tile = count_dot(weighted, alleles)
    upper_tile = count_dot(weighted, upper[:rows])
    lower_tile = count_dot(lower[:rows], weighted[:, half:])
    weight_row = weight[None, :]
    nearby = jnp.concatenate([upper[:rows], lower[:rows]], axis=1)
    own_totals = jnp.dot(weight_row, alleles, preferred_element_type=jnp.float32)
    near_totals = jnp.dot(weight_row, nearby, preferred_element_type=jnp.float32)
    other = jnp.concatenate(
        [upper_tile, jnp.concatenate([jnp.zeros_like(lower_tile), lower_tile], axis=0)], axis=1
    )
    square = jnp.where(col >= row, own_tile, other)
    far = jnp.sum(jnp.where(col == row, other, 0.0), axis=0, keepdims=True)
    sizes = jnp.broadcast_to(jnp.sum(weight.astype(jnp.float32)), (1, snps))
    extras = jnp.concatenate([own_totals, near_totals, far, sizes, jnp.zeros((4, snps))], axis=0)
    square, extras = to_fields(square), to_fields(extras)

    def for_group(group):
        part = lax.dynamic_slice_in_dim(square, group * share, share, 0)
        return jnp.concatenate([part, extras], axis=0)

    summed = for_group(hap_index)
    received = []
    for step in range(1, groups):
        received.append(
            lax.ppermute(
                for_group((hap_index + step) % groups),
                "hap",
                [(source, (source + step) % groups) for source in range(groups)],
            )
        )
    for piece in received:
        summed = summed + piece

    counts = from_fields(summed[:share])
    extra = from_fields(summed[share:])
    col = jnp.arange(snps, dtype=jnp.int32)[None, :]
    row = hap_index * share + jnp.arange(share, dtype=jnp.int32)[:, None]
    in_own = col >= row
    in_upper = (col < row) & (col < half)
    in_lower = (col < row) & (col >= half)
    distance = jnp.where(in_own, col - row, snps + col - row)

    product = 1.0
    far_product = 1.0
    for pop in range(2):
        count = extra[pop][3, 0]
        own = column_stats(extra[pop][0], count)
        near = column_stats(extra[pop][1], count)
        own_rows = [lax.dynamic_slice_in_dim(v, hap_index * share, share, 0) for v in own]
        near_rows = [lax.dynamic_slice_in_dim(v, hap_index * share, share, 0) for v in near]
        at_row = [jnp.where(in_lower, n[:, None], o[:, None]) for o, n in zip(own_rows, near_rows)]
        at_col = [jnp.where(in_upper, n[None, :], o[None, :]) for o, n in zip(own, near)]
        corr = (
            at_row[0] * at_col[0] * counts[pop]
            - at_row[1] * at_col[1]
            + at_row[2] * at_col[2]
        )
        product = product * corr
        far_count = lax.dynamic_slice_in_dim(extra[pop][2], hap_index * share, share, 0)
        far_product = far_product * (
            own_rows[0] * near_rows[0] * far_count
            - own_rows[1] * near_rows[1]
            + own_rows[2] * near_rows[2]
        )

    reach_here = lookup(reach, snp_index)
    reach_up = lookup(reach, snp_index + 1)
    reach_down = lookup(reach, snp_index - 1)
    near_annots = jnp.concatenate([upper[rows:], lower[rows:]], axis=1).astype(jnp.float32)
    annots = annots.astype(jnp.float32)
    annots_rows = lax.dynamic_slice_in_dim(annots, hap_index * share, share, 1)
    near_rows = lax.dynamic_slice_in_dim(near_annots, hap_index * share, share, 1)
    is_upper = hap_index < groups // 2

    def kept(where, limit):
        return jnp.where(where & (distance <= limit), product, 0.0)

    def dot(left, right):
        return jnp.dot(left, right, precision=PRECISE)

    direct_own = dot(annots, kept(in_own, reach_here).T) + dot(
        near_annots[:, :half], kept(in_upper, reach_here)[:, :half].T
    )
    direct_down = dot(annots[:, half:], kept(in_lower, reach_down)[:, half:].T)
    mirrored_own = dot(annots_rows, kept(in_own & (col > row), reach_here)) + dot(
        near_rows, kept(in_lower, reach_here)
    )
    mirrored_up = dot(annots_rows, kept(in_upper, reach_up)[:, :half])
    mirrored_up = jnp.concatenate([mirrored_up, jnp.zeros_like(mirrored_up)], axis=1)
    far_own = near_rows * jnp.where(snps <= reach_here, far_product, 0.0)[None, :]
    reach_far = jnp.where(is_upper, reach_up, reach_down)
    far_near = annots_rows * jnp.where(snps <= reach_far, far_product, 0.0)[None, :]

    mirrored = jnp.stack([mirrored_own, mirrored_up])

    def scores_for(group):
        return lax.dynamic_slice_in_dim(mirrored, group * share, share, 2)

    scores = scores_for(hap_index)
    received = []
    for step in range(1, groups):
        received.append(
            lax.ppermute(
                scores_for((hap_index + step) % groups),
                "hap",
                [(source, (source + step) % groups) for source in range(groups)],
            )
        )
    for piece in received:
        scores = scores + piece
    own_scores = scores[0] + direct_own + far_own
    near_scores = scores[1] + direct_down + far_near
    pairs = []
    for block in range(blocks):
        for group in range(groups):
            target = block + 1 if group < groups // 2 else block - 1
            if 0 <= target < blocks:
                pairs.append((block * groups + group, target * groups + group))
    return own_scores + lax.ppermute(near_scores, ("snp", "hap"), pairs)


def solution(mesh):
    in_specs = (
        P("hap", ("parts", "snp")),
        P(("parts", "hap")),
        P(None, ("parts", "snp")),
        P("parts"),
    )
    out_specs = P(None, ("parts", "snp", "hap"))
    return jax.shard_map(
        per_device, mesh=mesh, in_specs=in_specs, out_specs=out_specs, check_vma=False
    )
```

time: 198 us -> 68.9 us (0.35)
  waiting for transfers between devices: 145 us -> 13 us
  starting transfers between devices: 7.67 us -> 18.9 us
  blocking collectives: 10.8 us -> 0 us
  between operations: 13.5 us -> 3.57 us
  local copies, waits for them, and re-layouts: 1.46 us -> 9.76 us
  other arithmetic: 7.59 us -> 12 us
    psum x1 -> x0, waiting for transfers between devices: 128 us -> none  [per_device(): lax.psum(jnp.stack([jnp.einsum('hpj,hk->jpk', masked, piece[:hap_rows], p...]
    ppermute x0 -> x7, starting transfers between devices: none -> 12.5 us  [the longest x3 4.73 us: per_device(): lax.ppermute(for_group((hap_index + step) % groups), 'hap', [(source, (so...]
    ppermute x2, waiting for transfers between devices: 16.9 us -> 5.31 us  [shifted(): lax.ppermute(value, axis, [(source, source + steps) for source in range(l...]
    psum x1 -> x0, blocking collectives: 10.8 us -> none  [per_device(): lax.psum((jnp.dot(weights, alleles, precision=PRECISE), jnp.sum(weights,...]
    ppermute x0 -> x7, waiting for transfers between devices: none -> 7.7 us  [the longest x3 4.1 us: per_device(): lax.ppermute(for_group((hap_index + step) % groups), 'hap', [(source, (so...]
    mul x0 -> x12, other arithmetic: none -> 6.43 us  [the longest x4 2.62 us: column_stats(): whole = (low * count + step * totals) * root]
    slice x1 -> x5, local copies, waits for them, and re-layouts: 0.03 us -> 4.27 us  [the longest x1 1.19 us: per_device(): upper_tile = count_dot(weighted, upper[:rows])]
    unnamed x8, local copies, waits for them, and re-layouts: 0.61 us -> 4.59 us
  transfers between devices with their start and end apart: 3 -> 9, of which waited for: 3 -> 5; matrix products, arithmetic and copies ran while one was open for 3% -> 10% of each run, Pallas kernels for 0% -> 0%
where the time goes in v1:
time: 68.9 us; the launch traced here: 68.2 us
  starting transfers between devices  18.9 us (27%)
  waiting for transfers between devices  13 us (19%)
  other arithmetic  12 us (17%)
  matrix products  11 us (16%)
  local copies, waits for them, and re-layouts  9.76 us (14%)
  between operations  3.57 us (5%)
    ppermute x2, starting transfers between devices, shifted(): lax.ppermute(value, axis, [(source, source + steps) for source in range(l...  6.42 us
    dot_general x6, matrix products, dot(): return jnp.dot(left, right, precision=PRECISE)  5.73 us
    ppermute x2, waiting for transfers between devices, shifted(): lax.ppermute(value, axis, [(source, source + steps) for source in range(l...  5.31 us
    ppermute x3, starting transfers between devices, per_device(): lax.ppermute(for_group((hap_index + step) % groups), 'hap', [(source, (so...  4.73 us
    unnamed x8, local copies, waits for them, and re-layouts  4.59 us
    ppermute x3, starting transfers between devices, per_device(): lax.ppermute(scores_for((hap_index + step) % groups), 'hap', [(source, (s...  4.28 us
    dot_general x3, matrix products, count_dot(): lax.dot_general(left, right, (((0,), (0,)), ((), ())), preferred_element_...  4.22 us
    ppermute x3, waiting for transfers between devices, per_device(): lax.ppermute(for_group((hap_index + step) % groups), 'hap', [(source, (so...  4.1 us
  transfers between devices with their start and end apart: 9, of which 5 were waited for; matrix products, arithmetic and copies ran while one was open for 10% of the time, Pallas kernels for 0%

profile of v1, /device:TPU:1, one launch (start us, length us, event | category | flops | bytes accessed | tf_op | source)
XLA Modules:
  0.0 68.2 jit_solution(3558138878368278395)
XLA Ops:
  0.0 1.3 %convert_reduce_fusion = (f32[]{:T(128)}, bf16[2048]{0:T(1024)(128)(2,1)S(1)}) fusion(s32[2048]{0:T(1024)} %param.5), kind=kLoop, calls=%fused_computation.104 | loop fusion | flops 10239 | bytes 12292 | tf_op jit(solution)/shard_map/reduce_sum | solution.py:86
  1.3 3.6 %copy.7 = s32[2048,384]{0,1:T(8,128)} copy(s32[2048,384]{1,0:T(8,128)} %param.4) | data formatting | bytes 6291456 | tf_op args[0]
  4.9 0.1 copy.8
  5.0 2.1 %broadcast_multiply_fusion = (bf16[2048,384]{0,1:T(8,128)(2,1)S(1)}, bf16[2048,384]{0,1:T(8,128)(2,1)S(1)}) fusion(bf16[2048]{0:T(1024)(128)(2,1)S(1)} %get-tuple-element.59, s32[2048,384]{0,1:T(8,128)} %copy.7), kind=kLoop, calls=%fused_computation.17 | loop fusion | flops 1572864 | bytes 6295552 | tf_op jit(solution)/shard_map/mul | solution.py:66
  7.1 1.4 %fusion.6 = (bf16[2098,192]{0,1:T(8,128)(2,1)}, bf16[2098,192]{0,1:T(8,128)(2,1)}) fusion(bf16[2048,384]{0,1:T(8,128)(2,1)S(1)} %get-tuple-element.61, bf16[50,384]{0,1:T(8,128)(2,1)S(1)} %copy.8), kind=kLoop, calls=%fused_computation.13 | loop fusion | flops 3222528 | bytes 3222528 | tf_op jit(solution)/shard_map/concatenate | solution.py:68
  8.5 2.0 %collective-permute-start = (bf16[2098,192]{0,1:T(8,128)(2,1)}, bf16[2098,192]{0,1:T(8,128)(2,1)}, u32[]{:S(2)}, u32[]{:S(2)}) collective-permute-start(bf16[2098,192]{0,1:T(8,128)(2,1)} %get-tuple-element.62), channel_id=1, source_target_pairs={{4,0},{8,4},{12,8},{5,1},{9,5},{13,9},{6,2},{10,6},{14,10},{7,3},{... | collective-permute-start | bytes 2416904 | tf_op jit(solution)/shard_map/ppermute | solution.py:16
  10.5 4.5 %collective-permute-start.1 = (bf16[2098,192]{0,1:T(8,128)(2,1)}, bf16[2098,192]{0,1:T(8,128)(2,1)}, u32[]{:S(2)}, u32[]{:S(2)}) collective-permute-start(bf16[2098,192]{0,1:T(8,128)(2,1)} %get-tuple-element.63), channel_id=1, source_target_pairs={{0,4},{4,8},{8,12},{1,5},{5,9},{9,13},{2,6},{6,10},{10,14},{3,7},{... | collective-permute-start | bytes 2416904 | tf_op jit(solution)/shard_map/ppermute | solution.py:16
  15.0 0.7 %fusion.115 = (s32[]{:T(128)}, s32[]{:T(128)}, s32[]{:T(128)}) fusion(s32[4]{0:T(128)S(1)} %copy-done.1, s32[]{:T(128)S(6)} %sub.166, s32[]{:T(128)S(6)} %axis_index.25, s32[]{:T(128)S(6)} %add.198), kind=kLoop, calls=%fused_computation.224 | loop fusion | flops 33 | bytes 40 | tf_op jit(solution)/shard_map/reduce_sum | solution.py:52
  17.7 0.5 fusion.140
  18.2 5.3 %collective-permute-done = bf16[2098,192]{0,1:T(8,128)(2,1)} collective-permute-done((bf16[2098,192]{0,1:T(8,128)(2,1)}, bf16[2098,192]{0,1:T(8,128)(2,1)}, u32[]{:S(2)}, u32[]{:S(2)}) %collective-permute-start) | collective-permute-done | bytes 805664 | tf_op jit(solution)/shard_map/ppermute | solution.py:16
  23.5 1.7 %fusion.9 = f32[384,192]{1,0:T(8,128)S(1)} fusion(bf16[2048,384]{0,1:T(8,128)(2,1)S(1)} %get-tuple-element.61, bf16[2048]{0:T(1024)(128)(2,1)S(1)} %get-tuple-element.59, bf16[2098,192]{0,1:T(8,128)(2,1)} %collective-permute-done), kind=kOutput, calls=%fused_computation.24 | convolution fusion | flops 302776320 | bytes 2658304 | tf_op jit(solution)/shard_map/dot_general | solution.py:45
  25.2 1.5 %fusion.7 = f32[192,192]{1,0:T(8,128)S(1)} fusion(bf16[2048,384]{0,1:T(8,128)(2,1)S(1)} %get-tuple-element.60, bf16[2098,192]{0,1:T(8,128)(2,1)} %collective-permute-done.1), kind=kOutput, calls=%fused_computation.15 | convolution fusion | flops 150994944 | bytes 1720320 | tf_op jit(solution)/shard_map/dot_general | solution.py:45
  26.8 1.0 %multiply_add_fusion = s32[384,384]{1,0:T(8,128)S(1)} fusion(bf16[2048,384]{0,1:T(8,128)(2,1)S(1)} %get-tuple-element.61, f32[192,192]{1,0:T(8,128)S(1)} %fusion.7, f32[384,192]{1,0:T(8,128)S(1)} %fusion.9, bf16[2048]{0:T(1024)(128)(2,1)S(1)} %get-tuple-element.59), kind=kOutput, calls=%fused_computation.22 | convolution fusion | flops 606093312 | bytes 2609152 | tf_op jit(solution)/shard_map/dot_general | solution.py:45
  27.9 1.2 %slice.97 = bf16[2048,192]{0,1:T(8,128)(2,1)S(1)} slice(bf16[2098,192]{0,1:T(8,128)(2,1)} %collective-permute-done), slice={[0:2048], [0:192]} | slice | bytes 1572864 | tf_op jit(solution)/shard_map/slice | solution.py:75
  29.1 1.2 %slice.98 = bf16[2048,192]{0,1:T(8,128)(2,1)S(1)} slice(bf16[2098,192]{0,1:T(8,128)(2,1)} %collective-permute-done.1), slice={[0:2048], [0:192]} | slice | bytes 1572864 | tf_op jit(solution)/shard_map/slice | solution.py:76
  30.3 0.5 fusion
  30.8 0.7 broadcast_in_dim.236
  31.6 1.4 %collective-permute-start.2 = (s32[104,384]{1,0:T(8,128)S(1)}, s32[104,384]{1,0:T(8,128)S(1)}, u32[]{:S(2)}, u32[]{:S(2)}) collective-permute-start(s32[104,384]{1,0:T(8,128)S(1)} %get-tuple-element.79), channel_id=1, source_target_pairs={{0,1},{1,2},{2,3},{3,0},{4,5},{5,6},{6,7},{7,4},{8,9},{9,10},{10,1... | collective-permute-start | bytes 479240 | tf_op jit(solution)/shard_map/ppermute | solution.py:98
  33.0 2.3 %collective-permute-start.3 = (s32[104,384]{1,0:T(8,128)S(1)}, s32[104,384]{1,0:T(8,128)S(1)}, u32[]{:S(2)}, u32[]{:S(2)}) collective-permute-start(s32[104,384]{1,0:T(8,128)S(1)} %get-tuple-element.80), channel_id=1, source_target_pairs={{0,2},{1,3},{2,0},{3,1},{4,6},{5,7},{6,4},{7,5},{8,10},{9,11},{10,... | collective-permute-start | bytes 479240 | tf_op jit(solution)/shard_map/ppermute | solution.py:98
  35.3 1.1 %collective-permute-start.4 = (s32[104,384]{1,0:T(8,128)S(1)}, s32[104,384]{1,0:T(8,128)S(1)}, u32[]{:S(2)}, u32[]{:S(2)}) collective-permute-start(s32[104,384]{1,0:T(8,128)S(1)} %get-tuple-element.81), channel_id=1, source_target_pairs={{0,3},{1,0},{2,1},{3,2},{4,7},{5,4},{6,5},{7,6},{8,11},{9,8},{10,9... | collective-permute-start | bytes 479240 | tf_op jit(solution)/shard_map/ppermute | solution.py:98
  36.3 0.8 %broadcast_compare_fusion = (pred[96,384]{1,0:T(32,128)(4,1)S(1)}, pred[96,384]{1,0:T(32,128)(4,1)S(1)}, pred[96,384]{1,0:T(32,128)(4,1)S(1)}) fusion(s32[]{:T(128)} %get-tuple-element.26, s32[384]{0:T(512)S(1)} %iota_add_fusion, s32[96]{0:T(128)S(1)} %iota_add_fusion.1, pred[384]{0:T(512)(128)(4,1)S(1)} %get-tuple-element.90, ...), kind=kLoop, calls=%fused_computation.73 | loop fusion | flops 294912 | bytes 113284 | tf_op jit(solution)/shard_map/le | solution.py:149
  37.1 0.8 %slice.108 = bf16[50,192]{0,1:T(8,128)(2,1)S(1)} slice(bf16[2098,192]{0,1:T(8,128)(2,1)} %collective-permute-done), slice={[2048:2098], [0:192]} | slice | bytes 38400
  38.0 0.8 %slice.109 = bf16[50,192]{0,1:T(8,128)(2,1)S(1)} slice(bf16[2098,192]{0,1:T(8,128)(2,1)} %collective-permute-done.1), slice={[2048:2098], [0:192]} | slice | bytes 38400 | tf_op jit(solution)/shard_map/slice | solution.py:142
  38.9 4.1 %collective-permute-done.3 = s32[104,384]{1,0:T(8,128)S(1)} collective-permute-done((s32[104,384]{1,0:T(8,128)S(1)}, s32[104,384]{1,0:T(8,128)S(1)}, u32[]{:S(2)}, u32[]{:S(2)}) %collective-permute-start.3) | collective-permute-done | bytes 159776 | tf_op jit(solution)/shard_map/ppermute | solution.py:98
  43.1 0.6 slice.102
  43.7 0.5 slice.106
  45.6 0.7 %multiply_reduce_fusion.3 = (f32[384]{0:T(512)S(1)}, f32[384]{0:T(512)S(1)}, f32[384]{0:T(512)S(1)}, f32[384]{0:T(512)S(1)}, f32[384]{0:T(512)S(1)}, /*index=5*/f32[384]{0:T(512)S(1)}, f32[384]{0:T(512)S(1)}, f32[384]{0:T(512)S(1)}) fusion(f32[]{:T(128)S(6)} %rsqrt.25, f32[1,384]{1,0:T(1,128)S(1)} %get-tuple-element.85, f32[8,384]{1,0:T(8,128)S(1)} %get-tuple-element.72, ...), kind=kLoop, calls=%fused_computation.199 | loop fusion | flops 9984 | bytes 21516 | tf_op jit(solution)/shard_map/mul | solution.py:39
  46.3 0.7 fusion.72
  47.0 0.7 fusion.70
  47.7 0.7 %multiply_reduce_fusion.7 = (f32[384]{0:T(512)S(1)}, f32[384]{0:T(512)S(1)}, f32[384]{0:T(512)S(1)}, f32[384]{0:T(512)S(1)}, f32[384]{0:T(512)S(1)}, /*index=5*/...) fusion(f32[]{:T(128)S(6)} %rsqrt.24, f32[1,384]{1,0:T(1,128)S(1)} %get-tuple-element.74, ...), kind=kLoop, calls=%fused_computation.205 | loop fusion | flops 9984 | bytes 24588 | tf_op jit(solution)/shard_map/mul | solution.py:39
  48.4 0.6 fusion.68
  49.0 0.6 fusion.66
  49.8 0.3 add_multiply_fusion
  50.1 1.0 %convolution_bitcast_fusion.1 = f32[50,96]{1,0:T(8,128)S(1)} fusion(bf16[50,384]{1,0:T(8,128)(2,1)S(1)} %convert_element_type.164, f32[96,384]{1,0:T(8,128)S(1)} %add_multiply_fusion, s32[96]{0:T(128)S(1)} %iota_add_fusion.1, s32[]{:T(128)} %get-tuple-element.26, s32[384]{0:T(512)S(1)} %iota_add_fusion), kind=kOutput, calls=%fused_computation.12 | convolution fusion | flops 22376448 | bytes 206980 | tf_op jit(solution)/shard_map/dot_general | solution.py:152
  51.0 1.0 %fusion.15 = f32[50,384]{1,0:T(8,128)S(1)} fusion(f32[96,384]{1,0:T(8,128)S(1)} %add_multiply_fusion, s32[96]{0:T(128)S(1)} %iota_add_fusion.1, bf16[50,384]{1,0:T(8,128)(2,1)S(1)} %convert_element_type.164, s32[]{:T(128)S(6)} %select_n.153, s32[]{:T(128)} %get-tuple-element.26, s32[384]{0:T(512)S(1)} %iota_add_fusion), kind=kOutput, calls=%fused_computation.42 | convolution fusion | flops 22450176 | bytes 241160 | tf_op jit(solution)/shard_map/dot_general | solution.py:152
  52.0 0.9 %fusion.26 = f32[50,192]{1,0:T(8,128)S(1)} fusion(s32[96,384]{1,0:T(8,128)S(1)} %subtract_select_fusion, f32[96,384]{1,0:T(8,128)S(1)} %add_multiply_fusion, pred[96,384]{1,0:T(32,128)(4,1)S(1)} %get-tuple-element.83, s32[]{:T(128)} %get-tuple-element.27, bf16[50,384]{1,0:T(8,128)(2,1)S(1)} %convert_element_type.164, s32[]{:T(128)S(6)} %select_n.153), kind=kOutput, calls=%fused_computation.59 | convolution fusion | flops 11114496 | bytes 273928 | tf_op jit(solution)/shard_map/dot_general | solution.py:152
  52.9 1.0 %fusion.5 = f32[1,50,384]{2,1,0:T(8,128)S(1)} fusion(f32[50,384]{1,0:T(8,128)S(1)} %fusion.15, f32[96,384]{1,0:T(8,128)S(1)} %add_multiply_fusion, s32[]{:T(128)S(6)} %select_n.153, bf16[50,192]{1,0:T(8,128)(2,1)S(1)} %copy.15, bf16[50,192]{1,0:T(8,128)(2,1)S(1)} %copy.16, s32[96]{0:T(128)S(1)} %iota_add_fusion.1, pred[384]{0:T(512)(128)(4,1)S(1)} %get-tuple-element.91, ...), kind=kOutput, calls=%fused_computation.9 | convolution fusion | flops 22488576 | bytes 341768 | tf_op jit(solution)/shard_map/dot_general | solution.py:152
  53.9 0.1 fusion.47
  54.0 2.1 %collective-permute-start.5 = (f32[2,50,96]{2,1,0:T(8,128)S(1)}, f32[2,50,96]{2,1,0:T(8,128)S(1)}, u32[]{:S(2)}, u32[]{:S(2)}) collective-permute-start(f32[2,50,96]{2,1,0:T(8,128)S(1)} %get-tuple-element.68), channel_id=1, source_target_pairs={{0,1},{1,2},{2,3},{3,0},{4,5},{5,6},{6,7},{7,4},{8,9},{9,10},{10,1... | collective-permute-start | bytes 115208 | tf_op jit(solution)/shard_map/ppermute | solution.py:176
  56.1 1.6 %collective-permute-start.6 = (f32[2,50,96]{2,1,0:T(8,128)S(1)}, f32[2,50,96]{2,1,0:T(8,128)S(1)}, u32[]{:S(2)}, u32[]{:S(2)}) collective-permute-start(f32[2,50,96]{2,1,0:T(8,128)S(1)} %get-tuple-element.69), channel_id=1, source_target_pairs={{0,2},{1,3},{2,0},{3,1},{4,6},{5,7},{6,4},{7,5},{8,10},{9,11},{10,... | collective-permute-start | bytes 115208 | tf_op jit(solution)/shard_map/ppermute | solution.py:176
  57.7 0.6 collective-permute-start.7
  58.3 1.1 %collective-permute-done.5 = f32[2,50,96]{2,1,0:T(8,128)S(1)} collective-permute-done((f32[2,50,96]{2,1,0:T(8,128)S(1)}, f32[2,50,96]{2,1,0:T(8,128)S(1)}, u32[]{:S(2)}, u32[]{:S(2)}) %collective-permute-start.5) | collective-permute-done | bytes 38432 | tf_op jit(solution)/shard_map/ppermute | solution.py:176
  59.3 2.4 %collective-permute-done.6 = f32[2,50,96]{2,1,0:T(8,128)S(1)} collective-permute-done((f32[2,50,96]{2,1,0:T(8,128)S(1)}, f32[2,50,96]{2,1,0:T(8,128)S(1)}, u32[]{:S(2)}, u32[]{:S(2)}) %collective-permute-start.6) | collective-permute-done | bytes 38432 | tf_op jit(solution)/shard_map/ppermute | solution.py:176
  61.7 0.1 collective-permute-done.7
  62.0 1.0 %fusion.56 = f32[50,96]{1,0:T(8,128)S(1)} fusion(f32[2,50,96]{2,1,0:T(8,128)S(1)} %fusion.46, f32[96]{0:T(128)S(1)} %broadcast_select_fusion, bf16[50,384]{1,0:T(8,128)(2,1)S(1)} %convert_element_type.164, s32[]{:T(128)S(6)} %select_n.153, f32[96,384]{1,0:T(8,128)S(1)} %add_multiply_fusion, s32[96,384]{1,0:T(8,128)S(1)} %subtract_select_fusion, ...), kind=kOutput, calls=%fused_computation.93 | convolution fusion | flops 11133696 | bytes 312584 | tf_op jit(solution)/shard_map/dot_general | solution.py:152
  62.9 3.5 %collective-permute-start.8 = (f32[50,96]{1,0:T(8,128)S(1)}, f32[50,96]{1,0:T(8,128)S(1)}, u32[]{:S(2)}, u32[]{:S(2)}) collective-permute-start(f32[50,96]{1,0:T(8,128)S(1)} %fusion.56), channel_id=1, source_target_pairs={{0,4},{1,5},{4,8},{5,9},{6,2},{7,3},{8,12},{9,13},{10,6},{11,7},{1... | collective-permute-start | bytes 57608 | tf_op jit(solution)/shard_map/ppermute | solution.py:192
  66.4 1.0 %convolution_add_fusion.1 = f32[50,96]{1,0:T(8,128)S(1)} fusion(f32[50,96]{1,0:T(8,128)S(1)} %convolution_bitcast_fusion.1, pred[96,384]{1,0:T(32,128)(4,1)S(1)} %get-tuple-element.82, f32[96,384]{1,0:T(8,128)S(1)} %add_multiply_fusion, pred[96,384]{1,0:T(32,128)(4,1)S(1)} %get-tuple-element.83, bf16[2098,192]{0,1:T(8,128)(2,1)} %collective-permute-done), kind=kOutput, calls=%fused_computation.11 | convolution fusion | flops 11100864 | bytes 244480 | tf_op jit(solution)/shard_map/dot_general | solution.py:152
  67.5 0.7 %fusion.59 = f32[50,96]{1,0:T(8,128)} fusion(f32[50,96]{1,0:T(8,128)S(1)} %collective-permute-done.8, f32[50,96]{1,0:T(8,128)S(1)} %convolution_add_fusion.1, f32[2,50,96]{2,1,0:T(8,128)S(1)} %fusion.46, f32[96]{0:T(128)S(1)} %get-tuple-element.28, s32[]{:T(128)S(6)} %select_n.153, bf16[50,192]{1,0:T(8,128)(2,1)S(1)} %copy.16, bf16[50,192]{1,0:T(8,128)(2,1)S(1)} %copy.15), kind=kLoop, calls=%fused_computation.97 | loop fusion | flops 38400 | bytes 115588 | tf_op jit(solution)/shard_map/add | solution.py:192
  (34 shorter events, 1.0 us)
Async XLA Ops:
  1.3 3.6 %copy-start = (s32[50,384]{1,0:T(8,128)S(1)}, s32[50,384]{1,0:T(8,128)}, u32[]{:S(2)}) copy-start(s32[50,384]{1,0:T(8,128)} %param.6) | copy-start | bytes 230404
  7.1 7.8 %copy-start.1 = (s32[4]{0:T(128)S(1)}, s32[4]{0:T(128)}, u32[]{:S(2)}) copy-start(s32[4]{0:T(128)} %param.7) | copy-start | bytes 52
  8.5 15.0 %collective-permute-start = (bf16[2098,192]{0,1:T(8,128)(2,1)}, bf16[2098,192]{0,1:T(8,128)(2,1)}, u32[]{:S(2)}, u32[]{:S(2)}) collective-permute-start(bf16[2098,192]{0,1:T(8,128)(2,1)} %get-tuple-element.62), channel_id=1, source_target_pairs={{4,0},{8,4},{12,8},{5,1},{9,5},{13,9},{6,2},{10,6},{14,10},{7,3},{... | collective-permute-start | bytes 2416904 | tf_op jit(solution)/shard_map/ppermute | solution.py:16
  10.5 14.8 %collective-permute-start.1 = (bf16[2098,192]{0,1:T(8,128)(2,1)}, bf16[2098,192]{0,1:T(8,128)(2,1)}, u32[]{:S(2)}, u32[]{:S(2)}) collective-permute-start(bf16[2098,192]{0,1:T(8,128)(2,1)} %get-tuple-element.63), channel_id=1, source_target_pairs={{0,4},{4,8},{8,12},{1,5},{5,9},{9,13},{2,6},{6,10},{10,14},{3,7},{... | collective-permute-start | bytes 2416904 | tf_op jit(solution)/shard_map/ppermute | solution.py:16
  31.6 7.3 %collective-permute-start.2 = (s32[104,384]{1,0:T(8,128)S(1)}, s32[104,384]{1,0:T(8,128)S(1)}, u32[]{:S(2)}, u32[]{:S(2)}) collective-permute-start(s32[104,384]{1,0:T(8,128)S(1)} %get-tuple-element.79), channel_id=1, source_target_pairs={{0,1},{1,2},{2,3},{3,0},{4,5},{5,6},{6,7},{7,4},{8,9},{9,10},{10,1... | collective-permute-start | bytes 479240 | tf_op jit(solution)/shard_map/ppermute | solution.py:98
  33.0 10.1 %collective-permute-start.3 = (s32[104,384]{1,0:T(8,128)S(1)}, s32[104,384]{1,0:T(8,128)S(1)}, u32[]{:S(2)}, u32[]{:S(2)}) collective-permute-start(s32[104,384]{1,0:T(8,128)S(1)} %get-tuple-element.80), channel_id=1, source_target_pairs={{0,2},{1,3},{2,0},{3,1},{4,6},{5,7},{6,4},{7,5},{8,10},{9,11},{10,... | collective-permute-start | bytes 479240 | tf_op jit(solution)/shard_map/ppermute | solution.py:98
  35.3 7.8 %collective-permute-start.4 = (s32[104,384]{1,0:T(8,128)S(1)}, s32[104,384]{1,0:T(8,128)S(1)}, u32[]{:S(2)}, u32[]{:S(2)}) collective-permute-start(s32[104,384]{1,0:T(8,128)S(1)} %get-tuple-element.81), channel_id=1, source_target_pairs={{0,3},{1,0},{2,1},{3,2},{4,7},{5,4},{6,5},{7,6},{8,11},{9,8},{10,9... | collective-permute-start | bytes 479240 | tf_op jit(solution)/shard_map/ppermute | solution.py:98
  54.0 5.4 %collective-permute-start.5 = (f32[2,50,96]{2,1,0:T(8,128)S(1)}, f32[2,50,96]{2,1,0:T(8,128)S(1)}, u32[]{:S(2)}, u32[]{:S(2)}) collective-permute-start(f32[2,50,96]{2,1,0:T(8,128)S(1)} %get-tuple-element.68), channel_id=1, source_target_pairs={{0,1},{1,2},{2,3},{3,0},{4,5},{5,6},{6,7},{7,4},{8,9},{9,10},{10,1... | collective-permute-start | bytes 115208 | tf_op jit(solution)/shard_map/ppermute | solution.py:176
  56.1 5.6 %collective-permute-start.6 = (f32[2,50,96]{2,1,0:T(8,128)S(1)}, f32[2,50,96]{2,1,0:T(8,128)S(1)}, u32[]{:S(2)}, u32[]{:S(2)}) collective-permute-start(f32[2,50,96]{2,1,0:T(8,128)S(1)} %get-tuple-element.69), channel_id=1, source_target_pairs={{0,2},{1,3},{2,0},{3,1},{4,6},{5,7},{6,4},{7,5},{8,10},{9,11},{10,... | collective-permute-start | bytes 115208 | tf_op jit(solution)/shard_map/ppermute | solution.py:176
  57.7 4.2 %collective-permute-start.7 = (f32[2,50,96]{2,1,0:T(8,128)S(1)}, f32[2,50,96]{2,1,0:T(8,128)S(1)}, u32[]{:S(2)}, u32[]{:S(2)}) collective-permute-start(f32[2,50,96]{2,1,0:T(8,128)S(1)} %get-tuple-element.70), channel_id=1, source_target_pairs={{0,3},{1,0},{2,1},{3,2},{4,7},{5,4},{6,5},{7,6},{8,11},{9,8},{10,9... | collective-permute-start | bytes 115208 | tf_op jit(solution)/shard_map/ppermute | solution.py:176
  62.9 4.5 %collective-permute-start.8 = (f32[50,96]{1,0:T(8,128)S(1)}, f32[50,96]{1,0:T(8,128)S(1)}, u32[]{:S(2)}, u32[]{:S(2)}) collective-permute-start(f32[50,96]{1,0:T(8,128)S(1)} %fusion.56), channel_id=1, source_target_pairs={{0,4},{1,5},{4,8},{5,9},{6,2},{7,3},{8,12},{9,13},{10,6},{11,7},{1... | collective-permute-start | bytes 57608 | tf_op jit(solution)/shard_map/ppermute | solution.py:192

commit v2 on v0

v2 whole, which is shorter than its diff:
```python
import functools

import jax
import jax.numpy as jnp
from jax import lax
from jax.experimental import pallas as pl
from jax.experimental.pallas import tpu as pltpu
from jax.sharding import PartitionSpec as P

VARIANCE_FLOOR = 0.01
BASE_BITS = 12
BASE = 1 << BASE_BITS
FIELD_BITS = 16
LANES = 128
HALF_LANES = LANES // 2
CHUNKS = 4
VMEM = pl.BlockSpec(memory_space=pltpu.VMEM)
SMEM = pl.BlockSpec(memory_space=pltpu.SMEM)
ANY = pl.BlockSpec(memory_space=pl.ANY)
VMEM_LIMIT = 24 * 1024 * 1024


def iota(shape, axis):
    return lax.broadcasted_iota(jnp.int32, shape, axis)


def round_up(value, step):
    return -(-value // step) * step


def to_fields(values):
    whole = values.astype(jnp.int32)
    return whole + (whole >> BASE_BITS) * ((1 << FIELD_BITS) - BASE)


def from_fields(packed):
    first = packed & ((1 << FIELD_BITS) - 1)
    second = lax.shift_right_logical(packed, FIELD_BITS)
    return first.astype(jnp.float32), second.astype(jnp.float32)


def call(kernel, out_shape, in_specs, scratch_shapes=(), flops=0, moved=0):
    several = isinstance(out_shape, (list, tuple))
    return pl.pallas_call(
        kernel,
        out_shape=out_shape,
        in_specs=in_specs,
        out_specs=[VMEM] * len(out_shape) if several else VMEM,
        scratch_shapes=list(scratch_shapes),
        compiler_params=pltpu.CompilerParams(vmem_limit_bytes=VMEM_LIMIT),
        cost_estimate=pl.CostEstimate(flops=flops, bytes_accessed=moved, transcendentals=0),
    )


def store_packed(up_ref, down_ref, where, first, second):
    left = iota((first.shape[0], LANES), 1) < HALF_LANES
    middle = first[:, LANES : 2 * LANES]
    turned = pltpu.roll(second[:, LANES : 2 * LANES], HALF_LANES, 1)
    for ref, side, mixed in (
        (up_ref, slice(0, LANES), jnp.where(left, middle, turned)),
        (down_ref, slice(2 * LANES, 3 * LANES), jnp.where(left, turned, middle)),
    ):
        ref[where, 0:LANES] = first[:, side].astype(jnp.bfloat16)
        ref[where, LANES : 2 * LANES] = second[:, side].astype(jnp.bfloat16)
        ref[where, 2 * LANES : 3 * LANES] = mixed.astype(jnp.bfloat16)


def load_packed(up, down):
    left = iota((up.shape[0], LANES), 1) < HALF_LANES
    up_mixed, down_mixed = up[:, 2 * LANES :], down[:, 2 * LANES :]
    first = jnp.where(left, up_mixed, down_mixed)
    second = jnp.where(left, down_mixed, up_mixed).astype(jnp.float32)
    second = pltpu.roll(second, HALF_LANES, 1).astype(jnp.bfloat16)
    return (
        (up[:, :LANES], first, down[:, :LANES]),
        (up[:, LANES : 2 * LANES], second, down[:, LANES : 2 * LANES]),
    )


def prepare_kernel(hap_ref, annot_ref, alleles_ref, up_ref, down_ref, held, sems):
    rows = hap_ref.shape[0]
    size = rows // (2 * CHUNKS)
    starts = [side * (rows // 2) + chunk * size for chunk in range(CHUNKS) for side in range(2)]
    copies = [
        pltpu.make_async_copy(
            hap_ref.at[pl.ds(start, size)], held.at[pl.ds(start, size)], sems.at[number]
        )
        for number, start in enumerate(starts)
    ]
    for copy in copies:
        copy.start()
    annots = annot_ref[...].astype(jnp.float32)
    part = (up_ref.shape[0] - rows // 2)
    annots = jnp.concatenate(
        [annots, jnp.zeros((2 * part - annots.shape[0], annots.shape[1]), jnp.float32)], axis=0
    )
    store_packed(up_ref, down_ref, slice(rows // 2, rows // 2 + part), annots[:part], annots[part:])
    for chunk in range(CHUNKS):
        pair = []
        for side in range(2):
            number = 2 * chunk + side
            copies[number].wait()
            where = slice(starts[number], starts[number] + size)
            values = held[where, :].astype(jnp.float32)
            alleles_ref[where, :] = values.astype(jnp.bfloat16)
            pair.append(values)
        store_packed(up_ref, down_ref, slice(chunk * size, (chunk + 1) * size), *pair)


def send_shares(groups, source, share, targets):
    me = lax.axis_index("hap")
    for step, target in enumerate(targets):
        group = lax.rem(me + step, groups)
        target[0:share, :] = source[pl.ds(pl.multiple_of(group * share, 8), share), :]


def own_kernel(groups, share, alleles_ref, label_ref, *refs):
    weighted_ref, totals_ref, *targets = refs[: 2 + groups]
    tile, folded = refs[2 + groups :]
    rows, snps = alleles_ref.shape
    half = snps // 2
    weight = jnp.where(label_ref[...] > 0, float(BASE), 1.0)
    weighted_ref[0:snps, :] = alleles_ref[...].T * weight.astype(jnp.bfloat16)
    extra = weighted_ref.shape[0] - snps
    weighted_ref[snps:, :] = jnp.broadcast_to(weight, (extra, rows)).astype(jnp.bfloat16)
    tile[...] = jnp.dot(weighted_ref[...], alleles_ref[...], preferred_element_type=jnp.float32)
    count = jnp.sum(weight, axis=1, keepdims=True)
    totals_ref[...] = jnp.concatenate(
        [tile[snps : snps + 1, :], jnp.broadcast_to(count, (1, snps)), jnp.zeros((6, snps))], axis=0
    )
    row, col = iota((half, snps), 0), iota((half, snps), 1)
    moved = (col < half) | (col - half > row)
    turned = pltpu.roll(tile[0:half, :], half, 1)
    folded[0:half, :] = to_fields(jnp.where(moved, turned, tile[half:snps, :]))
    if folded.shape[0] > half:
        folded[half:, :] = jnp.zeros((folded.shape[0] - half, snps), jnp.int32)
    send_shares(groups, folded, share, targets)


def near_kernel(groups, share, weighted_ref, up_ref, down_ref, totals_ref, *refs):
    targets, (near, tile, folded) = refs[:groups], refs[groups:]
    rows, snps = near.shape
    half = snps // 2
    pieces = load_packed(up_ref[0 : rows // 2, :], down_ref[0 : rows // 2, :])
    for side in range(2):
        for number in range(3):
            near[side * (rows // 2) : (side + 1) * (rows // 2), number * LANES : (number + 1) * LANES] = pieces[side][number]
    tile[...] = jnp.dot(weighted_ref[...], near[...], preferred_element_type=jnp.float32)
    row, col = iota((half, snps), 0), iota((half, snps), 1)
    moved = (col >= half) & (col - half < row)
    turned = pltpu.roll(tile[0:half, :], half, 1)
    folded[0:half, :] = to_fields(jnp.where(moved, turned, tile[half:snps, :]))
    if folded.shape[0] > half:
        folded[half:, :] = jnp.zeros((folded.shape[0] - half, snps), jnp.int32)
    square = (snps, snps)
    far = jnp.sum(
        jnp.where(iota(square, 0) == iota(square, 1), tile[0:snps, :], 0.0), axis=0, keepdims=True
    )
    extras = to_fields(
        jnp.concatenate(
            [totals_ref[0:2, :], tile[snps : snps + 1, :], far, jnp.zeros((4, snps))], axis=0
        )
    )
    send_shares(groups, folded, share, targets)
    for target in targets:
        target[share:, :] = extras


def annots_kernel(annot_ref, up_ref, down_ref, own_ref, near_ref):
    snps = annot_ref.shape[1]
    part = up_ref.shape[0]
    wide = 2 * part
    own = annot_ref[...].astype(jnp.float32)
    own = jnp.concatenate([own, jnp.zeros((LANES - own.shape[0], snps), jnp.float32)], axis=0)
    own_ref[...] = own.T
    first, second = load_packed(up_ref[...], down_ref[...])
    near = jnp.concatenate(
        [
            jnp.concatenate([piece.astype(jnp.float32) for piece in first], axis=1),
            jnp.concatenate([piece.astype(jnp.float32) for piece in second], axis=1),
            jnp.zeros((LANES - wide, snps), jnp.float32),
        ],
        axis=0,
    )
    near_ref[...] = near.T


def column_stats(totals, count):
    size = jnp.maximum(count, 1.0)
    frequency = totals / size
    variance = jnp.maximum(frequency * (1.0 - frequency), VARIANCE_FLOOR)
    inverse = 1.0 / jnp.sqrt(size * variance)
    low = ((0.0 - frequency) * inverse).astype(jnp.bfloat16).astype(jnp.float32)
    high = ((1.0 - frequency) * inverse).astype(jnp.bfloat16).astype(jnp.float32)
    step = high - low
    root = 1.0 / jnp.sqrt(size)
    return step, step * totals * root, (low * count + step * totals) * root


def correlation(row, col, count):
    return row[0] * col[0] * count - row[1] * col[1] + row[2] * col[2]


def split(values):
    high = values.astype(jnp.bfloat16)
    return high, (values - high.astype(jnp.float32)).astype(jnp.bfloat16)


def dot_split(values, right, axis):
    dims = (((axis,), (0,)), ((), ()))
    return sum(
        lax.dot_general(part, right, dims, preferred_element_type=jnp.float32)
        for part in split(values)
    )


def score_kernel(groups, share, reach_ref, *refs):
    own_parts, near_parts = refs[:groups], refs[groups : 2 * groups]
    annot_ref, near_annot_ref = refs[2 * groups : 2 * groups + 2]
    targets = refs[2 * groups + 2 : 3 * groups + 2]
    table, annots, near_annots, scores = refs[3 * groups + 2 :]
    snps = annot_ref.shape[0]
    half = snps // 2
    out_share = snps // groups
    me = lax.axis_index("hap")
    block = lax.axis_index("snp")
    last = reach_ref.shape[0] - 1
    reach_here = reach_ref[block]
    reach_up = reach_ref[jnp.minimum(block + 1, last)]
    reach_down = reach_ref[jnp.maximum(block - 1, 0)]

    own_counts = sum((part[...] for part in own_parts[1:]), own_parts[0][...])
    near_sums = sum((part[...] for part in near_parts[1:]), near_parts[0][...])
    extras = from_fields(near_sums[share:, :])
    near_counts = near_sums[0:share, :]

    own_stats, near_stats, lines = [], [], []
    for pop in range(2):
        count = extras[pop][1:2, :]
        own_stats.append(column_stats(extras[pop][0:1, :], count))
        near_stats.append(column_stats(extras[pop][2:3, :], count))
        lines += [*own_stats[pop], *near_stats[pop], extras[pop][0:1, :], extras[pop][3:4, :]]
    by_row = jnp.concatenate(lines, axis=0).T
    table[0:snps, 0:16] = by_row
    if table.shape[0] > snps:
        table[snps:, 0:16] = jnp.zeros((table.shape[0] - snps, 16), jnp.float32)
    annots[0:snps, :] = annot_ref[...]
    near_annots[0:snps, :] = near_annot_ref[...]
    if annots.shape[0] > snps:
        annots[snps:, :] = jnp.zeros((annots.shape[0] - snps, LANES), jnp.float32)

    low_rows = pl.multiple_of(me * share, 8)
    high_rows = pl.multiple_of(half + me * share, 8)

    def both(ref):
        return jnp.concatenate([ref[pl.ds(low_rows, share), :], ref[pl.ds(high_rows, share), :]], axis=0)

    here = both(table)
    own_count = jnp.concatenate([pltpu.roll(own_counts, half, 1), own_counts], axis=0)
    near_count = jnp.concatenate([pltpu.roll(near_counts, half, 1), near_counts], axis=0)
    shape = (2 * share, snps)
    local, col = iota(shape, 0), iota(shape, 1)
    low = local < share
    place = jnp.where(low, local, local - share) + me * share
    row = jnp.where(low, place, place + half)
    own_fields, near_fields = from_fields(own_count), from_fields(near_count)
    own_product, near_product = 1.0, 1.0
    for pop in range(2):
        row_stats = [here[:, 8 * pop + k : 8 * pop + k + 1] for k in range(3)]
        own_product *= correlation(row_stats, own_stats[pop], own_fields[pop])
        near_product *= correlation(row_stats, near_stats[pop], near_fields[pop])
    real = place < half
    own_inside = real & ((low & (col > row)) | (~low & (col >= half) & (col < row)))
    own_inside &= jnp.abs(col - row) <= reach_here
    own_kept = jnp.where(own_inside, own_product, 0.0)
    in_upper = col < half
    near_inside = real & ((low & (col < row)) | (~low & (in_upper | (col > row))))
    distance = jnp.where(in_upper, snps + col - row, snps + row - col)
    near_here = jnp.where(near_inside & (distance <= reach_here), near_product, 0.0)
    reach_there = jnp.where(in_upper, reach_up, reach_down)
    near_there = jnp.where(near_inside & (distance <= reach_there), near_product, 0.0)

    rows_here = both(annots)
    rows_there = pltpu.roll(rows_here, HALF_LANES, 1)
    scores[0:snps, :] = dot_split(
        jnp.concatenate([own_kept, near_there], axis=0),
        jnp.concatenate([rows_here, rows_there], axis=0).astype(jnp.bfloat16),
        0,
    )
    direct = dot_split(
        jnp.concatenate([own_kept, near_here], axis=1),
        jnp.concatenate([annot_ref[...], near_annot_ref[...]], axis=0).astype(jnp.bfloat16),
        1,
    )
    scores[pl.ds(low_rows, share), :] += direct[0:share, :]
    scores[pl.ds(high_rows, share), :] += direct[share:, :]

    out_rows = pl.ds(pl.multiple_of(me * out_share, 8), out_share)
    mine = table[out_rows, :]
    self_product, far_product = 1.0, 1.0
    for pop in range(2):
        k = 8 * pop
        own_row = [mine[:, k + s : k + s + 1] for s in range(3)]
        near_row = [mine[:, k + 3 + s : k + 4 + s] for s in range(3)]
        self_product *= correlation(own_row, own_row, mine[:, k + 6 : k + 7])
        far_product *= correlation(own_row, near_row, mine[:, k + 7 : k + 8])
    mine_annots = annots[out_rows, :]
    far_reach = jnp.where(me < groups // 2, reach_up, reach_down)
    scores[out_rows, :] += (
        mine_annots * self_product
        + near_annots[out_rows, :] * jnp.where(reach_here >= snps, far_product, 0.0)
        + pltpu.roll(mine_annots, HALF_LANES, 1) * jnp.where(far_reach >= snps, far_product, 0.0)
    )
    for step, target in enumerate(targets):
        group = lax.rem(me + step, groups)
        target[...] = scores[pl.ds(pl.multiple_of(group * out_share, 8), out_share), :]


def sum_kernel(*refs):
    *parts, out_ref = refs
    out_ref[...] = sum((part[...] for part in parts[1:]), parts[0][...])


def finish_kernel(own_ref, there_ref, out_ref):
    annots = out_ref.shape[0]
    there = pltpu.roll(there_ref[...], HALF_LANES, 1)
    out_ref[...] = (own_ref[...] + there).T[0:annots, :]


def around(value, groups, step):
    return lax.ppermute(
        value, "hap", [(source, (source + step) % groups) for source in range(groups)]
    )


def shifted(value, axis, steps):
    count = lax.axis_size(axis)
    leading, last = (max(0, -steps), min(count, count - steps))
    return lax.ppermute(value, axis, [(source, source + steps) for source in range(leading, last)])


def per_device(haplotypes, labels, annotations, reach):
    rows, snps = haplotypes.shape
    half = snps // 2
    groups = lax.axis_size("hap")
    blocks = lax.axis_size("snp")
    share = round_up(-(-half // groups), 16)
    folded_rows = share * groups
    out_share = snps // groups
    padded = half + folded_rows
    annot_part = 32
    bf16, f32, i32 = jnp.bfloat16, jnp.float32, jnp.int32
    shape = jax.ShapeDtypeStruct

    packed = shape((rows // 2 + annot_part, snps), bf16)
    alleles, up, down = call(
        prepare_kernel,
        [shape((rows, snps), bf16), packed, packed],
        [ANY, VMEM],
        [pltpu.VMEM((rows, snps), i32), pltpu.SemaphoreType.DMA((2 * CHUNKS,))],
        moved=rows * snps * 8,
    )(haplotypes, annotations)
    from_up = shifted(up, "snp", -1)
    from_down = shifted(down, "snp", 1)

    tile = pltpu.VMEM((snps + 16, snps), f32)
    folded = pltpu.VMEM((folded_rows, snps), i32)
    weighted, totals, *own_parts = call(
        functools.partial(own_kernel, groups, share),
        [shape((snps + 16, rows), bf16), shape((8, snps), f32)] + [shape((share, snps), i32)] * groups,
        [VMEM, VMEM],
        [tile, folded],
        flops=2 * rows * snps * snps,
        moved=rows * snps * 4,
    )(alleles, labels.reshape(1, rows))
    own_parts = [own_parts[0]] + [around(own_parts[k], groups, k) for k in range(1, groups)]

    near_parts = call(
        functools.partial(near_kernel, groups, share),
        [shape((share + 8, snps), i32)] * groups,
        [VMEM] * 4,
        [pltpu.VMEM((rows, snps), bf16), tile, folded],
        flops=2 * rows * snps * snps,
        moved=rows * snps * 4,
    )(weighted, from_up, from_down, totals)
    near_parts = [near_parts[0]] + [around(near_parts[k], groups, k) for k in range(1, groups)]

    by_snp = shape((snps, LANES), f32)
    own_annots, near_annots = call(annots_kernel, [by_snp, by_snp], [VMEM] * 3, moved=1 << 20)(
        annotations, from_up[rows // 2 :], from_down[rows // 2 :]
    )
    tall = pltpu.VMEM((padded, LANES), f32)
    scores = call(
        functools.partial(score_kernel, groups, share),
        [shape((out_share, LANES), f32)] * groups,
        [SMEM] + [VMEM] * (2 * groups + 2),
        [tall, tall, tall, tall],
        flops=1 << 26,
        moved=1 << 21,
    )(reach, *own_parts, *near_parts, own_annots, near_annots)
    scores = [scores[0]] + [around(scores[k], groups, k) for k in range(1, groups)]
    summed = call(sum_kernel, shape((out_share, LANES), f32), [VMEM] * groups)(*scores)
    pairs = []
    for block in range(blocks):
        for group in range(groups):
            target = block + 1 if group < groups // 2 else block - 1
            if 0 <= target < blocks:
                pairs.append((block * groups + group, target * groups + group))
    there = lax.ppermute(summed, ("snp", "hap"), pairs)
    return call(finish_kernel, shape((annotations.shape[0], out_share), f32), [VMEM] * 2)(summed, there)


def solution(mesh):
    in_specs = (
        P("hap", ("parts", "snp")),
        P(("parts", "hap")),
        P(None, ("parts", "snp")),
        P("parts"),
    )
    out_specs = P(None, ("parts", "snp", "hap"))
    return jax.shard_map(
        per_device, mesh=mesh, in_specs=in_specs, out_specs=out_specs, check_vma=False
    )
```

time: 198 us -> 50.5 us (0.26)
  waiting for transfers between devices: 145 us -> 13 us
  starting transfers between devices: 7.67 us -> 27 us
  between operations: 13.5 us -> 0.1 us
  matrix products: 10.9 us -> 0 us
  blocking collectives: 10.8 us -> 0 us
  other arithmetic: 7.59 us -> 0 us
  Pallas kernels: 0 us -> 7.3 us
    psum x1 -> x0, waiting for transfers between devices: 128 us -> none  [per_device(): lax.psum(jnp.stack([jnp.einsum('hpj,hk->jpk', masked, piece[:hap_rows], p...]
    ppermute x0 -> x10, starting transfers between devices: none -> 20.6 us  [the longest x9 12 us: around(): lax.ppermute(value, 'hap', [(source, (source + step) % groups) for source...]
    dot_general x5 -> x0, matrix products: 10.9 us -> none  [the longest x3 4.33 us: per_device(): jnp.einsum('hpj,hk->jpk', masked, piece[:hap_rows], preferred_element_typ...]
    psum x1 -> x0, blocking collectives: 10.8 us -> none  [per_device(): lax.psum((jnp.dot(weights, alleles, precision=PRECISE), jnp.sum(weights,...]
    ppermute x2, waiting for transfers between devices: 16.9 us -> 6.67 us  [shifted(): lax.ppermute(value, axis, [(source, source + steps) for source in range(l...]
    pallas_call x0 -> x7, Pallas kernels: none -> 7.3 us  [the longest x1 2.24 us: per_device(): call(prepare_kernel, [shape((rows, snps), bf16), packed, packed], [ANY, V...]
    ppermute x0 -> x10, waiting for transfers between devices: none -> 6.33 us  [the longest x9 5.17 us: around(): lax.ppermute(value, 'hap', [(source, (source + step) % groups) for source...]
    another operation x4 -> x0, other arithmetic: 3.55 us -> none  [the longest x1 2.08 us: per_device(): jnp.stack([jnp.einsum('hpj,hk->jpk', masked, piece[:hap_rows], preferred_...]
  transfers between devices with their start and end apart: 3 -> 12, of which waited for: 3 -> 7; matrix products, arithmetic and copies ran while one was open for 3% -> 0% of each run, Pallas kernels for 0% -> 5%
where the time goes in v2:
time: 50.5 us; the launch traced here: 50.2 us
  starting transfers between devices  27 us (53%)
  waiting for transfers between devices  13 us (26%)
  Pallas kernels  7.3 us (14%)
  local copies, waits for them, and re-layouts  2.79 us (6%)
    ppermute x9, starting transfers between devices, around(): lax.ppermute(value, 'hap', [(source, (source + step) % groups) for source...  12 us
    ppermute x1, starting transfers between devices, per_device(): there = lax.ppermute(summed, ('snp', 'hap'), pairs)  8.6 us
    ppermute x2, waiting for transfers between devices, shifted(): lax.ppermute(value, axis, [(source, source + steps) for source in range(l...  6.67 us
    ppermute x2, starting transfers between devices, shifted(): lax.ppermute(value, axis, [(source, source + steps) for source in range(l...  6.43 us
    ppermute x9, waiting for transfers between devices, around(): lax.ppermute(value, 'hap', [(source, (source + step) % groups) for source...  5.17 us
    unnamed x10, local copies, waits for them, and re-layouts  2.79 us
    pallas_call x1, Pallas kernels, per_device(): call(prepare_kernel, [shape((rows, snps), bf16), packed, packed], [ANY, V...  2.24 us
    pallas_call x1, Pallas kernels, per_device(): call(functools.partial(score_kernel, groups, share), [shape((out_share, L...  1.64 us
  transfers between devices with their start and end apart: 12, of which 7 were waited for; matrix products, arithmetic and copies ran while one was open for 0% of the time, Pallas kernels for 5%

profile of v2, /device:TPU:1, one launch (start us, length us, event | category | flops | bytes accessed | tf_op | source)
XLA Modules:
  0.0 50.2 jit_solution(5061513637932253851)
XLA Ops:
  0.0 0.0 copy-start
  0.0 1.9 %copy-done = s32[2048,384]{1,0:T(8,128)S(1)} copy-done((s32[2048,384]{1,0:T(8,128)S(1)}, s32[2048,384]{1,0:T(8,128)}, u32[]{:S(2)}) %copy-start) | copy-done | bytes 3145752
  1.9 0.0 copy-start.1
  1.9 0.9 %copy-done.1 = s32[50,384]{1,0:T(8,128)S(1)} copy-done((s32[50,384]{1,0:T(8,128)S(1)}, s32[50,384]{1,0:T(8,128)}, u32[]{:S(2)}) %copy-start.1) | copy-done | bytes 76824
  2.8 0.0 copy-start.4
  2.8 2.2 %shard_map.46 = (bf16[2048,384]{1,0:T(8,128)(2,1)S(1)}, bf16[1056,384]{1,0:T(8,128)(2,1)S(1)}, bf16[1056,384]{1,0:T(8,128)(2,1)S(1)}) custom-call(s32[2048,384]{1,0:T(8,128)S(1)} %copy-done, s32[50,384]{1,0:T(8,128)S(1)} %copy-done.1), custom_call_target="tpu_custom_call" | custom-call | bytes 6291456 | tf_op jit(solution)/shard_map/pallas_call | solution.py:356
  5.0 2.0 %collective-permute-start.3 = (bf16[1056,384]{1,0:T(8,128)(2,1)S(1)}, bf16[1056,384]{1,0:T(8,128)(2,1)S(1)}, u32[]{:S(2)}, u32[]{:S(2)}) collective-permute-start(bf16[1056,384]{1,0:T(8,128)(2,1)S(1)} %get-tuple-element.30), channel_id=1, source_target_pairs={{4,0},{8,4},{12,8},{5,1},{9,5},{13,9},{6,2},{10,6},{14,10},{7,3},{... | collective-permute-start | bytes 2433032 | tf_op jit(solution)/shard_map/ppermute | solution.py:339
  7.0 4.5 %collective-permute-start.4 = (bf16[1056,384]{1,0:T(8,128)(2,1)S(1)}, bf16[1056,384]{1,0:T(8,128)(2,1)S(1)}, u32[]{:S(2)}, u32[]{:S(2)}) collective-permute-start(bf16[1056,384]{1,0:T(8,128)(2,1)S(1)} %get-tuple-element.31), channel_id=1, source_target_pairs={{0,4},{4,8},{8,12},{1,5},{5,9},{9,13},{2,6},{6,10},{10,14},{3,7},{... | collective-permute-start | bytes 2433032 | tf_op jit(solution)/shard_map/ppermute | solution.py:339
  11.5 0.0 copy-done.4
  11.5 1.1 %shard_map.47 = (bf16[400,2048]{1,0:T(8,128)(2,1)S(1)}, f32[8,384]{1,0:T(8,128)S(1)}, s32[48,384]{1,0:T(8,128)S(1)}, s32[48,384]{1,0:T(8,128)S(1)}, s32[48,384]{1,0:T(8,128)S(1)}, /*index=5*/s32[48,384]{1,0:T(8,128)S(1)}) custom-call(bf16[2048,384]{1,0:T(8,128)(2,1)S(1)} %get-tuple-element.24.alleles_ref, s32[1,2048]{1,0:T(1,128)S(1)} %bitcast.1), custom_call_target="tpu_custom_call" | custom-call | flops 603979776 | bytes 3145728 | tf_op jit(solution)/shard_map/pallas_call | solution.py:368
  12.6 1.4 %collective-permute-start = (s32[48,384]{1,0:T(8,128)S(1)}, s32[48,384]{1,0:T(8,128)S(1)}, u32[]{:S(2)}, u32[]{:S(2)}) collective-permute-start(s32[48,384]{1,0:T(8,128)S(1)} %get-tuple-element.26), channel_id=1, source_target_pairs={{0,1},{1,2},{2,3},{3,0},{4,5},{5,6},{6,7},{7,4},{8,9},{9,10},{10,1... | collective-permute-start | bytes 221192 | tf_op jit(solution)/shard_map/ppermute | solution.py:331
  14.0 5.5 %collective-permute-done.3.up_ref = bf16[1056,384]{1,0:T(8,128)(2,1)S(1)} collective-permute-done((bf16[1056,384]{1,0:T(8,128)(2,1)S(1)}, bf16[1056,384]{1,0:T(8,128)(2,1)S(1)}, u32[]{:S(2)}, u32[]{:S(2)}) %collective-permute-start.3) | collective-permute-done | bytes 811040 | tf_op jit(solution)/shard_map/ppermute | solution.py:339
  19.5 1.2 %collective-permute-done.4.down_ref = bf16[1056,384]{1,0:T(8,128)(2,1)S(1)} collective-permute-done((bf16[1056,384]{1,0:T(8,128)(2,1)S(1)}, bf16[1056,384]{1,0:T(8,128)(2,1)S(1)}, u32[]{:S(2)}, u32[]{:S(2)}) %collective-permute-start.4) | collective-permute-done | bytes 811040 | tf_op jit(solution)/shard_map/ppermute | solution.py:339
  20.7 0.0 copy-start.2
  20.7 0.0 copy-start.3
  20.7 1.2 %shard_map.48 = (s32[56,384]{1,0:T(8,128)S(1)}, s32[56,384]{1,0:T(8,128)S(1)}, s32[56,384]{1,0:T(8,128)S(1)}, s32[56,384]{1,0:T(8,128)S(1)}) custom-call(bf16[400,2048]{1,0:T(8,128)(2,1)S(1)} %get-tuple-element.29.weighted_ref, bf16[1056,384]{1,0:T(8,128)(2,1)S(1)} %collective-permute-done.3.up_ref, bf16[1056,384]{1,0:T(8,128)(2,1)S(1)} %collective-permute-done.4.down_ref, ...), custom_call_target="tpu_custom_call" | custom-call | flops 603979776 | bytes 3145728 | tf_op jit(solution)/shard_map/pallas_call | solution.py:378
  21.9 1.4 %collective-permute-start.5 = (s32[56,384]{1,0:T(8,128)S(1)}, s32[56,384]{1,0:T(8,128)S(1)}, u32[]{:S(2)}, u32[]{:S(2)}) collective-permute-start(s32[56,384]{1,0:T(8,128)S(1)} %get-tuple-element.34), channel_id=1, source_target_pairs={{0,1},{1,2},{2,3},{3,0},{4,5},{5,6},{6,7},{7,4},{8,9},{9,10},{10,1... | collective-permute-start | bytes 258056 | tf_op jit(solution)/shard_map/ppermute | solution.py:331
  23.3 2.3 %collective-permute-start.6 = (s32[56,384]{1,0:T(8,128)S(1)}, s32[56,384]{1,0:T(8,128)S(1)}, u32[]{:S(2)}, u32[]{:S(2)}) collective-permute-start(s32[56,384]{1,0:T(8,128)S(1)} %get-tuple-element.35), channel_id=1, source_target_pairs={{0,2},{1,3},{2,0},{3,1},{4,6},{5,7},{6,4},{7,5},{8,10},{9,11},{10,... | collective-permute-start | bytes 258056 | tf_op jit(solution)/shard_map/ppermute | solution.py:331
  25.6 1.1 %collective-permute-start.7 = (s32[56,384]{1,0:T(8,128)S(1)}, s32[56,384]{1,0:T(8,128)S(1)}, u32[]{:S(2)}, u32[]{:S(2)}) collective-permute-start(s32[56,384]{1,0:T(8,128)S(1)} %get-tuple-element.36), channel_id=1, source_target_pairs={{0,3},{1,0},{2,1},{3,2},{4,7},{5,4},{6,5},{7,6},{8,11},{9,8},{10,9... | collective-permute-start | bytes 258056 | tf_op jit(solution)/shard_map/ppermute | solution.py:331
  26.6 0.2 collective-permute-start.1
  26.8 0.0 collective-permute-done.refs_1_
  26.8 2.3 %collective-permute-start.2 = (s32[48,384]{1,0:T(8,128)S(1)}, s32[48,384]{1,0:T(8,128)S(1)}, u32[]{:S(2)}, u32[]{:S(2)}) collective-permute-start(s32[48,384]{1,0:T(8,128)S(1)} %get-tuple-element.28), channel_id=1, source_target_pairs={{0,3},{1,0},{2,1},{3,2},{4,7},{5,4},{6,5},{7,6},{8,11},{9,8},{10,9... | collective-permute-start | bytes 221192 | tf_op jit(solution)/shard_map/ppermute | solution.py:331
  29.1 0.0 copy-done.2
  29.1 0.3 shard_map.49
  29.4 2.2 %collective-permute-done.1.refs_2_ = s32[48,384]{1,0:T(8,128)S(1)} collective-permute-done((s32[48,384]{1,0:T(8,128)S(1)}, s32[48,384]{1,0:T(8,128)S(1)}, u32[]{:S(2)}, u32[]{:S(2)}) %collective-permute-start.1) | collective-permute-done | bytes 73760 | tf_op jit(solution)/shard_map/ppermute | solution.py:331
  31.6 0.0 collective-permute-done.2.refs_3_
  31.6 0.0 collective-permute-done.5.refs_5_
  31.6 0.0 collective-permute-done.6.refs_6_
  31.6 0.0 collective-permute-done.7.refs_7_
  31.6 0.0 copy-done.3
  31.7 1.6 %shard_map.50 = (f32[96,128]{1,0:T(8,128)S(1)}, f32[96,128]{1,0:T(8,128)S(1)}, f32[96,128]{1,0:T(8,128)S(1)}, f32[96,128]{1,0:T(8,128)S(1)}) custom-call(s32[4]{0:T(128)S(1)} %copy-done.3, s32[48,384]{1,0:T(8,128)S(1)} %get-tuple-element.25.refs_0_, s32[48,384]{1,0:T(8,128)S(1)} %collective-permute-done.refs_1_, ...), custom_call_target="tpu_custom_call" | custom-call | flops 67108864 | bytes 2097152 | tf_op jit(solution)/shard_map/pallas_call | solution.py:393
  33.3 1.2 %collective-permute-start.8 = (f32[96,128]{1,0:T(8,128)S(1)}, f32[96,128]{1,0:T(8,128)S(1)}, u32[]{:S(2)}, u32[]{:S(2)}) collective-permute-start(f32[96,128]{1,0:T(8,128)S(1)} %get-tuple-element.40), channel_id=1, source_target_pairs={{0,1},{1,2},{2,3},{3,0},{4,5},{5,6},{6,7},{7,4},{8,9},{9,10},{10,1... | collective-permute-start | bytes 147464 | tf_op jit(solution)/shard_map/ppermute | solution.py:331
  34.5 2.3 %collective-permute-start.9 = (f32[96,128]{1,0:T(8,128)S(1)}, f32[96,128]{1,0:T(8,128)S(1)}, u32[]{:S(2)}, u32[]{:S(2)}) collective-permute-start(f32[96,128]{1,0:T(8,128)S(1)} %get-tuple-element.41), channel_id=1, source_target_pairs={{0,2},{1,3},{2,0},{3,1},{4,6},{5,7},{6,4},{7,5},{8,10},{9,11},{10,... | collective-permute-start | bytes 147464 | tf_op jit(solution)/shard_map/ppermute | solution.py:331
  36.7 0.0 collective-permute-start.10
  36.7 1.4 %collective-permute-done.8.refs_1_ = f32[96,128]{1,0:T(8,128)S(1)} collective-permute-done((f32[96,128]{1,0:T(8,128)S(1)}, f32[96,128]{1,0:T(8,128)S(1)}, u32[]{:S(2)}, u32[]{:S(2)}) %collective-permute-start.8) | collective-permute-done | bytes 49184 | tf_op jit(solution)/shard_map/ppermute | solution.py:331
  38.1 1.0 %collective-permute-done.9.refs_2_ = f32[96,128]{1,0:T(8,128)S(1)} collective-permute-done((f32[96,128]{1,0:T(8,128)S(1)}, f32[96,128]{1,0:T(8,128)S(1)}, u32[]{:S(2)}, u32[]{:S(2)}) %collective-permute-start.9) | collective-permute-done | bytes 49184 | tf_op jit(solution)/shard_map/ppermute | solution.py:331
  39.1 0.5 %collective-permute-done.10.refs_3_ = f32[96,128]{1,0:T(8,128)S(1)} collective-permute-done((f32[96,128]{1,0:T(8,128)S(1)}, f32[96,128]{1,0:T(8,128)S(1)}, u32[]{:S(2)}, u32[]{:S(2)}) %collective-permute-start.10) | collective-permute-done | bytes 49184 | tf_op jit(solution)/shard_map/ppermute | solution.py:331
  39.7 8.6 %collective-permute-start.11 = (f32[96,128]{1,0:T(8,128)S(1)}, f32[96,128]{1,0:T(8,128)S(1)}, u32[]{:S(2)}, u32[]{:S(2)}) collective-permute-start(f32[96,128]{1,0:T(8,128)S(1)} %shard_map.51.own_ref), channel_id=1, source_target_pairs={{0,4},{1,5},{4,8},{5,9},{6,2},{7,3},{8,12},{9,13},{10,6},{11,7},{1... | collective-permute-start | bytes 147464 | tf_op jit(solution)/shard_map/ppermute | solution.py:409
  48.3 1.2 %collective-permute-done.11.there_ref = f32[96,128]{1,0:T(8,128)S(1)} collective-permute-done((f32[96,128]{1,0:T(8,128)S(1)}, f32[96,128]{1,0:T(8,128)S(1)}, u32[]{:S(2)}, u32[]{:S(2)}) %collective-permute-start.11) | collective-permute-done | bytes 49184 | tf_op jit(solution)/shard_map/ppermute | solution.py:409
  49.5 0.8 %shard_map.52 = f32[50,96]{1,0:T(8,128)} custom-call(f32[96,128]{1,0:T(8,128)S(1)} %shard_map.51.own_ref, f32[96,128]{1,0:T(8,128)S(1)} %collective-permute-done.11.there_ref), custom_call_target="tpu_custom_call" | custom-call | tf_op jit(solution)/shard_map/pallas_call | solution.py:410
  (3 shorter events, 0.0 us)
Async XLA Ops:
  0.0 1.9 %copy-start = (s32[2048,384]{1,0:T(8,128)S(1)}, s32[2048,384]{1,0:T(8,128)}, u32[]{:S(2)}) copy-start(s32[2048,384]{1,0:T(8,128)} %hap_ref.1) | copy-start | bytes 9437188
  1.9 0.9 %copy-start.1 = (s32[50,384]{1,0:T(8,128)S(1)}, s32[50,384]{1,0:T(8,128)}, u32[]{:S(2)}) copy-start(s32[50,384]{1,0:T(8,128)} %annot_ref.3) | copy-start | bytes 230404
  2.8 8.7 %copy-start.4 = (s32[2048]{0:T(1024)S(1)}, s32[2048]{0:T(1024)}, u32[]{:S(2)}) copy-start(s32[2048]{0:T(1024)} %param.5) | copy-start | bytes 24580
  5.0 14.4 %collective-permute-start.3 = (bf16[1056,384]{1,0:T(8,128)(2,1)S(1)}, bf16[1056,384]{1,0:T(8,128)(2,1)S(1)}, u32[]{:S(2)}, u32[]{:S(2)}) collective-permute-start(bf16[1056,384]{1,0:T(8,128)(2,1)S(1)} %get-tuple-element.30), channel_id=1, source_target_pairs={{4,0},{8,4},{12,8},{5,1},{9,5},{13,9},{6,2},{10,6},{14,10},{7,3},{... | collective-permute-start | bytes 2433032 | tf_op jit(solution)/shard_map/ppermute | solution.py:339
  7.0 13.6 %collective-permute-start.4 = (bf16[1056,384]{1,0:T(8,128)(2,1)S(1)}, bf16[1056,384]{1,0:T(8,128)(2,1)S(1)}, u32[]{:S(2)}, u32[]{:S(2)}) collective-permute-start(bf16[1056,384]{1,0:T(8,128)(2,1)S(1)} %get-tuple-element.31), channel_id=1, source_target_pairs={{0,4},{4,8},{8,12},{1,5},{5,9},{9,13},{2,6},{6,10},{10,14},{3,7},{... | collective-permute-start | bytes 2433032 | tf_op jit(solution)/shard_map/ppermute | solution.py:339
  12.6 14.2 %collective-permute-start = (s32[48,384]{1,0:T(8,128)S(1)}, s32[48,384]{1,0:T(8,128)S(1)}, u32[]{:S(2)}, u32[]{:S(2)}) collective-permute-start(s32[48,384]{1,0:T(8,128)S(1)} %get-tuple-element.26), channel_id=1, source_target_pairs={{0,1},{1,2},{2,3},{3,0},{4,5},{5,6},{6,7},{7,4},{8,9},{9,10},{10,1... | collective-permute-start | bytes 221192 | tf_op jit(solution)/shard_map/ppermute | solution.py:331
  20.7 8.5 %copy-start.2 = (s32[50,384]{1,0:T(8,128)S(1)}, s32[50,384]{1,0:T(8,128)}, u32[]{:S(2)}) copy-start(s32[50,384]{1,0:T(8,128)} %annot_ref.3) | copy-start | bytes 230404
  20.7 11.0 %copy-start.3 = (s32[4]{0:T(128)S(1)}, s32[4]{0:T(128)}, u32[]{:S(2)}) copy-start(s32[4]{0:T(128)} %reach_ref.1) | copy-start | bytes 52
  21.9 9.7 %collective-permute-start.5 = (s32[56,384]{1,0:T(8,128)S(1)}, s32[56,384]{1,0:T(8,128)S(1)}, u32[]{:S(2)}, u32[]{:S(2)}) collective-permute-start(s32[56,384]{1,0:T(8,128)S(1)} %get-tuple-element.34), channel_id=1, source_target_pairs={{0,1},{1,2},{2,3},{3,0},{4,5},{5,6},{6,7},{7,4},{8,9},{9,10},{10,1... | collective-permute-start | bytes 258056 | tf_op jit(solution)/shard_map/ppermute | solution.py:331
  23.3 8.4 %collective-permute-start.6 = (s32[56,384]{1,0:T(8,128)S(1)}, s32[56,384]{1,0:T(8,128)S(1)}, u32[]{:S(2)}, u32[]{:S(2)}) collective-permute-start(s32[56,384]{1,0:T(8,128)S(1)} %get-tuple-element.35), channel_id=1, source_target_pairs={{0,2},{1,3},{2,0},{3,1},{4,6},{5,7},{6,4},{7,5},{8,10},{9,11},{10,... | collective-permute-start | bytes 258056 | tf_op jit(solution)/shard_map/ppermute | solution.py:331
  25.6 6.1 %collective-permute-start.7 = (s32[56,384]{1,0:T(8,128)S(1)}, s32[56,384]{1,0:T(8,128)S(1)}, u32[]{:S(2)}, u32[]{:S(2)}) collective-permute-start(s32[56,384]{1,0:T(8,128)S(1)} %get-tuple-element.36), channel_id=1, source_target_pairs={{0,3},{1,0},{2,1},{3,2},{4,7},{5,4},{6,5},{7,6},{8,11},{9,8},{10,9... | collective-permute-start | bytes 258056 | tf_op jit(solution)/shard_map/ppermute | solution.py:331
  26.6 5.0 %collective-permute-start.1 = (s32[48,384]{1,0:T(8,128)S(1)}, s32[48,384]{1,0:T(8,128)S(1)}, u32[]{:S(2)}, u32[]{:S(2)}) collective-permute-start(s32[48,384]{1,0:T(8,128)S(1)} %get-tuple-element.27), channel_id=1, source_target_pairs={{0,2},{1,3},{2,0},{3,1},{4,6},{5,7},{6,4},{7,5},{8,10},{9,11},{10,... | collective-permute-start | bytes 221192 | tf_op jit(solution)/shard_map/ppermute | solution.py:331
  26.8 4.8 %collective-permute-start.2 = (s32[48,384]{1,0:T(8,128)S(1)}, s32[48,384]{1,0:T(8,128)S(1)}, u32[]{:S(2)}, u32[]{:S(2)}) collective-permute-start(s32[48,384]{1,0:T(8,128)S(1)} %get-tuple-element.28), channel_id=1, source_target_pairs={{0,3},{1,0},{2,1},{3,2},{4,7},{5,4},{6,5},{7,6},{8,11},{9,8},{10,9... | collective-permute-start | bytes 221192 | tf_op jit(solution)/shard_map/ppermute | solution.py:331
  33.3 4.8 %collective-permute-start.8 = (f32[96,128]{1,0:T(8,128)S(1)}, f32[96,128]{1,0:T(8,128)S(1)}, u32[]{:S(2)}, u32[]{:S(2)}) collective-permute-start(f32[96,128]{1,0:T(8,128)S(1)} %get-tuple-element.40), channel_id=1, source_target_pairs={{0,1},{1,2},{2,3},{3,0},{4,5},{5,6},{6,7},{7,4},{8,9},{9,10},{10,1... | collective-permute-start | bytes 147464 | tf_op jit(solution)/shard_map/ppermute | solution.py:331
  34.5 4.7 %collective-permute-start.9 = (f32[96,128]{1,0:T(8,128)S(1)}, f32[96,128]{1,0:T(8,128)S(1)}, u32[]{:S(2)}, u32[]{:S(2)}) collective-permute-start(f32[96,128]{1,0:T(8,128)S(1)} %get-tuple-element.41), channel_id=1, source_target_pairs={{0,2},{1,3},{2,0},{3,1},{4,6},{5,7},{6,4},{7,5},{8,10},{9,11},{10,... | collective-permute-start | bytes 147464 | tf_op jit(solution)/shard_map/ppermute | solution.py:331
  36.7 2.9 %collective-permute-start.10 = (f32[96,128]{1,0:T(8,128)S(1)}, f32[96,128]{1,0:T(8,128)S(1)}, u32[]{:S(2)}, u32[]{:S(2)}) collective-permute-start(f32[96,128]{1,0:T(8,128)S(1)} %get-tuple-element.42), channel_id=1, source_target_pairs={{0,3},{1,0},{2,1},{3,2},{4,7},{5,4},{6,5},{7,6},{8,11},{9,8},{10,9... | collective-permute-start | bytes 147464 | tf_op jit(solution)/shard_map/ppermute | solution.py:331
  39.7 9.8 %collective-permute-start.11 = (f32[96,128]{1,0:T(8,128)S(1)}, f32[96,128]{1,0:T(8,128)S(1)}, u32[]{:S(2)}, u32[]{:S(2)}) collective-permute-start(f32[96,128]{1,0:T(8,128)S(1)} %shard_map.51.own_ref), channel_id=1, source_target_pairs={{0,4},{1,5},{4,8},{5,9},{6,2},{7,3},{8,12},{9,13},{10,6},{11,7},{1... | collective-permute-start | bytes 147464 | tf_op jit(solution)/shard_map/ppermute | solution.py:409

commit v3 on v2

--- a/solution.py
+++ b/solution.py
@@ -16,7 +16,7 @@
 CHUNKS = 4
 VMEM = pl.BlockSpec(memory_space=pltpu.VMEM)
 SMEM = pl.BlockSpec(memory_space=pltpu.SMEM)
-ANY = pl.BlockSpec(memory_space=pl.ANY)
+HBM = pl.BlockSpec(memory_space=pltpu.HBM)
 VMEM_LIMIT = 24 * 1024 * 1024
 
 
@@ -50,6 +50,10 @@
         compiler_params=pltpu.CompilerParams(vmem_limit_bytes=VMEM_LIMIT),
         cost_estimate=pl.CostEstimate(flops=flops, bytes_accessed=moved, transcendentals=0),
     )
+
+
+def odd_block():
+    return lax.rem(lax.axis_index("snp"), 2) == 1
 
 
 def store_packed(up_ref, down_ref, where, first, second):
@@ -69,16 +73,17 @@
     left = iota((up.shape[0], LANES), 1) < HALF_LANES
     up_mixed, down_mixed = up[:, 2 * LANES :], down[:, 2 * LANES :]
     first = jnp.where(left, up_mixed, down_mixed)
-    second = jnp.where(left, down_mixed, up_mixed).astype(jnp.float32)
-    second = pltpu.roll(second, HALF_LANES, 1).astype(jnp.bfloat16)
+    second = jnp.where(left, down_mixed, up_mixed)
+    second = pltpu.roll(second.astype(jnp.float32), HALF_LANES, 1).astype(second.dtype)
     return (
         (up[:, :LANES], first, down[:, :LANES]),
         (up[:, LANES : 2 * LANES], second, down[:, LANES : 2 * LANES]),
     )
 
 
-def prepare_kernel(hap_ref, annot_ref, alleles_ref, up_ref, down_ref, held, sems):
+def prepare_kernel(hap_ref, annot_ref, alleles_ref, far_ref, close_ref, held, held_annots, sems):
     rows = hap_ref.shape[0]
+    annot_rows = annot_ref.shape[0]
     size = rows // (2 * CHUNKS)
     starts = [side * (rows // 2) + chunk * size for chunk in range(CHUNKS) for side in range(2)]
     copies = [
@@ -87,14 +92,21 @@
         )
         for number, start in enumerate(starts)
     ]
+    copies.append(pltpu.make_async_copy(annot_ref, held_annots, sems.at[2 * CHUNKS]))
     for copy in copies:
         copy.start()
-    annots = annot_ref[...].astype(jnp.float32)
-    part = (up_ref.shape[0] - rows // 2)
-    annots = jnp.concatenate(
-        [annots, jnp.zeros((2 * part - annots.shape[0], annots.shape[1]), jnp.float32)], axis=0
-    )
-    store_packed(up_ref, down_ref, slice(rows // 2, rows // 2 + part), annots[:part], annots[part:])
+    part = far_ref.shape[0] - rows // 2
+    odd = odd_block()
+
+    def store(where, first, second):
+        @pl.when(odd)
+        def _():
+            store_packed(close_ref, far_ref, where, first, second)
+
+        @pl.when(jnp.logical_not(odd))
+        def _():
+            store_packed(far_ref, close_ref, where, first, second)
+
     for chunk in range(CHUNKS):
         pair = []
         for side in range(2):
@@ -104,7 +116,16 @@
             values = held[where, :].astype(jnp.float32)
             alleles_ref[where, :] = values.astype(jnp.bfloat16)
             pair.append(values)
-        store_packed(up_ref, down_ref, slice(chunk * size, (chunk + 1) * size), *pair)
+        store(slice(chunk * size, (chunk + 1) * size), *pair)
+    copies[-1].wait()
+    annots = jnp.concatenate(
+        [
+            held_annots[...].astype(jnp.float32),
+            jnp.zeros((2 * part - annot_rows, annot_ref.shape[1]), jnp.float32),
+        ],
+        axis=0,
+    )
+    store(slice(rows // 2, rows // 2 + part), annots[:part], annots[part:])
 
 
 def send_shares(groups, source, share, targets):
@@ -137,14 +158,28 @@
     send_shares(groups, folded, share, targets)
 
 
-def near_kernel(groups, share, weighted_ref, up_ref, down_ref, totals_ref, *refs):
-    targets, (near, tile, folded) = refs[:groups], refs[groups:]
+def near_kernel(groups, share, weighted_ref, far_ref, close_ref, totals_ref, *refs):
+    own_parts, own_sum_ref = refs[:groups], refs[groups]
+    targets, (near, tile, folded) = refs[groups + 1 : 2 * groups + 1], refs[2 * groups + 1 :]
     rows, snps = near.shape
     half = snps // 2
-    pieces = load_packed(up_ref[0 : rows // 2, :], down_ref[0 : rows // 2, :])
-    for side in range(2):
-        for number in range(3):
-            near[side * (rows // 2) : (side + 1) * (rows // 2), number * LANES : (number + 1) * LANES] = pieces[side][number]
+    odd = odd_block()
+
+    def unpack(up_ref, down_ref):
+        pieces = load_packed(up_ref[0 : rows // 2, :], down_ref[0 : rows // 2, :])
+        for side in range(2):
+            where = slice(side * (rows // 2), (side + 1) * (rows // 2))
+            for number in range(3):
+                near[where, number * LANES : (number + 1) * LANES] = pieces[side][number]
+
+    @pl.when(odd)
+    def _():
+        unpack(far_ref, close_ref)
+
+    @pl.when(jnp.logical_not(odd))
+    def _():
+        unpack(close_ref, far_ref)
+
     tile[...] = jnp.dot(weighted_ref[...], near[...], preferred_element_type=jnp.float32)
     row, col = iota((half, snps), 0), iota((half, snps), 1)
     moved = (col >= half) & (col - half < row)
@@ -164,16 +199,19 @@
     send_shares(groups, folded, share, targets)
     for target in targets:
         target[share:, :] = extras
-
-
-def annots_kernel(annot_ref, up_ref, down_ref, own_ref, near_ref):
+    own_sum_ref[...] = sum((part[...] for part in own_parts[1:]), own_parts[0][...])
+
+
+def annots_kernel(annot_ref, far_ref, close_ref, own_ref, near_ref):
     snps = annot_ref.shape[1]
-    part = up_ref.shape[0]
+    part = far_ref.shape[0]
     wide = 2 * part
     own = annot_ref[...].astype(jnp.float32)
     own = jnp.concatenate([own, jnp.zeros((LANES - own.shape[0], snps), jnp.float32)], axis=0)
     own_ref[...] = own.T
-    first, second = load_packed(up_ref[...], down_ref[...])
+    odd = odd_block()
+    far, close = far_ref[...].astype(jnp.float32), close_ref[...].astype(jnp.float32)
+    first, second = load_packed(jnp.where(odd, far, close), jnp.where(odd, close, far))
     near = jnp.concatenate(
         [
             jnp.concatenate([piece.astype(jnp.float32) for piece in first], axis=1),
@@ -215,10 +253,10 @@
 
 
 def score_kernel(groups, share, reach_ref, *refs):
-    own_parts, near_parts = refs[:groups], refs[groups : 2 * groups]
-    annot_ref, near_annot_ref = refs[2 * groups : 2 * groups + 2]
-    targets = refs[2 * groups + 2 : 3 * groups + 2]
-    table, annots, near_annots, scores = refs[3 * groups + 2 :]
+    own_sum_ref, near_parts = refs[0], refs[1 : groups + 1]
+    annot_ref, near_annot_ref = refs[groups + 1 : groups + 3]
+    targets = refs[groups + 3 : 2 * groups + 3]
+    table, annots, near_annots, scores = refs[2 * groups + 3 :]
     snps = annot_ref.shape[0]
     half = snps // 2
     out_share = snps // groups
@@ -229,7 +267,7 @@
     reach_up = reach_ref[jnp.minimum(block + 1, last)]
     reach_down = reach_ref[jnp.maximum(block - 1, 0)]
 
-    own_counts = sum((part[...] for part in own_parts[1:]), own_parts[0][...])
+    own_counts = own_sum_ref[...]
     near_sums = sum((part[...] for part in near_parts[1:]), near_parts[0][...])
     extras = from_fields(near_sums[share:, :])
     near_counts = near_sums[0:share, :]
@@ -333,10 +371,11 @@
     )
 
 
-def shifted(value, axis, steps):
-    count = lax.axis_size(axis)
-    leading, last = (max(0, -steps), min(count, count - steps))
-    return lax.ppermute(value, axis, [(source, source + steps) for source in range(leading, last)])
+def swapped(value, first):
+    pairs = []
+    for block in range(first, lax.axis_size("snp") - 1, 2):
+        pairs += [(block, block + 1), (block + 1, block)]
+    return lax.ppermute(value, "snp", pairs)
 
 
 def per_device(haplotypes, labels, annotations, reach):
@@ -353,15 +392,21 @@
     shape = jax.ShapeDtypeStruct
 
     packed = shape((rows // 2 + annot_part, snps), bf16)
-    alleles, up, down = call(
+    haplotypes = pltpu.with_memory_space_constraint(haplotypes, pltpu.HBM)
+    annots_in = pltpu.with_memory_space_constraint(annotations, pltpu.HBM)
+    alleles, far, close = call(
         prepare_kernel,
         [shape((rows, snps), bf16), packed, packed],
-        [ANY, VMEM],
-        [pltpu.VMEM((rows, snps), i32), pltpu.SemaphoreType.DMA((2 * CHUNKS,))],
+        [HBM, HBM],
+        [
+            pltpu.VMEM((rows, snps), i32),
+            pltpu.VMEM(annotations.shape, i32),
+            pltpu.SemaphoreType.DMA((2 * CHUNKS + 1,)),
+        ],
         moved=rows * snps * 8,
-    )(haplotypes, annotations)
-    from_up = shifted(up, "snp", -1)
-    from_down = shifted(down, "snp", 1)
+    )(haplotypes, annots_in)
+    from_far = swapped(far, 1)
+    from_close = swapped(close, 0)
 
     tile = pltpu.VMEM((snps + 16, snps), f32)
     folded = pltpu.VMEM((folded_rows, snps), i32)
@@ -375,29 +420,29 @@
     )(alleles, labels.reshape(1, rows))
     own_parts = [own_parts[0]] + [around(own_parts[k], groups, k) for k in range(1, groups)]
 
-    near_parts = call(
+    own_sum, *near_parts = call(
         functools.partial(near_kernel, groups, share),
-        [shape((share + 8, snps), i32)] * groups,
-        [VMEM] * 4,
+        [shape((share, snps), i32)] + [shape((share + 8, snps), i32)] * groups,
+        [VMEM] * (4 + groups),
         [pltpu.VMEM((rows, snps), bf16), tile, folded],
         flops=2 * rows * snps * snps,
         moved=rows * snps * 4,
-    )(weighted, from_up, from_down, totals)
+    )(weighted, from_far, from_close, totals, *own_parts)
     near_parts = [near_parts[0]] + [around(near_parts[k], groups, k) for k in range(1, groups)]
 
     by_snp = shape((snps, LANES), f32)
     own_annots, near_annots = call(annots_kernel, [by_snp, by_snp], [VMEM] * 3, moved=1 << 20)(
-        annotations, from_up[rows // 2 :], from_down[rows // 2 :]
+        annotations, from_far[rows // 2 :], from_close[rows // 2 :]
     )
     tall = pltpu.VMEM((padded, LANES), f32)
     scores = call(
         functools.partial(score_kernel, groups, share),
         [shape((out_share, LANES), f32)] * groups,
-        [SMEM] + [VMEM] * (2 * groups + 2),
+        [SMEM] + [VMEM] * (groups + 3),
         [tall, tall, tall, tall],
         flops=1 << 26,
         moved=1 << 21,
-    )(reach, *own_parts, *near_parts, own_annots, near_annots)
+    )(reach, own_sum, *near_parts, own_annots, near_annots)
     scores = [scores[0]] + [around(scores[k], groups, k) for k in range(1, groups)]
     summed = call(sum_kernel, shape((out_share, LANES), f32), [VMEM] * groups)(*scores)
     pairs = []

time: 50.5 us -> 43.5 us (0.86)
  starting transfers between devices: 27 us -> 20.7 us
  local copies, waits for them, and re-layouts: 2.79 us -> 0.02 us
  waiting for transfers between devices: 13 us -> 15.1 us
    ppermute x9, waiting for transfers between devices: 5.17 us -> 13.9 us  [around(): lax.ppermute(value, 'hap', [(source, (source + step) % groups) for source...]
    ppermute x2, waiting for transfers between devices: 6.67 us -> 0.01 us  [swapped(): return lax.ppermute(value, 'snp', pairs)]
    ppermute x1, starting transfers between devices: 8.6 us -> 2.98 us  [per_device(): there = lax.ppermute(summed, ('snp', 'hap'), pairs)]
    unnamed x10 -> x6, local copies, waits for them, and re-layouts: 2.79 us -> 0.02 us
    ppermute x2, starting transfers between devices: 6.43 us -> 4.58 us  [swapped(): return lax.ppermute(value, 'snp', pairs)]
    ppermute x9, starting transfers between devices: 12 us -> 13.2 us  [around(): lax.ppermute(value, 'hap', [(source, (source + step) % groups) for source...]
  transfers between devices with their start and end apart: 12 -> 12, of which waited for: 7 -> 7; matrix products, arithmetic and copies ran while one was open for 0% -> 0% of each run, Pallas kernels for 5% -> 3%
where the time goes in v3:
time: 43.5 us; the launch traced here: 43.3 us
  starting transfers between devices  20.7 us (48%)
  waiting for transfers between devices  15.1 us (35%)
  Pallas kernels  7.37 us (17%)
    ppermute x9, waiting for transfers between devices, around(): lax.ppermute(value, 'hap', [(source, (source + step) % groups) for source...  13.9 us
    ppermute x9, starting transfers between devices, around(): lax.ppermute(value, 'hap', [(source, (source + step) % groups) for source...  13.2 us
    ppermute x2, starting transfers between devices, swapped(): return lax.ppermute(value, 'snp', pairs)  4.58 us
    ppermute x1, starting transfers between devices, per_device(): there = lax.ppermute(summed, ('snp', 'hap'), pairs)  2.98 us
    pallas_call x1, Pallas kernels, per_device(): call(prepare_kernel, [shape((rows, snps), bf16), packed, packed], [HBM, H...  2.14 us
    pallas_call x1, Pallas kernels, per_device(): call(functools.partial(score_kernel, groups, share), [shape((out_share, L...  1.64 us
    pallas_call x1, Pallas kernels, per_device(): call(functools.partial(near_kernel, groups, share), [shape((share, snps),...  1.41 us
    ppermute x1, waiting for transfers between devices, per_device(): there = lax.ppermute(summed, ('snp', 'hap'), pairs)  1.16 us
  transfers between devices with their start and end apart: 12, of which 7 were waited for; matrix products, arithmetic and copies ran while one was open for 0% of the time, Pallas kernels for 3%

profile of v3, /device:TPU:1, one launch (start us, length us, event | category | flops | bytes accessed | tf_op | source)
XLA Modules:
  0.0 43.3 jit_solution(4897708521435852228)
XLA Ops:
  0.0 0.0 copy-start.2
  0.0 2.1 %shard_map.46 = (bf16[2048,384]{1,0:T(8,128)(2,1)S(1)}, bf16[1056,384]{1,0:T(8,128)(2,1)S(1)}, bf16[1056,384]{1,0:T(8,128)(2,1)S(1)}) custom-call(s32[2048,384]{1,0:T(8,128)} %hap_ref.1, s32[50,384]{1,0:T(8,128)} %annot_ref.3), custom_call_target="tpu_custom_call" | custom-call | bytes 6291456 | tf_op jit(solution)/shard_map/pallas_call | solution.py:397
  2.1 4.5 %collective-permute-start = (bf16[1056,384]{1,0:T(8,128)(2,1)S(1)}, bf16[1056,384]{1,0:T(8,128)(2,1)S(1)}, u32[]{:S(2)}, u32[]{:S(2)}) collective-permute-start(bf16[1056,384]{1,0:T(8,128)(2,1)S(1)} %get-tuple-element.27), channel_id=1, source_target_pairs={{4,8},{8,4},{5,9},{9,5},{6,10},{10,6},{7,11},{11,7},{20,24},{24,20... | collective-permute-start | bytes 2433032 | tf_op jit(solution)/shard_map/ppermute | solution.py:378
  6.7 0.1 collective-permute-start.1
  6.7 0.0 copy-done.2
  6.8 1.1 %shard_map.47 = (bf16[400,2048]{1,0:T(8,128)(2,1)S(1)}, f32[8,384]{1,0:T(8,128)S(1)}, s32[48,384]{1,0:T(8,128)S(1)}, s32[48,384]{1,0:T(8,128)S(1)}, s32[48,384]{1,0:T(8,128)S(1)}, /*index=5*/s32[48,384]{1,0:T(8,128)S(1)}) custom-call(bf16[2048,384]{1,0:T(8,128)(2,1)S(1)} %get-tuple-element.25.alleles_ref, s32[1,2048]{1,0:T(1,128)S(1)} %bitcast.1), custom_call_target="tpu_custom_call" | custom-call | flops 603979776 | bytes 3145728 | tf_op jit(solution)/shard_map/pallas_call | solution.py:413
  7.9 1.4 %collective-permute-start.2 = (s32[48,384]{1,0:T(8,128)S(1)}, s32[48,384]{1,0:T(8,128)S(1)}, u32[]{:S(2)}, u32[]{:S(2)}) collective-permute-start(s32[48,384]{1,0:T(8,128)S(1)} %get-tuple-element.31), channel_id=1, source_target_pairs={{0,1},{1,2},{2,3},{3,0},{4,5},{5,6},{6,7},{7,4},{8,9},{9,10},{10,1... | collective-permute-start | bytes 221192 | tf_op jit(solution)/shard_map/ppermute | solution.py:369
  9.2 2.3 %collective-permute-start.3 = (s32[48,384]{1,0:T(8,128)S(1)}, s32[48,384]{1,0:T(8,128)S(1)}, u32[]{:S(2)}, u32[]{:S(2)}) collective-permute-start(s32[48,384]{1,0:T(8,128)S(1)} %get-tuple-element.32), channel_id=1, source_target_pairs={{0,2},{1,3},{2,0},{3,1},{4,6},{5,7},{6,4},{7,5},{8,10},{9,11},{10,... | collective-permute-start | bytes 221192 | tf_op jit(solution)/shard_map/ppermute | solution.py:369
  11.6 1.1 %collective-permute-start.4 = (s32[48,384]{1,0:T(8,128)S(1)}, s32[48,384]{1,0:T(8,128)S(1)}, u32[]{:S(2)}, u32[]{:S(2)}) collective-permute-start(s32[48,384]{1,0:T(8,128)S(1)} %get-tuple-element.33), channel_id=1, source_target_pairs={{0,3},{1,0},{2,1},{3,2},{4,7},{5,4},{6,5},{7,6},{8,11},{9,8},{10,9... | collective-permute-start | bytes 221192 | tf_op jit(solution)/shard_map/ppermute | solution.py:369
  12.6 0.4 %collective-permute-done.2.refs_1_ = s32[48,384]{1,0:T(8,128)S(1)} collective-permute-done((s32[48,384]{1,0:T(8,128)S(1)}, s32[48,384]{1,0:T(8,128)S(1)}, u32[]{:S(2)}, u32[]{:S(2)}) %collective-permute-start.2) | collective-permute-done | bytes 73760 | tf_op jit(solution)/shard_map/ppermute | solution.py:369
  13.1 4.1 %collective-permute-done.3.refs_2_ = s32[48,384]{1,0:T(8,128)S(1)} collective-permute-done((s32[48,384]{1,0:T(8,128)S(1)}, s32[48,384]{1,0:T(8,128)S(1)}, u32[]{:S(2)}, u32[]{:S(2)}) %collective-permute-start.3) | collective-permute-done | bytes 73760 | tf_op jit(solution)/shard_map/ppermute | solution.py:369
  17.2 0.0 collective-permute-done.4.refs_3_
  17.2 0.0 collective-permute-done.far_ref
  17.2 0.0 collective-permute-done.1.close_ref
  17.2 0.0 copy-start
  17.2 0.0 copy-start.1
  17.2 1.4 %shard_map.48 = (s32[48,384]{1,0:T(8,128)S(1)}, s32[56,384]{1,0:T(8,128)S(1)}, s32[56,384]{1,0:T(8,128)S(1)}, s32[56,384]{1,0:T(8,128)S(1)}, s32[56,384]{1,0:T(8,128)S(1)}) custom-call(bf16[400,2048]{1,0:T(8,128)(2,1)S(1)} %get-tuple-element.26.weighted_ref, bf16[1056,384]{1,0:T(8,128)(2,1)S(1)} %collective-permute-done.far_ref, ...), custom_call_target="tpu_custom_call" | custom-call | flops 603979776 | bytes 3145728 | tf_op jit(solution)/shard_map/pallas_call | solution.py:423
  18.6 1.9 %collective-permute-start.5 = (s32[56,384]{1,0:T(8,128)S(1)}, s32[56,384]{1,0:T(8,128)S(1)}, u32[]{:S(2)}, u32[]{:S(2)}) collective-permute-start(s32[56,384]{1,0:T(8,128)S(1)} %get-tuple-element.36), channel_id=1, source_target_pairs={{0,1},{1,2},{2,3},{3,0},{4,5},{5,6},{6,7},{7,4},{8,9},{9,10},{10,1... | collective-permute-start | bytes 258056 | tf_op jit(solution)/shard_map/ppermute | solution.py:369
  20.5 1.4 %collective-permute-start.6 = (s32[56,384]{1,0:T(8,128)S(1)}, s32[56,384]{1,0:T(8,128)S(1)}, u32[]{:S(2)}, u32[]{:S(2)}) collective-permute-start(s32[56,384]{1,0:T(8,128)S(1)} %get-tuple-element.37), channel_id=1, source_target_pairs={{0,2},{1,3},{2,0},{3,1},{4,6},{5,7},{6,4},{7,5},{8,10},{9,11},{10,... | collective-permute-start | bytes 258056 | tf_op jit(solution)/shard_map/ppermute | solution.py:369
  22.0 0.8 %collective-permute-start.7 = (s32[56,384]{1,0:T(8,128)S(1)}, s32[56,384]{1,0:T(8,128)S(1)}, u32[]{:S(2)}, u32[]{:S(2)}) collective-permute-start(s32[56,384]{1,0:T(8,128)S(1)} %get-tuple-element.38), channel_id=1, source_target_pairs={{0,3},{1,0},{2,1},{3,2},{4,7},{5,4},{6,5},{7,6},{8,11},{9,8},{10,9... | collective-permute-start | bytes 258056 | tf_op jit(solution)/shard_map/ppermute | solution.py:369
  22.7 0.0 copy-done
  22.7 0.3 shard_map.49
  23.0 0.8 %collective-permute-done.5.refs_2_ = s32[56,384]{1,0:T(8,128)S(1)} collective-permute-done((s32[56,384]{1,0:T(8,128)S(1)}, s32[56,384]{1,0:T(8,128)S(1)}, u32[]{:S(2)}, u32[]{:S(2)}) %collective-permute-start.5) | collective-permute-done | bytes 86048 | tf_op jit(solution)/shard_map/ppermute | solution.py:369
  23.8 4.8 %collective-permute-done.6.refs_3_ = s32[56,384]{1,0:T(8,128)S(1)} collective-permute-done((s32[56,384]{1,0:T(8,128)S(1)}, s32[56,384]{1,0:T(8,128)S(1)}, u32[]{:S(2)}, u32[]{:S(2)}) %collective-permute-start.6) | collective-permute-done | bytes 86048 | tf_op jit(solution)/shard_map/ppermute | solution.py:369
  28.6 0.0 collective-permute-done.7.refs_4_
  28.6 0.0 copy-done.1
  28.6 1.6 %shard_map.50 = (f32[96,128]{1,0:T(8,128)S(1)}, f32[96,128]{1,0:T(8,128)S(1)}, f32[96,128]{1,0:T(8,128)S(1)}, f32[96,128]{1,0:T(8,128)S(1)}) custom-call(s32[4]{0:T(128)S(1)} %copy-done.1, s32[48,384]{1,0:T(8,128)S(1)} %get-tuple-element.34.refs_0_, s32[56,384]{1,0:T(8,128)S(1)} %get-tuple-element.35.refs_1_, s32[56,384]{1,0:T(8,128)S(1)} %collective-permute-done.5.refs_2_, ...), custom_call_target="tpu_custom_call" | custom-call | flops 67108864 | bytes 2097152 | tf_op jit(solution)/shard_map/pallas_call | solution.py:438
  30.3 2.2 %collective-permute-start.8 = (f32[96,128]{1,0:T(8,128)S(1)}, f32[96,128]{1,0:T(8,128)S(1)}, u32[]{:S(2)}, u32[]{:S(2)}) collective-permute-start(f32[96,128]{1,0:T(8,128)S(1)} %get-tuple-element.42), channel_id=1, source_target_pairs={{0,1},{1,2},{2,3},{3,0},{4,5},{5,6},{6,7},{7,4},{8,9},{9,10},{10,1... | collective-permute-start | bytes 147464 | tf_op jit(solution)/shard_map/ppermute | solution.py:369
  32.4 0.0 collective-permute-start.9
  32.4 2.2 %collective-permute-start.10 = (f32[96,128]{1,0:T(8,128)S(1)}, f32[96,128]{1,0:T(8,128)S(1)}, u32[]{:S(2)}, u32[]{:S(2)}) collective-permute-start(f32[96,128]{1,0:T(8,128)S(1)} %get-tuple-element.44), channel_id=1, source_target_pairs={{0,3},{1,0},{2,1},{3,2},{4,7},{5,4},{6,5},{7,6},{8,11},{9,8},{10,9... | collective-permute-start | bytes 147464 | tf_op jit(solution)/shard_map/ppermute | solution.py:369
  34.6 0.5 %collective-permute-done.8.refs_1_ = f32[96,128]{1,0:T(8,128)S(1)} collective-permute-done((f32[96,128]{1,0:T(8,128)S(1)}, f32[96,128]{1,0:T(8,128)S(1)}, u32[]{:S(2)}, u32[]{:S(2)}) %collective-permute-start.8) | collective-permute-done | bytes 49184 | tf_op jit(solution)/shard_map/ppermute | solution.py:369
  35.1 3.3 %collective-permute-done.9.refs_2_ = f32[96,128]{1,0:T(8,128)S(1)} collective-permute-done((f32[96,128]{1,0:T(8,128)S(1)}, f32[96,128]{1,0:T(8,128)S(1)}, u32[]{:S(2)}, u32[]{:S(2)}) %collective-permute-start.9) | collective-permute-done | bytes 49184 | tf_op jit(solution)/shard_map/ppermute | solution.py:369
  38.4 0.0 collective-permute-done.10.refs_3_
  38.4 3.0 %collective-permute-start.11 = (f32[96,128]{1,0:T(8,128)S(1)}, f32[96,128]{1,0:T(8,128)S(1)}, u32[]{:S(2)}, u32[]{:S(2)}) collective-permute-start(f32[96,128]{1,0:T(8,128)S(1)} %shard_map.51.own_ref), channel_id=1, source_target_pairs={{0,4},{1,5},{4,8},{5,9},{6,2},{7,3},{8,12},{9,13},{10,6},{11,7},{1... | collective-permute-start | bytes 147464 | tf_op jit(solution)/shard_map/ppermute | solution.py:454
  41.4 1.2 %collective-permute-done.11.there_ref = f32[96,128]{1,0:T(8,128)S(1)} collective-permute-done((f32[96,128]{1,0:T(8,128)S(1)}, f32[96,128]{1,0:T(8,128)S(1)}, u32[]{:S(2)}, u32[]{:S(2)}) %collective-permute-start.11) | collective-permute-done | bytes 49184 | tf_op jit(solution)/shard_map/ppermute | solution.py:454
  42.5 0.8 %shard_map.52 = f32[50,96]{1,0:T(8,128)} custom-call(f32[96,128]{1,0:T(8,128)S(1)} %shard_map.51.own_ref, f32[96,128]{1,0:T(8,128)S(1)} %collective-permute-done.11.there_ref), custom_call_target="tpu_custom_call" | custom-call | tf_op jit(solution)/shard_map/pallas_call | solution.py:455
  (3 shorter events, 0.0 us)
Async XLA Ops:
  0.0 6.7 %copy-start.2 = (s32[2048]{0:T(1024)S(1)}, s32[2048]{0:T(1024)}, u32[]{:S(2)}) copy-start(s32[2048]{0:T(1024)} %param.5) | copy-start | bytes 24580
  2.1 15.0 %collective-permute-start = (bf16[1056,384]{1,0:T(8,128)(2,1)S(1)}, bf16[1056,384]{1,0:T(8,128)(2,1)S(1)}, u32[]{:S(2)}, u32[]{:S(2)}) collective-permute-start(bf16[1056,384]{1,0:T(8,128)(2,1)S(1)} %get-tuple-element.27), channel_id=1, source_target_pairs={{4,8},{8,4},{5,9},{9,5},{6,10},{10,6},{7,11},{11,7},{20,24},{24,20... | collective-permute-start | bytes 2433032 | tf_op jit(solution)/shard_map/ppermute | solution.py:378
  6.7 10.5 %collective-permute-start.1 = (bf16[1056,384]{1,0:T(8,128)(2,1)S(1)}, bf16[1056,384]{1,0:T(8,128)(2,1)S(1)}, u32[]{:S(2)}, u32[]{:S(2)}) collective-permute-start(bf16[1056,384]{1,0:T(8,128)(2,1)S(1)} %get-tuple-element.28), channel_id=1, source_target_pairs={{0,4},{4,0},{8,12},{12,8},{1,5},{5,1},{9,13},{13,9},{2,6},{6,2},{1... | collective-permute-start | bytes 2433032 | tf_op jit(solution)/shard_map/ppermute | solution.py:378
  7.9 5.2 %collective-permute-start.2 = (s32[48,384]{1,0:T(8,128)S(1)}, s32[48,384]{1,0:T(8,128)S(1)}, u32[]{:S(2)}, u32[]{:S(2)}) collective-permute-start(s32[48,384]{1,0:T(8,128)S(1)} %get-tuple-element.31), channel_id=1, source_target_pairs={{0,1},{1,2},{2,3},{3,0},{4,5},{5,6},{6,7},{7,4},{8,9},{9,10},{10,1... | collective-permute-start | bytes 221192 | tf_op jit(solution)/shard_map/ppermute | solution.py:369
  9.2 7.9 %collective-permute-start.3 = (s32[48,384]{1,0:T(8,128)S(1)}, s32[48,384]{1,0:T(8,128)S(1)}, u32[]{:S(2)}, u32[]{:S(2)}) collective-permute-start(s32[48,384]{1,0:T(8,128)S(1)} %get-tuple-element.32), channel_id=1, source_target_pairs={{0,2},{1,3},{2,0},{3,1},{4,6},{5,7},{6,4},{7,5},{8,10},{9,11},{10,... | collective-permute-start | bytes 221192 | tf_op jit(solution)/shard_map/ppermute | solution.py:369
  11.6 5.6 %collective-permute-start.4 = (s32[48,384]{1,0:T(8,128)S(1)}, s32[48,384]{1,0:T(8,128)S(1)}, u32[]{:S(2)}, u32[]{:S(2)}) collective-permute-start(s32[48,384]{1,0:T(8,128)S(1)} %get-tuple-element.33), channel_id=1, source_target_pairs={{0,3},{1,0},{2,1},{3,2},{4,7},{5,4},{6,5},{7,6},{8,11},{9,8},{10,9... | collective-permute-start | bytes 221192 | tf_op jit(solution)/shard_map/ppermute | solution.py:369
  17.2 5.6 %copy-start = (s32[50,384]{1,0:T(8,128)S(1)}, s32[50,384]{1,0:T(8,128)}, u32[]{:S(2)}) copy-start(s32[50,384]{1,0:T(8,128)} %annot_ref.3) | copy-start | bytes 230404
  17.2 11.4 %copy-start.1 = (s32[4]{0:T(128)S(1)}, s32[4]{0:T(128)}, u32[]{:S(2)}) copy-start(s32[4]{0:T(128)} %reach_ref.1) | copy-start | bytes 52
  18.6 5.2 %collective-permute-start.5 = (s32[56,384]{1,0:T(8,128)S(1)}, s32[56,384]{1,0:T(8,128)S(1)}, u32[]{:S(2)}, u32[]{:S(2)}) collective-permute-start(s32[56,384]{1,0:T(8,128)S(1)} %get-tuple-element.36), channel_id=1, source_target_pairs={{0,1},{1,2},{2,3},{3,0},{4,5},{5,6},{6,7},{7,4},{8,9},{9,10},{10,1... | collective-permute-start | bytes 258056 | tf_op jit(solution)/shard_map/ppermute | solution.py:369
  20.5 8.1 %collective-permute-start.6 = (s32[56,384]{1,0:T(8,128)S(1)}, s32[56,384]{1,0:T(8,128)S(1)}, u32[]{:S(2)}, u32[]{:S(2)}) collective-permute-start(s32[56,384]{1,0:T(8,128)S(1)} %get-tuple-element.37), channel_id=1, source_target_pairs={{0,2},{1,3},{2,0},{3,1},{4,6},{5,7},{6,4},{7,5},{8,10},{9,11},{10,... | collective-permute-start | bytes 258056 | tf_op jit(solution)/shard_map/ppermute | solution.py:369
  22.0 6.6 %collective-permute-start.7 = (s32[56,384]{1,0:T(8,128)S(1)}, s32[56,384]{1,0:T(8,128)S(1)}, u32[]{:S(2)}, u32[]{:S(2)}) collective-permute-start(s32[56,384]{1,0:T(8,128)S(1)} %get-tuple-element.38), channel_id=1, source_target_pairs={{0,3},{1,0},{2,1},{3,2},{4,7},{5,4},{6,5},{7,6},{8,11},{9,8},{10,9... | collective-permute-start | bytes 258056 | tf_op jit(solution)/shard_map/ppermute | solution.py:369
  30.3 4.8 %collective-permute-start.8 = (f32[96,128]{1,0:T(8,128)S(1)}, f32[96,128]{1,0:T(8,128)S(1)}, u32[]{:S(2)}, u32[]{:S(2)}) collective-permute-start(f32[96,128]{1,0:T(8,128)S(1)} %get-tuple-element.42), channel_id=1, source_target_pairs={{0,1},{1,2},{2,3},{3,0},{4,5},{5,6},{6,7},{7,4},{8,9},{9,10},{10,1... | collective-permute-start | bytes 147464 | tf_op jit(solution)/shard_map/ppermute | solution.py:369
  32.4 5.9 %collective-permute-start.9 = (f32[96,128]{1,0:T(8,128)S(1)}, f32[96,128]{1,0:T(8,128)S(1)}, u32[]{:S(2)}, u32[]{:S(2)}) collective-permute-start(f32[96,128]{1,0:T(8,128)S(1)} %get-tuple-element.43), channel_id=1, source_target_pairs={{0,2},{1,3},{2,0},{3,1},{4,6},{5,7},{6,4},{7,5},{8,10},{9,11},{10,... | collective-permute-start | bytes 147464 | tf_op jit(solution)/shard_map/ppermute | solution.py:369
  32.4 5.9 %collective-permute-start.10 = (f32[96,128]{1,0:T(8,128)S(1)}, f32[96,128]{1,0:T(8,128)S(1)}, u32[]{:S(2)}, u32[]{:S(2)}) collective-permute-start(f32[96,128]{1,0:T(8,128)S(1)} %get-tuple-element.44), channel_id=1, source_target_pairs={{0,3},{1,0},{2,1},{3,2},{4,7},{5,4},{6,5},{7,6},{8,11},{9,8},{10,9... | collective-permute-start | bytes 147464 | tf_op jit(solution)/shard_map/ppermute | solution.py:369
  38.4 4.1 %collective-permute-start.11 = (f32[96,128]{1,0:T(8,128)S(1)}, f32[96,128]{1,0:T(8,128)S(1)}, u32[]{:S(2)}, u32[]{:S(2)}) collective-permute-start(f32[96,128]{1,0:T(8,128)S(1)} %shard_map.51.own_ref), channel_id=1, source_target_pairs={{0,4},{1,5},{4,8},{5,9},{6,2},{7,3},{8,12},{9,13},{10,6},{11,7},{1... | collective-permute-start | bytes 147464 | tf_op jit(solution)/shard_map/ppermute | solution.py:454

commit v4 on v3

--- a/solution.py
+++ b/solution.py
@@ -128,16 +128,17 @@
     store(slice(rows // 2, rows // 2 + part), annots[:part], annots[part:])
 
 
-def send_shares(groups, source, share, targets):
-    me = lax.axis_index("hap")
-    for step, target in enumerate(targets):
-        group = lax.rem(me + step, groups)
-        target[0:share, :] = source[pl.ds(pl.multiple_of(group * share, 8), share), :]
-
-
-def own_kernel(groups, share, alleles_ref, label_ref, *refs):
-    weighted_ref, totals_ref, *targets = refs[: 2 + groups]
-    tile, folded = refs[2 + groups :]
+def pad_rows(ref, done):
+    if ref.shape[0] > done:
+        ref[done:, :] = jnp.zeros((ref.shape[0] - done, ref.shape[1]), ref.dtype)
+
+
+def sum_of_parts(ref, groups):
+    size = ref.shape[0] // groups
+    return sum((ref[k * size : (k + 1) * size, :] for k in range(1, groups)), ref[0:size, :])
+
+
+def own_kernel(alleles_ref, label_ref, weighted_ref, totals_ref, folded, tile):
     rows, snps = alleles_ref.shape
     half = snps // 2
     weight = jnp.where(label_ref[...] > 0, float(BASE), 1.0)
@@ -153,14 +154,12 @@
     moved = (col < half) | (col - half > row)
     turned = pltpu.roll(tile[0:half, :], half, 1)
     folded[0:half, :] = to_fields(jnp.where(moved, turned, tile[half:snps, :]))
-    if folded.shape[0] > half:
-        folded[half:, :] = jnp.zeros((folded.shape[0] - half, snps), jnp.int32)
-    send_shares(groups, folded, share, targets)
-
-
-def near_kernel(groups, share, weighted_ref, far_ref, close_ref, totals_ref, *refs):
-    own_parts, own_sum_ref = refs[:groups], refs[groups]
-    targets, (near, tile, folded) = refs[groups + 1 : 2 * groups + 1], refs[2 * groups + 1 :]
+    pad_rows(folded, half)
+
+
+def near_kernel(
+    groups, weighted_ref, far_ref, close_ref, totals_ref, own_parts_ref, own_sum_ref, out_ref, near, tile
+):
     rows, snps = near.shape
     half = snps // 2
     odd = odd_block()
@@ -184,9 +183,7 @@
     row, col = iota((half, snps), 0), iota((half, snps), 1)
     moved = (col >= half) & (col - half < row)
     turned = pltpu.roll(tile[0:half, :], half, 1)
-    folded[0:half, :] = to_fields(jnp.where(moved, turned, tile[half:snps, :]))
-    if folded.shape[0] > half:
-        folded[half:, :] = jnp.zeros((folded.shape[0] - half, snps), jnp.int32)
+    folded = to_fields(jnp.where(moved, turned, tile[half:snps, :]))
     square = (snps, snps)
     far = jnp.sum(
         jnp.where(iota(square, 0) == iota(square, 1), tile[0:snps, :], 0.0), axis=0, keepdims=True
@@ -196,10 +193,17 @@
             [totals_ref[0:2, :], tile[snps : snps + 1, :], far, jnp.zeros((4, snps))], axis=0
         )
     )
-    send_shares(groups, folded, share, targets)
-    for target in targets:
-        target[share:, :] = extras
-    own_sum_ref[...] = sum((part[...] for part in own_parts[1:]), own_parts[0][...])
+    size = out_ref.shape[0] // groups
+    share = size - extras.shape[0]
+    for group in range(groups):
+        start = group * size
+        real = min(max(half - group * share, 0), share)
+        if real:
+            out_ref[start : start + real, :] = folded[group * share : group * share + real, :]
+        if real < share:
+            out_ref[start + real : start + share, :] = jnp.zeros((share - real, snps), jnp.int32)
+        out_ref[start + share : start + size, :] = extras
+    own_sum_ref[...] = sum_of_parts(own_parts_ref, groups)
 
 
 def annots_kernel(annot_ref, far_ref, close_ref, own_ref, near_ref):
@@ -252,11 +256,11 @@
     )
 
 
-def score_kernel(groups, share, reach_ref, *refs):
-    own_sum_ref, near_parts = refs[0], refs[1 : groups + 1]
-    annot_ref, near_annot_ref = refs[groups + 1 : groups + 3]
-    targets = refs[groups + 3 : 2 * groups + 3]
-    table, annots, near_annots, scores = refs[2 * groups + 3 :]
+def score_kernel(
+    groups, reach_ref, own_sum_ref, near_parts_ref, annot_ref, near_annot_ref, out_ref, table, annots, near_annots, *more
+):
+    scores = more[0] if more else out_ref
+    share = own_sum_ref.shape[0]
     snps = annot_ref.shape[0]
     half = snps // 2
     out_share = snps // groups
@@ -268,7 +272,7 @@
     reach_down = reach_ref[jnp.maximum(block - 1, 0)]
 
     own_counts = own_sum_ref[...]
-    near_sums = sum((part[...] for part in near_parts[1:]), near_parts[0][...])
+    near_sums = sum_of_parts(near_parts_ref, groups)
     extras = from_fields(near_sums[share:, :])
     near_counts = near_sums[0:share, :]
 
@@ -349,14 +353,12 @@
         + near_annots[out_rows, :] * jnp.where(reach_here >= snps, far_product, 0.0)
         + pltpu.roll(mine_annots, HALF_LANES, 1) * jnp.where(far_reach >= snps, far_product, 0.0)
     )
-    for step, target in enumerate(targets):
-        group = lax.rem(me + step, groups)
-        target[...] = scores[pl.ds(pl.multiple_of(group * out_share, 8), out_share), :]
-
-
-def sum_kernel(*refs):
-    *parts, out_ref = refs
-    out_ref[...] = sum((part[...] for part in parts[1:]), parts[0][...])
+    if more:
+        out_ref[...] = scores[0:snps, :]
+
+
+def sum_kernel(groups, parts_ref, out_ref):
+    out_ref[...] = sum_of_parts(parts_ref, groups)
 
 
 def finish_kernel(own_ref, there_ref, out_ref):
@@ -365,10 +367,8 @@
     out_ref[...] = (own_ref[...] + there).T[0:annots, :]
 
 
-def around(value, groups, step):
-    return lax.ppermute(
-        value, "hap", [(source, (source + step) % groups) for source in range(groups)]
-    )
+def exchanged(value):
+    return lax.all_to_all(value, "hap", 0, 0, tiled=True)
 
 
 def swapped(value, first):
@@ -409,26 +409,25 @@
     from_close = swapped(close, 0)
 
     tile = pltpu.VMEM((snps + 16, snps), f32)
-    folded = pltpu.VMEM((folded_rows, snps), i32)
-    weighted, totals, *own_parts = call(
-        functools.partial(own_kernel, groups, share),
-        [shape((snps + 16, rows), bf16), shape((8, snps), f32)] + [shape((share, snps), i32)] * groups,
+    weighted, totals, own_parts = call(
+        own_kernel,
+        [shape((snps + 16, rows), bf16), shape((8, snps), f32), shape((folded_rows, snps), i32)],
         [VMEM, VMEM],
-        [tile, folded],
+        [tile],
         flops=2 * rows * snps * snps,
         moved=rows * snps * 4,
     )(alleles, labels.reshape(1, rows))
-    own_parts = [own_parts[0]] + [around(own_parts[k], groups, k) for k in range(1, groups)]
-
-    own_sum, *near_parts = call(
-        functools.partial(near_kernel, groups, share),
-        [shape((share, snps), i32)] + [shape((share + 8, snps), i32)] * groups,
-        [VMEM] * (4 + groups),
-        [pltpu.VMEM((rows, snps), bf16), tile, folded],
+    own_parts = exchanged(own_parts)
+
+    own_sum, near_parts = call(
+        functools.partial(near_kernel, groups),
+        [shape((share, snps), i32), shape(((share + 8) * groups, snps), i32)],
+        [VMEM] * 5,
+        [pltpu.VMEM((rows, snps), bf16), tile],
         flops=2 * rows * snps * snps,
         moved=rows * snps * 4,
-    )(weighted, from_far, from_close, totals, *own_parts)
-    near_parts = [near_parts[0]] + [around(near_parts[k], groups, k) for k in range(1, groups)]
+    )(weighted, from_far, from_close, totals, own_parts)
+    near_parts = exchanged(near_parts)
 
     by_snp = shape((snps, LANES), f32)
     own_annots, near_annots = call(annots_kernel, [by_snp, by_snp], [VMEM] * 3, moved=1 << 20)(
@@ -436,15 +435,16 @@
     )
     tall = pltpu.VMEM((padded, LANES), f32)
     scores = call(
-        functools.partial(score_kernel, groups, share),
-        [shape((out_share, LANES), f32)] * groups,
-        [SMEM] + [VMEM] * (groups + 3),
-        [tall, tall, tall, tall],
+        functools.partial(score_kernel, groups),
+        by_snp,
+        [SMEM] + [VMEM] * 4,
+        [tall] * (3 if padded == snps else 4),
         flops=1 << 26,
         moved=1 << 21,
-    )(reach, own_sum, *near_parts, own_annots, near_annots)
-    scores = [scores[0]] + [around(scores[k], groups, k) for k in range(1, groups)]
-    summed = call(sum_kernel, shape((out_share, LANES), f32), [VMEM] * groups)(*scores)
+    )(reach, own_sum, near_parts, own_annots, near_annots)
+    summed = call(functools.partial(sum_kernel, groups), shape((out_share, LANES), f32), [VMEM])(
+        exchanged(scores)
+    )
     pairs = []
     for block in range(blocks):
         for group in range(groups):

time: 43.5 us -> 53.7 us (1.23)
  blocking collectives: 0 us -> 22.4 us
  starting transfers between devices: 20.7 us -> 13.6 us
  waiting for transfers between devices: 15.1 us -> 9.26 us
  Pallas kernels: 7.37 us -> 7.96 us
    all_to_all x0 -> x2, blocking collectives: none -> 22.4 us  [exchanged(): return lax.all_to_all(value, 'hap', 0, 0, tiled=True)]
    ppermute x9 -> x0, waiting for transfers between devices: 13.9 us -> none  [around(): lax.ppermute(value, 'hap', [(source, (source + step) % groups) for source...]
    ppermute x9 -> x0, starting transfers between devices: 13.2 us -> none  [around(): lax.ppermute(value, 'hap', [(source, (source + step) % groups) for source...]
    all_to_all x0 -> x1, waiting for transfers between devices: none -> 8.1 us  [exchanged(): return lax.all_to_all(value, 'hap', 0, 0, tiled=True)]
    all_to_all x0 -> x1, starting transfers between devices: none -> 3.45 us  [exchanged(): return lax.all_to_all(value, 'hap', 0, 0, tiled=True)]
    ppermute x1, starting transfers between devices: 2.98 us -> 5.61 us  [per_device(): there = lax.ppermute(summed, ('snp', 'hap'), pairs)]
    pallas_call x4, Pallas kernels: 4.19 us -> 4.79 us  [the longest x1 2.08 us: per_device(): call(functools.partial(near_kernel, groups), [shape((share, snps), i32),...]
  transfers between devices with their start and end apart: 12 -> 4, of which waited for: 7 -> 2; matrix products, arithmetic and copies ran while one was open for 0% -> 0% of each run, Pallas kernels for 3% -> 3%
where the time goes in v4:
time: 53.7 us; the launch traced here: 53.4 us
  blocking collectives  22.4 us (42%)
  starting transfers between devices  13.6 us (25%)
  waiting for transfers between devices  9.26 us (17%)
  Pallas kernels  7.96 us (15%)
    all_to_all x2, blocking collectives, exchanged(): return lax.all_to_all(value, 'hap', 0, 0, tiled=True)  22.4 us
    all_to_all x1, waiting for transfers between devices, exchanged(): return lax.all_to_all(value, 'hap', 0, 0, tiled=True)  8.1 us
    ppermute x1, starting transfers between devices, per_device(): there = lax.ppermute(summed, ('snp', 'hap'), pairs)  5.61 us
    ppermute x2, starting transfers between devices, swapped(): return lax.ppermute(value, 'snp', pairs)  4.58 us
    all_to_all x1, starting transfers between devices, exchanged(): return lax.all_to_all(value, 'hap', 0, 0, tiled=True)  3.45 us
    pallas_call x1, Pallas kernels, per_device(): call(prepare_kernel, [shape((rows, snps), bf16), packed, packed], [HBM, H...  2.14 us
    pallas_call x1, Pallas kernels, per_device(): call(functools.partial(near_kernel, groups), [shape((share, snps), i32),...  2.08 us
    pallas_call x1, Pallas kernels, per_device(): call(functools.partial(score_kernel, groups), by_snp, [SMEM] + [VMEM] * 4...  1.59 us
  transfers between devices with their start and end apart: 4, of which 2 were waited for; matrix products, arithmetic and copies ran while one was open for 0% of the time, Pallas kernels for 3%

profile of v4, /device:TPU:1, one launch (start us, length us, event | category | flops | bytes accessed | tf_op | source)
XLA Modules:
  0.0 53.4 jit_solution(6065411210428858224)
XLA Ops:
  0.0 0.0 copy-start.2
  0.0 2.1 %shard_map.46 = (bf16[2048,384]{1,0:T(8,128)(2,1)S(1)}, bf16[1056,384]{1,0:T(8,128)(2,1)S(1)}, bf16[1056,384]{1,0:T(8,128)(2,1)S(1)}) custom-call(s32[2048,384]{1,0:T(8,128)} %hap_ref.1, s32[50,384]{1,0:T(8,128)} %annot_ref.3), custom_call_target="tpu_custom_call" | custom-call | bytes 6291456 | tf_op jit(solution)/shard_map/pallas_call | solution.py:397
  2.1 4.5 %collective-permute-start = (bf16[1056,384]{1,0:T(8,128)(2,1)S(1)}, bf16[1056,384]{1,0:T(8,128)(2,1)S(1)}, u32[]{:S(2)}, u32[]{:S(2)}) collective-permute-start(bf16[1056,384]{1,0:T(8,128)(2,1)S(1)} %get-tuple-element.17), channel_id=1, source_target_pairs={{4,8},{8,4},{5,9},{9,5},{6,10},{10,6},{7,11},{11,7},{20,24},{24,20... | collective-permute-start | bytes 2433032 | tf_op jit(solution)/shard_map/ppermute | solution.py:378
  6.7 0.1 collective-permute-start.1
  6.7 0.0 copy-done.2
  6.8 1.1 %shard_map.47 = (bf16[400,2048]{1,0:T(8,128)(2,1)S(1)}, f32[8,384]{1,0:T(8,128)S(1)}, s32[192,384]{1,0:T(8,128)S(1)}) custom-call(bf16[2048,384]{1,0:T(8,128)(2,1)S(1)} %get-tuple-element.15.alleles_ref, s32[1,2048]{1,0:T(1,128)S(1)} %bitcast.12), custom_call_target="tpu_custom_call" | custom-call | flops 603979776 | bytes 3145728 | tf_op jit(solution)/shard_map/pallas_call | solution.py:412
  7.9 13.0 %all_to_all.33 = s32[4,48,384]{2,1,0:T(8,128)S(1)} all-to-all(s32[4,48,384]{2,1,0:T(8,128)S(1)} %bitcast.11), channel_id=1, replica_groups=mesh['parts'=2,'snp'=4,'hap'=4] {'hap'}, dimensions={0} | all-to-all | bytes 589824 | tf_op jit(solution)/shard_map/all_to_all | solution.py:371
  20.8 0.0 collective-permute-done.far_ref
  20.8 0.0 collective-permute-done.1.close_ref
  20.8 0.0 copy-start
  20.9 0.0 copy-start.1
  20.9 2.1 %shard_map.48 = (s32[48,384]{1,0:T(8,128)S(1)}, s32[224,384]{1,0:T(8,128)}) custom-call(bf16[400,2048]{1,0:T(8,128)(2,1)S(1)} %get-tuple-element.16.weighted_ref, bf16[1056,384]{1,0:T(8,128)(2,1)S(1)} %collective-permute-done.far_ref, bf16[1056,384]{1,0:T(8,128)(2,1)S(1)} %collective-permute-done.1.close_ref, f32[8,384]{1,0:T(8,128)S(1)} %get-tuple-element.19.totals_ref, ...), custom_call_target="tpu_custom_call" | custom-call | flops 603979776 | bytes 3145728 | tf_op jit(solution)/shard_map/pallas_call | solution.py:422
  22.9 3.5 %all-to-all-start.1 = ((s32[4,56,384]{2,1,0:T(8,128)}), s32[4,56,384]{2,1,0:T(8,128)S(1)}, u32[]{:S(2)}, u32[]{:S(2)}) async-start(s32[4,56,384]{2,1,0:T(8,128)} %bitcast.3), calls=%async_computation.1 | async-start | bytes 688128 | tf_op jit(solution)/shard_map/all_to_all | solution.py:371
  26.4 0.0 copy-done
  26.4 0.3 shard_map.49
  26.7 8.1 %all-to-all-done.1 = s32[4,56,384]{2,1,0:T(8,128)S(1)} async-done(((s32[4,56,384]{2,1,0:T(8,128)}), s32[4,56,384]{2,1,0:T(8,128)S(1)}, u32[]{:S(2)}, u32[]{:S(2)}) %all-to-all-start.1) | async-done | bytes 344096 | tf_op jit(solution)/shard_map/all_to_all | solution.py:371
  34.8 0.0 copy-done.1
  34.8 1.6 %shard_map.50 = f32[384,128]{1,0:T(8,128)S(1)} custom-call(s32[4]{0:T(128)S(1)} %copy-done.1, s32[48,384]{1,0:T(8,128)S(1)} %get-tuple-element.21.own_sum_ref, s32[224,384]{1,0:T(8,128)S(1)} %bitcast.7, f32[384,128]{1,0:T(8,128)S(1)} %get-tuple-element.23.annot_ref, f32[384,128]{1,0:T(8,128)S(1)} %get-tuple-element.24.near_annot_ref), custom_call_target="tpu_custom_call" | custom-call | flops 67108864 | bytes 2097152 | tf_op jit(solution)/shard_map/pallas_call | solution.py:437
  36.4 9.4 %all_to_all.34 = f32[4,96,128]{2,1,0:T(8,128)S(1)} all-to-all(f32[4,96,128]{2,1,0:T(8,128)S(1)} %bitcast.9), channel_id=1, replica_groups=mesh['parts'=2,'snp'=4,'hap'=4] {'hap'}, dimensions={0} | all-to-all | bytes 393216 | tf_op jit(solution)/shard_map/all_to_all | solution.py:371
  45.9 5.6 %collective-permute-start.2 = (f32[96,128]{1,0:T(8,128)S(1)}, f32[96,128]{1,0:T(8,128)S(1)}, u32[]{:S(2)}, u32[]{:S(2)}) collective-permute-start(f32[96,128]{1,0:T(8,128)S(1)} %shard_map.51.own_ref), channel_id=1, source_target_pairs={{0,4},{1,5},{4,8},{5,9},{6,2},{7,3},{8,12},{9,13},{10,6},{11,7},{1... | collective-permute-start | bytes 147464 | tf_op jit(solution)/shard_map/ppermute | solution.py:454
  51.5 1.2 %collective-permute-done.2.there_ref = f32[96,128]{1,0:T(8,128)S(1)} collective-permute-done((f32[96,128]{1,0:T(8,128)S(1)}, f32[96,128]{1,0:T(8,128)S(1)}, u32[]{:S(2)}, u32[]{:S(2)}) %collective-permute-start.2) | collective-permute-done | bytes 49184 | tf_op jit(solution)/shard_map/ppermute | solution.py:454
  52.7 0.8 %shard_map.52 = f32[50,96]{1,0:T(8,128)} custom-call(f32[96,128]{1,0:T(8,128)S(1)} %shard_map.51.own_ref, f32[96,128]{1,0:T(8,128)S(1)} %collective-permute-done.2.there_ref), custom_call_target="tpu_custom_call" | custom-call | tf_op jit(solution)/shard_map/pallas_call | solution.py:455
  (3 shorter events, 0.0 us)
Async XLA Ops:
  0.0 6.7 %copy-start.2 = (s32[2048]{0:T(1024)S(1)}, s32[2048]{0:T(1024)}, u32[]{:S(2)}) copy-start(s32[2048]{0:T(1024)} %param.5) | copy-start | bytes 24580
  2.1 18.7 %collective-permute-start = (bf16[1056,384]{1,0:T(8,128)(2,1)S(1)}, bf16[1056,384]{1,0:T(8,128)(2,1)S(1)}, u32[]{:S(2)}, u32[]{:S(2)}) collective-permute-start(bf16[1056,384]{1,0:T(8,128)(2,1)S(1)} %get-tuple-element.17), channel_id=1, source_target_pairs={{4,8},{8,4},{5,9},{9,5},{6,10},{10,6},{7,11},{11,7},{20,24},{24,20... | collective-permute-start | bytes 2433032 | tf_op jit(solution)/shard_map/ppermute | solution.py:378
  6.7 14.2 %collective-permute-start.1 = (bf16[1056,384]{1,0:T(8,128)(2,1)S(1)}, bf16[1056,384]{1,0:T(8,128)(2,1)S(1)}, u32[]{:S(2)}, u32[]{:S(2)}) collective-permute-start(bf16[1056,384]{1,0:T(8,128)(2,1)S(1)} %get-tuple-element.18), channel_id=1, source_target_pairs={{0,4},{4,0},{8,12},{12,8},{1,5},{5,1},{9,13},{13,9},{2,6},{6,2},{1... | collective-permute-start | bytes 2433032 | tf_op jit(solution)/shard_map/ppermute | solution.py:378
  20.8 5.6 %copy-start = (s32[50,384]{1,0:T(8,128)S(1)}, s32[50,384]{1,0:T(8,128)}, u32[]{:S(2)}) copy-start(s32[50,384]{1,0:T(8,128)} %annot_ref.3) | copy-start | bytes 230404
  20.9 14.0 %copy-start.1 = (s32[4]{0:T(128)S(1)}, s32[4]{0:T(128)}, u32[]{:S(2)}) copy-start(s32[4]{0:T(128)} %reach_ref.1) | copy-start | bytes 52
  22.9 11.9 %all-to-all-start.1 = ((s32[4,56,384]{2,1,0:T(8,128)}), s32[4,56,384]{2,1,0:T(8,128)S(1)}, u32[]{:S(2)}, u32[]{:S(2)}) async-start(s32[4,56,384]{2,1,0:T(8,128)} %bitcast.3), calls=%async_computation.1 | async-start | bytes 688128 | tf_op jit(solution)/shard_map/all_to_all | solution.py:371
  45.9 6.8 %collective-permute-start.2 = (f32[96,128]{1,0:T(8,128)S(1)}, f32[96,128]{1,0:T(8,128)S(1)}, u32[]{:S(2)}, u32[]{:S(2)}) collective-permute-start(f32[96,128]{1,0:T(8,128)S(1)} %shard_map.51.own_ref), channel_id=1, source_target_pairs={{0,4},{1,5},{4,8},{5,9},{6,2},{7,3},{8,12},{9,13},{10,6},{11,7},{1... | collective-permute-start | bytes 147464 | tf_op jit(solution)/shard_map/ppermute | solution.py:454

commit v5 on v3

--- a/solution.py
+++ b/solution.py
@@ -128,11 +128,18 @@
     store(slice(rows // 2, rows // 2 + part), annots[:part], annots[part:])
 
 
+def partner(group, step, groups):
+    if groups & (groups - 1) == 0:
+        return group ^ step
+    return (group + step) % groups
+
+
 def send_shares(groups, source, share, targets):
     me = lax.axis_index("hap")
     for step, target in enumerate(targets):
-        group = lax.rem(me + step, groups)
-        target[0:share, :] = source[pl.ds(pl.multiple_of(group * share, 8), share), :]
+        group = partner(me, step, groups)
+        rows = source[pl.ds(pl.multiple_of(group * share, 8), share), :]
+        target[0:share, :] = rows.astype(target.dtype)
 
 
 def own_kernel(groups, share, alleles_ref, label_ref, *refs):
@@ -349,25 +356,31 @@
         + near_annots[out_rows, :] * jnp.where(reach_here >= snps, far_product, 0.0)
         + pltpu.roll(mine_annots, HALF_LANES, 1) * jnp.where(far_reach >= snps, far_product, 0.0)
     )
-    for step, target in enumerate(targets):
-        group = lax.rem(me + step, groups)
-        target[...] = scores[pl.ds(pl.multiple_of(group * out_share, 8), out_share), :]
+    send_shares(groups, scores, out_share, targets)
 
 
 def sum_kernel(*refs):
-    *parts, out_ref = refs
-    out_ref[...] = sum((part[...] for part in parts[1:]), parts[0][...])
+    *parts, own_ref, there_ref = refs
+    total = sum((part[...].astype(jnp.float32) for part in parts[1:]), parts[0][...])
+    own_ref[...] = total
+    half = there_ref.shape[0]
+    left = iota((half, LANES), 1) < HALF_LANES
+    second = total[half:]
+    if second.shape[0] < half:
+        second = jnp.concatenate([second, jnp.zeros((half - second.shape[0], LANES))], axis=0)
+    there_ref[...] = jnp.where(left, pltpu.roll(total[0:half], HALF_LANES, 1), second)
 
 
 def finish_kernel(own_ref, there_ref, out_ref):
-    annots = out_ref.shape[0]
-    there = pltpu.roll(there_ref[...], HALF_LANES, 1)
-    out_ref[...] = (own_ref[...] + there).T[0:annots, :]
+    annots, rows = out_ref.shape
+    there = there_ref[...]
+    there = jnp.concatenate([there, pltpu.roll(there, HALF_LANES, 1)], axis=0)
+    out_ref[...] = (own_ref[...] + there[0:rows]).T[0:annots, :]
 
 
 def around(value, groups, step):
     return lax.ppermute(
-        value, "hap", [(source, (source + step) % groups) for source in range(groups)]
+        value, "hap", [(source, partner(source, step, groups)) for source in range(groups)]
     )
 
 
@@ -418,7 +431,7 @@
         flops=2 * rows * snps * snps,
         moved=rows * snps * 4,
     )(alleles, labels.reshape(1, rows))
-    own_parts = [own_parts[0]] + [around(own_parts[k], groups, k) for k in range(1, groups)]
+    own_parts = [own_parts[0]] + [around(own_parts[k], groups, k) for k in range(groups - 1, 0, -1)]
 
     own_sum, *near_parts = call(
         functools.partial(near_kernel, groups, share),
@@ -428,7 +441,7 @@
         flops=2 * rows * snps * snps,
         moved=rows * snps * 4,
     )(weighted, from_far, from_close, totals, *own_parts)
-    near_parts = [near_parts[0]] + [around(near_parts[k], groups, k) for k in range(1, groups)]
+    near_parts = [near_parts[0]] + [around(near_parts[k], groups, k) for k in range(groups - 1, 0, -1)]
 
     by_snp = shape((snps, LANES), f32)
     own_annots, near_annots = call(annots_kernel, [by_snp, by_snp], [VMEM] * 3, moved=1 << 20)(
@@ -437,22 +450,27 @@
     tall = pltpu.VMEM((padded, LANES), f32)
     scores = call(
         functools.partial(score_kernel, groups, share),
-        [shape((out_share, LANES), f32)] * groups,
+        [shape((out_share, LANES), f32)] + [shape((out_share, LANES), bf16)] * (groups - 1),
         [SMEM] + [VMEM] * (groups + 3),
         [tall, tall, tall, tall],
         flops=1 << 26,
         moved=1 << 21,
     )(reach, own_sum, *near_parts, own_annots, near_annots)
-    scores = [scores[0]] + [around(scores[k], groups, k) for k in range(1, groups)]
-    summed = call(sum_kernel, shape((out_share, LANES), f32), [VMEM] * groups)(*scores)
+    scores = [scores[0]] + [around(scores[k], groups, k) for k in range(groups - 1, 0, -1)]
+    half_share = round_up(-(-out_share // 2), 8)
+    own_scores, near_scores = call(
+        sum_kernel,
+        [shape((out_share, LANES), f32), shape((half_share, LANES), f32)],
+        [VMEM] * groups,
+    )(*scores)
     pairs = []
     for block in range(blocks):
         for group in range(groups):
             target = block + 1 if group < groups // 2 else block - 1
             if 0 <= target < blocks:
                 pairs.append((block * groups + group, target * groups + group))
-    there = lax.ppermute(summed, ("snp", "hap"), pairs)
-    return call(finish_kernel, shape((annotations.shape[0], out_share), f32), [VMEM] * 2)(summed, there)
+    there = lax.ppermute(near_scores, ("snp", "hap"), pairs)
+    return call(finish_kernel, shape((annotations.shape[0], out_share), f32), [VMEM] * 2)(own_scores, there)
 
 
 def solution(mesh):

time: 43.5 us -> 43.2 us (level)
  no operation moved by 1% of the time
where the time goes in v5:
time: 43.2 us; the launch traced here: 43 us
  starting transfers between devices  20.8 us (48%)
  waiting for transfers between devices  14.7 us (34%)
  Pallas kernels  7.38 us (17%)
    ppermute x9, waiting for transfers between devices, around(): lax.ppermute(value, 'hap', [(source, partner(source, step, groups)) for s...  13.7 us
    ppermute x9, starting transfers between devices, around(): lax.ppermute(value, 'hap', [(source, partner(source, step, groups)) for s...  11 us
    ppermute x1, starting transfers between devices, per_device(): there = lax.ppermute(near_scores, ('snp', 'hap'), pairs)  5.28 us
    ppermute x2, starting transfers between devices, swapped(): return lax.ppermute(value, 'snp', pairs)  4.58 us
    pallas_call x1, Pallas kernels, per_device(): call(prepare_kernel, [shape((rows, snps), bf16), packed, packed], [HBM, H...  2.14 us
    pallas_call x1, Pallas kernels, per_device(): call(functools.partial(score_kernel, groups, share), [shape((out_share, L...  1.62 us
    pallas_call x1, Pallas kernels, per_device(): call(functools.partial(near_kernel, groups, share), [shape((share, snps),...  1.39 us
    pallas_call x1, Pallas kernels, per_device(): call(functools.partial(own_kernel, groups, share), [shape((snps + 16, row...  1.13 us
  transfers between devices with their start and end apart: 12, of which 7 were waited for; matrix products, arithmetic and copies ran while one was open for 0% of the time, Pallas kernels for 3%

profile of v5, /device:TPU:1, one launch (start us, length us, event | category | flops | bytes accessed | tf_op | source)
XLA Modules:
  0.0 43.0 jit_solution(17858190923093775584)
XLA Ops:
  0.0 0.0 copy-start.2
  0.0 2.1 %shard_map.46 = (bf16[2048,384]{1,0:T(8,128)(2,1)S(1)}, bf16[1056,384]{1,0:T(8,128)(2,1)S(1)}, bf16[1056,384]{1,0:T(8,128)(2,1)S(1)}) custom-call(s32[2048,384]{1,0:T(8,128)} %hap_ref.1, s32[50,384]{1,0:T(8,128)} %annot_ref.3), custom_call_target="tpu_custom_call" | custom-call | bytes 6291456 | tf_op jit(solution)/shard_map/pallas_call | solution.py:410
  2.1 4.5 %collective-permute-start = (bf16[1056,384]{1,0:T(8,128)(2,1)S(1)}, bf16[1056,384]{1,0:T(8,128)(2,1)S(1)}, u32[]{:S(2)}, u32[]{:S(2)}) collective-permute-start(bf16[1056,384]{1,0:T(8,128)(2,1)S(1)} %get-tuple-element.29), channel_id=1, source_target_pairs={{4,8},{8,4},{5,9},{9,5},{6,10},{10,6},{7,11},{11,7},{20,24},{24,20... | collective-permute-start | bytes 2433032 | tf_op jit(solution)/shard_map/ppermute | solution.py:391
  6.7 0.1 collective-permute-start.1
  6.7 0.0 copy-done.2
  6.8 1.1 %shard_map.47 = (bf16[400,2048]{1,0:T(8,128)(2,1)S(1)}, f32[8,384]{1,0:T(8,128)S(1)}, s32[48,384]{1,0:T(8,128)S(1)}, s32[48,384]{1,0:T(8,128)S(1)}, s32[48,384]{1,0:T(8,128)S(1)}, /*index=5*/s32[48,384]{1,0:T(8,128)S(1)}) custom-call(bf16[2048,384]{1,0:T(8,128)(2,1)S(1)} %get-tuple-element.27.alleles_ref, s32[1,2048]{1,0:T(1,128)S(1)} %bitcast.1), custom_call_target="tpu_custom_call" | custom-call | flops 603979776 | bytes 3145728 | tf_op jit(solution)/shard_map/pallas_call | solution.py:426
  7.9 3.4 %collective-permute-start.2 = (s32[48,384]{1,0:T(8,128)S(1)}, s32[48,384]{1,0:T(8,128)S(1)}, u32[]{:S(2)}, u32[]{:S(2)}) collective-permute-start(s32[48,384]{1,0:T(8,128)S(1)} %get-tuple-element.33), channel_id=1, source_target_pairs={{0,3},{1,2},{2,1},{3,0},{4,7},{5,6},{6,5},{7,4},{8,11},{9,10},{10,... | collective-permute-start | bytes 221192 | tf_op jit(solution)/shard_map/ppermute | solution.py:382
  11.3 0.0 collective-permute-start.3
  11.3 0.4 collective-permute-start.4
  11.6 1.5 %collective-permute-done.2.refs_1_ = s32[48,384]{1,0:T(8,128)S(1)} collective-permute-done((s32[48,384]{1,0:T(8,128)S(1)}, s32[48,384]{1,0:T(8,128)S(1)}, u32[]{:S(2)}, u32[]{:S(2)}) %collective-permute-start.2) | collective-permute-done | bytes 73760 | tf_op jit(solution)/shard_map/ppermute | solution.py:382
  13.1 4.3 %collective-permute-done.3.refs_2_ = s32[48,384]{1,0:T(8,128)S(1)} collective-permute-done((s32[48,384]{1,0:T(8,128)S(1)}, s32[48,384]{1,0:T(8,128)S(1)}, u32[]{:S(2)}, u32[]{:S(2)}) %collective-permute-start.3) | collective-permute-done | bytes 73760 | tf_op jit(solution)/shard_map/ppermute | solution.py:382
  17.4 0.0 collective-permute-done.4.refs_3_
  17.4 0.0 collective-permute-done.far_ref
  17.4 0.0 collective-permute-done.1.close_ref
  17.4 0.0 copy-start
  17.4 0.0 copy-start.1
  17.4 1.4 %shard_map.48 = (s32[48,384]{1,0:T(8,128)S(1)}, s32[56,384]{1,0:T(8,128)S(1)}, s32[56,384]{1,0:T(8,128)S(1)}, s32[56,384]{1,0:T(8,128)S(1)}, s32[56,384]{1,0:T(8,128)S(1)}) custom-call(bf16[400,2048]{1,0:T(8,128)(2,1)S(1)} %get-tuple-element.28.weighted_ref, bf16[1056,384]{1,0:T(8,128)(2,1)S(1)} %collective-permute-done.far_ref, ...), custom_call_target="tpu_custom_call" | custom-call | flops 603979776 | bytes 3145728 | tf_op jit(solution)/shard_map/pallas_call | solution.py:436
  18.8 2.8 %collective-permute-start.5 = (s32[56,384]{1,0:T(8,128)S(1)}, s32[56,384]{1,0:T(8,128)S(1)}, u32[]{:S(2)}, u32[]{:S(2)}) collective-permute-start(s32[56,384]{1,0:T(8,128)S(1)} %get-tuple-element.38), channel_id=1, source_target_pairs={{0,3},{1,2},{2,1},{3,0},{4,7},{5,6},{6,5},{7,4},{8,11},{9,10},{10,... | collective-permute-start | bytes 258056 | tf_op jit(solution)/shard_map/ppermute | solution.py:382
  21.7 0.0 collective-permute-start.6
  21.7 0.8 %collective-permute-start.7 = (s32[56,384]{1,0:T(8,128)S(1)}, s32[56,384]{1,0:T(8,128)S(1)}, u32[]{:S(2)}, u32[]{:S(2)}) collective-permute-start(s32[56,384]{1,0:T(8,128)S(1)} %get-tuple-element.40), channel_id=1, source_target_pairs={{0,1},{1,0},{2,3},{3,2},{4,5},{5,4},{6,7},{7,6},{8,9},{9,8},{10,11... | collective-permute-start | bytes 258056 | tf_op jit(solution)/shard_map/ppermute | solution.py:382
  22.5 0.0 copy-done
  22.5 0.3 shard_map.49
  22.8 1.4 %collective-permute-done.5.refs_2_ = s32[56,384]{1,0:T(8,128)S(1)} collective-permute-done((s32[56,384]{1,0:T(8,128)S(1)}, s32[56,384]{1,0:T(8,128)S(1)}, u32[]{:S(2)}, u32[]{:S(2)}) %collective-permute-start.5) | collective-permute-done | bytes 86048 | tf_op jit(solution)/shard_map/ppermute | solution.py:382
  24.1 4.9 %collective-permute-done.6.refs_3_ = s32[56,384]{1,0:T(8,128)S(1)} collective-permute-done((s32[56,384]{1,0:T(8,128)S(1)}, s32[56,384]{1,0:T(8,128)S(1)}, u32[]{:S(2)}, u32[]{:S(2)}) %collective-permute-start.6) | collective-permute-done | bytes 86048 | tf_op jit(solution)/shard_map/ppermute | solution.py:382
  29.0 0.0 collective-permute-done.7.refs_4_
  29.0 0.0 copy-done.1
  29.0 1.6 %shard_map.50 = (f32[96,128]{1,0:T(8,128)S(1)}, bf16[96,128]{1,0:T(8,128)(2,1)S(1)}, bf16[96,128]{1,0:T(8,128)(2,1)S(1)}, bf16[96,128]{1,0:T(8,128)(2,1)S(1)}) custom-call(s32[4]{0:T(128)S(1)} %copy-done.1, s32[48,384]{1,0:T(8,128)S(1)} %get-tuple-element.36.refs_0_, s32[56,384]{1,0:T(8,128)S(1)} %get-tuple-element.37.refs_1_, ...), custom_call_target="tpu_custom_call" | custom-call | flops 67108864 | bytes 2097152 | tf_op jit(solution)/shard_map/pallas_call | solution.py:451
  30.7 1.7 %collective-permute-start.8 = (bf16[96,128]{1,0:T(8,128)(2,1)S(1)}, bf16[96,128]{1,0:T(8,128)(2,1)S(1)}, u32[]{:S(2)}, u32[]{:S(2)}) collective-permute-start(bf16[96,128]{1,0:T(8,128)(2,1)S(1)} %get-tuple-element.44), channel_id=1, source_target_pairs={{0,3},{1,2},{2,1},{3,0},{4,7},{5,6},{6,5},{7,4},{8,11},{9,10},{10,... | collective-permute-start | bytes 73736 | tf_op jit(solution)/shard_map/ppermute | solution.py:382
  32.4 0.0 collective-permute-start.9
  32.4 1.9 %collective-permute-start.10 = (bf16[96,128]{1,0:T(8,128)(2,1)S(1)}, bf16[96,128]{1,0:T(8,128)(2,1)S(1)}, u32[]{:S(2)}, u32[]{:S(2)}) collective-permute-start(bf16[96,128]{1,0:T(8,128)(2,1)S(1)} %get-tuple-element.46), channel_id=1, source_target_pairs={{0,1},{1,0},{2,3},{3,2},{4,5},{5,4},{6,7},{7,6},{8,9},{9,8},{10,11... | collective-permute-start | bytes 73736 | tf_op jit(solution)/shard_map/ppermute | solution.py:382
  34.3 0.9 %collective-permute-done.8.refs_1_ = bf16[96,128]{1,0:T(8,128)(2,1)S(1)} collective-permute-done((bf16[96,128]{1,0:T(8,128)(2,1)S(1)}, bf16[96,128]{1,0:T(8,128)(2,1)S(1)}, u32[]{:S(2)}, u32[]{:S(2)}) %collective-permute-start.8) | collective-permute-done | bytes 24608 | tf_op jit(solution)/shard_map/ppermute | solution.py:382
  35.2 0.8 %collective-permute-done.9.refs_2_ = bf16[96,128]{1,0:T(8,128)(2,1)S(1)} collective-permute-done((bf16[96,128]{1,0:T(8,128)(2,1)S(1)}, bf16[96,128]{1,0:T(8,128)(2,1)S(1)}, u32[]{:S(2)}, u32[]{:S(2)}) %collective-permute-start.9) | collective-permute-done | bytes 24608 | tf_op jit(solution)/shard_map/ppermute | solution.py:382
  36.0 0.0 collective-permute-done.10.refs_3_
  36.0 0.1 shard_map.51
  36.1 5.3 %collective-permute-start.11 = (f32[48,128]{1,0:T(8,128)S(1)}, f32[48,128]{1,0:T(8,128)S(1)}, u32[]{:S(2)}, u32[]{:S(2)}) collective-permute-start(f32[48,128]{1,0:T(8,128)S(1)} %get-tuple-element.48), channel_id=1, source_target_pairs={{0,4},{1,5},{4,8},{5,9},{6,2},{7,3},{8,12},{9,13},{10,6},{11,7},{1... | collective-permute-start | bytes 73736 | tf_op jit(solution)/shard_map/ppermute | solution.py:472
  41.3 0.9 %collective-permute-done.11.there_ref = f32[48,128]{1,0:T(8,128)S(1)} collective-permute-done((f32[48,128]{1,0:T(8,128)S(1)}, f32[48,128]{1,0:T(8,128)S(1)}, u32[]{:S(2)}, u32[]{:S(2)}) %collective-permute-start.11) | collective-permute-done | bytes 24608 | tf_op jit(solution)/shard_map/ppermute | solution.py:472
  42.3 0.7 %shard_map.52 = f32[50,96]{1,0:T(8,128)} custom-call(f32[96,128]{1,0:T(8,128)S(1)} %get-tuple-element.47.own_ref, f32[48,128]{1,0:T(8,128)S(1)} %collective-permute-done.11.there_ref), custom_call_target="tpu_custom_call" | custom-call | tf_op jit(solution)/shard_map/pallas_call | solution.py:473
  (2 shorter events, 0.0 us)
Async XLA Ops:
  0.0 6.7 %copy-start.2 = (s32[2048]{0:T(1024)S(1)}, s32[2048]{0:T(1024)}, u32[]{:S(2)}) copy-start(s32[2048]{0:T(1024)} %param.5) | copy-start | bytes 24580
  2.1 15.3 %collective-permute-start = (bf16[1056,384]{1,0:T(8,128)(2,1)S(1)}, bf16[1056,384]{1,0:T(8,128)(2,1)S(1)}, u32[]{:S(2)}, u32[]{:S(2)}) collective-permute-start(bf16[1056,384]{1,0:T(8,128)(2,1)S(1)} %get-tuple-element.29), channel_id=1, source_target_pairs={{4,8},{8,4},{5,9},{9,5},{6,10},{10,6},{7,11},{11,7},{20,24},{24,20... | collective-permute-start | bytes 2433032 | tf_op jit(solution)/shard_map/ppermute | solution.py:391
  6.7 10.8 %collective-permute-start.1 = (bf16[1056,384]{1,0:T(8,128)(2,1)S(1)}, bf16[1056,384]{1,0:T(8,128)(2,1)S(1)}, u32[]{:S(2)}, u32[]{:S(2)}) collective-permute-start(bf16[1056,384]{1,0:T(8,128)(2,1)S(1)} %get-tuple-element.30), channel_id=1, source_target_pairs={{0,4},{4,0},{8,12},{12,8},{1,5},{5,1},{9,13},{13,9},{2,6},{6,2},{1... | collective-permute-start | bytes 2433032 | tf_op jit(solution)/shard_map/ppermute | solution.py:391
  7.9 5.2 %collective-permute-start.2 = (s32[48,384]{1,0:T(8,128)S(1)}, s32[48,384]{1,0:T(8,128)S(1)}, u32[]{:S(2)}, u32[]{:S(2)}) collective-permute-start(s32[48,384]{1,0:T(8,128)S(1)} %get-tuple-element.33), channel_id=1, source_target_pairs={{0,3},{1,2},{2,1},{3,0},{4,7},{5,6},{6,5},{7,4},{8,11},{9,10},{10,... | collective-permute-start | bytes 221192 | tf_op jit(solution)/shard_map/ppermute | solution.py:382
  11.3 6.1 %collective-permute-start.3 = (s32[48,384]{1,0:T(8,128)S(1)}, s32[48,384]{1,0:T(8,128)S(1)}, u32[]{:S(2)}, u32[]{:S(2)}) collective-permute-start(s32[48,384]{1,0:T(8,128)S(1)} %get-tuple-element.34), channel_id=1, source_target_pairs={{0,2},{1,3},{2,0},{3,1},{4,6},{5,7},{6,4},{7,5},{8,10},{9,11},{10,... | collective-permute-start | bytes 221192 | tf_op jit(solution)/shard_map/ppermute | solution.py:382
  11.3 6.1 %collective-permute-start.4 = (s32[48,384]{1,0:T(8,128)S(1)}, s32[48,384]{1,0:T(8,128)S(1)}, u32[]{:S(2)}, u32[]{:S(2)}) collective-permute-start(s32[48,384]{1,0:T(8,128)S(1)} %get-tuple-element.35), channel_id=1, source_target_pairs={{0,1},{1,0},{2,3},{3,2},{4,5},{5,4},{6,7},{7,6},{8,9},{9,8},{10,11... | collective-permute-start | bytes 221192 | tf_op jit(solution)/shard_map/ppermute | solution.py:382
  17.4 5.0 %copy-start = (s32[50,384]{1,0:T(8,128)S(1)}, s32[50,384]{1,0:T(8,128)}, u32[]{:S(2)}) copy-start(s32[50,384]{1,0:T(8,128)} %annot_ref.3) | copy-start | bytes 230404
  17.4 11.6 %copy-start.1 = (s32[4]{0:T(128)S(1)}, s32[4]{0:T(128)}, u32[]{:S(2)}) copy-start(s32[4]{0:T(128)} %reach_ref.1) | copy-start | bytes 52
  18.8 5.3 %collective-permute-start.5 = (s32[56,384]{1,0:T(8,128)S(1)}, s32[56,384]{1,0:T(8,128)S(1)}, u32[]{:S(2)}, u32[]{:S(2)}) collective-permute-start(s32[56,384]{1,0:T(8,128)S(1)} %get-tuple-element.38), channel_id=1, source_target_pairs={{0,3},{1,2},{2,1},{3,0},{4,7},{5,6},{6,5},{7,4},{8,11},{9,10},{10,... | collective-permute-start | bytes 258056 | tf_op jit(solution)/shard_map/ppermute | solution.py:382
  21.7 7.3 %collective-permute-start.6 = (s32[56,384]{1,0:T(8,128)S(1)}, s32[56,384]{1,0:T(8,128)S(1)}, u32[]{:S(2)}, u32[]{:S(2)}) collective-permute-start(s32[56,384]{1,0:T(8,128)S(1)} %get-tuple-element.39), channel_id=1, source_target_pairs={{0,2},{1,3},{2,0},{3,1},{4,6},{5,7},{6,4},{7,5},{8,10},{9,11},{10,... | collective-permute-start | bytes 258056 | tf_op jit(solution)/shard_map/ppermute | solution.py:382
  21.7 7.3 %collective-permute-start.7 = (s32[56,384]{1,0:T(8,128)S(1)}, s32[56,384]{1,0:T(8,128)S(1)}, u32[]{:S(2)}, u32[]{:S(2)}) collective-permute-start(s32[56,384]{1,0:T(8,128)S(1)} %get-tuple-element.40), channel_id=1, source_target_pairs={{0,1},{1,0},{2,3},{3,2},{4,5},{5,4},{6,7},{7,6},{8,9},{9,8},{10,11... | collective-permute-start | bytes 258056 | tf_op jit(solution)/shard_map/ppermute | solution.py:382
  30.7 4.5 %collective-permute-start.8 = (bf16[96,128]{1,0:T(8,128)(2,1)S(1)}, bf16[96,128]{1,0:T(8,128)(2,1)S(1)}, u32[]{:S(2)}, u32[]{:S(2)}) collective-permute-start(bf16[96,128]{1,0:T(8,128)(2,1)S(1)} %get-tuple-element.44), channel_id=1, source_target_pairs={{0,3},{1,2},{2,1},{3,0},{4,7},{5,6},{6,5},{7,4},{8,11},{9,10},{10,... | collective-permute-start | bytes 73736 | tf_op jit(solution)/shard_map/ppermute | solution.py:382
  32.4 3.6 %collective-permute-start.9 = (bf16[96,128]{1,0:T(8,128)(2,1)S(1)}, bf16[96,128]{1,0:T(8,128)(2,1)S(1)}, u32[]{:S(2)}, u32[]{:S(2)}) collective-permute-start(bf16[96,128]{1,0:T(8,128)(2,1)S(1)} %get-tuple-element.45), channel_id=1, source_target_pairs={{0,2},{1,3},{2,0},{3,1},{4,6},{5,7},{6,4},{7,5},{8,10},{9,11},{10,... | collective-permute-start | bytes 73736 | tf_op jit(solution)/shard_map/ppermute | solution.py:382
  32.4 3.6 %collective-permute-start.10 = (bf16[96,128]{1,0:T(8,128)(2,1)S(1)}, bf16[96,128]{1,0:T(8,128)(2,1)S(1)}, u32[]{:S(2)}, u32[]{:S(2)}) collective-permute-start(bf16[96,128]{1,0:T(8,128)(2,1)S(1)} %get-tuple-element.46), channel_id=1, source_target_pairs={{0,1},{1,0},{2,3},{3,2},{4,5},{5,4},{6,7},{7,6},{8,9},{9,8},{10,11... | collective-permute-start | bytes 73736 | tf_op jit(solution)/shard_map/ppermute | solution.py:382
  36.1 6.2 %collective-permute-start.11 = (f32[48,128]{1,0:T(8,128)S(1)}, f32[48,128]{1,0:T(8,128)S(1)}, u32[]{:S(2)}, u32[]{:S(2)}) collective-permute-start(f32[48,128]{1,0:T(8,128)S(1)} %get-tuple-element.48), channel_id=1, source_target_pairs={{0,4},{1,5},{4,8},{5,9},{6,2},{7,3},{8,12},{9,13},{10,6},{11,7},{1... | collective-permute-start | bytes 73736 | tf_op jit(solution)/shard_map/ppermute | solution.py:472

commit v6 on v5

--- a/solution.py
+++ b/solution.py
@@ -165,9 +165,56 @@
     send_shares(groups, folded, share, targets)
 
 
+LEFT_BLOCKS = ((0, 1, 2, 3), (2, 3, 6, 7), (4, 0, 1, 2), (6, 0, 4, 5))
+RIGHT_BLOCKS = ((2, 3, 6, 7), (4, 5, 6, 7), (0, 1, 2, 4), (0, 4, 5, 6))
+
+
+def fold_by_column(tile, flipped, folded):
+    owners = len(LEFT_BLOCKS)
+    snps = folded.shape[1]
+    wide = snps // owners
+    size = wide // 2
+    shape = (size, snps)
+    row, lane = iota(shape, 0), iota(shape, 1)
+
+    def block(number):
+        return tile[number * size : (number + 1) * size, :]
+
+    diagonal = block(0)
+    for number in range(1, 2 * owners):
+        diagonal = jnp.where(lane >= number * size, block(number), diagonal)
+    flipped[:, 0:size] = diagonal.T
+    corner = diagonal
+    for owner in range(owners):
+        start = (2 * owner + 1) * size
+        turned = jnp.concatenate(
+            [flipped[start : start + size, :], jnp.zeros((size, snps - LANES), jnp.float32)], axis=1
+        )
+        if owner:
+            turned = pltpu.roll(turned, owner * wide, 1)
+        inside = lane - owner * wide
+        other = (row <= inside) if owner < owners // 2 else (row >= inside)
+        corner = jnp.where((inside >= 0) & (inside < size) & other, turned, corner)
+    rolled = []
+    for shift in range(owners):
+        mixed = None
+        for owner in range(owners):
+            slot = (owner + shift) % owners
+            left = block(LEFT_BLOCKS[owner][slot]) if slot else corner
+            start = owner * wide
+            mixed = left if mixed is None else jnp.where(lane >= start, left, mixed)
+            mixed = jnp.where(lane >= start + size, block(RIGHT_BLOCKS[owner][slot]), mixed)
+        rolled.append(pltpu.roll(mixed, shift * wide, 1) if shift else mixed)
+    for owner in range(owners):
+        mixed = rolled[(0 - owner) % owners]
+        for slot in range(1, owners):
+            mixed = jnp.where(lane >= slot * wide, rolled[(slot - owner) % owners], mixed)
+        folded[owner * size : (owner + 1) * size, :] = to_fields(mixed)
+
+
 def near_kernel(groups, share, weighted_ref, far_ref, close_ref, totals_ref, *refs):
     own_parts, own_sum_ref = refs[:groups], refs[groups]
-    targets, (near, tile, folded) = refs[groups + 1 : 2 * groups + 1], refs[2 * groups + 1 :]
+    targets, (near, tile, folded, flipped) = refs[groups + 1 : 2 * groups + 1], refs[2 * groups + 1 :]
     rows, snps = near.shape
     half = snps // 2
     odd = odd_block()
@@ -188,12 +235,15 @@
         unpack(close_ref, far_ref)
 
     tile[...] = jnp.dot(weighted_ref[...], near[...], preferred_element_type=jnp.float32)
-    row, col = iota((half, snps), 0), iota((half, snps), 1)
-    moved = (col >= half) & (col - half < row)
-    turned = pltpu.roll(tile[0:half, :], half, 1)
-    folded[0:half, :] = to_fields(jnp.where(moved, turned, tile[half:snps, :]))
-    if folded.shape[0] > half:
-        folded[half:, :] = jnp.zeros((folded.shape[0] - half, snps), jnp.int32)
+    if groups == len(LEFT_BLOCKS):
+        fold_by_column(tile, flipped, folded)
+    else:
+        row, col = iota((half, snps), 0), iota((half, snps), 1)
+        moved = (col >= half) & (col - half < row)
+        turned = pltpu.roll(tile[0:half, :], half, 1)
+        folded[0:half, :] = to_fields(jnp.where(moved, turned, tile[half:snps, :]))
+        if folded.shape[0] > half:
+            folded[half:, :] = jnp.zeros((folded.shape[0] - half, snps), jnp.int32)
     square = (snps, snps)
     far = jnp.sum(
         jnp.where(iota(square, 0) == iota(square, 1), tile[0:snps, :], 0.0), axis=0, keepdims=True
@@ -359,6 +409,169 @@
     send_shares(groups, scores, out_share, targets)
 
 
+def pack_halves(values):
+    half = values.shape[0] // 2
+    left = iota((half, LANES), 1) < HALF_LANES
+    return jnp.where(left, values[0:half], pltpu.roll(values[half:], HALF_LANES, 1))
+
+
+def unpack_halves(packed):
+    return jnp.concatenate([packed, pltpu.roll(packed, HALF_LANES, 1)], axis=0)
+
+
+def column_score_kernel(groups, share, reach_ref, *refs):
+    own_sum_ref, near_parts = refs[0], refs[1 : groups + 1]
+    annot_ref, near_annot_ref = refs[groups + 1 : groups + 3]
+    out_ref, *targets = refs[groups + 3 : 2 * groups + 3]
+    near_out_ref, table, flipped, scores = refs[2 * groups + 3 :]
+    snps = annot_ref.shape[0]
+    half = snps // 2
+    wide = snps // groups
+    size = wide // 2
+    me = lax.axis_index("hap")
+    block = lax.axis_index("snp")
+    last = reach_ref.shape[0] - 1
+    upper = me < groups // 2
+    reach_here = reach_ref[block]
+    reach_there = jnp.where(
+        upper, reach_ref[jnp.minimum(block + 1, last)], reach_ref[jnp.maximum(block - 1, 0)]
+    )
+
+    def mine(choices):
+        value = choices[0]
+        for group in range(1, groups):
+            value = jnp.where(me == group, choices[group], value)
+        return value
+
+    own_counts = own_sum_ref[...]
+    near_sums = sum((part[...] for part in near_parts[1:]), near_parts[0][...])
+    extras = from_fields(near_sums[share:, :])
+    near_counts = near_sums[0:share, :]
+
+    own_stats, near_stats, lines = [], [], []
+    for pop in range(2):
+        count = extras[pop][1:2, :]
+        own_stats.append(column_stats(extras[pop][0:1, :], count))
+        near_stats.append(column_stats(extras[pop][2:3, :], count))
+        lines += [*own_stats[pop], *near_stats[pop], extras[pop][0:1, :], extras[pop][3:4, :]]
+    table[:, 0:16] = jnp.concatenate(lines, axis=0).T
+
+    low_rows = pl.multiple_of(me * share, 8)
+    high_rows = pl.multiple_of(half + me * share, 8)
+
+    def both(ref):
+        return jnp.concatenate([ref[pl.ds(low_rows, share), :], ref[pl.ds(high_rows, share), :]], axis=0)
+
+    here = both(table)
+    own_fields = from_fields(
+        jnp.concatenate([pltpu.roll(own_counts, half, 1), own_counts], axis=0)
+    )
+    shape = (2 * share, snps)
+    local, col = iota(shape, 0), iota(shape, 1)
+    low = local < share
+    row = jnp.where(low, local, local + half - share) + me * share
+    product = 1.0
+    for pop in range(2):
+        row_stats = [here[:, 8 * pop + k : 8 * pop + k + 1] for k in range(3)]
+        product *= correlation(row_stats, own_stats[pop], own_fields[pop])
+    inside = (low & (col > row)) | (~low & (col >= half) & (col < row))
+    own_kept = jnp.where(inside & (jnp.abs(col - row) <= reach_here), product, 0.0)
+    rows_here = both(annot_ref).astype(jnp.bfloat16)
+    scores[...] = dot_split(own_kept, rows_here, 0)
+    direct = dot_split(own_kept, annot_ref[...].astype(jnp.bfloat16), 1)
+    scores[pl.ds(low_rows, share), :] += direct[0:share, :]
+    scores[pl.ds(high_rows, share), :] += direct[share:, :]
+
+    slots = [near_counts[:, 0:LANES]]
+    for slot in range(1, groups):
+        slots.append(pltpu.roll(near_counts, snps - slot * wide, 1)[:, 0:LANES])
+    flipped[:, 0:size] = slots[0].T
+    slots.append(pltpu.roll(flipped[0:size, :], size, 1))
+    left_places = [mine([LEFT_BLOCKS[g][slot] for g in range(groups)]) * size for slot in range(groups)]
+    right_places = [mine([RIGHT_BLOCKS[g][slot] for g in range(groups)]) * size for slot in range(groups)]
+    left_places.append(left_places[0])
+    right_places.append((2 * me + 1) * size)
+
+    def rows_of(ref, places):
+        return [ref[pl.ds(pl.multiple_of(place, 8), size), :] for place in places]
+
+    near_fields = from_fields(jnp.concatenate(slots, axis=0))
+    left_table = jnp.concatenate(rows_of(table, left_places), axis=0)
+    right_table = jnp.concatenate(rows_of(table, right_places), axis=0)
+    local, lane = iota((size, LANES), 0), iota((size, LANES), 1)
+    is_left = lane < size
+    own_row = jnp.concatenate(
+        [local + jnp.where(is_left, a, b) for a, b in zip(left_places, right_places)], axis=0
+    )
+    shape = own_row.shape
+    lane = iota(shape, 1)
+    is_left = lane < size
+    apart = jnp.abs(own_row - (lane + me * wide))
+    ahead = (own_row - (lane + me * wide)) * jnp.where(upper, 1, -1) > 0
+    real = ahead & (lane < wide) & ((lane >= size) | (iota(shape, 0) < groups * size))
+    near_lines = jnp.concatenate([*near_stats[0], *near_stats[1], *near_stats[0][0:2]], axis=0)
+    near_lines = mine(
+        [near_lines[:, 0:LANES]]
+        + [pltpu.roll(near_lines, snps - group * wide, 1)[:, 0:LANES] for group in range(1, groups)]
+    )
+    product = 1.0
+    for pop in range(2):
+        row_stats = [
+            jnp.where(
+                is_left,
+                left_table[:, 8 * pop + k : 8 * pop + k + 1],
+                right_table[:, 8 * pop + k : 8 * pop + k + 1],
+            )
+            for k in range(3)
+        ]
+        col_stats = [near_lines[3 * pop + k : 3 * pop + k + 1, :] for k in range(3)]
+        product *= correlation(row_stats, col_stats, near_fields[pop])
+    near_here = jnp.where(real & (snps - apart <= reach_here), product, 0.0)
+    near_there = jnp.where(real & (snps - apart <= reach_there), product, 0.0)
+
+    def sides(values):
+        return jnp.concatenate(
+            [jnp.where(is_left, values, 0.0), jnp.where(is_left, 0.0, values)], axis=0
+        )
+
+    slice_rows = pl.ds(pl.multiple_of(me * wide, 8), wide)
+    their_annots = near_annot_ref[slice_rows, :]
+    columns = jnp.concatenate([their_annots, jnp.zeros((LANES - wide, LANES), jnp.float32)], axis=0)
+    direct = dot_split(sides(near_here), columns.astype(jnp.bfloat16), 1)
+    places = left_places + right_places
+    for number, place in enumerate(places):
+        scores[pl.ds(pl.multiple_of(place, 8), size), :] += direct[number * size : (number + 1) * size, :]
+    own_rows = jnp.concatenate(rows_of(annot_ref, places), axis=0).astype(jnp.bfloat16)
+    near_scores = dot_split(sides(near_there), own_rows, 0)[0:wide, :]
+
+    mine_table = table[slice_rows, :]
+    self_product, far_product = 1.0, 1.0
+    for pop in range(2):
+        k = 8 * pop
+        own_row = [mine_table[:, k + s : k + s + 1] for s in range(3)]
+        near_row = [mine_table[:, k + 3 + s : k + 4 + s] for s in range(3)]
+        self_product *= correlation(own_row, own_row, mine_table[:, k + 6 : k + 7])
+        far_product *= correlation(own_row, near_row, mine_table[:, k + 7 : k + 8])
+    my_annots = annot_ref[slice_rows, :]
+    out_ref[...] = (
+        scores[slice_rows, :]
+        + my_annots * self_product
+        + their_annots * jnp.where(reach_here >= snps, far_product, 0.0)
+    )
+    near_scores += my_annots * jnp.where(reach_there >= snps, far_product, 0.0)
+    near_out_ref[...] = pack_halves(near_scores)
+    for step, target in enumerate(targets, 1):
+        group = partner(me, step, groups)
+        rows = scores[pl.ds(pl.multiple_of(group * wide, 8), wide), :]
+        target[...] = pack_halves(rows).astype(target.dtype)
+
+
+def column_finish_kernel(own_ref, there_ref, *refs):
+    *parts, out_ref = refs
+    packed = sum((part[...].astype(jnp.float32) for part in parts), there_ref[...])
+    out_ref[...] = (own_ref[...] + unpack_halves(packed)).T[0 : out_ref.shape[0], :]
+
+
 def sum_kernel(*refs):
     *parts, own_ref, there_ref = refs
     total = sum((part[...].astype(jnp.float32) for part in parts[1:]), parts[0][...])
@@ -437,7 +650,7 @@
         functools.partial(near_kernel, groups, share),
         [shape((share, snps), i32)] + [shape((share + 8, snps), i32)] * groups,
         [VMEM] * (4 + groups),
-        [pltpu.VMEM((rows, snps), bf16), tile, folded],
+        [pltpu.VMEM((rows, snps), bf16), tile, folded, pltpu.VMEM((snps, LANES), f32)],
         flops=2 * rows * snps * snps,
         moved=rows * snps * 4,
     )(weighted, from_far, from_close, totals, *own_parts)
@@ -447,30 +660,45 @@
     own_annots, near_annots = call(annots_kernel, [by_snp, by_snp], [VMEM] * 3, moved=1 << 20)(
         annotations, from_far[rows // 2 :], from_close[rows // 2 :]
     )
+    pairs = []
+    for block in range(blocks):
+        for group in range(groups):
+            target = block + 1 if group < groups // 2 else block - 1
+            if 0 <= target < blocks:
+                pairs.append((block * groups + group, target * groups + group))
+
+    def to_neighbour(value):
+        return lax.ppermute(value, ("snp", "hap"), pairs)
+
+    result = shape((annotations.shape[0], out_share), f32)
+    half_share = round_up(-(-out_share // 2), 8)
+    own_share = shape((out_share, LANES), f32)
+    packed_share = shape((half_share, LANES), f32)
+    if groups == len(LEFT_BLOCKS):
+        own_scores, *scores, near_scores = call(
+            functools.partial(column_score_kernel, groups, share),
+            [own_share] + [shape((half_share, LANES), bf16)] * (groups - 1) + [packed_share],
+            [SMEM] + [VMEM] * (groups + 3),
+            [pltpu.VMEM((snps, LANES), f32), pltpu.VMEM((LANES, LANES), i32), pltpu.VMEM((snps, LANES), f32)],
+            flops=1 << 26,
+            moved=1 << 21,
+        )(reach, own_sum, *near_parts, own_annots, near_annots)
+        scores = [around(scores[k - 1], groups, k) for k in range(groups - 1, 0, -1)]
+        there = to_neighbour(near_scores)
+        return call(column_finish_kernel, result, [VMEM] * (groups + 1))(own_scores, there, *scores)
+
     tall = pltpu.VMEM((padded, LANES), f32)
     scores = call(
         functools.partial(score_kernel, groups, share),
-        [shape((out_share, LANES), f32)] + [shape((out_share, LANES), bf16)] * (groups - 1),
+        [own_share] + [shape((out_share, LANES), bf16)] * (groups - 1),
         [SMEM] + [VMEM] * (groups + 3),
         [tall, tall, tall, tall],
         flops=1 << 26,
         moved=1 << 21,
     )(reach, own_sum, *near_parts, own_annots, near_annots)
     scores = [scores[0]] + [around(scores[k], groups, k) for k in range(groups - 1, 0, -1)]
-    half_share = round_up(-(-out_share // 2), 8)
-    own_scores, near_scores = call(
-        sum_kernel,
-        [shape((out_share, LANES), f32), shape((half_share, LANES), f32)],
-        [VMEM] * groups,
-    )(*scores)
-    pairs = []
-    for block in range(blocks):
-        for group in range(groups):
-            target = block + 1 if group < groups // 2 else block - 1
-            if 0 <= target < blocks:
-                pairs.append((block * groups + group, target * groups + group))
-    there = lax.ppermute(near_scores, ("snp", "hap"), pairs)
-    return call(finish_kernel, shape((annotations.shape[0], out_share), f32), [VMEM] * 2)(own_scores, there)
+    own_scores, near_scores = call(sum_kernel, [own_share, packed_share], [VMEM] * groups)(*scores)
+    return call(finish_kernel, result, [VMEM] * 2)(own_scores, to_neighbour(near_scores))
 
 
 def solution(mesh):

time: 43.2 us -> 41.4 us (0.958); the launches traced: 43 us -> 40.6 us
  starting transfers between devices: 20.8 us -> 18.9 us
  waiting for transfers between devices: 14.7 us -> 13.6 us
  Pallas kernels: 7.38 us -> 8.1 us
    ppermute x1, starting transfers between devices: 5.28 us -> 3.3 us  [to_neighbour(): return lax.ppermute(value, ('snp', 'hap'), pairs)]
    ppermute x1, waiting for transfers between devices: 0.92 us -> 0.01 us  [to_neighbour(): return lax.ppermute(value, ('snp', 'hap'), pairs)]
    pallas_call x3 -> x2, Pallas kernels: 2.44 us -> 2.91 us  [the longest x1 2.15 us: per_device(): call(functools.partial(column_score_kernel, groups, share), [own_share] +...]
  transfers between devices with their start and end apart: 12 -> 12, of which waited for: 7 -> 6; matrix products, arithmetic and copies ran while one was open for 0% -> 0% of each run, Pallas kernels for 3% -> 3%
where the time goes in v6:
time: 41.4 us; the launch traced here: 40.6 us
  starting transfers between devices  18.9 us (46%)
  waiting for transfers between devices  13.6 us (33%)
  Pallas kernels  8.1 us (20%)
    ppermute x9, waiting for transfers between devices, around(): lax.ppermute(value, 'hap', [(source, partner(source, step, groups)) for s...  13.6 us
    ppermute x9, starting transfers between devices, around(): lax.ppermute(value, 'hap', [(source, partner(source, step, groups)) for s...  11 us
    ppermute x2, starting transfers between devices, swapped(): return lax.ppermute(value, 'snp', pairs)  4.58 us
    ppermute x1, starting transfers between devices, to_neighbour(): return lax.ppermute(value, ('snp', 'hap'), pairs)  3.3 us
    pallas_call x1, Pallas kernels, per_device(): call(functools.partial(column_score_kernel, groups, share), [own_share] +...  2.15 us
    pallas_call x1, Pallas kernels, per_device(): call(prepare_kernel, [shape((rows, snps), bf16), packed, packed], [HBM, H...  2.14 us
    pallas_call x1, Pallas kernels, per_device(): call(functools.partial(near_kernel, groups, share), [shape((share, snps),...  1.65 us
    pallas_call x1, Pallas kernels, per_device(): call(functools.partial(own_kernel, groups, share), [shape((snps + 16, row...  1.13 us
  transfers between devices with their start and end apart: 12, of which 6 were waited for; matrix products, arithmetic and copies ran while one was open for 0% of the time, Pallas kernels for 3%

profile of v6, /device:TPU:1, one launch (start us, length us, event | category | flops | bytes accessed | tf_op | source)
XLA Modules:
  0.0 40.6 jit_solution(1256692712637192110)
XLA Ops:
  0.0 0.0 copy-start.2
  0.0 2.1 %shard_map.46 = (bf16[2048,384]{1,0:T(8,128)(2,1)S(1)}, bf16[1056,384]{1,0:T(8,128)(2,1)S(1)}, bf16[1056,384]{1,0:T(8,128)(2,1)S(1)}) custom-call(s32[2048,384]{1,0:T(8,128)} %hap_ref.1, s32[50,384]{1,0:T(8,128)} %annot_ref.3), custom_call_target="tpu_custom_call" | custom-call | bytes 6291456 | tf_op jit(solution)/shard_map/pallas_call | solution.py:623
  2.1 4.5 %collective-permute-start = (bf16[1056,384]{1,0:T(8,128)(2,1)S(1)}, bf16[1056,384]{1,0:T(8,128)(2,1)S(1)}, u32[]{:S(2)}, u32[]{:S(2)}) collective-permute-start(bf16[1056,384]{1,0:T(8,128)(2,1)S(1)} %get-tuple-element.28), channel_id=1, source_target_pairs={{4,8},{8,4},{5,9},{9,5},{6,10},{10,6},{7,11},{11,7},{20,24},{24,20... | collective-permute-start | bytes 2433032 | tf_op jit(solution)/shard_map/ppermute | solution.py:604
  6.7 0.1 collective-permute-start.1
  6.7 0.0 copy-done.2
  6.8 1.1 %shard_map.47 = (bf16[400,2048]{1,0:T(8,128)(2,1)S(1)}, f32[8,384]{1,0:T(8,128)S(1)}, s32[48,384]{1,0:T(8,128)S(1)}, s32[48,384]{1,0:T(8,128)S(1)}, s32[48,384]{1,0:T(8,128)S(1)}, /*index=5*/s32[48,384]{1,0:T(8,128)S(1)}) custom-call(bf16[2048,384]{1,0:T(8,128)(2,1)S(1)} %get-tuple-element.26.alleles_ref, s32[1,2048]{1,0:T(1,128)S(1)} %bitcast.1), custom_call_target="tpu_custom_call" | custom-call | flops 603979776 | bytes 3145728 | tf_op jit(solution)/shard_map/pallas_call | solution.py:639
  7.9 3.4 %collective-permute-start.2 = (s32[48,384]{1,0:T(8,128)S(1)}, s32[48,384]{1,0:T(8,128)S(1)}, u32[]{:S(2)}, u32[]{:S(2)}) collective-permute-start(s32[48,384]{1,0:T(8,128)S(1)} %get-tuple-element.32), channel_id=1, source_target_pairs={{0,3},{1,2},{2,1},{3,0},{4,7},{5,6},{6,5},{7,4},{8,11},{9,10},{10,... | collective-permute-start | bytes 221192 | tf_op jit(solution)/shard_map/ppermute | solution.py:595
  11.3 0.0 collective-permute-start.3
  11.3 0.4 collective-permute-start.4
  11.6 1.5 %collective-permute-done.2.refs_1_ = s32[48,384]{1,0:T(8,128)S(1)} collective-permute-done((s32[48,384]{1,0:T(8,128)S(1)}, s32[48,384]{1,0:T(8,128)S(1)}, u32[]{:S(2)}, u32[]{:S(2)}) %collective-permute-start.2) | collective-permute-done | bytes 73760 | tf_op jit(solution)/shard_map/ppermute | solution.py:595
  13.1 4.3 %collective-permute-done.3.refs_2_ = s32[48,384]{1,0:T(8,128)S(1)} collective-permute-done((s32[48,384]{1,0:T(8,128)S(1)}, s32[48,384]{1,0:T(8,128)S(1)}, u32[]{:S(2)}, u32[]{:S(2)}) %collective-permute-start.3) | collective-permute-done | bytes 73760 | tf_op jit(solution)/shard_map/ppermute | solution.py:595
  17.4 0.0 collective-permute-done.4.refs_3_
  17.4 0.0 collective-permute-done.far_ref
  17.4 0.0 collective-permute-done.1.close_ref
  17.4 0.0 copy-start
  17.4 0.0 copy-start.1
  17.4 1.6 %shard_map.48 = (s32[48,384]{1,0:T(8,128)S(1)}, s32[56,384]{1,0:T(8,128)S(1)}, s32[56,384]{1,0:T(8,128)S(1)}, s32[56,384]{1,0:T(8,128)S(1)}, s32[56,384]{1,0:T(8,128)S(1)}) custom-call(bf16[400,2048]{1,0:T(8,128)(2,1)S(1)} %get-tuple-element.27.weighted_ref, bf16[1056,384]{1,0:T(8,128)(2,1)S(1)} %collective-permute-done.far_ref, ...), custom_call_target="tpu_custom_call" | custom-call | flops 603979776 | bytes 3145728 | tf_op jit(solution)/shard_map/pallas_call | solution.py:649
  19.1 2.8 %collective-permute-start.5 = (s32[56,384]{1,0:T(8,128)S(1)}, s32[56,384]{1,0:T(8,128)S(1)}, u32[]{:S(2)}, u32[]{:S(2)}) collective-permute-start(s32[56,384]{1,0:T(8,128)S(1)} %get-tuple-element.37), channel_id=1, source_target_pairs={{0,3},{1,2},{2,1},{3,0},{4,7},{5,6},{6,5},{7,4},{8,11},{9,10},{10,... | collective-permute-start | bytes 258056 | tf_op jit(solution)/shard_map/ppermute | solution.py:595
  21.9 0.0 collective-permute-start.6
  21.9 0.8 %collective-permute-start.7 = (s32[56,384]{1,0:T(8,128)S(1)}, s32[56,384]{1,0:T(8,128)S(1)}, u32[]{:S(2)}, u32[]{:S(2)}) collective-permute-start(s32[56,384]{1,0:T(8,128)S(1)} %get-tuple-element.39), channel_id=1, source_target_pairs={{0,1},{1,0},{2,3},{3,2},{4,5},{5,4},{6,7},{7,6},{8,9},{9,8},{10,11... | collective-permute-start | bytes 258056 | tf_op jit(solution)/shard_map/ppermute | solution.py:595
  22.7 0.0 copy-done
  22.7 0.3 shard_map.49
  23.0 1.4 %collective-permute-done.5.refs_2_ = s32[56,384]{1,0:T(8,128)S(1)} collective-permute-done((s32[56,384]{1,0:T(8,128)S(1)}, s32[56,384]{1,0:T(8,128)S(1)}, u32[]{:S(2)}, u32[]{:S(2)}) %collective-permute-start.5) | collective-permute-done | bytes 86048 | tf_op jit(solution)/shard_map/ppermute | solution.py:595
  24.4 4.9 %collective-permute-done.6.refs_3_ = s32[56,384]{1,0:T(8,128)S(1)} collective-permute-done((s32[56,384]{1,0:T(8,128)S(1)}, s32[56,384]{1,0:T(8,128)S(1)}, u32[]{:S(2)}, u32[]{:S(2)}) %collective-permute-start.6) | collective-permute-done | bytes 86048 | tf_op jit(solution)/shard_map/ppermute | solution.py:595
  29.3 0.0 collective-permute-done.7.refs_4_
  29.3 0.0 copy-done.1
  29.3 2.2 %shard_map.50 = (f32[96,128]{1,0:T(8,128)S(1)}, bf16[48,128]{1,0:T(8,128)(2,1)S(1)}, bf16[48,128]{1,0:T(8,128)(2,1)S(1)}, bf16[48,128]{1,0:T(8,128)(2,1)S(1)}, f32[48,128]{1,0:T(8,128)S(1)}) custom-call(s32[4]{0:T(128)S(1)} %copy-done.1, s32[48,384]{1,0:T(8,128)S(1)} %get-tuple-element.35.refs_0_, s32[56,384]{1,0:T(8,128)S(1)} %get-tuple-element.36.refs_1_, ...), custom_call_target="tpu_custom_call" | custom-call | flops 67108864 | bytes 2097152 | tf_op jit(solution)/shard_map/pallas_call | solution.py:678
  31.5 3.3 %collective-permute-start.8 = (f32[48,128]{1,0:T(8,128)S(1)}, f32[48,128]{1,0:T(8,128)S(1)}, u32[]{:S(2)}, u32[]{:S(2)}) collective-permute-start(f32[48,128]{1,0:T(8,128)S(1)} %get-tuple-element.43), channel_id=1, source_target_pairs={{0,4},{1,5},{4,8},{5,9},{6,2},{7,3},{8,12},{9,13},{10,6},{11,7},{1... | collective-permute-start | bytes 73736 | tf_op jit(solution)/shard_map/ppermute | solution.py:671
  34.8 1.4 %collective-permute-start.9 = (bf16[48,128]{1,0:T(8,128)(2,1)S(1)}, bf16[48,128]{1,0:T(8,128)(2,1)S(1)}, u32[]{:S(2)}, u32[]{:S(2)}) collective-permute-start(bf16[48,128]{1,0:T(8,128)(2,1)S(1)} %get-tuple-element.44), channel_id=1, source_target_pairs={{0,3},{1,2},{2,1},{3,0},{4,7},{5,6},{6,5},{7,4},{8,11},{9,10},{10,... | collective-permute-start | bytes 36872 | tf_op jit(solution)/shard_map/ppermute | solution.py:595
  36.1 0.0 collective-permute-start.10
  36.1 2.2 %collective-permute-start.11 = (bf16[48,128]{1,0:T(8,128)(2,1)S(1)}, bf16[48,128]{1,0:T(8,128)(2,1)S(1)}, u32[]{:S(2)}, u32[]{:S(2)}) collective-permute-start(bf16[48,128]{1,0:T(8,128)(2,1)S(1)} %get-tuple-element.46), channel_id=1, source_target_pairs={{0,1},{1,0},{2,3},{3,2},{4,5},{5,4},{6,7},{7,6},{8,9},{9,8},{10,11... | collective-permute-start | bytes 36872 | tf_op jit(solution)/shard_map/ppermute | solution.py:595
  38.4 0.8 %collective-permute-done.9.refs_0_ = bf16[48,128]{1,0:T(8,128)(2,1)S(1)} collective-permute-done((bf16[48,128]{1,0:T(8,128)(2,1)S(1)}, bf16[48,128]{1,0:T(8,128)(2,1)S(1)}, u32[]{:S(2)}, u32[]{:S(2)}) %collective-permute-start.9) | collective-permute-done | bytes 12320 | tf_op jit(solution)/shard_map/ppermute | solution.py:595
  39.2 0.7 %collective-permute-done.10.refs_1_ = bf16[48,128]{1,0:T(8,128)(2,1)S(1)} collective-permute-done((bf16[48,128]{1,0:T(8,128)(2,1)S(1)}, bf16[48,128]{1,0:T(8,128)(2,1)S(1)}, u32[]{:S(2)}, u32[]{:S(2)}) %collective-permute-start.10) | collective-permute-done | bytes 12320 | tf_op jit(solution)/shard_map/ppermute | solution.py:595
  39.9 0.0 collective-permute-done.11.refs_2_
  39.9 0.0 collective-permute-done.8.there_ref
  39.9 0.8 %shard_map.51 = f32[50,96]{1,0:T(8,128)} custom-call(f32[96,128]{1,0:T(8,128)S(1)} %get-tuple-element.42.own_ref, f32[48,128]{1,0:T(8,128)S(1)} %collective-permute-done.8.there_ref, bf16[48,128]{1,0:T(8,128)(2,1)S(1)} %collective-permute-done.9.refs_0_, bf16[48,128]{1,0:T(8,128)(2,1)S(1)} %collective-permute-done.10.refs_1_, ...), custom_call_target="tpu_custom_call" | custom-call | tf_op jit(solution)/shard_map/pallas_call | solution.py:688
  (2 shorter events, 0.0 us)
Async XLA Ops:
  0.0 6.7 %copy-start.2 = (s32[2048]{0:T(1024)S(1)}, s32[2048]{0:T(1024)}, u32[]{:S(2)}) copy-start(s32[2048]{0:T(1024)} %param.5) | copy-start | bytes 24580
  2.1 15.3 %collective-permute-start = (bf16[1056,384]{1,0:T(8,128)(2,1)S(1)}, bf16[1056,384]{1,0:T(8,128)(2,1)S(1)}, u32[]{:S(2)}, u32[]{:S(2)}) collective-permute-start(bf16[1056,384]{1,0:T(8,128)(2,1)S(1)} %get-tuple-element.28), channel_id=1, source_target_pairs={{4,8},{8,4},{5,9},{9,5},{6,10},{10,6},{7,11},{11,7},{20,24},{24,20... | collective-permute-start | bytes 2433032 | tf_op jit(solution)/shard_map/ppermute | solution.py:604
  6.7 10.8 %collective-permute-start.1 = (bf16[1056,384]{1,0:T(8,128)(2,1)S(1)}, bf16[1056,384]{1,0:T(8,128)(2,1)S(1)}, u32[]{:S(2)}, u32[]{:S(2)}) collective-permute-start(bf16[1056,384]{1,0:T(8,128)(2,1)S(1)} %get-tuple-element.29), channel_id=1, source_target_pairs={{0,4},{4,0},{8,12},{12,8},{1,5},{5,1},{9,13},{13,9},{2,6},{6,2},{1... | collective-permute-start | bytes 2433032 | tf_op jit(solution)/shard_map/ppermute | solution.py:604
  7.9 5.2 %collective-permute-start.2 = (s32[48,384]{1,0:T(8,128)S(1)}, s32[48,384]{1,0:T(8,128)S(1)}, u32[]{:S(2)}, u32[]{:S(2)}) collective-permute-start(s32[48,384]{1,0:T(8,128)S(1)} %get-tuple-element.32), channel_id=1, source_target_pairs={{0,3},{1,2},{2,1},{3,0},{4,7},{5,6},{6,5},{7,4},{8,11},{9,10},{10,... | collective-permute-start | bytes 221192 | tf_op jit(solution)/shard_map/ppermute | solution.py:595
  11.3 6.1 %collective-permute-start.3 = (s32[48,384]{1,0:T(8,128)S(1)}, s32[48,384]{1,0:T(8,128)S(1)}, u32[]{:S(2)}, u32[]{:S(2)}) collective-permute-start(s32[48,384]{1,0:T(8,128)S(1)} %get-tuple-element.33), channel_id=1, source_target_pairs={{0,2},{1,3},{2,0},{3,1},{4,6},{5,7},{6,4},{7,5},{8,10},{9,11},{10,... | collective-permute-start | bytes 221192 | tf_op jit(solution)/shard_map/ppermute | solution.py:595
  11.3 6.1 %collective-permute-start.4 = (s32[48,384]{1,0:T(8,128)S(1)}, s32[48,384]{1,0:T(8,128)S(1)}, u32[]{:S(2)}, u32[]{:S(2)}) collective-permute-start(s32[48,384]{1,0:T(8,128)S(1)} %get-tuple-element.34), channel_id=1, source_target_pairs={{0,1},{1,0},{2,3},{3,2},{4,5},{5,4},{6,7},{7,6},{8,9},{9,8},{10,11... | collective-permute-start | bytes 221192 | tf_op jit(solution)/shard_map/ppermute | solution.py:595
  17.4 5.3 %copy-start = (s32[50,384]{1,0:T(8,128)S(1)}, s32[50,384]{1,0:T(8,128)}, u32[]{:S(2)}) copy-start(s32[50,384]{1,0:T(8,128)} %annot_ref.3) | copy-start | bytes 230404
  17.4 11.9 %copy-start.1 = (s32[4]{0:T(128)S(1)}, s32[4]{0:T(128)}, u32[]{:S(2)}) copy-start(s32[4]{0:T(128)} %reach_ref.1) | copy-start | bytes 52
  19.1 5.3 %collective-permute-start.5 = (s32[56,384]{1,0:T(8,128)S(1)}, s32[56,384]{1,0:T(8,128)S(1)}, u32[]{:S(2)}, u32[]{:S(2)}) collective-permute-start(s32[56,384]{1,0:T(8,128)S(1)} %get-tuple-element.37), channel_id=1, source_target_pairs={{0,3},{1,2},{2,1},{3,0},{4,7},{5,6},{6,5},{7,4},{8,11},{9,10},{10,... | collective-permute-start | bytes 258056 | tf_op jit(solution)/shard_map/ppermute | solution.py:595
  21.9 7.4 %collective-permute-start.6 = (s32[56,384]{1,0:T(8,128)S(1)}, s32[56,384]{1,0:T(8,128)S(1)}, u32[]{:S(2)}, u32[]{:S(2)}) collective-permute-start(s32[56,384]{1,0:T(8,128)S(1)} %get-tuple-element.38), channel_id=1, source_target_pairs={{0,2},{1,3},{2,0},{3,1},{4,6},{5,7},{6,4},{7,5},{8,10},{9,11},{10,... | collective-permute-start | bytes 258056 | tf_op jit(solution)/shard_map/ppermute | solution.py:595
  21.9 7.4 %collective-permute-start.7 = (s32[56,384]{1,0:T(8,128)S(1)}, s32[56,384]{1,0:T(8,128)S(1)}, u32[]{:S(2)}, u32[]{:S(2)}) collective-permute-start(s32[56,384]{1,0:T(8,128)S(1)} %get-tuple-element.39), channel_id=1, source_target_pairs={{0,1},{1,0},{2,3},{3,2},{4,5},{5,4},{6,7},{7,6},{8,9},{9,8},{10,11... | collective-permute-start | bytes 258056 | tf_op jit(solution)/shard_map/ppermute | solution.py:595
  31.5 8.4 %collective-permute-start.8 = (f32[48,128]{1,0:T(8,128)S(1)}, f32[48,128]{1,0:T(8,128)S(1)}, u32[]{:S(2)}, u32[]{:S(2)}) collective-permute-start(f32[48,128]{1,0:T(8,128)S(1)} %get-tuple-element.43), channel_id=1, source_target_pairs={{0,4},{1,5},{4,8},{5,9},{6,2},{7,3},{8,12},{9,13},{10,6},{11,7},{1... | collective-permute-start | bytes 73736 | tf_op jit(solution)/shard_map/ppermute | solution.py:671
  34.8 4.4 %collective-permute-start.9 = (bf16[48,128]{1,0:T(8,128)(2,1)S(1)}, bf16[48,128]{1,0:T(8,128)(2,1)S(1)}, u32[]{:S(2)}, u32[]{:S(2)}) collective-permute-start(bf16[48,128]{1,0:T(8,128)(2,1)S(1)} %get-tuple-element.44), channel_id=1, source_target_pairs={{0,3},{1,2},{2,1},{3,0},{4,7},{5,6},{6,5},{7,4},{8,11},{9,10},{10,... | collective-permute-start | bytes 36872 | tf_op jit(solution)/shard_map/ppermute | solution.py:595
  36.1 3.7 %collective-permute-start.10 = (bf16[48,128]{1,0:T(8,128)(2,1)S(1)}, bf16[48,128]{1,0:T(8,128)(2,1)S(1)}, u32[]{:S(2)}, u32[]{:S(2)}) collective-permute-start(bf16[48,128]{1,0:T(8,128)(2,1)S(1)} %get-tuple-element.45), channel_id=1, source_target_pairs={{0,2},{1,3},{2,0},{3,1},{4,6},{5,7},{6,4},{7,5},{8,10},{9,11},{10,... | collective-permute-start | bytes 36872 | tf_op jit(solution)/shard_map/ppermute | solution.py:595
  36.1 3.7 %collective-permute-start.11 = (bf16[48,128]{1,0:T(8,128)(2,1)S(1)}, bf16[48,128]{1,0:T(8,128)(2,1)S(1)}, u32[]{:S(2)}, u32[]{:S(2)}) collective-permute-start(bf16[48,128]{1,0:T(8,128)(2,1)S(1)} %get-tuple-element.46), channel_id=1, source_target_pairs={{0,1},{1,0},{2,3},{3,2},{4,5},{5,4},{6,7},{7,6},{8,9},{9,8},{10,11... | collective-permute-start | bytes 36872 | tf_op jit(solution)/shard_map/ppermute | solution.py:595

commit v7 on v6

--- a/solution.py
+++ b/solution.py
@@ -169,10 +169,11 @@
 RIGHT_BLOCKS = ((2, 3, 6, 7), (4, 5, 6, 7), (0, 1, 2, 4), (0, 4, 5, 6))
 
 
-def fold_by_column(tile, flipped, folded):
-    owners = len(LEFT_BLOCKS)
+def fold_by_column(tile, flipped, folded, first):
+    groups = len(LEFT_BLOCKS)
+    owners = range(first, first + groups // 2)
     snps = folded.shape[1]
-    wide = snps // owners
+    wide = snps // groups
     size = wide // 2
     shape = (size, snps)
     row, lane = iota(shape, 0), iota(shape, 1)
@@ -180,12 +181,12 @@
     def block(number):
         return tile[number * size : (number + 1) * size, :]
 
-    diagonal = block(0)
-    for number in range(1, 2 * owners):
+    diagonal = block(2 * first)
+    for number in range(2 * first + 1, 2 * first + groups):
         diagonal = jnp.where(lane >= number * size, block(number), diagonal)
     flipped[:, 0:size] = diagonal.T
     corner = diagonal
-    for owner in range(owners):
+    for owner in owners:
         start = (2 * owner + 1) * size
         turned = jnp.concatenate(
             [flipped[start : start + size, :], jnp.zeros((size, snps - LANES), jnp.float32)], axis=1
@@ -193,28 +194,84 @@
         if owner:
             turned = pltpu.roll(turned, owner * wide, 1)
         inside = lane - owner * wide
-        other = (row <= inside) if owner < owners // 2 else (row >= inside)
+        other = (row <= inside) if first == 0 else (row >= inside)
         corner = jnp.where((inside >= 0) & (inside < size) & other, turned, corner)
     rolled = []
-    for shift in range(owners):
+    for shift in range(groups):
         mixed = None
-        for owner in range(owners):
-            slot = (owner + shift) % owners
+        for owner in owners:
+            slot = (owner + shift) % groups
             left = block(LEFT_BLOCKS[owner][slot]) if slot else corner
             start = owner * wide
             mixed = left if mixed is None else jnp.where(lane >= start, left, mixed)
             mixed = jnp.where(lane >= start + size, block(RIGHT_BLOCKS[owner][slot]), mixed)
         rolled.append(pltpu.roll(mixed, shift * wide, 1) if shift else mixed)
-    for owner in range(owners):
-        mixed = rolled[(0 - owner) % owners]
-        for slot in range(1, owners):
-            mixed = jnp.where(lane >= slot * wide, rolled[(slot - owner) % owners], mixed)
-        folded[owner * size : (owner + 1) * size, :] = to_fields(mixed)
+    for owner in owners:
+        mixed = rolled[(0 - owner) % groups]
+        for slot in range(1, groups):
+            mixed = jnp.where(lane >= slot * wide, rolled[(slot - owner) % groups], mixed)
+        where = slice((owner - first) * size, (owner - first + 1) * size)
+        folded[where, :] = to_fields(mixed)
+
+
+def side_kernel(far, share, weighted_ref, side_ref, totals_ref, *refs):
+    groups = len(LEFT_BLOCKS)
+    if far:
+        own_parts, refs = refs[:groups], refs[groups + 1 :]
+        own_sum_ref, refs = refs[0], refs[1:]
+        own_sum_ref[...] = sum((part[...] for part in own_parts[1:]), own_parts[0][...])
+    targets, (near, window, tile, folded, flipped) = refs[:groups], refs[groups:]
+    rows, snps = near.shape[0], tile.shape[1]
+    half = rows // 2
+    above = odd_block() == far
+    mixed = side_ref[0:half, 2 * LANES :]
+    turned = pltpu.roll(mixed.astype(jnp.float32), HALF_LANES, 1).astype(mixed.dtype)
+
+    def fill(whole, shared):
+        near[0:half, whole : whole + LANES] = side_ref[0:half, 0:LANES]
+        near[half:, whole : whole + LANES] = side_ref[0:half, LANES : 2 * LANES]
+        near[0:half, shared : shared + LANES] = mixed
+        near[half:, shared : shared + LANES] = turned
+
+    @pl.when(above)
+    def _():
+        fill(0, LANES)
+
+    @pl.when(jnp.logical_not(above))
+    def _():
+        fill(LANES, 0)
+
+    window[...] = jnp.dot(weighted_ref[...], near[...], preferred_element_type=jnp.float32)
+
+    @pl.when(above)
+    def _():
+        tile[:, 0 : 2 * LANES] = window[...]
+        fold_by_column(tile, flipped, folded, 0)
+
+    @pl.when(jnp.logical_not(above))
+    def _():
+        tile[:, LANES:] = window[...]
+        fold_by_column(tile, flipped, folded, groups // 2)
+
+    square = (snps, snps)
+    apart = jnp.sum(
+        jnp.where(iota(square, 0) == iota(square, 1), tile[0:snps, :], 0.0), axis=0, keepdims=True
+    )
+    extras = to_fields(
+        jnp.concatenate(
+            [totals_ref[0:2, :], tile[snps : snps + 1, :], apart, jnp.zeros((4, snps))], axis=0
+        )
+    )
+    me = lax.axis_index("hap")
+    for step, target in enumerate(targets):
+        chunk = partner(me, step, groups) & 1
+        target[0:share, :] = folded[pl.ds(pl.multiple_of(chunk * share, 8), share), :]
+        target[share:, :] = extras
 
 
 def near_kernel(groups, share, weighted_ref, far_ref, close_ref, totals_ref, *refs):
     own_parts, own_sum_ref = refs[:groups], refs[groups]
-    targets, (near, tile, folded, flipped) = refs[groups + 1 : 2 * groups + 1], refs[2 * groups + 1 :]
+    targets, (near, tile, folded) = refs[groups + 1 : 2 * groups + 1], refs[2 * groups + 1 :]
     rows, snps = near.shape
     half = snps // 2
     odd = odd_block()
@@ -235,15 +292,12 @@
         unpack(close_ref, far_ref)
 
     tile[...] = jnp.dot(weighted_ref[...], near[...], preferred_element_type=jnp.float32)
-    if groups == len(LEFT_BLOCKS):
-        fold_by_column(tile, flipped, folded)
-    else:
-        row, col = iota((half, snps), 0), iota((half, snps), 1)
-        moved = (col >= half) & (col - half < row)
-        turned = pltpu.roll(tile[0:half, :], half, 1)
-        folded[0:half, :] = to_fields(jnp.where(moved, turned, tile[half:snps, :]))
-        if folded.shape[0] > half:
-            folded[half:, :] = jnp.zeros((folded.shape[0] - half, snps), jnp.int32)
+    row, col = iota((half, snps), 0), iota((half, snps), 1)
+    moved = (col >= half) & (col - half < row)
+    turned = pltpu.roll(tile[0:half, :], half, 1)
+    folded[0:half, :] = to_fields(jnp.where(moved, turned, tile[half:snps, :]))
+    if folded.shape[0] > half:
+        folded[half:, :] = jnp.zeros((folded.shape[0] - half, snps), jnp.int32)
     square = (snps, snps)
     far = jnp.sum(
         jnp.where(iota(square, 0) == iota(square, 1), tile[0:snps, :], 0.0), axis=0, keepdims=True
@@ -420,10 +474,10 @@
 
 
 def column_score_kernel(groups, share, reach_ref, *refs):
-    own_sum_ref, near_parts = refs[0], refs[1 : groups + 1]
-    annot_ref, near_annot_ref = refs[groups + 1 : groups + 3]
-    out_ref, *targets = refs[groups + 3 : 2 * groups + 3]
-    near_out_ref, table, flipped, scores = refs[2 * groups + 3 :]
+    own_sum_ref, far_parts, close_parts = refs[0], refs[1 : groups + 1], refs[groups + 1 : 2 * groups + 1]
+    annot_ref, near_annot_ref = refs[2 * groups + 1 : 2 * groups + 3]
+    out_ref, *targets = refs[2 * groups + 3 : 3 * groups + 3]
+    near_out_ref, table, flipped, scores = refs[3 * groups + 3 :]
     snps = annot_ref.shape[0]
     half = snps // 2
     wide = snps // groups
@@ -444,7 +498,10 @@
         return value
 
     own_counts = own_sum_ref[...]
-    near_sums = sum((part[...] for part in near_parts[1:]), near_parts[0][...])
+    from_far = odd_block() == upper
+    near_sums = sum(
+        jnp.where(from_far, far[...], close[...]) for far, close in zip(far_parts, close_parts)
+    )
     extras = from_fields(near_sums[share:, :])
     near_counts = near_sums[0:share, :]
 
@@ -595,6 +652,17 @@
     return lax.ppermute(
         value, "hap", [(source, partner(source, step, groups)) for source in range(groups)]
     )
+
+
+def to_owners(value, groups, step, far):
+    pairs = []
+    for block in range(lax.axis_size("snp")):
+        above = (block % 2 == 1) == far
+        for group in range(groups):
+            target = partner(group, step, groups)
+            if (target < groups // 2) == above:
+                pairs.append((block * groups + group, block * groups + target))
+    return lax.ppermute(value, ("snp", "hap"), pairs)
 
 
 def swapped(value, first):
@@ -646,15 +714,41 @@
     )(alleles, labels.reshape(1, rows))
     own_parts = [own_parts[0]] + [around(own_parts[k], groups, k) for k in range(groups - 1, 0, -1)]
 
-    own_sum, *near_parts = call(
-        functools.partial(near_kernel, groups, share),
-        [shape((share, snps), i32)] + [shape((share + 8, snps), i32)] * groups,
-        [VMEM] * (4 + groups),
-        [pltpu.VMEM((rows, snps), bf16), tile, folded, pltpu.VMEM((snps, LANES), f32)],
-        flops=2 * rows * snps * snps,
-        moved=rows * snps * 4,
-    )(weighted, from_far, from_close, totals, *own_parts)
-    near_parts = [near_parts[0]] + [around(near_parts[k], groups, k) for k in range(groups - 1, 0, -1)]
+    side_share = shape((share + 8, snps), i32)
+
+    def side(far, payload, *more):
+        outs = call(
+            functools.partial(side_kernel, far, share),
+            [shape((share, snps), i32)] * far + [side_share] * groups,
+            [VMEM] * (3 + len(more)),
+            [
+                pltpu.VMEM((rows, 2 * LANES), bf16),
+                pltpu.VMEM((snps + 16, 2 * LANES), f32),
+                tile,
+                pltpu.VMEM((folded_rows // 2, snps), i32),
+                pltpu.VMEM((snps, LANES), f32),
+            ],
+            flops=4 * rows * snps * LANES,
+            moved=rows * snps * 4,
+        )(weighted, payload, totals, *more)
+        parts = list(outs[far:])
+        parts[1:] = [to_owners(parts[k], groups, k, far) for k in range(1, groups)]
+        return outs[:far], parts
+
+    by_column = groups == len(LEFT_BLOCKS)
+    if by_column:
+        _, close_parts = side(False, from_close)
+        (own_sum,), far_parts = side(True, from_far, *own_parts, close_parts[0])
+    else:
+        own_sum, *near_parts = call(
+            functools.partial(near_kernel, groups, share),
+            [shape((share, snps), i32)] + [shape((share + 8, snps), i32)] * groups,
+            [VMEM] * (4 + groups),
+            [pltpu.VMEM((rows, snps), bf16), tile, folded],
+            flops=2 * rows * snps * snps,
+            moved=rows * snps * 4,
+        )(weighted, from_far, from_close, totals, *own_parts)
+        near_parts = [near_parts[0]] + [around(near_parts[k], groups, k) for k in range(groups - 1, 0, -1)]
 
     by_snp = shape((snps, LANES), f32)
     own_annots, near_annots = call(annots_kernel, [by_snp, by_snp], [VMEM] * 3, moved=1 << 20)(
@@ -674,15 +768,15 @@
     half_share = round_up(-(-out_share // 2), 8)
     own_share = shape((out_share, LANES), f32)
     packed_share = shape((half_share, LANES), f32)
-    if groups == len(LEFT_BLOCKS):
+    if by_column:
         own_scores, *scores, near_scores = call(
             functools.partial(column_score_kernel, groups, share),
             [own_share] + [shape((half_share, LANES), bf16)] * (groups - 1) + [packed_share],
-            [SMEM] + [VMEM] * (groups + 3),
+            [SMEM] + [VMEM] * (2 * groups + 3),
             [pltpu.VMEM((snps, LANES), f32), pltpu.VMEM((LANES, LANES), i32), pltpu.VMEM((snps, LANES), f32)],
             flops=1 << 26,
             moved=1 << 21,
-        )(reach, own_sum, *near_parts, own_annots, near_annots)
+        )(reach, own_sum, *far_parts, *close_parts, own_annots, near_annots)
         scores = [around(scores[k - 1], groups, k) for k in range(groups - 1, 0, -1)]
         there = to_neighbour(near_scores)
         return call(column_finish_kernel, result, [VMEM] * (groups + 1))(own_scores, there, *scores)

time: 41.4 us -> 45.2 us (1.092)
  the two profiles are of different devices: /device:TPU:1 before, /device:TPU:0 now
where the time goes in v7:
time: 45.2 us; the launch traced here: 45 us
  starting transfers between devices  31.4 us (69%)
  Pallas kernels  8.86 us (20%)
  waiting for transfers between devices  4.46 us (10%)
    ppermute x6, starting transfers between devices, to_owners(): return lax.ppermute(value, ('snp', 'hap'), pairs)  16.1 us
    ppermute x6, starting transfers between devices, around(): lax.ppermute(value, 'hap', [(source, partner(source, step, groups)) for s...  9.79 us
    ppermute x1, starting transfers between devices, to_neighbour(): return lax.ppermute(value, ('snp', 'hap'), pairs)  4.29 us
    ppermute x6, waiting for transfers between devices, around(): lax.ppermute(value, 'hap', [(source, partner(source, step, groups)) for s...  2.71 us
    pallas_call x2, Pallas kernels, side(): call(functools.partial(side_kernel, far, share), [shape((share, snps), i3...  2.42 us
    pallas_call x1, Pallas kernels, per_device(): call(functools.partial(column_score_kernel, groups, share), [own_share] +...  2.15 us
    pallas_call x1, Pallas kernels, per_device(): call(prepare_kernel, [shape((rows, snps), bf16), packed, packed], [HBM, H...  2.14 us
    ppermute x6, waiting for transfers between devices, to_owners(): return lax.ppermute(value, ('snp', 'hap'), pairs)  1.74 us
  transfers between devices with their start and end apart: 15, of which 6 were waited for; matrix products, arithmetic and copies ran while one was open for 0% of the time, Pallas kernels for 8%

profile of v7, /device:TPU:0, one launch (start us, length us, event | category | flops | bytes accessed | tf_op | source)
XLA Modules:
  0.0 45.0 jit_solution(4804170431614477962)
XLA Ops:
  0.0 0.0 copy-start.2
  0.0 2.1 %shard_map.46 = (bf16[2048,384]{1,0:T(8,128)(2,1)S(1)}, bf16[1056,384]{1,0:T(8,128)(2,1)S(1)}, bf16[1056,384]{1,0:T(8,128)(2,1)S(1)}) custom-call(s32[2048,384]{1,0:T(8,128)} %hap_ref.1, s32[50,384]{1,0:T(8,128)} %annot_ref.3), custom_call_target="tpu_custom_call" | custom-call | bytes 6291456 | tf_op jit(solution)/shard_map/pallas_call | solution.py:691
  2.1 0.5 %collective-permute-start.4 = (bf16[1056,384]{1,0:T(8,128)(2,1)S(1)}, bf16[1056,384]{1,0:T(8,128)(2,1)S(1)}, u32[]{:S(2)}, u32[]{:S(2)}) collective-permute-start(bf16[1056,384]{1,0:T(8,128)(2,1)S(1)} %get-tuple-element.38), channel_id=1, source_target_pairs={{0,4},{4,0},{8,12},{12,8},{1,5},{5,1},{9,13},{13,9},{2,6},{6,2},{1... | collective-permute-start | bytes 2433032 | tf_op jit(solution)/shard_map/ppermute | solution.py:672
  2.7 0.7 %collective-permute-start = (bf16[1056,384]{1,0:T(8,128)(2,1)S(1)}, bf16[1056,384]{1,0:T(8,128)(2,1)S(1)}, u32[]{:S(2)}, u32[]{:S(2)}) collective-permute-start(bf16[1056,384]{1,0:T(8,128)(2,1)S(1)} %get-tuple-element.32), channel_id=1, source_target_pairs={{4,8},{8,4},{5,9},{9,5},{6,10},{10,6},{7,11},{11,7},{20,24},{24,20... | collective-permute-start | bytes 2433032 | tf_op jit(solution)/shard_map/ppermute | solution.py:672
  3.4 0.0 copy-done.2
  3.4 1.1 %shard_map.47 = (bf16[400,2048]{1,0:T(8,128)(2,1)S(1)}, f32[8,384]{1,0:T(8,128)S(1)}, s32[48,384]{1,0:T(8,128)S(1)}, s32[48,384]{1,0:T(8,128)S(1)}, s32[48,384]{1,0:T(8,128)S(1)}, /*index=5*/s32[48,384]{1,0:T(8,128)S(1)}) custom-call(bf16[2048,384]{1,0:T(8,128)(2,1)S(1)} %get-tuple-element.30.alleles_ref, s32[1,2048]{1,0:T(1,128)S(1)} %bitcast.1), custom_call_target="tpu_custom_call" | custom-call | flops 603979776 | bytes 3145728 | tf_op jit(solution)/shard_map/pallas_call | solution.py:707
  4.5 4.7 %collective-permute-start.1 = (s32[48,384]{1,0:T(8,128)S(1)}, s32[48,384]{1,0:T(8,128)S(1)}, u32[]{:S(2)}, u32[]{:S(2)}) collective-permute-start(s32[48,384]{1,0:T(8,128)S(1)} %get-tuple-element.35), channel_id=1, source_target_pairs={{0,3},{1,2},{2,1},{3,0},{4,7},{5,6},{6,5},{7,4},{8,11},{9,10},{10,... | collective-permute-start | bytes 221192 | tf_op jit(solution)/shard_map/ppermute | solution.py:652
  9.2 0.0 collective-permute-start.2
  9.2 0.6 %collective-permute-start.3 = (s32[48,384]{1,0:T(8,128)S(1)}, s32[48,384]{1,0:T(8,128)S(1)}, u32[]{:S(2)}, u32[]{:S(2)}) collective-permute-start(s32[48,384]{1,0:T(8,128)S(1)} %get-tuple-element.37), channel_id=1, source_target_pairs={{0,1},{1,0},{2,3},{3,2},{4,5},{5,4},{6,7},{7,6},{8,9},{9,8},{10,11... | collective-permute-start | bytes 221192 | tf_op jit(solution)/shard_map/ppermute | solution.py:652
  9.9 0.0 collective-permute-done.4.side_ref
  9.9 1.2 %shard_map.48 = (s32[56,384]{1,0:T(8,128)S(1)}, s32[56,384]{1,0:T(8,128)S(1)}, s32[56,384]{1,0:T(8,128)S(1)}, s32[56,384]{1,0:T(8,128)S(1)}) custom-call(bf16[400,2048]{1,0:T(8,128)(2,1)S(1)} %get-tuple-element.31.weighted_ref, bf16[1056,384]{1,0:T(8,128)(2,1)S(1)} %collective-permute-done.4.side_ref, f32[8,384]{1,0:T(8,128)S(1)} %get-tuple-element.33.totals_ref), custom_call_target="tpu_custom_call" | custom-call | flops 402653184 | bytes 3145728 | tf_op jit(solution)/shard_map/pallas_call | solution.py:720
  11.0 0.0 copy-start
  11.0 0.0 copy-start.1
  11.1 3.4 %collective-permute-start.8 = (s32[56,384]{1,0:T(8,128)S(1)}, s32[56,384]{1,0:T(8,128)S(1)}, u32[]{:S(2)}, u32[]{:S(2)}) collective-permute-start(s32[56,384]{1,0:T(8,128)S(1)} %get-tuple-element.45), channel_id=1, source_target_pairs={{0,1},{1,0},{6,7},{7,6},{8,9},{9,8},{14,15},{15,14},{16,17},{17,16... | collective-permute-start | bytes 258056 | tf_op jit(solution)/shard_map/ppermute | solution.py:665
  14.5 0.0 collective-permute-done.1.refs_1_
  14.5 1.3 %collective-permute-start.9 = (s32[56,384]{1,0:T(8,128)S(1)}, s32[56,384]{1,0:T(8,128)S(1)}, u32[]{:S(2)}, u32[]{:S(2)}) collective-permute-start(s32[56,384]{1,0:T(8,128)S(1)} %get-tuple-element.46), channel_id=1, source_target_pairs={{2,0},{3,1},{4,6},{5,7},{10,8},{11,9},{12,14},{13,15},{18,16},{19,... | collective-permute-start | bytes 258056 | tf_op jit(solution)/shard_map/ppermute | solution.py:665
  15.8 0.9 %collective-permute-done.2.refs_2_ = s32[48,384]{1,0:T(8,128)S(1)} collective-permute-done((s32[48,384]{1,0:T(8,128)S(1)}, s32[48,384]{1,0:T(8,128)S(1)}, u32[]{:S(2)}, u32[]{:S(2)}) %collective-permute-start.2) | collective-permute-done | bytes 73760 | tf_op jit(solution)/shard_map/ppermute | solution.py:652
  16.7 1.3 %collective-permute-start.10 = (s32[56,384]{1,0:T(8,128)S(1)}, s32[56,384]{1,0:T(8,128)S(1)}, u32[]{:S(2)}, u32[]{:S(2)}) collective-permute-start(s32[56,384]{1,0:T(8,128)S(1)} %get-tuple-element.47), channel_id=1, source_target_pairs={{2,1},{3,0},{4,7},{5,6},{10,9},{11,8},{12,15},{13,14},{18,17},{19,... | collective-permute-start | bytes 258056 | tf_op jit(solution)/shard_map/ppermute | solution.py:665
  18.0 0.0 collective-permute-done.3.refs_3_
  18.0 0.0 collective-permute-done.side_ref
  18.0 1.2 %shard_map.49 = (s32[48,384]{1,0:T(8,128)S(1)}, s32[56,384]{1,0:T(8,128)S(1)}, s32[56,384]{1,0:T(8,128)S(1)}, s32[56,384]{1,0:T(8,128)S(1)}, s32[56,384]{1,0:T(8,128)S(1)}) custom-call(bf16[400,2048]{1,0:T(8,128)(2,1)S(1)} %get-tuple-element.31.weighted_ref, bf16[1056,384]{1,0:T(8,128)(2,1)S(1)} %collective-permute-done.side_ref, ...), custom_call_target="tpu_custom_call" | custom-call | flops 402653184 | bytes 3145728 | tf_op jit(solution)/shard_map/pallas_call | solution.py:720
  19.2 0.7 %collective-permute-start.5 = (s32[56,384]{1,0:T(8,128)S(1)}, s32[56,384]{1,0:T(8,128)S(1)}, u32[]{:S(2)}, u32[]{:S(2)}) collective-permute-start(s32[56,384]{1,0:T(8,128)S(1)} %get-tuple-element.42), channel_id=1, source_target_pairs={{2,3},{3,2},{4,5},{5,4},{10,11},{11,10},{12,13},{13,12},{18,19},{1... | collective-permute-start | bytes 258056 | tf_op jit(solution)/shard_map/ppermute | solution.py:665
  19.9 8.2 %collective-permute-start.6 = (s32[56,384]{1,0:T(8,128)S(1)}, s32[56,384]{1,0:T(8,128)S(1)}, u32[]{:S(2)}, u32[]{:S(2)}) collective-permute-start(s32[56,384]{1,0:T(8,128)S(1)} %get-tuple-element.43), channel_id=1, source_target_pairs={{0,2},{1,3},{6,4},{7,5},{8,10},{9,11},{14,12},{15,13},{16,18},{17,... | collective-permute-start | bytes 258056 | tf_op jit(solution)/shard_map/ppermute | solution.py:665
  28.1 0.0 collective-permute-done.8.refs_6_
  28.1 1.3 %collective-permute-start.7 = (s32[56,384]{1,0:T(8,128)S(1)}, s32[56,384]{1,0:T(8,128)S(1)}, u32[]{:S(2)}, u32[]{:S(2)}) collective-permute-start(s32[56,384]{1,0:T(8,128)S(1)} %get-tuple-element.44), channel_id=1, source_target_pairs={{0,3},{1,2},{6,5},{7,4},{8,11},{9,10},{14,13},{15,12},{16,19},{17,... | collective-permute-start | bytes 258056 | tf_op jit(solution)/shard_map/ppermute | solution.py:665
  29.4 0.0 copy-done
  29.4 0.3 shard_map.50
  29.7 0.0 collective-permute-done.9.refs_7_
  29.7 0.0 collective-permute-done.10.refs_8_
  29.7 0.0 collective-permute-done.5.refs_2_
  29.7 0.4 collective-permute-done.6.refs_3_
  30.2 1.3 %collective-permute-done.7.refs_4_ = s32[56,384]{1,0:T(8,128)S(1)} collective-permute-done((s32[56,384]{1,0:T(8,128)S(1)}, s32[56,384]{1,0:T(8,128)S(1)}, u32[]{:S(2)}, u32[]{:S(2)}) %collective-permute-start.7) | collective-permute-done | bytes 86048 | tf_op jit(solution)/shard_map/ppermute | solution.py:665
  31.5 0.0 copy-done.1
  31.5 2.2 %shard_map.51 = (f32[96,128]{1,0:T(8,128)S(1)}, bf16[48,128]{1,0:T(8,128)(2,1)S(1)}, bf16[48,128]{1,0:T(8,128)(2,1)S(1)}, bf16[48,128]{1,0:T(8,128)(2,1)S(1)}, f32[48,128]{1,0:T(8,128)S(1)}) custom-call(s32[4]{0:T(128)S(1)} %copy-done.1, s32[48,384]{1,0:T(8,128)S(1)} %get-tuple-element.40.refs_0_, s32[56,384]{1,0:T(8,128)S(1)} %get-tuple-element.41.refs_1_, ...), custom_call_target="tpu_custom_call" | custom-call | flops 67108864 | bytes 2097152 | tf_op jit(solution)/shard_map/pallas_call | solution.py:772
  33.6 4.3 %collective-permute-start.11 = (f32[48,128]{1,0:T(8,128)S(1)}, f32[48,128]{1,0:T(8,128)S(1)}, u32[]{:S(2)}, u32[]{:S(2)}) collective-permute-start(f32[48,128]{1,0:T(8,128)S(1)} %get-tuple-element.51), channel_id=1, source_target_pairs={{0,4},{1,5},{4,8},{5,9},{6,2},{7,3},{8,12},{9,13},{10,6},{11,7},{1... | collective-permute-start | bytes 73736 | tf_op jit(solution)/shard_map/ppermute | solution.py:765
  37.9 1.3 %collective-permute-start.12 = (bf16[48,128]{1,0:T(8,128)(2,1)S(1)}, bf16[48,128]{1,0:T(8,128)(2,1)S(1)}, u32[]{:S(2)}, u32[]{:S(2)}) collective-permute-start(bf16[48,128]{1,0:T(8,128)(2,1)S(1)} %get-tuple-element.52), channel_id=1, source_target_pairs={{0,3},{1,2},{2,1},{3,0},{4,7},{5,6},{6,5},{7,4},{8,11},{9,10},{10,... | collective-permute-start | bytes 36872 | tf_op jit(solution)/shard_map/ppermute | solution.py:652
  39.2 1.3 %collective-permute-start.13 = (bf16[48,128]{1,0:T(8,128)(2,1)S(1)}, bf16[48,128]{1,0:T(8,128)(2,1)S(1)}, u32[]{:S(2)}, u32[]{:S(2)}) collective-permute-start(bf16[48,128]{1,0:T(8,128)(2,1)S(1)} %get-tuple-element.53), channel_id=1, source_target_pairs={{0,2},{1,3},{2,0},{3,1},{4,6},{5,7},{6,4},{7,5},{8,10},{9,11},{10,... | collective-permute-start | bytes 36872 | tf_op jit(solution)/shard_map/ppermute | solution.py:652
  40.5 1.9 %collective-permute-start.14 = (bf16[48,128]{1,0:T(8,128)(2,1)S(1)}, bf16[48,128]{1,0:T(8,128)(2,1)S(1)}, u32[]{:S(2)}, u32[]{:S(2)}) collective-permute-start(bf16[48,128]{1,0:T(8,128)(2,1)S(1)} %get-tuple-element.54), channel_id=1, source_target_pairs={{0,1},{1,0},{2,3},{3,2},{4,5},{5,4},{6,7},{7,6},{8,9},{9,8},{10,11... | collective-permute-start | bytes 36872 | tf_op jit(solution)/shard_map/ppermute | solution.py:652
  42.4 1.1 %collective-permute-done.12.refs_0_ = bf16[48,128]{1,0:T(8,128)(2,1)S(1)} collective-permute-done((bf16[48,128]{1,0:T(8,128)(2,1)S(1)}, bf16[48,128]{1,0:T(8,128)(2,1)S(1)}, u32[]{:S(2)}, u32[]{:S(2)}) %collective-permute-start.12) | collective-permute-done | bytes 12320 | tf_op jit(solution)/shard_map/ppermute | solution.py:652
  43.5 0.4 collective-permute-done.13.refs_1_
  43.9 0.3 collective-permute-done.14.refs_2_
  44.2 0.0 collective-permute-done.11.there_ref
  44.2 0.8 %shard_map.52 = f32[50,96]{1,0:T(8,128)} custom-call(f32[96,128]{1,0:T(8,128)S(1)} %get-tuple-element.50.own_ref, f32[48,128]{1,0:T(8,128)S(1)} %collective-permute-done.11.there_ref, bf16[48,128]{1,0:T(8,128)(2,1)S(1)} %collective-permute-done.12.refs_0_, bf16[48,128]{1,0:T(8,128)(2,1)S(1)} %collective-permute-done.13.refs_1_, ...), custom_call_target="tpu_custom_call" | custom-call | tf_op jit(solution)/shard_map/pallas_call | solution.py:782
  (2 shorter events, 0.0 us)
Async XLA Ops:
  0.0 3.4 %copy-start.2 = (s32[2048]{0:T(1024)S(1)}, s32[2048]{0:T(1024)}, u32[]{:S(2)}) copy-start(s32[2048]{0:T(1024)} %param.5) | copy-start | bytes 24580
  2.1 7.7 %collective-permute-start.4 = (bf16[1056,384]{1,0:T(8,128)(2,1)S(1)}, bf16[1056,384]{1,0:T(8,128)(2,1)S(1)}, u32[]{:S(2)}, u32[]{:S(2)}) collective-permute-start(bf16[1056,384]{1,0:T(8,128)(2,1)S(1)} %get-tuple-element.38), channel_id=1, source_target_pairs={{0,4},{4,0},{8,12},{12,8},{1,5},{5,1},{9,13},{13,9},{2,6},{6,2},{1... | collective-permute-start | bytes 2433032 | tf_op jit(solution)/shard_map/ppermute | solution.py:672
  2.7 15.3 %collective-permute-start = (bf16[1056,384]{1,0:T(8,128)(2,1)S(1)}, bf16[1056,384]{1,0:T(8,128)(2,1)S(1)}, u32[]{:S(2)}, u32[]{:S(2)}) collective-permute-start(bf16[1056,384]{1,0:T(8,128)(2,1)S(1)} %get-tuple-element.32), channel_id=1, source_target_pairs={{4,8},{8,4},{5,9},{9,5},{6,10},{10,6},{7,11},{11,7},{20,24},{24,20... | collective-permute-start | bytes 2433032 | tf_op jit(solution)/shard_map/ppermute | solution.py:672
  4.5 10.0 %collective-permute-start.1 = (s32[48,384]{1,0:T(8,128)S(1)}, s32[48,384]{1,0:T(8,128)S(1)}, u32[]{:S(2)}, u32[]{:S(2)}) collective-permute-start(s32[48,384]{1,0:T(8,128)S(1)} %get-tuple-element.35), channel_id=1, source_target_pairs={{0,3},{1,2},{2,1},{3,0},{4,7},{5,6},{6,5},{7,4},{8,11},{9,10},{10,... | collective-permute-start | bytes 221192 | tf_op jit(solution)/shard_map/ppermute | solution.py:652
  9.2 7.5 %collective-permute-start.2 = (s32[48,384]{1,0:T(8,128)S(1)}, s32[48,384]{1,0:T(8,128)S(1)}, u32[]{:S(2)}, u32[]{:S(2)}) collective-permute-start(s32[48,384]{1,0:T(8,128)S(1)} %get-tuple-element.36), channel_id=1, source_target_pairs={{0,2},{1,3},{2,0},{3,1},{4,6},{5,7},{6,4},{7,5},{8,10},{9,11},{10,... | collective-permute-start | bytes 221192 | tf_op jit(solution)/shard_map/ppermute | solution.py:652
  9.2 8.8 %collective-permute-start.3 = (s32[48,384]{1,0:T(8,128)S(1)}, s32[48,384]{1,0:T(8,128)S(1)}, u32[]{:S(2)}, u32[]{:S(2)}) collective-permute-start(s32[48,384]{1,0:T(8,128)S(1)} %get-tuple-element.37), channel_id=1, source_target_pairs={{0,1},{1,0},{2,3},{3,2},{4,5},{5,4},{6,7},{7,6},{8,9},{9,8},{10,11... | collective-permute-start | bytes 221192 | tf_op jit(solution)/shard_map/ppermute | solution.py:652
  11.0 18.4 %copy-start = (s32[50,384]{1,0:T(8,128)S(1)}, s32[50,384]{1,0:T(8,128)}, u32[]{:S(2)}) copy-start(s32[50,384]{1,0:T(8,128)} %annot_ref.3) | copy-start | bytes 230404
  11.0 20.4 %copy-start.1 = (s32[4]{0:T(128)S(1)}, s32[4]{0:T(128)}, u32[]{:S(2)}) copy-start(s32[4]{0:T(128)} %reach_ref.1) | copy-start | bytes 52
  11.1 17.0 %collective-permute-start.8 = (s32[56,384]{1,0:T(8,128)S(1)}, s32[56,384]{1,0:T(8,128)S(1)}, u32[]{:S(2)}, u32[]{:S(2)}) collective-permute-start(s32[56,384]{1,0:T(8,128)S(1)} %get-tuple-element.45), channel_id=1, source_target_pairs={{0,1},{1,0},{6,7},{7,6},{8,9},{9,8},{14,15},{15,14},{16,17},{17,16... | collective-permute-start | bytes 258056 | tf_op jit(solution)/shard_map/ppermute | solution.py:665
  14.5 15.2 %collective-permute-start.9 = (s32[56,384]{1,0:T(8,128)S(1)}, s32[56,384]{1,0:T(8,128)S(1)}, u32[]{:S(2)}, u32[]{:S(2)}) collective-permute-start(s32[56,384]{1,0:T(8,128)S(1)} %get-tuple-element.46), channel_id=1, source_target_pairs={{2,0},{3,1},{4,6},{5,7},{10,8},{11,9},{12,14},{13,15},{18,16},{19,... | collective-permute-start | bytes 258056 | tf_op jit(solution)/shard_map/ppermute | solution.py:665
  16.7 13.0 %collective-permute-start.10 = (s32[56,384]{1,0:T(8,128)S(1)}, s32[56,384]{1,0:T(8,128)S(1)}, u32[]{:S(2)}, u32[]{:S(2)}) collective-permute-start(s32[56,384]{1,0:T(8,128)S(1)} %get-tuple-element.47), channel_id=1, source_target_pairs={{2,1},{3,0},{4,7},{5,6},{10,9},{11,8},{12,15},{13,14},{18,17},{19,... | collective-permute-start | bytes 258056 | tf_op jit(solution)/shard_map/ppermute | solution.py:665
  19.2 10.5 %collective-permute-start.5 = (s32[56,384]{1,0:T(8,128)S(1)}, s32[56,384]{1,0:T(8,128)S(1)}, u32[]{:S(2)}, u32[]{:S(2)}) collective-permute-start(s32[56,384]{1,0:T(8,128)S(1)} %get-tuple-element.42), channel_id=1, source_target_pairs={{2,3},{3,2},{4,5},{5,4},{10,11},{11,10},{12,13},{13,12},{18,19},{1... | collective-permute-start | bytes 258056 | tf_op jit(solution)/shard_map/ppermute | solution.py:665
  19.9 10.2 %collective-permute-start.6 = (s32[56,384]{1,0:T(8,128)S(1)}, s32[56,384]{1,0:T(8,128)S(1)}, u32[]{:S(2)}, u32[]{:S(2)}) collective-permute-start(s32[56,384]{1,0:T(8,128)S(1)} %get-tuple-element.43), channel_id=1, source_target_pairs={{0,2},{1,3},{6,4},{7,5},{8,10},{9,11},{14,12},{15,13},{16,18},{17,... | collective-permute-start | bytes 258056 | tf_op jit(solution)/shard_map/ppermute | solution.py:665
  28.1 3.4 %collective-permute-start.7 = (s32[56,384]{1,0:T(8,128)S(1)}, s32[56,384]{1,0:T(8,128)S(1)}, u32[]{:S(2)}, u32[]{:S(2)}) collective-permute-start(s32[56,384]{1,0:T(8,128)S(1)} %get-tuple-element.44), channel_id=1, source_target_pairs={{0,3},{1,2},{6,5},{7,4},{8,11},{9,10},{14,13},{15,12},{16,19},{17,... | collective-permute-start | bytes 258056 | tf_op jit(solution)/shard_map/ppermute | solution.py:665
  33.6 10.6 %collective-permute-start.11 = (f32[48,128]{1,0:T(8,128)S(1)}, f32[48,128]{1,0:T(8,128)S(1)}, u32[]{:S(2)}, u32[]{:S(2)}) collective-permute-start(f32[48,128]{1,0:T(8,128)S(1)} %get-tuple-element.51), channel_id=1, source_target_pairs={{0,4},{1,5},{4,8},{5,9},{6,2},{7,3},{8,12},{9,13},{10,6},{11,7},{1... | collective-permute-start | bytes 73736 | tf_op jit(solution)/shard_map/ppermute | solution.py:765
  37.9 5.6 %collective-permute-start.12 = (bf16[48,128]{1,0:T(8,128)(2,1)S(1)}, bf16[48,128]{1,0:T(8,128)(2,1)S(1)}, u32[]{:S(2)}, u32[]{:S(2)}) collective-permute-start(bf16[48,128]{1,0:T(8,128)(2,1)S(1)} %get-tuple-element.52), channel_id=1, source_target_pairs={{0,3},{1,2},{2,1},{3,0},{4,7},{5,6},{6,5},{7,4},{8,11},{9,10},{10,... | collective-permute-start | bytes 36872 | tf_op jit(solution)/shard_map/ppermute | solution.py:652
  39.2 4.7 %collective-permute-start.13 = (bf16[48,128]{1,0:T(8,128)(2,1)S(1)}, bf16[48,128]{1,0:T(8,128)(2,1)S(1)}, u32[]{:S(2)}, u32[]{:S(2)}) collective-permute-start(bf16[48,128]{1,0:T(8,128)(2,1)S(1)} %get-tuple-element.53), channel_id=1, source_target_pairs={{0,2},{1,3},{2,0},{3,1},{4,6},{5,7},{6,4},{7,5},{8,10},{9,11},{10,... | collective-permute-start | bytes 36872 | tf_op jit(solution)/shard_map/ppermute | solution.py:652
  40.5 3.7 %collective-permute-start.14 = (bf16[48,128]{1,0:T(8,128)(2,1)S(1)}, bf16[48,128]{1,0:T(8,128)(2,1)S(1)}, u32[]{:S(2)}, u32[]{:S(2)}) collective-permute-start(bf16[48,128]{1,0:T(8,128)(2,1)S(1)} %get-tuple-element.54), channel_id=1, source_target_pairs={{0,1},{1,0},{2,3},{3,2},{4,5},{5,4},{6,7},{7,6},{8,9},{9,8},{10,11... | collective-permute-start | bytes 36872 | tf_op jit(solution)/shard_map/ppermute | solution.py:652

commit v8 on v6

--- a/solution.py
+++ b/solution.py
@@ -212,9 +212,75 @@
         folded[owner * size : (owner + 1) * size, :] = to_fields(mixed)
 
 
+def above(far):
+    return odd_block() == far
+
+
+def side_dot(far, weighted_ref, side_ref, near):
+    half = near.shape[0] // 2
+    mixed = side_ref[0:half, 2 * LANES :]
+    turned = pltpu.roll(mixed.astype(jnp.float32), HALF_LANES, 1).astype(mixed.dtype)
+
+    def fill(whole, shared):
+        near[0:half, whole : whole + LANES] = side_ref[0:half, 0:LANES]
+        near[half:, whole : whole + LANES] = side_ref[0:half, LANES : 2 * LANES]
+        near[0:half, shared : shared + LANES] = mixed
+        near[half:, shared : shared + LANES] = turned
+
+    @pl.when(above(far))
+    def _():
+        fill(0, LANES)
+
+    @pl.when(jnp.logical_not(above(far)))
+    def _():
+        fill(LANES, 0)
+
+    return jnp.dot(weighted_ref[...], near[...], preferred_element_type=jnp.float32)
+
+
+def close_kernel(weighted_ref, side_ref, window_ref, near):
+    window_ref[...] = side_dot(False, weighted_ref, side_ref, near)
+
+
+def far_kernel(groups, share, weighted_ref, side_ref, close_ref, totals_ref, *refs):
+    own_parts, own_sum_ref = refs[:groups], refs[groups]
+    targets, (near, window, tile, folded, flipped) = refs[groups + 1 : 2 * groups + 1], refs[2 * groups + 1 :]
+    snps = tile.shape[1]
+    own_sum_ref[...] = sum((part[...] for part in own_parts[1:]), own_parts[0][...])
+    window[...] = side_dot(True, weighted_ref, side_ref, near)
+    left = iota((tile.shape[0], LANES), 1) < HALF_LANES
+
+    def place(up, down):
+        tile[:, 0:LANES] = up[:, 0:LANES]
+        tile[:, LANES : 2 * LANES] = jnp.where(left, up[:, LANES:], down[:, 0:LANES])
+        tile[:, 2 * LANES :] = down[:, LANES:]
+
+    @pl.when(above(True))
+    def _():
+        place(window, close_ref)
+
+    @pl.when(jnp.logical_not(above(True)))
+    def _():
+        place(close_ref, window)
+
+    fold_by_column(tile, flipped, folded)
+    square = (snps, snps)
+    apart = jnp.sum(
+        jnp.where(iota(square, 0) == iota(square, 1), tile[0:snps, :], 0.0), axis=0, keepdims=True
+    )
+    extras = to_fields(
+        jnp.concatenate(
+            [totals_ref[0:2, :], tile[snps : snps + 1, :], apart, jnp.zeros((4, snps))], axis=0
+        )
+    )
+    send_shares(groups, folded, share, targets)
+    for target in targets:
+        target[share:, :] = extras
+
+
 def near_kernel(groups, share, weighted_ref, far_ref, close_ref, totals_ref, *refs):
     own_parts, own_sum_ref = refs[:groups], refs[groups]
-    targets, (near, tile, folded, flipped) = refs[groups + 1 : 2 * groups + 1], refs[2 * groups + 1 :]
+    targets, (near, tile, folded) = refs[groups + 1 : 2 * groups + 1], refs[2 * groups + 1 :]
     rows, snps = near.shape
     half = snps // 2
     odd = odd_block()
@@ -235,15 +301,12 @@
         unpack(close_ref, far_ref)
 
     tile[...] = jnp.dot(weighted_ref[...], near[...], preferred_element_type=jnp.float32)
-    if groups == len(LEFT_BLOCKS):
-        fold_by_column(tile, flipped, folded)
-    else:
-        row, col = iota((half, snps), 0), iota((half, snps), 1)
-        moved = (col >= half) & (col - half < row)
-        turned = pltpu.roll(tile[0:half, :], half, 1)
-        folded[0:half, :] = to_fields(jnp.where(moved, turned, tile[half:snps, :]))
-        if folded.shape[0] > half:
-            folded[half:, :] = jnp.zeros((folded.shape[0] - half, snps), jnp.int32)
+    row, col = iota((half, snps), 0), iota((half, snps), 1)
+    moved = (col >= half) & (col - half < row)
+    turned = pltpu.roll(tile[0:half, :], half, 1)
+    folded[0:half, :] = to_fields(jnp.where(moved, turned, tile[half:snps, :]))
+    if folded.shape[0] > half:
+        folded[half:, :] = jnp.zeros((folded.shape[0] - half, snps), jnp.int32)
     square = (snps, snps)
     far = jnp.sum(
         jnp.where(iota(square, 0) == iota(square, 1), tile[0:snps, :], 0.0), axis=0, keepdims=True
@@ -566,8 +629,8 @@
         target[...] = pack_halves(rows).astype(target.dtype)
 
 
-def column_finish_kernel(own_ref, there_ref, *refs):
-    *parts, out_ref = refs
+def column_finish_kernel(own_ref, *refs):
+    *parts, there_ref, out_ref = refs
     packed = sum((part[...].astype(jnp.float32) for part in parts), there_ref[...])
     out_ref[...] = (own_ref[...] + unpack_halves(packed)).T[0 : out_ref.shape[0], :]
 
@@ -646,14 +709,31 @@
     )(alleles, labels.reshape(1, rows))
     own_parts = [own_parts[0]] + [around(own_parts[k], groups, k) for k in range(groups - 1, 0, -1)]
 
-    own_sum, *near_parts = call(
-        functools.partial(near_kernel, groups, share),
-        [shape((share, snps), i32)] + [shape((share + 8, snps), i32)] * groups,
-        [VMEM] * (4 + groups),
-        [pltpu.VMEM((rows, snps), bf16), tile, folded, pltpu.VMEM((snps, LANES), f32)],
-        flops=2 * rows * snps * snps,
-        moved=rows * snps * 4,
-    )(weighted, from_far, from_close, totals, *own_parts)
+    by_column = groups == len(LEFT_BLOCKS)
+    near_shapes = [shape((share, snps), i32)] + [shape((share + 8, snps), i32)] * groups
+    if by_column:
+        near = pltpu.VMEM((rows, 2 * LANES), bf16)
+        window = (snps + 16, 2 * LANES)
+        work = dict(flops=4 * rows * snps * LANES, moved=rows * snps * 4)
+        close_counts = call(close_kernel, shape(window, f32), [VMEM] * 2, [near], **work)(
+            weighted, from_close
+        )
+        own_sum, *near_parts = call(
+            functools.partial(far_kernel, groups, share),
+            near_shapes,
+            [VMEM] * (4 + groups),
+            [near, pltpu.VMEM(window, f32), tile, folded, pltpu.VMEM((snps, LANES), f32)],
+            **work,
+        )(weighted, from_far, close_counts, totals, *own_parts)
+    else:
+        own_sum, *near_parts = call(
+            functools.partial(near_kernel, groups, share),
+            near_shapes,
+            [VMEM] * (4 + groups),
+            [pltpu.VMEM((rows, snps), bf16), tile, folded],
+            flops=2 * rows * snps * snps,
+            moved=rows * snps * 4,
+        )(weighted, from_far, from_close, totals, *own_parts)
     near_parts = [near_parts[0]] + [around(near_parts[k], groups, k) for k in range(groups - 1, 0, -1)]
 
     by_snp = shape((snps, LANES), f32)
@@ -674,7 +754,7 @@
     half_share = round_up(-(-out_share // 2), 8)
     own_share = shape((out_share, LANES), f32)
     packed_share = shape((half_share, LANES), f32)
-    if groups == len(LEFT_BLOCKS):
+    if by_column:
         own_scores, *scores, near_scores = call(
             functools.partial(column_score_kernel, groups, share),
             [own_share] + [shape((half_share, LANES), bf16)] * (groups - 1) + [packed_share],
@@ -685,7 +765,7 @@
         )(reach, own_sum, *near_parts, own_annots, near_annots)
         scores = [around(scores[k - 1], groups, k) for k in range(groups - 1, 0, -1)]
         there = to_neighbour(near_scores)
-        return call(column_finish_kernel, result, [VMEM] * (groups + 1))(own_scores, there, *scores)
+        return call(column_finish_kernel, result, [VMEM] * (groups + 1))(own_scores, *scores, there)
 
     tall = pltpu.VMEM((padded, LANES), f32)
     scores = call(

time: 41.4 us -> 40 us (0.966)
  the two profiles are of different devices: /device:TPU:1 before, /device:TPU:0 now
where the time goes in v8:
time: 40 us; the launch traced here: 39.8 us
  starting transfers between devices  18.2 us (46%)
  waiting for transfers between devices  13 us (32%)
  Pallas kernels  8.59 us (21%)
    ppermute x9, starting transfers between devices, around(): lax.ppermute(value, 'hap', [(source, partner(source, step, groups)) for s...  14.3 us
    ppermute x9, waiting for transfers between devices, around(): lax.ppermute(value, 'hap', [(source, partner(source, step, groups)) for s...  13 us
    ppermute x1, starting transfers between devices, to_neighbour(): return lax.ppermute(value, ('snp', 'hap'), pairs)  2.68 us
    pallas_call x1, Pallas kernels, per_device(): call(functools.partial(column_score_kernel, groups, share), [own_share] +...  2.15 us
    pallas_call x1, Pallas kernels, per_device(): call(prepare_kernel, [shape((rows, snps), bf16), packed, packed], [HBM, H...  2.14 us
    pallas_call x1, Pallas kernels, per_device(): call(functools.partial(far_kernel, groups, share), near_shapes, [VMEM] *...  1.29 us
    ppermute x2, starting transfers between devices, swapped(): return lax.ppermute(value, 'snp', pairs)  1.22 us
    pallas_call x1, Pallas kernels, per_device(): call(functools.partial(own_kernel, groups, share), [shape((snps + 16, row...  1.13 us
  transfers between devices with their start and end apart: 12, of which 6 were waited for; matrix products, arithmetic and copies ran while one was open for 0% of the time, Pallas kernels for 6%

profile of v8, /device:TPU:0, one launch (start us, length us, event | category | flops | bytes accessed | tf_op | source)
XLA Modules:
  0.0 39.8 jit_solution(12631207139027401931)
XLA Ops:
  0.0 0.0 copy-start.2
  0.0 2.1 %shard_map.46 = (bf16[2048,384]{1,0:T(8,128)(2,1)S(1)}, bf16[1056,384]{1,0:T(8,128)(2,1)S(1)}, bf16[1056,384]{1,0:T(8,128)(2,1)S(1)}) custom-call(s32[2048,384]{1,0:T(8,128)} %hap_ref.1, s32[50,384]{1,0:T(8,128)} %annot_ref.3), custom_call_target="tpu_custom_call" | custom-call | bytes 6291456 | tf_op jit(solution)/shard_map/pallas_call | solution.py:686
  2.1 0.5 %collective-permute-start.1 = (bf16[1056,384]{1,0:T(8,128)(2,1)S(1)}, bf16[1056,384]{1,0:T(8,128)(2,1)S(1)}, u32[]{:S(2)}, u32[]{:S(2)}) collective-permute-start(bf16[1056,384]{1,0:T(8,128)(2,1)S(1)} %get-tuple-element.29), channel_id=1, source_target_pairs={{0,4},{4,0},{8,12},{12,8},{1,5},{5,1},{9,13},{13,9},{2,6},{6,2},{1... | collective-permute-start | bytes 2433032 | tf_op jit(solution)/shard_map/ppermute | solution.py:667
  2.7 0.7 %collective-permute-start = (bf16[1056,384]{1,0:T(8,128)(2,1)S(1)}, bf16[1056,384]{1,0:T(8,128)(2,1)S(1)}, u32[]{:S(2)}, u32[]{:S(2)}) collective-permute-start(bf16[1056,384]{1,0:T(8,128)(2,1)S(1)} %get-tuple-element.28), channel_id=1, source_target_pairs={{4,8},{8,4},{5,9},{9,5},{6,10},{10,6},{7,11},{11,7},{20,24},{24,20... | collective-permute-start | bytes 2433032 | tf_op jit(solution)/shard_map/ppermute | solution.py:667
  3.4 0.0 copy-done.2
  3.4 1.1 %shard_map.47 = (bf16[400,2048]{1,0:T(8,128)(2,1)S(1)}, f32[8,384]{1,0:T(8,128)S(1)}, s32[48,384]{1,0:T(8,128)S(1)}, s32[48,384]{1,0:T(8,128)S(1)}, s32[48,384]{1,0:T(8,128)S(1)}, /*index=5*/s32[48,384]{1,0:T(8,128)S(1)}) custom-call(bf16[2048,384]{1,0:T(8,128)(2,1)S(1)} %get-tuple-element.26.alleles_ref, s32[1,2048]{1,0:T(1,128)S(1)} %bitcast.1), custom_call_target="tpu_custom_call" | custom-call | flops 603979776 | bytes 3145728 | tf_op jit(solution)/shard_map/pallas_call | solution.py:702
  4.5 4.7 %collective-permute-start.2 = (s32[48,384]{1,0:T(8,128)S(1)}, s32[48,384]{1,0:T(8,128)S(1)}, u32[]{:S(2)}, u32[]{:S(2)}) collective-permute-start(s32[48,384]{1,0:T(8,128)S(1)} %get-tuple-element.32), channel_id=1, source_target_pairs={{0,3},{1,2},{2,1},{3,0},{4,7},{5,6},{6,5},{7,4},{8,11},{9,10},{10,... | collective-permute-start | bytes 221192 | tf_op jit(solution)/shard_map/ppermute | solution.py:658
  9.2 0.0 collective-permute-start.3
  9.2 0.6 %collective-permute-start.4 = (s32[48,384]{1,0:T(8,128)S(1)}, s32[48,384]{1,0:T(8,128)S(1)}, u32[]{:S(2)}, u32[]{:S(2)}) collective-permute-start(s32[48,384]{1,0:T(8,128)S(1)} %get-tuple-element.34), channel_id=1, source_target_pairs={{0,1},{1,0},{2,3},{3,2},{4,5},{5,4},{6,7},{7,6},{8,9},{9,8},{10,11... | collective-permute-start | bytes 221192 | tf_op jit(solution)/shard_map/ppermute | solution.py:658
  9.9 0.0 collective-permute-done.1.side_ref
  9.9 0.9 %shard_map.48.close_ref = f32[400,256]{1,0:T(8,128)S(1)} custom-call(bf16[400,2048]{1,0:T(8,128)(2,1)S(1)} %get-tuple-element.27.weighted_ref, bf16[1056,384]{1,0:T(8,128)(2,1)S(1)} %collective-permute-done.1.side_ref), custom_call_target="tpu_custom_call" | custom-call | flops 402653184 | bytes 3145728 | tf_op jit(solution)/shard_map/pallas_call | solution.py:718
  10.7 0.0 copy-start
  10.7 0.9 %collective-permute-done.2.refs_1_ = s32[48,384]{1,0:T(8,128)S(1)} collective-permute-done((s32[48,384]{1,0:T(8,128)S(1)}, s32[48,384]{1,0:T(8,128)S(1)}, u32[]{:S(2)}, u32[]{:S(2)}) %collective-permute-start.2) | collective-permute-done | bytes 73760 | tf_op jit(solution)/shard_map/ppermute | solution.py:658
  11.7 5.0 %collective-permute-done.3.refs_2_ = s32[48,384]{1,0:T(8,128)S(1)} collective-permute-done((s32[48,384]{1,0:T(8,128)S(1)}, s32[48,384]{1,0:T(8,128)S(1)}, u32[]{:S(2)}, u32[]{:S(2)}) %collective-permute-start.3) | collective-permute-done | bytes 73760 | tf_op jit(solution)/shard_map/ppermute | solution.py:658
  16.7 0.0 collective-permute-done.4.refs_3_
  16.7 0.0 collective-permute-done.side_ref
  16.7 0.0 copy-start.1
  16.7 1.3 %shard_map.49 = (s32[48,384]{1,0:T(8,128)S(1)}, s32[56,384]{1,0:T(8,128)S(1)}, s32[56,384]{1,0:T(8,128)S(1)}, s32[56,384]{1,0:T(8,128)S(1)}, s32[56,384]{1,0:T(8,128)S(1)}) custom-call(bf16[400,2048]{1,0:T(8,128)(2,1)S(1)} %get-tuple-element.27.weighted_ref, bf16[1056,384]{1,0:T(8,128)(2,1)S(1)} %collective-permute-done.side_ref, ...), custom_call_target="tpu_custom_call" | custom-call | flops 402653184 | bytes 3145728 | tf_op jit(solution)/shard_map/pallas_call | solution.py:721
  18.0 0.1 collective-permute-start.5
  18.1 0.5 %collective-permute-start.6 = (s32[56,384]{1,0:T(8,128)S(1)}, s32[56,384]{1,0:T(8,128)S(1)}, u32[]{:S(2)}, u32[]{:S(2)}) collective-permute-start(s32[56,384]{1,0:T(8,128)S(1)} %get-tuple-element.38), channel_id=1, source_target_pairs={{0,2},{1,3},{2,0},{3,1},{4,6},{5,7},{6,4},{7,5},{8,10},{9,11},{10,... | collective-permute-start | bytes 258056 | tf_op jit(solution)/shard_map/ppermute | solution.py:658
  18.5 3.9 %collective-permute-start.7 = (s32[56,384]{1,0:T(8,128)S(1)}, s32[56,384]{1,0:T(8,128)S(1)}, u32[]{:S(2)}, u32[]{:S(2)}) collective-permute-start(s32[56,384]{1,0:T(8,128)S(1)} %get-tuple-element.39), channel_id=1, source_target_pairs={{0,1},{1,0},{2,3},{3,2},{4,5},{5,4},{6,7},{7,6},{8,9},{9,8},{10,11... | collective-permute-start | bytes 258056 | tf_op jit(solution)/shard_map/ppermute | solution.py:658
  22.5 0.0 copy-done
  22.5 0.3 shard_map.50
  22.8 2.7 %collective-permute-done.5.refs_2_ = s32[56,384]{1,0:T(8,128)S(1)} collective-permute-done((s32[56,384]{1,0:T(8,128)S(1)}, s32[56,384]{1,0:T(8,128)S(1)}, u32[]{:S(2)}, u32[]{:S(2)}) %collective-permute-start.5) | collective-permute-done | bytes 86048 | tf_op jit(solution)/shard_map/ppermute | solution.py:658
  25.4 2.7 %collective-permute-done.6.refs_3_ = s32[56,384]{1,0:T(8,128)S(1)} collective-permute-done((s32[56,384]{1,0:T(8,128)S(1)}, s32[56,384]{1,0:T(8,128)S(1)}, u32[]{:S(2)}, u32[]{:S(2)}) %collective-permute-start.6) | collective-permute-done | bytes 86048 | tf_op jit(solution)/shard_map/ppermute | solution.py:658
  28.1 0.0 collective-permute-done.7.refs_4_
  28.1 0.0 copy-done.1
  28.1 2.2 %shard_map.51 = (f32[96,128]{1,0:T(8,128)S(1)}, bf16[48,128]{1,0:T(8,128)(2,1)S(1)}, bf16[48,128]{1,0:T(8,128)(2,1)S(1)}, bf16[48,128]{1,0:T(8,128)(2,1)S(1)}, f32[48,128]{1,0:T(8,128)S(1)}) custom-call(s32[4]{0:T(128)S(1)} %copy-done.1, s32[48,384]{1,0:T(8,128)S(1)} %get-tuple-element.35.refs_0_, s32[56,384]{1,0:T(8,128)S(1)} %get-tuple-element.36.refs_1_, ...), custom_call_target="tpu_custom_call" | custom-call | flops 67108864 | bytes 2097152 | tf_op jit(solution)/shard_map/pallas_call | solution.py:758
  30.3 2.7 %collective-permute-start.11 = (f32[48,128]{1,0:T(8,128)S(1)}, f32[48,128]{1,0:T(8,128)S(1)}, u32[]{:S(2)}, u32[]{:S(2)}) collective-permute-start(f32[48,128]{1,0:T(8,128)S(1)} %get-tuple-element.46), channel_id=1, source_target_pairs={{0,4},{1,5},{4,8},{5,9},{6,2},{7,3},{8,12},{9,13},{10,6},{11,7},{1... | collective-permute-start | bytes 73736 | tf_op jit(solution)/shard_map/ppermute | solution.py:751
  32.9 0.5 %collective-permute-start.8 = (bf16[48,128]{1,0:T(8,128)(2,1)S(1)}, bf16[48,128]{1,0:T(8,128)(2,1)S(1)}, u32[]{:S(2)}, u32[]{:S(2)}) collective-permute-start(bf16[48,128]{1,0:T(8,128)(2,1)S(1)} %get-tuple-element.43), channel_id=1, source_target_pairs={{0,3},{1,2},{2,1},{3,0},{4,7},{5,6},{6,5},{7,4},{8,11},{9,10},{10,... | collective-permute-start | bytes 36872 | tf_op jit(solution)/shard_map/ppermute | solution.py:658
  33.5 0.9 %collective-permute-start.9 = (bf16[48,128]{1,0:T(8,128)(2,1)S(1)}, bf16[48,128]{1,0:T(8,128)(2,1)S(1)}, u32[]{:S(2)}, u32[]{:S(2)}) collective-permute-start(bf16[48,128]{1,0:T(8,128)(2,1)S(1)} %get-tuple-element.44), channel_id=1, source_target_pairs={{0,2},{1,3},{2,0},{3,1},{4,6},{5,7},{6,4},{7,5},{8,10},{9,11},{10,... | collective-permute-start | bytes 36872 | tf_op jit(solution)/shard_map/ppermute | solution.py:658
  34.3 3.1 %collective-permute-start.10 = (bf16[48,128]{1,0:T(8,128)(2,1)S(1)}, bf16[48,128]{1,0:T(8,128)(2,1)S(1)}, u32[]{:S(2)}, u32[]{:S(2)}) collective-permute-start(bf16[48,128]{1,0:T(8,128)(2,1)S(1)} %get-tuple-element.45), channel_id=1, source_target_pairs={{0,1},{1,0},{2,3},{3,2},{4,5},{5,4},{6,7},{7,6},{8,9},{9,8},{10,11... | collective-permute-start | bytes 36872 | tf_op jit(solution)/shard_map/ppermute | solution.py:658
  37.4 1.1 %collective-permute-done.8.refs_0_ = bf16[48,128]{1,0:T(8,128)(2,1)S(1)} collective-permute-done((bf16[48,128]{1,0:T(8,128)(2,1)S(1)}, bf16[48,128]{1,0:T(8,128)(2,1)S(1)}, u32[]{:S(2)}, u32[]{:S(2)}) %collective-permute-start.8) | collective-permute-done | bytes 12320 | tf_op jit(solution)/shard_map/ppermute | solution.py:658
  38.5 0.0 collective-permute-done.9.refs_1_
  38.5 0.6 %collective-permute-done.10.refs_2_ = bf16[48,128]{1,0:T(8,128)(2,1)S(1)} collective-permute-done((bf16[48,128]{1,0:T(8,128)(2,1)S(1)}, bf16[48,128]{1,0:T(8,128)(2,1)S(1)}, u32[]{:S(2)}, u32[]{:S(2)}) %collective-permute-start.10) | collective-permute-done | bytes 12320 | tf_op jit(solution)/shard_map/ppermute | solution.py:658
  39.1 0.0 collective-permute-done.11.refs_3_
  39.1 0.8 %shard_map.52 = f32[50,96]{1,0:T(8,128)} custom-call(f32[96,128]{1,0:T(8,128)S(1)} %get-tuple-element.42.own_ref, bf16[48,128]{1,0:T(8,128)(2,1)S(1)} %collective-permute-done.8.refs_0_, bf16[48,128]{1,0:T(8,128)(2,1)S(1)} %collective-permute-done.9.refs_1_, bf16[48,128]{1,0:T(8,128)(2,1)S(1)} %collective-permute-done.10.refs_2_, ...), custom_call_target="tpu_custom_call" | custom-call | tf_op jit(solution)/shard_map/pallas_call | solution.py:768
  (2 shorter events, 0.0 us)
Async XLA Ops:
  0.0 3.4 %copy-start.2 = (s32[2048]{0:T(1024)S(1)}, s32[2048]{0:T(1024)}, u32[]{:S(2)}) copy-start(s32[2048]{0:T(1024)} %param.5) | copy-start | bytes 24580
  2.1 7.7 %collective-permute-start.1 = (bf16[1056,384]{1,0:T(8,128)(2,1)S(1)}, bf16[1056,384]{1,0:T(8,128)(2,1)S(1)}, u32[]{:S(2)}, u32[]{:S(2)}) collective-permute-start(bf16[1056,384]{1,0:T(8,128)(2,1)S(1)} %get-tuple-element.29), channel_id=1, source_target_pairs={{0,4},{4,0},{8,12},{12,8},{1,5},{5,1},{9,13},{13,9},{2,6},{6,2},{1... | collective-permute-start | bytes 2433032 | tf_op jit(solution)/shard_map/ppermute | solution.py:667
  2.7 14.0 %collective-permute-start = (bf16[1056,384]{1,0:T(8,128)(2,1)S(1)}, bf16[1056,384]{1,0:T(8,128)(2,1)S(1)}, u32[]{:S(2)}, u32[]{:S(2)}) collective-permute-start(bf16[1056,384]{1,0:T(8,128)(2,1)S(1)} %get-tuple-element.28), channel_id=1, source_target_pairs={{4,8},{8,4},{5,9},{9,5},{6,10},{10,6},{7,11},{11,7},{20,24},{24,20... | collective-permute-start | bytes 2433032 | tf_op jit(solution)/shard_map/ppermute | solution.py:667
  4.5 7.1 %collective-permute-start.2 = (s32[48,384]{1,0:T(8,128)S(1)}, s32[48,384]{1,0:T(8,128)S(1)}, u32[]{:S(2)}, u32[]{:S(2)}) collective-permute-start(s32[48,384]{1,0:T(8,128)S(1)} %get-tuple-element.32), channel_id=1, source_target_pairs={{0,3},{1,2},{2,1},{3,0},{4,7},{5,6},{6,5},{7,4},{8,11},{9,10},{10,... | collective-permute-start | bytes 221192 | tf_op jit(solution)/shard_map/ppermute | solution.py:658
  9.2 7.5 %collective-permute-start.3 = (s32[48,384]{1,0:T(8,128)S(1)}, s32[48,384]{1,0:T(8,128)S(1)}, u32[]{:S(2)}, u32[]{:S(2)}) collective-permute-start(s32[48,384]{1,0:T(8,128)S(1)} %get-tuple-element.33), channel_id=1, source_target_pairs={{0,2},{1,3},{2,0},{3,1},{4,6},{5,7},{6,4},{7,5},{8,10},{9,11},{10,... | collective-permute-start | bytes 221192 | tf_op jit(solution)/shard_map/ppermute | solution.py:658
  9.2 7.5 %collective-permute-start.4 = (s32[48,384]{1,0:T(8,128)S(1)}, s32[48,384]{1,0:T(8,128)S(1)}, u32[]{:S(2)}, u32[]{:S(2)}) collective-permute-start(s32[48,384]{1,0:T(8,128)S(1)} %get-tuple-element.34), channel_id=1, source_target_pairs={{0,1},{1,0},{2,3},{3,2},{4,5},{5,4},{6,7},{7,6},{8,9},{9,8},{10,11... | collective-permute-start | bytes 221192 | tf_op jit(solution)/shard_map/ppermute | solution.py:658
  10.7 11.8 %copy-start = (s32[50,384]{1,0:T(8,128)S(1)}, s32[50,384]{1,0:T(8,128)}, u32[]{:S(2)}) copy-start(s32[50,384]{1,0:T(8,128)} %annot_ref.3) | copy-start | bytes 230404
  16.7 11.4 %copy-start.1 = (s32[4]{0:T(128)S(1)}, s32[4]{0:T(128)}, u32[]{:S(2)}) copy-start(s32[4]{0:T(128)} %reach_ref.1) | copy-start | bytes 52
  18.0 7.4 %collective-permute-start.5 = (s32[56,384]{1,0:T(8,128)S(1)}, s32[56,384]{1,0:T(8,128)S(1)}, u32[]{:S(2)}, u32[]{:S(2)}) collective-permute-start(s32[56,384]{1,0:T(8,128)S(1)} %get-tuple-element.37), channel_id=1, source_target_pairs={{0,3},{1,2},{2,1},{3,0},{4,7},{5,6},{6,5},{7,4},{8,11},{9,10},{10,... | collective-permute-start | bytes 258056 | tf_op jit(solution)/shard_map/ppermute | solution.py:658
  18.1 10.0 %collective-permute-start.6 = (s32[56,384]{1,0:T(8,128)S(1)}, s32[56,384]{1,0:T(8,128)S(1)}, u32[]{:S(2)}, u32[]{:S(2)}) collective-permute-start(s32[56,384]{1,0:T(8,128)S(1)} %get-tuple-element.38), channel_id=1, source_target_pairs={{0,2},{1,3},{2,0},{3,1},{4,6},{5,7},{6,4},{7,5},{8,10},{9,11},{10,... | collective-permute-start | bytes 258056 | tf_op jit(solution)/shard_map/ppermute | solution.py:658
  18.5 9.6 %collective-permute-start.7 = (s32[56,384]{1,0:T(8,128)S(1)}, s32[56,384]{1,0:T(8,128)S(1)}, u32[]{:S(2)}, u32[]{:S(2)}) collective-permute-start(s32[56,384]{1,0:T(8,128)S(1)} %get-tuple-element.39), channel_id=1, source_target_pairs={{0,1},{1,0},{2,3},{3,2},{4,5},{5,4},{6,7},{7,6},{8,9},{9,8},{10,11... | collective-permute-start | bytes 258056 | tf_op jit(solution)/shard_map/ppermute | solution.py:658
  30.3 8.8 %collective-permute-start.11 = (f32[48,128]{1,0:T(8,128)S(1)}, f32[48,128]{1,0:T(8,128)S(1)}, u32[]{:S(2)}, u32[]{:S(2)}) collective-permute-start(f32[48,128]{1,0:T(8,128)S(1)} %get-tuple-element.46), channel_id=1, source_target_pairs={{0,4},{1,5},{4,8},{5,9},{6,2},{7,3},{8,12},{9,13},{10,6},{11,7},{1... | collective-permute-start | bytes 73736 | tf_op jit(solution)/shard_map/ppermute | solution.py:751
  32.9 5.6 %collective-permute-start.8 = (bf16[48,128]{1,0:T(8,128)(2,1)S(1)}, bf16[48,128]{1,0:T(8,128)(2,1)S(1)}, u32[]{:S(2)}, u32[]{:S(2)}) collective-permute-start(bf16[48,128]{1,0:T(8,128)(2,1)S(1)} %get-tuple-element.43), channel_id=1, source_target_pairs={{0,3},{1,2},{2,1},{3,0},{4,7},{5,6},{6,5},{7,4},{8,11},{9,10},{10,... | collective-permute-start | bytes 36872 | tf_op jit(solution)/shard_map/ppermute | solution.py:658
  33.5 5.0 %collective-permute-start.9 = (bf16[48,128]{1,0:T(8,128)(2,1)S(1)}, bf16[48,128]{1,0:T(8,128)(2,1)S(1)}, u32[]{:S(2)}, u32[]{:S(2)}) collective-permute-start(bf16[48,128]{1,0:T(8,128)(2,1)S(1)} %get-tuple-element.44), channel_id=1, source_target_pairs={{0,2},{1,3},{2,0},{3,1},{4,6},{5,7},{6,4},{7,5},{8,10},{9,11},{10,... | collective-permute-start | bytes 36872 | tf_op jit(solution)/shard_map/ppermute | solution.py:658
  34.3 4.7 %collective-permute-start.10 = (bf16[48,128]{1,0:T(8,128)(2,1)S(1)}, bf16[48,128]{1,0:T(8,128)(2,1)S(1)}, u32[]{:S(2)}, u32[]{:S(2)}) collective-permute-start(bf16[48,128]{1,0:T(8,128)(2,1)S(1)} %get-tuple-element.45), channel_id=1, source_target_pairs={{0,1},{1,0},{2,3},{3,2},{4,5},{5,4},{6,7},{7,6},{8,9},{9,8},{10,11... | collective-permute-start | bytes 36872 | tf_op jit(solution)/shard_map/ppermute | solution.py:658

commit v9 on v8

--- a/solution.py
+++ b/solution.py
@@ -244,7 +244,7 @@
 
 def far_kernel(groups, share, weighted_ref, side_ref, close_ref, totals_ref, *refs):
     own_parts, own_sum_ref = refs[:groups], refs[groups]
-    targets, (near, window, tile, folded, flipped) = refs[groups + 1 : 2 * groups + 1], refs[2 * groups + 1 :]
+    targets, (near, window, tile, folded, flipped, extras) = refs[groups + 1 : 2 * groups + 1], refs[2 * groups + 1 :]
     snps = tile.shape[1]
     own_sum_ref[...] = sum((part[...] for part in own_parts[1:]), own_parts[0][...])
     window[...] = side_dot(True, weighted_ref, side_ref, near)
@@ -268,14 +268,25 @@
     apart = jnp.sum(
         jnp.where(iota(square, 0) == iota(square, 1), tile[0:snps, :], 0.0), axis=0, keepdims=True
     )
-    extras = to_fields(
-        jnp.concatenate(
-            [totals_ref[0:2, :], tile[snps : snps + 1, :], apart, jnp.zeros((4, snps))], axis=0
+    tiles = snps // LANES
+    shared = [totals_ref[0:1, k * LANES : (k + 1) * LANES] for k in range(tiles)]
+    shared.append(totals_ref[1:2, 0:LANES])
+    by_column = jnp.concatenate([tile[snps : snps + 1, :], apart, jnp.zeros((6, snps))], axis=0)
+    for owner in range(groups):
+        start = owner * (snps // groups)
+        columns = pltpu.roll(by_column, snps - start, 1) if owner else by_column
+        extras[8 * owner : 8 * (owner + 1), :] = to_fields(
+            jnp.concatenate(
+                [*shared, columns[0:2, 0:LANES], jnp.zeros((6 - tiles - 1, LANES))], axis=0
+            )
         )
-    )
-    send_shares(groups, folded, share, targets)
-    for target in targets:
-        target[share:, :] = extras
+    me = lax.axis_index("hap")
+    for step, target in enumerate(targets):
+        owner = partner(me, step, groups)
+        counts = folded[pl.ds(pl.multiple_of(owner * share, 8), share), :]
+        for k in range(tiles):
+            target[k * share : (k + 1) * share, :] = counts[:, k * LANES : (k + 1) * LANES]
+        target[tiles * share :, :] = extras[pl.ds(pl.multiple_of(owner * 8, 8), 8), :]
 
 
 def near_kernel(groups, share, weighted_ref, far_ref, close_ref, totals_ref, *refs):
@@ -482,6 +493,13 @@
     return jnp.concatenate([packed, pltpu.roll(packed, HALF_LANES, 1)], axis=0)
 
 
+def dot_rounded(values, right, axis):
+    dims = (((axis,), (0,)), ((), ()))
+    return lax.dot_general(
+        values.astype(jnp.bfloat16), right, dims, preferred_element_type=jnp.float32
+    )
+
+
 def column_score_kernel(groups, share, reach_ref, *refs):
     own_sum_ref, near_parts = refs[0], refs[1 : groups + 1]
     annot_ref, near_annot_ref = refs[groups + 1 : groups + 3]
@@ -508,16 +526,22 @@
 
     own_counts = own_sum_ref[...]
     near_sums = sum((part[...] for part in near_parts[1:]), near_parts[0][...])
-    extras = from_fields(near_sums[share:, :])
-    near_counts = near_sums[0:share, :]
-
-    own_stats, near_stats, lines = [], [], []
+    tiles = snps // LANES
+    near_counts = jnp.concatenate(
+        [near_sums[k * share : (k + 1) * share, :] for k in range(tiles)], axis=1
+    )
+    extras = from_fields(near_sums[tiles * share :, :])
+
+    own_stats, near_stats, lines, near_lines = [], [], [], []
     for pop in range(2):
-        count = extras[pop][1:2, :]
-        own_stats.append(column_stats(extras[pop][0:1, :], count))
-        near_stats.append(column_stats(extras[pop][2:3, :], count))
-        lines += [*own_stats[pop], *near_stats[pop], extras[pop][0:1, :], extras[pop][3:4, :]]
-    table[:, 0:16] = jnp.concatenate(lines, axis=0).T
+        count = extras[pop][tiles : tiles + 1, :]
+        totals = jnp.concatenate([extras[pop][k : k + 1, :] for k in range(tiles)], axis=1)
+        own_stats.append(column_stats(totals, jnp.concatenate([count] * tiles, axis=1)))
+        near_stats.append(column_stats(extras[pop][tiles + 1 : tiles + 2, :], count))
+        lines += [*own_stats[pop], totals]
+        near_lines += [*near_stats[pop], extras[pop][tiles + 2 : tiles + 3, :]]
+    table[:, 0:8] = jnp.concatenate(lines, axis=0).T
+    near_table = jnp.concatenate(near_lines, axis=0).T[0:wide, :]
 
     low_rows = pl.multiple_of(me * share, 8)
     high_rows = pl.multiple_of(half + me * share, 8)
@@ -535,13 +559,13 @@
     row = jnp.where(low, local, local + half - share) + me * share
     product = 1.0
     for pop in range(2):
-        row_stats = [here[:, 8 * pop + k : 8 * pop + k + 1] for k in range(3)]
+        row_stats = [here[:, 4 * pop + k : 4 * pop + k + 1] for k in range(3)]
         product *= correlation(row_stats, own_stats[pop], own_fields[pop])
     inside = (low & (col > row)) | (~low & (col >= half) & (col < row))
     own_kept = jnp.where(inside & (jnp.abs(col - row) <= reach_here), product, 0.0)
     rows_here = both(annot_ref).astype(jnp.bfloat16)
-    scores[...] = dot_split(own_kept, rows_here, 0)
-    direct = dot_split(own_kept, annot_ref[...].astype(jnp.bfloat16), 1)
+    scores[...] = dot_rounded(own_kept, rows_here, 0)
+    direct = dot_rounded(own_kept, annot_ref[...].astype(jnp.bfloat16), 1)
     scores[pl.ds(low_rows, share), :] += direct[0:share, :]
     scores[pl.ds(high_rows, share), :] += direct[share:, :]
 
@@ -572,23 +596,17 @@
     apart = jnp.abs(own_row - (lane + me * wide))
     ahead = (own_row - (lane + me * wide)) * jnp.where(upper, 1, -1) > 0
     real = ahead & (lane < wide) & ((lane >= size) | (iota(shape, 0) < groups * size))
-    near_lines = jnp.concatenate([*near_stats[0], *near_stats[1], *near_stats[0][0:2]], axis=0)
-    near_lines = mine(
-        [near_lines[:, 0:LANES]]
-        + [pltpu.roll(near_lines, snps - group * wide, 1)[:, 0:LANES] for group in range(1, groups)]
-    )
     product = 1.0
     for pop in range(2):
         row_stats = [
             jnp.where(
                 is_left,
-                left_table[:, 8 * pop + k : 8 * pop + k + 1],
-                right_table[:, 8 * pop + k : 8 * pop + k + 1],
+                left_table[:, 4 * pop + k : 4 * pop + k + 1],
+                right_table[:, 4 * pop + k : 4 * pop + k + 1],
             )
             for k in range(3)
         ]
-        col_stats = [near_lines[3 * pop + k : 3 * pop + k + 1, :] for k in range(3)]
-        product *= correlation(row_stats, col_stats, near_fields[pop])
+        product *= correlation(row_stats, near_stats[pop], near_fields[pop])
     near_here = jnp.where(real & (snps - apart <= reach_here), product, 0.0)
     near_there = jnp.where(real & (snps - apart <= reach_there), product, 0.0)
 
@@ -600,21 +618,20 @@
     slice_rows = pl.ds(pl.multiple_of(me * wide, 8), wide)
     their_annots = near_annot_ref[slice_rows, :]
     columns = jnp.concatenate([their_annots, jnp.zeros((LANES - wide, LANES), jnp.float32)], axis=0)
-    direct = dot_split(sides(near_here), columns.astype(jnp.bfloat16), 1)
+    direct = dot_rounded(sides(near_here), columns.astype(jnp.bfloat16), 1)
     places = left_places + right_places
     for number, place in enumerate(places):
         scores[pl.ds(pl.multiple_of(place, 8), size), :] += direct[number * size : (number + 1) * size, :]
     own_rows = jnp.concatenate(rows_of(annot_ref, places), axis=0).astype(jnp.bfloat16)
-    near_scores = dot_split(sides(near_there), own_rows, 0)[0:wide, :]
+    near_scores = dot_rounded(sides(near_there), own_rows, 0)[0:wide, :]
 
     mine_table = table[slice_rows, :]
     self_product, far_product = 1.0, 1.0
     for pop in range(2):
-        k = 8 * pop
-        own_row = [mine_table[:, k + s : k + s + 1] for s in range(3)]
-        near_row = [mine_table[:, k + 3 + s : k + 4 + s] for s in range(3)]
-        self_product *= correlation(own_row, own_row, mine_table[:, k + 6 : k + 7])
-        far_product *= correlation(own_row, near_row, mine_table[:, k + 7 : k + 8])
+        own_row = [mine_table[:, 4 * pop + k : 4 * pop + k + 1] for k in range(4)]
+        near_row = [near_table[:, 4 * pop + k : 4 * pop + k + 1] for k in range(4)]
+        self_product *= correlation(own_row, own_row, own_row[3])
+        far_product *= correlation(own_row, near_row, near_row[3])
     my_annots = annot_ref[slice_rows, :]
     out_ref[...] = (
         scores[slice_rows, :]
@@ -720,9 +737,16 @@
         )
         own_sum, *near_parts = call(
             functools.partial(far_kernel, groups, share),
-            near_shapes,
+            [near_shapes[0]] + [shape((share * (snps // LANES) + 8, LANES), i32)] * groups,
             [VMEM] * (4 + groups),
-            [near, pltpu.VMEM(window, f32), tile, folded, pltpu.VMEM((snps, LANES), f32)],
+            [
+                near,
+                pltpu.VMEM(window, f32),
+                tile,
+                folded,
+                pltpu.VMEM((snps, LANES), f32),
+                pltpu.VMEM((8 * groups, LANES), i32),
+            ],
             **work,
         )(weighted, from_far, close_counts, totals, *own_parts)
     else:

time: 40 us -> 39.2 us (0.980)
  waiting for transfers between devices: 13 us -> 12.5 us
    ppermute x9, waiting for transfers between devices: 13 us -> 12.4 us  [around(): lax.ppermute(value, 'hap', [(source, partner(source, step, groups)) for s...]
where the time goes in v9:
time: 39.2 us; the launch traced here: 39.1 us
  starting transfers between devices  18.1 us (46%)
  waiting for transfers between devices  12.5 us (32%)
  Pallas kernels  8.46 us (22%)
    ppermute x9, starting transfers between devices, around(): lax.ppermute(value, 'hap', [(source, partner(source, step, groups)) for s...  14.2 us
    ppermute x9, waiting for transfers between devices, around(): lax.ppermute(value, 'hap', [(source, partner(source, step, groups)) for s...  12.4 us
    ppermute x1, starting transfers between devices, to_neighbour(): return lax.ppermute(value, ('snp', 'hap'), pairs)  2.6 us
    pallas_call x1, Pallas kernels, per_device(): call(prepare_kernel, [shape((rows, snps), bf16), packed, packed], [HBM, H...  2.14 us
    pallas_call x1, Pallas kernels, per_device(): call(functools.partial(column_score_kernel, groups, share), [own_share] +...  2.01 us
    pallas_call x1, Pallas kernels, per_device(): call(functools.partial(far_kernel, groups, share), [near_shapes[0]] + [sh...  1.3 us
    ppermute x2, starting transfers between devices, swapped(): return lax.ppermute(value, 'snp', pairs)  1.22 us
    pallas_call x1, Pallas kernels, per_device(): call(functools.partial(own_kernel, groups, share), [shape((snps + 16, row...  1.13 us
  transfers between devices with their start and end apart: 12, of which 6 were waited for; matrix products, arithmetic and copies ran while one was open for 0% of the time, Pallas kernels for 6%

profile of v9, /device:TPU:0, one launch (start us, length us, event | category | flops | bytes accessed | tf_op | source)
XLA Modules:
  0.0 39.1 jit_solution(14033111075608855403)
XLA Ops:
  0.0 0.0 copy-start.2
  0.0 2.1 %shard_map.46 = (bf16[2048,384]{1,0:T(8,128)(2,1)S(1)}, bf16[1056,384]{1,0:T(8,128)(2,1)S(1)}, bf16[1056,384]{1,0:T(8,128)(2,1)S(1)}) custom-call(s32[2048,384]{1,0:T(8,128)} %hap_ref.1, s32[50,384]{1,0:T(8,128)} %annot_ref.3), custom_call_target="tpu_custom_call" | custom-call | bytes 6291456 | tf_op jit(solution)/shard_map/pallas_call | solution.py:703
  2.1 0.5 %collective-permute-start.1 = (bf16[1056,384]{1,0:T(8,128)(2,1)S(1)}, bf16[1056,384]{1,0:T(8,128)(2,1)S(1)}, u32[]{:S(2)}, u32[]{:S(2)}) collective-permute-start(bf16[1056,384]{1,0:T(8,128)(2,1)S(1)} %get-tuple-element.29), channel_id=1, source_target_pairs={{0,4},{4,0},{8,12},{12,8},{1,5},{5,1},{9,13},{13,9},{2,6},{6,2},{1... | collective-permute-start | bytes 2433032 | tf_op jit(solution)/shard_map/ppermute | solution.py:684
  2.7 0.7 %collective-permute-start = (bf16[1056,384]{1,0:T(8,128)(2,1)S(1)}, bf16[1056,384]{1,0:T(8,128)(2,1)S(1)}, u32[]{:S(2)}, u32[]{:S(2)}) collective-permute-start(bf16[1056,384]{1,0:T(8,128)(2,1)S(1)} %get-tuple-element.28), channel_id=1, source_target_pairs={{4,8},{8,4},{5,9},{9,5},{6,10},{10,6},{7,11},{11,7},{20,24},{24,20... | collective-permute-start | bytes 2433032 | tf_op jit(solution)/shard_map/ppermute | solution.py:684
  3.4 0.0 copy-done.2
  3.4 1.1 %shard_map.47 = (bf16[400,2048]{1,0:T(8,128)(2,1)S(1)}, f32[8,384]{1,0:T(8,128)S(1)}, s32[48,384]{1,0:T(8,128)S(1)}, s32[48,384]{1,0:T(8,128)S(1)}, s32[48,384]{1,0:T(8,128)S(1)}, /*index=5*/s32[48,384]{1,0:T(8,128)S(1)}) custom-call(bf16[2048,384]{1,0:T(8,128)(2,1)S(1)} %get-tuple-element.26.alleles_ref, s32[1,2048]{1,0:T(1,128)S(1)} %bitcast.1), custom_call_target="tpu_custom_call" | custom-call | flops 603979776 | bytes 3145728 | tf_op jit(solution)/shard_map/pallas_call | solution.py:719
  4.5 4.7 %collective-permute-start.2 = (s32[48,384]{1,0:T(8,128)S(1)}, s32[48,384]{1,0:T(8,128)S(1)}, u32[]{:S(2)}, u32[]{:S(2)}) collective-permute-start(s32[48,384]{1,0:T(8,128)S(1)} %get-tuple-element.32), channel_id=1, source_target_pairs={{0,3},{1,2},{2,1},{3,0},{4,7},{5,6},{6,5},{7,4},{8,11},{9,10},{10,... | collective-permute-start | bytes 221192 | tf_op jit(solution)/shard_map/ppermute | solution.py:675
  9.2 0.0 collective-permute-start.3
  9.2 0.6 %collective-permute-start.4 = (s32[48,384]{1,0:T(8,128)S(1)}, s32[48,384]{1,0:T(8,128)S(1)}, u32[]{:S(2)}, u32[]{:S(2)}) collective-permute-start(s32[48,384]{1,0:T(8,128)S(1)} %get-tuple-element.34), channel_id=1, source_target_pairs={{0,1},{1,0},{2,3},{3,2},{4,5},{5,4},{6,7},{7,6},{8,9},{9,8},{10,11... | collective-permute-start | bytes 221192 | tf_op jit(solution)/shard_map/ppermute | solution.py:675
  9.9 0.0 collective-permute-done.1.side_ref
  9.9 0.9 %shard_map.48.close_ref = f32[400,256]{1,0:T(8,128)S(1)} custom-call(bf16[400,2048]{1,0:T(8,128)(2,1)S(1)} %get-tuple-element.27.weighted_ref, bf16[1056,384]{1,0:T(8,128)(2,1)S(1)} %collective-permute-done.1.side_ref), custom_call_target="tpu_custom_call" | custom-call | flops 402653184 | bytes 3145728 | tf_op jit(solution)/shard_map/pallas_call | solution.py:735
  10.7 0.0 copy-start
  10.7 0.9 %collective-permute-done.2.refs_1_ = s32[48,384]{1,0:T(8,128)S(1)} collective-permute-done((s32[48,384]{1,0:T(8,128)S(1)}, s32[48,384]{1,0:T(8,128)S(1)}, u32[]{:S(2)}, u32[]{:S(2)}) %collective-permute-start.2) | collective-permute-done | bytes 73760 | tf_op jit(solution)/shard_map/ppermute | solution.py:675
  11.7 5.0 %collective-permute-done.3.refs_2_ = s32[48,384]{1,0:T(8,128)S(1)} collective-permute-done((s32[48,384]{1,0:T(8,128)S(1)}, s32[48,384]{1,0:T(8,128)S(1)}, u32[]{:S(2)}, u32[]{:S(2)}) %collective-permute-start.3) | collective-permute-done | bytes 73760 | tf_op jit(solution)/shard_map/ppermute | solution.py:675
  16.7 0.0 collective-permute-done.4.refs_3_
  16.7 0.0 collective-permute-done.side_ref
  16.7 0.0 copy-start.1
  16.7 1.3 %shard_map.49 = (s32[48,384]{1,0:T(8,128)S(1)}, s32[152,128]{1,0:T(8,128)S(1)}, s32[152,128]{1,0:T(8,128)S(1)}, s32[152,128]{1,0:T(8,128)S(1)}, s32[152,128]{1,0:T(8,128)S(1)}) custom-call(bf16[400,2048]{1,0:T(8,128)(2,1)S(1)} %get-tuple-element.27.weighted_ref, bf16[1056,384]{1,0:T(8,128)(2,1)S(1)} %collective-permute-done.side_ref, ...), custom_call_target="tpu_custom_call" | custom-call | flops 402653184 | bytes 3145728 | tf_op jit(solution)/shard_map/pallas_call | solution.py:738
  18.0 0.1 collective-permute-start.5
  18.1 0.5 %collective-permute-start.6 = (s32[152,128]{1,0:T(8,128)S(1)}, s32[152,128]{1,0:T(8,128)S(1)}, u32[]{:S(2)}, u32[]{:S(2)}) collective-permute-start(s32[152,128]{1,0:T(8,128)S(1)} %get-tuple-element.38), channel_id=1, source_target_pairs={{0,2},{1,3},{2,0},{3,1},{4,6},{5,7},{6,4},{7,5},{8,10},{9,11},{10,... | collective-permute-start | bytes 233480 | tf_op jit(solution)/shard_map/ppermute | solution.py:675
  18.5 3.9 %collective-permute-start.7 = (s32[152,128]{1,0:T(8,128)S(1)}, s32[152,128]{1,0:T(8,128)S(1)}, u32[]{:S(2)}, u32[]{:S(2)}) collective-permute-start(s32[152,128]{1,0:T(8,128)S(1)} %get-tuple-element.39), channel_id=1, source_target_pairs={{0,1},{1,0},{2,3},{3,2},{4,5},{5,4},{6,7},{7,6},{8,9},{9,8},{10,11... | collective-permute-start | bytes 233480 | tf_op jit(solution)/shard_map/ppermute | solution.py:675
  22.5 0.0 copy-done
  22.5 0.3 shard_map.50
  22.8 2.5 %collective-permute-done.5.refs_2_ = s32[152,128]{1,0:T(8,128)S(1)} collective-permute-done((s32[152,128]{1,0:T(8,128)S(1)}, s32[152,128]{1,0:T(8,128)S(1)}, u32[]{:S(2)}, u32[]{:S(2)}) %collective-permute-start.5) | collective-permute-done | bytes 77856 | tf_op jit(solution)/shard_map/ppermute | solution.py:675
  25.3 2.3 %collective-permute-done.6.refs_3_ = s32[152,128]{1,0:T(8,128)S(1)} collective-permute-done((s32[152,128]{1,0:T(8,128)S(1)}, s32[152,128]{1,0:T(8,128)S(1)}, u32[]{:S(2)}, u32[]{:S(2)}) %collective-permute-start.6) | collective-permute-done | bytes 77856 | tf_op jit(solution)/shard_map/ppermute | solution.py:675
  27.6 0.0 collective-permute-done.7.refs_4_
  27.6 0.0 copy-done.1
  27.6 2.0 %shard_map.51 = (f32[96,128]{1,0:T(8,128)S(1)}, bf16[48,128]{1,0:T(8,128)(2,1)S(1)}, bf16[48,128]{1,0:T(8,128)(2,1)S(1)}, bf16[48,128]{1,0:T(8,128)(2,1)S(1)}, f32[48,128]{1,0:T(8,128)S(1)}) custom-call(s32[4]{0:T(128)S(1)} %copy-done.1, s32[48,384]{1,0:T(8,128)S(1)} %get-tuple-element.35.refs_0_, s32[152,128]{1,0:T(8,128)S(1)} %get-tuple-element.36.refs_1_, ...), custom_call_target="tpu_custom_call" | custom-call | flops 67108864 | bytes 2097152 | tf_op jit(solution)/shard_map/pallas_call | solution.py:782
  29.6 2.6 %collective-permute-start.11 = (f32[48,128]{1,0:T(8,128)S(1)}, f32[48,128]{1,0:T(8,128)S(1)}, u32[]{:S(2)}, u32[]{:S(2)}) collective-permute-start(f32[48,128]{1,0:T(8,128)S(1)} %get-tuple-element.46), channel_id=1, source_target_pairs={{0,4},{1,5},{4,8},{5,9},{6,2},{7,3},{8,12},{9,13},{10,6},{11,7},{1... | collective-permute-start | bytes 73736 | tf_op jit(solution)/shard_map/ppermute | solution.py:775
  32.2 0.8 %collective-permute-start.8 = (bf16[48,128]{1,0:T(8,128)(2,1)S(1)}, bf16[48,128]{1,0:T(8,128)(2,1)S(1)}, u32[]{:S(2)}, u32[]{:S(2)}) collective-permute-start(bf16[48,128]{1,0:T(8,128)(2,1)S(1)} %get-tuple-element.43), channel_id=1, source_target_pairs={{0,3},{1,2},{2,1},{3,0},{4,7},{5,6},{6,5},{7,4},{8,11},{9,10},{10,... | collective-permute-start | bytes 36872 | tf_op jit(solution)/shard_map/ppermute | solution.py:675
  33.0 0.9 %collective-permute-start.9 = (bf16[48,128]{1,0:T(8,128)(2,1)S(1)}, bf16[48,128]{1,0:T(8,128)(2,1)S(1)}, u32[]{:S(2)}, u32[]{:S(2)}) collective-permute-start(bf16[48,128]{1,0:T(8,128)(2,1)S(1)} %get-tuple-element.44), channel_id=1, source_target_pairs={{0,2},{1,3},{2,0},{3,1},{4,6},{5,7},{6,4},{7,5},{8,10},{9,11},{10,... | collective-permute-start | bytes 36872 | tf_op jit(solution)/shard_map/ppermute | solution.py:675
  33.9 2.8 %collective-permute-start.10 = (bf16[48,128]{1,0:T(8,128)(2,1)S(1)}, bf16[48,128]{1,0:T(8,128)(2,1)S(1)}, u32[]{:S(2)}, u32[]{:S(2)}) collective-permute-start(bf16[48,128]{1,0:T(8,128)(2,1)S(1)} %get-tuple-element.45), channel_id=1, source_target_pairs={{0,1},{1,0},{2,3},{3,2},{4,5},{5,4},{6,7},{7,6},{8,9},{9,8},{10,11... | collective-permute-start | bytes 36872 | tf_op jit(solution)/shard_map/ppermute | solution.py:675
  36.7 1.3 %collective-permute-done.8.refs_0_ = bf16[48,128]{1,0:T(8,128)(2,1)S(1)} collective-permute-done((bf16[48,128]{1,0:T(8,128)(2,1)S(1)}, bf16[48,128]{1,0:T(8,128)(2,1)S(1)}, u32[]{:S(2)}, u32[]{:S(2)}) %collective-permute-start.8) | collective-permute-done | bytes 12320 | tf_op jit(solution)/shard_map/ppermute | solution.py:675
  38.0 0.0 collective-permute-done.9.refs_1_
  38.0 0.4 collective-permute-done.10.refs_2_
  38.3 0.0 collective-permute-done.11.refs_3_
  38.3 0.8 %shard_map.52 = f32[50,96]{1,0:T(8,128)} custom-call(f32[96,128]{1,0:T(8,128)S(1)} %get-tuple-element.42.own_ref, bf16[48,128]{1,0:T(8,128)(2,1)S(1)} %collective-permute-done.8.refs_0_, bf16[48,128]{1,0:T(8,128)(2,1)S(1)} %collective-permute-done.9.refs_1_, bf16[48,128]{1,0:T(8,128)(2,1)S(1)} %collective-permute-done.10.refs_2_, ...), custom_call_target="tpu_custom_call" | custom-call | tf_op jit(solution)/shard_map/pallas_call | solution.py:792
  (2 shorter events, 0.0 us)
Async XLA Ops:
  0.0 3.4 %copy-start.2 = (s32[2048]{0:T(1024)S(1)}, s32[2048]{0:T(1024)}, u32[]{:S(2)}) copy-start(s32[2048]{0:T(1024)} %param.5) | copy-start | bytes 24580
  2.1 7.7 %collective-permute-start.1 = (bf16[1056,384]{1,0:T(8,128)(2,1)S(1)}, bf16[1056,384]{1,0:T(8,128)(2,1)S(1)}, u32[]{:S(2)}, u32[]{:S(2)}) collective-permute-start(bf16[1056,384]{1,0:T(8,128)(2,1)S(1)} %get-tuple-element.29), channel_id=1, source_target_pairs={{0,4},{4,0},{8,12},{12,8},{1,5},{5,1},{9,13},{13,9},{2,6},{6,2},{1... | collective-permute-start | bytes 2433032 | tf_op jit(solution)/shard_map/ppermute | solution.py:684
  2.7 14.0 %collective-permute-start = (bf16[1056,384]{1,0:T(8,128)(2,1)S(1)}, bf16[1056,384]{1,0:T(8,128)(2,1)S(1)}, u32[]{:S(2)}, u32[]{:S(2)}) collective-permute-start(bf16[1056,384]{1,0:T(8,128)(2,1)S(1)} %get-tuple-element.28), channel_id=1, source_target_pairs={{4,8},{8,4},{5,9},{9,5},{6,10},{10,6},{7,11},{11,7},{20,24},{24,20... | collective-permute-start | bytes 2433032 | tf_op jit(solution)/shard_map/ppermute | solution.py:684
  4.5 7.1 %collective-permute-start.2 = (s32[48,384]{1,0:T(8,128)S(1)}, s32[48,384]{1,0:T(8,128)S(1)}, u32[]{:S(2)}, u32[]{:S(2)}) collective-permute-start(s32[48,384]{1,0:T(8,128)S(1)} %get-tuple-element.32), channel_id=1, source_target_pairs={{0,3},{1,2},{2,1},{3,0},{4,7},{5,6},{6,5},{7,4},{8,11},{9,10},{10,... | collective-permute-start | bytes 221192 | tf_op jit(solution)/shard_map/ppermute | solution.py:675
  9.2 7.5 %collective-permute-start.3 = (s32[48,384]{1,0:T(8,128)S(1)}, s32[48,384]{1,0:T(8,128)S(1)}, u32[]{:S(2)}, u32[]{:S(2)}) collective-permute-start(s32[48,384]{1,0:T(8,128)S(1)} %get-tuple-element.33), channel_id=1, source_target_pairs={{0,2},{1,3},{2,0},{3,1},{4,6},{5,7},{6,4},{7,5},{8,10},{9,11},{10,... | collective-permute-start | bytes 221192 | tf_op jit(solution)/shard_map/ppermute | solution.py:675
  9.2 7.5 %collective-permute-start.4 = (s32[48,384]{1,0:T(8,128)S(1)}, s32[48,384]{1,0:T(8,128)S(1)}, u32[]{:S(2)}, u32[]{:S(2)}) collective-permute-start(s32[48,384]{1,0:T(8,128)S(1)} %get-tuple-element.34), channel_id=1, source_target_pairs={{0,1},{1,0},{2,3},{3,2},{4,5},{5,4},{6,7},{7,6},{8,9},{9,8},{10,11... | collective-permute-start | bytes 221192 | tf_op jit(solution)/shard_map/ppermute | solution.py:675
  10.7 11.8 %copy-start = (s32[50,384]{1,0:T(8,128)S(1)}, s32[50,384]{1,0:T(8,128)}, u32[]{:S(2)}) copy-start(s32[50,384]{1,0:T(8,128)} %annot_ref.3) | copy-start | bytes 230404
  16.7 10.9 %copy-start.1 = (s32[4]{0:T(128)S(1)}, s32[4]{0:T(128)}, u32[]{:S(2)}) copy-start(s32[4]{0:T(128)} %reach_ref.1) | copy-start | bytes 52
  18.0 7.3 %collective-permute-start.5 = (s32[152,128]{1,0:T(8,128)S(1)}, s32[152,128]{1,0:T(8,128)S(1)}, u32[]{:S(2)}, u32[]{:S(2)}) collective-permute-start(s32[152,128]{1,0:T(8,128)S(1)} %get-tuple-element.37), channel_id=1, source_target_pairs={{0,3},{1,2},{2,1},{3,0},{4,7},{5,6},{6,5},{7,4},{8,11},{9,10},{10,... | collective-permute-start | bytes 233480 | tf_op jit(solution)/shard_map/ppermute | solution.py:675
  18.1 9.5 %collective-permute-start.6 = (s32[152,128]{1,0:T(8,128)S(1)}, s32[152,128]{1,0:T(8,128)S(1)}, u32[]{:S(2)}, u32[]{:S(2)}) collective-permute-start(s32[152,128]{1,0:T(8,128)S(1)} %get-tuple-element.38), channel_id=1, source_target_pairs={{0,2},{1,3},{2,0},{3,1},{4,6},{5,7},{6,4},{7,5},{8,10},{9,11},{10,... | collective-permute-start | bytes 233480 | tf_op jit(solution)/shard_map/ppermute | solution.py:675
  18.5 9.0 %collective-permute-start.7 = (s32[152,128]{1,0:T(8,128)S(1)}, s32[152,128]{1,0:T(8,128)S(1)}, u32[]{:S(2)}, u32[]{:S(2)}) collective-permute-start(s32[152,128]{1,0:T(8,128)S(1)} %get-tuple-element.39), channel_id=1, source_target_pairs={{0,1},{1,0},{2,3},{3,2},{4,5},{5,4},{6,7},{7,6},{8,9},{9,8},{10,11... | collective-permute-start | bytes 233480 | tf_op jit(solution)/shard_map/ppermute | solution.py:675
  29.6 8.7 %collective-permute-start.11 = (f32[48,128]{1,0:T(8,128)S(1)}, f32[48,128]{1,0:T(8,128)S(1)}, u32[]{:S(2)}, u32[]{:S(2)}) collective-permute-start(f32[48,128]{1,0:T(8,128)S(1)} %get-tuple-element.46), channel_id=1, source_target_pairs={{0,4},{1,5},{4,8},{5,9},{6,2},{7,3},{8,12},{9,13},{10,6},{11,7},{1... | collective-permute-start | bytes 73736 | tf_op jit(solution)/shard_map/ppermute | solution.py:775
  32.2 5.8 %collective-permute-start.8 = (bf16[48,128]{1,0:T(8,128)(2,1)S(1)}, bf16[48,128]{1,0:T(8,128)(2,1)S(1)}, u32[]{:S(2)}, u32[]{:S(2)}) collective-permute-start(bf16[48,128]{1,0:T(8,128)(2,1)S(1)} %get-tuple-element.43), channel_id=1, source_target_pairs={{0,3},{1,2},{2,1},{3,0},{4,7},{5,6},{6,5},{7,4},{8,11},{9,10},{10,... | collective-permute-start | bytes 36872 | tf_op jit(solution)/shard_map/ppermute | solution.py:675
  33.0 5.0 %collective-permute-start.9 = (bf16[48,128]{1,0:T(8,128)(2,1)S(1)}, bf16[48,128]{1,0:T(8,128)(2,1)S(1)}, u32[]{:S(2)}, u32[]{:S(2)}) collective-permute-start(bf16[48,128]{1,0:T(8,128)(2,1)S(1)} %get-tuple-element.44), channel_id=1, source_target_pairs={{0,2},{1,3},{2,0},{3,1},{4,6},{5,7},{6,4},{7,5},{8,10},{9,11},{10,... | collective-permute-start | bytes 36872 | tf_op jit(solution)/shard_map/ppermute | solution.py:675
  33.9 4.5 %collective-permute-start.10 = (bf16[48,128]{1,0:T(8,128)(2,1)S(1)}, bf16[48,128]{1,0:T(8,128)(2,1)S(1)}, u32[]{:S(2)}, u32[]{:S(2)}) collective-permute-start(bf16[48,128]{1,0:T(8,128)(2,1)S(1)} %get-tuple-element.45), channel_id=1, source_target_pairs={{0,1},{1,0},{2,3},{3,2},{4,5},{5,4},{6,7},{7,6},{8,9},{9,8},{10,11... | collective-permute-start | bytes 36872 | tf_op jit(solution)/shard_map/ppermute | solution.py:675

commit v10 on v9

--- a/solution.py
+++ b/solution.py
@@ -142,6 +142,20 @@
         target[0:share, :] = rows.astype(target.dtype)
 
 
+def send_tiles(groups, source, share, targets):
+    me = lax.axis_index("hap")
+    for step, target in enumerate(targets):
+        owner = partner(me, step, groups)
+        counts = source[pl.ds(pl.multiple_of(owner * share, 8), share), :]
+        for k in range(source.shape[1] // LANES):
+            target[k * share : (k + 1) * share, :] = counts[:, k * LANES : (k + 1) * LANES]
+
+
+def from_tiles(counts, share):
+    tiles = counts.shape[0] // share
+    return jnp.concatenate([counts[k * share : (k + 1) * share, :] for k in range(tiles)], axis=1)
+
+
 def own_kernel(groups, share, alleles_ref, label_ref, *refs):
     weighted_ref, totals_ref, *targets = refs[: 2 + groups]
     tile, folded = refs[2 + groups :]
@@ -162,7 +176,16 @@
     folded[0:half, :] = to_fields(jnp.where(moved, turned, tile[half:snps, :]))
     if folded.shape[0] > half:
         folded[half:, :] = jnp.zeros((folded.shape[0] - half, snps), jnp.int32)
-    send_shares(groups, folded, share, targets)
+    if groups != len(LEFT_BLOCKS):
+        send_shares(groups, folded, share, targets)
+        return
+    tiles = snps // LANES
+    shared = [totals_ref[0:1, k * LANES : (k + 1) * LANES] for k in range(tiles)]
+    shared += [totals_ref[1:2, 0:LANES], jnp.zeros((7 - tiles, LANES))]
+    extras = to_fields(jnp.concatenate(shared, axis=0))
+    send_tiles(groups, folded, share, targets)
+    for target in targets:
+        target[tiles * share :, :] = extras
 
 
 LEFT_BLOCKS = ((0, 1, 2, 3), (2, 3, 6, 7), (4, 0, 1, 2), (6, 0, 4, 5))
@@ -269,23 +292,16 @@
         jnp.where(iota(square, 0) == iota(square, 1), tile[0:snps, :], 0.0), axis=0, keepdims=True
     )
     tiles = snps // LANES
-    shared = [totals_ref[0:1, k * LANES : (k + 1) * LANES] for k in range(tiles)]
-    shared.append(totals_ref[1:2, 0:LANES])
-    by_column = jnp.concatenate([tile[snps : snps + 1, :], apart, jnp.zeros((6, snps))], axis=0)
+    sizes = totals_ref[1:2, :]
+    by_column = jnp.concatenate([sizes, tile[snps : snps + 1, :], apart, jnp.zeros((5, snps))], axis=0)
     for owner in range(groups):
         start = owner * (snps // groups)
         columns = pltpu.roll(by_column, snps - start, 1) if owner else by_column
-        extras[8 * owner : 8 * (owner + 1), :] = to_fields(
-            jnp.concatenate(
-                [*shared, columns[0:2, 0:LANES], jnp.zeros((6 - tiles - 1, LANES))], axis=0
-            )
-        )
+        extras[8 * owner : 8 * (owner + 1), :] = to_fields(columns[:, 0:LANES])
     me = lax.axis_index("hap")
+    send_tiles(groups, folded, share, targets)
     for step, target in enumerate(targets):
         owner = partner(me, step, groups)
-        counts = folded[pl.ds(pl.multiple_of(owner * share, 8), share), :]
-        for k in range(tiles):
-            target[k * share : (k + 1) * share, :] = counts[:, k * LANES : (k + 1) * LANES]
         target[tiles * share :, :] = extras[pl.ds(pl.multiple_of(owner * 8, 8), 8), :]
 
 
@@ -500,48 +516,23 @@
     )
 
 
-def column_score_kernel(groups, share, reach_ref, *refs):
-    own_sum_ref, near_parts = refs[0], refs[1 : groups + 1]
-    annot_ref, near_annot_ref = refs[groups + 1 : groups + 3]
-    out_ref, *targets = refs[groups + 3 : 2 * groups + 3]
-    near_out_ref, table, flipped, scores = refs[2 * groups + 3 :]
+def own_score_kernel(groups, share, reach_ref, own_sum_ref, annot_ref, scores, table):
     snps = annot_ref.shape[0]
     half = snps // 2
     wide = snps // groups
-    size = wide // 2
+    tiles = snps // LANES
     me = lax.axis_index("hap")
-    block = lax.axis_index("snp")
-    last = reach_ref.shape[0] - 1
-    upper = me < groups // 2
-    reach_here = reach_ref[block]
-    reach_there = jnp.where(
-        upper, reach_ref[jnp.minimum(block + 1, last)], reach_ref[jnp.maximum(block - 1, 0)]
-    )
-
-    def mine(choices):
-        value = choices[0]
-        for group in range(1, groups):
-            value = jnp.where(me == group, choices[group], value)
-        return value
-
-    own_counts = own_sum_ref[...]
-    near_sums = sum((part[...] for part in near_parts[1:]), near_parts[0][...])
-    tiles = snps // LANES
-    near_counts = jnp.concatenate(
-        [near_sums[k * share : (k + 1) * share, :] for k in range(tiles)], axis=1
-    )
-    extras = from_fields(near_sums[tiles * share :, :])
-
-    own_stats, near_stats, lines, near_lines = [], [], [], []
+    reach_here = reach_ref[lax.axis_index("snp")]
+    own_counts = from_tiles(own_sum_ref[0 : tiles * share, :], share)
+    extras = from_fields(own_sum_ref[tiles * share :, :])
+
+    own_stats, lines = [], []
     for pop in range(2):
-        count = extras[pop][tiles : tiles + 1, :]
+        count = jnp.concatenate([extras[pop][tiles : tiles + 1, :]] * tiles, axis=1)
         totals = jnp.concatenate([extras[pop][k : k + 1, :] for k in range(tiles)], axis=1)
-        own_stats.append(column_stats(totals, jnp.concatenate([count] * tiles, axis=1)))
-        near_stats.append(column_stats(extras[pop][tiles + 1 : tiles + 2, :], count))
+        own_stats.append(column_stats(totals, count))
         lines += [*own_stats[pop], totals]
-        near_lines += [*near_stats[pop], extras[pop][tiles + 2 : tiles + 3, :]]
     table[:, 0:8] = jnp.concatenate(lines, axis=0).T
-    near_table = jnp.concatenate(near_lines, axis=0).T[0:wide, :]
 
     low_rows = pl.multiple_of(me * share, 8)
     high_rows = pl.multiple_of(half + me * share, 8)
@@ -568,6 +559,47 @@
     direct = dot_rounded(own_kept, annot_ref[...].astype(jnp.bfloat16), 1)
     scores[pl.ds(low_rows, share), :] += direct[0:share, :]
     scores[pl.ds(high_rows, share), :] += direct[share:, :]
+
+    slice_rows = pl.ds(pl.multiple_of(me * wide, 8), wide)
+    mine = table[slice_rows, :]
+    product = 1.0
+    for pop in range(2):
+        own_row = [mine[:, 4 * pop + k : 4 * pop + k + 1] for k in range(4)]
+        product *= correlation(own_row, own_row, own_row[3])
+    scores[slice_rows, :] += annot_ref[slice_rows, :] * product
+
+
+def near_score_kernel(groups, share, reach_ref, *refs):
+    near_parts, (own_ref, table, annot_ref, near_annot_ref) = refs[:groups], refs[groups : groups + 4]
+    keep_ref, send_ref, near_out_ref, flipped, scores = refs[groups + 4 :]
+    snps = annot_ref.shape[0]
+    wide = snps // groups
+    size = wide // 2
+    tiles = snps // LANES
+    me = lax.axis_index("hap")
+    block = lax.axis_index("snp")
+    last = reach_ref.shape[0] - 1
+    upper = me < groups // 2
+    reach_here = reach_ref[block]
+    reach_there = jnp.where(
+        upper, reach_ref[jnp.minimum(block + 1, last)], reach_ref[jnp.maximum(block - 1, 0)]
+    )
+
+    def mine(choices):
+        value = choices[0]
+        for group in range(1, groups):
+            value = jnp.where(me == group, choices[group], value)
+        return value
+
+    scores[...] = own_ref[...]
+    near_sums = sum((part[...] for part in near_parts[1:]), near_parts[0][...])
+    near_counts = from_tiles(near_sums[0 : tiles * share, :], share)
+    extras = from_fields(near_sums[tiles * share :, :])
+    near_stats, near_lines = [], []
+    for pop in range(2):
+        near_stats.append(column_stats(extras[pop][1:2, :], extras[pop][0:1, :]))
+        near_lines += [*near_stats[pop], extras[pop][2:3, :]]
+    near_table = jnp.concatenate(near_lines, axis=0).T[0:wide, :]
 
     slots = [near_counts[:, 0:LANES]]
     for slot in range(1, groups):
@@ -626,30 +658,34 @@
     near_scores = dot_rounded(sides(near_there), own_rows, 0)[0:wide, :]
 
     mine_table = table[slice_rows, :]
-    self_product, far_product = 1.0, 1.0
+    far_product = 1.0
     for pop in range(2):
-        own_row = [mine_table[:, 4 * pop + k : 4 * pop + k + 1] for k in range(4)]
+        own_row = [mine_table[:, 4 * pop + k : 4 * pop + k + 1] for k in range(3)]
         near_row = [near_table[:, 4 * pop + k : 4 * pop + k + 1] for k in range(4)]
-        self_product *= correlation(own_row, own_row, own_row[3])
         far_product *= correlation(own_row, near_row, near_row[3])
-    my_annots = annot_ref[slice_rows, :]
-    out_ref[...] = (
-        scores[slice_rows, :]
-        + my_annots * self_product
-        + their_annots * jnp.where(reach_here >= snps, far_product, 0.0)
-    )
-    near_scores += my_annots * jnp.where(reach_there >= snps, far_product, 0.0)
+    scores[slice_rows, :] += their_annots * jnp.where(reach_here >= snps, far_product, 0.0)
+    near_scores += annot_ref[slice_rows, :] * jnp.where(reach_there >= snps, far_product, 0.0)
     near_out_ref[...] = pack_halves(near_scores)
-    for step, target in enumerate(targets, 1):
+
+    def packed(step):
         group = partner(me, step, groups)
-        rows = scores[pl.ds(pl.multiple_of(group * wide, 8), wide), :]
-        target[...] = pack_halves(rows).astype(target.dtype)
-
-
-def column_finish_kernel(own_ref, *refs):
-    *parts, there_ref, out_ref = refs
-    packed = sum((part[...].astype(jnp.float32) for part in parts), there_ref[...])
-    out_ref[...] = (own_ref[...] + unpack_halves(packed)).T[0 : out_ref.shape[0], :]
+        return pack_halves(scores[pl.ds(pl.multiple_of(group * wide, 8), wide), :])
+
+    for ref, steps in ((keep_ref, (0, 2)), (send_ref, (1, 3))):
+        for number, step in enumerate(steps):
+            ref[number * size : (number + 1) * size, :] = packed(step).astype(ref.dtype)
+
+
+def middle_kernel(keep_ref, part_ref, mine_ref, send_ref):
+    total = keep_ref[...] + part_ref[...].astype(jnp.float32)
+    half = mine_ref.shape[0]
+    mine_ref[...] = total[0:half]
+    send_ref[...] = total[half:].astype(send_ref.dtype)
+
+
+def column_finish_kernel(mine_ref, part_ref, there_ref, out_ref):
+    packed = mine_ref[...] + part_ref[...].astype(jnp.float32) + there_ref[...]
+    out_ref[...] = unpack_halves(packed).T[0 : out_ref.shape[0], :]
 
 
 def sum_kernel(*refs):
@@ -714,11 +750,14 @@
     from_far = swapped(far, 1)
     from_close = swapped(close, 0)
 
+    by_column = groups == len(LEFT_BLOCKS)
+    compact = shape((share * (snps // LANES) + 8, LANES), i32)
+    own_share_counts = compact if by_column else shape((share, snps), i32)
     tile = pltpu.VMEM((snps + 16, snps), f32)
     folded = pltpu.VMEM((folded_rows, snps), i32)
     weighted, totals, *own_parts = call(
         functools.partial(own_kernel, groups, share),
-        [shape((snps + 16, rows), bf16), shape((8, snps), f32)] + [shape((share, snps), i32)] * groups,
+        [shape((snps + 16, rows), bf16), shape((8, snps), f32)] + [own_share_counts] * groups,
         [VMEM, VMEM],
         [tile, folded],
         flops=2 * rows * snps * snps,
@@ -726,8 +765,7 @@
     )(alleles, labels.reshape(1, rows))
     own_parts = [own_parts[0]] + [around(own_parts[k], groups, k) for k in range(groups - 1, 0, -1)]
 
-    by_column = groups == len(LEFT_BLOCKS)
-    near_shapes = [shape((share, snps), i32)] + [shape((share + 8, snps), i32)] * groups
+    near_shapes = [own_share_counts] + [compact if by_column else shape((share + 8, snps), i32)] * groups
     if by_column:
         near = pltpu.VMEM((rows, 2 * LANES), bf16)
         window = (snps + 16, 2 * LANES)
@@ -737,7 +775,7 @@
         )
         own_sum, *near_parts = call(
             functools.partial(far_kernel, groups, share),
-            [near_shapes[0]] + [shape((share * (snps // LANES) + 8, LANES), i32)] * groups,
+            near_shapes,
             [VMEM] * (4 + groups),
             [
                 near,
@@ -779,17 +817,29 @@
     own_share = shape((out_share, LANES), f32)
     packed_share = shape((half_share, LANES), f32)
     if by_column:
-        own_scores, *scores, near_scores = call(
-            functools.partial(column_score_kernel, groups, share),
-            [own_share] + [shape((half_share, LANES), bf16)] * (groups - 1) + [packed_share],
-            [SMEM] + [VMEM] * (groups + 3),
-            [pltpu.VMEM((snps, LANES), f32), pltpu.VMEM((LANES, LANES), i32), pltpu.VMEM((snps, LANES), f32)],
+        own_scores, table = call(
+            functools.partial(own_score_kernel, groups, share),
+            [by_snp, by_snp],
+            [SMEM, VMEM, VMEM],
+            flops=1 << 25,
+            moved=1 << 20,
+        )(reach, own_sum, own_annots)
+        both = (2 * half_share, LANES)
+        keep, send, near_scores = call(
+            functools.partial(near_score_kernel, groups, share),
+            [shape(both, f32), shape(both, bf16), packed_share],
+            [SMEM] + [VMEM] * (groups + 4),
+            [pltpu.VMEM((LANES, LANES), i32), pltpu.VMEM((snps, LANES), f32)],
             flops=1 << 26,
             moved=1 << 21,
-        )(reach, own_sum, *near_parts, own_annots, near_annots)
-        scores = [around(scores[k - 1], groups, k) for k in range(groups - 1, 0, -1)]
+        )(reach, *near_parts, own_scores, table, own_annots, near_annots)
+        part = around(send, groups, 1)
         there = to_neighbour(near_scores)
-        return call(column_finish_kernel, result, [VMEM] * (groups + 1))(own_scores, *scores, there)
+        mine, send = call(
+            middle_kernel, [packed_share, shape((half_share, LANES), bf16)], [VMEM] * 2
+        )(keep, part)
+        part = around(send, groups, 2)
+        return call(column_finish_kernel, result, [VMEM] * 3)(mine, part, there)
 
     tall = pltpu.VMEM((padded, LANES), f32)
     scores = call(

time: 39.2 us -> 39 us (level)
  starting transfers between devices: 18.1 us -> 14.4 us
  waiting for transfers between devices: 12.5 us -> 15.1 us
  Pallas kernels: 8.46 us -> 9.18 us
    ppermute x9 -> x8, starting transfers between devices: 14.2 us -> 11 us  [around(): lax.ppermute(value, 'hap', [(source, partner(source, step, groups)) for s...]
    ppermute x9 -> x8, waiting for transfers between devices: 12.4 us -> 15.1 us  [around(): lax.ppermute(value, 'hap', [(source, partner(source, step, groups)) for s...]
    pallas_call x3 -> x5, Pallas kernels: 4.06 us -> 4.79 us  [the longest x1 1.52 us: per_device(): call(functools.partial(near_score_kernel, groups, share), [shape(both, f3...]
    ppermute x1, starting transfers between devices: 2.6 us -> 2.2 us  [to_neighbour(): return lax.ppermute(value, ('snp', 'hap'), pairs)]
  transfers between devices with their start and end apart: 12 -> 11, of which waited for: 6 -> 6; matrix products, arithmetic and copies ran while one was open for 0% -> 0% of each run, Pallas kernels for 6% -> 9%
where the time goes in v10:
time: 39 us; the launch traced here: 38.8 us
  waiting for transfers between devices  15.1 us (39%)
  starting transfers between devices  14.4 us (37%)
  Pallas kernels  9.18 us (24%)
    ppermute x8, waiting for transfers between devices, around(): lax.ppermute(value, 'hap', [(source, partner(source, step, groups)) for s...  15.1 us
    ppermute x8, starting transfers between devices, around(): lax.ppermute(value, 'hap', [(source, partner(source, step, groups)) for s...  11 us
    ppermute x1, starting transfers between devices, to_neighbour(): return lax.ppermute(value, ('snp', 'hap'), pairs)  2.2 us
    pallas_call x1, Pallas kernels, per_device(): call(prepare_kernel, [shape((rows, snps), bf16), packed, packed], [HBM, H...  2.14 us
    pallas_call x1, Pallas kernels, per_device(): call(functools.partial(near_score_kernel, groups, share), [shape(both, f3...  1.52 us
    pallas_call x1, Pallas kernels, per_device(): call(functools.partial(far_kernel, groups, share), near_shapes, [VMEM] *...  1.3 us
    pallas_call x1, Pallas kernels, per_device(): call(functools.partial(own_score_kernel, groups, share), [by_snp, by_snp]...  1.23 us
    ppermute x2, starting transfers between devices, swapped(): return lax.ppermute(value, 'snp', pairs)  1.22 us
  transfers between devices with their start and end apart: 11, of which 6 were waited for; matrix products, arithmetic and copies ran while one was open for 0% of the time, Pallas kernels for 9%

profile of v10, /device:TPU:0, one launch (start us, length us, event | category | flops | bytes accessed | tf_op | source)
XLA Modules:
  0.0 38.8 jit_solution(10946733017004653124)
XLA Ops:
  0.0 0.0 copy-start.2
  0.0 2.1 %shard_map.46 = (bf16[2048,384]{1,0:T(8,128)(2,1)S(1)}, bf16[1056,384]{1,0:T(8,128)(2,1)S(1)}, bf16[1056,384]{1,0:T(8,128)(2,1)S(1)}) custom-call(s32[2048,384]{1,0:T(8,128)} %hap_ref.1, s32[50,384]{1,0:T(8,128)} %annot_ref.3), custom_call_target="tpu_custom_call" | custom-call | bytes 6291456 | tf_op jit(solution)/shard_map/pallas_call | solution.py:739
  2.1 0.5 %collective-permute-start.1 = (bf16[1056,384]{1,0:T(8,128)(2,1)S(1)}, bf16[1056,384]{1,0:T(8,128)(2,1)S(1)}, u32[]{:S(2)}, u32[]{:S(2)}) collective-permute-start(bf16[1056,384]{1,0:T(8,128)(2,1)S(1)} %get-tuple-element.31), channel_id=1, source_target_pairs={{0,4},{4,0},{8,12},{12,8},{1,5},{5,1},{9,13},{13,9},{2,6},{6,2},{1... | collective-permute-start | bytes 2433032 | tf_op jit(solution)/shard_map/ppermute | solution.py:720
  2.7 0.7 %collective-permute-start = (bf16[1056,384]{1,0:T(8,128)(2,1)S(1)}, bf16[1056,384]{1,0:T(8,128)(2,1)S(1)}, u32[]{:S(2)}, u32[]{:S(2)}) collective-permute-start(bf16[1056,384]{1,0:T(8,128)(2,1)S(1)} %get-tuple-element.30), channel_id=1, source_target_pairs={{4,8},{8,4},{5,9},{9,5},{6,10},{10,6},{7,11},{11,7},{20,24},{24,20... | collective-permute-start | bytes 2433032 | tf_op jit(solution)/shard_map/ppermute | solution.py:720
  3.4 0.0 copy-done.2
  3.4 1.1 %shard_map.47 = (bf16[400,2048]{1,0:T(8,128)(2,1)S(1)}, f32[8,384]{1,0:T(8,128)S(1)}, s32[152,128]{1,0:T(8,128)S(1)}, s32[152,128]{1,0:T(8,128)S(1)}, s32[152,128]{1,0:T(8,128)S(1)}, /*index=5*/s32[152,128]{1,0:T(8,128)S(1)}) custom-call(bf16[2048,384]{1,0:T(8,128)(2,1)S(1)} %get-tuple-element.28.alleles_ref, s32[1,2048]{1,0:T(1,128)S(1)} %bitcast.1), custom_call_target="tpu_custom_call" | custom-call | flops 603979776 | bytes 3145728 | tf_op jit(solution)/shard_map/pallas_call | solution.py:758
  4.5 4.7 %collective-permute-start.2 = (s32[152,128]{1,0:T(8,128)S(1)}, s32[152,128]{1,0:T(8,128)S(1)}, u32[]{:S(2)}, u32[]{:S(2)}) collective-permute-start(s32[152,128]{1,0:T(8,128)S(1)} %get-tuple-element.34), channel_id=1, source_target_pairs={{0,3},{1,2},{2,1},{3,0},{4,7},{5,6},{6,5},{7,4},{8,11},{9,10},{10,... | collective-permute-start | bytes 233480 | tf_op jit(solution)/shard_map/ppermute | solution.py:711
  9.2 0.0 collective-permute-start.3
  9.2 0.6 %collective-permute-start.4 = (s32[152,128]{1,0:T(8,128)S(1)}, s32[152,128]{1,0:T(8,128)S(1)}, u32[]{:S(2)}, u32[]{:S(2)}) collective-permute-start(s32[152,128]{1,0:T(8,128)S(1)} %get-tuple-element.36), channel_id=1, source_target_pairs={{0,1},{1,0},{2,3},{3,2},{4,5},{5,4},{6,7},{7,6},{8,9},{9,8},{10,11... | collective-permute-start | bytes 233480 | tf_op jit(solution)/shard_map/ppermute | solution.py:711
  9.9 0.0 collective-permute-done.1.side_ref
  9.9 0.8 %shard_map.48.close_ref = f32[400,256]{1,0:T(8,128)S(1)} custom-call(bf16[400,2048]{1,0:T(8,128)(2,1)S(1)} %get-tuple-element.29.weighted_ref, bf16[1056,384]{1,0:T(8,128)(2,1)S(1)} %collective-permute-done.1.side_ref), custom_call_target="tpu_custom_call" | custom-call | flops 402653184 | bytes 3145728 | tf_op jit(solution)/shard_map/pallas_call | solution.py:773
  10.7 1.0 %collective-permute-done.2.refs_1_ = s32[152,128]{1,0:T(8,128)S(1)} collective-permute-done((s32[152,128]{1,0:T(8,128)S(1)}, s32[152,128]{1,0:T(8,128)S(1)}, u32[]{:S(2)}, u32[]{:S(2)}) %collective-permute-start.2) | collective-permute-done | bytes 77856 | tf_op jit(solution)/shard_map/ppermute | solution.py:711
  11.7 5.3 %collective-permute-done.3.refs_2_ = s32[152,128]{1,0:T(8,128)S(1)} collective-permute-done((s32[152,128]{1,0:T(8,128)S(1)}, s32[152,128]{1,0:T(8,128)S(1)}, u32[]{:S(2)}, u32[]{:S(2)}) %collective-permute-start.3) | collective-permute-done | bytes 77856 | tf_op jit(solution)/shard_map/ppermute | solution.py:711
  17.0 0.0 collective-permute-done.4.refs_3_
  17.0 0.0 collective-permute-done.side_ref
  17.0 0.0 copy-start
  17.0 0.0 copy-start.1
  17.0 1.3 %shard_map.49 = (s32[152,128]{1,0:T(8,128)S(1)}, s32[152,128]{1,0:T(8,128)S(1)}, s32[152,128]{1,0:T(8,128)S(1)}, s32[152,128]{1,0:T(8,128)S(1)}, s32[152,128]{1,0:T(8,128)S(1)}) custom-call(bf16[400,2048]{1,0:T(8,128)(2,1)S(1)} %get-tuple-element.29.weighted_ref, bf16[1056,384]{1,0:T(8,128)(2,1)S(1)} %collective-permute-done.side_ref, ...), custom_call_target="tpu_custom_call" | custom-call | flops 402653184 | bytes 3145728 | tf_op jit(solution)/shard_map/pallas_call | solution.py:776
  18.3 0.1 collective-permute-start.5
  18.4 0.4 %collective-permute-start.6 = (s32[152,128]{1,0:T(8,128)S(1)}, s32[152,128]{1,0:T(8,128)S(1)}, u32[]{:S(2)}, u32[]{:S(2)}) collective-permute-start(s32[152,128]{1,0:T(8,128)S(1)} %get-tuple-element.39), channel_id=1, source_target_pairs={{0,2},{1,3},{2,0},{3,1},{4,6},{5,7},{6,4},{7,5},{8,10},{9,11},{10,... | collective-permute-start | bytes 233480 | tf_op jit(solution)/shard_map/ppermute | solution.py:711
  18.8 4.0 %collective-permute-start.7 = (s32[152,128]{1,0:T(8,128)S(1)}, s32[152,128]{1,0:T(8,128)S(1)}, u32[]{:S(2)}, u32[]{:S(2)}) collective-permute-start(s32[152,128]{1,0:T(8,128)S(1)} %get-tuple-element.40), channel_id=1, source_target_pairs={{0,1},{1,0},{2,3},{3,2},{4,5},{5,4},{6,7},{7,6},{8,9},{9,8},{10,11... | collective-permute-start | bytes 233480 | tf_op jit(solution)/shard_map/ppermute | solution.py:711
  22.8 0.0 copy-done
  22.8 0.3 shard_map.50
  23.1 0.0 copy-done.1
  23.1 1.2 %shard_map.51 = (f32[384,128]{1,0:T(8,128)S(1)}, f32[384,128]{1,0:T(8,128)S(1)}) custom-call(s32[4]{0:T(128)S(1)} %copy-done.1, s32[152,128]{1,0:T(8,128)S(1)} %get-tuple-element.41.own_sum_ref, f32[384,128]{1,0:T(8,128)S(1)} %get-tuple-element.42.annot_ref.refs_6_), custom_call_target="tpu_custom_call" | custom-call | flops 33554432 | bytes 1048576 | tf_op jit(solution)/shard_map/pallas_call | solution.py:820
  24.3 1.2 %collective-permute-done.5.refs_1_ = s32[152,128]{1,0:T(8,128)S(1)} collective-permute-done((s32[152,128]{1,0:T(8,128)S(1)}, s32[152,128]{1,0:T(8,128)S(1)}, u32[]{:S(2)}, u32[]{:S(2)}) %collective-permute-start.5) | collective-permute-done | bytes 77856 | tf_op jit(solution)/shard_map/ppermute | solution.py:711
  25.5 2.4 %collective-permute-done.6.refs_2_ = s32[152,128]{1,0:T(8,128)S(1)} collective-permute-done((s32[152,128]{1,0:T(8,128)S(1)}, s32[152,128]{1,0:T(8,128)S(1)}, u32[]{:S(2)}, u32[]{:S(2)}) %collective-permute-start.6) | collective-permute-done | bytes 77856 | tf_op jit(solution)/shard_map/ppermute | solution.py:711
  27.9 0.0 collective-permute-done.7.refs_3_
  27.9 1.5 %shard_map.52 = (f32[96,128]{1,0:T(8,128)S(1)}, bf16[96,128]{1,0:T(8,128)(2,1)S(1)}, f32[48,128]{1,0:T(8,128)S(1)}) custom-call(s32[4]{0:T(128)S(1)} %copy-done.1, s32[152,128]{1,0:T(8,128)S(1)} %get-tuple-element.37.refs_0_, s32[152,128]{1,0:T(8,128)S(1)} %collective-permute-done.5.refs_1_, s32[152,128]{1,0:T(8,128)S(1)} %collective-permute-done.6.refs_2_, ...), custom_call_target="tpu_custom_call" | custom-call | flops 67108864 | bytes 2097152 | tf_op jit(solution)/shard_map/pallas_call | solution.py:828
  29.4 0.2 collective-permute-start.8
  29.6 2.2 %collective-permute-start.10 = (f32[48,128]{1,0:T(8,128)S(1)}, f32[48,128]{1,0:T(8,128)S(1)}, u32[]{:S(2)}, u32[]{:S(2)}) collective-permute-start(f32[48,128]{1,0:T(8,128)S(1)} %get-tuple-element.50), channel_id=1, source_target_pairs={{0,4},{1,5},{4,8},{5,9},{6,2},{7,3},{8,12},{9,13},{10,6},{11,7},{1... | collective-permute-start | bytes 73736 | tf_op jit(solution)/shard_map/ppermute | solution.py:813
  31.8 1.5 %collective-permute-done.8.part_ref = bf16[96,128]{1,0:T(8,128)(2,1)S(1)} collective-permute-done((bf16[96,128]{1,0:T(8,128)(2,1)S(1)}, bf16[96,128]{1,0:T(8,128)(2,1)S(1)}, u32[]{:S(2)}, u32[]{:S(2)}) %collective-permute-start.8) | collective-permute-done | bytes 24608 | tf_op jit(solution)/shard_map/ppermute | solution.py:711
  33.4 1.0 %collective-permute-start.9 = (bf16[48,128]{1,0:T(8,128)(2,1)S(1)}, bf16[48,128]{1,0:T(8,128)(2,1)S(1)}, u32[]{:S(2)}, u32[]{:S(2)}) collective-permute-start(bf16[48,128]{1,0:T(8,128)(2,1)S(1)} %get-tuple-element.49), channel_id=1, source_target_pairs={{0,2},{1,3},{2,0},{3,1},{4,6},{5,7},{6,4},{7,5},{8,10},{9,11},{10,... | collective-permute-start | bytes 36872 | tf_op jit(solution)/shard_map/ppermute | solution.py:711
  34.4 0.0 collective-permute-done.10.there_ref
  34.4 3.7 %collective-permute-done.9.part_ref = bf16[48,128]{1,0:T(8,128)(2,1)S(1)} collective-permute-done((bf16[48,128]{1,0:T(8,128)(2,1)S(1)}, bf16[48,128]{1,0:T(8,128)(2,1)S(1)}, u32[]{:S(2)}, u32[]{:S(2)}) %collective-permute-start.9) | collective-permute-done | bytes 12320 | tf_op jit(solution)/shard_map/ppermute | solution.py:711
  38.0 0.7 %shard_map.54 = f32[50,96]{1,0:T(8,128)} custom-call(f32[48,128]{1,0:T(8,128)S(1)} %get-tuple-element.48.mine_ref, bf16[48,128]{1,0:T(8,128)(2,1)S(1)} %collective-permute-done.9.part_ref, f32[48,128]{1,0:T(8,128)S(1)} %collective-permute-done.10.there_ref), custom_call_target="tpu_custom_call" | custom-call | tf_op jit(solution)/shard_map/pallas_call | solution.py:842
  (3 shorter events, 0.0 us)
Async XLA Ops:
  0.0 3.4 %copy-start.2 = (s32[2048]{0:T(1024)S(1)}, s32[2048]{0:T(1024)}, u32[]{:S(2)}) copy-start(s32[2048]{0:T(1024)} %param.5) | copy-start | bytes 24580
  2.1 7.7 %collective-permute-start.1 = (bf16[1056,384]{1,0:T(8,128)(2,1)S(1)}, bf16[1056,384]{1,0:T(8,128)(2,1)S(1)}, u32[]{:S(2)}, u32[]{:S(2)}) collective-permute-start(bf16[1056,384]{1,0:T(8,128)(2,1)S(1)} %get-tuple-element.31), channel_id=1, source_target_pairs={{0,4},{4,0},{8,12},{12,8},{1,5},{5,1},{9,13},{13,9},{2,6},{6,2},{1... | collective-permute-start | bytes 2433032 | tf_op jit(solution)/shard_map/ppermute | solution.py:720
  2.7 14.3 %collective-permute-start = (bf16[1056,384]{1,0:T(8,128)(2,1)S(1)}, bf16[1056,384]{1,0:T(8,128)(2,1)S(1)}, u32[]{:S(2)}, u32[]{:S(2)}) collective-permute-start(bf16[1056,384]{1,0:T(8,128)(2,1)S(1)} %get-tuple-element.30), channel_id=1, source_target_pairs={{4,8},{8,4},{5,9},{9,5},{6,10},{10,6},{7,11},{11,7},{20,24},{24,20... | collective-permute-start | bytes 2433032 | tf_op jit(solution)/shard_map/ppermute | solution.py:720
  4.5 7.2 %collective-permute-start.2 = (s32[152,128]{1,0:T(8,128)S(1)}, s32[152,128]{1,0:T(8,128)S(1)}, u32[]{:S(2)}, u32[]{:S(2)}) collective-permute-start(s32[152,128]{1,0:T(8,128)S(1)} %get-tuple-element.34), channel_id=1, source_target_pairs={{0,3},{1,2},{2,1},{3,0},{4,7},{5,6},{6,5},{7,4},{8,11},{9,10},{10,... | collective-permute-start | bytes 233480 | tf_op jit(solution)/shard_map/ppermute | solution.py:711
  9.2 7.8 %collective-permute-start.3 = (s32[152,128]{1,0:T(8,128)S(1)}, s32[152,128]{1,0:T(8,128)S(1)}, u32[]{:S(2)}, u32[]{:S(2)}) collective-permute-start(s32[152,128]{1,0:T(8,128)S(1)} %get-tuple-element.35), channel_id=1, source_target_pairs={{0,2},{1,3},{2,0},{3,1},{4,6},{5,7},{6,4},{7,5},{8,10},{9,11},{10,... | collective-permute-start | bytes 233480 | tf_op jit(solution)/shard_map/ppermute | solution.py:711
  9.2 7.8 %collective-permute-start.4 = (s32[152,128]{1,0:T(8,128)S(1)}, s32[152,128]{1,0:T(8,128)S(1)}, u32[]{:S(2)}, u32[]{:S(2)}) collective-permute-start(s32[152,128]{1,0:T(8,128)S(1)} %get-tuple-element.36), channel_id=1, source_target_pairs={{0,1},{1,0},{2,3},{3,2},{4,5},{5,4},{6,7},{7,6},{8,9},{9,8},{10,11... | collective-permute-start | bytes 233480 | tf_op jit(solution)/shard_map/ppermute | solution.py:711
  17.0 5.8 %copy-start = (s32[50,384]{1,0:T(8,128)S(1)}, s32[50,384]{1,0:T(8,128)}, u32[]{:S(2)}) copy-start(s32[50,384]{1,0:T(8,128)} %annot_ref.3) | copy-start | bytes 230404
  17.0 6.1 %copy-start.1 = (s32[4]{0:T(128)S(1)}, s32[4]{0:T(128)}, u32[]{:S(2)}) copy-start(s32[4]{0:T(128)} %reach_ref.3) | copy-start | bytes 52
  18.3 7.2 %collective-permute-start.5 = (s32[152,128]{1,0:T(8,128)S(1)}, s32[152,128]{1,0:T(8,128)S(1)}, u32[]{:S(2)}, u32[]{:S(2)}) collective-permute-start(s32[152,128]{1,0:T(8,128)S(1)} %get-tuple-element.38), channel_id=1, source_target_pairs={{0,3},{1,2},{2,1},{3,0},{4,7},{5,6},{6,5},{7,4},{8,11},{9,10},{10,... | collective-permute-start | bytes 233480 | tf_op jit(solution)/shard_map/ppermute | solution.py:711
  18.4 9.5 %collective-permute-start.6 = (s32[152,128]{1,0:T(8,128)S(1)}, s32[152,128]{1,0:T(8,128)S(1)}, u32[]{:S(2)}, u32[]{:S(2)}) collective-permute-start(s32[152,128]{1,0:T(8,128)S(1)} %get-tuple-element.39), channel_id=1, source_target_pairs={{0,2},{1,3},{2,0},{3,1},{4,6},{5,7},{6,4},{7,5},{8,10},{9,11},{10,... | collective-permute-start | bytes 233480 | tf_op jit(solution)/shard_map/ppermute | solution.py:711
  18.8 9.1 %collective-permute-start.7 = (s32[152,128]{1,0:T(8,128)S(1)}, s32[152,128]{1,0:T(8,128)S(1)}, u32[]{:S(2)}, u32[]{:S(2)}) collective-permute-start(s32[152,128]{1,0:T(8,128)S(1)} %get-tuple-element.40), channel_id=1, source_target_pairs={{0,1},{1,0},{2,3},{3,2},{4,5},{5,4},{6,7},{7,6},{8,9},{9,8},{10,11... | collective-permute-start | bytes 233480 | tf_op jit(solution)/shard_map/ppermute | solution.py:711
  29.4 3.9 %collective-permute-start.8 = (bf16[96,128]{1,0:T(8,128)(2,1)S(1)}, bf16[96,128]{1,0:T(8,128)(2,1)S(1)}, u32[]{:S(2)}, u32[]{:S(2)}) collective-permute-start(bf16[96,128]{1,0:T(8,128)(2,1)S(1)} %get-tuple-element.47), channel_id=1, source_target_pairs={{0,1},{1,0},{2,3},{3,2},{4,5},{5,4},{6,7},{7,6},{8,9},{9,8},{10,11... | collective-permute-start | bytes 73736 | tf_op jit(solution)/shard_map/ppermute | solution.py:711
  29.6 4.8 %collective-permute-start.10 = (f32[48,128]{1,0:T(8,128)S(1)}, f32[48,128]{1,0:T(8,128)S(1)}, u32[]{:S(2)}, u32[]{:S(2)}) collective-permute-start(f32[48,128]{1,0:T(8,128)S(1)} %get-tuple-element.50), channel_id=1, source_target_pairs={{0,4},{1,5},{4,8},{5,9},{6,2},{7,3},{8,12},{9,13},{10,6},{11,7},{1... | collective-permute-start | bytes 73736 | tf_op jit(solution)/shard_map/ppermute | solution.py:813
  33.4 4.7 %collective-permute-start.9 = (bf16[48,128]{1,0:T(8,128)(2,1)S(1)}, bf16[48,128]{1,0:T(8,128)(2,1)S(1)}, u32[]{:S(2)}, u32[]{:S(2)}) collective-permute-start(bf16[48,128]{1,0:T(8,128)(2,1)S(1)} %get-tuple-element.49), channel_id=1, source_target_pairs={{0,2},{1,3},{2,0},{3,1},{4,6},{5,7},{6,4},{7,5},{8,10},{9,11},{10,... | collective-permute-start | bytes 36872 | tf_op jit(solution)/shard_map/ppermute | solution.py:711

commit v11 on v10

--- a/solution.py
+++ b/solution.py
@@ -65,19 +65,19 @@
         (down_ref, slice(2 * LANES, 3 * LANES), jnp.where(left, turned, middle)),
     ):
         ref[where, 0:LANES] = first[:, side].astype(jnp.bfloat16)
-        ref[where, LANES : 2 * LANES] = second[:, side].astype(jnp.bfloat16)
-        ref[where, 2 * LANES : 3 * LANES] = mixed.astype(jnp.bfloat16)
+        ref[where, LANES : 2 * LANES] = mixed.astype(jnp.bfloat16)
+        ref[where, 2 * LANES : 3 * LANES] = second[:, side].astype(jnp.bfloat16)
 
 
 def load_packed(up, down):
     left = iota((up.shape[0], LANES), 1) < HALF_LANES
-    up_mixed, down_mixed = up[:, 2 * LANES :], down[:, 2 * LANES :]
+    up_mixed, down_mixed = up[:, LANES : 2 * LANES], down[:, LANES : 2 * LANES]
     first = jnp.where(left, up_mixed, down_mixed)
     second = jnp.where(left, down_mixed, up_mixed)
     second = pltpu.roll(second.astype(jnp.float32), HALF_LANES, 1).astype(second.dtype)
     return (
         (up[:, :LANES], first, down[:, :LANES]),
-        (up[:, LANES : 2 * LANES], second, down[:, LANES : 2 * LANES]),
+        (up[:, 2 * LANES :], second, down[:, 2 * LANES :]),
     )
 
 
@@ -239,52 +239,44 @@
     return odd_block() == far
 
 
-def side_dot(far, weighted_ref, side_ref, near):
-    half = near.shape[0] // 2
-    mixed = side_ref[0:half, 2 * LANES :]
-    turned = pltpu.roll(mixed.astype(jnp.float32), HALF_LANES, 1).astype(mixed.dtype)
-
-    def fill(whole, shared):
-        near[0:half, whole : whole + LANES] = side_ref[0:half, 0:LANES]
-        near[half:, whole : whole + LANES] = side_ref[0:half, LANES : 2 * LANES]
-        near[0:half, shared : shared + LANES] = mixed
-        near[half:, shared : shared + LANES] = turned
-
-    @pl.when(above(far))
-    def _():
-        fill(0, LANES)
-
-    @pl.when(jnp.logical_not(above(far)))
-    def _():
-        fill(LANES, 0)
-
-    return jnp.dot(weighted_ref[...], near[...], preferred_element_type=jnp.float32)
-
-
-def close_kernel(weighted_ref, side_ref, window_ref, near):
-    window_ref[...] = side_dot(False, weighted_ref, side_ref, near)
-
-
-def far_kernel(groups, share, weighted_ref, side_ref, close_ref, totals_ref, *refs):
+def side_dot(weighted_ref, side_ref):
+    rows = weighted_ref.shape[1]
+    half = rows // 2
+
+    def dot(which, columns):
+        return jnp.dot(
+            weighted_ref[:, which], side_ref[0:half, columns], preferred_element_type=jnp.float32
+        )
+
+    first = dot(slice(0, half), slice(0, 2 * LANES))
+    second = dot(slice(half, rows), slice(LANES, 3 * LANES))
+    whole = first[:, 0:LANES] + second[:, LANES:]
+    return whole, first[:, LANES:] + pltpu.roll(second[:, 0:LANES], HALF_LANES, 1)
+
+
+def close_kernel(weighted_ref, side_ref, whole_ref, shared_ref):
+    whole_ref[...], shared_ref[...] = side_dot(weighted_ref, side_ref)
+
+
+def far_kernel(groups, share, weighted_ref, side_ref, whole_ref, shared_ref, totals_ref, *refs):
     own_parts, own_sum_ref = refs[:groups], refs[groups]
-    targets, (near, window, tile, folded, flipped, extras) = refs[groups + 1 : 2 * groups + 1], refs[2 * groups + 1 :]
+    targets, (tile, folded, flipped, extras) = refs[groups + 1 : 2 * groups + 1], refs[2 * groups + 1 :]
     snps = tile.shape[1]
     own_sum_ref[...] = sum((part[...] for part in own_parts[1:]), own_parts[0][...])
-    window[...] = side_dot(True, weighted_ref, side_ref, near)
-    left = iota((tile.shape[0], LANES), 1) < HALF_LANES
-
-    def place(up, down):
-        tile[:, 0:LANES] = up[:, 0:LANES]
-        tile[:, LANES : 2 * LANES] = jnp.where(left, up[:, LANES:], down[:, 0:LANES])
-        tile[:, 2 * LANES :] = down[:, LANES:]
+    whole, shared = side_dot(weighted_ref, side_ref)
+    left = iota(shared.shape, 1) < HALF_LANES
 
     @pl.when(above(True))
     def _():
-        place(window, close_ref)
+        tile[:, 0:LANES] = whole
+        tile[:, LANES : 2 * LANES] = jnp.where(left, shared, shared_ref[...])
+        tile[:, 2 * LANES :] = whole_ref[...]
 
     @pl.when(jnp.logical_not(above(True)))
     def _():
-        place(close_ref, window)
+        tile[:, 0:LANES] = whole_ref[...]
+        tile[:, LANES : 2 * LANES] = jnp.where(left, shared_ref[...], shared)
+        tile[:, 2 * LANES :] = whole
 
     fold_by_column(tile, flipped, folded)
     square = (snps, snps)
@@ -516,7 +508,27 @@
     )
 
 
-def own_score_kernel(groups, share, reach_ref, own_sum_ref, annot_ref, scores, table):
+def owner_places(groups, size):
+    me = lax.axis_index("hap")
+
+    def mine(blocks, slot):
+        value = blocks[0][slot]
+        for group in range(1, groups):
+            value = jnp.where(me == group, blocks[group][slot], value)
+        return value * size
+
+    left = [mine(LEFT_BLOCKS, slot) for slot in range(groups)]
+    right = [mine(RIGHT_BLOCKS, slot) for slot in range(groups)]
+    return left + left[0:1], right + [(2 * me + 1) * size]
+
+
+def rows_at(ref, places, size):
+    return jnp.concatenate([ref[pl.ds(pl.multiple_of(place, 8), size), :] for place in places], axis=0)
+
+
+def own_score_kernel(
+    groups, share, reach_ref, own_sum_ref, annot_ref, near_annot_ref, scores, mine_ref, rows_ref, masks_ref, columns_ref, own_rows_ref, table
+):
     snps = annot_ref.shape[0]
     half = snps // 2
     wide = snps // groups
@@ -562,16 +574,48 @@
 
     slice_rows = pl.ds(pl.multiple_of(me * wide, 8), wide)
     mine = table[slice_rows, :]
+    mine_ref[...] = mine
     product = 1.0
     for pop in range(2):
         own_row = [mine[:, 4 * pop + k : 4 * pop + k + 1] for k in range(4)]
         product *= correlation(own_row, own_row, own_row[3])
     scores[slice_rows, :] += annot_ref[slice_rows, :] * product
 
+    size = wide // 2
+    left_places, right_places = owner_places(groups, size)
+    left_table, right_table = rows_at(table, left_places, size), rows_at(table, right_places, size)
+    local, lane = iota((size, LANES), 0), iota((size, LANES), 1)
+    own_row = jnp.concatenate(
+        [local + jnp.where(lane < size, a, b) for a, b in zip(left_places, right_places)], axis=0
+    )
+    shape = own_row.shape
+    lane = iota(shape, 1)
+    is_left = lane < size
+    for pop in range(2):
+        for k in range(3):
+            column = slice(4 * pop + k, 4 * pop + k + 1)
+            rows_ref[3 * pop + k] = jnp.where(is_left, left_table[:, column], right_table[:, column])
+    upper = me < groups // 2
+    block = lax.axis_index("snp")
+    last = reach_ref.shape[0] - 1
+    reach_there = jnp.where(
+        upper, reach_ref[jnp.minimum(block + 1, last)], reach_ref[jnp.maximum(block - 1, 0)]
+    )
+    apart = jnp.abs(own_row - (lane + me * wide))
+    ahead = (own_row - (lane + me * wide)) * jnp.where(upper, 1, -1) > 0
+    real = ahead & (lane < wide) & ((lane >= size) | (iota(shape, 0) < groups * size))
+    for number, limit in enumerate((reach_here, reach_there)):
+        masks_ref[number] = jnp.where(real & (snps - apart <= limit), 1.0, 0.0)
+    their_annots = near_annot_ref[slice_rows, :]
+    columns = jnp.concatenate([their_annots, jnp.zeros((LANES - wide, LANES), jnp.float32)], axis=0)
+    columns_ref[...] = columns.astype(jnp.bfloat16)
+    own_rows_ref[...] = rows_at(annot_ref, left_places + right_places, size).astype(jnp.bfloat16)
+
 
 def near_score_kernel(groups, share, reach_ref, *refs):
-    near_parts, (own_ref, table, annot_ref, near_annot_ref) = refs[:groups], refs[groups : groups + 4]
-    keep_ref, send_ref, near_out_ref, flipped, scores = refs[groups + 4 :]
+    near_parts, refs = refs[:groups], refs[groups:]
+    own_ref, mine_ref, rows_ref, masks_ref, columns_ref, own_rows_ref, annot_ref, near_annot_ref = refs[:8]
+    keep_ref, send_ref, near_out_ref, flipped, scores = refs[8:]
     snps = annot_ref.shape[0]
     wide = snps // groups
     size = wide // 2
@@ -579,17 +623,10 @@
     me = lax.axis_index("hap")
     block = lax.axis_index("snp")
     last = reach_ref.shape[0] - 1
-    upper = me < groups // 2
     reach_here = reach_ref[block]
     reach_there = jnp.where(
-        upper, reach_ref[jnp.minimum(block + 1, last)], reach_ref[jnp.maximum(block - 1, 0)]
-    )
-
-    def mine(choices):
-        value = choices[0]
-        for group in range(1, groups):
-            value = jnp.where(me == group, choices[group], value)
-        return value
+        me < groups // 2, reach_ref[jnp.minimum(block + 1, last)], reach_ref[jnp.maximum(block - 1, 0)]
+    )
 
     scores[...] = own_ref[...]
     near_sums = sum((part[...] for part in near_parts[1:]), near_parts[0][...])
@@ -606,41 +643,14 @@
         slots.append(pltpu.roll(near_counts, snps - slot * wide, 1)[:, 0:LANES])
     flipped[:, 0:size] = slots[0].T
     slots.append(pltpu.roll(flipped[0:size, :], size, 1))
-    left_places = [mine([LEFT_BLOCKS[g][slot] for g in range(groups)]) * size for slot in range(groups)]
-    right_places = [mine([RIGHT_BLOCKS[g][slot] for g in range(groups)]) * size for slot in range(groups)]
-    left_places.append(left_places[0])
-    right_places.append((2 * me + 1) * size)
-
-    def rows_of(ref, places):
-        return [ref[pl.ds(pl.multiple_of(place, 8), size), :] for place in places]
-
     near_fields = from_fields(jnp.concatenate(slots, axis=0))
-    left_table = jnp.concatenate(rows_of(table, left_places), axis=0)
-    right_table = jnp.concatenate(rows_of(table, right_places), axis=0)
-    local, lane = iota((size, LANES), 0), iota((size, LANES), 1)
-    is_left = lane < size
-    own_row = jnp.concatenate(
-        [local + jnp.where(is_left, a, b) for a, b in zip(left_places, right_places)], axis=0
-    )
-    shape = own_row.shape
-    lane = iota(shape, 1)
-    is_left = lane < size
-    apart = jnp.abs(own_row - (lane + me * wide))
-    ahead = (own_row - (lane + me * wide)) * jnp.where(upper, 1, -1) > 0
-    real = ahead & (lane < wide) & ((lane >= size) | (iota(shape, 0) < groups * size))
     product = 1.0
     for pop in range(2):
-        row_stats = [
-            jnp.where(
-                is_left,
-                left_table[:, 4 * pop + k : 4 * pop + k + 1],
-                right_table[:, 4 * pop + k : 4 * pop + k + 1],
-            )
-            for k in range(3)
-        ]
+        row_stats = [rows_ref[3 * pop + k] for k in range(3)]
         product *= correlation(row_stats, near_stats[pop], near_fields[pop])
-    near_here = jnp.where(real & (snps - apart <= reach_here), product, 0.0)
-    near_there = jnp.where(real & (snps - apart <= reach_there), product, 0.0)
+    near_here = jnp.where(masks_ref[0] > 0.0, product, 0.0)
+    near_there = jnp.where(masks_ref[1] > 0.0, product, 0.0)
+    is_left = iota(product.shape, 1) < size
 
     def sides(values):
         return jnp.concatenate(
@@ -648,22 +658,19 @@
         )
 
     slice_rows = pl.ds(pl.multiple_of(me * wide, 8), wide)
-    their_annots = near_annot_ref[slice_rows, :]
-    columns = jnp.concatenate([their_annots, jnp.zeros((LANES - wide, LANES), jnp.float32)], axis=0)
-    direct = dot_rounded(sides(near_here), columns.astype(jnp.bfloat16), 1)
-    places = left_places + right_places
-    for number, place in enumerate(places):
+    direct = dot_rounded(sides(near_here), columns_ref[...], 1)
+    left_places, right_places = owner_places(groups, size)
+    for number, place in enumerate(left_places + right_places):
         scores[pl.ds(pl.multiple_of(place, 8), size), :] += direct[number * size : (number + 1) * size, :]
-    own_rows = jnp.concatenate(rows_of(annot_ref, places), axis=0).astype(jnp.bfloat16)
-    near_scores = dot_rounded(sides(near_there), own_rows, 0)[0:wide, :]
-
-    mine_table = table[slice_rows, :]
+    near_scores = dot_rounded(sides(near_there), own_rows_ref[...], 0)[0:wide, :]
+
+    mine_table = mine_ref[...]
     far_product = 1.0
     for pop in range(2):
         own_row = [mine_table[:, 4 * pop + k : 4 * pop + k + 1] for k in range(3)]
         near_row = [near_table[:, 4 * pop + k : 4 * pop + k + 1] for k in range(4)]
         far_product *= correlation(own_row, near_row, near_row[3])
-    scores[slice_rows, :] += their_annots * jnp.where(reach_here >= snps, far_product, 0.0)
+    scores[slice_rows, :] += near_annot_ref[slice_rows, :] * jnp.where(reach_here >= snps, far_product, 0.0)
     near_scores += annot_ref[slice_rows, :] * jnp.where(reach_there >= snps, far_product, 0.0)
     near_out_ref[...] = pack_halves(near_scores)
 
@@ -671,7 +678,7 @@
         group = partner(me, step, groups)
         return pack_halves(scores[pl.ds(pl.multiple_of(group * wide, 8), wide), :])
 
-    for ref, steps in ((keep_ref, (0, 2)), (send_ref, (1, 3))):
+    for ref, steps in ((keep_ref, (0, 1)), (send_ref, (2, 3))):
         for number, step in enumerate(steps):
             ref[number * size : (number + 1) * size, :] = packed(step).astype(ref.dtype)
 
@@ -767,26 +774,21 @@
 
     near_shapes = [own_share_counts] + [compact if by_column else shape((share + 8, snps), i32)] * groups
     if by_column:
-        near = pltpu.VMEM((rows, 2 * LANES), bf16)
-        window = (snps + 16, 2 * LANES)
+        piece = shape((snps + 16, LANES), f32)
         work = dict(flops=4 * rows * snps * LANES, moved=rows * snps * 4)
-        close_counts = call(close_kernel, shape(window, f32), [VMEM] * 2, [near], **work)(
-            weighted, from_close
-        )
+        close_counts = call(close_kernel, [piece, piece], [VMEM] * 2, **work)(weighted, from_close)
         own_sum, *near_parts = call(
             functools.partial(far_kernel, groups, share),
             near_shapes,
-            [VMEM] * (4 + groups),
+            [VMEM] * (5 + groups),
             [
-                near,
-                pltpu.VMEM(window, f32),
                 tile,
                 folded,
                 pltpu.VMEM((snps, LANES), f32),
                 pltpu.VMEM((8 * groups, LANES), i32),
             ],
             **work,
-        )(weighted, from_far, close_counts, totals, *own_parts)
+        )(weighted, from_far, *close_counts, totals, *own_parts)
     else:
         own_sum, *near_parts = call(
             functools.partial(near_kernel, groups, share),
@@ -817,28 +819,37 @@
     own_share = shape((out_share, LANES), f32)
     packed_share = shape((half_share, LANES), f32)
     if by_column:
-        own_scores, table = call(
+        pair_rows = (groups + 1) * (out_share // 2)
+        prepared = call(
             functools.partial(own_score_kernel, groups, share),
-            [by_snp, by_snp],
-            [SMEM, VMEM, VMEM],
+            [
+                by_snp,
+                shape((out_share, LANES), f32),
+                shape((6, pair_rows, LANES), f32),
+                shape((2, pair_rows, LANES), f32),
+                shape((LANES, LANES), bf16),
+                shape((2 * pair_rows, LANES), bf16),
+            ],
+            [SMEM] + [VMEM] * 3,
+            [pltpu.VMEM((snps, LANES), f32)],
             flops=1 << 25,
             moved=1 << 20,
-        )(reach, own_sum, own_annots)
+        )(reach, own_sum, own_annots, near_annots)
         both = (2 * half_share, LANES)
         keep, send, near_scores = call(
             functools.partial(near_score_kernel, groups, share),
             [shape(both, f32), shape(both, bf16), packed_share],
-            [SMEM] + [VMEM] * (groups + 4),
+            [SMEM] + [VMEM] * (groups + 8),
             [pltpu.VMEM((LANES, LANES), i32), pltpu.VMEM((snps, LANES), f32)],
             flops=1 << 26,
             moved=1 << 21,
-        )(reach, *near_parts, own_scores, table, own_annots, near_annots)
-        part = around(send, groups, 1)
+        )(reach, *near_parts, *prepared, own_annots, near_annots)
+        part = around(send, groups, 2)
         there = to_neighbour(near_scores)
         mine, send = call(
             middle_kernel, [packed_share, shape((half_share, LANES), bf16)], [VMEM] * 2
         )(keep, part)
-        part = around(send, groups, 2)
+        part = around(send, groups, 1)
         return call(column_finish_kernel, result, [VMEM] * 3)(mine, part, there)
 
     tall = pltpu.VMEM((padded, LANES), f32)

time: 39 us -> 38.4 us (0.985)
    ppermute x1, starting transfers between devices: 2.2 us -> 1.73 us  [to_neighbour(): return lax.ppermute(value, ('snp', 'hap'), pairs)]
  transfers between devices with their start and end apart: 11 -> 11, of which waited for: 6 -> 6; matrix products, arithmetic and copies ran while one was open for 0% -> 0% of each run, Pallas kernels for 9% -> 10%
where the time goes in v11:
time: 38.4 us; the launch traced here: 38.2 us
  waiting for transfers between devices  15.2 us (40%)
  starting transfers between devices  14.1 us (37%)
  Pallas kernels  8.83 us (23%)
    ppermute x8, waiting for transfers between devices, around(): lax.ppermute(value, 'hap', [(source, partner(source, step, groups)) for s...  15.2 us
    ppermute x8, starting transfers between devices, around(): lax.ppermute(value, 'hap', [(source, partner(source, step, groups)) for s...  11.1 us
    pallas_call x1, Pallas kernels, per_device(): call(prepare_kernel, [shape((rows, snps), bf16), packed, packed], [HBM, H...  2.14 us
    ppermute x1, starting transfers between devices, to_neighbour(): return lax.ppermute(value, ('snp', 'hap'), pairs)  1.73 us
    pallas_call x1, Pallas kernels, per_device(): call(functools.partial(own_score_kernel, groups, share), [by_snp, shape((...  1.59 us
    ppermute x2, starting transfers between devices, swapped(): return lax.ppermute(value, 'snp', pairs)  1.22 us
    pallas_call x1, Pallas kernels, per_device(): call(functools.partial(near_score_kernel, groups, share), [shape(both, f3...  1.21 us
    pallas_call x1, Pallas kernels, per_device(): call(functools.partial(own_kernel, groups, share), [shape((snps + 16, row...  1.13 us
  transfers between devices with their start and end apart: 11, of which 6 were waited for; matrix products, arithmetic and copies ran while one was open for 0% of the time, Pallas kernels for 10%

profile of v11, /device:TPU:0, one launch (start us, length us, event | category | flops | bytes accessed | tf_op | source)
XLA Modules:
  0.0 38.2 jit_solution(6530380298481072216)
XLA Ops:
  0.0 0.0 copy-start.2
  0.0 2.1 %shard_map.46 = (bf16[2048,384]{1,0:T(8,128)(2,1)S(1)}, bf16[1056,384]{1,0:T(8,128)(2,1)S(1)}, bf16[1056,384]{1,0:T(8,128)(2,1)S(1)}) custom-call(s32[2048,384]{1,0:T(8,128)} %hap_ref.1, s32[50,384]{1,0:T(8,128)} %annot_ref.3), custom_call_target="tpu_custom_call" | custom-call | bytes 6291456 | tf_op jit(solution)/shard_map/pallas_call | solution.py:746
  2.1 0.5 %collective-permute-start.1 = (bf16[1056,384]{1,0:T(8,128)(2,1)S(1)}, bf16[1056,384]{1,0:T(8,128)(2,1)S(1)}, u32[]{:S(2)}, u32[]{:S(2)}) collective-permute-start(bf16[1056,384]{1,0:T(8,128)(2,1)S(1)} %get-tuple-element.37), channel_id=1, source_target_pairs={{0,4},{4,0},{8,12},{12,8},{1,5},{5,1},{9,13},{13,9},{2,6},{6,2},{1... | collective-permute-start | bytes 2433032 | tf_op jit(solution)/shard_map/ppermute | solution.py:727
  2.7 0.7 %collective-permute-start = (bf16[1056,384]{1,0:T(8,128)(2,1)S(1)}, bf16[1056,384]{1,0:T(8,128)(2,1)S(1)}, u32[]{:S(2)}, u32[]{:S(2)}) collective-permute-start(bf16[1056,384]{1,0:T(8,128)(2,1)S(1)} %get-tuple-element.36), channel_id=1, source_target_pairs={{4,8},{8,4},{5,9},{9,5},{6,10},{10,6},{7,11},{11,7},{20,24},{24,20... | collective-permute-start | bytes 2433032 | tf_op jit(solution)/shard_map/ppermute | solution.py:727
  3.4 0.0 copy-done.2
  3.4 1.1 %shard_map.47 = (bf16[400,2048]{1,0:T(8,128)(2,1)S(1)}, f32[8,384]{1,0:T(8,128)S(1)}, s32[152,128]{1,0:T(8,128)S(1)}, s32[152,128]{1,0:T(8,128)S(1)}, s32[152,128]{1,0:T(8,128)S(1)}, /*index=5*/s32[152,128]{1,0:T(8,128)S(1)}) custom-call(bf16[2048,384]{1,0:T(8,128)(2,1)S(1)} %get-tuple-element.34.alleles_ref, s32[1,2048]{1,0:T(1,128)S(1)} %bitcast.1), custom_call_target="tpu_custom_call" | custom-call | flops 603979776 | bytes 3145728 | tf_op jit(solution)/shard_map/pallas_call | solution.py:765
  4.5 4.7 %collective-permute-start.2 = (s32[152,128]{1,0:T(8,128)S(1)}, s32[152,128]{1,0:T(8,128)S(1)}, u32[]{:S(2)}, u32[]{:S(2)}) collective-permute-start(s32[152,128]{1,0:T(8,128)S(1)} %get-tuple-element.42), channel_id=1, source_target_pairs={{0,3},{1,2},{2,1},{3,0},{4,7},{5,6},{6,5},{7,4},{8,11},{9,10},{10,... | collective-permute-start | bytes 233480 | tf_op jit(solution)/shard_map/ppermute | solution.py:718
  9.2 0.0 collective-permute-start.3
  9.2 0.6 %collective-permute-start.4 = (s32[152,128]{1,0:T(8,128)S(1)}, s32[152,128]{1,0:T(8,128)S(1)}, u32[]{:S(2)}, u32[]{:S(2)}) collective-permute-start(s32[152,128]{1,0:T(8,128)S(1)} %get-tuple-element.44), channel_id=1, source_target_pairs={{0,1},{1,0},{2,3},{3,2},{4,5},{5,4},{6,7},{7,6},{8,9},{9,8},{10,11... | collective-permute-start | bytes 233480 | tf_op jit(solution)/shard_map/ppermute | solution.py:718
  9.9 0.0 collective-permute-done.1.side_ref
  9.9 0.7 %shard_map.48 = (f32[400,128]{1,0:T(8,128)S(1)}, f32[400,128]{1,0:T(8,128)S(1)}) custom-call(bf16[400,2048]{1,0:T(8,128)(2,1)S(1)} %get-tuple-element.35.weighted_ref, bf16[1056,384]{1,0:T(8,128)(2,1)S(1)} %collective-permute-done.1.side_ref), custom_call_target="tpu_custom_call" | custom-call | flops 402653184 | bytes 3145728 | tf_op jit(solution)/shard_map/pallas_call | solution.py:779
  10.5 1.2 %collective-permute-done.2.refs_1_ = s32[152,128]{1,0:T(8,128)S(1)} collective-permute-done((s32[152,128]{1,0:T(8,128)S(1)}, s32[152,128]{1,0:T(8,128)S(1)}, u32[]{:S(2)}, u32[]{:S(2)}) %collective-permute-start.2) | collective-permute-done | bytes 77856 | tf_op jit(solution)/shard_map/ppermute | solution.py:718
  11.7 5.3 %collective-permute-done.3.refs_2_ = s32[152,128]{1,0:T(8,128)S(1)} collective-permute-done((s32[152,128]{1,0:T(8,128)S(1)}, s32[152,128]{1,0:T(8,128)S(1)}, u32[]{:S(2)}, u32[]{:S(2)}) %collective-permute-start.3) | collective-permute-done | bytes 77856 | tf_op jit(solution)/shard_map/ppermute | solution.py:718
  17.0 0.0 collective-permute-done.4.refs_3_
  17.0 0.0 collective-permute-done.side_ref
  17.0 0.0 copy-start
  17.0 0.0 copy-start.1
  17.0 1.1 %shard_map.49 = (s32[152,128]{1,0:T(8,128)S(1)}, s32[152,128]{1,0:T(8,128)S(1)}, s32[152,128]{1,0:T(8,128)S(1)}, s32[152,128]{1,0:T(8,128)S(1)}, s32[152,128]{1,0:T(8,128)S(1)}) custom-call(bf16[400,2048]{1,0:T(8,128)(2,1)S(1)} %get-tuple-element.35.weighted_ref, bf16[1056,384]{1,0:T(8,128)(2,1)S(1)} %collective-permute-done.side_ref, ...), custom_call_target="tpu_custom_call" | custom-call | flops 402653184 | bytes 3145728 | tf_op jit(solution)/shard_map/pallas_call | solution.py:780
  18.1 0.1 collective-permute-start.5
  18.2 0.4 %collective-permute-start.6 = (s32[152,128]{1,0:T(8,128)S(1)}, s32[152,128]{1,0:T(8,128)S(1)}, u32[]{:S(2)}, u32[]{:S(2)}) collective-permute-start(s32[152,128]{1,0:T(8,128)S(1)} %get-tuple-element.47), channel_id=1, source_target_pairs={{0,2},{1,3},{2,0},{3,1},{4,6},{5,7},{6,4},{7,5},{8,10},{9,11},{10,... | collective-permute-start | bytes 233480 | tf_op jit(solution)/shard_map/ppermute | solution.py:718
  18.6 4.0 %collective-permute-start.7 = (s32[152,128]{1,0:T(8,128)S(1)}, s32[152,128]{1,0:T(8,128)S(1)}, u32[]{:S(2)}, u32[]{:S(2)}) collective-permute-start(s32[152,128]{1,0:T(8,128)S(1)} %get-tuple-element.48), channel_id=1, source_target_pairs={{0,1},{1,0},{2,3},{3,2},{4,5},{5,4},{6,7},{7,6},{8,9},{9,8},{10,11... | collective-permute-start | bytes 233480 | tf_op jit(solution)/shard_map/ppermute | solution.py:718
  22.6 0.0 copy-done
  22.6 0.3 shard_map.50
  22.8 0.0 copy-done.1
  22.9 1.6 %shard_map.51 = (f32[384,128]{1,0:T(8,128)S(1)}, f32[96,128]{1,0:T(8,128)S(1)}, f32[6,240,128]{2,1,0:T(8,128)S(1)}, f32[2,240,128]{2,1,0:T(8,128)S(1)}, bf16[128...) custom-call(s32[4]{0:T(128)S(1)} %copy-done.1, s32[152,128]{1,0:T(8,128)S(1)} %get-tuple-element.49.own_sum_ref, ...), custom_call_target="tpu_custom_call" | custom-call | flops 33554432 | bytes 1048576 | tf_op jit(solution)/shard_map/pallas_call | solution.py:823
  24.4 0.8 %collective-permute-done.5.refs_1_ = s32[152,128]{1,0:T(8,128)S(1)} collective-permute-done((s32[152,128]{1,0:T(8,128)S(1)}, s32[152,128]{1,0:T(8,128)S(1)}, u32[]{:S(2)}, u32[]{:S(2)}) %collective-permute-start.5) | collective-permute-done | bytes 77856 | tf_op jit(solution)/shard_map/ppermute | solution.py:718
  25.3 2.4 %collective-permute-done.6.refs_2_ = s32[152,128]{1,0:T(8,128)S(1)} collective-permute-done((s32[152,128]{1,0:T(8,128)S(1)}, s32[152,128]{1,0:T(8,128)S(1)}, u32[]{:S(2)}, u32[]{:S(2)}) %collective-permute-start.6) | collective-permute-done | bytes 77856 | tf_op jit(solution)/shard_map/ppermute | solution.py:718
  27.7 0.0 collective-permute-done.7.refs_3_
  27.7 1.2 %shard_map.52 = (f32[96,128]{1,0:T(8,128)S(1)}, bf16[96,128]{1,0:T(8,128)(2,1)S(1)}, f32[48,128]{1,0:T(8,128)S(1)}) custom-call(s32[4]{0:T(128)S(1)} %copy-done.1, s32[152,128]{1,0:T(8,128)S(1)} %get-tuple-element.45.refs_0_, s32[152,128]{1,0:T(8,128)S(1)} %collective-permute-done.5.refs_1_, s32[152,128]{1,0:T(8,128)S(1)} %collective-permute-done.6.refs_2_, ...), custom_call_target="tpu_custom_call" | custom-call | flops 67108864 | bytes 2097152 | tf_op jit(solution)/shard_map/pallas_call | solution.py:839
  28.9 1.1 %collective-permute-start.8 = (bf16[96,128]{1,0:T(8,128)(2,1)S(1)}, bf16[96,128]{1,0:T(8,128)(2,1)S(1)}, u32[]{:S(2)}, u32[]{:S(2)}) collective-permute-start(bf16[96,128]{1,0:T(8,128)(2,1)S(1)} %get-tuple-element.59), channel_id=1, source_target_pairs={{0,2},{1,3},{2,0},{3,1},{4,6},{5,7},{6,4},{7,5},{8,10},{9,11},{10,... | collective-permute-start | bytes 73736 | tf_op jit(solution)/shard_map/ppermute | solution.py:718
  30.0 1.7 %collective-permute-start.10 = (f32[48,128]{1,0:T(8,128)S(1)}, f32[48,128]{1,0:T(8,128)S(1)}, u32[]{:S(2)}, u32[]{:S(2)}) collective-permute-start(f32[48,128]{1,0:T(8,128)S(1)} %get-tuple-element.62), channel_id=1, source_target_pairs={{0,4},{1,5},{4,8},{5,9},{6,2},{7,3},{8,12},{9,13},{10,6},{11,7},{1... | collective-permute-start | bytes 73736 | tf_op jit(solution)/shard_map/ppermute | solution.py:815
  31.7 2.0 %collective-permute-done.8.part_ref = bf16[96,128]{1,0:T(8,128)(2,1)S(1)} collective-permute-done((bf16[96,128]{1,0:T(8,128)(2,1)S(1)}, bf16[96,128]{1,0:T(8,128)(2,1)S(1)}, u32[]{:S(2)}, u32[]{:S(2)}) %collective-permute-start.8) | collective-permute-done | bytes 24608 | tf_op jit(solution)/shard_map/ppermute | solution.py:718
  33.7 0.3 collective-permute-start.9
  34.0 0.0 collective-permute-done.10.there_ref
  34.0 3.5 %collective-permute-done.9.part_ref = bf16[48,128]{1,0:T(8,128)(2,1)S(1)} collective-permute-done((bf16[48,128]{1,0:T(8,128)(2,1)S(1)}, bf16[48,128]{1,0:T(8,128)(2,1)S(1)}, u32[]{:S(2)}, u32[]{:S(2)}) %collective-permute-start.9) | collective-permute-done | bytes 12320 | tf_op jit(solution)/shard_map/ppermute | solution.py:718
  37.5 0.7 %shard_map.54 = f32[50,96]{1,0:T(8,128)} custom-call(f32[48,128]{1,0:T(8,128)S(1)} %get-tuple-element.60.mine_ref, bf16[48,128]{1,0:T(8,128)(2,1)S(1)} %collective-permute-done.9.part_ref, f32[48,128]{1,0:T(8,128)S(1)} %collective-permute-done.10.there_ref), custom_call_target="tpu_custom_call" | custom-call | tf_op jit(solution)/shard_map/pallas_call | solution.py:853
  (3 shorter events, 0.0 us)
Async XLA Ops:
  0.0 3.4 %copy-start.2 = (s32[2048]{0:T(1024)S(1)}, s32[2048]{0:T(1024)}, u32[]{:S(2)}) copy-start(s32[2048]{0:T(1024)} %param.5) | copy-start | bytes 24580
  2.1 7.7 %collective-permute-start.1 = (bf16[1056,384]{1,0:T(8,128)(2,1)S(1)}, bf16[1056,384]{1,0:T(8,128)(2,1)S(1)}, u32[]{:S(2)}, u32[]{:S(2)}) collective-permute-start(bf16[1056,384]{1,0:T(8,128)(2,1)S(1)} %get-tuple-element.37), channel_id=1, source_target_pairs={{0,4},{4,0},{8,12},{12,8},{1,5},{5,1},{9,13},{13,9},{2,6},{6,2},{1... | collective-permute-start | bytes 2433032 | tf_op jit(solution)/shard_map/ppermute | solution.py:727
  2.7 14.3 %collective-permute-start = (bf16[1056,384]{1,0:T(8,128)(2,1)S(1)}, bf16[1056,384]{1,0:T(8,128)(2,1)S(1)}, u32[]{:S(2)}, u32[]{:S(2)}) collective-permute-start(bf16[1056,384]{1,0:T(8,128)(2,1)S(1)} %get-tuple-element.36), channel_id=1, source_target_pairs={{4,8},{8,4},{5,9},{9,5},{6,10},{10,6},{7,11},{11,7},{20,24},{24,20... | collective-permute-start | bytes 2433032 | tf_op jit(solution)/shard_map/ppermute | solution.py:727
  4.5 7.2 %collective-permute-start.2 = (s32[152,128]{1,0:T(8,128)S(1)}, s32[152,128]{1,0:T(8,128)S(1)}, u32[]{:S(2)}, u32[]{:S(2)}) collective-permute-start(s32[152,128]{1,0:T(8,128)S(1)} %get-tuple-element.42), channel_id=1, source_target_pairs={{0,3},{1,2},{2,1},{3,0},{4,7},{5,6},{6,5},{7,4},{8,11},{9,10},{10,... | collective-permute-start | bytes 233480 | tf_op jit(solution)/shard_map/ppermute | solution.py:718
  9.2 7.8 %collective-permute-start.3 = (s32[152,128]{1,0:T(8,128)S(1)}, s32[152,128]{1,0:T(8,128)S(1)}, u32[]{:S(2)}, u32[]{:S(2)}) collective-permute-start(s32[152,128]{1,0:T(8,128)S(1)} %get-tuple-element.43), channel_id=1, source_target_pairs={{0,2},{1,3},{2,0},{3,1},{4,6},{5,7},{6,4},{7,5},{8,10},{9,11},{10,... | collective-permute-start | bytes 233480 | tf_op jit(solution)/shard_map/ppermute | solution.py:718
  9.2 7.8 %collective-permute-start.4 = (s32[152,128]{1,0:T(8,128)S(1)}, s32[152,128]{1,0:T(8,128)S(1)}, u32[]{:S(2)}, u32[]{:S(2)}) collective-permute-start(s32[152,128]{1,0:T(8,128)S(1)} %get-tuple-element.44), channel_id=1, source_target_pairs={{0,1},{1,0},{2,3},{3,2},{4,5},{5,4},{6,7},{7,6},{8,9},{9,8},{10,11... | collective-permute-start | bytes 233480 | tf_op jit(solution)/shard_map/ppermute | solution.py:718
  17.0 5.6 %copy-start = (s32[50,384]{1,0:T(8,128)S(1)}, s32[50,384]{1,0:T(8,128)}, u32[]{:S(2)}) copy-start(s32[50,384]{1,0:T(8,128)} %annot_ref.3) | copy-start | bytes 230404
  17.0 5.8 %copy-start.1 = (s32[4]{0:T(128)S(1)}, s32[4]{0:T(128)}, u32[]{:S(2)}) copy-start(s32[4]{0:T(128)} %reach_ref.3) | copy-start | bytes 52
  18.1 7.2 %collective-permute-start.5 = (s32[152,128]{1,0:T(8,128)S(1)}, s32[152,128]{1,0:T(8,128)S(1)}, u32[]{:S(2)}, u32[]{:S(2)}) collective-permute-start(s32[152,128]{1,0:T(8,128)S(1)} %get-tuple-element.46), channel_id=1, source_target_pairs={{0,3},{1,2},{2,1},{3,0},{4,7},{5,6},{6,5},{7,4},{8,11},{9,10},{10,... | collective-permute-start | bytes 233480 | tf_op jit(solution)/shard_map/ppermute | solution.py:718
  18.2 9.5 %collective-permute-start.6 = (s32[152,128]{1,0:T(8,128)S(1)}, s32[152,128]{1,0:T(8,128)S(1)}, u32[]{:S(2)}, u32[]{:S(2)}) collective-permute-start(s32[152,128]{1,0:T(8,128)S(1)} %get-tuple-element.47), channel_id=1, source_target_pairs={{0,2},{1,3},{2,0},{3,1},{4,6},{5,7},{6,4},{7,5},{8,10},{9,11},{10,... | collective-permute-start | bytes 233480 | tf_op jit(solution)/shard_map/ppermute | solution.py:718
  18.6 9.1 %collective-permute-start.7 = (s32[152,128]{1,0:T(8,128)S(1)}, s32[152,128]{1,0:T(8,128)S(1)}, u32[]{:S(2)}, u32[]{:S(2)}) collective-permute-start(s32[152,128]{1,0:T(8,128)S(1)} %get-tuple-element.48), channel_id=1, source_target_pairs={{0,1},{1,0},{2,3},{3,2},{4,5},{5,4},{6,7},{7,6},{8,9},{9,8},{10,11... | collective-permute-start | bytes 233480 | tf_op jit(solution)/shard_map/ppermute | solution.py:718
  28.9 4.8 %collective-permute-start.8 = (bf16[96,128]{1,0:T(8,128)(2,1)S(1)}, bf16[96,128]{1,0:T(8,128)(2,1)S(1)}, u32[]{:S(2)}, u32[]{:S(2)}) collective-permute-start(bf16[96,128]{1,0:T(8,128)(2,1)S(1)} %get-tuple-element.59), channel_id=1, source_target_pairs={{0,2},{1,3},{2,0},{3,1},{4,6},{5,7},{6,4},{7,5},{8,10},{9,11},{10,... | collective-permute-start | bytes 73736 | tf_op jit(solution)/shard_map/ppermute | solution.py:718
  30.0 4.0 %collective-permute-start.10 = (f32[48,128]{1,0:T(8,128)S(1)}, f32[48,128]{1,0:T(8,128)S(1)}, u32[]{:S(2)}, u32[]{:S(2)}) collective-permute-start(f32[48,128]{1,0:T(8,128)S(1)} %get-tuple-element.62), channel_id=1, source_target_pairs={{0,4},{1,5},{4,8},{5,9},{6,2},{7,3},{8,12},{9,13},{10,6},{11,7},{1... | collective-permute-start | bytes 73736 | tf_op jit(solution)/shard_map/ppermute | solution.py:815
  33.7 3.8 %collective-permute-start.9 = (bf16[48,128]{1,0:T(8,128)(2,1)S(1)}, bf16[48,128]{1,0:T(8,128)(2,1)S(1)}, u32[]{:S(2)}, u32[]{:S(2)}) collective-permute-start(bf16[48,128]{1,0:T(8,128)(2,1)S(1)} %get-tuple-element.61), channel_id=1, source_target_pairs={{0,1},{1,0},{2,3},{3,2},{4,5},{5,4},{6,7},{7,6},{8,9},{9,8},{10,11... | collective-permute-start | bytes 36872 | tf_op jit(solution)/shard_map/ppermute | solution.py:718

commit v12 on v11

--- a/solution.py
+++ b/solution.py
@@ -13,7 +13,7 @@
 FIELD_BITS = 16
 LANES = 128
 HALF_LANES = LANES // 2
-CHUNKS = 4
+CHUNKS = 8
 VMEM = pl.BlockSpec(memory_space=pltpu.VMEM)
 SMEM = pl.BlockSpec(memory_space=pltpu.SMEM)
 HBM = pl.BlockSpec(memory_space=pltpu.HBM)
@@ -93,8 +93,8 @@
         for number, start in enumerate(starts)
     ]
     copies.append(pltpu.make_async_copy(annot_ref, held_annots, sems.at[2 * CHUNKS]))
-    for copy in copies:
-        copy.start()
+    for number, copy in enumerate(copies):
+        copy.start(priority=number % 2)
     part = far_ref.shape[0] - rows // 2
     odd = odd_block()
 
@@ -206,6 +206,10 @@
     diagonal = block(0)
     for number in range(1, 2 * owners):
         diagonal = jnp.where(lane >= number * size, block(number), diagonal)
+    inside = lane
+    for number in range(1, 2 * owners):
+        inside = jnp.where(lane >= number * size, lane - number * size, inside)
+    apart = jnp.sum(jnp.where(row == inside, diagonal, 0.0), axis=0, keepdims=True)
     flipped[:, 0:size] = diagonal.T
     corner = diagonal
     for owner in range(owners):
@@ -233,6 +237,7 @@
         for slot in range(1, owners):
             mixed = jnp.where(lane >= slot * wide, rolled[(slot - owner) % owners], mixed)
         folded[owner * size : (owner + 1) * size, :] = to_fields(mixed)
+    return apart
 
 
 def above(far):
@@ -278,11 +283,7 @@
         tile[:, LANES : 2 * LANES] = jnp.where(left, shared_ref[...], shared)
         tile[:, 2 * LANES :] = whole
 
-    fold_by_column(tile, flipped, folded)
-    square = (snps, snps)
-    apart = jnp.sum(
-        jnp.where(iota(square, 0) == iota(square, 1), tile[0:snps, :], 0.0), axis=0, keepdims=True
-    )
+    apart = fold_by_column(tile, flipped, folded)
     tiles = snps // LANES
     sizes = totals_ref[1:2, :]
     by_column = jnp.concatenate([sizes, tile[snps : snps + 1, :], apart, jnp.zeros((5, snps))], axis=0)
@@ -614,19 +615,14 @@
 
 def near_score_kernel(groups, share, reach_ref, *refs):
     near_parts, refs = refs[:groups], refs[groups:]
-    own_ref, mine_ref, rows_ref, masks_ref, columns_ref, own_rows_ref, annot_ref, near_annot_ref = refs[:8]
-    keep_ref, send_ref, near_out_ref, flipped, scores = refs[8:]
-    snps = annot_ref.shape[0]
+    own_ref, mine_ref, rows_ref, masks_ref, columns_ref, near_annot_ref = refs[:6]
+    keep_ref, send_ref, there_ref, far_ref, flipped, scores = refs[6:]
+    snps = near_annot_ref.shape[0]
     wide = snps // groups
     size = wide // 2
     tiles = snps // LANES
     me = lax.axis_index("hap")
-    block = lax.axis_index("snp")
-    last = reach_ref.shape[0] - 1
-    reach_here = reach_ref[block]
-    reach_there = jnp.where(
-        me < groups // 2, reach_ref[jnp.minimum(block + 1, last)], reach_ref[jnp.maximum(block - 1, 0)]
-    )
+    reach_here = reach_ref[lax.axis_index("snp")]
 
     scores[...] = own_ref[...]
     near_sums = sum((part[...] for part in near_parts[1:]), near_parts[0][...])
@@ -648,21 +644,12 @@
     for pop in range(2):
         row_stats = [rows_ref[3 * pop + k] for k in range(3)]
         product *= correlation(row_stats, near_stats[pop], near_fields[pop])
-    near_here = jnp.where(masks_ref[0] > 0.0, product, 0.0)
-    near_there = jnp.where(masks_ref[1] > 0.0, product, 0.0)
-    is_left = iota(product.shape, 1) < size
-
-    def sides(values):
-        return jnp.concatenate(
-            [jnp.where(is_left, values, 0.0), jnp.where(is_left, 0.0, values)], axis=0
-        )
-
-    slice_rows = pl.ds(pl.multiple_of(me * wide, 8), wide)
-    direct = dot_rounded(sides(near_here), columns_ref[...], 1)
+    here = jnp.where(masks_ref[0] > 0.0, product, 0.0)
+    there_ref[...] = jnp.where(masks_ref[1] > 0.0, product, 0.0)
+    direct = dot_rounded(sides(here, size), columns_ref[...], 1)
     left_places, right_places = owner_places(groups, size)
     for number, place in enumerate(left_places + right_places):
         scores[pl.ds(pl.multiple_of(place, 8), size), :] += direct[number * size : (number + 1) * size, :]
-    near_scores = dot_rounded(sides(near_there), own_rows_ref[...], 0)[0:wide, :]
 
     mine_table = mine_ref[...]
     far_product = 1.0
@@ -670,9 +657,9 @@
         own_row = [mine_table[:, 4 * pop + k : 4 * pop + k + 1] for k in range(3)]
         near_row = [near_table[:, 4 * pop + k : 4 * pop + k + 1] for k in range(4)]
         far_product *= correlation(own_row, near_row, near_row[3])
+    far_ref[...] = jnp.broadcast_to(far_product, far_ref.shape)
+    slice_rows = pl.ds(pl.multiple_of(me * wide, 8), wide)
     scores[slice_rows, :] += near_annot_ref[slice_rows, :] * jnp.where(reach_here >= snps, far_product, 0.0)
-    near_scores += annot_ref[slice_rows, :] * jnp.where(reach_there >= snps, far_product, 0.0)
-    near_out_ref[...] = pack_halves(near_scores)
 
     def packed(step):
         group = partner(me, step, groups)
@@ -681,6 +668,28 @@
     for ref, steps in ((keep_ref, (0, 1)), (send_ref, (2, 3))):
         for number, step in enumerate(steps):
             ref[number * size : (number + 1) * size, :] = packed(step).astype(ref.dtype)
+
+
+def sides(values, size):
+    is_left = iota(values.shape, 1) < size
+    return jnp.concatenate(
+        [jnp.where(is_left, values, 0.0), jnp.where(is_left, 0.0, values)], axis=0
+    )
+
+
+def there_kernel(groups, reach_ref, there_ref, far_ref, own_rows_ref, annot_ref, out_ref):
+    snps = annot_ref.shape[0]
+    wide = snps // groups
+    me = lax.axis_index("hap")
+    block = lax.axis_index("snp")
+    last = reach_ref.shape[0] - 1
+    reach_there = jnp.where(
+        me < groups // 2, reach_ref[jnp.minimum(block + 1, last)], reach_ref[jnp.maximum(block - 1, 0)]
+    )
+    scores = dot_rounded(sides(there_ref[...], wide // 2), own_rows_ref[...], 0)[0:wide, :]
+    slice_rows = pl.ds(pl.multiple_of(me * wide, 8), wide)
+    scores += annot_ref[slice_rows, :] * jnp.where(reach_there >= snps, far_ref[...], 0.0)
+    out_ref[...] = pack_halves(scores)
 
 
 def middle_kernel(keep_ref, part_ref, mine_ref, send_ref):
@@ -820,7 +829,7 @@
     packed_share = shape((half_share, LANES), f32)
     if by_column:
         pair_rows = (groups + 1) * (out_share // 2)
-        prepared = call(
+        own_scores, mine, rows_stats, masks, columns, own_rows = call(
             functools.partial(own_score_kernel, groups, share),
             [
                 by_snp,
@@ -836,14 +845,17 @@
             moved=1 << 20,
         )(reach, own_sum, own_annots, near_annots)
         both = (2 * half_share, LANES)
-        keep, send, near_scores = call(
+        keep, send, near_there, far_product = call(
             functools.partial(near_score_kernel, groups, share),
-            [shape(both, f32), shape(both, bf16), packed_share],
-            [SMEM] + [VMEM] * (groups + 8),
+            [shape(both, f32), shape(both, bf16), shape((pair_rows, LANES), f32), own_share],
+            [SMEM] + [VMEM] * (groups + 6),
             [pltpu.VMEM((LANES, LANES), i32), pltpu.VMEM((snps, LANES), f32)],
             flops=1 << 26,
             moved=1 << 21,
-        )(reach, *near_parts, *prepared, own_annots, near_annots)
+        )(reach, *near_parts, own_scores, mine, rows_stats, masks, columns, near_annots)
+        near_scores = call(
+            functools.partial(there_kernel, groups), packed_share, [SMEM] + [VMEM] * 4, moved=1 << 19
+        )(reach, near_there, far_product, own_rows, own_annots)
         part = around(send, groups, 2)
         there = to_neighbour(near_scores)
         mine, send = call(

time: 38.4 us -> 38.9 us (1.013)
  the two profiles are of different devices: /device:TPU:0 before, /device:TPU:1 now
where the time goes in v12:
time: 38.9 us; the launch traced here: 38.4 us
  starting transfers between devices  17.7 us (46%)
  waiting for transfers between devices  10.5 us (27%)
  Pallas kernels  10.1 us (26%)
    ppermute x8, waiting for transfers between devices, around(): lax.ppermute(value, 'hap', [(source, partner(source, step, groups)) for s...  9.75 us
    ppermute x8, starting transfers between devices, around(): lax.ppermute(value, 'hap', [(source, partner(source, step, groups)) for s...  8.8 us
    ppermute x2, starting transfers between devices, swapped(): return lax.ppermute(value, 'snp', pairs)  4.63 us
    ppermute x1, starting transfers between devices, to_neighbour(): return lax.ppermute(value, ('snp', 'hap'), pairs)  4.29 us
    pallas_call x1, Pallas kernels, per_device(): call(prepare_kernel, [shape((rows, snps), bf16), packed, packed], [HBM, H...  2.67 us
    pallas_call x1, Pallas kernels, per_device(): call(functools.partial(own_score_kernel, groups, share), [by_snp, shape((...  1.58 us
    pallas_call x1, Pallas kernels, per_device(): call(functools.partial(own_kernel, groups, share), [shape((snps + 16, row...  1.13 us
    pallas_call x1, Pallas kernels, per_device(): call(functools.partial(near_score_kernel, groups, share), [shape(both, f3...  1.11 us
  transfers between devices with their start and end apart: 11, of which 6 were waited for; matrix products, arithmetic and copies ran while one was open for 0% of the time, Pallas kernels for 12%

profile of v12, /device:TPU:1, one launch (start us, length us, event | category | flops | bytes accessed | tf_op | source)
XLA Modules:
  0.0 38.4 jit_solution(5082675401839489193)
XLA Ops:
  0.0 0.0 copy-start.2
  0.0 2.7 %shard_map.46 = (bf16[2048,384]{1,0:T(8,128)(2,1)S(1)}, bf16[1056,384]{1,0:T(8,128)(2,1)S(1)}, bf16[1056,384]{1,0:T(8,128)(2,1)S(1)}) custom-call(s32[2048,384]{1,0:T(8,128)} %hap_ref.1, s32[50,384]{1,0:T(8,128)} %annot_ref.3), custom_call_target="tpu_custom_call" | custom-call | bytes 6291456 | tf_op jit(solution)/shard_map/pallas_call | solution.py:755
  2.7 0.2 collective-permute-start.1
  2.8 4.5 %collective-permute-start = (bf16[1056,384]{1,0:T(8,128)(2,1)S(1)}, bf16[1056,384]{1,0:T(8,128)(2,1)S(1)}, u32[]{:S(2)}, u32[]{:S(2)}) collective-permute-start(bf16[1056,384]{1,0:T(8,128)(2,1)S(1)} %get-tuple-element.37), channel_id=1, source_target_pairs={{4,8},{8,4},{5,9},{9,5},{6,10},{10,6},{7,11},{11,7},{20,24},{24,20... | collective-permute-start | bytes 2433032 | tf_op jit(solution)/shard_map/ppermute | solution.py:736
  7.3 0.0 copy-done.2
  7.3 1.1 %shard_map.47 = (bf16[400,2048]{1,0:T(8,128)(2,1)S(1)}, f32[8,384]{1,0:T(8,128)S(1)}, s32[152,128]{1,0:T(8,128)S(1)}, s32[152,128]{1,0:T(8,128)S(1)}, s32[152,128]{1,0:T(8,128)S(1)}, /*index=5*/s32[152,128]{1,0:T(8,128)S(1)}) custom-call(bf16[2048,384]{1,0:T(8,128)(2,1)S(1)} %get-tuple-element.35.alleles_ref, s32[1,2048]{1,0:T(1,128)S(1)} %bitcast.1), custom_call_target="tpu_custom_call" | custom-call | flops 603979776 | bytes 3145728 | tf_op jit(solution)/shard_map/pallas_call | solution.py:774
  8.5 3.4 %collective-permute-start.2 = (s32[152,128]{1,0:T(8,128)S(1)}, s32[152,128]{1,0:T(8,128)S(1)}, u32[]{:S(2)}, u32[]{:S(2)}) collective-permute-start(s32[152,128]{1,0:T(8,128)S(1)} %get-tuple-element.43), channel_id=1, source_target_pairs={{0,3},{1,2},{2,1},{3,0},{4,7},{5,6},{6,5},{7,4},{8,11},{9,10},{10,... | collective-permute-start | bytes 233480 | tf_op jit(solution)/shard_map/ppermute | solution.py:727
  11.9 0.0 collective-permute-start.3
  11.9 0.4 collective-permute-start.4
  12.2 0.0 collective-permute-done.1.side_ref
  12.2 0.7 %shard_map.48 = (f32[400,128]{1,0:T(8,128)S(1)}, f32[400,128]{1,0:T(8,128)S(1)}) custom-call(bf16[400,2048]{1,0:T(8,128)(2,1)S(1)} %get-tuple-element.36.weighted_ref, bf16[1056,384]{1,0:T(8,128)(2,1)S(1)} %collective-permute-done.1.side_ref), custom_call_target="tpu_custom_call" | custom-call | flops 402653184 | bytes 3145728 | tf_op jit(solution)/shard_map/pallas_call | solution.py:788
  12.9 1.5 %collective-permute-done.2.refs_1_ = s32[152,128]{1,0:T(8,128)S(1)} collective-permute-done((s32[152,128]{1,0:T(8,128)S(1)}, s32[152,128]{1,0:T(8,128)S(1)}, u32[]{:S(2)}, u32[]{:S(2)}) %collective-permute-start.2) | collective-permute-done | bytes 77856 | tf_op jit(solution)/shard_map/ppermute | solution.py:727
  14.4 2.8 %collective-permute-done.3.refs_2_ = s32[152,128]{1,0:T(8,128)S(1)} collective-permute-done((s32[152,128]{1,0:T(8,128)S(1)}, s32[152,128]{1,0:T(8,128)S(1)}, u32[]{:S(2)}, u32[]{:S(2)}) %collective-permute-start.3) | collective-permute-done | bytes 77856 | tf_op jit(solution)/shard_map/ppermute | solution.py:727
  17.2 0.0 collective-permute-done.4.refs_3_
  17.2 0.0 collective-permute-done.side_ref
  17.2 0.0 copy-start
  17.2 0.0 copy-start.1
  17.2 1.1 %shard_map.49 = (s32[152,128]{1,0:T(8,128)S(1)}, s32[152,128]{1,0:T(8,128)S(1)}, s32[152,128]{1,0:T(8,128)S(1)}, s32[152,128]{1,0:T(8,128)S(1)}, s32[152,128]{1,0:T(8,128)S(1)}) custom-call(bf16[400,2048]{1,0:T(8,128)(2,1)S(1)} %get-tuple-element.36.weighted_ref, bf16[1056,384]{1,0:T(8,128)(2,1)S(1)} %collective-permute-done.side_ref, ...), custom_call_target="tpu_custom_call" | custom-call | flops 402653184 | bytes 3145728 | tf_op jit(solution)/shard_map/pallas_call | solution.py:789
  18.3 4.0 %collective-permute-start.5 = (s32[152,128]{1,0:T(8,128)S(1)}, s32[152,128]{1,0:T(8,128)S(1)}, u32[]{:S(2)}, u32[]{:S(2)}) collective-permute-start(s32[152,128]{1,0:T(8,128)S(1)} %get-tuple-element.47), channel_id=1, source_target_pairs={{0,3},{1,2},{2,1},{3,0},{4,7},{5,6},{6,5},{7,4},{8,11},{9,10},{10,... | collective-permute-start | bytes 233480 | tf_op jit(solution)/shard_map/ppermute | solution.py:727
  22.3 0.0 collective-permute-start.6
  22.3 0.4 collective-permute-start.7
  22.7 0.0 copy-done
  22.7 0.3 shard_map.50
  23.0 0.0 copy-done.1
  23.0 1.6 %shard_map.51 = (f32[384,128]{1,0:T(8,128)S(1)}, f32[96,128]{1,0:T(8,128)S(1)}, f32[6,240,128]{2,1,0:T(8,128)S(1)}, f32[2,240,128]{2,1,0:T(8,128)S(1)}, bf16[128...) custom-call(s32[4]{0:T(128)S(1)} %copy-done.1, s32[152,128]{1,0:T(8,128)S(1)} %get-tuple-element.50.own_sum_ref, ...), custom_call_target="tpu_custom_call" | custom-call | flops 33554432 | bytes 1048576 | tf_op jit(solution)/shard_map/pallas_call | solution.py:832
  24.6 0.5 %collective-permute-done.5.refs_1_ = s32[152,128]{1,0:T(8,128)S(1)} collective-permute-done((s32[152,128]{1,0:T(8,128)S(1)}, s32[152,128]{1,0:T(8,128)S(1)}, u32[]{:S(2)}, u32[]{:S(2)}) %collective-permute-start.5) | collective-permute-done | bytes 77856 | tf_op jit(solution)/shard_map/ppermute | solution.py:727
  25.1 3.2 %collective-permute-done.6.refs_2_ = s32[152,128]{1,0:T(8,128)S(1)} collective-permute-done((s32[152,128]{1,0:T(8,128)S(1)}, s32[152,128]{1,0:T(8,128)S(1)}, u32[]{:S(2)}, u32[]{:S(2)}) %collective-permute-start.6) | collective-permute-done | bytes 77856 | tf_op jit(solution)/shard_map/ppermute | solution.py:727
  28.3 0.0 collective-permute-done.7.refs_3_
  28.3 1.1 %shard_map.52 = (f32[96,128]{1,0:T(8,128)S(1)}, bf16[96,128]{1,0:T(8,128)(2,1)S(1)}, f32[240,128]{1,0:T(8,128)S(1)}, f32[96,128]{1,0:T(8,128)S(1)}) custom-call(s32[4]{0:T(128)S(1)} %copy-done.1, s32[152,128]{1,0:T(8,128)S(1)} %get-tuple-element.46.refs_0_, s32[152,128]{1,0:T(8,128)S(1)} %collective-permute-done.5.refs_1_, ...), custom_call_target="tpu_custom_call" | custom-call | flops 67108864 | bytes 2097152 | tf_op jit(solution)/shard_map/pallas_call | solution.py:848
  29.4 0.5 %collective-permute-start.8 = (bf16[96,128]{1,0:T(8,128)(2,1)S(1)}, bf16[96,128]{1,0:T(8,128)(2,1)S(1)}, u32[]{:S(2)}, u32[]{:S(2)}) collective-permute-start(bf16[96,128]{1,0:T(8,128)(2,1)S(1)} %get-tuple-element.59), channel_id=1, source_target_pairs={{0,2},{1,3},{2,0},{3,1},{4,6},{5,7},{6,4},{7,5},{8,10},{9,11},{10,... | collective-permute-start | bytes 73736 | tf_op jit(solution)/shard_map/ppermute | solution.py:727
  29.9 0.8 %shard_map.54 = f32[48,128]{1,0:T(8,128)S(1)} custom-call(s32[4]{0:T(128)S(1)} %copy-done.1, f32[240,128]{1,0:T(8,128)S(1)} %get-tuple-element.62.there_ref, f32[96,128]{1,0:T(8,128)S(1)} %get-tuple-element.63.far_ref, bf16[480,128]{1,0:T(8,128)(2,1)S(1)} %get-tuple-element.64.own_rows_ref, f32[384,128]{1,0:T(8,128)S(1)} %get-tuple-element.51.annot_ref), custom_call_target="tpu_custom_call" | custom-call | bytes 524288 | tf_op jit(solution)/shard_map/pallas_call | solution.py:856
  30.7 4.3 %collective-permute-start.10 = (f32[48,128]{1,0:T(8,128)S(1)}, f32[48,128]{1,0:T(8,128)S(1)}, u32[]{:S(2)}, u32[]{:S(2)}) collective-permute-start(f32[48,128]{1,0:T(8,128)S(1)} %shard_map.54), channel_id=1, source_target_pairs={{0,4},{1,5},{4,8},{5,9},{6,2},{7,3},{8,12},{9,13},{10,6},{11,7},{1... | collective-permute-start | bytes 73736 | tf_op jit(solution)/shard_map/ppermute | solution.py:824
  35.0 0.0 collective-permute-done.8.part_ref
  35.0 0.2 collective-permute-start.9
  35.2 0.7 %collective-permute-done.10.there_ref = f32[48,128]{1,0:T(8,128)S(1)} collective-permute-done((f32[48,128]{1,0:T(8,128)S(1)}, f32[48,128]{1,0:T(8,128)S(1)}, u32[]{:S(2)}, u32[]{:S(2)}) %collective-permute-start.10) | collective-permute-done | bytes 24608 | tf_op jit(solution)/shard_map/ppermute | solution.py:824
  35.9 1.7 %collective-permute-done.9.part_ref = bf16[48,128]{1,0:T(8,128)(2,1)S(1)} collective-permute-done((bf16[48,128]{1,0:T(8,128)(2,1)S(1)}, bf16[48,128]{1,0:T(8,128)(2,1)S(1)}, u32[]{:S(2)}, u32[]{:S(2)}) %collective-permute-start.9) | collective-permute-done | bytes 12320 | tf_op jit(solution)/shard_map/ppermute | solution.py:727
  37.6 0.7 %shard_map.55 = f32[50,96]{1,0:T(8,128)} custom-call(f32[48,128]{1,0:T(8,128)S(1)} %get-tuple-element.60.mine_ref, bf16[48,128]{1,0:T(8,128)(2,1)S(1)} %collective-permute-done.9.part_ref, f32[48,128]{1,0:T(8,128)S(1)} %collective-permute-done.10.there_ref), custom_call_target="tpu_custom_call" | custom-call | tf_op jit(solution)/shard_map/pallas_call | solution.py:865
  (3 shorter events, 0.0 us)
Async XLA Ops:
  0.0 7.3 %copy-start.2 = (s32[2048]{0:T(1024)S(1)}, s32[2048]{0:T(1024)}, u32[]{:S(2)}) copy-start(s32[2048]{0:T(1024)} %param.5) | copy-start | bytes 24580
  2.7 9.5 %collective-permute-start.1 = (bf16[1056,384]{1,0:T(8,128)(2,1)S(1)}, bf16[1056,384]{1,0:T(8,128)(2,1)S(1)}, u32[]{:S(2)}, u32[]{:S(2)}) collective-permute-start(bf16[1056,384]{1,0:T(8,128)(2,1)S(1)} %get-tuple-element.38), channel_id=1, source_target_pairs={{0,4},{4,0},{8,12},{12,8},{1,5},{5,1},{9,13},{13,9},{2,6},{6,2},{1... | collective-permute-start | bytes 2433032 | tf_op jit(solution)/shard_map/ppermute | solution.py:736
  2.8 14.4 %collective-permute-start = (bf16[1056,384]{1,0:T(8,128)(2,1)S(1)}, bf16[1056,384]{1,0:T(8,128)(2,1)S(1)}, u32[]{:S(2)}, u32[]{:S(2)}) collective-permute-start(bf16[1056,384]{1,0:T(8,128)(2,1)S(1)} %get-tuple-element.37), channel_id=1, source_target_pairs={{4,8},{8,4},{5,9},{9,5},{6,10},{10,6},{7,11},{11,7},{20,24},{24,20... | collective-permute-start | bytes 2433032 | tf_op jit(solution)/shard_map/ppermute | solution.py:736
  8.5 5.9 %collective-permute-start.2 = (s32[152,128]{1,0:T(8,128)S(1)}, s32[152,128]{1,0:T(8,128)S(1)}, u32[]{:S(2)}, u32[]{:S(2)}) collective-permute-start(s32[152,128]{1,0:T(8,128)S(1)} %get-tuple-element.43), channel_id=1, source_target_pairs={{0,3},{1,2},{2,1},{3,0},{4,7},{5,6},{6,5},{7,4},{8,11},{9,10},{10,... | collective-permute-start | bytes 233480 | tf_op jit(solution)/shard_map/ppermute | solution.py:727
  11.9 5.4 %collective-permute-start.3 = (s32[152,128]{1,0:T(8,128)S(1)}, s32[152,128]{1,0:T(8,128)S(1)}, u32[]{:S(2)}, u32[]{:S(2)}) collective-permute-start(s32[152,128]{1,0:T(8,128)S(1)} %get-tuple-element.44), channel_id=1, source_target_pairs={{0,2},{1,3},{2,0},{3,1},{4,6},{5,7},{6,4},{7,5},{8,10},{9,11},{10,... | collective-permute-start | bytes 233480 | tf_op jit(solution)/shard_map/ppermute | solution.py:727
  11.9 5.4 %collective-permute-start.4 = (s32[152,128]{1,0:T(8,128)S(1)}, s32[152,128]{1,0:T(8,128)S(1)}, u32[]{:S(2)}, u32[]{:S(2)}) collective-permute-start(s32[152,128]{1,0:T(8,128)S(1)} %get-tuple-element.45), channel_id=1, source_target_pairs={{0,1},{1,0},{2,3},{3,2},{4,5},{5,4},{6,7},{7,6},{8,9},{9,8},{10,11... | collective-permute-start | bytes 233480 | tf_op jit(solution)/shard_map/ppermute | solution.py:727
  17.2 5.5 %copy-start = (s32[50,384]{1,0:T(8,128)S(1)}, s32[50,384]{1,0:T(8,128)}, u32[]{:S(2)}) copy-start(s32[50,384]{1,0:T(8,128)} %annot_ref.3) | copy-start | bytes 230404
  17.2 5.7 %copy-start.1 = (s32[4]{0:T(128)S(1)}, s32[4]{0:T(128)}, u32[]{:S(2)}) copy-start(s32[4]{0:T(128)} %reach_ref.5) | copy-start | bytes 52
  18.3 6.8 %collective-permute-start.5 = (s32[152,128]{1,0:T(8,128)S(1)}, s32[152,128]{1,0:T(8,128)S(1)}, u32[]{:S(2)}, u32[]{:S(2)}) collective-permute-start(s32[152,128]{1,0:T(8,128)S(1)} %get-tuple-element.47), channel_id=1, source_target_pairs={{0,3},{1,2},{2,1},{3,0},{4,7},{5,6},{6,5},{7,4},{8,11},{9,10},{10,... | collective-permute-start | bytes 233480 | tf_op jit(solution)/shard_map/ppermute | solution.py:727
  22.3 5.9 %collective-permute-start.6 = (s32[152,128]{1,0:T(8,128)S(1)}, s32[152,128]{1,0:T(8,128)S(1)}, u32[]{:S(2)}, u32[]{:S(2)}) collective-permute-start(s32[152,128]{1,0:T(8,128)S(1)} %get-tuple-element.48), channel_id=1, source_target_pairs={{0,2},{1,3},{2,0},{3,1},{4,6},{5,7},{6,4},{7,5},{8,10},{9,11},{10,... | collective-permute-start | bytes 233480 | tf_op jit(solution)/shard_map/ppermute | solution.py:727
  22.3 5.9 %collective-permute-start.7 = (s32[152,128]{1,0:T(8,128)S(1)}, s32[152,128]{1,0:T(8,128)S(1)}, u32[]{:S(2)}, u32[]{:S(2)}) collective-permute-start(s32[152,128]{1,0:T(8,128)S(1)} %get-tuple-element.49), channel_id=1, source_target_pairs={{0,1},{1,0},{2,3},{3,2},{4,5},{5,4},{6,7},{7,6},{8,9},{9,8},{10,11... | collective-permute-start | bytes 233480 | tf_op jit(solution)/shard_map/ppermute | solution.py:727
  29.4 5.6 %collective-permute-start.8 = (bf16[96,128]{1,0:T(8,128)(2,1)S(1)}, bf16[96,128]{1,0:T(8,128)(2,1)S(1)}, u32[]{:S(2)}, u32[]{:S(2)}) collective-permute-start(bf16[96,128]{1,0:T(8,128)(2,1)S(1)} %get-tuple-element.59), channel_id=1, source_target_pairs={{0,2},{1,3},{2,0},{3,1},{4,6},{5,7},{6,4},{7,5},{8,10},{9,11},{10,... | collective-permute-start | bytes 73736 | tf_op jit(solution)/shard_map/ppermute | solution.py:727
  30.7 5.2 %collective-permute-start.10 = (f32[48,128]{1,0:T(8,128)S(1)}, f32[48,128]{1,0:T(8,128)S(1)}, u32[]{:S(2)}, u32[]{:S(2)}) collective-permute-start(f32[48,128]{1,0:T(8,128)S(1)} %shard_map.54), channel_id=1, source_target_pairs={{0,4},{1,5},{4,8},{5,9},{6,2},{7,3},{8,12},{9,13},{10,6},{11,7},{1... | collective-permute-start | bytes 73736 | tf_op jit(solution)/shard_map/ppermute | solution.py:824
  35.0 2.6 %collective-permute-start.9 = (bf16[48,128]{1,0:T(8,128)(2,1)S(1)}, bf16[48,128]{1,0:T(8,128)(2,1)S(1)}, u32[]{:S(2)}, u32[]{:S(2)}) collective-permute-start(bf16[48,128]{1,0:T(8,128)(2,1)S(1)} %get-tuple-element.61), channel_id=1, source_target_pairs={{0,1},{1,0},{2,3},{3,2},{4,5},{5,4},{6,7},{7,6},{8,9},{9,8},{10,11... | collective-permute-start | bytes 36872 | tf_op jit(solution)/shard_map/ppermute | solution.py:727

commit v13 on v11

--- a/solution.py
+++ b/solution.py
@@ -13,7 +13,7 @@
 FIELD_BITS = 16
 LANES = 128
 HALF_LANES = LANES // 2
-CHUNKS = 4
+CHUNKS = 8
 VMEM = pl.BlockSpec(memory_space=pltpu.VMEM)
 SMEM = pl.BlockSpec(memory_space=pltpu.SMEM)
 HBM = pl.BlockSpec(memory_space=pltpu.HBM)
@@ -258,11 +258,12 @@
     whole_ref[...], shared_ref[...] = side_dot(weighted_ref, side_ref)
 
 
-def far_kernel(groups, share, weighted_ref, side_ref, whole_ref, shared_ref, totals_ref, *refs):
-    own_parts, own_sum_ref = refs[:groups], refs[groups]
-    targets, (tile, folded, flipped, extras) = refs[groups + 1 : 2 * groups + 1], refs[2 * groups + 1 :]
+def far_kernel(
+    groups, share, weighted_ref, side_ref, whole_ref, shared_ref, totals_ref, mine_ref, nearest_ref, own_sum_ref, *refs
+):
+    targets, (tile, folded, flipped, extras) = refs[:groups], refs[groups:]
     snps = tile.shape[1]
-    own_sum_ref[...] = sum((part[...] for part in own_parts[1:]), own_parts[0][...])
+    own_sum_ref[...] = mine_ref[...] + nearest_ref[...]
     whole, shared = side_dot(weighted_ref, side_ref)
     left = iota(shared.shape, 1) < HALF_LANES
 
@@ -527,16 +528,19 @@
 
 
 def own_score_kernel(
-    groups, share, reach_ref, own_sum_ref, annot_ref, near_annot_ref, scores, mine_ref, rows_ref, masks_ref, columns_ref, own_rows_ref, table
+    groups, share, reach_ref, *refs
 ):
+    own_parts, refs = refs[: groups - 1], refs[groups - 1 :]
+    annot_ref, near_annot_ref, scores, mine_ref, rows_ref, masks_ref, columns_ref, own_rows_ref, table = refs
     snps = annot_ref.shape[0]
     half = snps // 2
     wide = snps // groups
     tiles = snps // LANES
     me = lax.axis_index("hap")
     reach_here = reach_ref[lax.axis_index("snp")]
-    own_counts = from_tiles(own_sum_ref[0 : tiles * share, :], share)
-    extras = from_fields(own_sum_ref[tiles * share :, :])
+    own_sums = sum((part[...] for part in own_parts[1:]), own_parts[0][...])
+    own_counts = from_tiles(own_sums[0 : tiles * share, :], share)
+    extras = from_fields(own_sums[tiles * share :, :])
 
     own_stats, lines = [], []
     for pop in range(2):
@@ -606,10 +610,13 @@
     real = ahead & (lane < wide) & ((lane >= size) | (iota(shape, 0) < groups * size))
     for number, limit in enumerate((reach_here, reach_there)):
         masks_ref[number] = jnp.where(real & (snps - apart <= limit), 1.0, 0.0)
-    their_annots = near_annot_ref[slice_rows, :]
-    columns = jnp.concatenate([their_annots, jnp.zeros((LANES - wide, LANES), jnp.float32)], axis=0)
-    columns_ref[...] = columns.astype(jnp.bfloat16)
-    own_rows_ref[...] = rows_at(annot_ref, left_places + right_places, size).astype(jnp.bfloat16)
+    theirs = near_annot_ref[slice_rows, :]
+    columns = [theirs[0:size], pltpu.roll(theirs[size:], HALF_LANES, 1), jnp.zeros((LANES - wide, LANES))]
+    columns_ref[...] = jnp.concatenate(columns, axis=0).astype(jnp.bfloat16)
+    own_rows = rows_at(annot_ref, left_places, size) + pltpu.roll(
+        rows_at(annot_ref, right_places, size), HALF_LANES, 1
+    )
+    own_rows_ref[...] = own_rows.astype(jnp.bfloat16)
 
 
 def near_score_kernel(groups, share, reach_ref, *refs):
@@ -650,19 +657,16 @@
         product *= correlation(row_stats, near_stats[pop], near_fields[pop])
     near_here = jnp.where(masks_ref[0] > 0.0, product, 0.0)
     near_there = jnp.where(masks_ref[1] > 0.0, product, 0.0)
-    is_left = iota(product.shape, 1) < size
-
-    def sides(values):
-        return jnp.concatenate(
-            [jnp.where(is_left, values, 0.0), jnp.where(is_left, 0.0, values)], axis=0
-        )
-
     slice_rows = pl.ds(pl.multiple_of(me * wide, 8), wide)
-    direct = dot_rounded(sides(near_here), columns_ref[...], 1)
-    left_places, right_places = owner_places(groups, size)
-    for number, place in enumerate(left_places + right_places):
-        scores[pl.ds(pl.multiple_of(place, 8), size), :] += direct[number * size : (number + 1) * size, :]
-    near_scores = dot_rounded(sides(near_there), own_rows_ref[...], 0)[0:wide, :]
+    direct = dot_rounded(near_here, columns_ref[...], 1)
+    turned = pltpu.roll(direct, HALF_LANES, 1)
+    for values, places in zip((direct, turned), owner_places(groups, size)):
+        for slot, place in enumerate(places):
+            scores[pl.ds(pl.multiple_of(place, 8), size), :] += values[slot * size : (slot + 1) * size, :]
+    near_scores = dot_rounded(near_there, own_rows_ref[...], 0)
+    near_scores = jnp.where(
+        iota((size, LANES), 1) < HALF_LANES, near_scores[0:size], near_scores[size:wide]
+    )
 
     mine_table = mine_ref[...]
     far_product = 1.0
@@ -671,8 +675,8 @@
         near_row = [near_table[:, 4 * pop + k : 4 * pop + k + 1] for k in range(4)]
         far_product *= correlation(own_row, near_row, near_row[3])
     scores[slice_rows, :] += near_annot_ref[slice_rows, :] * jnp.where(reach_here >= snps, far_product, 0.0)
-    near_scores += annot_ref[slice_rows, :] * jnp.where(reach_there >= snps, far_product, 0.0)
-    near_out_ref[...] = pack_halves(near_scores)
+    far_scores = annot_ref[slice_rows, :] * jnp.where(reach_there >= snps, far_product, 0.0)
+    near_out_ref[...] = near_scores + pack_halves(far_scores)
 
     def packed(step):
         group = partner(me, step, groups)
@@ -780,7 +784,7 @@
         own_sum, *near_parts = call(
             functools.partial(far_kernel, groups, share),
             near_shapes,
-            [VMEM] * (5 + groups),
+            [VMEM] * 7,
             [
                 tile,
                 folded,
@@ -788,7 +792,7 @@
                 pltpu.VMEM((8 * groups, LANES), i32),
             ],
             **work,
-        )(weighted, from_far, *close_counts, totals, *own_parts)
+        )(weighted, from_far, *close_counts, totals, own_parts[0], own_parts[-1])
     else:
         own_sum, *near_parts = call(
             functools.partial(near_kernel, groups, share),
@@ -828,13 +832,13 @@
                 shape((6, pair_rows, LANES), f32),
                 shape((2, pair_rows, LANES), f32),
                 shape((LANES, LANES), bf16),
-                shape((2 * pair_rows, LANES), bf16),
+                shape((pair_rows, LANES), bf16),
             ],
-            [SMEM] + [VMEM] * 3,
+            [SMEM] + [VMEM] * (groups + 1),
             [pltpu.VMEM((snps, LANES), f32)],
             flops=1 << 25,
             moved=1 << 20,
-        )(reach, own_sum, own_annots, near_annots)
+        )(reach, own_sum, *own_parts[1:-1], own_annots, near_annots)
         both = (2 * half_share, LANES)
         keep, send, near_scores = call(
             functools.partial(near_score_kernel, groups, share),

time: 38.4 us -> 37.3 us (0.971)
  the two profiles are of different devices: /device:TPU:0 before, /device:TPU:1 now
where the time goes in v13:
time: 37.3 us; the launch traced here: 37.1 us
  starting transfers between devices  19.6 us (53%)
  Pallas kernels  8.9 us (24%)
  waiting for transfers between devices  8.47 us (23%)
    ppermute x8, starting transfers between devices, around(): lax.ppermute(value, 'hap', [(source, partner(source, step, groups)) for s...  10.8 us
    ppermute x2, waiting for transfers between devices, swapped(): return lax.ppermute(value, 'snp', pairs)  4.71 us
    ppermute x2, starting transfers between devices, swapped(): return lax.ppermute(value, 'snp', pairs)  4.6 us
    ppermute x1, starting transfers between devices, to_neighbour(): return lax.ppermute(value, ('snp', 'hap'), pairs)  4.2 us
    ppermute x8, waiting for transfers between devices, around(): lax.ppermute(value, 'hap', [(source, partner(source, step, groups)) for s...  3.55 us
    pallas_call x1, Pallas kernels, per_device(): call(prepare_kernel, [shape((rows, snps), bf16), packed, packed], [HBM, H...  2.26 us
    pallas_call x1, Pallas kernels, per_device(): call(functools.partial(own_score_kernel, groups, share), [by_snp, shape((...  1.62 us
    pallas_call x1, Pallas kernels, per_device(): call(functools.partial(near_score_kernel, groups, share), [shape(both, f3...  1.13 us
  transfers between devices with their start and end apart: 11, of which 4 were waited for; matrix products, arithmetic and copies ran while one was open for 0% of the time, Pallas kernels for 13%

profile of v13, /device:TPU:1, one launch (start us, length us, event | category | flops | bytes accessed | tf_op | source)
XLA Modules:
  0.0 37.1 jit_solution(9565284379944777592)
XLA Ops:
  0.0 0.0 copy-start.2
  0.0 2.3 %shard_map.46 = (bf16[2048,384]{1,0:T(8,128)(2,1)S(1)}, bf16[1056,384]{1,0:T(8,128)(2,1)S(1)}, bf16[1056,384]{1,0:T(8,128)(2,1)S(1)}) custom-call(s32[2048,384]{1,0:T(8,128)} %hap_ref.1, s32[50,384]{1,0:T(8,128)} %annot_ref.3), custom_call_target="tpu_custom_call" | custom-call | bytes 6291456 | tf_op jit(solution)/shard_map/pallas_call | solution.py:750
  2.3 0.1 collective-permute-start.1
  2.4 4.5 %collective-permute-start = (bf16[1056,384]{1,0:T(8,128)(2,1)S(1)}, bf16[1056,384]{1,0:T(8,128)(2,1)S(1)}, u32[]{:S(2)}, u32[]{:S(2)}) collective-permute-start(bf16[1056,384]{1,0:T(8,128)(2,1)S(1)} %get-tuple-element.36), channel_id=1, source_target_pairs={{4,8},{8,4},{5,9},{9,5},{6,10},{10,6},{7,11},{11,7},{20,24},{24,20... | collective-permute-start | bytes 2433032 | tf_op jit(solution)/shard_map/ppermute | solution.py:731
  6.9 0.0 copy-done.2
  6.9 1.1 %shard_map.47 = (bf16[400,2048]{1,0:T(8,128)(2,1)S(1)}, f32[8,384]{1,0:T(8,128)S(1)}, s32[152,128]{1,0:T(8,128)S(1)}, s32[152,128]{1,0:T(8,128)S(1)}, s32[152,128]{1,0:T(8,128)S(1)}, /*index=5*/s32[152,128]{1,0:T(8,128)S(1)}) custom-call(bf16[2048,384]{1,0:T(8,128)(2,1)S(1)} %get-tuple-element.34.alleles_ref, s32[1,2048]{1,0:T(1,128)S(1)} %bitcast.1), custom_call_target="tpu_custom_call" | custom-call | flops 603979776 | bytes 3145728 | tf_op jit(solution)/shard_map/pallas_call | solution.py:769
  8.0 1.4 %collective-permute-start.2 = (s32[152,128]{1,0:T(8,128)S(1)}, s32[152,128]{1,0:T(8,128)S(1)}, u32[]{:S(2)}, u32[]{:S(2)}) collective-permute-start(s32[152,128]{1,0:T(8,128)S(1)} %get-tuple-element.42), channel_id=1, source_target_pairs={{0,1},{1,0},{2,3},{3,2},{4,5},{5,4},{6,7},{7,6},{8,9},{9,8},{10,11... | collective-permute-start | bytes 233480 | tf_op jit(solution)/shard_map/ppermute | solution.py:722
  9.4 2.2 %collective-permute-start.6 = (s32[152,128]{1,0:T(8,128)S(1)}, s32[152,128]{1,0:T(8,128)S(1)}, u32[]{:S(2)}, u32[]{:S(2)}) collective-permute-start(s32[152,128]{1,0:T(8,128)S(1)} %get-tuple-element.48), channel_id=1, source_target_pairs={{0,3},{1,2},{2,1},{3,0},{4,7},{5,6},{6,5},{7,4},{8,11},{9,10},{10,... | collective-permute-start | bytes 233480 | tf_op jit(solution)/shard_map/ppermute | solution.py:722
  11.6 0.1 collective-permute-start.7
  11.7 0.0 collective-permute-done.1.side_ref
  11.7 0.7 %shard_map.48 = (f32[400,128]{1,0:T(8,128)S(1)}, f32[400,128]{1,0:T(8,128)S(1)}) custom-call(bf16[400,2048]{1,0:T(8,128)(2,1)S(1)} %get-tuple-element.35.weighted_ref, bf16[1056,384]{1,0:T(8,128)(2,1)S(1)} %collective-permute-done.1.side_ref), custom_call_target="tpu_custom_call" | custom-call | flops 402653184 | bytes 3145728 | tf_op jit(solution)/shard_map/pallas_call | solution.py:783
  12.4 0.0 copy-start
  12.4 0.0 collective-permute-done.2.nearest_ref
  12.4 4.7 %collective-permute-done.side_ref = bf16[1056,384]{1,0:T(8,128)(2,1)S(1)} collective-permute-done((bf16[1056,384]{1,0:T(8,128)(2,1)S(1)}, bf16[1056,384]{1,0:T(8,128)(2,1)S(1)}, u32[]{:S(2)}, u32[]{:S(2)}) %collective-permute-start) | collective-permute-done | bytes 811040 | tf_op jit(solution)/shard_map/ppermute | solution.py:731
  17.1 0.0 copy-start.1
  17.1 1.1 %shard_map.49 = (s32[152,128]{1,0:T(8,128)S(1)}, s32[152,128]{1,0:T(8,128)S(1)}, s32[152,128]{1,0:T(8,128)S(1)}, s32[152,128]{1,0:T(8,128)S(1)}, s32[152,128]{1,0:T(8,128)S(1)}) custom-call(bf16[400,2048]{1,0:T(8,128)(2,1)S(1)} %get-tuple-element.35.weighted_ref, bf16[1056,384]{1,0:T(8,128)(2,1)S(1)} %collective-permute-done.side_ref, ...), custom_call_target="tpu_custom_call" | custom-call | flops 402653184 | bytes 3145728 | tf_op jit(solution)/shard_map/pallas_call | solution.py:784
  18.2 4.0 %collective-permute-start.3 = (s32[152,128]{1,0:T(8,128)S(1)}, s32[152,128]{1,0:T(8,128)S(1)}, u32[]{:S(2)}, u32[]{:S(2)}) collective-permute-start(s32[152,128]{1,0:T(8,128)S(1)} %get-tuple-element.44), channel_id=1, source_target_pairs={{0,3},{1,2},{2,1},{3,0},{4,7},{5,6},{6,5},{7,4},{8,11},{9,10},{10,... | collective-permute-start | bytes 233480 | tf_op jit(solution)/shard_map/ppermute | solution.py:722
  22.2 0.0 collective-permute-start.4
  22.2 0.4 collective-permute-start.5
  22.6 0.0 copy-done
  22.6 0.3 shard_map.50
  22.8 0.0 collective-permute-done.6.refs_1_
  22.9 0.0 collective-permute-done.7.refs_2_
  22.9 0.0 copy-done.1
  22.9 1.6 %shard_map.51 = (f32[384,128]{1,0:T(8,128)S(1)}, f32[96,128]{1,0:T(8,128)S(1)}, f32[6,240,128]{2,1,0:T(8,128)S(1)}, f32[2,240,128]{2,1,0:T(8,128)S(1)}, bf16[128...) custom-call(s32[4]{0:T(128)S(1)} %copy-done.1, s32[152,128]{1,0:T(8,128)S(1)} %get-tuple-element.47.refs_0_, ...), custom_call_target="tpu_custom_call" | custom-call | flops 33554432 | bytes 1048576 | tf_op jit(solution)/shard_map/pallas_call | solution.py:827
  24.5 0.0 collective-permute-done.3.refs_1_
  24.5 1.8 %collective-permute-done.4.refs_2_ = s32[152,128]{1,0:T(8,128)S(1)} collective-permute-done((s32[152,128]{1,0:T(8,128)S(1)}, s32[152,128]{1,0:T(8,128)S(1)}, u32[]{:S(2)}, u32[]{:S(2)}) %collective-permute-start.4) | collective-permute-done | bytes 77856 | tf_op jit(solution)/shard_map/ppermute | solution.py:722
  26.3 0.0 collective-permute-done.5.refs_3_
  26.3 1.1 %shard_map.52 = (f32[96,128]{1,0:T(8,128)S(1)}, bf16[96,128]{1,0:T(8,128)(2,1)S(1)}, f32[48,128]{1,0:T(8,128)S(1)}) custom-call(s32[4]{0:T(128)S(1)} %copy-done.1, s32[152,128]{1,0:T(8,128)S(1)} %get-tuple-element.43.refs_0_, s32[152,128]{1,0:T(8,128)S(1)} %collective-permute-done.3.refs_1_, s32[152,128]{1,0:T(8,128)S(1)} %collective-permute-done.4.refs_2_, ...), custom_call_target="tpu_custom_call" | custom-call | flops 67108864 | bytes 2097152 | tf_op jit(solution)/shard_map/pallas_call | solution.py:843
  27.5 2.0 %collective-permute-start.8 = (bf16[96,128]{1,0:T(8,128)(2,1)S(1)}, bf16[96,128]{1,0:T(8,128)(2,1)S(1)}, u32[]{:S(2)}, u32[]{:S(2)}) collective-permute-start(bf16[96,128]{1,0:T(8,128)(2,1)S(1)} %get-tuple-element.59), channel_id=1, source_target_pairs={{0,2},{1,3},{2,0},{3,1},{4,6},{5,7},{6,4},{7,5},{8,10},{9,11},{10,... | collective-permute-start | bytes 73736 | tf_op jit(solution)/shard_map/ppermute | solution.py:722
  29.5 4.2 %collective-permute-start.10 = (f32[48,128]{1,0:T(8,128)S(1)}, f32[48,128]{1,0:T(8,128)S(1)}, u32[]{:S(2)}, u32[]{:S(2)}) collective-permute-start(f32[48,128]{1,0:T(8,128)S(1)} %get-tuple-element.62), channel_id=1, source_target_pairs={{0,4},{1,5},{4,8},{5,9},{6,2},{7,3},{8,12},{9,13},{10,6},{11,7},{1... | collective-permute-start | bytes 73736 | tf_op jit(solution)/shard_map/ppermute | solution.py:819
  33.7 0.0 collective-permute-done.8.part_ref
  33.8 0.7 %collective-permute-start.9 = (bf16[48,128]{1,0:T(8,128)(2,1)S(1)}, bf16[48,128]{1,0:T(8,128)(2,1)S(1)}, u32[]{:S(2)}, u32[]{:S(2)}) collective-permute-start(bf16[48,128]{1,0:T(8,128)(2,1)S(1)} %get-tuple-element.61), channel_id=1, source_target_pairs={{0,1},{1,0},{2,3},{3,2},{4,5},{5,4},{6,7},{7,6},{8,9},{9,8},{10,11... | collective-permute-start | bytes 36872 | tf_op jit(solution)/shard_map/ppermute | solution.py:722
  34.5 0.2 collective-permute-done.10.there_ref
  34.7 1.7 %collective-permute-done.9.part_ref = bf16[48,128]{1,0:T(8,128)(2,1)S(1)} collective-permute-done((bf16[48,128]{1,0:T(8,128)(2,1)S(1)}, bf16[48,128]{1,0:T(8,128)(2,1)S(1)}, u32[]{:S(2)}, u32[]{:S(2)}) %collective-permute-start.9) | collective-permute-done | bytes 12320 | tf_op jit(solution)/shard_map/ppermute | solution.py:722
  36.4 0.7 %shard_map.54 = f32[50,96]{1,0:T(8,128)} custom-call(f32[48,128]{1,0:T(8,128)S(1)} %get-tuple-element.60.mine_ref, bf16[48,128]{1,0:T(8,128)(2,1)S(1)} %collective-permute-done.9.part_ref, f32[48,128]{1,0:T(8,128)S(1)} %collective-permute-done.10.there_ref), custom_call_target="tpu_custom_call" | custom-call | tf_op jit(solution)/shard_map/pallas_call | solution.py:857
  (3 shorter events, 0.0 us)
Async XLA Ops:
  0.0 6.9 %copy-start.2 = (s32[2048]{0:T(1024)S(1)}, s32[2048]{0:T(1024)}, u32[]{:S(2)}) copy-start(s32[2048]{0:T(1024)} %param.5) | copy-start | bytes 24580
  2.3 9.4 %collective-permute-start.1 = (bf16[1056,384]{1,0:T(8,128)(2,1)S(1)}, bf16[1056,384]{1,0:T(8,128)(2,1)S(1)}, u32[]{:S(2)}, u32[]{:S(2)}) collective-permute-start(bf16[1056,384]{1,0:T(8,128)(2,1)S(1)} %get-tuple-element.37), channel_id=1, source_target_pairs={{0,4},{4,0},{8,12},{12,8},{1,5},{5,1},{9,13},{13,9},{2,6},{6,2},{1... | collective-permute-start | bytes 2433032 | tf_op jit(solution)/shard_map/ppermute | solution.py:731
  2.4 14.7 %collective-permute-start = (bf16[1056,384]{1,0:T(8,128)(2,1)S(1)}, bf16[1056,384]{1,0:T(8,128)(2,1)S(1)}, u32[]{:S(2)}, u32[]{:S(2)}) collective-permute-start(bf16[1056,384]{1,0:T(8,128)(2,1)S(1)} %get-tuple-element.36), channel_id=1, source_target_pairs={{4,8},{8,4},{5,9},{9,5},{6,10},{10,6},{7,11},{11,7},{20,24},{24,20... | collective-permute-start | bytes 2433032 | tf_op jit(solution)/shard_map/ppermute | solution.py:731
  8.0 4.4 %collective-permute-start.2 = (s32[152,128]{1,0:T(8,128)S(1)}, s32[152,128]{1,0:T(8,128)S(1)}, u32[]{:S(2)}, u32[]{:S(2)}) collective-permute-start(s32[152,128]{1,0:T(8,128)S(1)} %get-tuple-element.42), channel_id=1, source_target_pairs={{0,1},{1,0},{2,3},{3,2},{4,5},{5,4},{6,7},{7,6},{8,9},{9,8},{10,11... | collective-permute-start | bytes 233480 | tf_op jit(solution)/shard_map/ppermute | solution.py:722
  9.4 13.5 %collective-permute-start.6 = (s32[152,128]{1,0:T(8,128)S(1)}, s32[152,128]{1,0:T(8,128)S(1)}, u32[]{:S(2)}, u32[]{:S(2)}) collective-permute-start(s32[152,128]{1,0:T(8,128)S(1)} %get-tuple-element.48), channel_id=1, source_target_pairs={{0,3},{1,2},{2,1},{3,0},{4,7},{5,6},{6,5},{7,4},{8,11},{9,10},{10,... | collective-permute-start | bytes 233480 | tf_op jit(solution)/shard_map/ppermute | solution.py:722
  11.6 11.3 %collective-permute-start.7 = (s32[152,128]{1,0:T(8,128)S(1)}, s32[152,128]{1,0:T(8,128)S(1)}, u32[]{:S(2)}, u32[]{:S(2)}) collective-permute-start(s32[152,128]{1,0:T(8,128)S(1)} %get-tuple-element.49), channel_id=1, source_target_pairs={{0,2},{1,3},{2,0},{3,1},{4,6},{5,7},{6,4},{7,5},{8,10},{9,11},{10,... | collective-permute-start | bytes 233480 | tf_op jit(solution)/shard_map/ppermute | solution.py:722
  12.4 10.2 %copy-start = (s32[50,384]{1,0:T(8,128)S(1)}, s32[50,384]{1,0:T(8,128)}, u32[]{:S(2)}) copy-start(s32[50,384]{1,0:T(8,128)} %annot_ref.3) | copy-start | bytes 230404
  17.1 5.8 %copy-start.1 = (s32[4]{0:T(128)S(1)}, s32[4]{0:T(128)}, u32[]{:S(2)}) copy-start(s32[4]{0:T(128)} %reach_ref.3) | copy-start | bytes 52
  18.2 6.3 %collective-permute-start.3 = (s32[152,128]{1,0:T(8,128)S(1)}, s32[152,128]{1,0:T(8,128)S(1)}, u32[]{:S(2)}, u32[]{:S(2)}) collective-permute-start(s32[152,128]{1,0:T(8,128)S(1)} %get-tuple-element.44), channel_id=1, source_target_pairs={{0,3},{1,2},{2,1},{3,0},{4,7},{5,6},{6,5},{7,4},{8,11},{9,10},{10,... | collective-permute-start | bytes 233480 | tf_op jit(solution)/shard_map/ppermute | solution.py:722
  22.2 4.1 %collective-permute-start.4 = (s32[152,128]{1,0:T(8,128)S(1)}, s32[152,128]{1,0:T(8,128)S(1)}, u32[]{:S(2)}, u32[]{:S(2)}) collective-permute-start(s32[152,128]{1,0:T(8,128)S(1)} %get-tuple-element.45), channel_id=1, source_target_pairs={{0,2},{1,3},{2,0},{3,1},{4,6},{5,7},{6,4},{7,5},{8,10},{9,11},{10,... | collective-permute-start | bytes 233480 | tf_op jit(solution)/shard_map/ppermute | solution.py:722
  22.2 4.1 %collective-permute-start.5 = (s32[152,128]{1,0:T(8,128)S(1)}, s32[152,128]{1,0:T(8,128)S(1)}, u32[]{:S(2)}, u32[]{:S(2)}) collective-permute-start(s32[152,128]{1,0:T(8,128)S(1)} %get-tuple-element.46), channel_id=1, source_target_pairs={{0,1},{1,0},{2,3},{3,2},{4,5},{5,4},{6,7},{7,6},{8,9},{9,8},{10,11... | collective-permute-start | bytes 233480 | tf_op jit(solution)/shard_map/ppermute | solution.py:722
  27.5 6.3 %collective-permute-start.8 = (bf16[96,128]{1,0:T(8,128)(2,1)S(1)}, bf16[96,128]{1,0:T(8,128)(2,1)S(1)}, u32[]{:S(2)}, u32[]{:S(2)}) collective-permute-start(bf16[96,128]{1,0:T(8,128)(2,1)S(1)} %get-tuple-element.59), channel_id=1, source_target_pairs={{0,2},{1,3},{2,0},{3,1},{4,6},{5,7},{6,4},{7,5},{8,10},{9,11},{10,... | collective-permute-start | bytes 73736 | tf_op jit(solution)/shard_map/ppermute | solution.py:722
  29.5 5.1 %collective-permute-start.10 = (f32[48,128]{1,0:T(8,128)S(1)}, f32[48,128]{1,0:T(8,128)S(1)}, u32[]{:S(2)}, u32[]{:S(2)}) collective-permute-start(f32[48,128]{1,0:T(8,128)S(1)} %get-tuple-element.62), channel_id=1, source_target_pairs={{0,4},{1,5},{4,8},{5,9},{6,2},{7,3},{8,12},{9,13},{10,6},{11,7},{1... | collective-permute-start | bytes 73736 | tf_op jit(solution)/shard_map/ppermute | solution.py:819
  33.8 2.6 %collective-permute-start.9 = (bf16[48,128]{1,0:T(8,128)(2,1)S(1)}, bf16[48,128]{1,0:T(8,128)(2,1)S(1)}, u32[]{:S(2)}, u32[]{:S(2)}) collective-permute-start(bf16[48,128]{1,0:T(8,128)(2,1)S(1)} %get-tuple-element.61), channel_id=1, source_target_pairs={{0,1},{1,0},{2,3},{3,2},{4,5},{5,4},{6,7},{7,6},{8,9},{9,8},{10,11... | collective-permute-start | bytes 36872 | tf_op jit(solution)/shard_map/ppermute | solution.py:722

commit v14 on v13

--- a/solution.py
+++ b/solution.py
@@ -13,7 +13,7 @@
 FIELD_BITS = 16
 LANES = 128
 HALF_LANES = LANES // 2
-CHUNKS = 8
+CHUNKS = 4
 VMEM = pl.BlockSpec(memory_space=pltpu.VMEM)
 SMEM = pl.BlockSpec(memory_space=pltpu.SMEM)
 HBM = pl.BlockSpec(memory_space=pltpu.HBM)
@@ -802,7 +802,8 @@
             flops=2 * rows * snps * snps,
             moved=rows * snps * 4,
         )(weighted, from_far, from_close, totals, *own_parts)
-    near_parts = [near_parts[0]] + [around(near_parts[k], groups, k) for k in range(groups - 1, 0, -1)]
+    order = (2, 3, 1) if by_column else range(groups - 1, 0, -1)
+    near_parts = [near_parts[0]] + [around(near_parts[k], groups, k) for k in order]
 
     by_snp = shape((snps, LANES), f32)
     own_annots, near_annots = call(annots_kernel, [by_snp, by_snp], [VMEM] * 3, moved=1 << 20)(

time: 37.3 us -> 37.1 us (level)
  waiting for transfers between devices: 8.47 us -> 8.08 us
    ppermute x1, starting transfers between devices: 4.2 us -> 4.98 us  [to_neighbour(): return lax.ppermute(value, ('snp', 'hap'), pairs)]
    ppermute x8, starting transfers between devices: 10.8 us -> 10.4 us  [around(): lax.ppermute(value, 'hap', [(source, partner(source, step, groups)) for s...]
where the time goes in v14:
time: 37.1 us; the launch traced here: 37 us
  starting transfers between devices  19.9 us (54%)
  Pallas kernels  8.79 us (24%)
  waiting for transfers between devices  8.08 us (22%)
    ppermute x8, starting transfers between devices, around(): lax.ppermute(value, 'hap', [(source, partner(source, step, groups)) for s...  10.4 us
    ppermute x1, starting transfers between devices, to_neighbour(): return lax.ppermute(value, ('snp', 'hap'), pairs)  4.98 us
    ppermute x2, waiting for transfers between devices, swapped(): return lax.ppermute(value, 'snp', pairs)  4.71 us
    ppermute x2, starting transfers between devices, swapped(): return lax.ppermute(value, 'snp', pairs)  4.59 us
    ppermute x8, waiting for transfers between devices, around(): lax.ppermute(value, 'hap', [(source, partner(source, step, groups)) for s...  3.37 us
    pallas_call x1, Pallas kernels, per_device(): call(prepare_kernel, [shape((rows, snps), bf16), packed, packed], [HBM, H...  2.14 us
    pallas_call x1, Pallas kernels, per_device(): call(functools.partial(own_score_kernel, groups, share), [by_snp, shape((...  1.62 us
    pallas_call x1, Pallas kernels, per_device(): call(functools.partial(near_score_kernel, groups, share), [shape(both, f3...  1.13 us
  transfers between devices with their start and end apart: 11, of which 4 were waited for; matrix products, arithmetic and copies ran while one was open for 0% of the time, Pallas kernels for 13%

profile of v14, /device:TPU:1, one launch (start us, length us, event | category | flops | bytes accessed | tf_op | source)
XLA Modules:
  0.0 37.0 jit_solution(5107611205091057174)
XLA Ops:
  0.0 0.0 copy-start.2
  0.0 2.1 %shard_map.46 = (bf16[2048,384]{1,0:T(8,128)(2,1)S(1)}, bf16[1056,384]{1,0:T(8,128)(2,1)S(1)}, bf16[1056,384]{1,0:T(8,128)(2,1)S(1)}) custom-call(s32[2048,384]{1,0:T(8,128)} %hap_ref.1, s32[50,384]{1,0:T(8,128)} %annot_ref.3), custom_call_target="tpu_custom_call" | custom-call | bytes 6291456 | tf_op jit(solution)/shard_map/pallas_call | solution.py:750
  2.1 0.1 collective-permute-start.1
  2.3 4.5 %collective-permute-start = (bf16[1056,384]{1,0:T(8,128)(2,1)S(1)}, bf16[1056,384]{1,0:T(8,128)(2,1)S(1)}, u32[]{:S(2)}, u32[]{:S(2)}) collective-permute-start(bf16[1056,384]{1,0:T(8,128)(2,1)S(1)} %get-tuple-element.36), channel_id=1, source_target_pairs={{4,8},{8,4},{5,9},{9,5},{6,10},{10,6},{7,11},{11,7},{20,24},{24,20... | collective-permute-start | bytes 2433032 | tf_op jit(solution)/shard_map/ppermute | solution.py:731
  6.7 0.0 copy-done.2
  6.8 1.1 %shard_map.47 = (bf16[400,2048]{1,0:T(8,128)(2,1)S(1)}, f32[8,384]{1,0:T(8,128)S(1)}, s32[152,128]{1,0:T(8,128)S(1)}, s32[152,128]{1,0:T(8,128)S(1)}, s32[152,128]{1,0:T(8,128)S(1)}, /*index=5*/s32[152,128]{1,0:T(8,128)S(1)}) custom-call(bf16[2048,384]{1,0:T(8,128)(2,1)S(1)} %get-tuple-element.34.alleles_ref, s32[1,2048]{1,0:T(1,128)S(1)} %bitcast.1), custom_call_target="tpu_custom_call" | custom-call | flops 603979776 | bytes 3145728 | tf_op jit(solution)/shard_map/pallas_call | solution.py:769
  7.9 1.4 %collective-permute-start.2 = (s32[152,128]{1,0:T(8,128)S(1)}, s32[152,128]{1,0:T(8,128)S(1)}, u32[]{:S(2)}, u32[]{:S(2)}) collective-permute-start(s32[152,128]{1,0:T(8,128)S(1)} %get-tuple-element.42), channel_id=1, source_target_pairs={{0,1},{1,0},{2,3},{3,2},{4,5},{5,4},{6,7},{7,6},{8,9},{9,8},{10,11... | collective-permute-start | bytes 233480 | tf_op jit(solution)/shard_map/ppermute | solution.py:722
  9.3 2.2 %collective-permute-start.6 = (s32[152,128]{1,0:T(8,128)S(1)}, s32[152,128]{1,0:T(8,128)S(1)}, u32[]{:S(2)}, u32[]{:S(2)}) collective-permute-start(s32[152,128]{1,0:T(8,128)S(1)} %get-tuple-element.48), channel_id=1, source_target_pairs={{0,3},{1,2},{2,1},{3,0},{4,7},{5,6},{6,5},{7,4},{8,11},{9,10},{10,... | collective-permute-start | bytes 233480 | tf_op jit(solution)/shard_map/ppermute | solution.py:722
  11.4 0.1 collective-permute-start.7
  11.6 0.0 collective-permute-done.1.side_ref
  11.6 0.7 %shard_map.48 = (f32[400,128]{1,0:T(8,128)S(1)}, f32[400,128]{1,0:T(8,128)S(1)}) custom-call(bf16[400,2048]{1,0:T(8,128)(2,1)S(1)} %get-tuple-element.35.weighted_ref, bf16[1056,384]{1,0:T(8,128)(2,1)S(1)} %collective-permute-done.1.side_ref), custom_call_target="tpu_custom_call" | custom-call | flops 402653184 | bytes 3145728 | tf_op jit(solution)/shard_map/pallas_call | solution.py:783
  12.2 0.0 copy-start
  12.2 0.0 collective-permute-done.2.nearest_ref
  12.3 4.7 %collective-permute-done.side_ref = bf16[1056,384]{1,0:T(8,128)(2,1)S(1)} collective-permute-done((bf16[1056,384]{1,0:T(8,128)(2,1)S(1)}, bf16[1056,384]{1,0:T(8,128)(2,1)S(1)}, u32[]{:S(2)}, u32[]{:S(2)}) %collective-permute-start) | collective-permute-done | bytes 811040 | tf_op jit(solution)/shard_map/ppermute | solution.py:731
  17.0 0.0 copy-start.1
  17.0 1.1 %shard_map.49 = (s32[152,128]{1,0:T(8,128)S(1)}, s32[152,128]{1,0:T(8,128)S(1)}, s32[152,128]{1,0:T(8,128)S(1)}, s32[152,128]{1,0:T(8,128)S(1)}, s32[152,128]{1,0:T(8,128)S(1)}) custom-call(bf16[400,2048]{1,0:T(8,128)(2,1)S(1)} %get-tuple-element.35.weighted_ref, bf16[1056,384]{1,0:T(8,128)(2,1)S(1)} %collective-permute-done.side_ref, ...), custom_call_target="tpu_custom_call" | custom-call | flops 402653184 | bytes 3145728 | tf_op jit(solution)/shard_map/pallas_call | solution.py:784
  18.0 2.7 %collective-permute-start.3 = (s32[152,128]{1,0:T(8,128)S(1)}, s32[152,128]{1,0:T(8,128)S(1)}, u32[]{:S(2)}, u32[]{:S(2)}) collective-permute-start(s32[152,128]{1,0:T(8,128)S(1)} %get-tuple-element.44), channel_id=1, source_target_pairs={{0,2},{1,3},{2,0},{3,1},{4,6},{5,7},{6,4},{7,5},{8,10},{9,11},{10,... | collective-permute-start | bytes 233480 | tf_op jit(solution)/shard_map/ppermute | solution.py:722
  20.7 1.4 %collective-permute-start.4 = (s32[152,128]{1,0:T(8,128)S(1)}, s32[152,128]{1,0:T(8,128)S(1)}, u32[]{:S(2)}, u32[]{:S(2)}) collective-permute-start(s32[152,128]{1,0:T(8,128)S(1)} %get-tuple-element.45), channel_id=1, source_target_pairs={{0,3},{1,2},{2,1},{3,0},{4,7},{5,6},{6,5},{7,4},{8,11},{9,10},{10,... | collective-permute-start | bytes 233480 | tf_op jit(solution)/shard_map/ppermute | solution.py:722
  22.1 0.2 collective-permute-start.5
  22.3 0.0 copy-done
  22.3 0.3 shard_map.50
  22.6 0.0 collective-permute-done.6.refs_1_
  22.6 0.0 collective-permute-done.7.refs_2_
  22.6 0.0 copy-done.1
  22.7 1.6 %shard_map.51 = (f32[384,128]{1,0:T(8,128)S(1)}, f32[96,128]{1,0:T(8,128)S(1)}, f32[6,240,128]{2,1,0:T(8,128)S(1)}, f32[2,240,128]{2,1,0:T(8,128)S(1)}, bf16[128...) custom-call(s32[4]{0:T(128)S(1)} %copy-done.1, s32[152,128]{1,0:T(8,128)S(1)} %get-tuple-element.47.refs_0_, ...), custom_call_target="tpu_custom_call" | custom-call | flops 33554432 | bytes 1048576 | tf_op jit(solution)/shard_map/pallas_call | solution.py:828
  24.3 0.0 collective-permute-done.3.refs_1_
  24.3 1.6 %collective-permute-done.4.refs_2_ = s32[152,128]{1,0:T(8,128)S(1)} collective-permute-done((s32[152,128]{1,0:T(8,128)S(1)}, s32[152,128]{1,0:T(8,128)S(1)}, u32[]{:S(2)}, u32[]{:S(2)}) %collective-permute-start.4) | collective-permute-done | bytes 77856 | tf_op jit(solution)/shard_map/ppermute | solution.py:722
  25.9 0.3 collective-permute-done.5.refs_3_
  26.2 1.1 %shard_map.52 = (f32[96,128]{1,0:T(8,128)S(1)}, bf16[96,128]{1,0:T(8,128)(2,1)S(1)}, f32[48,128]{1,0:T(8,128)S(1)}) custom-call(s32[4]{0:T(128)S(1)} %copy-done.1, s32[152,128]{1,0:T(8,128)S(1)} %get-tuple-element.43.refs_0_, s32[152,128]{1,0:T(8,128)S(1)} %collective-permute-done.3.refs_1_, s32[152,128]{1,0:T(8,128)S(1)} %collective-permute-done.4.refs_2_, ...), custom_call_target="tpu_custom_call" | custom-call | flops 67108864 | bytes 2097152 | tf_op jit(solution)/shard_map/pallas_call | solution.py:844
  27.3 1.2 %collective-permute-start.8 = (bf16[96,128]{1,0:T(8,128)(2,1)S(1)}, bf16[96,128]{1,0:T(8,128)(2,1)S(1)}, u32[]{:S(2)}, u32[]{:S(2)}) collective-permute-start(bf16[96,128]{1,0:T(8,128)(2,1)S(1)} %get-tuple-element.59), channel_id=1, source_target_pairs={{0,2},{1,3},{2,0},{3,1},{4,6},{5,7},{6,4},{7,5},{8,10},{9,11},{10,... | collective-permute-start | bytes 73736 | tf_op jit(solution)/shard_map/ppermute | solution.py:722
  28.6 5.0 %collective-permute-start.10 = (f32[48,128]{1,0:T(8,128)S(1)}, f32[48,128]{1,0:T(8,128)S(1)}, u32[]{:S(2)}, u32[]{:S(2)}) collective-permute-start(f32[48,128]{1,0:T(8,128)S(1)} %get-tuple-element.62), channel_id=1, source_target_pairs={{0,4},{1,5},{4,8},{5,9},{6,2},{7,3},{8,12},{9,13},{10,6},{11,7},{1... | collective-permute-start | bytes 73736 | tf_op jit(solution)/shard_map/ppermute | solution.py:820
  33.6 0.0 collective-permute-done.8.part_ref
  33.6 1.2 %collective-permute-start.9 = (bf16[48,128]{1,0:T(8,128)(2,1)S(1)}, bf16[48,128]{1,0:T(8,128)(2,1)S(1)}, u32[]{:S(2)}, u32[]{:S(2)}) collective-permute-start(bf16[48,128]{1,0:T(8,128)(2,1)S(1)} %get-tuple-element.61), channel_id=1, source_target_pairs={{0,1},{1,0},{2,3},{3,2},{4,5},{5,4},{6,7},{7,6},{8,9},{9,8},{10,11... | collective-permute-start | bytes 36872 | tf_op jit(solution)/shard_map/ppermute | solution.py:722
  34.8 0.0 collective-permute-done.10.there_ref
  34.8 1.4 %collective-permute-done.9.part_ref = bf16[48,128]{1,0:T(8,128)(2,1)S(1)} collective-permute-done((bf16[48,128]{1,0:T(8,128)(2,1)S(1)}, bf16[48,128]{1,0:T(8,128)(2,1)S(1)}, u32[]{:S(2)}, u32[]{:S(2)}) %collective-permute-start.9) | collective-permute-done | bytes 12320 | tf_op jit(solution)/shard_map/ppermute | solution.py:722
  36.2 0.7 %shard_map.54 = f32[50,96]{1,0:T(8,128)} custom-call(f32[48,128]{1,0:T(8,128)S(1)} %get-tuple-element.60.mine_ref, bf16[48,128]{1,0:T(8,128)(2,1)S(1)} %collective-permute-done.9.part_ref, f32[48,128]{1,0:T(8,128)S(1)} %collective-permute-done.10.there_ref), custom_call_target="tpu_custom_call" | custom-call | tf_op jit(solution)/shard_map/pallas_call | solution.py:858
  (3 shorter events, 0.0 us)
Async XLA Ops:
  0.0 6.7 %copy-start.2 = (s32[2048]{0:T(1024)S(1)}, s32[2048]{0:T(1024)}, u32[]{:S(2)}) copy-start(s32[2048]{0:T(1024)} %param.5) | copy-start | bytes 24580
  2.1 9.4 %collective-permute-start.1 = (bf16[1056,384]{1,0:T(8,128)(2,1)S(1)}, bf16[1056,384]{1,0:T(8,128)(2,1)S(1)}, u32[]{:S(2)}, u32[]{:S(2)}) collective-permute-start(bf16[1056,384]{1,0:T(8,128)(2,1)S(1)} %get-tuple-element.37), channel_id=1, source_target_pairs={{0,4},{4,0},{8,12},{12,8},{1,5},{5,1},{9,13},{13,9},{2,6},{6,2},{1... | collective-permute-start | bytes 2433032 | tf_op jit(solution)/shard_map/ppermute | solution.py:731
  2.3 14.7 %collective-permute-start = (bf16[1056,384]{1,0:T(8,128)(2,1)S(1)}, bf16[1056,384]{1,0:T(8,128)(2,1)S(1)}, u32[]{:S(2)}, u32[]{:S(2)}) collective-permute-start(bf16[1056,384]{1,0:T(8,128)(2,1)S(1)} %get-tuple-element.36), channel_id=1, source_target_pairs={{4,8},{8,4},{5,9},{9,5},{6,10},{10,6},{7,11},{11,7},{20,24},{24,20... | collective-permute-start | bytes 2433032 | tf_op jit(solution)/shard_map/ppermute | solution.py:731
  7.9 4.4 %collective-permute-start.2 = (s32[152,128]{1,0:T(8,128)S(1)}, s32[152,128]{1,0:T(8,128)S(1)}, u32[]{:S(2)}, u32[]{:S(2)}) collective-permute-start(s32[152,128]{1,0:T(8,128)S(1)} %get-tuple-element.42), channel_id=1, source_target_pairs={{0,1},{1,0},{2,3},{3,2},{4,5},{5,4},{6,7},{7,6},{8,9},{9,8},{10,11... | collective-permute-start | bytes 233480 | tf_op jit(solution)/shard_map/ppermute | solution.py:722
  9.3 13.4 %collective-permute-start.6 = (s32[152,128]{1,0:T(8,128)S(1)}, s32[152,128]{1,0:T(8,128)S(1)}, u32[]{:S(2)}, u32[]{:S(2)}) collective-permute-start(s32[152,128]{1,0:T(8,128)S(1)} %get-tuple-element.48), channel_id=1, source_target_pairs={{0,3},{1,2},{2,1},{3,0},{4,7},{5,6},{6,5},{7,4},{8,11},{9,10},{10,... | collective-permute-start | bytes 233480 | tf_op jit(solution)/shard_map/ppermute | solution.py:722
  11.4 11.2 %collective-permute-start.7 = (s32[152,128]{1,0:T(8,128)S(1)}, s32[152,128]{1,0:T(8,128)S(1)}, u32[]{:S(2)}, u32[]{:S(2)}) collective-permute-start(s32[152,128]{1,0:T(8,128)S(1)} %get-tuple-element.49), channel_id=1, source_target_pairs={{0,2},{1,3},{2,0},{3,1},{4,6},{5,7},{6,4},{7,5},{8,10},{9,11},{10,... | collective-permute-start | bytes 233480 | tf_op jit(solution)/shard_map/ppermute | solution.py:722
  12.2 10.1 %copy-start = (s32[50,384]{1,0:T(8,128)S(1)}, s32[50,384]{1,0:T(8,128)}, u32[]{:S(2)}) copy-start(s32[50,384]{1,0:T(8,128)} %annot_ref.3) | copy-start | bytes 230404
  17.0 5.7 %copy-start.1 = (s32[4]{0:T(128)S(1)}, s32[4]{0:T(128)}, u32[]{:S(2)}) copy-start(s32[4]{0:T(128)} %reach_ref.3) | copy-start | bytes 52
  18.0 6.2 %collective-permute-start.3 = (s32[152,128]{1,0:T(8,128)S(1)}, s32[152,128]{1,0:T(8,128)S(1)}, u32[]{:S(2)}, u32[]{:S(2)}) collective-permute-start(s32[152,128]{1,0:T(8,128)S(1)} %get-tuple-element.44), channel_id=1, source_target_pairs={{0,2},{1,3},{2,0},{3,1},{4,6},{5,7},{6,4},{7,5},{8,10},{9,11},{10,... | collective-permute-start | bytes 233480 | tf_op jit(solution)/shard_map/ppermute | solution.py:722
  20.7 5.2 %collective-permute-start.4 = (s32[152,128]{1,0:T(8,128)S(1)}, s32[152,128]{1,0:T(8,128)S(1)}, u32[]{:S(2)}, u32[]{:S(2)}) collective-permute-start(s32[152,128]{1,0:T(8,128)S(1)} %get-tuple-element.45), channel_id=1, source_target_pairs={{0,3},{1,2},{2,1},{3,0},{4,7},{5,6},{6,5},{7,4},{8,11},{9,10},{10,... | collective-permute-start | bytes 233480 | tf_op jit(solution)/shard_map/ppermute | solution.py:722
  22.1 4.1 %collective-permute-start.5 = (s32[152,128]{1,0:T(8,128)S(1)}, s32[152,128]{1,0:T(8,128)S(1)}, u32[]{:S(2)}, u32[]{:S(2)}) collective-permute-start(s32[152,128]{1,0:T(8,128)S(1)} %get-tuple-element.46), channel_id=1, source_target_pairs={{0,1},{1,0},{2,3},{3,2},{4,5},{5,4},{6,7},{7,6},{8,9},{9,8},{10,11... | collective-permute-start | bytes 233480 | tf_op jit(solution)/shard_map/ppermute | solution.py:722
  27.3 6.2 %collective-permute-start.8 = (bf16[96,128]{1,0:T(8,128)(2,1)S(1)}, bf16[96,128]{1,0:T(8,128)(2,1)S(1)}, u32[]{:S(2)}, u32[]{:S(2)}) collective-permute-start(bf16[96,128]{1,0:T(8,128)(2,1)S(1)} %get-tuple-element.59), channel_id=1, source_target_pairs={{0,2},{1,3},{2,0},{3,1},{4,6},{5,7},{6,4},{7,5},{8,10},{9,11},{10,... | collective-permute-start | bytes 73736 | tf_op jit(solution)/shard_map/ppermute | solution.py:722
  28.6 6.2 %collective-permute-start.10 = (f32[48,128]{1,0:T(8,128)S(1)}, f32[48,128]{1,0:T(8,128)S(1)}, u32[]{:S(2)}, u32[]{:S(2)}) collective-permute-start(f32[48,128]{1,0:T(8,128)S(1)} %get-tuple-element.62), channel_id=1, source_target_pairs={{0,4},{1,5},{4,8},{5,9},{6,2},{7,3},{8,12},{9,13},{10,6},{11,7},{1... | collective-permute-start | bytes 73736 | tf_op jit(solution)/shard_map/ppermute | solution.py:820
  33.6 2.6 %collective-permute-start.9 = (bf16[48,128]{1,0:T(8,128)(2,1)S(1)}, bf16[48,128]{1,0:T(8,128)(2,1)S(1)}, u32[]{:S(2)}, u32[]{:S(2)}) collective-permute-start(bf16[48,128]{1,0:T(8,128)(2,1)S(1)} %get-tuple-element.61), channel_id=1, source_target_pairs={{0,1},{1,0},{2,3},{3,2},{4,5},{5,4},{6,7},{7,6},{8,9},{9,8},{10,11... | collective-permute-start | bytes 36872 | tf_op jit(solution)/shard_map/ppermute | solution.py:722

commit v15 on v14

--- a/solution.py
+++ b/solution.py
@@ -622,7 +622,7 @@
 def near_score_kernel(groups, share, reach_ref, *refs):
     near_parts, refs = refs[:groups], refs[groups:]
     own_ref, mine_ref, rows_ref, masks_ref, columns_ref, own_rows_ref, annot_ref, near_annot_ref = refs[:8]
-    keep_ref, send_ref, near_out_ref, flipped, scores = refs[8:]
+    out_ref, *targets, near_out_ref, flipped, scores = refs[8:]
     snps = annot_ref.shape[0]
     wide = snps // groups
     size = wide // 2
@@ -676,26 +676,20 @@
         far_product *= correlation(own_row, near_row, near_row[3])
     scores[slice_rows, :] += near_annot_ref[slice_rows, :] * jnp.where(reach_here >= snps, far_product, 0.0)
     far_scores = annot_ref[slice_rows, :] * jnp.where(reach_there >= snps, far_product, 0.0)
-    near_out_ref[...] = near_scores + pack_halves(far_scores)
+    near_out_ref[...] = (near_scores + pack_halves(far_scores)).astype(near_out_ref.dtype)
 
     def packed(step):
         group = partner(me, step, groups)
         return pack_halves(scores[pl.ds(pl.multiple_of(group * wide, 8), wide), :])
 
-    for ref, steps in ((keep_ref, (0, 1)), (send_ref, (2, 3))):
-        for number, step in enumerate(steps):
-            ref[number * size : (number + 1) * size, :] = packed(step).astype(ref.dtype)
-
-
-def middle_kernel(keep_ref, part_ref, mine_ref, send_ref):
-    total = keep_ref[...] + part_ref[...].astype(jnp.float32)
-    half = mine_ref.shape[0]
-    mine_ref[...] = total[0:half]
-    send_ref[...] = total[half:].astype(send_ref.dtype)
-
-
-def column_finish_kernel(mine_ref, part_ref, there_ref, out_ref):
-    packed = mine_ref[...] + part_ref[...].astype(jnp.float32) + there_ref[...]
+    out_ref[...] = packed(0)
+    for step, target in enumerate(targets, 1):
+        target[...] = packed(step).astype(target.dtype)
+
+
+def column_finish_kernel(*refs):
+    *parts, out_ref = refs
+    packed = sum(part[...].astype(jnp.float32) for part in parts)
     out_ref[...] = unpack_halves(packed).T[0 : out_ref.shape[0], :]
 
 
@@ -840,22 +834,20 @@
             flops=1 << 25,
             moved=1 << 20,
         )(reach, own_sum, *own_parts[1:-1], own_annots, near_annots)
-        both = (2 * half_share, LANES)
-        keep, send, near_scores = call(
+        sent = shape((half_share, LANES), bf16)
+        own_scores, *scores = call(
             functools.partial(near_score_kernel, groups, share),
-            [shape(both, f32), shape(both, bf16), packed_share],
+            [packed_share] + [sent] * groups,
             [SMEM] + [VMEM] * (groups + 8),
             [pltpu.VMEM((LANES, LANES), i32), pltpu.VMEM((snps, LANES), f32)],
             flops=1 << 26,
             moved=1 << 21,
         )(reach, *near_parts, *prepared, own_annots, near_annots)
-        part = around(send, groups, 2)
-        there = to_neighbour(near_scores)
-        mine, send = call(
-            middle_kernel, [packed_share, shape((half_share, LANES), bf16)], [VMEM] * 2
-        )(keep, part)
-        part = around(send, groups, 1)
-        return call(column_finish_kernel, result, [VMEM] * 3)(mine, part, there)
+        *scores, there = scores
+        scores = [around(scores[k - 1], groups, k) for k in order]
+        return call(column_finish_kernel, result, [VMEM] * (groups + 1))(
+            own_scores, *scores, to_neighbour(there)
+        )
 
     tall = pltpu.VMEM((padded, LANES), f32)
     scores = call(

time: 37.1 us -> 37.1 us (level)
  starting transfers between devices: 19.9 us -> 20.6 us
  waiting for transfers between devices: 8.08 us -> 7.42 us
    ppermute x8 -> x9, waiting for transfers between devices: 3.37 us -> 1.93 us  [around(): lax.ppermute(value, 'hap', [(source, partner(source, step, groups)) for s...]
    ppermute x1, waiting for transfers between devices: 0.01 us -> 0.78 us  [to_neighbour(): return lax.ppermute(value, ('snp', 'hap'), pairs)]
    ppermute x8 -> x9, starting transfers between devices: 10.4 us -> 10.7 us  [around(): lax.ppermute(value, 'hap', [(source, partner(source, step, groups)) for s...]
    pallas_call x3 -> x2, Pallas kernels: 1.89 us -> 1.89 us  [the longest x1 1.14 us: per_device(): call(functools.partial(near_score_kernel, groups, share), [packed_share]...]
  transfers between devices with their start and end apart: 11 -> 12, of which waited for: 4 -> 4; matrix products, arithmetic and copies ran while one was open for 0% -> 0% of each run, Pallas kernels for 13% -> 13%
where the time goes in v15:
time: 37.1 us; the launch traced here: 36.9 us
  starting transfers between devices  20.6 us (56%)
  Pallas kernels  8.78 us (24%)
  waiting for transfers between devices  7.42 us (20%)
    ppermute x9, starting transfers between devices, around(): lax.ppermute(value, 'hap', [(source, partner(source, step, groups)) for s...  10.7 us
    ppermute x1, starting transfers between devices, to_neighbour(): return lax.ppermute(value, ('snp', 'hap'), pairs)  5.29 us
    ppermute x2, waiting for transfers between devices, swapped(): return lax.ppermute(value, 'snp', pairs)  4.71 us
    ppermute x2, starting transfers between devices, swapped(): return lax.ppermute(value, 'snp', pairs)  4.59 us
    pallas_call x1, Pallas kernels, per_device(): call(prepare_kernel, [shape((rows, snps), bf16), packed, packed], [HBM, H...  2.14 us
    ppermute x9, waiting for transfers between devices, around(): lax.ppermute(value, 'hap', [(source, partner(source, step, groups)) for s...  1.93 us
    pallas_call x1, Pallas kernels, per_device(): call(functools.partial(own_score_kernel, groups, share), [by_snp, shape((...  1.62 us
    pallas_call x1, Pallas kernels, per_device(): call(functools.partial(near_score_kernel, groups, share), [packed_share]...  1.14 us
  transfers between devices with their start and end apart: 12, of which 4 were waited for; matrix products, arithmetic and copies ran while one was open for 0% of the time, Pallas kernels for 13%

profile of v15, /device:TPU:1, one launch (start us, length us, event | category | flops | bytes accessed | tf_op | source)
XLA Modules:
  0.0 36.9 jit_solution(16544448982561266074)
XLA Ops:
  0.0 0.0 copy-start.2
  0.0 2.1 %shard_map.46 = (bf16[2048,384]{1,0:T(8,128)(2,1)S(1)}, bf16[1056,384]{1,0:T(8,128)(2,1)S(1)}, bf16[1056,384]{1,0:T(8,128)(2,1)S(1)}) custom-call(s32[2048,384]{1,0:T(8,128)} %hap_ref.1, s32[50,384]{1,0:T(8,128)} %annot_ref.3), custom_call_target="tpu_custom_call" | custom-call | bytes 6291456 | tf_op jit(solution)/shard_map/pallas_call | solution.py:744
  2.1 0.1 collective-permute-start.1
  2.3 4.5 %collective-permute-start = (bf16[1056,384]{1,0:T(8,128)(2,1)S(1)}, bf16[1056,384]{1,0:T(8,128)(2,1)S(1)}, u32[]{:S(2)}, u32[]{:S(2)}) collective-permute-start(bf16[1056,384]{1,0:T(8,128)(2,1)S(1)} %get-tuple-element.36), channel_id=1, source_target_pairs={{4,8},{8,4},{5,9},{9,5},{6,10},{10,6},{7,11},{11,7},{20,24},{24,20... | collective-permute-start | bytes 2433032 | tf_op jit(solution)/shard_map/ppermute | solution.py:725
  6.7 0.0 copy-done.2
  6.8 1.1 %shard_map.47 = (bf16[400,2048]{1,0:T(8,128)(2,1)S(1)}, f32[8,384]{1,0:T(8,128)S(1)}, s32[152,128]{1,0:T(8,128)S(1)}, s32[152,128]{1,0:T(8,128)S(1)}, s32[152,128]{1,0:T(8,128)S(1)}, /*index=5*/s32[152,128]{1,0:T(8,128)S(1)}) custom-call(bf16[2048,384]{1,0:T(8,128)(2,1)S(1)} %get-tuple-element.34.alleles_ref, s32[1,2048]{1,0:T(1,128)S(1)} %bitcast.1), custom_call_target="tpu_custom_call" | custom-call | flops 603979776 | bytes 3145728 | tf_op jit(solution)/shard_map/pallas_call | solution.py:763
  7.9 1.4 %collective-permute-start.2 = (s32[152,128]{1,0:T(8,128)S(1)}, s32[152,128]{1,0:T(8,128)S(1)}, u32[]{:S(2)}, u32[]{:S(2)}) collective-permute-start(s32[152,128]{1,0:T(8,128)S(1)} %get-tuple-element.42), channel_id=1, source_target_pairs={{0,1},{1,0},{2,3},{3,2},{4,5},{5,4},{6,7},{7,6},{8,9},{9,8},{10,11... | collective-permute-start | bytes 233480 | tf_op jit(solution)/shard_map/ppermute | solution.py:716
  9.3 2.2 %collective-permute-start.6 = (s32[152,128]{1,0:T(8,128)S(1)}, s32[152,128]{1,0:T(8,128)S(1)}, u32[]{:S(2)}, u32[]{:S(2)}) collective-permute-start(s32[152,128]{1,0:T(8,128)S(1)} %get-tuple-element.48), channel_id=1, source_target_pairs={{0,3},{1,2},{2,1},{3,0},{4,7},{5,6},{6,5},{7,4},{8,11},{9,10},{10,... | collective-permute-start | bytes 233480 | tf_op jit(solution)/shard_map/ppermute | solution.py:716
  11.4 0.1 collective-permute-start.7
  11.6 0.0 collective-permute-done.1.side_ref
  11.6 0.7 %shard_map.48 = (f32[400,128]{1,0:T(8,128)S(1)}, f32[400,128]{1,0:T(8,128)S(1)}) custom-call(bf16[400,2048]{1,0:T(8,128)(2,1)S(1)} %get-tuple-element.35.weighted_ref, bf16[1056,384]{1,0:T(8,128)(2,1)S(1)} %collective-permute-done.1.side_ref), custom_call_target="tpu_custom_call" | custom-call | flops 402653184 | bytes 3145728 | tf_op jit(solution)/shard_map/pallas_call | solution.py:777
  12.2 0.0 copy-start
  12.2 0.0 collective-permute-done.2.nearest_ref
  12.3 4.7 %collective-permute-done.side_ref = bf16[1056,384]{1,0:T(8,128)(2,1)S(1)} collective-permute-done((bf16[1056,384]{1,0:T(8,128)(2,1)S(1)}, bf16[1056,384]{1,0:T(8,128)(2,1)S(1)}, u32[]{:S(2)}, u32[]{:S(2)}) %collective-permute-start) | collective-permute-done | bytes 811040 | tf_op jit(solution)/shard_map/ppermute | solution.py:725
  17.0 0.0 copy-start.1
  17.0 1.1 %shard_map.49 = (s32[152,128]{1,0:T(8,128)S(1)}, s32[152,128]{1,0:T(8,128)S(1)}, s32[152,128]{1,0:T(8,128)S(1)}, s32[152,128]{1,0:T(8,128)S(1)}, s32[152,128]{1,0:T(8,128)S(1)}) custom-call(bf16[400,2048]{1,0:T(8,128)(2,1)S(1)} %get-tuple-element.35.weighted_ref, bf16[1056,384]{1,0:T(8,128)(2,1)S(1)} %collective-permute-done.side_ref, ...), custom_call_target="tpu_custom_call" | custom-call | flops 402653184 | bytes 3145728 | tf_op jit(solution)/shard_map/pallas_call | solution.py:778
  18.0 2.7 %collective-permute-start.3 = (s32[152,128]{1,0:T(8,128)S(1)}, s32[152,128]{1,0:T(8,128)S(1)}, u32[]{:S(2)}, u32[]{:S(2)}) collective-permute-start(s32[152,128]{1,0:T(8,128)S(1)} %get-tuple-element.44), channel_id=1, source_target_pairs={{0,2},{1,3},{2,0},{3,1},{4,6},{5,7},{6,4},{7,5},{8,10},{9,11},{10,... | collective-permute-start | bytes 233480 | tf_op jit(solution)/shard_map/ppermute | solution.py:716
  20.7 1.4 %collective-permute-start.4 = (s32[152,128]{1,0:T(8,128)S(1)}, s32[152,128]{1,0:T(8,128)S(1)}, u32[]{:S(2)}, u32[]{:S(2)}) collective-permute-start(s32[152,128]{1,0:T(8,128)S(1)} %get-tuple-element.45), channel_id=1, source_target_pairs={{0,3},{1,2},{2,1},{3,0},{4,7},{5,6},{6,5},{7,4},{8,11},{9,10},{10,... | collective-permute-start | bytes 233480 | tf_op jit(solution)/shard_map/ppermute | solution.py:716
  22.1 0.2 collective-permute-start.5
  22.3 0.0 copy-done
  22.3 0.3 shard_map.50
  22.6 0.0 collective-permute-done.6.refs_1_
  22.6 0.0 collective-permute-done.7.refs_2_
  22.6 0.0 copy-done.1
  22.7 1.6 %shard_map.51 = (f32[384,128]{1,0:T(8,128)S(1)}, f32[96,128]{1,0:T(8,128)S(1)}, f32[6,240,128]{2,1,0:T(8,128)S(1)}, f32[2,240,128]{2,1,0:T(8,128)S(1)}, bf16[128...) custom-call(s32[4]{0:T(128)S(1)} %copy-done.1, s32[152,128]{1,0:T(8,128)S(1)} %get-tuple-element.47.refs_0_, ...), custom_call_target="tpu_custom_call" | custom-call | flops 33554432 | bytes 1048576 | tf_op jit(solution)/shard_map/pallas_call | solution.py:822
  24.3 0.0 collective-permute-done.3.refs_1_
  24.3 1.6 %collective-permute-done.4.refs_2_ = s32[152,128]{1,0:T(8,128)S(1)} collective-permute-done((s32[152,128]{1,0:T(8,128)S(1)}, s32[152,128]{1,0:T(8,128)S(1)}, u32[]{:S(2)}, u32[]{:S(2)}) %collective-permute-start.4) | collective-permute-done | bytes 77856 | tf_op jit(solution)/shard_map/ppermute | solution.py:716
  25.9 0.3 collective-permute-done.5.refs_3_
  26.2 1.1 %shard_map.52 = (f32[48,128]{1,0:T(8,128)S(1)}, bf16[48,128]{1,0:T(8,128)(2,1)S(1)}, bf16[48,128]{1,0:T(8,128)(2,1)S(1)}, bf16[48,128]{1,0:T(8,128)(2,1)S(1)}, bf16[48,128]{1,0:T(8,128)(2,1)S(1)}) custom-call(s32[4]{0:T(128)S(1)} %copy-done.1, s32[152,128]{1,0:T(8,128)S(1)} %get-tuple-element.43.refs_0_, s32[152,128]{1,0:T(8,128)S(1)} %collective-permute-done.3.refs_1_, ...), custom_call_target="tpu_custom_call" | custom-call | flops 67108864 | bytes 2097152 | tf_op jit(solution)/shard_map/pallas_call | solution.py:838
  27.3 1.2 %collective-permute-start.8 = (bf16[48,128]{1,0:T(8,128)(2,1)S(1)}, bf16[48,128]{1,0:T(8,128)(2,1)S(1)}, u32[]{:S(2)}, u32[]{:S(2)}) collective-permute-start(bf16[48,128]{1,0:T(8,128)(2,1)S(1)} %get-tuple-element.59), channel_id=1, source_target_pairs={{0,2},{1,3},{2,0},{3,1},{4,6},{5,7},{6,4},{7,5},{8,10},{9,11},{10,... | collective-permute-start | bytes 36872 | tf_op jit(solution)/shard_map/ppermute | solution.py:716
  28.6 1.1 %collective-permute-start.9 = (bf16[48,128]{1,0:T(8,128)(2,1)S(1)}, bf16[48,128]{1,0:T(8,128)(2,1)S(1)}, u32[]{:S(2)}, u32[]{:S(2)}) collective-permute-start(bf16[48,128]{1,0:T(8,128)(2,1)S(1)} %get-tuple-element.60), channel_id=1, source_target_pairs={{0,3},{1,2},{2,1},{3,0},{4,7},{5,6},{6,5},{7,4},{8,11},{9,10},{10,... | collective-permute-start | bytes 36872 | tf_op jit(solution)/shard_map/ppermute | solution.py:716
  29.7 0.4 collective-permute-start.10
  30.1 5.3 %collective-permute-start.11 = (bf16[48,128]{1,0:T(8,128)(2,1)S(1)}, bf16[48,128]{1,0:T(8,128)(2,1)S(1)}, u32[]{:S(2)}, u32[]{:S(2)}) collective-permute-start(bf16[48,128]{1,0:T(8,128)(2,1)S(1)} %get-tuple-element.62), channel_id=1, source_target_pairs={{0,4},{1,5},{4,8},{5,9},{6,2},{7,3},{8,12},{9,13},{10,6},{11,7},{1... | collective-permute-start | bytes 36872 | tf_op jit(solution)/shard_map/ppermute | solution.py:814
  35.4 0.0 collective-permute-done.8.refs_1_
  35.4 0.0 collective-permute-done.9.refs_2_
  35.4 0.0 collective-permute-done.10.refs_3_
  35.4 0.8 %collective-permute-done.11.refs_4_ = bf16[48,128]{1,0:T(8,128)(2,1)S(1)} collective-permute-done((bf16[48,128]{1,0:T(8,128)(2,1)S(1)}, bf16[48,128]{1,0:T(8,128)(2,1)S(1)}, u32[]{:S(2)}, u32[]{:S(2)}) %collective-permute-start.11) | collective-permute-done | bytes 12320 | tf_op jit(solution)/shard_map/ppermute | solution.py:814
  36.2 0.7 %shard_map.53 = f32[50,96]{1,0:T(8,128)} custom-call(f32[48,128]{1,0:T(8,128)S(1)} %get-tuple-element.58.refs_0_, bf16[48,128]{1,0:T(8,128)(2,1)S(1)} %collective-permute-done.8.refs_1_, bf16[48,128]{1,0:T(8,128)(2,1)S(1)} %collective-permute-done.9.refs_2_, bf16[48,128]{1,0:T(8,128)(2,1)S(1)} %collective-permute-done.10.refs_3_, ...), custom_call_target="tpu_custom_call" | custom-call | tf_op jit(solution)/shard_map/pallas_call | solution.py:848
  (2 shorter events, 0.0 us)
Async XLA Ops:
  0.0 6.7 %copy-start.2 = (s32[2048]{0:T(1024)S(1)}, s32[2048]{0:T(1024)}, u32[]{:S(2)}) copy-start(s32[2048]{0:T(1024)} %param.5) | copy-start | bytes 24580
  2.1 9.4 %collective-permute-start.1 = (bf16[1056,384]{1,0:T(8,128)(2,1)S(1)}, bf16[1056,384]{1,0:T(8,128)(2,1)S(1)}, u32[]{:S(2)}, u32[]{:S(2)}) collective-permute-start(bf16[1056,384]{1,0:T(8,128)(2,1)S(1)} %get-tuple-element.37), channel_id=1, source_target_pairs={{0,4},{4,0},{8,12},{12,8},{1,5},{5,1},{9,13},{13,9},{2,6},{6,2},{1... | collective-permute-start | bytes 2433032 | tf_op jit(solution)/shard_map/ppermute | solution.py:725
  2.3 14.7 %collective-permute-start = (bf16[1056,384]{1,0:T(8,128)(2,1)S(1)}, bf16[1056,384]{1,0:T(8,128)(2,1)S(1)}, u32[]{:S(2)}, u32[]{:S(2)}) collective-permute-start(bf16[1056,384]{1,0:T(8,128)(2,1)S(1)} %get-tuple-element.36), channel_id=1, source_target_pairs={{4,8},{8,4},{5,9},{9,5},{6,10},{10,6},{7,11},{11,7},{20,24},{24,20... | collective-permute-start | bytes 2433032 | tf_op jit(solution)/shard_map/ppermute | solution.py:725
  7.9 4.4 %collective-permute-start.2 = (s32[152,128]{1,0:T(8,128)S(1)}, s32[152,128]{1,0:T(8,128)S(1)}, u32[]{:S(2)}, u32[]{:S(2)}) collective-permute-start(s32[152,128]{1,0:T(8,128)S(1)} %get-tuple-element.42), channel_id=1, source_target_pairs={{0,1},{1,0},{2,3},{3,2},{4,5},{5,4},{6,7},{7,6},{8,9},{9,8},{10,11... | collective-permute-start | bytes 233480 | tf_op jit(solution)/shard_map/ppermute | solution.py:716
  9.3 13.4 %collective-permute-start.6 = (s32[152,128]{1,0:T(8,128)S(1)}, s32[152,128]{1,0:T(8,128)S(1)}, u32[]{:S(2)}, u32[]{:S(2)}) collective-permute-start(s32[152,128]{1,0:T(8,128)S(1)} %get-tuple-element.48), channel_id=1, source_target_pairs={{0,3},{1,2},{2,1},{3,0},{4,7},{5,6},{6,5},{7,4},{8,11},{9,10},{10,... | collective-permute-start | bytes 233480 | tf_op jit(solution)/shard_map/ppermute | solution.py:716
  11.4 11.2 %collective-permute-start.7 = (s32[152,128]{1,0:T(8,128)S(1)}, s32[152,128]{1,0:T(8,128)S(1)}, u32[]{:S(2)}, u32[]{:S(2)}) collective-permute-start(s32[152,128]{1,0:T(8,128)S(1)} %get-tuple-element.49), channel_id=1, source_target_pairs={{0,2},{1,3},{2,0},{3,1},{4,6},{5,7},{6,4},{7,5},{8,10},{9,11},{10,... | collective-permute-start | bytes 233480 | tf_op jit(solution)/shard_map/ppermute | solution.py:716
  12.2 10.1 %copy-start = (s32[50,384]{1,0:T(8,128)S(1)}, s32[50,384]{1,0:T(8,128)}, u32[]{:S(2)}) copy-start(s32[50,384]{1,0:T(8,128)} %annot_ref.3) | copy-start | bytes 230404
  17.0 5.7 %copy-start.1 = (s32[4]{0:T(128)S(1)}, s32[4]{0:T(128)}, u32[]{:S(2)}) copy-start(s32[4]{0:T(128)} %reach_ref.3) | copy-start | bytes 52
  18.0 6.2 %collective-permute-start.3 = (s32[152,128]{1,0:T(8,128)S(1)}, s32[152,128]{1,0:T(8,128)S(1)}, u32[]{:S(2)}, u32[]{:S(2)}) collective-permute-start(s32[152,128]{1,0:T(8,128)S(1)} %get-tuple-element.44), channel_id=1, source_target_pairs={{0,2},{1,3},{2,0},{3,1},{4,6},{5,7},{6,4},{7,5},{8,10},{9,11},{10,... | collective-permute-start | bytes 233480 | tf_op jit(solution)/shard_map/ppermute | solution.py:716
  20.7 5.2 %collective-permute-start.4 = (s32[152,128]{1,0:T(8,128)S(1)}, s32[152,128]{1,0:T(8,128)S(1)}, u32[]{:S(2)}, u32[]{:S(2)}) collective-permute-start(s32[152,128]{1,0:T(8,128)S(1)} %get-tuple-element.45), channel_id=1, source_target_pairs={{0,3},{1,2},{2,1},{3,0},{4,7},{5,6},{6,5},{7,4},{8,11},{9,10},{10,... | collective-permute-start | bytes 233480 | tf_op jit(solution)/shard_map/ppermute | solution.py:716
  22.1 4.1 %collective-permute-start.5 = (s32[152,128]{1,0:T(8,128)S(1)}, s32[152,128]{1,0:T(8,128)S(1)}, u32[]{:S(2)}, u32[]{:S(2)}) collective-permute-start(s32[152,128]{1,0:T(8,128)S(1)} %get-tuple-element.46), channel_id=1, source_target_pairs={{0,1},{1,0},{2,3},{3,2},{4,5},{5,4},{6,7},{7,6},{8,9},{9,8},{10,11... | collective-permute-start | bytes 233480 | tf_op jit(solution)/shard_map/ppermute | solution.py:716
  27.3 8.0 %collective-permute-start.8 = (bf16[48,128]{1,0:T(8,128)(2,1)S(1)}, bf16[48,128]{1,0:T(8,128)(2,1)S(1)}, u32[]{:S(2)}, u32[]{:S(2)}) collective-permute-start(bf16[48,128]{1,0:T(8,128)(2,1)S(1)} %get-tuple-element.59), channel_id=1, source_target_pairs={{0,2},{1,3},{2,0},{3,1},{4,6},{5,7},{6,4},{7,5},{8,10},{9,11},{10,... | collective-permute-start | bytes 36872 | tf_op jit(solution)/shard_map/ppermute | solution.py:716
  28.6 6.8 %collective-permute-start.9 = (bf16[48,128]{1,0:T(8,128)(2,1)S(1)}, bf16[48,128]{1,0:T(8,128)(2,1)S(1)}, u32[]{:S(2)}, u32[]{:S(2)}) collective-permute-start(bf16[48,128]{1,0:T(8,128)(2,1)S(1)} %get-tuple-element.60), channel_id=1, source_target_pairs={{0,3},{1,2},{2,1},{3,0},{4,7},{5,6},{6,5},{7,4},{8,11},{9,10},{10,... | collective-permute-start | bytes 36872 | tf_op jit(solution)/shard_map/ppermute | solution.py:716
  29.7 5.7 %collective-permute-start.10 = (bf16[48,128]{1,0:T(8,128)(2,1)S(1)}, bf16[48,128]{1,0:T(8,128)(2,1)S(1)}, u32[]{:S(2)}, u32[]{:S(2)}) collective-permute-start(bf16[48,128]{1,0:T(8,128)(2,1)S(1)} %get-tuple-element.61), channel_id=1, source_target_pairs={{0,1},{1,0},{2,3},{3,2},{4,5},{5,4},{6,7},{7,6},{8,9},{9,8},{10,11... | collective-permute-start | bytes 36872 | tf_op jit(solution)/shard_map/ppermute | solution.py:716
  30.1 6.1 %collective-permute-start.11 = (bf16[48,128]{1,0:T(8,128)(2,1)S(1)}, bf16[48,128]{1,0:T(8,128)(2,1)S(1)}, u32[]{:S(2)}, u32[]{:S(2)}) collective-permute-start(bf16[48,128]{1,0:T(8,128)(2,1)S(1)} %get-tuple-element.62), channel_id=1, source_target_pairs={{0,4},{1,5},{4,8},{5,9},{6,2},{7,3},{8,12},{9,13},{10,6},{11,7},{1... | collective-permute-start | bytes 36872 | tf_op jit(solution)/shard_map/ppermute | solution.py:814

commit v16 on v15

--- a/solution.py
+++ b/solution.py
@@ -170,26 +170,87 @@
     totals_ref[...] = jnp.concatenate(
         [tile[snps : snps + 1, :], jnp.broadcast_to(count, (1, snps)), jnp.zeros((6, snps))], axis=0
     )
+    if groups == len(LEFT_BLOCKS):
+        fold_halves(tile, folded)
+        shared = [totals_ref[0:1, k * LANES : (k + 1) * LANES] for k in range(snps // LANES)]
+        shared += [totals_ref[1:2, 0:LANES], jnp.zeros((7 - len(shared), LANES))]
+        extras = to_fields(jnp.concatenate(shared, axis=0))
+        me = lax.axis_index("hap")
+        count = folded.shape[0] // groups
+        for step, target in enumerate(targets):
+            start = partner(me, step, groups) * count
+            done = 0
+            for first, size in ((0, share), (share, share // 2)):
+                counts = folded[pl.ds(pl.multiple_of(start + first, 8), size), :]
+                for k in range(snps // LANES):
+                    target[done : done + size, :] = counts[:, k * LANES : (k + 1) * LANES]
+                    done += size
+            target[done:, :] = extras
+        return
     row, col = iota((half, snps), 0), iota((half, snps), 1)
     moved = (col < half) | (col - half > row)
     turned = pltpu.roll(tile[0:half, :], half, 1)
     folded[0:half, :] = to_fields(jnp.where(moved, turned, tile[half:snps, :]))
     if folded.shape[0] > half:
         folded[half:, :] = jnp.zeros((folded.shape[0] - half, snps), jnp.int32)
-    if groups != len(LEFT_BLOCKS):
-        send_shares(groups, folded, share, targets)
-        return
-    tiles = snps // LANES
-    shared = [totals_ref[0:1, k * LANES : (k + 1) * LANES] for k in range(tiles)]
-    shared += [totals_ref[1:2, 0:LANES], jnp.zeros((7 - tiles, LANES))]
-    extras = to_fields(jnp.concatenate(shared, axis=0))
-    send_tiles(groups, folded, share, targets)
-    for target in targets:
-        target[tiles * share :, :] = extras
+    send_shares(groups, folded, share, targets)
+
+
+def fold_halves(tile, folded):
+    snps = tile.shape[1]
+    half, wide = snps // 2, snps // 4
+    size, count = wide // 2, folded.shape[0] // 4
+    top, bottom = tile[0:half, :], tile[half:snps, :]
+    top_turned, bottom_turned = pltpu.roll(top, half, 1), pltpu.roll(bottom, half, 1)
+    row, lane = iota((wide, snps), 0), iota((wide, snps), 1)
+    for side, square in enumerate((top, bottom_turned)):
+        first = square[0:wide]
+        within = jnp.where(
+            lane < wide,
+            pltpu.roll(first, snps - wide, 1),
+            jnp.where(lane - wide > row, pltpu.roll(first, wide, 1), square[wide:]),
+        )
+        for part in range(2):
+            start = (2 * side + part) * count
+            rows = part * wide
+            between = jnp.where(
+                lane[0:size] < half, top_turned[rows : rows + size], top[rows + size : rows + wide]
+            )
+            folded[start : start + size, :] = to_fields(between)
+            rows = within[part * size : (part + 1) * size]
+            rows = jnp.where(
+                lane[0 : size // 2] < half, rows[0 : size // 2], pltpu.roll(rows[size // 2 :], half, 1)
+            )
+            folded[start + size : start + count, :] = to_fields(rows)
 
 
 LEFT_BLOCKS = ((0, 1, 2, 3), (2, 3, 6, 7), (4, 0, 1, 2), (6, 0, 4, 5))
 RIGHT_BLOCKS = ((2, 3, 6, 7), (4, 5, 6, 7), (0, 1, 2, 4), (0, 4, 5, 6))
+
+
+SPARE_OWN = ((0, 0, 0, 0), (1, 1, 2, 2), (4, 5, 6, 7), (6, 6, 7, 7))
+SPARE_NEAR = ((4, 5, 6, 7), (4, 5, 4, 5), (3, 3, 3, 3), (1, 2, 1, 2))
+
+
+def fold_spare(tile, spare):
+    owners = len(SPARE_OWN)
+    snps = tile.shape[1]
+    size = snps // (2 * owners)
+    count = spare.shape[0] // owners
+    totals = tile[snps : snps + count - size, :]
+    lane = iota((count, snps), 1)
+    for owner in range(owners):
+        mixed = None
+        for slot in range(owners):
+            own, near = SPARE_OWN[owner][slot], SPARE_NEAR[owner][slot]
+            before = (SPARE_OWN[owner][slot - 1], SPARE_NEAR[owner][slot - 1] + 1) if slot else None
+            if before == (own, near):
+                continue
+            values = jnp.concatenate([tile[own * size : (own + 1) * size, :], totals], axis=0)
+            shift = (slot - near) * size % snps
+            values = pltpu.roll(values, shift, 1) if shift else values
+            mixed = values if mixed is None else jnp.where(lane >= slot * size, values, mixed)
+        spare[owner * count : (owner + 1) * count, :] = to_fields(mixed[:, 0 : spare.shape[1]])
 
 
 def fold_by_column(tile, flipped, folded):
@@ -261,7 +322,7 @@
 def far_kernel(
     groups, share, weighted_ref, side_ref, whole_ref, shared_ref, totals_ref, mine_ref, nearest_ref, own_sum_ref, *refs
 ):
-    targets, (tile, folded, flipped, extras) = refs[:groups], refs[groups:]
+    targets, (tile, folded, flipped, spare, extras) = refs[:groups], refs[groups:]
     snps = tile.shape[1]
     own_sum_ref[...] = mine_ref[...] + nearest_ref[...]
     whole, shared = side_dot(weighted_ref, side_ref)
@@ -284,18 +345,38 @@
     apart = jnp.sum(
         jnp.where(iota(square, 0) == iota(square, 1), tile[0:snps, :], 0.0), axis=0, keepdims=True
     )
+    fold_spare(tile, spare)
     tiles = snps // LANES
+    size = share
+    count = spare.shape[0] // groups
     sizes = totals_ref[1:2, :]
     by_column = jnp.concatenate([sizes, tile[snps : snps + 1, :], apart, jnp.zeros((5, snps))], axis=0)
     for owner in range(groups):
         start = owner * (snps // groups)
         columns = pltpu.roll(by_column, snps - start, 1) if owner else by_column
-        extras[8 * owner : 8 * (owner + 1), :] = to_fields(columns[:, 0:LANES])
+        spare_totals = spare[owner * count + size : owner * count + size + 1, :]
+        extras[8 * owner : 8 * (owner + 1), :] = jnp.concatenate(
+            [
+                to_fields(columns[0:3, 0:LANES]),
+                spare_totals[:, 0:LANES],
+                spare_totals[:, LANES:],
+                jnp.zeros((3, LANES), jnp.int32),
+            ],
+            axis=0,
+        )
     me = lax.axis_index("hap")
     send_tiles(groups, folded, share, targets)
+    left = iota((size // 2, LANES), 1) < HALF_LANES
     for step, target in enumerate(targets):
         owner = partner(me, step, groups)
-        target[tiles * share :, :] = extras[pl.ds(pl.multiple_of(owner * 8, 8), 8), :]
+        counts = spare[pl.ds(pl.multiple_of(owner * count, 8), size), :]
+        start = tiles * size
+        target[start : start + size, :] = counts[:, 0:LANES]
+        rest = counts[:, LANES:]
+        target[start + size : start + size + size // 2, :] = jnp.where(
+            left, rest[0 : size // 2], pltpu.roll(rest[size // 2 :], HALF_LANES, 1)
+        )
+        target[start + size + size // 2 :, :] = extras[pl.ds(pl.multiple_of(owner * 8, 8), 8), :]
 
 
 def near_kernel(groups, share, weighted_ref, far_ref, close_ref, totals_ref, *refs):
@@ -523,6 +604,18 @@
     return left + left[0:1], right + [(2 * me + 1) * size]
 
 
+def spare_places(groups, size):
+    me = lax.axis_index("hap")
+
+    def mine(blocks, slot):
+        value = blocks[0][slot]
+        for group in range(1, groups):
+            value = jnp.where(me == group, blocks[group][slot], value)
+        return value * size
+
+    return [[mine(blocks, slot) for slot in range(groups)] for blocks in (SPARE_OWN, SPARE_NEAR)]
+
+
 def rows_at(ref, places, size):
     return jnp.concatenate([ref[pl.ds(pl.multiple_of(place, 8), size), :] for place in places], axis=0)
 
@@ -531,7 +624,8 @@
     groups, share, reach_ref, *refs
 ):
     own_parts, refs = refs[: groups - 1], refs[groups - 1 :]
-    annot_ref, near_annot_ref, scores, mine_ref, rows_ref, masks_ref, columns_ref, own_rows_ref, table = refs
+    annot_ref, near_annot_ref, scores, mine_ref, rows_ref, masks_ref, columns_ref, own_rows_ref, *refs = refs
+    spare_rows_ref, spare_mask_ref, spare_columns_ref, table = refs
     snps = annot_ref.shape[0]
     half = snps // 2
     wide = snps // groups
@@ -539,8 +633,11 @@
     me = lax.axis_index("hap")
     reach_here = reach_ref[lax.axis_index("snp")]
     own_sums = sum((part[...] for part in own_parts[1:]), own_parts[0][...])
-    own_counts = from_tiles(own_sums[0 : tiles * share, :], share)
-    extras = from_fields(own_sums[tiles * share :, :])
+    size = wide // 2
+    between = from_tiles(own_sums[0 : tiles * size, :], size)
+    done = tiles * (size + size // 2)
+    within = from_tiles(own_sums[tiles * size : done, :], size // 2)
+    extras = from_fields(own_sums[done:, :])
 
     own_stats, lines = [], []
     for pop in range(2):
@@ -550,31 +647,68 @@
         lines += [*own_stats[pop], totals]
     table[:, 0:8] = jnp.concatenate(lines, axis=0).T
 
-    low_rows = pl.multiple_of(me * share, 8)
-    high_rows = pl.multiple_of(half + me * share, 8)
-
-    def both(ref):
-        return jnp.concatenate([ref[pl.ds(low_rows, share), :], ref[pl.ds(high_rows, share), :]], axis=0)
-
-    here = both(table)
-    own_fields = from_fields(
-        jnp.concatenate([pltpu.roll(own_counts, half, 1), own_counts], axis=0)
-    )
-    shape = (2 * share, snps)
+    upper = me < groups // 2
+    part = me & 1
+    base = jnp.where(upper, 0, half)
+    lanes = 2 * LANES
+    between = jnp.concatenate([between, pltpu.roll(between, half, 1)], axis=0)[:, 0:lanes]
+    within = jnp.concatenate([within, pltpu.roll(within, half, 1)], axis=0)
+    within = jnp.concatenate(
+        [
+            jnp.where(
+                iota(within.shape, 1) >= wide,
+                pltpu.roll(within, wide, 1),
+                pltpu.roll(within, snps - wide, 1),
+            ),
+            within,
+        ],
+        axis=0,
+    )[:, 0:lanes]
+    between_place = pl.multiple_of(part * wide, 8)
+    within_places = [base + part * size, base + wide + part * size]
+    between_table = table[pl.ds(between_place, wide), :]
+    within_table = rows_at(table, within_places, size)
+    between_fields, within_fields = from_fields(between), from_fields(within)
+    between_product, within_product = 1.0, 1.0
+    for pop in range(2):
+        turned = [pltpu.roll(stat, half, 1)[:, 0:lanes] for stat in own_stats[pop]]
+        mine = [jnp.where(upper, stat[:, 0:lanes], other) for stat, other in zip(own_stats[pop], turned)]
+        columns = [slice(4 * pop + k, 4 * pop + k + 1) for k in range(3)]
+        row_stats = [between_table[:, column] for column in columns]
+        between_product *= correlation(row_stats, turned, between_fields[pop])
+        row_stats = [within_table[:, column] for column in columns]
+        within_product *= correlation(row_stats, mine, within_fields[pop])
+    shape = (wide, lanes)
     local, col = iota(shape, 0), iota(shape, 1)
-    low = local < share
-    row = jnp.where(low, local, local + half - share) + me * share
-    product = 1.0
-    for pop in range(2):
-        row_stats = [here[:, 4 * pop + k : 4 * pop + k + 1] for k in range(3)]
-        product *= correlation(row_stats, own_stats[pop], own_fields[pop])
-    inside = (low & (col > row)) | (~low & (col >= half) & (col < row))
-    own_kept = jnp.where(inside & (jnp.abs(col - row) <= reach_here), product, 0.0)
-    rows_here = both(annot_ref).astype(jnp.bfloat16)
-    scores[...] = dot_rounded(own_kept, rows_here, 0)
-    direct = dot_rounded(own_kept, annot_ref[...].astype(jnp.bfloat16), 1)
-    scores[pl.ds(low_rows, share), :] += direct[0:share, :]
-    scores[pl.ds(high_rows, share), :] += direct[share:, :]
+    inside = (col < half) & (half + col - local - part * wide <= reach_here)
+    between_kept = jnp.where(inside, between_product, 0.0)
+    low = local < size
+    row = jnp.where(low, local, local + size) + part * size
+    inside = (low & (col > row)) | (~low & (col >= wide) & (col < row))
+    inside &= (col < half) & (jnp.abs(col - row) <= reach_here)
+    within_kept = jnp.where(inside, within_product, 0.0)
+
+    def half_annots(place):
+        rows = annot_ref[pl.ds(pl.multiple_of(place, 8), half), :]
+        rows = jnp.concatenate([rows, jnp.zeros((lanes - half, LANES), jnp.float32)], axis=0)
+        return rows.astype(jnp.bfloat16)
+
+    scores[...] = jnp.zeros_like(scores)
+    half_rows = pl.ds(pl.multiple_of(base, 8), half)
+    rows = rows_at(annot_ref, within_places, size).astype(jnp.bfloat16)
+    scores[half_rows, :] = dot_rounded(within_kept, rows, 0)[0:half, :]
+    direct = dot_rounded(within_kept, half_annots(base), 1)
+    for number, place in enumerate(within_places):
+        scores[pl.ds(pl.multiple_of(place, 8), size), :] += direct[number * size : (number + 1) * size, :]
+
+    @pl.when(upper)
+    def _():
+        scores[pl.ds(between_place, wide), :] += dot_rounded(between_kept, half_annots(half), 1)
+
+    @pl.when(jnp.logical_not(upper))
+    def _():
+        rows = annot_ref[pl.ds(between_place, wide), :].astype(jnp.bfloat16)
+        scores[half:, :] += dot_rounded(between_kept, rows, 0)[0:half, :]
 
     slice_rows = pl.ds(pl.multiple_of(me * wide, 8), wide)
     mine = table[slice_rows, :]
@@ -584,8 +718,6 @@
         own_row = [mine[:, 4 * pop + k : 4 * pop + k + 1] for k in range(4)]
         product *= correlation(own_row, own_row, own_row[3])
     scores[slice_rows, :] += annot_ref[slice_rows, :] * product
-
-    size = wide // 2
     left_places, right_places = owner_places(groups, size)
     left_table, right_table = rows_at(table, left_places, size), rows_at(table, right_places, size)
     local, lane = iota((size, LANES), 0), iota((size, LANES), 1)
@@ -599,7 +731,6 @@
         for k in range(3):
             column = slice(4 * pop + k, 4 * pop + k + 1)
             rows_ref[3 * pop + k] = jnp.where(is_left, left_table[:, column], right_table[:, column])
-    upper = me < groups // 2
     block = lax.axis_index("snp")
     last = reach_ref.shape[0] - 1
     reach_there = jnp.where(
@@ -608,8 +739,9 @@
     apart = jnp.abs(own_row - (lane + me * wide))
     ahead = (own_row - (lane + me * wide)) * jnp.where(upper, 1, -1) > 0
     real = ahead & (lane < wide) & ((lane >= size) | (iota(shape, 0) < groups * size))
-    for number, limit in enumerate((reach_here, reach_there)):
-        masks_ref[number] = jnp.where(real & (snps - apart <= limit), 1.0, 0.0)
+    inside = (own_row - half) * jnp.where(upper, 1, -1) < jnp.where(upper, 0, 1)
+    masks_ref[0] = jnp.where(real & inside & (snps - apart <= reach_here), 1.0, 0.0)
+    masks_ref[1] = jnp.where(real & (snps - apart <= reach_there), 1.0, 0.0)
     theirs = near_annot_ref[slice_rows, :]
     columns = [theirs[0:size], pltpu.roll(theirs[size:], HALF_LANES, 1), jnp.zeros((LANES - wide, LANES))]
     columns_ref[...] = jnp.concatenate(columns, axis=0).astype(jnp.bfloat16)
@@ -618,11 +750,37 @@
     )
     own_rows_ref[...] = own_rows.astype(jnp.bfloat16)
 
+    own_places, near_places = spare_places(groups, size)
+    shape = (size, spare_mask_ref.shape[1])
+    local, lane = iota(shape, 0), iota(shape, 1)
+
+    def by_slot(values):
+        mixed = values[0]
+        for slot in range(1, groups):
+            mixed = jnp.where(lane >= slot * size, values[slot], mixed)
+        return mixed
+
+    tables = [table[pl.ds(pl.multiple_of(place, 8), size), :] for place in own_places]
+    for pop in range(2):
+        for k in range(3):
+            column = slice(4 * pop + k, 4 * pop + k + 1)
+            spare_rows_ref[3 * pop + k] = by_slot(
+                [jnp.broadcast_to(values[:, column], shape) for values in tables]
+            )
+    own_row = by_slot([local + place for place in own_places])
+    near_col = by_slot([lane + (place - slot * size) for slot, place in enumerate(near_places)])
+    close = snps - jnp.abs(own_row - near_col) <= reach_here
+    spare_mask_ref[...] = jnp.where(close & (lane < groups * size), 1.0, 0.0)
+    columns = [rows_at(near_annot_ref, near_places, size)]
+    columns.append(jnp.zeros((shape[1] - groups * size, LANES), jnp.float32))
+    spare_columns_ref[...] = jnp.concatenate(columns, axis=0).astype(jnp.bfloat16)
+
 
 def near_score_kernel(groups, share, reach_ref, *refs):
     near_parts, refs = refs[:groups], refs[groups:]
-    own_ref, mine_ref, rows_ref, masks_ref, columns_ref, own_rows_ref, annot_ref, near_annot_ref = refs[:8]
-    out_ref, *targets, near_out_ref, flipped, scores = refs[8:]
+    own_ref, mine_ref, rows_ref, masks_ref, columns_ref, own_rows_ref = refs[:6]
+    spare_rows_ref, spare_mask_ref, spare_columns_ref, annot_ref, near_annot_ref = refs[6:11]
+    out_ref, send_ref, near_out_ref, flipped, scores = refs[11:]
     snps = annot_ref.shape[0]
     wide = snps // groups
     size = wide // 2
@@ -638,9 +796,16 @@
     scores[...] = own_ref[...]
     near_sums = sum((part[...] for part in near_parts[1:]), near_parts[0][...])
     near_counts = from_tiles(near_sums[0 : tiles * share, :], share)
-    extras = from_fields(near_sums[tiles * share :, :])
-    near_stats, near_lines = [], []
-    for pop in range(2):
+    start = tiles * share
+    rest = near_sums[start + size : start + size + size // 2, :]
+    rest = jnp.concatenate([rest, pltpu.roll(rest, HALF_LANES, 1)], axis=0)
+    spare_fields = from_fields(jnp.concatenate([near_sums[start : start + size, :], rest], axis=1))
+    extras = from_fields(near_sums[start + size + size // 2 :, :])
+    near_stats, near_lines, spare_stats = [], [], []
+    for pop in range(2):
+        count = extras[pop][0:1, :]
+        totals = jnp.concatenate([extras[pop][3:4, :], extras[pop][4:5, :]], axis=1)
+        spare_stats.append(column_stats(totals, jnp.concatenate([count, count], axis=1)))
         near_stats.append(column_stats(extras[pop][1:2, :], extras[pop][0:1, :]))
         near_lines += [*near_stats[pop], extras[pop][2:3, :]]
     near_table = jnp.concatenate(near_lines, axis=0).T[0:wide, :]
@@ -663,6 +828,19 @@
     for values, places in zip((direct, turned), owner_places(groups, size)):
         for slot, place in enumerate(places):
             scores[pl.ds(pl.multiple_of(place, 8), size), :] += values[slot * size : (slot + 1) * size, :]
+    product = 1.0
+    for pop in range(2):
+        row_stats = [spare_rows_ref[3 * pop + k] for k in range(3)]
+        product *= correlation(row_stats, spare_stats[pop], spare_fields[pop])
+    spare_here = jnp.where(spare_mask_ref[...] > 0.0, product, 0.0)
+    lane = iota(spare_here.shape, 1)
+    spare_here = [
+        jnp.where((lane >= slot * size) & (lane < (slot + 1) * size), spare_here, 0.0)
+        for slot in range(groups)
+    ]
+    direct = dot_rounded(jnp.concatenate(spare_here, axis=0), spare_columns_ref[...], 1)
+    for slot, place in enumerate(spare_places(groups, size)[0]):
+        scores[pl.ds(pl.multiple_of(place, 8), size), :] += direct[slot * size : (slot + 1) * size, :]
     near_scores = dot_rounded(near_there, own_rows_ref[...], 0)
     near_scores = jnp.where(
         iota((size, LANES), 1) < HALF_LANES, near_scores[0:size], near_scores[size:wide]
@@ -683,8 +861,7 @@
         return pack_halves(scores[pl.ds(pl.multiple_of(group * wide, 8), wide), :])
 
     out_ref[...] = packed(0)
-    for step, target in enumerate(targets, 1):
-        target[...] = packed(step).astype(target.dtype)
+    send_ref[...] = packed(1)
 
 
 def column_finish_kernel(*refs):
@@ -756,7 +933,7 @@
     from_close = swapped(close, 0)
 
     by_column = groups == len(LEFT_BLOCKS)
-    compact = shape((share * (snps // LANES) + 8, LANES), i32)
+    compact = shape(((share + share // 2) * (snps // LANES) + 8, LANES), i32)
     own_share_counts = compact if by_column else shape((share, snps), i32)
     tile = pltpu.VMEM((snps + 16, snps), f32)
     folded = pltpu.VMEM((folded_rows, snps), i32)
@@ -764,7 +941,7 @@
         functools.partial(own_kernel, groups, share),
         [shape((snps + 16, rows), bf16), shape((8, snps), f32)] + [own_share_counts] * groups,
         [VMEM, VMEM],
-        [tile, folded],
+        [tile, pltpu.VMEM((groups * (share + share // 2), snps), i32) if by_column else folded],
         flops=2 * rows * snps * snps,
         moved=rows * snps * 4,
     )(alleles, labels.reshape(1, rows))
@@ -783,6 +960,7 @@
                 tile,
                 folded,
                 pltpu.VMEM((snps, LANES), f32),
+                pltpu.VMEM(((share + 8) * groups, 2 * LANES), i32),
                 pltpu.VMEM((8 * groups, LANES), i32),
             ],
             **work,
@@ -828,25 +1006,25 @@
                 shape((2, pair_rows, LANES), f32),
                 shape((LANES, LANES), bf16),
                 shape((pair_rows, LANES), bf16),
+                shape((6, share, 2 * LANES), f32),
+                shape((share, 2 * LANES), f32),
+                shape((2 * LANES, LANES), bf16),
             ],
             [SMEM] + [VMEM] * (groups + 1),
             [pltpu.VMEM((snps, LANES), f32)],
             flops=1 << 25,
             moved=1 << 20,
         )(reach, own_sum, *own_parts[1:-1], own_annots, near_annots)
-        sent = shape((half_share, LANES), bf16)
-        own_scores, *scores = call(
+        own_scores, send, there = call(
             functools.partial(near_score_kernel, groups, share),
-            [packed_share] + [sent] * groups,
-            [SMEM] + [VMEM] * (groups + 8),
+            [packed_share] * 3,
+            [SMEM] + [VMEM] * (groups + 11),
             [pltpu.VMEM((LANES, LANES), i32), pltpu.VMEM((snps, LANES), f32)],
             flops=1 << 26,
             moved=1 << 21,
         )(reach, *near_parts, *prepared, own_annots, near_annots)
-        *scores, there = scores
-        scores = [around(scores[k - 1], groups, k) for k in order]
-        return call(column_finish_kernel, result, [VMEM] * (groups + 1))(
-            own_scores, *scores, to_neighbour(there)
+        return call(column_finish_kernel, result, [VMEM] * 3)(
+            own_scores, around(send, groups, 1), to_neighbour(there)
         )
 
     tall = pltpu.VMEM((padded, LANES), f32)

time: 37.1 us -> 37.5 us (1.011)
  starting transfers between devices: 20.6 us -> 17.5 us
  waiting for transfers between devices: 7.42 us -> 9.97 us
  Pallas kernels: 8.78 us -> 9.76 us
    ppermute x9 -> x7, waiting for transfers between devices: 1.93 us -> 4.58 us  [around(): lax.ppermute(value, 'hap', [(source, partner(source, step, groups)) for s...]
    ppermute x1, starting transfers between devices: 5.29 us -> 3.29 us  [to_neighbour(): return lax.ppermute(value, ('snp', 'hap'), pairs)]
    ppermute x9 -> x7, starting transfers between devices: 10.7 us -> 9.61 us  [around(): lax.ppermute(value, 'hap', [(source, partner(source, step, groups)) for s...]
    pallas_call x1, Pallas kernels: 1.62 us -> 2.09 us  [per_device(): call(functools.partial(own_score_kernel, groups, share), [by_snp, shape((...]
  transfers between devices with their start and end apart: 12 -> 10, of which waited for: 4 -> 5; matrix products, arithmetic and copies ran while one was open for 0% -> 0% of each run, Pallas kernels for 13% -> 15%
where the time goes in v16:
time: 37.5 us; the launch traced here: 37.3 us
  starting transfers between devices  17.5 us (47%)
  waiting for transfers between devices  9.97 us (27%)
  Pallas kernels  9.76 us (26%)
    ppermute x7, starting transfers between devices, around(): lax.ppermute(value, 'hap', [(source, partner(source, step, groups)) for s...  9.61 us
    ppermute x2, starting transfers between devices, swapped(): return lax.ppermute(value, 'snp', pairs)  4.59 us
    ppermute x7, waiting for transfers between devices, around(): lax.ppermute(value, 'hap', [(source, partner(source, step, groups)) for s...  4.58 us
    ppermute x2, waiting for transfers between devices, swapped(): return lax.ppermute(value, 'snp', pairs)  4.47 us
    ppermute x1, starting transfers between devices, to_neighbour(): return lax.ppermute(value, ('snp', 'hap'), pairs)  3.29 us
    pallas_call x1, Pallas kernels, per_device(): call(prepare_kernel, [shape((rows, snps), bf16), packed, packed], [HBM, H...  2.14 us
    pallas_call x1, Pallas kernels, per_device(): call(functools.partial(own_score_kernel, groups, share), [by_snp, shape((...  2.09 us
    pallas_call x1, Pallas kernels, per_device(): call(functools.partial(own_kernel, groups, share), [shape((snps + 16, row...  1.35 us
  transfers between devices with their start and end apart: 10, of which 5 were waited for; matrix products, arithmetic and copies ran while one was open for 0% of the time, Pallas kernels for 15%

profile of v16, /device:TPU:1, one launch (start us, length us, event | category | flops | bytes accessed | tf_op | source)
XLA Modules:
  0.0 37.3 jit_solution(16902123915906351338)
XLA Ops:
  0.0 0.0 copy-start.2
  0.0 2.1 %shard_map.46 = (bf16[2048,384]{1,0:T(8,128)(2,1)S(1)}, bf16[1056,384]{1,0:T(8,128)(2,1)S(1)}, bf16[1056,384]{1,0:T(8,128)(2,1)S(1)}) custom-call(s32[2048,384]{1,0:T(8,128)} %hap_ref.1, s32[50,384]{1,0:T(8,128)} %annot_ref.3), custom_call_target="tpu_custom_call" | custom-call | bytes 6291456 | tf_op jit(solution)/shard_map/pallas_call | solution.py:921
  2.1 0.1 collective-permute-start.1
  2.3 4.5 %collective-permute-start = (bf16[1056,384]{1,0:T(8,128)(2,1)S(1)}, bf16[1056,384]{1,0:T(8,128)(2,1)S(1)}, u32[]{:S(2)}, u32[]{:S(2)}) collective-permute-start(bf16[1056,384]{1,0:T(8,128)(2,1)S(1)} %get-tuple-element.37), channel_id=1, source_target_pairs={{4,8},{8,4},{5,9},{9,5},{6,10},{10,6},{7,11},{11,7},{20,24},{24,20... | collective-permute-start | bytes 2433032 | tf_op jit(solution)/shard_map/ppermute | solution.py:902
  6.7 0.0 copy-done.2
  6.8 1.4 %shard_map.47 = (bf16[400,2048]{1,0:T(8,128)(2,1)S(1)}, f32[8,384]{1,0:T(8,128)S(1)}, s32[224,128]{1,0:T(8,128)S(1)}, s32[224,128]{1,0:T(8,128)S(1)}, s32[224,128]{1,0:T(8,128)S(1)}, /*index=5*/s32[224,128]{1,0:T(8,128)S(1)}) custom-call(bf16[2048,384]{1,0:T(8,128)(2,1)S(1)} %get-tuple-element.35.alleles_ref, s32[1,2048]{1,0:T(1,128)S(1)} %bitcast.1), custom_call_target="tpu_custom_call" | custom-call | flops 603979776 | bytes 3145728 | tf_op jit(solution)/shard_map/pallas_call | solution.py:940
  8.1 1.4 %collective-permute-start.2 = (s32[224,128]{1,0:T(8,128)S(1)}, s32[224,128]{1,0:T(8,128)S(1)}, u32[]{:S(2)}, u32[]{:S(2)}) collective-permute-start(s32[224,128]{1,0:T(8,128)S(1)} %get-tuple-element.43), channel_id=1, source_target_pairs={{0,1},{1,0},{2,3},{3,2},{4,5},{5,4},{6,7},{7,6},{8,9},{9,8},{10,11... | collective-permute-start | bytes 344072 | tf_op jit(solution)/shard_map/ppermute | solution.py:893
  9.5 2.2 %collective-permute-start.6 = (s32[224,128]{1,0:T(8,128)S(1)}, s32[224,128]{1,0:T(8,128)S(1)}, u32[]{:S(2)}, u32[]{:S(2)}) collective-permute-start(s32[224,128]{1,0:T(8,128)S(1)} %get-tuple-element.49), channel_id=1, source_target_pairs={{0,3},{1,2},{2,1},{3,0},{4,7},{5,6},{6,5},{7,4},{8,11},{9,10},{10,... | collective-permute-start | bytes 344072 | tf_op jit(solution)/shard_map/ppermute | solution.py:893
  11.7 0.1 collective-permute-start.7
  11.8 0.0 collective-permute-done.1.side_ref
  11.8 0.7 %shard_map.48 = (f32[400,128]{1,0:T(8,128)S(1)}, f32[400,128]{1,0:T(8,128)S(1)}) custom-call(bf16[400,2048]{1,0:T(8,128)(2,1)S(1)} %get-tuple-element.36.weighted_ref, bf16[1056,384]{1,0:T(8,128)(2,1)S(1)} %collective-permute-done.1.side_ref), custom_call_target="tpu_custom_call" | custom-call | flops 402653184 | bytes 3145728 | tf_op jit(solution)/shard_map/pallas_call | solution.py:954
  12.5 0.0 copy-start
  12.5 0.0 collective-permute-done.2.nearest_ref
  12.5 4.5 %collective-permute-done.side_ref = bf16[1056,384]{1,0:T(8,128)(2,1)S(1)} collective-permute-done((bf16[1056,384]{1,0:T(8,128)(2,1)S(1)}, bf16[1056,384]{1,0:T(8,128)(2,1)S(1)}, u32[]{:S(2)}, u32[]{:S(2)}) %collective-permute-start) | collective-permute-done | bytes 811040 | tf_op jit(solution)/shard_map/ppermute | solution.py:902
  17.0 0.0 copy-start.1
  17.0 1.3 %shard_map.49 = (s32[224,128]{1,0:T(8,128)S(1)}, s32[224,128]{1,0:T(8,128)S(1)}, s32[224,128]{1,0:T(8,128)S(1)}, s32[224,128]{1,0:T(8,128)S(1)}, s32[224,128]{1,0:T(8,128)S(1)}) custom-call(bf16[400,2048]{1,0:T(8,128)(2,1)S(1)} %get-tuple-element.36.weighted_ref, bf16[1056,384]{1,0:T(8,128)(2,1)S(1)} %collective-permute-done.side_ref, ...), custom_call_target="tpu_custom_call" | custom-call | flops 402653184 | bytes 3145728 | tf_op jit(solution)/shard_map/pallas_call | solution.py:955
  18.2 3.0 %collective-permute-start.3 = (s32[224,128]{1,0:T(8,128)S(1)}, s32[224,128]{1,0:T(8,128)S(1)}, u32[]{:S(2)}, u32[]{:S(2)}) collective-permute-start(s32[224,128]{1,0:T(8,128)S(1)} %get-tuple-element.45), channel_id=1, source_target_pairs={{0,2},{1,3},{2,0},{3,1},{4,6},{5,7},{6,4},{7,5},{8,10},{9,11},{10,... | collective-permute-start | bytes 344072 | tf_op jit(solution)/shard_map/ppermute | solution.py:893
  21.2 1.1 %collective-permute-start.4 = (s32[224,128]{1,0:T(8,128)S(1)}, s32[224,128]{1,0:T(8,128)S(1)}, u32[]{:S(2)}, u32[]{:S(2)}) collective-permute-start(s32[224,128]{1,0:T(8,128)S(1)} %get-tuple-element.46), channel_id=1, source_target_pairs={{0,3},{1,2},{2,1},{3,0},{4,7},{5,6},{6,5},{7,4},{8,11},{9,10},{10,... | collective-permute-start | bytes 344072 | tf_op jit(solution)/shard_map/ppermute | solution.py:893
  22.3 0.2 collective-permute-start.5
  22.5 0.0 copy-done
  22.5 0.3 shard_map.50
  22.8 0.0 collective-permute-done.6.refs_1_
  22.8 2.8 %collective-permute-done.7.refs_2_ = s32[224,128]{1,0:T(8,128)S(1)} collective-permute-done((s32[224,128]{1,0:T(8,128)S(1)}, s32[224,128]{1,0:T(8,128)S(1)}, u32[]{:S(2)}, u32[]{:S(2)}) %collective-permute-start.7) | collective-permute-done | bytes 114720 | tf_op jit(solution)/shard_map/ppermute | solution.py:893
  25.6 0.0 copy-done.1
  25.6 2.1 %shard_map.51 = (f32[384,128]{1,0:T(8,128)S(1)}, f32[96,128]{1,0:T(8,128)S(1)}, f32[6,240,128]{2,1,0:T(8,128)S(1)}, f32[2,240,128]{2,1,0:T(8,128)S(1)}, bf16[128...) custom-call(s32[4]{0:T(128)S(1)} %copy-done.1, ...), custom_call_target="tpu_custom_call" | custom-call | flops 33554432 | bytes 1048576 | tf_op jit(solution)/shard_map/pallas_call | solution.py:1000
  27.7 1.3 %collective-permute-done.3.refs_1_ = s32[224,128]{1,0:T(8,128)S(1)} collective-permute-done((s32[224,128]{1,0:T(8,128)S(1)}, s32[224,128]{1,0:T(8,128)S(1)}, u32[]{:S(2)}, u32[]{:S(2)}) %collective-permute-start.3) | collective-permute-done | bytes 114720 | tf_op jit(solution)/shard_map/ppermute | solution.py:893
  29.1 0.0 collective-permute-done.4.refs_2_
  29.1 0.4 %collective-permute-done.5.refs_3_ = s32[224,128]{1,0:T(8,128)S(1)} collective-permute-done((s32[224,128]{1,0:T(8,128)S(1)}, s32[224,128]{1,0:T(8,128)S(1)}, u32[]{:S(2)}, u32[]{:S(2)}) %collective-permute-start.5) | collective-permute-done | bytes 114720 | tf_op jit(solution)/shard_map/ppermute | solution.py:893
  29.5 1.2 %shard_map.52 = (f32[48,128]{1,0:T(8,128)S(1)}, f32[48,128]{1,0:T(8,128)S(1)}, f32[48,128]{1,0:T(8,128)S(1)}) custom-call(s32[4]{0:T(128)S(1)} %copy-done.1, s32[224,128]{1,0:T(8,128)S(1)} %get-tuple-element.44.refs_0_, s32[224,128]{1,0:T(8,128)S(1)} %collective-permute-done.3.refs_1_, s32[224,128]{1,0:T(8,128)S(1)} %collective-permute-done.4.refs_2_, ...), custom_call_target="tpu_custom_call" | custom-call | flops 67108864 | bytes 2097152 | tf_op jit(solution)/shard_map/pallas_call | solution.py:1018
  30.7 1.6 %collective-permute-start.8 = (f32[48,128]{1,0:T(8,128)S(1)}, f32[48,128]{1,0:T(8,128)S(1)}, u32[]{:S(2)}, u32[]{:S(2)}) collective-permute-start(f32[48,128]{1,0:T(8,128)S(1)} %get-tuple-element.63), channel_id=1, source_target_pairs={{0,1},{1,0},{2,3},{3,2},{4,5},{5,4},{6,7},{7,6},{8,9},{9,8},{10,11... | collective-permute-start | bytes 73736 | tf_op jit(solution)/shard_map/ppermute | solution.py:893
  32.4 3.3 %collective-permute-start.9 = (f32[48,128]{1,0:T(8,128)S(1)}, f32[48,128]{1,0:T(8,128)S(1)}, u32[]{:S(2)}, u32[]{:S(2)}) collective-permute-start(f32[48,128]{1,0:T(8,128)S(1)} %get-tuple-element.64), channel_id=1, source_target_pairs={{0,4},{1,5},{4,8},{5,9},{6,2},{7,3},{8,12},{9,13},{10,6},{11,7},{1... | collective-permute-start | bytes 73736 | tf_op jit(solution)/shard_map/ppermute | solution.py:992
  35.7 0.0 collective-permute-done.8.refs_1_
  35.7 0.9 %collective-permute-done.9.refs_2_ = f32[48,128]{1,0:T(8,128)S(1)} collective-permute-done((f32[48,128]{1,0:T(8,128)S(1)}, f32[48,128]{1,0:T(8,128)S(1)}, u32[]{:S(2)}, u32[]{:S(2)}) %collective-permute-start.9) | collective-permute-done | bytes 24608 | tf_op jit(solution)/shard_map/ppermute | solution.py:992
  36.6 0.7 %shard_map.53 = f32[50,96]{1,0:T(8,128)} custom-call(f32[48,128]{1,0:T(8,128)S(1)} %get-tuple-element.62.refs_0_, f32[48,128]{1,0:T(8,128)S(1)} %collective-permute-done.8.refs_1_, f32[48,128]{1,0:T(8,128)S(1)} %collective-permute-done.9.refs_2_), custom_call_target="tpu_custom_call" | custom-call | tf_op jit(solution)/shard_map/pallas_call | solution.py:1026
  (2 shorter events, 0.0 us)
Async XLA Ops:
  0.0 6.7 %copy-start.2 = (s32[2048]{0:T(1024)S(1)}, s32[2048]{0:T(1024)}, u32[]{:S(2)}) copy-start(s32[2048]{0:T(1024)} %param.5) | copy-start | bytes 24580
  2.1 9.7 %collective-permute-start.1 = (bf16[1056,384]{1,0:T(8,128)(2,1)S(1)}, bf16[1056,384]{1,0:T(8,128)(2,1)S(1)}, u32[]{:S(2)}, u32[]{:S(2)}) collective-permute-start(bf16[1056,384]{1,0:T(8,128)(2,1)S(1)} %get-tuple-element.38), channel_id=1, source_target_pairs={{0,4},{4,0},{8,12},{12,8},{1,5},{5,1},{9,13},{13,9},{2,6},{6,2},{1... | collective-permute-start | bytes 2433032 | tf_op jit(solution)/shard_map/ppermute | solution.py:902
  2.3 14.7 %collective-permute-start = (bf16[1056,384]{1,0:T(8,128)(2,1)S(1)}, bf16[1056,384]{1,0:T(8,128)(2,1)S(1)}, u32[]{:S(2)}, u32[]{:S(2)}) collective-permute-start(bf16[1056,384]{1,0:T(8,128)(2,1)S(1)} %get-tuple-element.37), channel_id=1, source_target_pairs={{4,8},{8,4},{5,9},{9,5},{6,10},{10,6},{7,11},{11,7},{20,24},{24,20... | collective-permute-start | bytes 2433032 | tf_op jit(solution)/shard_map/ppermute | solution.py:902
  8.1 4.4 %collective-permute-start.2 = (s32[224,128]{1,0:T(8,128)S(1)}, s32[224,128]{1,0:T(8,128)S(1)}, u32[]{:S(2)}, u32[]{:S(2)}) collective-permute-start(s32[224,128]{1,0:T(8,128)S(1)} %get-tuple-element.43), channel_id=1, source_target_pairs={{0,1},{1,0},{2,3},{3,2},{4,5},{5,4},{6,7},{7,6},{8,9},{9,8},{10,11... | collective-permute-start | bytes 344072 | tf_op jit(solution)/shard_map/ppermute | solution.py:893
  9.5 13.3 %collective-permute-start.6 = (s32[224,128]{1,0:T(8,128)S(1)}, s32[224,128]{1,0:T(8,128)S(1)}, u32[]{:S(2)}, u32[]{:S(2)}) collective-permute-start(s32[224,128]{1,0:T(8,128)S(1)} %get-tuple-element.49), channel_id=1, source_target_pairs={{0,3},{1,2},{2,1},{3,0},{4,7},{5,6},{6,5},{7,4},{8,11},{9,10},{10,... | collective-permute-start | bytes 344072 | tf_op jit(solution)/shard_map/ppermute | solution.py:893
  11.7 14.0 %collective-permute-start.7 = (s32[224,128]{1,0:T(8,128)S(1)}, s32[224,128]{1,0:T(8,128)S(1)}, u32[]{:S(2)}, u32[]{:S(2)}) collective-permute-start(s32[224,128]{1,0:T(8,128)S(1)} %get-tuple-element.50), channel_id=1, source_target_pairs={{0,2},{1,3},{2,0},{3,1},{4,6},{5,7},{6,4},{7,5},{8,10},{9,11},{10,... | collective-permute-start | bytes 344072 | tf_op jit(solution)/shard_map/ppermute | solution.py:893
  12.5 10.1 %copy-start = (s32[50,384]{1,0:T(8,128)S(1)}, s32[50,384]{1,0:T(8,128)}, u32[]{:S(2)}) copy-start(s32[50,384]{1,0:T(8,128)} %annot_ref.3) | copy-start | bytes 230404
  17.0 8.7 %copy-start.1 = (s32[4]{0:T(128)S(1)}, s32[4]{0:T(128)}, u32[]{:S(2)}) copy-start(s32[4]{0:T(128)} %reach_ref.3) | copy-start | bytes 52
  18.2 10.8 %collective-permute-start.3 = (s32[224,128]{1,0:T(8,128)S(1)}, s32[224,128]{1,0:T(8,128)S(1)}, u32[]{:S(2)}, u32[]{:S(2)}) collective-permute-start(s32[224,128]{1,0:T(8,128)S(1)} %get-tuple-element.45), channel_id=1, source_target_pairs={{0,2},{1,3},{2,0},{3,1},{4,6},{5,7},{6,4},{7,5},{8,10},{9,11},{10,... | collective-permute-start | bytes 344072 | tf_op jit(solution)/shard_map/ppermute | solution.py:893
  21.2 7.8 %collective-permute-start.4 = (s32[224,128]{1,0:T(8,128)S(1)}, s32[224,128]{1,0:T(8,128)S(1)}, u32[]{:S(2)}, u32[]{:S(2)}) collective-permute-start(s32[224,128]{1,0:T(8,128)S(1)} %get-tuple-element.46), channel_id=1, source_target_pairs={{0,3},{1,2},{2,1},{3,0},{4,7},{5,6},{6,5},{7,4},{8,11},{9,10},{10,... | collective-permute-start | bytes 344072 | tf_op jit(solution)/shard_map/ppermute | solution.py:893
  22.3 7.2 %collective-permute-start.5 = (s32[224,128]{1,0:T(8,128)S(1)}, s32[224,128]{1,0:T(8,128)S(1)}, u32[]{:S(2)}, u32[]{:S(2)}) collective-permute-start(s32[224,128]{1,0:T(8,128)S(1)} %get-tuple-element.47), channel_id=1, source_target_pairs={{0,1},{1,0},{2,3},{3,2},{4,5},{5,4},{6,7},{7,6},{8,9},{9,8},{10,11... | collective-permute-start | bytes 344072 | tf_op jit(solution)/shard_map/ppermute | solution.py:893
  30.7 4.9 %collective-permute-start.8 = (f32[48,128]{1,0:T(8,128)S(1)}, f32[48,128]{1,0:T(8,128)S(1)}, u32[]{:S(2)}, u32[]{:S(2)}) collective-permute-start(f32[48,128]{1,0:T(8,128)S(1)} %get-tuple-element.63), channel_id=1, source_target_pairs={{0,1},{1,0},{2,3},{3,2},{4,5},{5,4},{6,7},{7,6},{8,9},{9,8},{10,11... | collective-permute-start | bytes 73736 | tf_op jit(solution)/shard_map/ppermute | solution.py:893
  32.4 4.2 %collective-permute-start.9 = (f32[48,128]{1,0:T(8,128)S(1)}, f32[48,128]{1,0:T(8,128)S(1)}, u32[]{:S(2)}, u32[]{:S(2)}) collective-permute-start(f32[48,128]{1,0:T(8,128)S(1)} %get-tuple-element.64), channel_id=1, source_target_pairs={{0,4},{1,5},{4,8},{5,9},{6,2},{7,3},{8,12},{9,13},{10,6},{11,7},{1... | collective-permute-start | bytes 73736 | tf_op jit(solution)/shard_map/ppermute | solution.py:992

commit v17 on v15

--- a/solution.py
+++ b/solution.py
@@ -190,6 +190,31 @@
 
 LEFT_BLOCKS = ((0, 1, 2, 3), (2, 3, 6, 7), (4, 0, 1, 2), (6, 0, 4, 5))
 RIGHT_BLOCKS = ((2, 3, 6, 7), (4, 5, 6, 7), (0, 1, 2, 4), (0, 4, 5, 6))
+
+
+SPARE_OWN = ((0, 0, 0, 0), (1, 1, 2, 2), (4, 5, 6, 7), (6, 6, 7, 7))
+SPARE_NEAR = ((4, 5, 6, 7), (4, 5, 4, 5), (3, 3, 3, 3), (1, 2, 1, 2))
+
+
+def fold_spare(tile, spare):
+    owners = len(SPARE_OWN)
+    snps = tile.shape[1]
+    size = snps // (2 * owners)
+    count = spare.shape[0] // owners
+    totals = tile[snps : snps + count - size, :]
+    lane = iota((count, snps), 1)
+    for owner in range(owners):
+        mixed = None
+        for slot in range(owners):
+            own, near = SPARE_OWN[owner][slot], SPARE_NEAR[owner][slot]
+            before = (SPARE_OWN[owner][slot - 1], SPARE_NEAR[owner][slot - 1] + 1) if slot else None
+            if before == (own, near):
+                continue
+            values = jnp.concatenate([tile[own * size : (own + 1) * size, :], totals], axis=0)
+            shift = (slot - near) * size % snps
+            values = pltpu.roll(values, shift, 1) if shift else values
+            mixed = values if mixed is None else jnp.where(lane >= slot * size, values, mixed)
+        spare[owner * count : (owner + 1) * count, :] = to_fields(mixed[:, 0 : spare.shape[1]])
 
 
 def fold_by_column(tile, flipped, folded):
@@ -261,7 +286,7 @@
 def far_kernel(
     groups, share, weighted_ref, side_ref, whole_ref, shared_ref, totals_ref, mine_ref, nearest_ref, own_sum_ref, *refs
 ):
-    targets, (tile, folded, flipped, extras) = refs[:groups], refs[groups:]
+    targets, (tile, folded, flipped, spare, extras) = refs[:groups], refs[groups:]
     snps = tile.shape[1]
     own_sum_ref[...] = mine_ref[...] + nearest_ref[...]
     whole, shared = side_dot(weighted_ref, side_ref)
@@ -284,18 +309,38 @@
     apart = jnp.sum(
         jnp.where(iota(square, 0) == iota(square, 1), tile[0:snps, :], 0.0), axis=0, keepdims=True
     )
+    fold_spare(tile, spare)
     tiles = snps // LANES
+    size = share
+    count = spare.shape[0] // groups
     sizes = totals_ref[1:2, :]
     by_column = jnp.concatenate([sizes, tile[snps : snps + 1, :], apart, jnp.zeros((5, snps))], axis=0)
     for owner in range(groups):
         start = owner * (snps // groups)
         columns = pltpu.roll(by_column, snps - start, 1) if owner else by_column
-        extras[8 * owner : 8 * (owner + 1), :] = to_fields(columns[:, 0:LANES])
+        spare_totals = spare[owner * count + size : owner * count + size + 1, :]
+        extras[8 * owner : 8 * (owner + 1), :] = jnp.concatenate(
+            [
+                to_fields(columns[0:3, 0:LANES]),
+                spare_totals[:, 0:LANES],
+                spare_totals[:, LANES:],
+                jnp.zeros((3, LANES), jnp.int32),
+            ],
+            axis=0,
+        )
     me = lax.axis_index("hap")
     send_tiles(groups, folded, share, targets)
+    left = iota((size // 2, LANES), 1) < HALF_LANES
     for step, target in enumerate(targets):
         owner = partner(me, step, groups)
-        target[tiles * share :, :] = extras[pl.ds(pl.multiple_of(owner * 8, 8), 8), :]
+        counts = spare[pl.ds(pl.multiple_of(owner * count, 8), size), :]
+        start = tiles * size
+        target[start : start + size, :] = counts[:, 0:LANES]
+        rest = counts[:, LANES:]
+        target[start + size : start + size + size // 2, :] = jnp.where(
+            left, rest[0 : size // 2], pltpu.roll(rest[size // 2 :], HALF_LANES, 1)
+        )
+        target[start + size + size // 2 :, :] = extras[pl.ds(pl.multiple_of(owner * 8, 8), 8), :]
 
 
 def near_kernel(groups, share, weighted_ref, far_ref, close_ref, totals_ref, *refs):
@@ -523,6 +568,18 @@
     return left + left[0:1], right + [(2 * me + 1) * size]
 
 
+def spare_places(groups, size):
+    me = lax.axis_index("hap")
+
+    def mine(blocks, slot):
+        value = blocks[0][slot]
+        for group in range(1, groups):
+            value = jnp.where(me == group, blocks[group][slot], value)
+        return value * size
+
+    return [[mine(blocks, slot) for slot in range(groups)] for blocks in (SPARE_OWN, SPARE_NEAR)]
+
+
 def rows_at(ref, places, size):
     return jnp.concatenate([ref[pl.ds(pl.multiple_of(place, 8), size), :] for place in places], axis=0)
 
@@ -531,7 +588,8 @@
     groups, share, reach_ref, *refs
 ):
     own_parts, refs = refs[: groups - 1], refs[groups - 1 :]
-    annot_ref, near_annot_ref, scores, mine_ref, rows_ref, masks_ref, columns_ref, own_rows_ref, table = refs
+    annot_ref, near_annot_ref, scores, mine_ref, rows_ref, masks_ref, columns_ref, own_rows_ref, *refs = refs
+    spare_rows_ref, spare_mask_ref, spare_columns_ref, *targets, table = refs
     snps = annot_ref.shape[0]
     half = snps // 2
     wide = snps // groups
@@ -584,6 +642,10 @@
         own_row = [mine[:, 4 * pop + k : 4 * pop + k + 1] for k in range(4)]
         product *= correlation(own_row, own_row, own_row[3])
     scores[slice_rows, :] += annot_ref[slice_rows, :] * product
+    for step, target in enumerate(targets, 2):
+        group = partner(me, step, groups)
+        rows = scores[pl.ds(pl.multiple_of(group * wide, 8), wide), :]
+        target[...] = pack_halves(rows).astype(target.dtype)
 
     size = wide // 2
     left_places, right_places = owner_places(groups, size)
@@ -608,8 +670,9 @@
     apart = jnp.abs(own_row - (lane + me * wide))
     ahead = (own_row - (lane + me * wide)) * jnp.where(upper, 1, -1) > 0
     real = ahead & (lane < wide) & ((lane >= size) | (iota(shape, 0) < groups * size))
-    for number, limit in enumerate((reach_here, reach_there)):
-        masks_ref[number] = jnp.where(real & (snps - apart <= limit), 1.0, 0.0)
+    inside = (own_row - half) * jnp.where(upper, 1, -1) < jnp.where(upper, 0, 1)
+    masks_ref[0] = jnp.where(real & inside & (snps - apart <= reach_here), 1.0, 0.0)
+    masks_ref[1] = jnp.where(real & (snps - apart <= reach_there), 1.0, 0.0)
     theirs = near_annot_ref[slice_rows, :]
     columns = [theirs[0:size], pltpu.roll(theirs[size:], HALF_LANES, 1), jnp.zeros((LANES - wide, LANES))]
     columns_ref[...] = jnp.concatenate(columns, axis=0).astype(jnp.bfloat16)
@@ -618,11 +681,37 @@
     )
     own_rows_ref[...] = own_rows.astype(jnp.bfloat16)
 
+    own_places, near_places = spare_places(groups, size)
+    shape = (size, spare_mask_ref.shape[1])
+    local, lane = iota(shape, 0), iota(shape, 1)
+
+    def by_slot(values):
+        mixed = values[0]
+        for slot in range(1, groups):
+            mixed = jnp.where(lane >= slot * size, values[slot], mixed)
+        return mixed
+
+    tables = [table[pl.ds(pl.multiple_of(place, 8), size), :] for place in own_places]
+    for pop in range(2):
+        for k in range(3):
+            column = slice(4 * pop + k, 4 * pop + k + 1)
+            spare_rows_ref[3 * pop + k] = by_slot(
+                [jnp.broadcast_to(values[:, column], shape) for values in tables]
+            )
+    own_row = by_slot([local + place for place in own_places])
+    near_col = by_slot([lane + (place - slot * size) for slot, place in enumerate(near_places)])
+    close = snps - jnp.abs(own_row - near_col) <= reach_here
+    spare_mask_ref[...] = jnp.where(close & (lane < groups * size), 1.0, 0.0)
+    columns = [rows_at(near_annot_ref, near_places, size)]
+    columns.append(jnp.zeros((shape[1] - groups * size, LANES), jnp.float32))
+    spare_columns_ref[...] = jnp.concatenate(columns, axis=0).astype(jnp.bfloat16)
+
 
 def near_score_kernel(groups, share, reach_ref, *refs):
     near_parts, refs = refs[:groups], refs[groups:]
-    own_ref, mine_ref, rows_ref, masks_ref, columns_ref, own_rows_ref, annot_ref, near_annot_ref = refs[:8]
-    out_ref, *targets, near_out_ref, flipped, scores = refs[8:]
+    own_ref, mine_ref, rows_ref, masks_ref, columns_ref, own_rows_ref = refs[:6]
+    spare_rows_ref, spare_mask_ref, spare_columns_ref, annot_ref, near_annot_ref = refs[6:11]
+    out_ref, send_ref, near_out_ref, flipped, scores = refs[11:]
     snps = annot_ref.shape[0]
     wide = snps // groups
     size = wide // 2
@@ -638,9 +727,16 @@
     scores[...] = own_ref[...]
     near_sums = sum((part[...] for part in near_parts[1:]), near_parts[0][...])
     near_counts = from_tiles(near_sums[0 : tiles * share, :], share)
-    extras = from_fields(near_sums[tiles * share :, :])
-    near_stats, near_lines = [], []
-    for pop in range(2):
+    start = tiles * share
+    rest = near_sums[start + size : start + size + size // 2, :]
+    rest = jnp.concatenate([rest, pltpu.roll(rest, HALF_LANES, 1)], axis=0)
+    spare_fields = from_fields(jnp.concatenate([near_sums[start : start + size, :], rest], axis=1))
+    extras = from_fields(near_sums[start + size + size // 2 :, :])
+    near_stats, near_lines, spare_stats = [], [], []
+    for pop in range(2):
+        count = extras[pop][0:1, :]
+        totals = jnp.concatenate([extras[pop][3:4, :], extras[pop][4:5, :]], axis=1)
+        spare_stats.append(column_stats(totals, jnp.concatenate([count, count], axis=1)))
         near_stats.append(column_stats(extras[pop][1:2, :], extras[pop][0:1, :]))
         near_lines += [*near_stats[pop], extras[pop][2:3, :]]
     near_table = jnp.concatenate(near_lines, axis=0).T[0:wide, :]
@@ -663,6 +759,19 @@
     for values, places in zip((direct, turned), owner_places(groups, size)):
         for slot, place in enumerate(places):
             scores[pl.ds(pl.multiple_of(place, 8), size), :] += values[slot * size : (slot + 1) * size, :]
+    product = 1.0
+    for pop in range(2):
+        row_stats = [spare_rows_ref[3 * pop + k] for k in range(3)]
+        product *= correlation(row_stats, spare_stats[pop], spare_fields[pop])
+    spare_here = jnp.where(spare_mask_ref[...] > 0.0, product, 0.0)
+    lane = iota(spare_here.shape, 1)
+    spare_here = [
+        jnp.where((lane >= slot * size) & (lane < (slot + 1) * size), spare_here, 0.0)
+        for slot in range(groups)
+    ]
+    direct = dot_rounded(jnp.concatenate(spare_here, axis=0), spare_columns_ref[...], 1)
+    for slot, place in enumerate(spare_places(groups, size)[0]):
+        scores[pl.ds(pl.multiple_of(place, 8), size), :] += direct[slot * size : (slot + 1) * size, :]
     near_scores = dot_rounded(near_there, own_rows_ref[...], 0)
     near_scores = jnp.where(
         iota((size, LANES), 1) < HALF_LANES, near_scores[0:size], near_scores[size:wide]
@@ -683,8 +792,7 @@
         return pack_halves(scores[pl.ds(pl.multiple_of(group * wide, 8), wide), :])
 
     out_ref[...] = packed(0)
-    for step, target in enumerate(targets, 1):
-        target[...] = packed(step).astype(target.dtype)
+    send_ref[...] = packed(1).astype(send_ref.dtype)
 
 
 def column_finish_kernel(*refs):
@@ -758,6 +866,7 @@
     by_column = groups == len(LEFT_BLOCKS)
     compact = shape((share * (snps // LANES) + 8, LANES), i32)
     own_share_counts = compact if by_column else shape((share, snps), i32)
+    near_share_counts = shape((compact.shape[0] + share + share // 2, LANES), i32)
     tile = pltpu.VMEM((snps + 16, snps), f32)
     folded = pltpu.VMEM((folded_rows, snps), i32)
     weighted, totals, *own_parts = call(
@@ -770,7 +879,7 @@
     )(alleles, labels.reshape(1, rows))
     own_parts = [own_parts[0]] + [around(own_parts[k], groups, k) for k in range(groups - 1, 0, -1)]
 
-    near_shapes = [own_share_counts] + [compact if by_column else shape((share + 8, snps), i32)] * groups
+    near_shapes = [own_share_counts] + [near_share_counts if by_column else shape((share + 8, snps), i32)] * groups
     if by_column:
         piece = shape((snps + 16, LANES), f32)
         work = dict(flops=4 * rows * snps * LANES, moved=rows * snps * 4)
@@ -783,6 +892,7 @@
                 tile,
                 folded,
                 pltpu.VMEM((snps, LANES), f32),
+                pltpu.VMEM(((share + 8) * groups, 2 * LANES), i32),
                 pltpu.VMEM((8 * groups, LANES), i32),
             ],
             **work,
@@ -819,7 +929,8 @@
     packed_share = shape((half_share, LANES), f32)
     if by_column:
         pair_rows = (groups + 1) * (out_share // 2)
-        prepared = call(
+        sent = shape((half_share, LANES), bf16)
+        *prepared, second, third = call(
             functools.partial(own_score_kernel, groups, share),
             [
                 by_snp,
@@ -828,26 +939,28 @@
                 shape((2, pair_rows, LANES), f32),
                 shape((LANES, LANES), bf16),
                 shape((pair_rows, LANES), bf16),
+                shape((6, share, 2 * LANES), f32),
+                shape((share, 2 * LANES), f32),
+                shape((2 * LANES, LANES), bf16),
+                packed_share,
+                packed_share,
             ],
             [SMEM] + [VMEM] * (groups + 1),
             [pltpu.VMEM((snps, LANES), f32)],
-            flops=1 << 25,
+            flops=1 << 33,
             moved=1 << 20,
         )(reach, own_sum, *own_parts[1:-1], own_annots, near_annots)
-        sent = shape((half_share, LANES), bf16)
-        own_scores, *scores = call(
+        parts = [around(second, groups, 2), around(third, groups, 3)]
+        own_scores, send, there = call(
             functools.partial(near_score_kernel, groups, share),
-            [packed_share] + [sent] * groups,
-            [SMEM] + [VMEM] * (groups + 8),
+            [packed_share, sent, sent],
+            [SMEM] + [VMEM] * (groups + 11),
             [pltpu.VMEM((LANES, LANES), i32), pltpu.VMEM((snps, LANES), f32)],
             flops=1 << 26,
             moved=1 << 21,
         )(reach, *near_parts, *prepared, own_annots, near_annots)
-        *scores, there = scores
-        scores = [around(scores[k - 1], groups, k) for k in order]
-        return call(column_finish_kernel, result, [VMEM] * (groups + 1))(
-            own_scores, *scores, to_neighbour(there)
-        )
+        parts += [around(send, groups, 1), to_neighbour(there)]
+        return call(column_finish_kernel, result, [VMEM] * 5)(own_scores, *parts)
 
     tall = pltpu.VMEM((padded, LANES), f32)
     scores = call(

time: 37.1 us -> 35.6 us (0.960)
  waiting for transfers between devices: 7.42 us -> 5.68 us
  Pallas kernels: 8.78 us -> 9.26 us
    ppermute x1, starting transfers between devices: 5.29 us -> 3.55 us  [to_neighbour(): return lax.ppermute(value, ('snp', 'hap'), pairs)]
    ppermute x9, waiting for transfers between devices: 1.93 us -> 0.19 us  [around(): lax.ppermute(value, 'hap', [(source, partner(source, step, groups)) for s...]
    ppermute x9, starting transfers between devices: 10.7 us -> 12.3 us  [around(): lax.ppermute(value, 'hap', [(source, partner(source, step, groups)) for s...]
  transfers between devices with their start and end apart: 12 -> 12, of which waited for: 4 -> 3; matrix products, arithmetic and copies ran while one was open for 0% -> 0% of each run, Pallas kernels for 13% -> 18%
where the time goes in v17:
time: 35.6 us; the launch traced here: 35.5 us
  starting transfers between devices  20.4 us (57%)
  Pallas kernels  9.26 us (26%)
  waiting for transfers between devices  5.68 us (16%)
    ppermute x9, starting transfers between devices, around(): lax.ppermute(value, 'hap', [(source, partner(source, step, groups)) for s...  12.3 us
    ppermute x2, waiting for transfers between devices, swapped(): return lax.ppermute(value, 'snp', pairs)  4.71 us
    ppermute x2, starting transfers between devices, swapped(): return lax.ppermute(value, 'snp', pairs)  4.59 us
    ppermute x1, starting transfers between devices, to_neighbour(): return lax.ppermute(value, ('snp', 'hap'), pairs)  3.55 us
    pallas_call x1, Pallas kernels, per_device(): call(prepare_kernel, [shape((rows, snps), bf16), packed, packed], [HBM, H...  2.14 us
    pallas_call x1, Pallas kernels, per_device(): call(functools.partial(own_score_kernel, groups, share), [by_snp, shape((...  1.81 us
    pallas_call x1, Pallas kernels, per_device(): call(functools.partial(far_kernel, groups, share), near_shapes, [VMEM] *...  1.27 us
    pallas_call x1, Pallas kernels, per_device(): call(functools.partial(near_score_kernel, groups, share), [packed_share,...  1.23 us
  transfers between devices with their start and end apart: 12, of which 3 were waited for; matrix products, arithmetic and copies ran while one was open for 0% of the time, Pallas kernels for 18%

profile of v17, /device:TPU:1, one launch (start us, length us, event | category | flops | bytes accessed | tf_op | source)
XLA Modules:
  0.0 35.5 jit_solution(4421806239071446705)
XLA Ops:
  0.0 0.0 copy-start.2
  0.0 2.1 %shard_map.46 = (bf16[2048,384]{1,0:T(8,128)(2,1)S(1)}, bf16[1056,384]{1,0:T(8,128)(2,1)S(1)}, bf16[1056,384]{1,0:T(8,128)(2,1)S(1)}) custom-call(s32[2048,384]{1,0:T(8,128)} %hap_ref.1, s32[50,384]{1,0:T(8,128)} %annot_ref.3), custom_call_target="tpu_custom_call" | custom-call | bytes 6291456 | tf_op jit(solution)/shard_map/pallas_call | solution.py:852
  2.1 0.1 collective-permute-start.1
  2.3 4.5 %collective-permute-start = (bf16[1056,384]{1,0:T(8,128)(2,1)S(1)}, bf16[1056,384]{1,0:T(8,128)(2,1)S(1)}, u32[]{:S(2)}, u32[]{:S(2)}) collective-permute-start(bf16[1056,384]{1,0:T(8,128)(2,1)S(1)} %get-tuple-element.39), channel_id=1, source_target_pairs={{4,8},{8,4},{5,9},{9,5},{6,10},{10,6},{7,11},{11,7},{20,24},{24,20... | collective-permute-start | bytes 2433032 | tf_op jit(solution)/shard_map/ppermute | solution.py:833
  6.7 0.0 copy-done.2
  6.8 1.1 %shard_map.47 = (bf16[400,2048]{1,0:T(8,128)(2,1)S(1)}, f32[8,384]{1,0:T(8,128)S(1)}, s32[152,128]{1,0:T(8,128)S(1)}, s32[152,128]{1,0:T(8,128)S(1)}, s32[152,128]{1,0:T(8,128)S(1)}, /*index=5*/s32[152,128]{1,0:T(8,128)S(1)}) custom-call(bf16[2048,384]{1,0:T(8,128)(2,1)S(1)} %get-tuple-element.37.alleles_ref, s32[1,2048]{1,0:T(1,128)S(1)} %bitcast.1), custom_call_target="tpu_custom_call" | custom-call | flops 603979776 | bytes 3145728 | tf_op jit(solution)/shard_map/pallas_call | solution.py:872
  7.9 1.4 %collective-permute-start.2 = (s32[152,128]{1,0:T(8,128)S(1)}, s32[152,128]{1,0:T(8,128)S(1)}, u32[]{:S(2)}, u32[]{:S(2)}) collective-permute-start(s32[152,128]{1,0:T(8,128)S(1)} %get-tuple-element.45), channel_id=1, source_target_pairs={{0,1},{1,0},{2,3},{3,2},{4,5},{5,4},{6,7},{7,6},{8,9},{9,8},{10,11... | collective-permute-start | bytes 233480 | tf_op jit(solution)/shard_map/ppermute | solution.py:824
  9.3 2.2 %collective-permute-start.6 = (s32[152,128]{1,0:T(8,128)S(1)}, s32[152,128]{1,0:T(8,128)S(1)}, u32[]{:S(2)}, u32[]{:S(2)}) collective-permute-start(s32[152,128]{1,0:T(8,128)S(1)} %get-tuple-element.51), channel_id=1, source_target_pairs={{0,3},{1,2},{2,1},{3,0},{4,7},{5,6},{6,5},{7,4},{8,11},{9,10},{10,... | collective-permute-start | bytes 233480 | tf_op jit(solution)/shard_map/ppermute | solution.py:824
  11.4 0.1 collective-permute-start.7
  11.6 0.0 collective-permute-done.1.side_ref
  11.6 0.7 %shard_map.48 = (f32[400,128]{1,0:T(8,128)S(1)}, f32[400,128]{1,0:T(8,128)S(1)}) custom-call(bf16[400,2048]{1,0:T(8,128)(2,1)S(1)} %get-tuple-element.38.weighted_ref, bf16[1056,384]{1,0:T(8,128)(2,1)S(1)} %collective-permute-done.1.side_ref), custom_call_target="tpu_custom_call" | custom-call | flops 402653184 | bytes 3145728 | tf_op jit(solution)/shard_map/pallas_call | solution.py:886
  12.2 0.0 copy-start
  12.2 0.0 collective-permute-done.2.nearest_ref
  12.3 4.7 %collective-permute-done.side_ref = bf16[1056,384]{1,0:T(8,128)(2,1)S(1)} collective-permute-done((bf16[1056,384]{1,0:T(8,128)(2,1)S(1)}, bf16[1056,384]{1,0:T(8,128)(2,1)S(1)}, u32[]{:S(2)}, u32[]{:S(2)}) %collective-permute-start) | collective-permute-done | bytes 811040 | tf_op jit(solution)/shard_map/ppermute | solution.py:833
  17.0 0.0 copy-start.1
  17.0 1.3 %shard_map.49 = (s32[152,128]{1,0:T(8,128)S(1)}, s32[224,128]{1,0:T(8,128)S(1)}, s32[224,128]{1,0:T(8,128)S(1)}, s32[224,128]{1,0:T(8,128)S(1)}, s32[224,128]{1,0:T(8,128)S(1)}) custom-call(bf16[400,2048]{1,0:T(8,128)(2,1)S(1)} %get-tuple-element.38.weighted_ref, bf16[1056,384]{1,0:T(8,128)(2,1)S(1)} %collective-permute-done.side_ref, ...), custom_call_target="tpu_custom_call" | custom-call | flops 402653184 | bytes 3145728 | tf_op jit(solution)/shard_map/pallas_call | solution.py:887
  18.2 2.9 %collective-permute-start.3 = (s32[224,128]{1,0:T(8,128)S(1)}, s32[224,128]{1,0:T(8,128)S(1)}, u32[]{:S(2)}, u32[]{:S(2)}) collective-permute-start(s32[224,128]{1,0:T(8,128)S(1)} %get-tuple-element.47), channel_id=1, source_target_pairs={{0,2},{1,3},{2,0},{3,1},{4,6},{5,7},{6,4},{7,5},{8,10},{9,11},{10,... | collective-permute-start | bytes 344072 | tf_op jit(solution)/shard_map/ppermute | solution.py:824
  21.1 1.2 %collective-permute-start.4 = (s32[224,128]{1,0:T(8,128)S(1)}, s32[224,128]{1,0:T(8,128)S(1)}, u32[]{:S(2)}, u32[]{:S(2)}) collective-permute-start(s32[224,128]{1,0:T(8,128)S(1)} %get-tuple-element.48), channel_id=1, source_target_pairs={{0,3},{1,2},{2,1},{3,0},{4,7},{5,6},{6,5},{7,4},{8,11},{9,10},{10,... | collective-permute-start | bytes 344072 | tf_op jit(solution)/shard_map/ppermute | solution.py:824
  22.3 0.2 collective-permute-start.5
  22.5 0.0 copy-done
  22.5 0.3 shard_map.50
  22.8 0.0 collective-permute-done.6.refs_1_
  22.8 0.0 collective-permute-done.7.refs_2_
  22.8 0.0 copy-done.1
  22.8 1.8 %shard_map.51 = (f32[384,128]{1,0:T(8,128)S(1)}, f32[96,128]{1,0:T(8,128)S(1)}, f32[6,240,128]{2,1,0:T(8,128)S(1)}, f32[2,240,128]{2,1,0:T(8,128)S(1)}, bf16[128...) custom-call(s32[4]{0:T(128)S(1)} %copy-done.1, ...), custom_call_target="tpu_custom_call" | custom-call | flops 8589934592 | bytes 1048576 | tf_op jit(solution)/shard_map/pallas_call | solution.py:933
  24.7 2.2 %collective-permute-start.8 = (f32[48,128]{1,0:T(8,128)S(1)}, f32[48,128]{1,0:T(8,128)S(1)}, u32[]{:S(2)}, u32[]{:S(2)}) collective-permute-start(f32[48,128]{1,0:T(8,128)S(1)} %get-tuple-element.65), channel_id=1, source_target_pairs={{0,2},{1,3},{2,0},{3,1},{4,6},{5,7},{6,4},{7,5},{8,10},{9,11},{10,... | collective-permute-start | bytes 73736 | tf_op jit(solution)/shard_map/ppermute | solution.py:824
  26.8 1.2 %collective-permute-start.9 = (f32[48,128]{1,0:T(8,128)S(1)}, f32[48,128]{1,0:T(8,128)S(1)}, u32[]{:S(2)}, u32[]{:S(2)}) collective-permute-start(f32[48,128]{1,0:T(8,128)S(1)} %get-tuple-element.66), channel_id=1, source_target_pairs={{0,3},{1,2},{2,1},{3,0},{4,7},{5,6},{6,5},{7,4},{8,11},{9,10},{10,... | collective-permute-start | bytes 73736 | tf_op jit(solution)/shard_map/ppermute | solution.py:824
  28.1 0.0 collective-permute-done.3.refs_1_
  28.1 0.0 collective-permute-done.4.refs_2_
  28.1 0.2 collective-permute-done.5.refs_3_
  28.2 1.2 %shard_map.52 = (f32[48,128]{1,0:T(8,128)S(1)}, bf16[48,128]{1,0:T(8,128)(2,1)S(1)}, bf16[48,128]{1,0:T(8,128)(2,1)S(1)}) custom-call(s32[4]{0:T(128)S(1)} %copy-done.1, s32[224,128]{1,0:T(8,128)S(1)} %get-tuple-element.46.refs_0_, s32[224,128]{1,0:T(8,128)S(1)} %collective-permute-done.3.refs_1_, s32[224,128]{1,0:T(8,128)S(1)} %collective-permute-done.4.refs_2_, ...), custom_call_target="tpu_custom_call" | custom-call | flops 67108864 | bytes 2097152 | tf_op jit(solution)/shard_map/pallas_call | solution.py:954
  29.5 0.9 %collective-permute-start.10 = (bf16[48,128]{1,0:T(8,128)(2,1)S(1)}, bf16[48,128]{1,0:T(8,128)(2,1)S(1)}, u32[]{:S(2)}, u32[]{:S(2)}) collective-permute-start(bf16[48,128]{1,0:T(8,128)(2,1)S(1)} %get-tuple-element.67), channel_id=1, source_target_pairs={{0,1},{1,0},{2,3},{3,2},{4,5},{5,4},{6,7},{7,6},{8,9},{9,8},{10,11... | collective-permute-start | bytes 36872 | tf_op jit(solution)/shard_map/ppermute | solution.py:824
  30.4 3.5 %collective-permute-start.11 = (bf16[48,128]{1,0:T(8,128)(2,1)S(1)}, bf16[48,128]{1,0:T(8,128)(2,1)S(1)}, u32[]{:S(2)}, u32[]{:S(2)}) collective-permute-start(bf16[48,128]{1,0:T(8,128)(2,1)S(1)} %get-tuple-element.68), channel_id=1, source_target_pairs={{0,4},{1,5},{4,8},{5,9},{6,2},{7,3},{8,12},{9,13},{10,6},{11,7},{1... | collective-permute-start | bytes 36872 | tf_op jit(solution)/shard_map/ppermute | solution.py:924
  33.9 0.0 collective-permute-done.8.refs_1_
  33.9 0.0 collective-permute-done.9.refs_2_
  33.9 0.0 collective-permute-done.10.refs_3_
  34.0 0.8 %collective-permute-done.11.refs_4_ = bf16[48,128]{1,0:T(8,128)(2,1)S(1)} collective-permute-done((bf16[48,128]{1,0:T(8,128)(2,1)S(1)}, bf16[48,128]{1,0:T(8,128)(2,1)S(1)}, u32[]{:S(2)}, u32[]{:S(2)}) %collective-permute-start.11) | collective-permute-done | bytes 12320 | tf_op jit(solution)/shard_map/ppermute | solution.py:924
  34.7 0.7 %shard_map.53 = f32[50,96]{1,0:T(8,128)} custom-call(f32[48,128]{1,0:T(8,128)S(1)} %get-tuple-element.64.refs_0_, f32[48,128]{1,0:T(8,128)S(1)} %collective-permute-done.8.refs_1_, f32[48,128]{1,0:T(8,128)S(1)} %collective-permute-done.9.refs_2_, bf16[48,128]{1,0:T(8,128)(2,1)S(1)} %collective-permute-done.10.refs_3_, ...), custom_call_target="tpu_custom_call" | custom-call | tf_op jit(solution)/shard_map/pallas_call | solution.py:963
  (2 shorter events, 0.0 us)
Async XLA Ops:
  0.0 6.7 %copy-start.2 = (s32[2048]{0:T(1024)S(1)}, s32[2048]{0:T(1024)}, u32[]{:S(2)}) copy-start(s32[2048]{0:T(1024)} %param.5) | copy-start | bytes 24580
  2.1 9.4 %collective-permute-start.1 = (bf16[1056,384]{1,0:T(8,128)(2,1)S(1)}, bf16[1056,384]{1,0:T(8,128)(2,1)S(1)}, u32[]{:S(2)}, u32[]{:S(2)}) collective-permute-start(bf16[1056,384]{1,0:T(8,128)(2,1)S(1)} %get-tuple-element.40), channel_id=1, source_target_pairs={{0,4},{4,0},{8,12},{12,8},{1,5},{5,1},{9,13},{13,9},{2,6},{6,2},{1... | collective-permute-start | bytes 2433032 | tf_op jit(solution)/shard_map/ppermute | solution.py:833
  2.3 14.7 %collective-permute-start = (bf16[1056,384]{1,0:T(8,128)(2,1)S(1)}, bf16[1056,384]{1,0:T(8,128)(2,1)S(1)}, u32[]{:S(2)}, u32[]{:S(2)}) collective-permute-start(bf16[1056,384]{1,0:T(8,128)(2,1)S(1)} %get-tuple-element.39), channel_id=1, source_target_pairs={{4,8},{8,4},{5,9},{9,5},{6,10},{10,6},{7,11},{11,7},{20,24},{24,20... | collective-permute-start | bytes 2433032 | tf_op jit(solution)/shard_map/ppermute | solution.py:833
  7.9 4.4 %collective-permute-start.2 = (s32[152,128]{1,0:T(8,128)S(1)}, s32[152,128]{1,0:T(8,128)S(1)}, u32[]{:S(2)}, u32[]{:S(2)}) collective-permute-start(s32[152,128]{1,0:T(8,128)S(1)} %get-tuple-element.45), channel_id=1, source_target_pairs={{0,1},{1,0},{2,3},{3,2},{4,5},{5,4},{6,7},{7,6},{8,9},{9,8},{10,11... | collective-permute-start | bytes 233480 | tf_op jit(solution)/shard_map/ppermute | solution.py:824
  9.3 13.6 %collective-permute-start.6 = (s32[152,128]{1,0:T(8,128)S(1)}, s32[152,128]{1,0:T(8,128)S(1)}, u32[]{:S(2)}, u32[]{:S(2)}) collective-permute-start(s32[152,128]{1,0:T(8,128)S(1)} %get-tuple-element.51), channel_id=1, source_target_pairs={{0,3},{1,2},{2,1},{3,0},{4,7},{5,6},{6,5},{7,4},{8,11},{9,10},{10,... | collective-permute-start | bytes 233480 | tf_op jit(solution)/shard_map/ppermute | solution.py:824
  11.4 11.4 %collective-permute-start.7 = (s32[152,128]{1,0:T(8,128)S(1)}, s32[152,128]{1,0:T(8,128)S(1)}, u32[]{:S(2)}, u32[]{:S(2)}) collective-permute-start(s32[152,128]{1,0:T(8,128)S(1)} %get-tuple-element.52), channel_id=1, source_target_pairs={{0,2},{1,3},{2,0},{3,1},{4,6},{5,7},{6,4},{7,5},{8,10},{9,11},{10,... | collective-permute-start | bytes 233480 | tf_op jit(solution)/shard_map/ppermute | solution.py:824
  12.2 10.3 %copy-start = (s32[50,384]{1,0:T(8,128)S(1)}, s32[50,384]{1,0:T(8,128)}, u32[]{:S(2)}) copy-start(s32[50,384]{1,0:T(8,128)} %annot_ref.3) | copy-start | bytes 230404
  17.0 5.9 %copy-start.1 = (s32[4]{0:T(128)S(1)}, s32[4]{0:T(128)}, u32[]{:S(2)}) copy-start(s32[4]{0:T(128)} %reach_ref.3) | copy-start | bytes 52
  18.2 9.8 %collective-permute-start.3 = (s32[224,128]{1,0:T(8,128)S(1)}, s32[224,128]{1,0:T(8,128)S(1)}, u32[]{:S(2)}, u32[]{:S(2)}) collective-permute-start(s32[224,128]{1,0:T(8,128)S(1)} %get-tuple-element.47), channel_id=1, source_target_pairs={{0,2},{1,3},{2,0},{3,1},{4,6},{5,7},{6,4},{7,5},{8,10},{9,11},{10,... | collective-permute-start | bytes 344072 | tf_op jit(solution)/shard_map/ppermute | solution.py:824
  21.1 7.0 %collective-permute-start.4 = (s32[224,128]{1,0:T(8,128)S(1)}, s32[224,128]{1,0:T(8,128)S(1)}, u32[]{:S(2)}, u32[]{:S(2)}) collective-permute-start(s32[224,128]{1,0:T(8,128)S(1)} %get-tuple-element.48), channel_id=1, source_target_pairs={{0,3},{1,2},{2,1},{3,0},{4,7},{5,6},{6,5},{7,4},{8,11},{9,10},{10,... | collective-permute-start | bytes 344072 | tf_op jit(solution)/shard_map/ppermute | solution.py:824
  22.3 5.9 %collective-permute-start.5 = (s32[224,128]{1,0:T(8,128)S(1)}, s32[224,128]{1,0:T(8,128)S(1)}, u32[]{:S(2)}, u32[]{:S(2)}) collective-permute-start(s32[224,128]{1,0:T(8,128)S(1)} %get-tuple-element.49), channel_id=1, source_target_pairs={{0,1},{1,0},{2,3},{3,2},{4,5},{5,4},{6,7},{7,6},{8,9},{9,8},{10,11... | collective-permute-start | bytes 344072 | tf_op jit(solution)/shard_map/ppermute | solution.py:824
  24.7 9.3 %collective-permute-start.8 = (f32[48,128]{1,0:T(8,128)S(1)}, f32[48,128]{1,0:T(8,128)S(1)}, u32[]{:S(2)}, u32[]{:S(2)}) collective-permute-start(f32[48,128]{1,0:T(8,128)S(1)} %get-tuple-element.65), channel_id=1, source_target_pairs={{0,2},{1,3},{2,0},{3,1},{4,6},{5,7},{6,4},{7,5},{8,10},{9,11},{10,... | collective-permute-start | bytes 73736 | tf_op jit(solution)/shard_map/ppermute | solution.py:824
  26.8 7.1 %collective-permute-start.9 = (f32[48,128]{1,0:T(8,128)S(1)}, f32[48,128]{1,0:T(8,128)S(1)}, u32[]{:S(2)}, u32[]{:S(2)}) collective-permute-start(f32[48,128]{1,0:T(8,128)S(1)} %get-tuple-element.66), channel_id=1, source_target_pairs={{0,3},{1,2},{2,1},{3,0},{4,7},{5,6},{6,5},{7,4},{8,11},{9,10},{10,... | collective-permute-start | bytes 73736 | tf_op jit(solution)/shard_map/ppermute | solution.py:824
  29.5 4.5 %collective-permute-start.10 = (bf16[48,128]{1,0:T(8,128)(2,1)S(1)}, bf16[48,128]{1,0:T(8,128)(2,1)S(1)}, u32[]{:S(2)}, u32[]{:S(2)}) collective-permute-start(bf16[48,128]{1,0:T(8,128)(2,1)S(1)} %get-tuple-element.67), channel_id=1, source_target_pairs={{0,1},{1,0},{2,3},{3,2},{4,5},{5,4},{6,7},{7,6},{8,9},{9,8},{10,11... | collective-permute-start | bytes 36872 | tf_op jit(solution)/shard_map/ppermute | solution.py:824
  30.4 4.4 %collective-permute-start.11 = (bf16[48,128]{1,0:T(8,128)(2,1)S(1)}, bf16[48,128]{1,0:T(8,128)(2,1)S(1)}, u32[]{:S(2)}, u32[]{:S(2)}) collective-permute-start(bf16[48,128]{1,0:T(8,128)(2,1)S(1)} %get-tuple-element.68), channel_id=1, source_target_pairs={{0,4},{1,5},{4,8},{5,9},{6,2},{7,3},{8,12},{9,13},{10,6},{11,7},{1... | collective-permute-start | bytes 36872 | tf_op jit(solution)/shard_map/ppermute | solution.py:924

commit v18 on v17

--- a/solution.py
+++ b/solution.py
@@ -950,7 +950,7 @@
             flops=1 << 33,
             moved=1 << 20,
         )(reach, own_sum, *own_parts[1:-1], own_annots, near_annots)
-        parts = [around(second, groups, 2), around(third, groups, 3)]
+        parts = [around(third, groups, 3), around(second, groups, 2)]
         own_scores, send, there = call(
             functools.partial(near_score_kernel, groups, share),
             [packed_share, sent, sent],

time: 35.6 us -> 35.7 us (level)
  waiting for transfers between devices: 5.68 us -> 6.31 us
  starting transfers between devices: 20.4 us -> 19.8 us
    ppermute x9, starting transfers between devices: 12.3 us -> 11.5 us  [around(): lax.ppermute(value, 'hap', [(source, partner(source, step, groups)) for s...]
    ppermute x9, waiting for transfers between devices: 0.19 us -> 0.83 us  [around(): lax.ppermute(value, 'hap', [(source, partner(source, step, groups)) for s...]
  transfers between devices with their start and end apart: 12 -> 12, of which waited for: 3 -> 4; matrix products, arithmetic and copies ran while one was open for 0% -> 0% of each run, Pallas kernels for 18% -> 18%
where the time goes in v18:
time: 35.7 us; the launch traced here: 35.5 us
  starting transfers between devices  19.8 us (55%)
  Pallas kernels  9.26 us (26%)
  waiting for transfers between devices  6.31 us (18%)
    ppermute x9, starting transfers between devices, around(): lax.ppermute(value, 'hap', [(source, partner(source, step, groups)) for s...  11.5 us
    ppermute x2, waiting for transfers between devices, swapped(): return lax.ppermute(value, 'snp', pairs)  4.71 us
    ppermute x2, starting transfers between devices, swapped(): return lax.ppermute(value, 'snp', pairs)  4.59 us
    ppermute x1, starting transfers between devices, to_neighbour(): return lax.ppermute(value, ('snp', 'hap'), pairs)  3.69 us
    pallas_call x1, Pallas kernels, per_device(): call(prepare_kernel, [shape((rows, snps), bf16), packed, packed], [HBM, H...  2.14 us
    pallas_call x1, Pallas kernels, per_device(): call(functools.partial(own_score_kernel, groups, share), [by_snp, shape((...  1.81 us
    pallas_call x1, Pallas kernels, per_device(): call(functools.partial(far_kernel, groups, share), near_shapes, [VMEM] *...  1.27 us
    pallas_call x1, Pallas kernels, per_device(): call(functools.partial(near_score_kernel, groups, share), [packed_share,...  1.23 us
  transfers between devices with their start and end apart: 12, of which 4 were waited for; matrix products, arithmetic and copies ran while one was open for 0% of the time, Pallas kernels for 18%

profile of v18, /device:TPU:1, one launch (start us, length us, event | category | flops | bytes accessed | tf_op | source)
XLA Modules:
  0.0 35.5 jit_solution(17904740874491630827)
XLA Ops:
  0.0 0.0 copy-start.2
  0.0 2.1 %shard_map.46 = (bf16[2048,384]{1,0:T(8,128)(2,1)S(1)}, bf16[1056,384]{1,0:T(8,128)(2,1)S(1)}, bf16[1056,384]{1,0:T(8,128)(2,1)S(1)}) custom-call(s32[2048,384]{1,0:T(8,128)} %hap_ref.1, s32[50,384]{1,0:T(8,128)} %annot_ref.3), custom_call_target="tpu_custom_call" | custom-call | bytes 6291456 | tf_op jit(solution)/shard_map/pallas_call | solution.py:852
  2.1 0.1 collective-permute-start.1
  2.3 4.5 %collective-permute-start = (bf16[1056,384]{1,0:T(8,128)(2,1)S(1)}, bf16[1056,384]{1,0:T(8,128)(2,1)S(1)}, u32[]{:S(2)}, u32[]{:S(2)}) collective-permute-start(bf16[1056,384]{1,0:T(8,128)(2,1)S(1)} %get-tuple-element.39), channel_id=1, source_target_pairs={{4,8},{8,4},{5,9},{9,5},{6,10},{10,6},{7,11},{11,7},{20,24},{24,20... | collective-permute-start | bytes 2433032 | tf_op jit(solution)/shard_map/ppermute | solution.py:833
  6.7 0.0 copy-done.2
  6.8 1.1 %shard_map.47 = (bf16[400,2048]{1,0:T(8,128)(2,1)S(1)}, f32[8,384]{1,0:T(8,128)S(1)}, s32[152,128]{1,0:T(8,128)S(1)}, s32[152,128]{1,0:T(8,128)S(1)}, s32[152,128]{1,0:T(8,128)S(1)}, /*index=5*/s32[152,128]{1,0:T(8,128)S(1)}) custom-call(bf16[2048,384]{1,0:T(8,128)(2,1)S(1)} %get-tuple-element.37.alleles_ref, s32[1,2048]{1,0:T(1,128)S(1)} %bitcast.1), custom_call_target="tpu_custom_call" | custom-call | flops 603979776 | bytes 3145728 | tf_op jit(solution)/shard_map/pallas_call | solution.py:872
  7.9 1.4 %collective-permute-start.2 = (s32[152,128]{1,0:T(8,128)S(1)}, s32[152,128]{1,0:T(8,128)S(1)}, u32[]{:S(2)}, u32[]{:S(2)}) collective-permute-start(s32[152,128]{1,0:T(8,128)S(1)} %get-tuple-element.45), channel_id=1, source_target_pairs={{0,1},{1,0},{2,3},{3,2},{4,5},{5,4},{6,7},{7,6},{8,9},{9,8},{10,11... | collective-permute-start | bytes 233480 | tf_op jit(solution)/shard_map/ppermute | solution.py:824
  9.3 2.2 %collective-permute-start.6 = (s32[152,128]{1,0:T(8,128)S(1)}, s32[152,128]{1,0:T(8,128)S(1)}, u32[]{:S(2)}, u32[]{:S(2)}) collective-permute-start(s32[152,128]{1,0:T(8,128)S(1)} %get-tuple-element.51), channel_id=1, source_target_pairs={{0,3},{1,2},{2,1},{3,0},{4,7},{5,6},{6,5},{7,4},{8,11},{9,10},{10,... | collective-permute-start | bytes 233480 | tf_op jit(solution)/shard_map/ppermute | solution.py:824
  11.4 0.1 collective-permute-start.7
  11.6 0.0 collective-permute-done.1.side_ref
  11.6 0.7 %shard_map.48 = (f32[400,128]{1,0:T(8,128)S(1)}, f32[400,128]{1,0:T(8,128)S(1)}) custom-call(bf16[400,2048]{1,0:T(8,128)(2,1)S(1)} %get-tuple-element.38.weighted_ref, bf16[1056,384]{1,0:T(8,128)(2,1)S(1)} %collective-permute-done.1.side_ref), custom_call_target="tpu_custom_call" | custom-call | flops 402653184 | bytes 3145728 | tf_op jit(solution)/shard_map/pallas_call | solution.py:886
  12.2 0.0 copy-start
  12.2 0.0 collective-permute-done.2.nearest_ref
  12.3 4.7 %collective-permute-done.side_ref = bf16[1056,384]{1,0:T(8,128)(2,1)S(1)} collective-permute-done((bf16[1056,384]{1,0:T(8,128)(2,1)S(1)}, bf16[1056,384]{1,0:T(8,128)(2,1)S(1)}, u32[]{:S(2)}, u32[]{:S(2)}) %collective-permute-start) | collective-permute-done | bytes 811040 | tf_op jit(solution)/shard_map/ppermute | solution.py:833
  17.0 0.0 copy-start.1
  17.0 1.3 %shard_map.49 = (s32[152,128]{1,0:T(8,128)S(1)}, s32[224,128]{1,0:T(8,128)S(1)}, s32[224,128]{1,0:T(8,128)S(1)}, s32[224,128]{1,0:T(8,128)S(1)}, s32[224,128]{1,0:T(8,128)S(1)}) custom-call(bf16[400,2048]{1,0:T(8,128)(2,1)S(1)} %get-tuple-element.38.weighted_ref, bf16[1056,384]{1,0:T(8,128)(2,1)S(1)} %collective-permute-done.side_ref, ...), custom_call_target="tpu_custom_call" | custom-call | flops 402653184 | bytes 3145728 | tf_op jit(solution)/shard_map/pallas_call | solution.py:887
  18.2 2.9 %collective-permute-start.3 = (s32[224,128]{1,0:T(8,128)S(1)}, s32[224,128]{1,0:T(8,128)S(1)}, u32[]{:S(2)}, u32[]{:S(2)}) collective-permute-start(s32[224,128]{1,0:T(8,128)S(1)} %get-tuple-element.47), channel_id=1, source_target_pairs={{0,2},{1,3},{2,0},{3,1},{4,6},{5,7},{6,4},{7,5},{8,10},{9,11},{10,... | collective-permute-start | bytes 344072 | tf_op jit(solution)/shard_map/ppermute | solution.py:824
  21.1 1.2 %collective-permute-start.4 = (s32[224,128]{1,0:T(8,128)S(1)}, s32[224,128]{1,0:T(8,128)S(1)}, u32[]{:S(2)}, u32[]{:S(2)}) collective-permute-start(s32[224,128]{1,0:T(8,128)S(1)} %get-tuple-element.48), channel_id=1, source_target_pairs={{0,3},{1,2},{2,1},{3,0},{4,7},{5,6},{6,5},{7,4},{8,11},{9,10},{10,... | collective-permute-start | bytes 344072 | tf_op jit(solution)/shard_map/ppermute | solution.py:824
  22.3 0.2 collective-permute-start.5
  22.5 0.0 copy-done
  22.5 0.3 shard_map.50
  22.8 0.0 collective-permute-done.6.refs_1_
  22.8 0.0 collective-permute-done.7.refs_2_
  22.8 0.0 copy-done.1
  22.8 1.8 %shard_map.51 = (f32[384,128]{1,0:T(8,128)S(1)}, f32[96,128]{1,0:T(8,128)S(1)}, f32[6,240,128]{2,1,0:T(8,128)S(1)}, f32[2,240,128]{2,1,0:T(8,128)S(1)}, bf16[128...) custom-call(s32[4]{0:T(128)S(1)} %copy-done.1, ...), custom_call_target="tpu_custom_call" | custom-call | flops 8589934592 | bytes 1048576 | tf_op jit(solution)/shard_map/pallas_call | solution.py:933
  24.7 2.4 %collective-permute-start.8 = (f32[48,128]{1,0:T(8,128)S(1)}, f32[48,128]{1,0:T(8,128)S(1)}, u32[]{:S(2)}, u32[]{:S(2)}) collective-permute-start(f32[48,128]{1,0:T(8,128)S(1)} %get-tuple-element.65), channel_id=1, source_target_pairs={{0,3},{1,2},{2,1},{3,0},{4,7},{5,6},{6,5},{7,4},{8,11},{9,10},{10,... | collective-permute-start | bytes 73736 | tf_op jit(solution)/shard_map/ppermute | solution.py:824
  27.1 0.1 collective-permute-start.9
  27.2 0.2 collective-permute-done.3.refs_1_
  27.3 0.0 collective-permute-done.4.refs_2_
  27.3 0.6 %collective-permute-done.5.refs_3_ = s32[224,128]{1,0:T(8,128)S(1)} collective-permute-done((s32[224,128]{1,0:T(8,128)S(1)}, s32[224,128]{1,0:T(8,128)S(1)}, u32[]{:S(2)}, u32[]{:S(2)}) %collective-permute-start.5) | collective-permute-done | bytes 114720 | tf_op jit(solution)/shard_map/ppermute | solution.py:824
  28.0 1.2 %shard_map.52 = (f32[48,128]{1,0:T(8,128)S(1)}, bf16[48,128]{1,0:T(8,128)(2,1)S(1)}, bf16[48,128]{1,0:T(8,128)(2,1)S(1)}) custom-call(s32[4]{0:T(128)S(1)} %copy-done.1, s32[224,128]{1,0:T(8,128)S(1)} %get-tuple-element.46.refs_0_, s32[224,128]{1,0:T(8,128)S(1)} %collective-permute-done.3.refs_1_, s32[224,128]{1,0:T(8,128)S(1)} %collective-permute-done.4.refs_2_, ...), custom_call_target="tpu_custom_call" | custom-call | flops 67108864 | bytes 2097152 | tf_op jit(solution)/shard_map/pallas_call | solution.py:954
  29.2 1.1 %collective-permute-start.10 = (bf16[48,128]{1,0:T(8,128)(2,1)S(1)}, bf16[48,128]{1,0:T(8,128)(2,1)S(1)}, u32[]{:S(2)}, u32[]{:S(2)}) collective-permute-start(bf16[48,128]{1,0:T(8,128)(2,1)S(1)} %get-tuple-element.67), channel_id=1, source_target_pairs={{0,1},{1,0},{2,3},{3,2},{4,5},{5,4},{6,7},{7,6},{8,9},{9,8},{10,11... | collective-permute-start | bytes 36872 | tf_op jit(solution)/shard_map/ppermute | solution.py:824
  30.3 3.7 %collective-permute-start.11 = (bf16[48,128]{1,0:T(8,128)(2,1)S(1)}, bf16[48,128]{1,0:T(8,128)(2,1)S(1)}, u32[]{:S(2)}, u32[]{:S(2)}) collective-permute-start(bf16[48,128]{1,0:T(8,128)(2,1)S(1)} %get-tuple-element.68), channel_id=1, source_target_pairs={{0,4},{1,5},{4,8},{5,9},{6,2},{7,3},{8,12},{9,13},{10,6},{11,7},{1... | collective-permute-start | bytes 36872 | tf_op jit(solution)/shard_map/ppermute | solution.py:924
  34.0 0.0 collective-permute-done.8.refs_1_
  34.0 0.0 collective-permute-done.9.refs_2_
  34.0 0.0 collective-permute-done.10.refs_3_
  34.0 0.8 %collective-permute-done.11.refs_4_ = bf16[48,128]{1,0:T(8,128)(2,1)S(1)} collective-permute-done((bf16[48,128]{1,0:T(8,128)(2,1)S(1)}, bf16[48,128]{1,0:T(8,128)(2,1)S(1)}, u32[]{:S(2)}, u32[]{:S(2)}) %collective-permute-start.11) | collective-permute-done | bytes 12320 | tf_op jit(solution)/shard_map/ppermute | solution.py:924
  34.8 0.7 %shard_map.53 = f32[50,96]{1,0:T(8,128)} custom-call(f32[48,128]{1,0:T(8,128)S(1)} %get-tuple-element.64.refs_0_, f32[48,128]{1,0:T(8,128)S(1)} %collective-permute-done.8.refs_1_, f32[48,128]{1,0:T(8,128)S(1)} %collective-permute-done.9.refs_2_, bf16[48,128]{1,0:T(8,128)(2,1)S(1)} %collective-permute-done.10.refs_3_, ...), custom_call_target="tpu_custom_call" | custom-call | tf_op jit(solution)/shard_map/pallas_call | solution.py:963
  (2 shorter events, 0.0 us)
Async XLA Ops:
  0.0 6.7 %copy-start.2 = (s32[2048]{0:T(1024)S(1)}, s32[2048]{0:T(1024)}, u32[]{:S(2)}) copy-start(s32[2048]{0:T(1024)} %param.5) | copy-start | bytes 24580
  2.1 9.4 %collective-permute-start.1 = (bf16[1056,384]{1,0:T(8,128)(2,1)S(1)}, bf16[1056,384]{1,0:T(8,128)(2,1)S(1)}, u32[]{:S(2)}, u32[]{:S(2)}) collective-permute-start(bf16[1056,384]{1,0:T(8,128)(2,1)S(1)} %get-tuple-element.40), channel_id=1, source_target_pairs={{0,4},{4,0},{8,12},{12,8},{1,5},{5,1},{9,13},{13,9},{2,6},{6,2},{1... | collective-permute-start | bytes 2433032 | tf_op jit(solution)/shard_map/ppermute | solution.py:833
  2.3 14.7 %collective-permute-start = (bf16[1056,384]{1,0:T(8,128)(2,1)S(1)}, bf16[1056,384]{1,0:T(8,128)(2,1)S(1)}, u32[]{:S(2)}, u32[]{:S(2)}) collective-permute-start(bf16[1056,384]{1,0:T(8,128)(2,1)S(1)} %get-tuple-element.39), channel_id=1, source_target_pairs={{4,8},{8,4},{5,9},{9,5},{6,10},{10,6},{7,11},{11,7},{20,24},{24,20... | collective-permute-start | bytes 2433032 | tf_op jit(solution)/shard_map/ppermute | solution.py:833
  7.9 4.4 %collective-permute-start.2 = (s32[152,128]{1,0:T(8,128)S(1)}, s32[152,128]{1,0:T(8,128)S(1)}, u32[]{:S(2)}, u32[]{:S(2)}) collective-permute-start(s32[152,128]{1,0:T(8,128)S(1)} %get-tuple-element.45), channel_id=1, source_target_pairs={{0,1},{1,0},{2,3},{3,2},{4,5},{5,4},{6,7},{7,6},{8,9},{9,8},{10,11... | collective-permute-start | bytes 233480 | tf_op jit(solution)/shard_map/ppermute | solution.py:824
  9.3 13.6 %collective-permute-start.6 = (s32[152,128]{1,0:T(8,128)S(1)}, s32[152,128]{1,0:T(8,128)S(1)}, u32[]{:S(2)}, u32[]{:S(2)}) collective-permute-start(s32[152,128]{1,0:T(8,128)S(1)} %get-tuple-element.51), channel_id=1, source_target_pairs={{0,3},{1,2},{2,1},{3,0},{4,7},{5,6},{6,5},{7,4},{8,11},{9,10},{10,... | collective-permute-start | bytes 233480 | tf_op jit(solution)/shard_map/ppermute | solution.py:824
  11.4 11.4 %collective-permute-start.7 = (s32[152,128]{1,0:T(8,128)S(1)}, s32[152,128]{1,0:T(8,128)S(1)}, u32[]{:S(2)}, u32[]{:S(2)}) collective-permute-start(s32[152,128]{1,0:T(8,128)S(1)} %get-tuple-element.52), channel_id=1, source_target_pairs={{0,2},{1,3},{2,0},{3,1},{4,6},{5,7},{6,4},{7,5},{8,10},{9,11},{10,... | collective-permute-start | bytes 233480 | tf_op jit(solution)/shard_map/ppermute | solution.py:824
  12.2 10.3 %copy-start = (s32[50,384]{1,0:T(8,128)S(1)}, s32[50,384]{1,0:T(8,128)}, u32[]{:S(2)}) copy-start(s32[50,384]{1,0:T(8,128)} %annot_ref.3) | copy-start | bytes 230404
  17.0 5.9 %copy-start.1 = (s32[4]{0:T(128)S(1)}, s32[4]{0:T(128)}, u32[]{:S(2)}) copy-start(s32[4]{0:T(128)} %reach_ref.3) | copy-start | bytes 52
  18.2 9.1 %collective-permute-start.3 = (s32[224,128]{1,0:T(8,128)S(1)}, s32[224,128]{1,0:T(8,128)S(1)}, u32[]{:S(2)}, u32[]{:S(2)}) collective-permute-start(s32[224,128]{1,0:T(8,128)S(1)} %get-tuple-element.47), channel_id=1, source_target_pairs={{0,2},{1,3},{2,0},{3,1},{4,6},{5,7},{6,4},{7,5},{8,10},{9,11},{10,... | collective-permute-start | bytes 344072 | tf_op jit(solution)/shard_map/ppermute | solution.py:824
  21.1 6.3 %collective-permute-start.4 = (s32[224,128]{1,0:T(8,128)S(1)}, s32[224,128]{1,0:T(8,128)S(1)}, u32[]{:S(2)}, u32[]{:S(2)}) collective-permute-start(s32[224,128]{1,0:T(8,128)S(1)} %get-tuple-element.48), channel_id=1, source_target_pairs={{0,3},{1,2},{2,1},{3,0},{4,7},{5,6},{6,5},{7,4},{8,11},{9,10},{10,... | collective-permute-start | bytes 344072 | tf_op jit(solution)/shard_map/ppermute | solution.py:824
  22.3 5.7 %collective-permute-start.5 = (s32[224,128]{1,0:T(8,128)S(1)}, s32[224,128]{1,0:T(8,128)S(1)}, u32[]{:S(2)}, u32[]{:S(2)}) collective-permute-start(s32[224,128]{1,0:T(8,128)S(1)} %get-tuple-element.49), channel_id=1, source_target_pairs={{0,1},{1,0},{2,3},{3,2},{4,5},{5,4},{6,7},{7,6},{8,9},{9,8},{10,11... | collective-permute-start | bytes 344072 | tf_op jit(solution)/shard_map/ppermute | solution.py:824
  24.7 9.3 %collective-permute-start.8 = (f32[48,128]{1,0:T(8,128)S(1)}, f32[48,128]{1,0:T(8,128)S(1)}, u32[]{:S(2)}, u32[]{:S(2)}) collective-permute-start(f32[48,128]{1,0:T(8,128)S(1)} %get-tuple-element.65), channel_id=1, source_target_pairs={{0,3},{1,2},{2,1},{3,0},{4,7},{5,6},{6,5},{7,4},{8,11},{9,10},{10,... | collective-permute-start | bytes 73736 | tf_op jit(solution)/shard_map/ppermute | solution.py:824
  27.1 6.9 %collective-permute-start.9 = (f32[48,128]{1,0:T(8,128)S(1)}, f32[48,128]{1,0:T(8,128)S(1)}, u32[]{:S(2)}, u32[]{:S(2)}) collective-permute-start(f32[48,128]{1,0:T(8,128)S(1)} %get-tuple-element.66), channel_id=1, source_target_pairs={{0,2},{1,3},{2,0},{3,1},{4,6},{5,7},{6,4},{7,5},{8,10},{9,11},{10,... | collective-permute-start | bytes 73736 | tf_op jit(solution)/shard_map/ppermute | solution.py:824
  29.2 4.8 %collective-permute-start.10 = (bf16[48,128]{1,0:T(8,128)(2,1)S(1)}, bf16[48,128]{1,0:T(8,128)(2,1)S(1)}, u32[]{:S(2)}, u32[]{:S(2)}) collective-permute-start(bf16[48,128]{1,0:T(8,128)(2,1)S(1)} %get-tuple-element.67), channel_id=1, source_target_pairs={{0,1},{1,0},{2,3},{3,2},{4,5},{5,4},{6,7},{7,6},{8,9},{9,8},{10,11... | collective-permute-start | bytes 36872 | tf_op jit(solution)/shard_map/ppermute | solution.py:824
  30.3 4.5 %collective-permute-start.11 = (bf16[48,128]{1,0:T(8,128)(2,1)S(1)}, bf16[48,128]{1,0:T(8,128)(2,1)S(1)}, u32[]{:S(2)}, u32[]{:S(2)}) collective-permute-start(bf16[48,128]{1,0:T(8,128)(2,1)S(1)} %get-tuple-element.68), channel_id=1, source_target_pairs={{0,4},{1,5},{4,8},{5,9},{6,2},{7,3},{8,12},{9,13},{10,6},{11,7},{1... | collective-permute-start | bytes 36872 | tf_op jit(solution)/shard_map/ppermute | solution.py:924

commit v19 on v18

--- a/solution.py
+++ b/solution.py
@@ -284,11 +284,11 @@
 
 
 def far_kernel(
-    groups, share, weighted_ref, side_ref, whole_ref, shared_ref, totals_ref, mine_ref, nearest_ref, own_sum_ref, *refs
+    groups, share, weighted_ref, side_ref, whole_ref, shared_ref, totals_ref, mine_ref, first_ref, own_sum_ref, *refs
 ):
     targets, (tile, folded, flipped, spare, extras) = refs[:groups], refs[groups:]
     snps = tile.shape[1]
-    own_sum_ref[...] = mine_ref[...] + nearest_ref[...]
+    own_sum_ref[...] = mine_ref[...] + first_ref[...]
     whole, shared = side_dot(weighted_ref, side_ref)
     left = iota(shared.shape, 1) < HALF_LANES
 
@@ -877,7 +877,8 @@
         flops=2 * rows * snps * snps,
         moved=rows * snps * 4,
     )(alleles, labels.reshape(1, rows))
-    own_parts = [own_parts[0]] + [around(own_parts[k], groups, k) for k in range(groups - 1, 0, -1)]
+    order = (2, 3, 1) if by_column else range(groups - 1, 0, -1)
+    own_parts = [own_parts[0]] + [around(own_parts[k], groups, k) for k in order]
 
     near_shapes = [own_share_counts] + [near_share_counts if by_column else shape((share + 8, snps), i32)] * groups
     if by_column:
@@ -896,7 +897,7 @@
                 pltpu.VMEM((8 * groups, LANES), i32),
             ],
             **work,
-        )(weighted, from_far, *close_counts, totals, own_parts[0], own_parts[-1])
+        )(weighted, from_far, *close_counts, totals, *own_parts[:2])
     else:
         own_sum, *near_parts = call(
             functools.partial(near_kernel, groups, share),
@@ -906,7 +907,6 @@
             flops=2 * rows * snps * snps,
             moved=rows * snps * 4,
         )(weighted, from_far, from_close, totals, *own_parts)
-    order = (2, 3, 1) if by_column else range(groups - 1, 0, -1)
     near_parts = [near_parts[0]] + [around(near_parts[k], groups, k) for k in order]
 
     by_snp = shape((snps, LANES), f32)
@@ -942,14 +942,14 @@
                 shape((6, share, 2 * LANES), f32),
                 shape((share, 2 * LANES), f32),
                 shape((2 * LANES, LANES), bf16),
-                packed_share,
-                packed_share,
+                sent,
+                sent,
             ],
             [SMEM] + [VMEM] * (groups + 1),
             [pltpu.VMEM((snps, LANES), f32)],
             flops=1 << 33,
             moved=1 << 20,
-        )(reach, own_sum, *own_parts[1:-1], own_annots, near_annots)
+        )(reach, own_sum, *own_parts[2:], own_annots, near_annots)
         parts = [around(third, groups, 3), around(second, groups, 2)]
         own_scores, send, there = call(
             functools.partial(near_score_kernel, groups, share),

time: 35.7 us -> 35.8 us (level)
    ppermute x9, starting transfers between devices: 11.5 us -> 12.1 us  [around(): lax.ppermute(value, 'hap', [(source, partner(source, step, groups)) for s...]
    ppermute x1, starting transfers between devices: 3.69 us -> 3.17 us  [to_neighbour(): return lax.ppermute(value, ('snp', 'hap'), pairs)]
  transfers between devices with their start and end apart: 12 -> 12, of which waited for: 4 -> 5; matrix products, arithmetic and copies ran while one was open for 0% -> 0% of each run, Pallas kernels for 18% -> 18%
where the time goes in v19:
time: 35.8 us; the launch traced here: 35.3 us
  starting transfers between devices  19.9 us (56%)
  Pallas kernels  9.25 us (26%)
  waiting for transfers between devices  6.01 us (17%)
    ppermute x9, starting transfers between devices, around(): lax.ppermute(value, 'hap', [(source, partner(source, step, groups)) for s...  12.1 us
    ppermute x2, waiting for transfers between devices, swapped(): return lax.ppermute(value, 'snp', pairs)  4.6 us
    ppermute x2, starting transfers between devices, swapped(): return lax.ppermute(value, 'snp', pairs)  4.59 us
    ppermute x1, starting transfers between devices, to_neighbour(): return lax.ppermute(value, ('snp', 'hap'), pairs)  3.17 us
    pallas_call x1, Pallas kernels, per_device(): call(prepare_kernel, [shape((rows, snps), bf16), packed, packed], [HBM, H...  2.14 us
    pallas_call x1, Pallas kernels, per_device(): call(functools.partial(own_score_kernel, groups, share), [by_snp, shape((...  1.8 us
    pallas_call x1, Pallas kernels, per_device(): call(functools.partial(far_kernel, groups, share), near_shapes, [VMEM] *...  1.27 us
    pallas_call x1, Pallas kernels, per_device(): call(functools.partial(near_score_kernel, groups, share), [packed_share,...  1.23 us
  transfers between devices with their start and end apart: 12, of which 5 were waited for; matrix products, arithmetic and copies ran while one was open for 0% of the time, Pallas kernels for 18%

profile of v19, /device:TPU:1, one launch (start us, length us, event | category | flops | bytes accessed | tf_op | source)
XLA Modules:
  0.0 35.3 jit_solution(9072504122188822558)
XLA Ops:
  0.0 0.0 copy-start.2
  0.0 2.1 %shard_map.46 = (bf16[2048,384]{1,0:T(8,128)(2,1)S(1)}, bf16[1056,384]{1,0:T(8,128)(2,1)S(1)}, bf16[1056,384]{1,0:T(8,128)(2,1)S(1)}) custom-call(s32[2048,384]{1,0:T(8,128)} %hap_ref.1, s32[50,384]{1,0:T(8,128)} %annot_ref.3), custom_call_target="tpu_custom_call" | custom-call | bytes 6291456 | tf_op jit(solution)/shard_map/pallas_call | solution.py:852
  2.1 0.1 collective-permute-start.1
  2.3 4.5 %collective-permute-start = (bf16[1056,384]{1,0:T(8,128)(2,1)S(1)}, bf16[1056,384]{1,0:T(8,128)(2,1)S(1)}, u32[]{:S(2)}, u32[]{:S(2)}) collective-permute-start(bf16[1056,384]{1,0:T(8,128)(2,1)S(1)} %get-tuple-element.39), channel_id=1, source_target_pairs={{4,8},{8,4},{5,9},{9,5},{6,10},{10,6},{7,11},{11,7},{20,24},{24,20... | collective-permute-start | bytes 2433032 | tf_op jit(solution)/shard_map/ppermute | solution.py:833
  6.7 0.0 copy-done.2
  6.8 1.1 %shard_map.47 = (bf16[400,2048]{1,0:T(8,128)(2,1)S(1)}, f32[8,384]{1,0:T(8,128)S(1)}, s32[152,128]{1,0:T(8,128)S(1)}, s32[152,128]{1,0:T(8,128)S(1)}, s32[152,128]{1,0:T(8,128)S(1)}, /*index=5*/s32[152,128]{1,0:T(8,128)S(1)}) custom-call(bf16[2048,384]{1,0:T(8,128)(2,1)S(1)} %get-tuple-element.37.alleles_ref, s32[1,2048]{1,0:T(1,128)S(1)} %bitcast.1), custom_call_target="tpu_custom_call" | custom-call | flops 603979776 | bytes 3145728 | tf_op jit(solution)/shard_map/pallas_call | solution.py:872
  7.9 2.4 %collective-permute-start.2 = (s32[152,128]{1,0:T(8,128)S(1)}, s32[152,128]{1,0:T(8,128)S(1)}, u32[]{:S(2)}, u32[]{:S(2)}) collective-permute-start(s32[152,128]{1,0:T(8,128)S(1)} %get-tuple-element.45), channel_id=1, source_target_pairs={{0,2},{1,3},{2,0},{3,1},{4,6},{5,7},{6,4},{7,5},{8,10},{9,11},{10,... | collective-permute-start | bytes 233480 | tf_op jit(solution)/shard_map/ppermute | solution.py:824
  10.3 1.1 %collective-permute-start.6 = (s32[152,128]{1,0:T(8,128)S(1)}, s32[152,128]{1,0:T(8,128)S(1)}, u32[]{:S(2)}, u32[]{:S(2)}) collective-permute-start(s32[152,128]{1,0:T(8,128)S(1)} %get-tuple-element.51), channel_id=1, source_target_pairs={{0,3},{1,2},{2,1},{3,0},{4,7},{5,6},{6,5},{7,4},{8,11},{9,10},{10,... | collective-permute-start | bytes 233480 | tf_op jit(solution)/shard_map/ppermute | solution.py:824
  11.4 0.2 collective-permute-start.7
  11.6 0.0 collective-permute-done.1.side_ref
  11.6 0.7 %shard_map.48 = (f32[400,128]{1,0:T(8,128)S(1)}, f32[400,128]{1,0:T(8,128)S(1)}) custom-call(bf16[400,2048]{1,0:T(8,128)(2,1)S(1)} %get-tuple-element.38.weighted_ref, bf16[1056,384]{1,0:T(8,128)(2,1)S(1)} %collective-permute-done.1.side_ref), custom_call_target="tpu_custom_call" | custom-call | flops 402653184 | bytes 3145728 | tf_op jit(solution)/shard_map/pallas_call | solution.py:887
  12.2 0.0 copy-start
  12.2 0.1 collective-permute-done.2.first_ref
  12.4 4.6 %collective-permute-done.side_ref = bf16[1056,384]{1,0:T(8,128)(2,1)S(1)} collective-permute-done((bf16[1056,384]{1,0:T(8,128)(2,1)S(1)}, bf16[1056,384]{1,0:T(8,128)(2,1)S(1)}, u32[]{:S(2)}, u32[]{:S(2)}) %collective-permute-start) | collective-permute-done | bytes 811040 | tf_op jit(solution)/shard_map/ppermute | solution.py:833
  17.0 0.0 copy-start.1
  17.0 1.3 %shard_map.49 = (s32[152,128]{1,0:T(8,128)S(1)}, s32[224,128]{1,0:T(8,128)S(1)}, s32[224,128]{1,0:T(8,128)S(1)}, s32[224,128]{1,0:T(8,128)S(1)}, s32[224,128]{1,0:T(8,128)S(1)}) custom-call(bf16[400,2048]{1,0:T(8,128)(2,1)S(1)} %get-tuple-element.38.weighted_ref, bf16[1056,384]{1,0:T(8,128)(2,1)S(1)} %collective-permute-done.side_ref, ...), custom_call_target="tpu_custom_call" | custom-call | flops 402653184 | bytes 3145728 | tf_op jit(solution)/shard_map/pallas_call | solution.py:888
  18.2 3.0 %collective-permute-start.3 = (s32[224,128]{1,0:T(8,128)S(1)}, s32[224,128]{1,0:T(8,128)S(1)}, u32[]{:S(2)}, u32[]{:S(2)}) collective-permute-start(s32[224,128]{1,0:T(8,128)S(1)} %get-tuple-element.47), channel_id=1, source_target_pairs={{0,2},{1,3},{2,0},{3,1},{4,6},{5,7},{6,4},{7,5},{8,10},{9,11},{10,... | collective-permute-start | bytes 344072 | tf_op jit(solution)/shard_map/ppermute | solution.py:824
  21.2 0.8 %collective-permute-start.4 = (s32[224,128]{1,0:T(8,128)S(1)}, s32[224,128]{1,0:T(8,128)S(1)}, u32[]{:S(2)}, u32[]{:S(2)}) collective-permute-start(s32[224,128]{1,0:T(8,128)S(1)} %get-tuple-element.48), channel_id=1, source_target_pairs={{0,3},{1,2},{2,1},{3,0},{4,7},{5,6},{6,5},{7,4},{8,11},{9,10},{10,... | collective-permute-start | bytes 344072 | tf_op jit(solution)/shard_map/ppermute | solution.py:824
  22.0 0.2 collective-permute-start.5
  22.2 0.0 copy-done
  22.2 0.3 shard_map.50
  22.5 0.0 collective-permute-done.6.refs_1_
  22.5 0.0 collective-permute-done.7.refs_2_
  22.5 0.0 copy-done.1
  22.5 1.8 %shard_map.51 = (f32[384,128]{1,0:T(8,128)S(1)}, f32[96,128]{1,0:T(8,128)S(1)}, f32[6,240,128]{2,1,0:T(8,128)S(1)}, f32[2,240,128]{2,1,0:T(8,128)S(1)}, bf16[128...) custom-call(s32[4]{0:T(128)S(1)} %copy-done.1, ...), custom_call_target="tpu_custom_call" | custom-call | flops 8589934592 | bytes 1048576 | tf_op jit(solution)/shard_map/pallas_call | solution.py:933
  24.3 2.4 %collective-permute-start.8 = (bf16[48,128]{1,0:T(8,128)(2,1)S(1)}, bf16[48,128]{1,0:T(8,128)(2,1)S(1)}, u32[]{:S(2)}, u32[]{:S(2)}) collective-permute-start(bf16[48,128]{1,0:T(8,128)(2,1)S(1)} %get-tuple-element.65), channel_id=1, source_target_pairs={{0,3},{1,2},{2,1},{3,0},{4,7},{5,6},{6,5},{7,4},{8,11},{9,10},{10,... | collective-permute-start | bytes 36872 | tf_op jit(solution)/shard_map/ppermute | solution.py:824
  26.8 0.2 collective-permute-start.9
  27.0 0.3 collective-permute-done.3.refs_1_
  27.3 0.0 collective-permute-done.4.refs_2_
  27.3 0.2 collective-permute-done.5.refs_3_
  27.5 1.2 %shard_map.52 = (f32[48,128]{1,0:T(8,128)S(1)}, bf16[48,128]{1,0:T(8,128)(2,1)S(1)}, bf16[48,128]{1,0:T(8,128)(2,1)S(1)}) custom-call(s32[4]{0:T(128)S(1)} %copy-done.1, s32[224,128]{1,0:T(8,128)S(1)} %get-tuple-element.46.refs_0_, s32[224,128]{1,0:T(8,128)S(1)} %collective-permute-done.3.refs_1_, s32[224,128]{1,0:T(8,128)S(1)} %collective-permute-done.4.refs_2_, ...), custom_call_target="tpu_custom_call" | custom-call | flops 67108864 | bytes 2097152 | tf_op jit(solution)/shard_map/pallas_call | solution.py:954
  28.8 1.8 %collective-permute-start.10 = (bf16[48,128]{1,0:T(8,128)(2,1)S(1)}, bf16[48,128]{1,0:T(8,128)(2,1)S(1)}, u32[]{:S(2)}, u32[]{:S(2)}) collective-permute-start(bf16[48,128]{1,0:T(8,128)(2,1)S(1)} %get-tuple-element.67), channel_id=1, source_target_pairs={{0,1},{1,0},{2,3},{3,2},{4,5},{5,4},{6,7},{7,6},{8,9},{9,8},{10,11... | collective-permute-start | bytes 36872 | tf_op jit(solution)/shard_map/ppermute | solution.py:824
  30.5 3.2 %collective-permute-start.11 = (bf16[48,128]{1,0:T(8,128)(2,1)S(1)}, bf16[48,128]{1,0:T(8,128)(2,1)S(1)}, u32[]{:S(2)}, u32[]{:S(2)}) collective-permute-start(bf16[48,128]{1,0:T(8,128)(2,1)S(1)} %get-tuple-element.68), channel_id=1, source_target_pairs={{0,4},{1,5},{4,8},{5,9},{6,2},{7,3},{8,12},{9,13},{10,6},{11,7},{1... | collective-permute-start | bytes 36872 | tf_op jit(solution)/shard_map/ppermute | solution.py:924
  33.7 0.0 collective-permute-done.8.refs_1_
  33.7 0.0 collective-permute-done.9.refs_2_
  33.7 0.0 collective-permute-done.10.refs_3_
  33.8 0.8 %collective-permute-done.11.refs_4_ = bf16[48,128]{1,0:T(8,128)(2,1)S(1)} collective-permute-done((bf16[48,128]{1,0:T(8,128)(2,1)S(1)}, bf16[48,128]{1,0:T(8,128)(2,1)S(1)}, u32[]{:S(2)}, u32[]{:S(2)}) %collective-permute-start.11) | collective-permute-done | bytes 12320 | tf_op jit(solution)/shard_map/ppermute | solution.py:924
  34.5 0.8 %shard_map.53 = f32[50,96]{1,0:T(8,128)} custom-call(f32[48,128]{1,0:T(8,128)S(1)} %get-tuple-element.64.refs_0_, bf16[48,128]{1,0:T(8,128)(2,1)S(1)} %collective-permute-done.8.refs_1_, bf16[48,128]{1,0:T(8,128)(2,1)S(1)} %collective-permute-done.9.refs_2_, bf16[48,128]{1,0:T(8,128)(2,1)S(1)} %collective-permute-done.10.refs_3_, ...), custom_call_target="tpu_custom_call" | custom-call | tf_op jit(solution)/shard_map/pallas_call | solution.py:963
  (2 shorter events, 0.0 us)
Async XLA Ops:
  0.0 6.7 %copy-start.2 = (s32[2048]{0:T(1024)S(1)}, s32[2048]{0:T(1024)}, u32[]{:S(2)}) copy-start(s32[2048]{0:T(1024)} %param.5) | copy-start | bytes 24580
  2.1 9.4 %collective-permute-start.1 = (bf16[1056,384]{1,0:T(8,128)(2,1)S(1)}, bf16[1056,384]{1,0:T(8,128)(2,1)S(1)}, u32[]{:S(2)}, u32[]{:S(2)}) collective-permute-start(bf16[1056,384]{1,0:T(8,128)(2,1)S(1)} %get-tuple-element.40), channel_id=1, source_target_pairs={{0,4},{4,0},{8,12},{12,8},{1,5},{5,1},{9,13},{13,9},{2,6},{6,2},{1... | collective-permute-start | bytes 2433032 | tf_op jit(solution)/shard_map/ppermute | solution.py:833
  2.3 14.7 %collective-permute-start = (bf16[1056,384]{1,0:T(8,128)(2,1)S(1)}, bf16[1056,384]{1,0:T(8,128)(2,1)S(1)}, u32[]{:S(2)}, u32[]{:S(2)}) collective-permute-start(bf16[1056,384]{1,0:T(8,128)(2,1)S(1)} %get-tuple-element.39), channel_id=1, source_target_pairs={{4,8},{8,4},{5,9},{9,5},{6,10},{10,6},{7,11},{11,7},{20,24},{24,20... | collective-permute-start | bytes 2433032 | tf_op jit(solution)/shard_map/ppermute | solution.py:833
  7.9 4.5 %collective-permute-start.2 = (s32[152,128]{1,0:T(8,128)S(1)}, s32[152,128]{1,0:T(8,128)S(1)}, u32[]{:S(2)}, u32[]{:S(2)}) collective-permute-start(s32[152,128]{1,0:T(8,128)S(1)} %get-tuple-element.45), channel_id=1, source_target_pairs={{0,2},{1,3},{2,0},{3,1},{4,6},{5,7},{6,4},{7,5},{8,10},{9,11},{10,... | collective-permute-start | bytes 233480 | tf_op jit(solution)/shard_map/ppermute | solution.py:824
  10.3 12.2 %collective-permute-start.6 = (s32[152,128]{1,0:T(8,128)S(1)}, s32[152,128]{1,0:T(8,128)S(1)}, u32[]{:S(2)}, u32[]{:S(2)}) collective-permute-start(s32[152,128]{1,0:T(8,128)S(1)} %get-tuple-element.51), channel_id=1, source_target_pairs={{0,3},{1,2},{2,1},{3,0},{4,7},{5,6},{6,5},{7,4},{8,11},{9,10},{10,... | collective-permute-start | bytes 233480 | tf_op jit(solution)/shard_map/ppermute | solution.py:824
  11.4 11.2 %collective-permute-start.7 = (s32[152,128]{1,0:T(8,128)S(1)}, s32[152,128]{1,0:T(8,128)S(1)}, u32[]{:S(2)}, u32[]{:S(2)}) collective-permute-start(s32[152,128]{1,0:T(8,128)S(1)} %get-tuple-element.52), channel_id=1, source_target_pairs={{0,1},{1,0},{2,3},{3,2},{4,5},{5,4},{6,7},{7,6},{8,9},{9,8},{10,11... | collective-permute-start | bytes 233480 | tf_op jit(solution)/shard_map/ppermute | solution.py:824
  12.2 10.0 %copy-start = (s32[50,384]{1,0:T(8,128)S(1)}, s32[50,384]{1,0:T(8,128)}, u32[]{:S(2)}) copy-start(s32[50,384]{1,0:T(8,128)} %annot_ref.3) | copy-start | bytes 230404
  17.0 5.6 %copy-start.1 = (s32[4]{0:T(128)S(1)}, s32[4]{0:T(128)}, u32[]{:S(2)}) copy-start(s32[4]{0:T(128)} %reach_ref.3) | copy-start | bytes 52
  18.2 9.1 %collective-permute-start.3 = (s32[224,128]{1,0:T(8,128)S(1)}, s32[224,128]{1,0:T(8,128)S(1)}, u32[]{:S(2)}, u32[]{:S(2)}) collective-permute-start(s32[224,128]{1,0:T(8,128)S(1)} %get-tuple-element.47), channel_id=1, source_target_pairs={{0,2},{1,3},{2,0},{3,1},{4,6},{5,7},{6,4},{7,5},{8,10},{9,11},{10,... | collective-permute-start | bytes 344072 | tf_op jit(solution)/shard_map/ppermute | solution.py:824
  21.2 6.1 %collective-permute-start.4 = (s32[224,128]{1,0:T(8,128)S(1)}, s32[224,128]{1,0:T(8,128)S(1)}, u32[]{:S(2)}, u32[]{:S(2)}) collective-permute-start(s32[224,128]{1,0:T(8,128)S(1)} %get-tuple-element.48), channel_id=1, source_target_pairs={{0,3},{1,2},{2,1},{3,0},{4,7},{5,6},{6,5},{7,4},{8,11},{9,10},{10,... | collective-permute-start | bytes 344072 | tf_op jit(solution)/shard_map/ppermute | solution.py:824
  22.0 5.5 %collective-permute-start.5 = (s32[224,128]{1,0:T(8,128)S(1)}, s32[224,128]{1,0:T(8,128)S(1)}, u32[]{:S(2)}, u32[]{:S(2)}) collective-permute-start(s32[224,128]{1,0:T(8,128)S(1)} %get-tuple-element.49), channel_id=1, source_target_pairs={{0,1},{1,0},{2,3},{3,2},{4,5},{5,4},{6,7},{7,6},{8,9},{9,8},{10,11... | collective-permute-start | bytes 344072 | tf_op jit(solution)/shard_map/ppermute | solution.py:824
  24.3 9.4 %collective-permute-start.8 = (bf16[48,128]{1,0:T(8,128)(2,1)S(1)}, bf16[48,128]{1,0:T(8,128)(2,1)S(1)}, u32[]{:S(2)}, u32[]{:S(2)}) collective-permute-start(bf16[48,128]{1,0:T(8,128)(2,1)S(1)} %get-tuple-element.65), channel_id=1, source_target_pairs={{0,3},{1,2},{2,1},{3,0},{4,7},{5,6},{6,5},{7,4},{8,11},{9,10},{10,... | collective-permute-start | bytes 36872 | tf_op jit(solution)/shard_map/ppermute | solution.py:824
  26.8 6.9 %collective-permute-start.9 = (bf16[48,128]{1,0:T(8,128)(2,1)S(1)}, bf16[48,128]{1,0:T(8,128)(2,1)S(1)}, u32[]{:S(2)}, u32[]{:S(2)}) collective-permute-start(bf16[48,128]{1,0:T(8,128)(2,1)S(1)} %get-tuple-element.66), channel_id=1, source_target_pairs={{0,2},{1,3},{2,0},{3,1},{4,6},{5,7},{6,4},{7,5},{8,10},{9,11},{10,... | collective-permute-start | bytes 36872 | tf_op jit(solution)/shard_map/ppermute | solution.py:824
  28.8 5.0 %collective-permute-start.10 = (bf16[48,128]{1,0:T(8,128)(2,1)S(1)}, bf16[48,128]{1,0:T(8,128)(2,1)S(1)}, u32[]{:S(2)}, u32[]{:S(2)}) collective-permute-start(bf16[48,128]{1,0:T(8,128)(2,1)S(1)} %get-tuple-element.67), channel_id=1, source_target_pairs={{0,1},{1,0},{2,3},{3,2},{4,5},{5,4},{6,7},{7,6},{8,9},{9,8},{10,11... | collective-permute-start | bytes 36872 | tf_op jit(solution)/shard_map/ppermute | solution.py:824
  30.5 4.0 %collective-permute-start.11 = (bf16[48,128]{1,0:T(8,128)(2,1)S(1)}, bf16[48,128]{1,0:T(8,128)(2,1)S(1)}, u32[]{:S(2)}, u32[]{:S(2)}) collective-permute-start(bf16[48,128]{1,0:T(8,128)(2,1)S(1)} %get-tuple-element.68), channel_id=1, source_target_pairs={{0,4},{1,5},{4,8},{5,9},{6,2},{7,3},{8,12},{9,13},{10,6},{11,7},{1... | collective-permute-start | bytes 36872 | tf_op jit(solution)/shard_map/ppermute | solution.py:924

commit v20 on v19

--- a/solution.py
+++ b/solution.py
@@ -284,11 +284,10 @@
 
 
 def far_kernel(
-    groups, share, weighted_ref, side_ref, whole_ref, shared_ref, totals_ref, mine_ref, first_ref, own_sum_ref, *refs
+    groups, share, weighted_ref, side_ref, whole_ref, shared_ref, totals_ref, *refs
 ):
     targets, (tile, folded, flipped, spare, extras) = refs[:groups], refs[groups:]
     snps = tile.shape[1]
-    own_sum_ref[...] = mine_ref[...] + first_ref[...]
     whole, shared = side_dot(weighted_ref, side_ref)
     left = iota(shared.shape, 1) < HALF_LANES
 
@@ -587,7 +586,7 @@
 def own_score_kernel(
     groups, share, reach_ref, *refs
 ):
-    own_parts, refs = refs[: groups - 1], refs[groups - 1 :]
+    own_parts, refs = refs[:groups], refs[groups:]
     annot_ref, near_annot_ref, scores, mine_ref, rows_ref, masks_ref, columns_ref, own_rows_ref, *refs = refs
     spare_rows_ref, spare_mask_ref, spare_columns_ref, *targets, table = refs
     snps = annot_ref.shape[0]
@@ -885,10 +884,10 @@
         piece = shape((snps + 16, LANES), f32)
         work = dict(flops=4 * rows * snps * LANES, moved=rows * snps * 4)
         close_counts = call(close_kernel, [piece, piece], [VMEM] * 2, **work)(weighted, from_close)
-        own_sum, *near_parts = call(
+        near_parts = call(
             functools.partial(far_kernel, groups, share),
-            near_shapes,
-            [VMEM] * 7,
+            near_shapes[1:],
+            [VMEM] * 5,
             [
                 tile,
                 folded,
@@ -897,7 +896,7 @@
                 pltpu.VMEM((8 * groups, LANES), i32),
             ],
             **work,
-        )(weighted, from_far, *close_counts, totals, *own_parts[:2])
+        )(weighted, from_far, *close_counts, totals)
     else:
         own_sum, *near_parts = call(
             functools.partial(near_kernel, groups, share),
@@ -945,11 +944,11 @@
                 sent,
                 sent,
             ],
-            [SMEM] + [VMEM] * (groups + 1),
+            [SMEM] + [VMEM] * (groups + 2),
             [pltpu.VMEM((snps, LANES), f32)],
             flops=1 << 33,
             moved=1 << 20,
-        )(reach, own_sum, *own_parts[2:], own_annots, near_annots)
+        )(reach, *own_parts, own_annots, near_annots)
         parts = [around(third, groups, 3), around(second, groups, 2)]
         own_scores, send, there = call(
             functools.partial(near_score_kernel, groups, share),

time: 35.8 us -> 35.5 us (level)
    ppermute x1, starting transfers between devices: 3.17 us -> 4.13 us  [to_neighbour(): return lax.ppermute(value, ('snp', 'hap'), pairs)]
    ppermute x9, starting transfers between devices: 12.1 us -> 11.3 us  [around(): lax.ppermute(value, 'hap', [(source, partner(source, step, groups)) for s...]
  transfers between devices with their start and end apart: 12 -> 12, of which waited for: 5 -> 3; matrix products, arithmetic and copies ran while one was open for 0% -> 0% of each run, Pallas kernels for 18% -> 18%
where the time goes in v20:
time: 35.5 us; the launch traced here: 35.3 us
  starting transfers between devices  20 us (56%)
  Pallas kernels  9.22 us (26%)
  waiting for transfers between devices  5.97 us (17%)
    ppermute x9, starting transfers between devices, around(): lax.ppermute(value, 'hap', [(source, partner(source, step, groups)) for s...  11.3 us
    ppermute x2, waiting for transfers between devices, swapped(): return lax.ppermute(value, 'snp', pairs)  4.7 us
    ppermute x2, starting transfers between devices, swapped(): return lax.ppermute(value, 'snp', pairs)  4.59 us
    ppermute x1, starting transfers between devices, to_neighbour(): return lax.ppermute(value, ('snp', 'hap'), pairs)  4.13 us
    pallas_call x1, Pallas kernels, per_device(): call(prepare_kernel, [shape((rows, snps), bf16), packed, packed], [HBM, H...  2.14 us
    pallas_call x1, Pallas kernels, per_device(): call(functools.partial(own_score_kernel, groups, share), [by_snp, shape((...  1.8 us
    pallas_call x1, Pallas kernels, per_device(): call(functools.partial(far_kernel, groups, share), near_shapes[1:], [VMEM...  1.25 us
    pallas_call x1, Pallas kernels, per_device(): call(functools.partial(near_score_kernel, groups, share), [packed_share,...  1.22 us
  transfers between devices with their start and end apart: 12, of which 3 were waited for; matrix products, arithmetic and copies ran while one was open for 0% of the time, Pallas kernels for 18%

profile of v20, /device:TPU:1, one launch (start us, length us, event | category | flops | bytes accessed | tf_op | source)
XLA Modules:
  0.0 35.3 jit_solution(6054256573775536077)
XLA Ops:
  0.0 0.0 copy-start.2
  0.0 2.1 %shard_map.46 = (bf16[2048,384]{1,0:T(8,128)(2,1)S(1)}, bf16[1056,384]{1,0:T(8,128)(2,1)S(1)}, bf16[1056,384]{1,0:T(8,128)(2,1)S(1)}) custom-call(s32[2048,384]{1,0:T(8,128)} %hap_ref.1, s32[50,384]{1,0:T(8,128)} %annot_ref.3), custom_call_target="tpu_custom_call" | custom-call | bytes 6291456 | tf_op jit(solution)/shard_map/pallas_call | solution.py:851
  2.1 0.1 collective-permute-start.1
  2.3 4.5 %collective-permute-start = (bf16[1056,384]{1,0:T(8,128)(2,1)S(1)}, bf16[1056,384]{1,0:T(8,128)(2,1)S(1)}, u32[]{:S(2)}, u32[]{:S(2)}) collective-permute-start(bf16[1056,384]{1,0:T(8,128)(2,1)S(1)} %get-tuple-element.38), channel_id=1, source_target_pairs={{4,8},{8,4},{5,9},{9,5},{6,10},{10,6},{7,11},{11,7},{20,24},{24,20... | collective-permute-start | bytes 2433032 | tf_op jit(solution)/shard_map/ppermute | solution.py:832
  6.7 0.0 copy-done.2
  6.8 1.1 %shard_map.47 = (bf16[400,2048]{1,0:T(8,128)(2,1)S(1)}, f32[8,384]{1,0:T(8,128)S(1)}, s32[152,128]{1,0:T(8,128)S(1)}, s32[152,128]{1,0:T(8,128)S(1)}, s32[152,128]{1,0:T(8,128)S(1)}, /*index=5*/s32[152,128]{1,0:T(8,128)S(1)}) custom-call(bf16[2048,384]{1,0:T(8,128)(2,1)S(1)} %get-tuple-element.36.alleles_ref, s32[1,2048]{1,0:T(1,128)S(1)} %bitcast.1), custom_call_target="tpu_custom_call" | custom-call | flops 603979776 | bytes 3145728 | tf_op jit(solution)/shard_map/pallas_call | solution.py:871
  7.9 2.4 %collective-permute-start.5 = (s32[152,128]{1,0:T(8,128)S(1)}, s32[152,128]{1,0:T(8,128)S(1)}, u32[]{:S(2)}, u32[]{:S(2)}) collective-permute-start(s32[152,128]{1,0:T(8,128)S(1)} %get-tuple-element.48), channel_id=1, source_target_pairs={{0,2},{1,3},{2,0},{3,1},{4,6},{5,7},{6,4},{7,5},{8,10},{9,11},{10,... | collective-permute-start | bytes 233480 | tf_op jit(solution)/shard_map/ppermute | solution.py:823
  10.3 1.1 %collective-permute-start.6 = (s32[152,128]{1,0:T(8,128)S(1)}, s32[152,128]{1,0:T(8,128)S(1)}, u32[]{:S(2)}, u32[]{:S(2)}) collective-permute-start(s32[152,128]{1,0:T(8,128)S(1)} %get-tuple-element.49), channel_id=1, source_target_pairs={{0,3},{1,2},{2,1},{3,0},{4,7},{5,6},{6,5},{7,4},{8,11},{9,10},{10,... | collective-permute-start | bytes 233480 | tf_op jit(solution)/shard_map/ppermute | solution.py:823
  11.4 0.2 collective-permute-start.7
  11.6 0.0 collective-permute-done.1.side_ref
  11.6 0.7 %shard_map.48 = (f32[400,128]{1,0:T(8,128)S(1)}, f32[400,128]{1,0:T(8,128)S(1)}) custom-call(bf16[400,2048]{1,0:T(8,128)(2,1)S(1)} %get-tuple-element.37.weighted_ref, bf16[1056,384]{1,0:T(8,128)(2,1)S(1)} %collective-permute-done.1.side_ref), custom_call_target="tpu_custom_call" | custom-call | flops 402653184 | bytes 3145728 | tf_op jit(solution)/shard_map/pallas_call | solution.py:886
  12.2 0.0 copy-start
  12.2 0.0 copy-start.1
  12.3 4.7 %collective-permute-done.side_ref = bf16[1056,384]{1,0:T(8,128)(2,1)S(1)} collective-permute-done((bf16[1056,384]{1,0:T(8,128)(2,1)S(1)}, bf16[1056,384]{1,0:T(8,128)(2,1)S(1)}, u32[]{:S(2)}, u32[]{:S(2)}) %collective-permute-start) | collective-permute-done | bytes 811040 | tf_op jit(solution)/shard_map/ppermute | solution.py:832
  17.0 1.3 %shard_map.49 = (s32[224,128]{1,0:T(8,128)S(1)}, s32[224,128]{1,0:T(8,128)S(1)}, s32[224,128]{1,0:T(8,128)S(1)}, s32[224,128]{1,0:T(8,128)S(1)}) custom-call(bf16[400,2048]{1,0:T(8,128)(2,1)S(1)} %get-tuple-element.37.weighted_ref, bf16[1056,384]{1,0:T(8,128)(2,1)S(1)} %collective-permute-done.side_ref, f32[400,128]{1,0:T(8,128)S(1)} %get-tuple-element.40.whole_ref, ...), custom_call_target="tpu_custom_call" | custom-call | flops 402653184 | bytes 3145728 | tf_op jit(solution)/shard_map/pallas_call | solution.py:887
  18.2 2.8 %collective-permute-start.2 = (s32[224,128]{1,0:T(8,128)S(1)}, s32[224,128]{1,0:T(8,128)S(1)}, u32[]{:S(2)}, u32[]{:S(2)}) collective-permute-start(s32[224,128]{1,0:T(8,128)S(1)} %get-tuple-element.44), channel_id=1, source_target_pairs={{0,2},{1,3},{2,0},{3,1},{4,6},{5,7},{6,4},{7,5},{8,10},{9,11},{10,... | collective-permute-start | bytes 344072 | tf_op jit(solution)/shard_map/ppermute | solution.py:823
  21.0 1.2 %collective-permute-start.3 = (s32[224,128]{1,0:T(8,128)S(1)}, s32[224,128]{1,0:T(8,128)S(1)}, u32[]{:S(2)}, u32[]{:S(2)}) collective-permute-start(s32[224,128]{1,0:T(8,128)S(1)} %get-tuple-element.45), channel_id=1, source_target_pairs={{0,3},{1,2},{2,1},{3,0},{4,7},{5,6},{6,5},{7,4},{8,11},{9,10},{10,... | collective-permute-start | bytes 344072 | tf_op jit(solution)/shard_map/ppermute | solution.py:823
  22.3 0.0 copy-done
  22.3 0.3 shard_map.50
  22.6 0.0 collective-permute-done.5.refs_1_
  22.6 0.3 collective-permute-start.4
  22.9 0.0 collective-permute-done.6.refs_2_
  22.9 0.0 collective-permute-done.7.refs_3_
  22.9 0.0 copy-done.1
  22.9 1.8 %shard_map.51 = (f32[384,128]{1,0:T(8,128)S(1)}, f32[96,128]{1,0:T(8,128)S(1)}, f32[6,240,128]{2,1,0:T(8,128)S(1)}, f32[2,240,128]{2,1,0:T(8,128)S(1)}, bf16[128...) custom-call(s32[4]{0:T(128)S(1)} %copy-done.1, ...), custom_call_target="tpu_custom_call" | custom-call | flops 8589934592 | bytes 1048576 | tf_op jit(solution)/shard_map/pallas_call | solution.py:932
  24.7 2.4 %collective-permute-start.8 = (bf16[48,128]{1,0:T(8,128)(2,1)S(1)}, bf16[48,128]{1,0:T(8,128)(2,1)S(1)}, u32[]{:S(2)}, u32[]{:S(2)}) collective-permute-start(bf16[48,128]{1,0:T(8,128)(2,1)S(1)} %get-tuple-element.63), channel_id=1, source_target_pairs={{0,3},{1,2},{2,1},{3,0},{4,7},{5,6},{6,5},{7,4},{8,11},{9,10},{10,... | collective-permute-start | bytes 36872 | tf_op jit(solution)/shard_map/ppermute | solution.py:823
  27.1 0.1 collective-permute-start.9
  27.2 0.0 collective-permute-done.2.refs_1_
  27.2 0.0 collective-permute-done.3.refs_2_
  27.2 0.5 %collective-permute-done.4.refs_3_ = s32[224,128]{1,0:T(8,128)S(1)} collective-permute-done((s32[224,128]{1,0:T(8,128)S(1)}, s32[224,128]{1,0:T(8,128)S(1)}, u32[]{:S(2)}, u32[]{:S(2)}) %collective-permute-start.4) | collective-permute-done | bytes 114720 | tf_op jit(solution)/shard_map/ppermute | solution.py:823
  27.7 1.2 %shard_map.52 = (f32[48,128]{1,0:T(8,128)S(1)}, bf16[48,128]{1,0:T(8,128)(2,1)S(1)}, bf16[48,128]{1,0:T(8,128)(2,1)S(1)}) custom-call(s32[4]{0:T(128)S(1)} %copy-done.1, s32[224,128]{1,0:T(8,128)S(1)} %get-tuple-element.43.refs_0_, s32[224,128]{1,0:T(8,128)S(1)} %collective-permute-done.2.refs_1_, s32[224,128]{1,0:T(8,128)S(1)} %collective-permute-done.3.refs_2_, ...), custom_call_target="tpu_custom_call" | custom-call | flops 67108864 | bytes 2097152 | tf_op jit(solution)/shard_map/pallas_call | solution.py:953
  28.9 0.7 %collective-permute-start.10 = (bf16[48,128]{1,0:T(8,128)(2,1)S(1)}, bf16[48,128]{1,0:T(8,128)(2,1)S(1)}, u32[]{:S(2)}, u32[]{:S(2)}) collective-permute-start(bf16[48,128]{1,0:T(8,128)(2,1)S(1)} %get-tuple-element.65), channel_id=1, source_target_pairs={{0,1},{1,0},{2,3},{3,2},{4,5},{5,4},{6,7},{7,6},{8,9},{9,8},{10,11... | collective-permute-start | bytes 36872 | tf_op jit(solution)/shard_map/ppermute | solution.py:823
  29.6 4.1 %collective-permute-start.11 = (bf16[48,128]{1,0:T(8,128)(2,1)S(1)}, bf16[48,128]{1,0:T(8,128)(2,1)S(1)}, u32[]{:S(2)}, u32[]{:S(2)}) collective-permute-start(bf16[48,128]{1,0:T(8,128)(2,1)S(1)} %get-tuple-element.66), channel_id=1, source_target_pairs={{0,4},{1,5},{4,8},{5,9},{6,2},{7,3},{8,12},{9,13},{10,6},{11,7},{1... | collective-permute-start | bytes 36872 | tf_op jit(solution)/shard_map/ppermute | solution.py:923
  33.8 0.0 collective-permute-done.8.refs_1_
  33.8 0.0 collective-permute-done.9.refs_2_
  33.8 0.0 collective-permute-done.10.refs_3_
  33.8 0.8 %collective-permute-done.11.refs_4_ = bf16[48,128]{1,0:T(8,128)(2,1)S(1)} collective-permute-done((bf16[48,128]{1,0:T(8,128)(2,1)S(1)}, bf16[48,128]{1,0:T(8,128)(2,1)S(1)}, u32[]{:S(2)}, u32[]{:S(2)}) %collective-permute-start.11) | collective-permute-done | bytes 12320 | tf_op jit(solution)/shard_map/ppermute | solution.py:923
  34.6 0.8 %shard_map.53 = f32[50,96]{1,0:T(8,128)} custom-call(f32[48,128]{1,0:T(8,128)S(1)} %get-tuple-element.62.refs_0_, bf16[48,128]{1,0:T(8,128)(2,1)S(1)} %collective-permute-done.8.refs_1_, bf16[48,128]{1,0:T(8,128)(2,1)S(1)} %collective-permute-done.9.refs_2_, bf16[48,128]{1,0:T(8,128)(2,1)S(1)} %collective-permute-done.10.refs_3_, ...), custom_call_target="tpu_custom_call" | custom-call | tf_op jit(solution)/shard_map/pallas_call | solution.py:962
  (2 shorter events, 0.0 us)
Async XLA Ops:
  0.0 6.7 %copy-start.2 = (s32[2048]{0:T(1024)S(1)}, s32[2048]{0:T(1024)}, u32[]{:S(2)}) copy-start(s32[2048]{0:T(1024)} %param.5) | copy-start | bytes 24580
  2.1 9.4 %collective-permute-start.1 = (bf16[1056,384]{1,0:T(8,128)(2,1)S(1)}, bf16[1056,384]{1,0:T(8,128)(2,1)S(1)}, u32[]{:S(2)}, u32[]{:S(2)}) collective-permute-start(bf16[1056,384]{1,0:T(8,128)(2,1)S(1)} %get-tuple-element.39), channel_id=1, source_target_pairs={{0,4},{4,0},{8,12},{12,8},{1,5},{5,1},{9,13},{13,9},{2,6},{6,2},{1... | collective-permute-start | bytes 2433032 | tf_op jit(solution)/shard_map/ppermute | solution.py:832
  2.3 14.7 %collective-permute-start = (bf16[1056,384]{1,0:T(8,128)(2,1)S(1)}, bf16[1056,384]{1,0:T(8,128)(2,1)S(1)}, u32[]{:S(2)}, u32[]{:S(2)}) collective-permute-start(bf16[1056,384]{1,0:T(8,128)(2,1)S(1)} %get-tuple-element.38), channel_id=1, source_target_pairs={{4,8},{8,4},{5,9},{9,5},{6,10},{10,6},{7,11},{11,7},{20,24},{24,20... | collective-permute-start | bytes 2433032 | tf_op jit(solution)/shard_map/ppermute | solution.py:832
  7.9 14.7 %collective-permute-start.5 = (s32[152,128]{1,0:T(8,128)S(1)}, s32[152,128]{1,0:T(8,128)S(1)}, u32[]{:S(2)}, u32[]{:S(2)}) collective-permute-start(s32[152,128]{1,0:T(8,128)S(1)} %get-tuple-element.48), channel_id=1, source_target_pairs={{0,2},{1,3},{2,0},{3,1},{4,6},{5,7},{6,4},{7,5},{8,10},{9,11},{10,... | collective-permute-start | bytes 233480 | tf_op jit(solution)/shard_map/ppermute | solution.py:823
  10.3 12.6 %collective-permute-start.6 = (s32[152,128]{1,0:T(8,128)S(1)}, s32[152,128]{1,0:T(8,128)S(1)}, u32[]{:S(2)}, u32[]{:S(2)}) collective-permute-start(s32[152,128]{1,0:T(8,128)S(1)} %get-tuple-element.49), channel_id=1, source_target_pairs={{0,3},{1,2},{2,1},{3,0},{4,7},{5,6},{6,5},{7,4},{8,11},{9,10},{10,... | collective-permute-start | bytes 233480 | tf_op jit(solution)/shard_map/ppermute | solution.py:823
  11.4 11.5 %collective-permute-start.7 = (s32[152,128]{1,0:T(8,128)S(1)}, s32[152,128]{1,0:T(8,128)S(1)}, u32[]{:S(2)}, u32[]{:S(2)}) collective-permute-start(s32[152,128]{1,0:T(8,128)S(1)} %get-tuple-element.50), channel_id=1, source_target_pairs={{0,1},{1,0},{2,3},{3,2},{4,5},{5,4},{6,7},{7,6},{8,9},{9,8},{10,11... | collective-permute-start | bytes 233480 | tf_op jit(solution)/shard_map/ppermute | solution.py:823
  12.2 10.1 %copy-start = (s32[50,384]{1,0:T(8,128)S(1)}, s32[50,384]{1,0:T(8,128)}, u32[]{:S(2)}) copy-start(s32[50,384]{1,0:T(8,128)} %annot_ref.3) | copy-start | bytes 230404
  12.2 10.6 %copy-start.1 = (s32[4]{0:T(128)S(1)}, s32[4]{0:T(128)}, u32[]{:S(2)}) copy-start(s32[4]{0:T(128)} %reach_ref.3) | copy-start | bytes 52
  18.2 9.0 %collective-permute-start.2 = (s32[224,128]{1,0:T(8,128)S(1)}, s32[224,128]{1,0:T(8,128)S(1)}, u32[]{:S(2)}, u32[]{:S(2)}) collective-permute-start(s32[224,128]{1,0:T(8,128)S(1)} %get-tuple-element.44), channel_id=1, source_target_pairs={{0,2},{1,3},{2,0},{3,1},{4,6},{5,7},{6,4},{7,5},{8,10},{9,11},{10,... | collective-permute-start | bytes 344072 | tf_op jit(solution)/shard_map/ppermute | solution.py:823
  21.0 6.2 %collective-permute-start.3 = (s32[224,128]{1,0:T(8,128)S(1)}, s32[224,128]{1,0:T(8,128)S(1)}, u32[]{:S(2)}, u32[]{:S(2)}) collective-permute-start(s32[224,128]{1,0:T(8,128)S(1)} %get-tuple-element.45), channel_id=1, source_target_pairs={{0,3},{1,2},{2,1},{3,0},{4,7},{5,6},{6,5},{7,4},{8,11},{9,10},{10,... | collective-permute-start | bytes 344072 | tf_op jit(solution)/shard_map/ppermute | solution.py:823
  22.6 5.1 %collective-permute-start.4 = (s32[224,128]{1,0:T(8,128)S(1)}, s32[224,128]{1,0:T(8,128)S(1)}, u32[]{:S(2)}, u32[]{:S(2)}) collective-permute-start(s32[224,128]{1,0:T(8,128)S(1)} %get-tuple-element.46), channel_id=1, source_target_pairs={{0,1},{1,0},{2,3},{3,2},{4,5},{5,4},{6,7},{7,6},{8,9},{9,8},{10,11... | collective-permute-start | bytes 344072 | tf_op jit(solution)/shard_map/ppermute | solution.py:823
  24.7 9.1 %collective-permute-start.8 = (bf16[48,128]{1,0:T(8,128)(2,1)S(1)}, bf16[48,128]{1,0:T(8,128)(2,1)S(1)}, u32[]{:S(2)}, u32[]{:S(2)}) collective-permute-start(bf16[48,128]{1,0:T(8,128)(2,1)S(1)} %get-tuple-element.63), channel_id=1, source_target_pairs={{0,3},{1,2},{2,1},{3,0},{4,7},{5,6},{6,5},{7,4},{8,11},{9,10},{10,... | collective-permute-start | bytes 36872 | tf_op jit(solution)/shard_map/ppermute | solution.py:823
  27.1 6.7 %collective-permute-start.9 = (bf16[48,128]{1,0:T(8,128)(2,1)S(1)}, bf16[48,128]{1,0:T(8,128)(2,1)S(1)}, u32[]{:S(2)}, u32[]{:S(2)}) collective-permute-start(bf16[48,128]{1,0:T(8,128)(2,1)S(1)} %get-tuple-element.64), channel_id=1, source_target_pairs={{0,2},{1,3},{2,0},{3,1},{4,6},{5,7},{6,4},{7,5},{8,10},{9,11},{10,... | collective-permute-start | bytes 36872 | tf_op jit(solution)/shard_map/ppermute | solution.py:823
  28.9 4.9 %collective-permute-start.10 = (bf16[48,128]{1,0:T(8,128)(2,1)S(1)}, bf16[48,128]{1,0:T(8,128)(2,1)S(1)}, u32[]{:S(2)}, u32[]{:S(2)}) collective-permute-start(bf16[48,128]{1,0:T(8,128)(2,1)S(1)} %get-tuple-element.65), channel_id=1, source_target_pairs={{0,1},{1,0},{2,3},{3,2},{4,5},{5,4},{6,7},{7,6},{8,9},{9,8},{10,11... | collective-permute-start | bytes 36872 | tf_op jit(solution)/shard_map/ppermute | solution.py:823
  29.6 5.0 %collective-permute-start.11 = (bf16[48,128]{1,0:T(8,128)(2,1)S(1)}, bf16[48,128]{1,0:T(8,128)(2,1)S(1)}, u32[]{:S(2)}, u32[]{:S(2)}) collective-permute-start(bf16[48,128]{1,0:T(8,128)(2,1)S(1)} %get-tuple-element.66), channel_id=1, source_target_pairs={{0,4},{1,5},{4,8},{5,9},{6,2},{7,3},{8,12},{9,13},{10,6},{11,7},{1... | collective-permute-start | bytes 36872 | tf_op jit(solution)/shard_map/ppermute | solution.py:923

commit v21 on v20

--- a/solution.py
+++ b/solution.py
@@ -196,14 +196,14 @@
 SPARE_NEAR = ((4, 5, 6, 7), (4, 5, 4, 5), (3, 3, 3, 3), (1, 2, 1, 2))
 
 
-def fold_spare(tile, spare):
+def fold_spare(tile, spare, first):
     owners = len(SPARE_OWN)
     snps = tile.shape[1]
     size = snps // (2 * owners)
-    count = spare.shape[0] // owners
+    count = spare.shape[0] // 2
     totals = tile[snps : snps + count - size, :]
     lane = iota((count, snps), 1)
-    for owner in range(owners):
+    for number, owner in enumerate(range(first, first + 2)):
         mixed = None
         for slot in range(owners):
             own, near = SPARE_OWN[owner][slot], SPARE_NEAR[owner][slot]
@@ -214,13 +214,14 @@
             shift = (slot - near) * size % snps
             values = pltpu.roll(values, shift, 1) if shift else values
             mixed = values if mixed is None else jnp.where(lane >= slot * size, values, mixed)
-        spare[owner * count : (owner + 1) * count, :] = to_fields(mixed[:, 0 : spare.shape[1]])
-
-
-def fold_by_column(tile, flipped, folded):
-    owners = len(LEFT_BLOCKS)
+        spare[number * count : (number + 1) * count, :] = to_fields(mixed[:, 0 : spare.shape[1]])
+
+
+def fold_by_column(tile, flipped, folded, first):
+    groups = len(LEFT_BLOCKS)
+    owners = range(first, first + groups // 2)
     snps = folded.shape[1]
-    wide = snps // owners
+    wide = snps // groups
     size = wide // 2
     shape = (size, snps)
     row, lane = iota(shape, 0), iota(shape, 1)
@@ -228,12 +229,14 @@
     def block(number):
         return tile[number * size : (number + 1) * size, :]
 
-    diagonal = block(0)
-    for number in range(1, 2 * owners):
+    diagonal, within = block(2 * first), lane - 2 * first * size
+    for number in range(2 * first + 1, 2 * first + groups):
         diagonal = jnp.where(lane >= number * size, block(number), diagonal)
+        within = jnp.where(lane >= number * size, lane - number * size, within)
+    apart = jnp.sum(jnp.where(row == within, diagonal, 0.0), axis=0, keepdims=True)
     flipped[:, 0:size] = diagonal.T
     corner = diagonal
-    for owner in range(owners):
+    for owner in owners:
         start = (2 * owner + 1) * size
         turned = jnp.concatenate(
             [flipped[start : start + size, :], jnp.zeros((size, snps - LANES), jnp.float32)], axis=1
@@ -241,23 +244,24 @@
         if owner:
             turned = pltpu.roll(turned, owner * wide, 1)
         inside = lane - owner * wide
-        other = (row <= inside) if owner < owners // 2 else (row >= inside)
+        other = (row <= inside) if first == 0 else (row >= inside)
         corner = jnp.where((inside >= 0) & (inside < size) & other, turned, corner)
     rolled = []
-    for shift in range(owners):
+    for shift in range(groups):
         mixed = None
-        for owner in range(owners):
-            slot = (owner + shift) % owners
+        for owner in owners:
+            slot = (owner + shift) % groups
             left = block(LEFT_BLOCKS[owner][slot]) if slot else corner
             start = owner * wide
             mixed = left if mixed is None else jnp.where(lane >= start, left, mixed)
             mixed = jnp.where(lane >= start + size, block(RIGHT_BLOCKS[owner][slot]), mixed)
         rolled.append(pltpu.roll(mixed, shift * wide, 1) if shift else mixed)
-    for owner in range(owners):
-        mixed = rolled[(0 - owner) % owners]
-        for slot in range(1, owners):
-            mixed = jnp.where(lane >= slot * wide, rolled[(slot - owner) % owners], mixed)
-        folded[owner * size : (owner + 1) * size, :] = to_fields(mixed)
+    for number, owner in enumerate(owners):
+        mixed = rolled[(0 - owner) % groups]
+        for slot in range(1, groups):
+            mixed = jnp.where(lane >= slot * wide, rolled[(slot - owner) % groups], mixed)
+        folded[number * size : (number + 1) * size, :] = to_fields(mixed)
+    return apart
 
 
 def above(far):
@@ -279,45 +283,101 @@
     return whole, first[:, LANES:] + pltpu.roll(second[:, 0:LANES], HALF_LANES, 1)
 
 
-def close_kernel(weighted_ref, side_ref, whole_ref, shared_ref):
-    whole_ref[...], shared_ref[...] = side_dot(weighted_ref, side_ref)
-
-
-def far_kernel(
-    groups, share, weighted_ref, side_ref, whole_ref, shared_ref, totals_ref, *refs
-):
-    targets, (tile, folded, flipped, spare, extras) = refs[:groups], refs[groups:]
+def fold_side(far, weighted_ref, side_ref, main, spare, lines, tile, flipped):
     snps = tile.shape[1]
     whole, shared = side_dot(weighted_ref, side_ref)
-    left = iota(shared.shape, 1) < HALF_LANES
-
-    @pl.when(above(True))
+    tile[:, LANES : 2 * LANES] = shared
+
+    def fold(first, start):
+        tile[:, start : start + LANES] = whole
+        apart = fold_by_column(tile, flipped, main, first)
+        fold_spare(tile, spare, 2 - first)
+        lines[0:1, :] = tile[snps : snps + 1, :]
+        lines[1:2, :] = apart
+
+    @pl.when(above(far))
     def _():
-        tile[:, 0:LANES] = whole
-        tile[:, LANES : 2 * LANES] = jnp.where(left, shared, shared_ref[...])
-        tile[:, 2 * LANES :] = whole_ref[...]
-
-    @pl.when(jnp.logical_not(above(True)))
+        fold(0, 0)
+
+    @pl.when(jnp.logical_not(above(far)))
     def _():
-        tile[:, 0:LANES] = whole_ref[...]
-        tile[:, LANES : 2 * LANES] = jnp.where(left, shared_ref[...], shared)
-        tile[:, 2 * LANES :] = whole
-
-    fold_by_column(tile, flipped, folded)
-    square = (snps, snps)
-    apart = jnp.sum(
-        jnp.where(iota(square, 0) == iota(square, 1), tile[0:snps, :], 0.0), axis=0, keepdims=True
-    )
-    fold_spare(tile, spare)
+        fold(2, 2 * LANES)
+
+
+def close_kernel(groups, reach_ref, weighted_ref, side_ref, annot_ref, *refs):
+    main_ref, spare_ref, lines_ref, annots, masks_ref, spare_mask_ref, own_rows_ref, tile, flipped = refs
+    fold_side(False, weighted_ref, side_ref, main_ref, spare_ref, lines_ref, tile, flipped)
+    snps = annot_ref.shape[1]
+    half, wide = snps // 2, snps // groups
+    size = wide // 2
+    own = annot_ref[...].astype(jnp.float32)
+    own = jnp.concatenate([own, jnp.zeros((LANES - own.shape[0], snps), jnp.float32)], axis=0)
+    annots[...] = own.T
+
+    me = lax.axis_index("hap")
+    block = lax.axis_index("snp")
+    last = reach_ref.shape[0] - 1
+    upper = me < groups // 2
+    reach_here = reach_ref[block]
+    reach_there = jnp.where(
+        upper, reach_ref[jnp.minimum(block + 1, last)], reach_ref[jnp.maximum(block - 1, 0)]
+    )
+    left_places, right_places = owner_places(groups, size)
+    local, lane = iota((size, LANES), 0), iota((size, LANES), 1)
+    own_row = jnp.concatenate(
+        [local + jnp.where(lane < size, a, b) for a, b in zip(left_places, right_places)], axis=0
+    )
+    shape = own_row.shape
+    lane = iota(shape, 1)
+    apart = jnp.abs(own_row - (lane + me * wide))
+    ahead = (own_row - (lane + me * wide)) * jnp.where(upper, 1, -1) > 0
+    real = ahead & (lane < wide) & ((lane >= size) | (iota(shape, 0) < groups * size))
+    inside = (own_row - half) * jnp.where(upper, 1, -1) < jnp.where(upper, 0, 1)
+    masks_ref[0] = jnp.where(real & inside & (snps - apart <= reach_here), 1.0, 0.0)
+    masks_ref[1] = jnp.where(real & (snps - apart <= reach_there), 1.0, 0.0)
+    own_rows = rows_at(annots, left_places, size) + pltpu.roll(
+        rows_at(annots, right_places, size), HALF_LANES, 1
+    )
+    own_rows_ref[...] = own_rows.astype(jnp.bfloat16)
+
+    own_places, near_places = spare_places(groups, size)
+    shape = spare_mask_ref.shape
+    local, lane = iota(shape, 0), iota(shape, 1)
+    own_row = by_slot([local + place for place in own_places], lane, size)
+    near_col = by_slot(
+        [lane + (place - slot * size) for slot, place in enumerate(near_places)], lane, size
+    )
+    close = snps - jnp.abs(own_row - near_col) <= reach_here
+    spare_mask_ref[...] = jnp.where(close & (lane < groups * size), 1.0, 0.0)
+
+
+def by_slot(values, lane, size):
+    mixed = values[0]
+    for slot in range(1, len(values)):
+        mixed = jnp.where(lane >= slot * size, values[slot], mixed)
+    return mixed
+
+
+def far_kernel(groups, share, weighted_ref, side_ref, close_ref, close_spare_ref, close_lines_ref, totals_ref, *refs):
+    targets, (main, spare, lines, tile, flipped, extras) = refs[:groups], refs[groups:]
+    fold_side(True, weighted_ref, side_ref, main, spare, lines, tile, flipped)
+    snps = tile.shape[1]
+    half, size = snps // 2, share
+    odd = odd_block()
+
     tiles = snps // LANES
-    size = share
-    count = spare.shape[0] // groups
-    sizes = totals_ref[1:2, :]
-    by_column = jnp.concatenate([sizes, tile[snps : snps + 1, :], apart, jnp.zeros((5, snps))], axis=0)
+    count = spare.shape[0] // 2
+    from_far = (iota((8, snps), 1) < half) == odd
+    by_column = jnp.concatenate(
+        [totals_ref[1:2, :], jnp.where(from_far, lines[...], close_lines_ref[...])[0:2, :]], axis=0
+    )
+    by_column = jnp.concatenate([by_column, jnp.zeros((5, snps))], axis=0)
     for owner in range(groups):
         start = owner * (snps // groups)
         columns = pltpu.roll(by_column, snps - start, 1) if owner else by_column
-        spare_totals = spare[owner * count + size : owner * count + size + 1, :]
+        where = slice((owner & 1) * count + size, (owner & 1) * count + size + 1)
+        second = odd if owner >= groups // 2 else jnp.logical_not(odd)
+        spare_totals = jnp.where(second, spare[where, :], close_spare_ref[where, :])
         extras[8 * owner : 8 * (owner + 1), :] = jnp.concatenate(
             [
                 to_fields(columns[0:3, 0:LANES]),
@@ -328,11 +388,16 @@
             axis=0,
         )
     me = lax.axis_index("hap")
-    send_tiles(groups, folded, share, targets)
     left = iota((size // 2, LANES), 1) < HALF_LANES
     for step, target in enumerate(targets):
         owner = partner(me, step, groups)
-        counts = spare[pl.ds(pl.multiple_of(owner * count, 8), size), :]
+        first = (owner < groups // 2) == odd
+        where = pl.ds(pl.multiple_of((owner & 1) * size, 8), size)
+        counts = jnp.where(first, main[where, :], close_ref[where, :])
+        for k in range(tiles):
+            target[k * size : (k + 1) * size, :] = counts[:, k * LANES : (k + 1) * LANES]
+        where = pl.ds(pl.multiple_of((owner & 1) * count, 8), size)
+        counts = jnp.where(first, close_spare_ref[where, :], spare[where, :])
         start = tiles * size
         target[start : start + size, :] = counts[:, 0:LANES]
         rest = counts[:, LANES:]
@@ -388,11 +453,15 @@
 
 def annots_kernel(annot_ref, far_ref, close_ref, own_ref, near_ref):
     snps = annot_ref.shape[1]
-    part = far_ref.shape[0]
-    wide = 2 * part
     own = annot_ref[...].astype(jnp.float32)
     own = jnp.concatenate([own, jnp.zeros((LANES - own.shape[0], snps), jnp.float32)], axis=0)
     own_ref[...] = own.T
+    near_ref[...] = near_annots_by_snp(far_ref, close_ref)
+
+
+def near_annots_by_snp(far_ref, close_ref):
+    part, snps = far_ref.shape
+    wide = 2 * part
     odd = odd_block()
     far, close = far_ref[...].astype(jnp.float32), close_ref[...].astype(jnp.float32)
     first, second = load_packed(jnp.where(odd, far, close), jnp.where(odd, close, far))
@@ -404,7 +473,7 @@
         ],
         axis=0,
     )
-    near_ref[...] = near.T
+    return near.T
 
 
 def column_stats(totals, count):
@@ -587,8 +656,9 @@
     groups, share, reach_ref, *refs
 ):
     own_parts, refs = refs[:groups], refs[groups:]
-    annot_ref, near_annot_ref, scores, mine_ref, rows_ref, masks_ref, columns_ref, own_rows_ref, *refs = refs
-    spare_rows_ref, spare_mask_ref, spare_columns_ref, *targets, table = refs
+    annot_ref, far_ref, close_ref, scores, mine_ref, rows_ref, columns_ref, *refs = refs
+    spare_rows_ref, spare_columns_ref, near_annot_ref, *targets, table = refs
+    near_annot_ref[...] = near_annots_by_snp(far_ref, close_ref)
     snps = annot_ref.shape[0]
     half = snps // 2
     wide = snps // groups
@@ -649,58 +719,25 @@
     size = wide // 2
     left_places, right_places = owner_places(groups, size)
     left_table, right_table = rows_at(table, left_places, size), rows_at(table, right_places, size)
-    local, lane = iota((size, LANES), 0), iota((size, LANES), 1)
-    own_row = jnp.concatenate(
-        [local + jnp.where(lane < size, a, b) for a, b in zip(left_places, right_places)], axis=0
-    )
-    shape = own_row.shape
-    lane = iota(shape, 1)
-    is_left = lane < size
+    is_left = iota(rows_ref.shape[1:], 1) < size
     for pop in range(2):
         for k in range(3):
             column = slice(4 * pop + k, 4 * pop + k + 1)
             rows_ref[3 * pop + k] = jnp.where(is_left, left_table[:, column], right_table[:, column])
-    upper = me < groups // 2
-    block = lax.axis_index("snp")
-    last = reach_ref.shape[0] - 1
-    reach_there = jnp.where(
-        upper, reach_ref[jnp.minimum(block + 1, last)], reach_ref[jnp.maximum(block - 1, 0)]
-    )
-    apart = jnp.abs(own_row - (lane + me * wide))
-    ahead = (own_row - (lane + me * wide)) * jnp.where(upper, 1, -1) > 0
-    real = ahead & (lane < wide) & ((lane >= size) | (iota(shape, 0) < groups * size))
-    inside = (own_row - half) * jnp.where(upper, 1, -1) < jnp.where(upper, 0, 1)
-    masks_ref[0] = jnp.where(real & inside & (snps - apart <= reach_here), 1.0, 0.0)
-    masks_ref[1] = jnp.where(real & (snps - apart <= reach_there), 1.0, 0.0)
     theirs = near_annot_ref[slice_rows, :]
     columns = [theirs[0:size], pltpu.roll(theirs[size:], HALF_LANES, 1), jnp.zeros((LANES - wide, LANES))]
     columns_ref[...] = jnp.concatenate(columns, axis=0).astype(jnp.bfloat16)
-    own_rows = rows_at(annot_ref, left_places, size) + pltpu.roll(
-        rows_at(annot_ref, right_places, size), HALF_LANES, 1
-    )
-    own_rows_ref[...] = own_rows.astype(jnp.bfloat16)
 
     own_places, near_places = spare_places(groups, size)
-    shape = (size, spare_mask_ref.shape[1])
-    local, lane = iota(shape, 0), iota(shape, 1)
-
-    def by_slot(values):
-        mixed = values[0]
-        for slot in range(1, groups):
-            mixed = jnp.where(lane >= slot * size, values[slot], mixed)
-        return mixed
-
+    shape = spare_rows_ref.shape[1:]
+    lane = iota(shape, 1)
     tables = [table[pl.ds(pl.multiple_of(place, 8), size), :] for place in own_places]
     for pop in range(2):
         for k in range(3):
             column = slice(4 * pop + k, 4 * pop + k + 1)
             spare_rows_ref[3 * pop + k] = by_slot(
-                [jnp.broadcast_to(values[:, column], shape) for values in tables]
+                [jnp.broadcast_to(values[:, column], shape) for values in tables], lane, size
             )
-    own_row = by_slot([local + place for place in own_places])
-    near_col = by_slot([lane + (place - slot * size) for slot, place in enumerate(near_places)])
-    close = snps - jnp.abs(own_row - near_col) <= reach_here
-    spare_mask_ref[...] = jnp.where(close & (lane < groups * size), 1.0, 0.0)
     columns = [rows_at(near_annot_ref, near_places, size)]
     columns.append(jnp.zeros((shape[1] - groups * size, LANES), jnp.float32))
     spare_columns_ref[...] = jnp.concatenate(columns, axis=0).astype(jnp.bfloat16)
@@ -708,8 +745,8 @@
 
 def near_score_kernel(groups, share, reach_ref, *refs):
     near_parts, refs = refs[:groups], refs[groups:]
-    own_ref, mine_ref, rows_ref, masks_ref, columns_ref, own_rows_ref = refs[:6]
-    spare_rows_ref, spare_mask_ref, spare_columns_ref, annot_ref, near_annot_ref = refs[6:11]
+    own_ref, mine_ref, rows_ref, columns_ref, spare_rows_ref, spare_columns_ref = refs[:6]
+    near_annot_ref, annot_ref, masks_ref, spare_mask_ref, own_rows_ref = refs[6:11]
     out_ref, send_ref, near_out_ref, flipped, scores = refs[11:]
     snps = annot_ref.shape[0]
     wide = snps // groups
@@ -863,6 +900,7 @@
     from_close = swapped(close, 0)
 
     by_column = groups == len(LEFT_BLOCKS)
+    by_snp = shape((snps, LANES), f32)
     compact = shape((share * (snps // LANES) + 8, LANES), i32)
     own_share_counts = compact if by_column else shape((share, snps), i32)
     near_share_counts = shape((compact.shape[0] + share + share // 2, LANES), i32)
@@ -881,20 +919,29 @@
 
     near_shapes = [own_share_counts] + [near_share_counts if by_column else shape((share + 8, snps), i32)] * groups
     if by_column:
-        piece = shape((snps + 16, LANES), f32)
         work = dict(flops=4 * rows * snps * LANES, moved=rows * snps * 4)
-        close_counts = call(close_kernel, [piece, piece], [VMEM] * 2, **work)(weighted, from_close)
+        flipped = pltpu.VMEM((snps, LANES), f32)
+        pair_rows = (groups + 1) * (out_share // 2)
+        side_shapes = [((2 * share, snps), i32), ((2 * (share + 8), 2 * LANES), i32), ((8, snps), f32)]
+        *close_counts, own_annots, masks, spare_mask, own_rows = call(
+            functools.partial(close_kernel, groups),
+            [shape(*args) for args in side_shapes]
+            + [
+                by_snp,
+                shape((2, pair_rows, LANES), f32),
+                shape((share, 2 * LANES), f32),
+                shape((pair_rows, LANES), bf16),
+            ],
+            [SMEM] + [VMEM] * 3,
+            [tile, flipped],
+            **work,
+        )(reach, weighted, from_close, annotations)
         near_parts = call(
             functools.partial(far_kernel, groups, share),
             near_shapes[1:],
-            [VMEM] * 5,
-            [
-                tile,
-                folded,
-                pltpu.VMEM((snps, LANES), f32),
-                pltpu.VMEM(((share + 8) * groups, 2 * LANES), i32),
-                pltpu.VMEM((8 * groups, LANES), i32),
-            ],
+            [VMEM] * 6,
+            [pltpu.VMEM(*args) for args in side_shapes]
+            + [tile, flipped, pltpu.VMEM((8 * groups, LANES), i32)],
             **work,
         )(weighted, from_far, *close_counts, totals)
     else:
@@ -908,10 +955,10 @@
         )(weighted, from_far, from_close, totals, *own_parts)
     near_parts = [near_parts[0]] + [around(near_parts[k], groups, k) for k in order]
 
-    by_snp = shape((snps, LANES), f32)
-    own_annots, near_annots = call(annots_kernel, [by_snp, by_snp], [VMEM] * 3, moved=1 << 20)(
-        annotations, from_far[rows // 2 :], from_close[rows // 2 :]
-    )
+    if not by_column:
+        own_annots, near_annots = call(annots_kernel, [by_snp, by_snp], [VMEM] * 3, moved=1 << 20)(
+            annotations, from_far[rows // 2 :], from_close[rows // 2 :]
+        )
     pairs = []
     for block in range(blocks):
         for group in range(groups):
@@ -927,7 +974,6 @@
     own_share = shape((out_share, LANES), f32)
     packed_share = shape((half_share, LANES), f32)
     if by_column:
-        pair_rows = (groups + 1) * (out_share // 2)
         sent = shape((half_share, LANES), bf16)
         *prepared, second, third = call(
             functools.partial(own_score_kernel, groups, share),
@@ -935,20 +981,18 @@
                 by_snp,
                 shape((out_share, LANES), f32),
                 shape((6, pair_rows, LANES), f32),
-                shape((2, pair_rows, LANES), f32),
                 shape((LANES, LANES), bf16),
-                shape((pair_rows, LANES), bf16),
                 shape((6, share, 2 * LANES), f32),
-                shape((share, 2 * LANES), f32),
                 shape((2 * LANES, LANES), bf16),
+                by_snp,
                 sent,
                 sent,
             ],
-            [SMEM] + [VMEM] * (groups + 2),
+            [SMEM] + [VMEM] * (groups + 3),
             [pltpu.VMEM((snps, LANES), f32)],
             flops=1 << 33,
             moved=1 << 20,
-        )(reach, *own_parts, own_annots, near_annots)
+        )(reach, *own_parts, own_annots, from_far[rows // 2 :], from_close[rows // 2 :])
         parts = [around(third, groups, 3), around(second, groups, 2)]
         own_scores, send, there = call(
             functools.partial(near_score_kernel, groups, share),
@@ -957,7 +1001,7 @@
             [pltpu.VMEM((LANES, LANES), i32), pltpu.VMEM((snps, LANES), f32)],
             flops=1 << 26,
             moved=1 << 21,
-        )(reach, *near_parts, *prepared, own_annots, near_annots)
+        )(reach, *near_parts, *prepared, own_annots, masks, spare_mask, own_rows)
         parts += [around(send, groups, 1), to_neighbour(there)]
         return call(column_finish_kernel, result, [VMEM] * 5)(own_scores, *parts)
 

time: 35.5 us -> 35.2 us (level)
  waiting for transfers between devices: 5.97 us -> 4.84 us
  Pallas kernels: 9.22 us -> 9.94 us
    ppermute x2, waiting for transfers between devices: 4.7 us -> 3.58 us  [swapped(): return lax.ppermute(value, 'snp', pairs)]
    pallas_call x2 -> x1, Pallas kernels: 0.93 us -> 1.79 us  [per_device(): call(functools.partial(close_kernel, groups), [shape(*args) for args in s...]
  transfers between devices with their start and end apart: 12 -> 12, of which waited for: 3 -> 3; matrix products, arithmetic and copies ran while one was open for 0% -> 0% of each run, Pallas kernels for 18% -> 20%
where the time goes in v21:
time: 35.2 us; the launch traced here: 34.9 us
  starting transfers between devices  20 us (57%)
  Pallas kernels  9.94 us (28%)
  waiting for transfers between devices  4.84 us (14%)
    ppermute x9, starting transfers between devices, around(): lax.ppermute(value, 'hap', [(source, partner(source, step, groups)) for s...  11.6 us
    ppermute x2, starting transfers between devices, swapped(): return lax.ppermute(value, 'snp', pairs)  4.59 us
    ppermute x1, starting transfers between devices, to_neighbour(): return lax.ppermute(value, ('snp', 'hap'), pairs)  3.83 us
    ppermute x2, waiting for transfers between devices, swapped(): return lax.ppermute(value, 'snp', pairs)  3.58 us
    pallas_call x1, Pallas kernels, per_device(): call(prepare_kernel, [shape((rows, snps), bf16), packed, packed], [HBM, H...  2.14 us
    pallas_call x1, Pallas kernels, per_device(): call(functools.partial(own_score_kernel, groups, share), [by_snp, shape((...  1.8 us
    pallas_call x1, Pallas kernels, per_device(): call(functools.partial(close_kernel, groups), [shape(*args) for args in s...  1.79 us
    pallas_call x1, Pallas kernels, per_device(): call(functools.partial(near_score_kernel, groups, share), [packed_share,...  1.21 us
  transfers between devices with their start and end apart: 12, of which 3 were waited for; matrix products, arithmetic and copies ran while one was open for 0% of the time, Pallas kernels for 20%

profile of v21, /device:TPU:1, one launch (start us, length us, event | category | flops | bytes accessed | tf_op | source)
XLA Modules:
  0.0 34.9 jit_solution(7718953455537373692)
XLA Ops:
  0.0 0.0 copy-start.2
  0.0 2.1 %shard_map.46 = (bf16[2048,384]{1,0:T(8,128)(2,1)S(1)}, bf16[1056,384]{1,0:T(8,128)(2,1)S(1)}, bf16[1056,384]{1,0:T(8,128)(2,1)S(1)}) custom-call(s32[2048,384]{1,0:T(8,128)} %hap_ref.1, s32[50,384]{1,0:T(8,128)} %annot_ref.3), custom_call_target="tpu_custom_call" | custom-call | bytes 6291456 | tf_op jit(solution)/shard_map/pallas_call | solution.py:888
  2.1 0.0 copy-start
  2.2 0.0 copy-start.1
  2.2 0.1 collective-permute-start.1
  2.3 4.5 %collective-permute-start = (bf16[1056,384]{1,0:T(8,128)(2,1)S(1)}, bf16[1056,384]{1,0:T(8,128)(2,1)S(1)}, u32[]{:S(2)}, u32[]{:S(2)}) collective-permute-start(bf16[1056,384]{1,0:T(8,128)(2,1)S(1)} %get-tuple-element.39), channel_id=1, source_target_pairs={{4,8},{8,4},{5,9},{9,5},{6,10},{10,6},{7,11},{11,7},{20,24},{24,20... | collective-permute-start | bytes 2433032 | tf_op jit(solution)/shard_map/ppermute | solution.py:869
  6.8 0.0 copy-done.2
  6.8 1.1 %shard_map.47 = (bf16[400,2048]{1,0:T(8,128)(2,1)S(1)}, f32[8,384]{1,0:T(8,128)S(1)}, s32[152,128]{1,0:T(8,128)S(1)}, s32[152,128]{1,0:T(8,128)S(1)}, s32[152,128]{1,0:T(8,128)S(1)}, /*index=5*/s32[152,128]{1,0:T(8,128)S(1)}) custom-call(bf16[2048,384]{1,0:T(8,128)(2,1)S(1)} %get-tuple-element.37.alleles_ref, s32[1,2048]{1,0:T(1,128)S(1)} %bitcast.1), custom_call_target="tpu_custom_call" | custom-call | flops 603979776 | bytes 3145728 | tf_op jit(solution)/shard_map/pallas_call | solution.py:909
  7.9 2.4 %collective-permute-start.5 = (s32[152,128]{1,0:T(8,128)S(1)}, s32[152,128]{1,0:T(8,128)S(1)}, u32[]{:S(2)}, u32[]{:S(2)}) collective-permute-start(s32[152,128]{1,0:T(8,128)S(1)} %get-tuple-element.50), channel_id=1, source_target_pairs={{0,2},{1,3},{2,0},{3,1},{4,6},{5,7},{6,4},{7,5},{8,10},{9,11},{10,... | collective-permute-start | bytes 233480 | tf_op jit(solution)/shard_map/ppermute | solution.py:860
  10.3 1.1 %collective-permute-start.6 = (s32[152,128]{1,0:T(8,128)S(1)}, s32[152,128]{1,0:T(8,128)S(1)}, u32[]{:S(2)}, u32[]{:S(2)}) collective-permute-start(s32[152,128]{1,0:T(8,128)S(1)} %get-tuple-element.51), channel_id=1, source_target_pairs={{0,3},{1,2},{2,1},{3,0},{4,7},{5,6},{6,5},{7,4},{8,11},{9,10},{10,... | collective-permute-start | bytes 233480 | tf_op jit(solution)/shard_map/ppermute | solution.py:860
  11.4 0.2 collective-permute-start.7
  11.6 0.0 collective-permute-done.1.side_ref
  11.6 0.0 copy-done
  11.6 0.0 copy-done.1
  11.6 1.8 %shard_map.48 = (s32[96,384]{1,0:T(8,128)S(1)}, s32[112,256]{1,0:T(8,128)S(1)}, f32[8,384]{1,0:T(8,128)S(1)}, f32[384,128]{1,0:T(8,128)S(1)}, f32[2,240,128]{2,1...) custom-call(s32[4]{0:T(128)S(1)} %copy-done.1, ...), custom_call_target="tpu_custom_call" | custom-call | flops 402653184 | bytes 3145728 | tf_op jit(solution)/shard_map/pallas_call | solution.py:926
  13.4 3.6 %collective-permute-done.side_ref = bf16[1056,384]{1,0:T(8,128)(2,1)S(1)} collective-permute-done((bf16[1056,384]{1,0:T(8,128)(2,1)S(1)}, bf16[1056,384]{1,0:T(8,128)(2,1)S(1)}, u32[]{:S(2)}, u32[]{:S(2)}) %collective-permute-start) | collective-permute-done | bytes 811040 | tf_op jit(solution)/shard_map/ppermute | solution.py:869
  17.0 1.1 %shard_map.49 = (s32[224,128]{1,0:T(8,128)S(1)}, s32[224,128]{1,0:T(8,128)S(1)}, s32[224,128]{1,0:T(8,128)S(1)}, s32[224,128]{1,0:T(8,128)S(1)}) custom-call(bf16[400,2048]{1,0:T(8,128)(2,1)S(1)} %get-tuple-element.38.weighted_ref, bf16[1056,384]{1,0:T(8,128)(2,1)S(1)} %collective-permute-done.side_ref, s32[96,384]{1,0:T(8,128)S(1)} %get-tuple-element.41.close_ref, ...), custom_call_target="tpu_custom_call" | custom-call | flops 402653184 | bytes 3145728 | tf_op jit(solution)/shard_map/pallas_call | solution.py:939
  18.1 3.0 %collective-permute-start.2 = (s32[224,128]{1,0:T(8,128)S(1)}, s32[224,128]{1,0:T(8,128)S(1)}, u32[]{:S(2)}, u32[]{:S(2)}) collective-permute-start(s32[224,128]{1,0:T(8,128)S(1)} %get-tuple-element.46), channel_id=1, source_target_pairs={{0,2},{1,3},{2,0},{3,1},{4,6},{5,7},{6,4},{7,5},{8,10},{9,11},{10,... | collective-permute-start | bytes 344072 | tf_op jit(solution)/shard_map/ppermute | solution.py:860
  21.1 1.1 %collective-permute-start.3 = (s32[224,128]{1,0:T(8,128)S(1)}, s32[224,128]{1,0:T(8,128)S(1)}, u32[]{:S(2)}, u32[]{:S(2)}) collective-permute-start(s32[224,128]{1,0:T(8,128)S(1)} %get-tuple-element.47), channel_id=1, source_target_pairs={{0,3},{1,2},{2,1},{3,0},{4,7},{5,6},{6,5},{7,4},{8,11},{9,10},{10,... | collective-permute-start | bytes 344072 | tf_op jit(solution)/shard_map/ppermute | solution.py:860
  22.2 0.0 collective-permute-done.5.refs_1_
  22.2 0.3 collective-permute-start.4
  22.5 0.0 collective-permute-done.6.refs_2_
  22.5 0.0 collective-permute-done.7.refs_3_
  22.5 1.8 %shard_map.50 = (f32[384,128]{1,0:T(8,128)S(1)}, f32[96,128]{1,0:T(8,128)S(1)}, f32[6,240,128]{2,1,0:T(8,128)S(1)}, bf16[128,128]{1,0:T(8,128)(2,1)S(1)}, f32[6,...) custom-call(s32[4]{0:T(128)S(1)} %copy-done.1, ...), custom_call_target="tpu_custom_call" | custom-call | flops 8589934592 | bytes 1048576 | tf_op jit(solution)/shard_map/pallas_call | solution.py:978
  24.3 2.4 %collective-permute-start.8 = (bf16[48,128]{1,0:T(8,128)(2,1)S(1)}, bf16[48,128]{1,0:T(8,128)(2,1)S(1)}, u32[]{:S(2)}, u32[]{:S(2)}) collective-permute-start(bf16[48,128]{1,0:T(8,128)(2,1)S(1)} %get-tuple-element.65), channel_id=1, source_target_pairs={{0,3},{1,2},{2,1},{3,0},{4,7},{5,6},{6,5},{7,4},{8,11},{9,10},{10,... | collective-permute-start | bytes 36872 | tf_op jit(solution)/shard_map/ppermute | solution.py:860
  26.7 0.1 collective-permute-start.9
  26.8 0.0 collective-permute-done.2.refs_1_
  26.8 0.0 collective-permute-done.3.refs_2_
  26.8 0.4 %collective-permute-done.4.refs_3_ = s32[224,128]{1,0:T(8,128)S(1)} collective-permute-done((s32[224,128]{1,0:T(8,128)S(1)}, s32[224,128]{1,0:T(8,128)S(1)}, u32[]{:S(2)}, u32[]{:S(2)}) %collective-permute-start.4) | collective-permute-done | bytes 114720 | tf_op jit(solution)/shard_map/ppermute | solution.py:860
  27.3 1.2 %shard_map.51 = (f32[48,128]{1,0:T(8,128)S(1)}, bf16[48,128]{1,0:T(8,128)(2,1)S(1)}, bf16[48,128]{1,0:T(8,128)(2,1)S(1)}) custom-call(s32[4]{0:T(128)S(1)} %copy-done.1, s32[224,128]{1,0:T(8,128)S(1)} %get-tuple-element.45.refs_0_, s32[224,128]{1,0:T(8,128)S(1)} %collective-permute-done.2.refs_1_, s32[224,128]{1,0:T(8,128)S(1)} %collective-permute-done.3.refs_2_, ...), custom_call_target="tpu_custom_call" | custom-call | flops 67108864 | bytes 2097152 | tf_op jit(solution)/shard_map/pallas_call | solution.py:997
  28.5 1.0 %collective-permute-start.10 = (bf16[48,128]{1,0:T(8,128)(2,1)S(1)}, bf16[48,128]{1,0:T(8,128)(2,1)S(1)}, u32[]{:S(2)}, u32[]{:S(2)}) collective-permute-start(bf16[48,128]{1,0:T(8,128)(2,1)S(1)} %get-tuple-element.67), channel_id=1, source_target_pairs={{0,1},{1,0},{2,3},{3,2},{4,5},{5,4},{6,7},{7,6},{8,9},{9,8},{10,11... | collective-permute-start | bytes 36872 | tf_op jit(solution)/shard_map/ppermute | solution.py:860
  29.5 3.8 %collective-permute-start.11 = (bf16[48,128]{1,0:T(8,128)(2,1)S(1)}, bf16[48,128]{1,0:T(8,128)(2,1)S(1)}, u32[]{:S(2)}, u32[]{:S(2)}) collective-permute-start(bf16[48,128]{1,0:T(8,128)(2,1)S(1)} %get-tuple-element.68), channel_id=1, source_target_pairs={{0,4},{1,5},{4,8},{5,9},{6,2},{7,3},{8,12},{9,13},{10,6},{11,7},{1... | collective-permute-start | bytes 36872 | tf_op jit(solution)/shard_map/ppermute | solution.py:970
  33.3 0.0 collective-permute-done.8.refs_1_
  33.3 0.0 collective-permute-done.9.refs_2_
  33.4 0.0 collective-permute-done.10.refs_3_
  33.4 0.8 %collective-permute-done.11.refs_4_ = bf16[48,128]{1,0:T(8,128)(2,1)S(1)} collective-permute-done((bf16[48,128]{1,0:T(8,128)(2,1)S(1)}, bf16[48,128]{1,0:T(8,128)(2,1)S(1)}, u32[]{:S(2)}, u32[]{:S(2)}) %collective-permute-start.11) | collective-permute-done | bytes 12320 | tf_op jit(solution)/shard_map/ppermute | solution.py:970
  34.1 0.7 %shard_map.52 = f32[50,96]{1,0:T(8,128)} custom-call(f32[48,128]{1,0:T(8,128)S(1)} %get-tuple-element.64.refs_0_, bf16[48,128]{1,0:T(8,128)(2,1)S(1)} %collective-permute-done.8.refs_1_, bf16[48,128]{1,0:T(8,128)(2,1)S(1)} %collective-permute-done.9.refs_2_, bf16[48,128]{1,0:T(8,128)(2,1)S(1)} %collective-permute-done.10.refs_3_, ...), custom_call_target="tpu_custom_call" | custom-call | tf_op jit(solution)/shard_map/pallas_call | solution.py:1006
  (2 shorter events, 0.0 us)
Async XLA Ops:
  0.0 6.8 %copy-start.2 = (s32[2048]{0:T(1024)S(1)}, s32[2048]{0:T(1024)}, u32[]{:S(2)}) copy-start(s32[2048]{0:T(1024)} %param.5) | copy-start | bytes 24580
  2.1 9.5 %copy-start = (s32[50,384]{1,0:T(8,128)S(1)}, s32[50,384]{1,0:T(8,128)}, u32[]{:S(2)}) copy-start(s32[50,384]{1,0:T(8,128)} %annot_ref.3) | copy-start | bytes 230404
  2.2 9.4 %copy-start.1 = (s32[4]{0:T(128)S(1)}, s32[4]{0:T(128)}, u32[]{:S(2)}) copy-start(s32[4]{0:T(128)} %reach_ref.5) | copy-start | bytes 52
  2.2 9.4 %collective-permute-start.1 = (bf16[1056,384]{1,0:T(8,128)(2,1)S(1)}, bf16[1056,384]{1,0:T(8,128)(2,1)S(1)}, u32[]{:S(2)}, u32[]{:S(2)}) collective-permute-start(bf16[1056,384]{1,0:T(8,128)(2,1)S(1)} %get-tuple-element.40), channel_id=1, source_target_pairs={{0,4},{4,0},{8,12},{12,8},{1,5},{5,1},{9,13},{13,9},{2,6},{6,2},{1... | collective-permute-start | bytes 2433032 | tf_op jit(solution)/shard_map/ppermute | solution.py:869
  2.3 14.7 %collective-permute-start = (bf16[1056,384]{1,0:T(8,128)(2,1)S(1)}, bf16[1056,384]{1,0:T(8,128)(2,1)S(1)}, u32[]{:S(2)}, u32[]{:S(2)}) collective-permute-start(bf16[1056,384]{1,0:T(8,128)(2,1)S(1)} %get-tuple-element.39), channel_id=1, source_target_pairs={{4,8},{8,4},{5,9},{9,5},{6,10},{10,6},{7,11},{11,7},{20,24},{24,20... | collective-permute-start | bytes 2433032 | tf_op jit(solution)/shard_map/ppermute | solution.py:869
  7.9 14.3 %collective-permute-start.5 = (s32[152,128]{1,0:T(8,128)S(1)}, s32[152,128]{1,0:T(8,128)S(1)}, u32[]{:S(2)}, u32[]{:S(2)}) collective-permute-start(s32[152,128]{1,0:T(8,128)S(1)} %get-tuple-element.50), channel_id=1, source_target_pairs={{0,2},{1,3},{2,0},{3,1},{4,6},{5,7},{6,4},{7,5},{8,10},{9,11},{10,... | collective-permute-start | bytes 233480 | tf_op jit(solution)/shard_map/ppermute | solution.py:860
  10.3 12.2 %collective-permute-start.6 = (s32[152,128]{1,0:T(8,128)S(1)}, s32[152,128]{1,0:T(8,128)S(1)}, u32[]{:S(2)}, u32[]{:S(2)}) collective-permute-start(s32[152,128]{1,0:T(8,128)S(1)} %get-tuple-element.51), channel_id=1, source_target_pairs={{0,3},{1,2},{2,1},{3,0},{4,7},{5,6},{6,5},{7,4},{8,11},{9,10},{10,... | collective-permute-start | bytes 233480 | tf_op jit(solution)/shard_map/ppermute | solution.py:860
  11.4 11.1 %collective-permute-start.7 = (s32[152,128]{1,0:T(8,128)S(1)}, s32[152,128]{1,0:T(8,128)S(1)}, u32[]{:S(2)}, u32[]{:S(2)}) collective-permute-start(s32[152,128]{1,0:T(8,128)S(1)} %get-tuple-element.52), channel_id=1, source_target_pairs={{0,1},{1,0},{2,3},{3,2},{4,5},{5,4},{6,7},{7,6},{8,9},{9,8},{10,11... | collective-permute-start | bytes 233480 | tf_op jit(solution)/shard_map/ppermute | solution.py:860
  18.1 8.7 %collective-permute-start.2 = (s32[224,128]{1,0:T(8,128)S(1)}, s32[224,128]{1,0:T(8,128)S(1)}, u32[]{:S(2)}, u32[]{:S(2)}) collective-permute-start(s32[224,128]{1,0:T(8,128)S(1)} %get-tuple-element.46), channel_id=1, source_target_pairs={{0,2},{1,3},{2,0},{3,1},{4,6},{5,7},{6,4},{7,5},{8,10},{9,11},{10,... | collective-permute-start | bytes 344072 | tf_op jit(solution)/shard_map/ppermute | solution.py:860
  21.1 5.7 %collective-permute-start.3 = (s32[224,128]{1,0:T(8,128)S(1)}, s32[224,128]{1,0:T(8,128)S(1)}, u32[]{:S(2)}, u32[]{:S(2)}) collective-permute-start(s32[224,128]{1,0:T(8,128)S(1)} %get-tuple-element.47), channel_id=1, source_target_pairs={{0,3},{1,2},{2,1},{3,0},{4,7},{5,6},{6,5},{7,4},{8,11},{9,10},{10,... | collective-permute-start | bytes 344072 | tf_op jit(solution)/shard_map/ppermute | solution.py:860
  22.2 5.1 %collective-permute-start.4 = (s32[224,128]{1,0:T(8,128)S(1)}, s32[224,128]{1,0:T(8,128)S(1)}, u32[]{:S(2)}, u32[]{:S(2)}) collective-permute-start(s32[224,128]{1,0:T(8,128)S(1)} %get-tuple-element.48), channel_id=1, source_target_pairs={{0,1},{1,0},{2,3},{3,2},{4,5},{5,4},{6,7},{7,6},{8,9},{9,8},{10,11... | collective-permute-start | bytes 344072 | tf_op jit(solution)/shard_map/ppermute | solution.py:860
  24.3 9.1 %collective-permute-start.8 = (bf16[48,128]{1,0:T(8,128)(2,1)S(1)}, bf16[48,128]{1,0:T(8,128)(2,1)S(1)}, u32[]{:S(2)}, u32[]{:S(2)}) collective-permute-start(bf16[48,128]{1,0:T(8,128)(2,1)S(1)} %get-tuple-element.65), channel_id=1, source_target_pairs={{0,3},{1,2},{2,1},{3,0},{4,7},{5,6},{6,5},{7,4},{8,11},{9,10},{10,... | collective-permute-start | bytes 36872 | tf_op jit(solution)/shard_map/ppermute | solution.py:860
  26.7 6.7 %collective-permute-start.9 = (bf16[48,128]{1,0:T(8,128)(2,1)S(1)}, bf16[48,128]{1,0:T(8,128)(2,1)S(1)}, u32[]{:S(2)}, u32[]{:S(2)}) collective-permute-start(bf16[48,128]{1,0:T(8,128)(2,1)S(1)} %get-tuple-element.66), channel_id=1, source_target_pairs={{0,2},{1,3},{2,0},{3,1},{4,6},{5,7},{6,4},{7,5},{8,10},{9,11},{10,... | collective-permute-start | bytes 36872 | tf_op jit(solution)/shard_map/ppermute | solution.py:860
  28.5 4.9 %collective-permute-start.10 = (bf16[48,128]{1,0:T(8,128)(2,1)S(1)}, bf16[48,128]{1,0:T(8,128)(2,1)S(1)}, u32[]{:S(2)}, u32[]{:S(2)}) collective-permute-start(bf16[48,128]{1,0:T(8,128)(2,1)S(1)} %get-tuple-element.67), channel_id=1, source_target_pairs={{0,1},{1,0},{2,3},{3,2},{4,5},{5,4},{6,7},{7,6},{8,9},{9,8},{10,11... | collective-permute-start | bytes 36872 | tf_op jit(solution)/shard_map/ppermute | solution.py:860
  29.5 4.6 %collective-permute-start.11 = (bf16[48,128]{1,0:T(8,128)(2,1)S(1)}, bf16[48,128]{1,0:T(8,128)(2,1)S(1)}, u32[]{:S(2)}, u32[]{:S(2)}) collective-permute-start(bf16[48,128]{1,0:T(8,128)(2,1)S(1)} %get-tuple-element.68), channel_id=1, source_target_pairs={{0,4},{1,5},{4,8},{5,9},{6,2},{7,3},{8,12},{9,13},{10,6},{11,7},{1... | collective-permute-start | bytes 36872 | tf_op jit(solution)/shard_map/ppermute | solution.py:970

commit v22 on v21

--- a/solution.py
+++ b/solution.py
@@ -13,7 +13,7 @@
 FIELD_BITS = 16
 LANES = 128
 HALF_LANES = LANES // 2
-CHUNKS = 4
+CHUNKS = (6, 5, 3, 2)
 VMEM = pl.BlockSpec(memory_space=pltpu.VMEM)
 SMEM = pl.BlockSpec(memory_space=pltpu.SMEM)
 HBM = pl.BlockSpec(memory_space=pltpu.HBM)
@@ -84,15 +84,18 @@
 def prepare_kernel(hap_ref, annot_ref, alleles_ref, far_ref, close_ref, held, held_annots, sems):
     rows = hap_ref.shape[0]
     annot_rows = annot_ref.shape[0]
-    size = rows // (2 * CHUNKS)
-    starts = [side * (rows // 2) + chunk * size for chunk in range(CHUNKS) for side in range(2)]
+    sizes = [chunk * (rows // 32) for chunk in CHUNKS]
+    places = [sum(sizes[:number]) for number in range(len(sizes))]
+    pieces = [
+        (side * (rows // 2) + place, size) for place, size in zip(places, sizes) for side in range(2)
+    ]
     copies = [
         pltpu.make_async_copy(
             hap_ref.at[pl.ds(start, size)], held.at[pl.ds(start, size)], sems.at[number]
         )
-        for number, start in enumerate(starts)
+        for number, (start, size) in enumerate(pieces)
     ]
-    copies.append(pltpu.make_async_copy(annot_ref, held_annots, sems.at[2 * CHUNKS]))
+    copies.append(pltpu.make_async_copy(annot_ref, held_annots, sems.at[len(pieces)]))
     for copy in copies:
         copy.start()
     part = far_ref.shape[0] - rows // 2
@@ -107,16 +110,15 @@
         def _():
             store_packed(far_ref, close_ref, where, first, second)
 
-    for chunk in range(CHUNKS):
+    for chunk, (place, size) in enumerate(zip(places, sizes)):
         pair = []
-        for side in range(2):
-            number = 2 * chunk + side
+        for number in (2 * chunk, 2 * chunk + 1):
             copies[number].wait()
-            where = slice(starts[number], starts[number] + size)
+            where = slice(pieces[number][0], pieces[number][0] + size)
             values = held[where, :].astype(jnp.float32)
             alleles_ref[where, :] = values.astype(jnp.bfloat16)
             pair.append(values)
-        store(slice(chunk * size, (chunk + 1) * size), *pair)
+        store(slice(place, place + size), *pair)
     copies[-1].wait()
     annots = jnp.concatenate(
         [
@@ -747,7 +749,7 @@
     near_parts, refs = refs[:groups], refs[groups:]
     own_ref, mine_ref, rows_ref, columns_ref, spare_rows_ref, spare_columns_ref = refs[:6]
     near_annot_ref, annot_ref, masks_ref, spare_mask_ref, own_rows_ref = refs[6:11]
-    out_ref, send_ref, near_out_ref, flipped, scores = refs[11:]
+    out_ref, wide_ref, send_ref, near_out_ref, flipped, scores = refs[11:]
     snps = annot_ref.shape[0]
     wide = snps // groups
     size = wide // 2
@@ -828,7 +830,8 @@
         return pack_halves(scores[pl.ds(pl.multiple_of(group * wide, 8), wide), :])
 
     out_ref[...] = packed(0)
-    send_ref[...] = packed(1).astype(send_ref.dtype)
+    wide_ref[...] = packed(1)
+    send_ref[...] = wide_ref[...].astype(send_ref.dtype)
 
 
 def column_finish_kernel(*refs):
@@ -860,6 +863,15 @@
     return lax.ppermute(
         value, "hap", [(source, partner(source, step, groups)) for source in range(groups)]
     )
+
+
+def swap_nearest(value, groups, of_blocks):
+    pairs = [
+        (block * groups + group, block * groups + partner(group, 1, groups))
+        for block in of_blocks
+        for group in range(groups)
+    ]
+    return lax.ppermute(value, ("snp", "hap"), pairs)
 
 
 def swapped(value, first):
@@ -892,7 +904,7 @@
         [
             pltpu.VMEM((rows, snps), i32),
             pltpu.VMEM(annotations.shape, i32),
-            pltpu.SemaphoreType.DMA((2 * CHUNKS + 1,)),
+            pltpu.SemaphoreType.DMA((2 * len(CHUNKS) + 1,)),
         ],
         moved=rows * snps * 8,
     )(haplotypes, annots_in)
@@ -985,8 +997,8 @@
                 shape((6, share, 2 * LANES), f32),
                 shape((2 * LANES, LANES), bf16),
                 by_snp,
-                sent,
-                sent,
+                packed_share,
+                packed_share,
             ],
             [SMEM] + [VMEM] * (groups + 3),
             [pltpu.VMEM((snps, LANES), f32)],
@@ -994,16 +1006,17 @@
             moved=1 << 20,
         )(reach, *own_parts, own_annots, from_far[rows // 2 :], from_close[rows // 2 :])
         parts = [around(third, groups, 3), around(second, groups, 2)]
-        own_scores, send, there = call(
+        own_scores, wide, send, there = call(
             functools.partial(near_score_kernel, groups, share),
-            [packed_share, sent, sent],
+            [packed_share, packed_share, sent, sent],
             [SMEM] + [VMEM] * (groups + 11),
             [pltpu.VMEM((LANES, LANES), i32), pltpu.VMEM((snps, LANES), f32)],
             flops=1 << 26,
             moved=1 << 21,
         )(reach, *near_parts, *prepared, own_annots, masks, spare_mask, own_rows)
-        parts += [around(send, groups, 1), to_neighbour(there)]
-        return call(column_finish_kernel, result, [VMEM] * 5)(own_scores, *parts)
+        early, late = range(blocks // 2), range(blocks // 2, blocks)
+        parts += [swap_nearest(wide, groups, early), to_neighbour(there), swap_nearest(send, groups, late)]
+        return call(column_finish_kernel, result, [VMEM] * 6)(own_scores, *parts)
 
     tall = pltpu.VMEM((padded, LANES), f32)
     scores = call(

time: 35.2 us -> 39.5 us (1.12)
  the two profiles are of different devices: /device:TPU:1 before, /device:TPU:26 now
where the time goes in v22:
time: 39.5 us; the launch traced here: 39.3 us
  starting transfers between devices  20.4 us (52%)
  Pallas kernels  9.96 us (25%)
  waiting for transfers between devices  8.79 us (22%)
    ppermute x8, starting transfers between devices, around(): lax.ppermute(value, 'hap', [(source, partner(source, step, groups)) for s...  10 us
    ppermute x1, starting transfers between devices, to_neighbour(): return lax.ppermute(value, ('snp', 'hap'), pairs)  4.81 us
    ppermute x2, waiting for transfers between devices, swapped(): return lax.ppermute(value, 'snp', pairs)  4.52 us
    ppermute x2, waiting for transfers between devices, swap_nearest(): return lax.ppermute(value, ('snp', 'hap'), pairs)  3.25 us
    ppermute x2, starting transfers between devices, swap_nearest(): return lax.ppermute(value, ('snp', 'hap'), pairs)  2.96 us
    ppermute x2, starting transfers between devices, swapped(): return lax.ppermute(value, 'snp', pairs)  2.6 us
    pallas_call x1, Pallas kernels, per_device(): call(prepare_kernel, [shape((rows, snps), bf16), packed, packed], [HBM, H...  2.14 us
    pallas_call x1, Pallas kernels, per_device(): call(functools.partial(own_score_kernel, groups, share), [by_snp, shape((...  1.81 us
  transfers between devices with their start and end apart: 13, of which 3 were waited for; matrix products, arithmetic and copies ran while one was open for 0% of the time, Pallas kernels for 18%

profile of v22, /device:TPU:26, one launch (start us, length us, event | category | flops | bytes accessed | tf_op | source)
XLA Modules:
  0.0 39.3 jit_solution(1971147589437162420)
XLA Ops:
  0.0 0.0 copy-start.2
  0.0 2.1 %shard_map.46 = (bf16[2048,384]{1,0:T(8,128)(2,1)S(1)}, bf16[1056,384]{1,0:T(8,128)(2,1)S(1)}, bf16[1056,384]{1,0:T(8,128)(2,1)S(1)}) custom-call(s32[2048,384]{1,0:T(8,128)} %hap_ref.1, s32[50,384]{1,0:T(8,128)} %annot_ref.3), custom_call_target="tpu_custom_call" | custom-call | bytes 6291456 | tf_op jit(solution)/shard_map/pallas_call | solution.py:900
  2.1 0.0 copy-start
  2.2 0.0 copy-start.1
  2.2 0.1 collective-permute-start.1
  2.3 2.5 %collective-permute-start = (bf16[1056,384]{1,0:T(8,128)(2,1)S(1)}, bf16[1056,384]{1,0:T(8,128)(2,1)S(1)}, u32[]{:S(2)}, u32[]{:S(2)}) collective-permute-start(bf16[1056,384]{1,0:T(8,128)(2,1)S(1)} %get-tuple-element.40), channel_id=1, source_target_pairs={{4,8},{8,4},{5,9},{9,5},{6,10},{10,6},{7,11},{11,7},{20,24},{24,20... | collective-permute-start | bytes 2433032 | tf_op jit(solution)/shard_map/ppermute | solution.py:881
  4.8 0.0 copy-done.2
  4.8 1.1 %shard_map.47 = (bf16[400,2048]{1,0:T(8,128)(2,1)S(1)}, f32[8,384]{1,0:T(8,128)S(1)}, s32[152,128]{1,0:T(8,128)S(1)}, s32[152,128]{1,0:T(8,128)S(1)}, s32[152,128]{1,0:T(8,128)S(1)}, /*index=5*/s32[152,128]{1,0:T(8,128)S(1)}) custom-call(bf16[2048,384]{1,0:T(8,128)(2,1)S(1)} %get-tuple-element.38.alleles_ref, s32[1,2048]{1,0:T(1,128)S(1)} %bitcast.1), custom_call_target="tpu_custom_call" | custom-call | flops 603979776 | bytes 3145728 | tf_op jit(solution)/shard_map/pallas_call | solution.py:921
  5.9 0.4 collective-permute-start.5
  6.3 2.5 %collective-permute-start.6 = (s32[152,128]{1,0:T(8,128)S(1)}, s32[152,128]{1,0:T(8,128)S(1)}, u32[]{:S(2)}, u32[]{:S(2)}) collective-permute-start(s32[152,128]{1,0:T(8,128)S(1)} %get-tuple-element.52), channel_id=1, source_target_pairs={{0,3},{1,2},{2,1},{3,0},{4,7},{5,6},{6,5},{7,4},{8,11},{9,10},{10,... | collective-permute-start | bytes 233480 | tf_op jit(solution)/shard_map/ppermute | solution.py:863
  8.8 0.7 %collective-permute-start.7 = (s32[152,128]{1,0:T(8,128)S(1)}, s32[152,128]{1,0:T(8,128)S(1)}, u32[]{:S(2)}, u32[]{:S(2)}) collective-permute-start(s32[152,128]{1,0:T(8,128)S(1)} %get-tuple-element.53), channel_id=1, source_target_pairs={{0,1},{1,0},{2,3},{3,2},{4,5},{5,4},{6,7},{7,6},{8,9},{9,8},{10,11... | collective-permute-start | bytes 233480 | tf_op jit(solution)/shard_map/ppermute | solution.py:863
  9.5 0.0 collective-permute-done.1.side_ref
  9.5 0.0 copy-done
  9.5 0.0 copy-done.1
  9.5 1.8 %shard_map.48 = (s32[96,384]{1,0:T(8,128)S(1)}, s32[112,256]{1,0:T(8,128)S(1)}, f32[8,384]{1,0:T(8,128)S(1)}, f32[384,128]{1,0:T(8,128)S(1)}, f32[2,240,128]{2,1...) custom-call(s32[4]{0:T(128)S(1)} %copy-done.1, ...), custom_call_target="tpu_custom_call" | custom-call | flops 402653184 | bytes 3145728 | tf_op jit(solution)/shard_map/pallas_call | solution.py:938
  11.3 4.5 %collective-permute-done.side_ref = bf16[1056,384]{1,0:T(8,128)(2,1)S(1)} collective-permute-done((bf16[1056,384]{1,0:T(8,128)(2,1)S(1)}, bf16[1056,384]{1,0:T(8,128)(2,1)S(1)}, u32[]{:S(2)}, u32[]{:S(2)}) %collective-permute-start) | collective-permute-done | bytes 811040 | tf_op jit(solution)/shard_map/ppermute | solution.py:881
  15.8 1.1 %shard_map.49 = (s32[224,128]{1,0:T(8,128)S(1)}, s32[224,128]{1,0:T(8,128)S(1)}, s32[224,128]{1,0:T(8,128)S(1)}, s32[224,128]{1,0:T(8,128)S(1)}) custom-call(bf16[400,2048]{1,0:T(8,128)(2,1)S(1)} %get-tuple-element.39.weighted_ref, bf16[1056,384]{1,0:T(8,128)(2,1)S(1)} %collective-permute-done.side_ref, s32[96,384]{1,0:T(8,128)S(1)} %get-tuple-element.42.close_ref, ...), custom_call_target="tpu_custom_call" | custom-call | flops 402653184 | bytes 3145728 | tf_op jit(solution)/shard_map/pallas_call | solution.py:951
  16.9 0.4 collective-permute-start.2
  17.3 2.5 %collective-permute-start.3 = (s32[224,128]{1,0:T(8,128)S(1)}, s32[224,128]{1,0:T(8,128)S(1)}, u32[]{:S(2)}, u32[]{:S(2)}) collective-permute-start(s32[224,128]{1,0:T(8,128)S(1)} %get-tuple-element.48), channel_id=1, source_target_pairs={{0,3},{1,2},{2,1},{3,0},{4,7},{5,6},{6,5},{7,4},{8,11},{9,10},{10,... | collective-permute-start | bytes 344072 | tf_op jit(solution)/shard_map/ppermute | solution.py:863
  19.8 0.0 collective-permute-done.5.refs_1_
  19.8 0.7 %collective-permute-start.4 = (s32[224,128]{1,0:T(8,128)S(1)}, s32[224,128]{1,0:T(8,128)S(1)}, u32[]{:S(2)}, u32[]{:S(2)}) collective-permute-start(s32[224,128]{1,0:T(8,128)S(1)} %get-tuple-element.49), channel_id=1, source_target_pairs={{0,1},{1,0},{2,3},{3,2},{4,5},{5,4},{6,7},{7,6},{8,9},{9,8},{10,11... | collective-permute-start | bytes 344072 | tf_op jit(solution)/shard_map/ppermute | solution.py:863
  20.6 0.0 collective-permute-done.6.refs_2_
  20.6 0.0 collective-permute-done.7.refs_3_
  20.6 1.8 %shard_map.50 = (f32[384,128]{1,0:T(8,128)S(1)}, f32[96,128]{1,0:T(8,128)S(1)}, f32[6,240,128]{2,1,0:T(8,128)S(1)}, bf16[128,128]{1,0:T(8,128)(2,1)S(1)}, f32[6,...) custom-call(s32[4]{0:T(128)S(1)} %copy-done.1, ...), custom_call_target="tpu_custom_call" | custom-call | flops 8589934592 | bytes 1048576 | tf_op jit(solution)/shard_map/pallas_call | solution.py:990
  22.4 1.0 %collective-permute-start.8 = (f32[48,128]{1,0:T(8,128)S(1)}, f32[48,128]{1,0:T(8,128)S(1)}, u32[]{:S(2)}, u32[]{:S(2)}) collective-permute-start(f32[48,128]{1,0:T(8,128)S(1)} %get-tuple-element.66), channel_id=1, source_target_pairs={{0,3},{1,2},{2,1},{3,0},{4,7},{5,6},{6,5},{7,4},{8,11},{9,10},{10,... | collective-permute-start | bytes 73736 | tf_op jit(solution)/shard_map/ppermute | solution.py:863
  23.4 1.9 %collective-permute-start.9 = (f32[48,128]{1,0:T(8,128)S(1)}, f32[48,128]{1,0:T(8,128)S(1)}, u32[]{:S(2)}, u32[]{:S(2)}) collective-permute-start(f32[48,128]{1,0:T(8,128)S(1)} %get-tuple-element.67), channel_id=1, source_target_pairs={{0,2},{1,3},{2,0},{3,1},{4,6},{5,7},{6,4},{7,5},{8,10},{9,11},{10,... | collective-permute-start | bytes 73736 | tf_op jit(solution)/shard_map/ppermute | solution.py:863
  25.3 0.0 collective-permute-done.2.refs_1_
  25.3 0.0 collective-permute-done.3.refs_2_
  25.3 1.0 %collective-permute-done.4.refs_3_ = s32[224,128]{1,0:T(8,128)S(1)} collective-permute-done((s32[224,128]{1,0:T(8,128)S(1)}, s32[224,128]{1,0:T(8,128)S(1)}, u32[]{:S(2)}, u32[]{:S(2)}) %collective-permute-start.4) | collective-permute-done | bytes 114720 | tf_op jit(solution)/shard_map/ppermute | solution.py:863
  26.3 1.2 %shard_map.51 = (f32[48,128]{1,0:T(8,128)S(1)}, f32[48,128]{1,0:T(8,128)S(1)}, bf16[48,128]{1,0:T(8,128)(2,1)S(1)}, bf16[48,128]{1,0:T(8,128)(2,1)S(1)}) custom-call(s32[4]{0:T(128)S(1)} %copy-done.1, s32[224,128]{1,0:T(8,128)S(1)} %get-tuple-element.46.refs_0_, s32[224,128]{1,0:T(8,128)S(1)} %collective-permute-done.2.refs_1_, ...), custom_call_target="tpu_custom_call" | custom-call | flops 67108864 | bytes 2097152 | tf_op jit(solution)/shard_map/pallas_call | solution.py:1009
  27.5 0.7 %collective-permute-start.10 = (f32[48,128]{1,0:T(8,128)S(1)}, f32[48,128]{1,0:T(8,128)S(1)}, u32[]{:S(2)}, u32[]{:S(2)}) collective-permute-start(f32[48,128]{1,0:T(8,128)S(1)} %get-tuple-element.68), channel_id=1, source_target_pairs={{0,1},{1,0},{2,3},{3,2},{4,5},{5,4},{6,7},{7,6},{16,17},{17,16},{1... | collective-permute-start | bytes 73736 | tf_op jit(solution)/shard_map/ppermute | solution.py:874
  28.2 4.8 %collective-permute-start.11 = (bf16[48,128]{1,0:T(8,128)(2,1)S(1)}, bf16[48,128]{1,0:T(8,128)(2,1)S(1)}, u32[]{:S(2)}, u32[]{:S(2)}) collective-permute-start(bf16[48,128]{1,0:T(8,128)(2,1)S(1)} %get-tuple-element.69), channel_id=1, source_target_pairs={{0,4},{1,5},{4,8},{5,9},{6,2},{7,3},{8,12},{9,13},{10,6},{11,7},{1... | collective-permute-start | bytes 36872 | tf_op jit(solution)/shard_map/ppermute | solution.py:982
  33.0 2.3 %collective-permute-start.12 = (bf16[48,128]{1,0:T(8,128)(2,1)S(1)}, bf16[48,128]{1,0:T(8,128)(2,1)S(1)}, u32[]{:S(2)}, u32[]{:S(2)}) collective-permute-start(bf16[48,128]{1,0:T(8,128)(2,1)S(1)} %get-tuple-element.70), channel_id=1, source_target_pairs={{8,9},{9,8},{10,11},{11,10},{12,13},{13,12},{14,15},{15,14},{24,25... | collective-permute-start | bytes 36872 | tf_op jit(solution)/shard_map/ppermute | solution.py:874
  35.3 0.0 collective-permute-done.8.refs_1_
  35.3 0.0 collective-permute-done.9.refs_2_
  35.3 0.0 collective-permute-done.11.refs_4_
  35.3 3.3 %collective-permute-done.12.refs_5_ = bf16[48,128]{1,0:T(8,128)(2,1)S(1)} collective-permute-done((bf16[48,128]{1,0:T(8,128)(2,1)S(1)}, bf16[48,128]{1,0:T(8,128)(2,1)S(1)}, u32[]{:S(2)}, u32[]{:S(2)}) %collective-permute-start.12) | collective-permute-done | bytes 12320 | tf_op jit(solution)/shard_map/ppermute | solution.py:874
  38.6 0.0 collective-permute-done.10.refs_3_
  38.6 0.8 %shard_map.52 = f32[50,96]{1,0:T(8,128)} custom-call(f32[48,128]{1,0:T(8,128)S(1)} %get-tuple-element.65.refs_0_, f32[48,128]{1,0:T(8,128)S(1)} %collective-permute-done.8.refs_1_, f32[48,128]{1,0:T(8,128)S(1)} %collective-permute-done.9.refs_2_, f32[48,128]{1,0:T(8,128)S(1)} %collective-permute-done.10.refs_3_, ...), custom_call_target="tpu_custom_call" | custom-call | tf_op jit(solution)/shard_map/pallas_call | solution.py:1019
  (2 shorter events, 0.0 us)
Async XLA Ops:
  0.0 4.8 %copy-start.2 = (s32[2048]{0:T(1024)S(1)}, s32[2048]{0:T(1024)}, u32[]{:S(2)}) copy-start(s32[2048]{0:T(1024)} %param.5) | copy-start | bytes 24580
  2.1 7.4 %copy-start = (s32[50,384]{1,0:T(8,128)S(1)}, s32[50,384]{1,0:T(8,128)}, u32[]{:S(2)}) copy-start(s32[50,384]{1,0:T(8,128)} %annot_ref.3) | copy-start | bytes 230404
  2.2 7.3 %copy-start.1 = (s32[4]{0:T(128)S(1)}, s32[4]{0:T(128)}, u32[]{:S(2)}) copy-start(s32[4]{0:T(128)} %reach_ref.5) | copy-start | bytes 52
  2.2 7.3 %collective-permute-start.1 = (bf16[1056,384]{1,0:T(8,128)(2,1)S(1)}, bf16[1056,384]{1,0:T(8,128)(2,1)S(1)}, u32[]{:S(2)}, u32[]{:S(2)}) collective-permute-start(bf16[1056,384]{1,0:T(8,128)(2,1)S(1)} %get-tuple-element.41), channel_id=1, source_target_pairs={{0,4},{4,0},{8,12},{12,8},{1,5},{5,1},{9,13},{13,9},{2,6},{6,2},{1... | collective-permute-start | bytes 2433032 | tf_op jit(solution)/shard_map/ppermute | solution.py:881
  2.3 13.6 %collective-permute-start = (bf16[1056,384]{1,0:T(8,128)(2,1)S(1)}, bf16[1056,384]{1,0:T(8,128)(2,1)S(1)}, u32[]{:S(2)}, u32[]{:S(2)}) collective-permute-start(bf16[1056,384]{1,0:T(8,128)(2,1)S(1)} %get-tuple-element.40), channel_id=1, source_target_pairs={{4,8},{8,4},{5,9},{9,5},{6,10},{10,6},{7,11},{11,7},{20,24},{24,20... | collective-permute-start | bytes 2433032 | tf_op jit(solution)/shard_map/ppermute | solution.py:881
  5.9 13.9 %collective-permute-start.5 = (s32[152,128]{1,0:T(8,128)S(1)}, s32[152,128]{1,0:T(8,128)S(1)}, u32[]{:S(2)}, u32[]{:S(2)}) collective-permute-start(s32[152,128]{1,0:T(8,128)S(1)} %get-tuple-element.51), channel_id=1, source_target_pairs={{0,2},{1,3},{2,0},{3,1},{4,6},{5,7},{6,4},{7,5},{8,10},{9,11},{10,... | collective-permute-start | bytes 233480 | tf_op jit(solution)/shard_map/ppermute | solution.py:863
  6.3 14.2 %collective-permute-start.6 = (s32[152,128]{1,0:T(8,128)S(1)}, s32[152,128]{1,0:T(8,128)S(1)}, u32[]{:S(2)}, u32[]{:S(2)}) collective-permute-start(s32[152,128]{1,0:T(8,128)S(1)} %get-tuple-element.52), channel_id=1, source_target_pairs={{0,3},{1,2},{2,1},{3,0},{4,7},{5,6},{6,5},{7,4},{8,11},{9,10},{10,... | collective-permute-start | bytes 233480 | tf_op jit(solution)/shard_map/ppermute | solution.py:863
  8.8 11.8 %collective-permute-start.7 = (s32[152,128]{1,0:T(8,128)S(1)}, s32[152,128]{1,0:T(8,128)S(1)}, u32[]{:S(2)}, u32[]{:S(2)}) collective-permute-start(s32[152,128]{1,0:T(8,128)S(1)} %get-tuple-element.53), channel_id=1, source_target_pairs={{0,1},{1,0},{2,3},{3,2},{4,5},{5,4},{6,7},{7,6},{8,9},{9,8},{10,11... | collective-permute-start | bytes 233480 | tf_op jit(solution)/shard_map/ppermute | solution.py:863
  16.9 8.3 %collective-permute-start.2 = (s32[224,128]{1,0:T(8,128)S(1)}, s32[224,128]{1,0:T(8,128)S(1)}, u32[]{:S(2)}, u32[]{:S(2)}) collective-permute-start(s32[224,128]{1,0:T(8,128)S(1)} %get-tuple-element.47), channel_id=1, source_target_pairs={{0,2},{1,3},{2,0},{3,1},{4,6},{5,7},{6,4},{7,5},{8,10},{9,11},{10,... | collective-permute-start | bytes 344072 | tf_op jit(solution)/shard_map/ppermute | solution.py:863
  17.3 7.9 %collective-permute-start.3 = (s32[224,128]{1,0:T(8,128)S(1)}, s32[224,128]{1,0:T(8,128)S(1)}, u32[]{:S(2)}, u32[]{:S(2)}) collective-permute-start(s32[224,128]{1,0:T(8,128)S(1)} %get-tuple-element.48), channel_id=1, source_target_pairs={{0,3},{1,2},{2,1},{3,0},{4,7},{5,6},{6,5},{7,4},{8,11},{9,10},{10,... | collective-permute-start | bytes 344072 | tf_op jit(solution)/shard_map/ppermute | solution.py:863
  19.8 6.4 %collective-permute-start.4 = (s32[224,128]{1,0:T(8,128)S(1)}, s32[224,128]{1,0:T(8,128)S(1)}, u32[]{:S(2)}, u32[]{:S(2)}) collective-permute-start(s32[224,128]{1,0:T(8,128)S(1)} %get-tuple-element.49), channel_id=1, source_target_pairs={{0,1},{1,0},{2,3},{3,2},{4,5},{5,4},{6,7},{7,6},{8,9},{9,8},{10,11... | collective-permute-start | bytes 344072 | tf_op jit(solution)/shard_map/ppermute | solution.py:863
  22.4 12.9 %collective-permute-start.8 = (f32[48,128]{1,0:T(8,128)S(1)}, f32[48,128]{1,0:T(8,128)S(1)}, u32[]{:S(2)}, u32[]{:S(2)}) collective-permute-start(f32[48,128]{1,0:T(8,128)S(1)} %get-tuple-element.66), channel_id=1, source_target_pairs={{0,3},{1,2},{2,1},{3,0},{4,7},{5,6},{6,5},{7,4},{8,11},{9,10},{10,... | collective-permute-start | bytes 73736 | tf_op jit(solution)/shard_map/ppermute | solution.py:863
  23.4 11.9 %collective-permute-start.9 = (f32[48,128]{1,0:T(8,128)S(1)}, f32[48,128]{1,0:T(8,128)S(1)}, u32[]{:S(2)}, u32[]{:S(2)}) collective-permute-start(f32[48,128]{1,0:T(8,128)S(1)} %get-tuple-element.67), channel_id=1, source_target_pairs={{0,2},{1,3},{2,0},{3,1},{4,6},{5,7},{6,4},{7,5},{8,10},{9,11},{10,... | collective-permute-start | bytes 73736 | tf_op jit(solution)/shard_map/ppermute | solution.py:863
  27.5 11.1 %collective-permute-start.10 = (f32[48,128]{1,0:T(8,128)S(1)}, f32[48,128]{1,0:T(8,128)S(1)}, u32[]{:S(2)}, u32[]{:S(2)}) collective-permute-start(f32[48,128]{1,0:T(8,128)S(1)} %get-tuple-element.68), channel_id=1, source_target_pairs={{0,1},{1,0},{2,3},{3,2},{4,5},{5,4},{6,7},{7,6},{16,17},{17,16},{1... | collective-permute-start | bytes 73736 | tf_op jit(solution)/shard_map/ppermute | solution.py:874
  28.2 7.1 %collective-permute-start.11 = (bf16[48,128]{1,0:T(8,128)(2,1)S(1)}, bf16[48,128]{1,0:T(8,128)(2,1)S(1)}, u32[]{:S(2)}, u32[]{:S(2)}) collective-permute-start(bf16[48,128]{1,0:T(8,128)(2,1)S(1)} %get-tuple-element.69), channel_id=1, source_target_pairs={{0,4},{1,5},{4,8},{5,9},{6,2},{7,3},{8,12},{9,13},{10,6},{11,7},{1... | collective-permute-start | bytes 36872 | tf_op jit(solution)/shard_map/ppermute | solution.py:982
  33.0 5.6 %collective-permute-start.12 = (bf16[48,128]{1,0:T(8,128)(2,1)S(1)}, bf16[48,128]{1,0:T(8,128)(2,1)S(1)}, u32[]{:S(2)}, u32[]{:S(2)}) collective-permute-start(bf16[48,128]{1,0:T(8,128)(2,1)S(1)} %get-tuple-element.70), channel_id=1, source_target_pairs={{8,9},{9,8},{10,11},{11,10},{12,13},{13,12},{14,15},{15,14},{24,25... | collective-permute-start | bytes 36872 | tf_op jit(solution)/shard_map/ppermute | solution.py:874

commit v23 on v21

--- a/solution.py
+++ b/solution.py
@@ -747,7 +747,7 @@
     near_parts, refs = refs[:groups], refs[groups:]
     own_ref, mine_ref, rows_ref, columns_ref, spare_rows_ref, spare_columns_ref = refs[:6]
     near_annot_ref, annot_ref, masks_ref, spare_mask_ref, own_rows_ref = refs[6:11]
-    out_ref, send_ref, near_out_ref, flipped, scores = refs[11:]
+    out_ref, send_ref, near_out_ref, flipped, scores, other = refs[11:]
     snps = annot_ref.shape[0]
     wide = snps // groups
     size = wide // 2
@@ -792,9 +792,11 @@
     slice_rows = pl.ds(pl.multiple_of(me * wide, 8), wide)
     direct = dot_rounded(near_here, columns_ref[...], 1)
     turned = pltpu.roll(direct, HALF_LANES, 1)
-    for values, places in zip((direct, turned), owner_places(groups, size)):
+    left_places, right_places = owner_places(groups, size)
+    other[...] = jnp.zeros_like(other)
+    for ref, values, places in ((scores, direct, left_places[:-1]), (other, turned, right_places)):
         for slot, place in enumerate(places):
-            scores[pl.ds(pl.multiple_of(place, 8), size), :] += values[slot * size : (slot + 1) * size, :]
+            ref[pl.ds(pl.multiple_of(place, 8), size), :] += values[slot * size : (slot + 1) * size, :]
     product = 1.0
     for pop in range(2):
         row_stats = [spare_rows_ref[3 * pop + k] for k in range(3)]
@@ -825,7 +827,8 @@
 
     def packed(step):
         group = partner(me, step, groups)
-        return pack_halves(scores[pl.ds(pl.multiple_of(group * wide, 8), wide), :])
+        rows = pl.ds(pl.multiple_of(group * wide, 8), wide)
+        return pack_halves(scores[rows, :] + other[rows, :])
 
     out_ref[...] = packed(0)
     send_ref[...] = packed(1).astype(send_ref.dtype)
@@ -998,7 +1001,7 @@
             functools.partial(near_score_kernel, groups, share),
             [packed_share, sent, sent],
             [SMEM] + [VMEM] * (groups + 11),
-            [pltpu.VMEM((LANES, LANES), i32), pltpu.VMEM((snps, LANES), f32)],
+            [pltpu.VMEM((LANES, LANES), i32)] + [pltpu.VMEM((snps, LANES), f32)] * 2,
             flops=1 << 26,
             moved=1 << 21,
         )(reach, *near_parts, *prepared, own_annots, masks, spare_mask, own_rows)

time: 35.2 us -> 35.2 us (level)
  no operation moved by 1% of the time
where the time goes in v23:
time: 35.2 us; the launch traced here: 34.8 us
  starting transfers between devices  20 us (57%)
  Pallas kernels  9.88 us (28%)
  waiting for transfers between devices  4.84 us (14%)
    ppermute x9, starting transfers between devices, around(): lax.ppermute(value, 'hap', [(source, partner(source, step, groups)) for s...  11.6 us
    ppermute x2, starting transfers between devices, swapped(): return lax.ppermute(value, 'snp', pairs)  4.59 us
    ppermute x1, starting transfers between devices, to_neighbour(): return lax.ppermute(value, ('snp', 'hap'), pairs)  3.83 us
    ppermute x2, waiting for transfers between devices, swapped(): return lax.ppermute(value, 'snp', pairs)  3.58 us
    pallas_call x1, Pallas kernels, per_device(): call(prepare_kernel, [shape((rows, snps), bf16), packed, packed], [HBM, H...  2.14 us
    pallas_call x1, Pallas kernels, per_device(): call(functools.partial(own_score_kernel, groups, share), [by_snp, shape((...  1.8 us
    pallas_call x1, Pallas kernels, per_device(): call(functools.partial(close_kernel, groups), [shape(*args) for args in s...  1.79 us
    pallas_call x1, Pallas kernels, per_device(): call(functools.partial(near_score_kernel, groups, share), [packed_share,...  1.15 us
  transfers between devices with their start and end apart: 12, of which 3 were waited for; matrix products, arithmetic and copies ran while one was open for 0% of the time, Pallas kernels for 20%

profile of v23, /device:TPU:1, one launch (start us, length us, event | category | flops | bytes accessed | tf_op | source)
XLA Modules:
  0.0 34.8 jit_solution(7039489881714326432)
XLA Ops:
  0.0 0.0 copy-start.2
  0.0 2.1 %shard_map.46 = (bf16[2048,384]{1,0:T(8,128)(2,1)S(1)}, bf16[1056,384]{1,0:T(8,128)(2,1)S(1)}, bf16[1056,384]{1,0:T(8,128)(2,1)S(1)}) custom-call(s32[2048,384]{1,0:T(8,128)} %hap_ref.1, s32[50,384]{1,0:T(8,128)} %annot_ref.3), custom_call_target="tpu_custom_call" | custom-call | bytes 6291456 | tf_op jit(solution)/shard_map/pallas_call | solution.py:891
  2.1 0.0 copy-start
  2.2 0.0 copy-start.1
  2.2 0.1 collective-permute-start.1
  2.3 4.5 %collective-permute-start = (bf16[1056,384]{1,0:T(8,128)(2,1)S(1)}, bf16[1056,384]{1,0:T(8,128)(2,1)S(1)}, u32[]{:S(2)}, u32[]{:S(2)}) collective-permute-start(bf16[1056,384]{1,0:T(8,128)(2,1)S(1)} %get-tuple-element.39), channel_id=1, source_target_pairs={{4,8},{8,4},{5,9},{9,5},{6,10},{10,6},{7,11},{11,7},{20,24},{24,20... | collective-permute-start | bytes 2433032 | tf_op jit(solution)/shard_map/ppermute | solution.py:872
  6.8 0.0 copy-done.2
  6.8 1.1 %shard_map.47 = (bf16[400,2048]{1,0:T(8,128)(2,1)S(1)}, f32[8,384]{1,0:T(8,128)S(1)}, s32[152,128]{1,0:T(8,128)S(1)}, s32[152,128]{1,0:T(8,128)S(1)}, s32[152,128]{1,0:T(8,128)S(1)}, /*index=5*/s32[152,128]{1,0:T(8,128)S(1)}) custom-call(bf16[2048,384]{1,0:T(8,128)(2,1)S(1)} %get-tuple-element.37.alleles_ref, s32[1,2048]{1,0:T(1,128)S(1)} %bitcast.1), custom_call_target="tpu_custom_call" | custom-call | flops 603979776 | bytes 3145728 | tf_op jit(solution)/shard_map/pallas_call | solution.py:912
  7.9 2.4 %collective-permute-start.5 = (s32[152,128]{1,0:T(8,128)S(1)}, s32[152,128]{1,0:T(8,128)S(1)}, u32[]{:S(2)}, u32[]{:S(2)}) collective-permute-start(s32[152,128]{1,0:T(8,128)S(1)} %get-tuple-element.50), channel_id=1, source_target_pairs={{0,2},{1,3},{2,0},{3,1},{4,6},{5,7},{6,4},{7,5},{8,10},{9,11},{10,... | collective-permute-start | bytes 233480 | tf_op jit(solution)/shard_map/ppermute | solution.py:863
  10.3 1.1 %collective-permute-start.6 = (s32[152,128]{1,0:T(8,128)S(1)}, s32[152,128]{1,0:T(8,128)S(1)}, u32[]{:S(2)}, u32[]{:S(2)}) collective-permute-start(s32[152,128]{1,0:T(8,128)S(1)} %get-tuple-element.51), channel_id=1, source_target_pairs={{0,3},{1,2},{2,1},{3,0},{4,7},{5,6},{6,5},{7,4},{8,11},{9,10},{10,... | collective-permute-start | bytes 233480 | tf_op jit(solution)/shard_map/ppermute | solution.py:863
  11.4 0.2 collective-permute-start.7
  11.6 0.0 collective-permute-done.1.side_ref
  11.6 0.0 copy-done
  11.6 0.0 copy-done.1
  11.6 1.8 %shard_map.48 = (s32[96,384]{1,0:T(8,128)S(1)}, s32[112,256]{1,0:T(8,128)S(1)}, f32[8,384]{1,0:T(8,128)S(1)}, f32[384,128]{1,0:T(8,128)S(1)}, f32[2,240,128]{2,1...) custom-call(s32[4]{0:T(128)S(1)} %copy-done.1, ...), custom_call_target="tpu_custom_call" | custom-call | flops 402653184 | bytes 3145728 | tf_op jit(solution)/shard_map/pallas_call | solution.py:929
  13.4 3.6 %collective-permute-done.side_ref = bf16[1056,384]{1,0:T(8,128)(2,1)S(1)} collective-permute-done((bf16[1056,384]{1,0:T(8,128)(2,1)S(1)}, bf16[1056,384]{1,0:T(8,128)(2,1)S(1)}, u32[]{:S(2)}, u32[]{:S(2)}) %collective-permute-start) | collective-permute-done | bytes 811040 | tf_op jit(solution)/shard_map/ppermute | solution.py:872
  17.0 1.1 %shard_map.49 = (s32[224,128]{1,0:T(8,128)S(1)}, s32[224,128]{1,0:T(8,128)S(1)}, s32[224,128]{1,0:T(8,128)S(1)}, s32[224,128]{1,0:T(8,128)S(1)}) custom-call(bf16[400,2048]{1,0:T(8,128)(2,1)S(1)} %get-tuple-element.38.weighted_ref, bf16[1056,384]{1,0:T(8,128)(2,1)S(1)} %collective-permute-done.side_ref, s32[96,384]{1,0:T(8,128)S(1)} %get-tuple-element.41.close_ref, ...), custom_call_target="tpu_custom_call" | custom-call | flops 402653184 | bytes 3145728 | tf_op jit(solution)/shard_map/pallas_call | solution.py:942
  18.1 3.0 %collective-permute-start.2 = (s32[224,128]{1,0:T(8,128)S(1)}, s32[224,128]{1,0:T(8,128)S(1)}, u32[]{:S(2)}, u32[]{:S(2)}) collective-permute-start(s32[224,128]{1,0:T(8,128)S(1)} %get-tuple-element.46), channel_id=1, source_target_pairs={{0,2},{1,3},{2,0},{3,1},{4,6},{5,7},{6,4},{7,5},{8,10},{9,11},{10,... | collective-permute-start | bytes 344072 | tf_op jit(solution)/shard_map/ppermute | solution.py:863
  21.1 1.1 %collective-permute-start.3 = (s32[224,128]{1,0:T(8,128)S(1)}, s32[224,128]{1,0:T(8,128)S(1)}, u32[]{:S(2)}, u32[]{:S(2)}) collective-permute-start(s32[224,128]{1,0:T(8,128)S(1)} %get-tuple-element.47), channel_id=1, source_target_pairs={{0,3},{1,2},{2,1},{3,0},{4,7},{5,6},{6,5},{7,4},{8,11},{9,10},{10,... | collective-permute-start | bytes 344072 | tf_op jit(solution)/shard_map/ppermute | solution.py:863
  22.2 0.0 collective-permute-done.5.refs_1_
  22.2 0.3 collective-permute-start.4
  22.5 0.0 collective-permute-done.6.refs_2_
  22.5 0.0 collective-permute-done.7.refs_3_
  22.5 1.8 %shard_map.50 = (f32[384,128]{1,0:T(8,128)S(1)}, f32[96,128]{1,0:T(8,128)S(1)}, f32[6,240,128]{2,1,0:T(8,128)S(1)}, bf16[128,128]{1,0:T(8,128)(2,1)S(1)}, f32[6,...) custom-call(s32[4]{0:T(128)S(1)} %copy-done.1, ...), custom_call_target="tpu_custom_call" | custom-call | flops 8589934592 | bytes 1048576 | tf_op jit(solution)/shard_map/pallas_call | solution.py:981
  24.3 2.4 %collective-permute-start.8 = (bf16[48,128]{1,0:T(8,128)(2,1)S(1)}, bf16[48,128]{1,0:T(8,128)(2,1)S(1)}, u32[]{:S(2)}, u32[]{:S(2)}) collective-permute-start(bf16[48,128]{1,0:T(8,128)(2,1)S(1)} %get-tuple-element.65), channel_id=1, source_target_pairs={{0,3},{1,2},{2,1},{3,0},{4,7},{5,6},{6,5},{7,4},{8,11},{9,10},{10,... | collective-permute-start | bytes 36872 | tf_op jit(solution)/shard_map/ppermute | solution.py:863
  26.7 0.1 collective-permute-start.9
  26.8 0.0 collective-permute-done.2.refs_1_
  26.8 0.0 collective-permute-done.3.refs_2_
  26.8 0.4 %collective-permute-done.4.refs_3_ = s32[224,128]{1,0:T(8,128)S(1)} collective-permute-done((s32[224,128]{1,0:T(8,128)S(1)}, s32[224,128]{1,0:T(8,128)S(1)}, u32[]{:S(2)}, u32[]{:S(2)}) %collective-permute-start.4) | collective-permute-done | bytes 114720 | tf_op jit(solution)/shard_map/ppermute | solution.py:863
  27.3 1.2 %shard_map.51 = (f32[48,128]{1,0:T(8,128)S(1)}, bf16[48,128]{1,0:T(8,128)(2,1)S(1)}, bf16[48,128]{1,0:T(8,128)(2,1)S(1)}) custom-call(s32[4]{0:T(128)S(1)} %copy-done.1, s32[224,128]{1,0:T(8,128)S(1)} %get-tuple-element.45.refs_0_, s32[224,128]{1,0:T(8,128)S(1)} %collective-permute-done.2.refs_1_, s32[224,128]{1,0:T(8,128)S(1)} %collective-permute-done.3.refs_2_, ...), custom_call_target="tpu_custom_call" | custom-call | flops 67108864 | bytes 2097152 | tf_op jit(solution)/shard_map/pallas_call | solution.py:1000
  28.4 1.0 %collective-permute-start.10 = (bf16[48,128]{1,0:T(8,128)(2,1)S(1)}, bf16[48,128]{1,0:T(8,128)(2,1)S(1)}, u32[]{:S(2)}, u32[]{:S(2)}) collective-permute-start(bf16[48,128]{1,0:T(8,128)(2,1)S(1)} %get-tuple-element.67), channel_id=1, source_target_pairs={{0,1},{1,0},{2,3},{3,2},{4,5},{5,4},{6,7},{7,6},{8,9},{9,8},{10,11... | collective-permute-start | bytes 36872 | tf_op jit(solution)/shard_map/ppermute | solution.py:863
  29.4 3.8 %collective-permute-start.11 = (bf16[48,128]{1,0:T(8,128)(2,1)S(1)}, bf16[48,128]{1,0:T(8,128)(2,1)S(1)}, u32[]{:S(2)}, u32[]{:S(2)}) collective-permute-start(bf16[48,128]{1,0:T(8,128)(2,1)S(1)} %get-tuple-element.68), channel_id=1, source_target_pairs={{0,4},{1,5},{4,8},{5,9},{6,2},{7,3},{8,12},{9,13},{10,6},{11,7},{1... | collective-permute-start | bytes 36872 | tf_op jit(solution)/shard_map/ppermute | solution.py:973
  33.3 0.0 collective-permute-done.8.refs_1_
  33.3 0.0 collective-permute-done.9.refs_2_
  33.3 0.0 collective-permute-done.10.refs_3_
  33.3 0.8 %collective-permute-done.11.refs_4_ = bf16[48,128]{1,0:T(8,128)(2,1)S(1)} collective-permute-done((bf16[48,128]{1,0:T(8,128)(2,1)S(1)}, bf16[48,128]{1,0:T(8,128)(2,1)S(1)}, u32[]{:S(2)}, u32[]{:S(2)}) %collective-permute-start.11) | collective-permute-done | bytes 12320 | tf_op jit(solution)/shard_map/ppermute | solution.py:973
  34.1 0.7 %shard_map.52 = f32[50,96]{1,0:T(8,128)} custom-call(f32[48,128]{1,0:T(8,128)S(1)} %get-tuple-element.64.refs_0_, bf16[48,128]{1,0:T(8,128)(2,1)S(1)} %collective-permute-done.8.refs_1_, bf16[48,128]{1,0:T(8,128)(2,1)S(1)} %collective-permute-done.9.refs_2_, bf16[48,128]{1,0:T(8,128)(2,1)S(1)} %collective-permute-done.10.refs_3_, ...), custom_call_target="tpu_custom_call" | custom-call | tf_op jit(solution)/shard_map/pallas_call | solution.py:1009
  (2 shorter events, 0.0 us)
Async XLA Ops:
  0.0 6.8 %copy-start.2 = (s32[2048]{0:T(1024)S(1)}, s32[2048]{0:T(1024)}, u32[]{:S(2)}) copy-start(s32[2048]{0:T(1024)} %param.5) | copy-start | bytes 24580
  2.1 9.5 %copy-start = (s32[50,384]{1,0:T(8,128)S(1)}, s32[50,384]{1,0:T(8,128)}, u32[]{:S(2)}) copy-start(s32[50,384]{1,0:T(8,128)} %annot_ref.3) | copy-start | bytes 230404
  2.2 9.4 %copy-start.1 = (s32[4]{0:T(128)S(1)}, s32[4]{0:T(128)}, u32[]{:S(2)}) copy-start(s32[4]{0:T(128)} %reach_ref.5) | copy-start | bytes 52
  2.2 9.4 %collective-permute-start.1 = (bf16[1056,384]{1,0:T(8,128)(2,1)S(1)}, bf16[1056,384]{1,0:T(8,128)(2,1)S(1)}, u32[]{:S(2)}, u32[]{:S(2)}) collective-permute-start(bf16[1056,384]{1,0:T(8,128)(2,1)S(1)} %get-tuple-element.40), channel_id=1, source_target_pairs={{0,4},{4,0},{8,12},{12,8},{1,5},{5,1},{9,13},{13,9},{2,6},{6,2},{1... | collective-permute-start | bytes 2433032 | tf_op jit(solution)/shard_map/ppermute | solution.py:872
  2.3 14.7 %collective-permute-start = (bf16[1056,384]{1,0:T(8,128)(2,1)S(1)}, bf16[1056,384]{1,0:T(8,128)(2,1)S(1)}, u32[]{:S(2)}, u32[]{:S(2)}) collective-permute-start(bf16[1056,384]{1,0:T(8,128)(2,1)S(1)} %get-tuple-element.39), channel_id=1, source_target_pairs={{4,8},{8,4},{5,9},{9,5},{6,10},{10,6},{7,11},{11,7},{20,24},{24,20... | collective-permute-start | bytes 2433032 | tf_op jit(solution)/shard_map/ppermute | solution.py:872
  7.9 14.3 %collective-permute-start.5 = (s32[152,128]{1,0:T(8,128)S(1)}, s32[152,128]{1,0:T(8,128)S(1)}, u32[]{:S(2)}, u32[]{:S(2)}) collective-permute-start(s32[152,128]{1,0:T(8,128)S(1)} %get-tuple-element.50), channel_id=1, source_target_pairs={{0,2},{1,3},{2,0},{3,1},{4,6},{5,7},{6,4},{7,5},{8,10},{9,11},{10,... | collective-permute-start | bytes 233480 | tf_op jit(solution)/shard_map/ppermute | solution.py:863
  10.3 12.2 %collective-permute-start.6 = (s32[152,128]{1,0:T(8,128)S(1)}, s32[152,128]{1,0:T(8,128)S(1)}, u32[]{:S(2)}, u32[]{:S(2)}) collective-permute-start(s32[152,128]{1,0:T(8,128)S(1)} %get-tuple-element.51), channel_id=1, source_target_pairs={{0,3},{1,2},{2,1},{3,0},{4,7},{5,6},{6,5},{7,4},{8,11},{9,10},{10,... | collective-permute-start | bytes 233480 | tf_op jit(solution)/shard_map/ppermute | solution.py:863
  11.4 11.1 %collective-permute-start.7 = (s32[152,128]{1,0:T(8,128)S(1)}, s32[152,128]{1,0:T(8,128)S(1)}, u32[]{:S(2)}, u32[]{:S(2)}) collective-permute-start(s32[152,128]{1,0:T(8,128)S(1)} %get-tuple-element.52), channel_id=1, source_target_pairs={{0,1},{1,0},{2,3},{3,2},{4,5},{5,4},{6,7},{7,6},{8,9},{9,8},{10,11... | collective-permute-start | bytes 233480 | tf_op jit(solution)/shard_map/ppermute | solution.py:863
  18.1 8.7 %collective-permute-start.2 = (s32[224,128]{1,0:T(8,128)S(1)}, s32[224,128]{1,0:T(8,128)S(1)}, u32[]{:S(2)}, u32[]{:S(2)}) collective-permute-start(s32[224,128]{1,0:T(8,128)S(1)} %get-tuple-element.46), channel_id=1, source_target_pairs={{0,2},{1,3},{2,0},{3,1},{4,6},{5,7},{6,4},{7,5},{8,10},{9,11},{10,... | collective-permute-start | bytes 344072 | tf_op jit(solution)/shard_map/ppermute | solution.py:863
  21.1 5.7 %collective-permute-start.3 = (s32[224,128]{1,0:T(8,128)S(1)}, s32[224,128]{1,0:T(8,128)S(1)}, u32[]{:S(2)}, u32[]{:S(2)}) collective-permute-start(s32[224,128]{1,0:T(8,128)S(1)} %get-tuple-element.47), channel_id=1, source_target_pairs={{0,3},{1,2},{2,1},{3,0},{4,7},{5,6},{6,5},{7,4},{8,11},{9,10},{10,... | collective-permute-start | bytes 344072 | tf_op jit(solution)/shard_map/ppermute | solution.py:863
  22.2 5.1 %collective-permute-start.4 = (s32[224,128]{1,0:T(8,128)S(1)}, s32[224,128]{1,0:T(8,128)S(1)}, u32[]{:S(2)}, u32[]{:S(2)}) collective-permute-start(s32[224,128]{1,0:T(8,128)S(1)} %get-tuple-element.48), channel_id=1, source_target_pairs={{0,1},{1,0},{2,3},{3,2},{4,5},{5,4},{6,7},{7,6},{8,9},{9,8},{10,11... | collective-permute-start | bytes 344072 | tf_op jit(solution)/shard_map/ppermute | solution.py:863
  24.3 9.0 %collective-permute-start.8 = (bf16[48,128]{1,0:T(8,128)(2,1)S(1)}, bf16[48,128]{1,0:T(8,128)(2,1)S(1)}, u32[]{:S(2)}, u32[]{:S(2)}) collective-permute-start(bf16[48,128]{1,0:T(8,128)(2,1)S(1)} %get-tuple-element.65), channel_id=1, source_target_pairs={{0,3},{1,2},{2,1},{3,0},{4,7},{5,6},{6,5},{7,4},{8,11},{9,10},{10,... | collective-permute-start | bytes 36872 | tf_op jit(solution)/shard_map/ppermute | solution.py:863
  26.7 6.6 %collective-permute-start.9 = (bf16[48,128]{1,0:T(8,128)(2,1)S(1)}, bf16[48,128]{1,0:T(8,128)(2,1)S(1)}, u32[]{:S(2)}, u32[]{:S(2)}) collective-permute-start(bf16[48,128]{1,0:T(8,128)(2,1)S(1)} %get-tuple-element.66), channel_id=1, source_target_pairs={{0,2},{1,3},{2,0},{3,1},{4,6},{5,7},{6,4},{7,5},{8,10},{9,11},{10,... | collective-permute-start | bytes 36872 | tf_op jit(solution)/shard_map/ppermute | solution.py:863
  28.4 4.9 %collective-permute-start.10 = (bf16[48,128]{1,0:T(8,128)(2,1)S(1)}, bf16[48,128]{1,0:T(8,128)(2,1)S(1)}, u32[]{:S(2)}, u32[]{:S(2)}) collective-permute-start(bf16[48,128]{1,0:T(8,128)(2,1)S(1)} %get-tuple-element.67), channel_id=1, source_target_pairs={{0,1},{1,0},{2,3},{3,2},{4,5},{5,4},{6,7},{7,6},{8,9},{9,8},{10,11... | collective-permute-start | bytes 36872 | tf_op jit(solution)/shard_map/ppermute | solution.py:863
  29.4 4.6 %collective-permute-start.11 = (bf16[48,128]{1,0:T(8,128)(2,1)S(1)}, bf16[48,128]{1,0:T(8,128)(2,1)S(1)}, u32[]{:S(2)}, u32[]{:S(2)}) collective-permute-start(bf16[48,128]{1,0:T(8,128)(2,1)S(1)} %get-tuple-element.68), channel_id=1, source_target_pairs={{0,4},{1,5},{4,8},{5,9},{6,2},{7,3},{8,12},{9,13},{10,6},{11,7},{1... | collective-permute-start | bytes 36872 | tf_op jit(solution)/shard_map/ppermute | solution.py:973

commit v24 on v23

--- a/solution.py
+++ b/solution.py
@@ -956,6 +956,7 @@
             flops=2 * rows * snps * snps,
             moved=rows * snps * 4,
         )(weighted, from_far, from_close, totals, *own_parts)
+    order = range(groups - 1, 0, -1)
     near_parts = [near_parts[0]] + [around(near_parts[k], groups, k) for k in order]
 
     if not by_column:

time: 35.2 us -> 35.4 us (level)
  starting transfers between devices: 20 us -> 21 us
  waiting for transfers between devices: 4.84 us -> 4.23 us
    ppermute x9, starting transfers between devices: 11.6 us -> 12.6 us  [around(): lax.ppermute(value, 'hap', [(source, partner(source, step, groups)) for s...]
where the time goes in v24:
time: 35.4 us; the launch traced here: 35.3 us
  starting transfers between devices  21 us (59%)
  Pallas kernels  9.88 us (28%)
  waiting for transfers between devices  4.23 us (12%)
    ppermute x9, starting transfers between devices, around(): lax.ppermute(value, 'hap', [(source, partner(source, step, groups)) for s...  12.6 us
    ppermute x2, starting transfers between devices, swapped(): return lax.ppermute(value, 'snp', pairs)  4.59 us
    ppermute x1, starting transfers between devices, to_neighbour(): return lax.ppermute(value, ('snp', 'hap'), pairs)  3.85 us
    ppermute x2, waiting for transfers between devices, swapped(): return lax.ppermute(value, 'snp', pairs)  3.29 us
    pallas_call x1, Pallas kernels, per_device(): call(prepare_kernel, [shape((rows, snps), bf16), packed, packed], [HBM, H...  2.14 us
    pallas_call x1, Pallas kernels, per_device(): call(functools.partial(own_score_kernel, groups, share), [by_snp, shape((...  1.8 us
    pallas_call x1, Pallas kernels, per_device(): call(functools.partial(close_kernel, groups), [shape(*args) for args in s...  1.79 us
    pallas_call x1, Pallas kernels, per_device(): call(functools.partial(near_score_kernel, groups, share), [packed_share,...  1.15 us
  transfers between devices with their start and end apart: 12, of which 3 were waited for; matrix products, arithmetic and copies ran while one was open for 0% of the time, Pallas kernels for 20%

profile of v24, /device:TPU:1, one launch (start us, length us, event | category | flops | bytes accessed | tf_op | source)
XLA Modules:
  0.0 35.3 jit_solution(2963807392772666897)
XLA Ops:
  0.0 0.0 copy-start.2
  0.0 2.1 %shard_map.46 = (bf16[2048,384]{1,0:T(8,128)(2,1)S(1)}, bf16[1056,384]{1,0:T(8,128)(2,1)S(1)}, bf16[1056,384]{1,0:T(8,128)(2,1)S(1)}) custom-call(s32[2048,384]{1,0:T(8,128)} %hap_ref.1, s32[50,384]{1,0:T(8,128)} %annot_ref.3), custom_call_target="tpu_custom_call" | custom-call | bytes 6291456 | tf_op jit(solution)/shard_map/pallas_call | solution.py:891
  2.1 0.0 copy-start
  2.2 0.0 copy-start.1
  2.2 0.1 collective-permute-start.1
  2.3 4.5 %collective-permute-start = (bf16[1056,384]{1,0:T(8,128)(2,1)S(1)}, bf16[1056,384]{1,0:T(8,128)(2,1)S(1)}, u32[]{:S(2)}, u32[]{:S(2)}) collective-permute-start(bf16[1056,384]{1,0:T(8,128)(2,1)S(1)} %get-tuple-element.39), channel_id=1, source_target_pairs={{4,8},{8,4},{5,9},{9,5},{6,10},{10,6},{7,11},{11,7},{20,24},{24,20... | collective-permute-start | bytes 2433032 | tf_op jit(solution)/shard_map/ppermute | solution.py:872
  6.8 0.0 copy-done.2
  6.8 1.1 %shard_map.47 = (bf16[400,2048]{1,0:T(8,128)(2,1)S(1)}, f32[8,384]{1,0:T(8,128)S(1)}, s32[152,128]{1,0:T(8,128)S(1)}, s32[152,128]{1,0:T(8,128)S(1)}, s32[152,128]{1,0:T(8,128)S(1)}, /*index=5*/s32[152,128]{1,0:T(8,128)S(1)}) custom-call(bf16[2048,384]{1,0:T(8,128)(2,1)S(1)} %get-tuple-element.37.alleles_ref, s32[1,2048]{1,0:T(1,128)S(1)} %bitcast.1), custom_call_target="tpu_custom_call" | custom-call | flops 603979776 | bytes 3145728 | tf_op jit(solution)/shard_map/pallas_call | solution.py:912
  7.9 2.4 %collective-permute-start.5 = (s32[152,128]{1,0:T(8,128)S(1)}, s32[152,128]{1,0:T(8,128)S(1)}, u32[]{:S(2)}, u32[]{:S(2)}) collective-permute-start(s32[152,128]{1,0:T(8,128)S(1)} %get-tuple-element.50), channel_id=1, source_target_pairs={{0,2},{1,3},{2,0},{3,1},{4,6},{5,7},{6,4},{7,5},{8,10},{9,11},{10,... | collective-permute-start | bytes 233480 | tf_op jit(solution)/shard_map/ppermute | solution.py:863
  10.3 1.1 %collective-permute-start.6 = (s32[152,128]{1,0:T(8,128)S(1)}, s32[152,128]{1,0:T(8,128)S(1)}, u32[]{:S(2)}, u32[]{:S(2)}) collective-permute-start(s32[152,128]{1,0:T(8,128)S(1)} %get-tuple-element.51), channel_id=1, source_target_pairs={{0,3},{1,2},{2,1},{3,0},{4,7},{5,6},{6,5},{7,4},{8,11},{9,10},{10,... | collective-permute-start | bytes 233480 | tf_op jit(solution)/shard_map/ppermute | solution.py:863
  11.4 0.2 collective-permute-start.7
  11.6 0.0 collective-permute-done.1.side_ref
  11.6 0.0 copy-done
  11.6 0.0 copy-done.1
  11.6 1.8 %shard_map.48 = (s32[96,384]{1,0:T(8,128)S(1)}, s32[112,256]{1,0:T(8,128)S(1)}, f32[8,384]{1,0:T(8,128)S(1)}, f32[384,128]{1,0:T(8,128)S(1)}, f32[2,240,128]{2,1...) custom-call(s32[4]{0:T(128)S(1)} %copy-done.1, ...), custom_call_target="tpu_custom_call" | custom-call | flops 402653184 | bytes 3145728 | tf_op jit(solution)/shard_map/pallas_call | solution.py:929
  13.4 3.3 %collective-permute-done.side_ref = bf16[1056,384]{1,0:T(8,128)(2,1)S(1)} collective-permute-done((bf16[1056,384]{1,0:T(8,128)(2,1)S(1)}, bf16[1056,384]{1,0:T(8,128)(2,1)S(1)}, u32[]{:S(2)}, u32[]{:S(2)}) %collective-permute-start) | collective-permute-done | bytes 811040 | tf_op jit(solution)/shard_map/ppermute | solution.py:872
  16.7 1.1 %shard_map.49 = (s32[224,128]{1,0:T(8,128)S(1)}, s32[224,128]{1,0:T(8,128)S(1)}, s32[224,128]{1,0:T(8,128)S(1)}, s32[224,128]{1,0:T(8,128)S(1)}) custom-call(bf16[400,2048]{1,0:T(8,128)(2,1)S(1)} %get-tuple-element.38.weighted_ref, bf16[1056,384]{1,0:T(8,128)(2,1)S(1)} %collective-permute-done.side_ref, s32[96,384]{1,0:T(8,128)S(1)} %get-tuple-element.41.close_ref, ...), custom_call_target="tpu_custom_call" | custom-call | flops 402653184 | bytes 3145728 | tf_op jit(solution)/shard_map/pallas_call | solution.py:942
  17.8 4.3 %collective-permute-start.2 = (s32[224,128]{1,0:T(8,128)S(1)}, s32[224,128]{1,0:T(8,128)S(1)}, u32[]{:S(2)}, u32[]{:S(2)}) collective-permute-start(s32[224,128]{1,0:T(8,128)S(1)} %get-tuple-element.46), channel_id=1, source_target_pairs={{0,3},{1,2},{2,1},{3,0},{4,7},{5,6},{6,5},{7,4},{8,11},{9,10},{10,... | collective-permute-start | bytes 344072 | tf_op jit(solution)/shard_map/ppermute | solution.py:863
  22.1 0.0 collective-permute-start.3
  22.1 0.0 collective-permute-done.5.refs_1_
  22.1 0.4 %collective-permute-start.4 = (s32[224,128]{1,0:T(8,128)S(1)}, s32[224,128]{1,0:T(8,128)S(1)}, u32[]{:S(2)}, u32[]{:S(2)}) collective-permute-start(s32[224,128]{1,0:T(8,128)S(1)} %get-tuple-element.48), channel_id=1, source_target_pairs={{0,1},{1,0},{2,3},{3,2},{4,5},{5,4},{6,7},{7,6},{8,9},{9,8},{10,11... | collective-permute-start | bytes 344072 | tf_op jit(solution)/shard_map/ppermute | solution.py:863
  22.5 0.0 collective-permute-done.6.refs_2_
  22.5 0.0 collective-permute-done.7.refs_3_
  22.5 1.8 %shard_map.50 = (f32[384,128]{1,0:T(8,128)S(1)}, f32[96,128]{1,0:T(8,128)S(1)}, f32[6,240,128]{2,1,0:T(8,128)S(1)}, bf16[128,128]{1,0:T(8,128)(2,1)S(1)}, f32[6,...) custom-call(s32[4]{0:T(128)S(1)} %copy-done.1, ...), custom_call_target="tpu_custom_call" | custom-call | flops 8589934592 | bytes 1048576 | tf_op jit(solution)/shard_map/pallas_call | solution.py:982
  24.3 3.2 %collective-permute-start.8 = (bf16[48,128]{1,0:T(8,128)(2,1)S(1)}, bf16[48,128]{1,0:T(8,128)(2,1)S(1)}, u32[]{:S(2)}, u32[]{:S(2)}) collective-permute-start(bf16[48,128]{1,0:T(8,128)(2,1)S(1)} %get-tuple-element.65), channel_id=1, source_target_pairs={{0,3},{1,2},{2,1},{3,0},{4,7},{5,6},{6,5},{7,4},{8,11},{9,10},{10,... | collective-permute-start | bytes 36872 | tf_op jit(solution)/shard_map/ppermute | solution.py:863
  27.6 0.0 collective-permute-start.9
  27.6 0.0 collective-permute-done.2.refs_1_
  27.6 0.1 collective-permute-done.3.refs_2_
  27.7 0.0 collective-permute-done.4.refs_3_
  27.7 1.2 %shard_map.51 = (f32[48,128]{1,0:T(8,128)S(1)}, bf16[48,128]{1,0:T(8,128)(2,1)S(1)}, bf16[48,128]{1,0:T(8,128)(2,1)S(1)}) custom-call(s32[4]{0:T(128)S(1)} %copy-done.1, s32[224,128]{1,0:T(8,128)S(1)} %get-tuple-element.45.refs_0_, s32[224,128]{1,0:T(8,128)S(1)} %collective-permute-done.2.refs_1_, s32[224,128]{1,0:T(8,128)S(1)} %collective-permute-done.3.refs_2_, ...), custom_call_target="tpu_custom_call" | custom-call | flops 67108864 | bytes 2097152 | tf_op jit(solution)/shard_map/pallas_call | solution.py:1001
  28.9 0.9 %collective-permute-start.10 = (bf16[48,128]{1,0:T(8,128)(2,1)S(1)}, bf16[48,128]{1,0:T(8,128)(2,1)S(1)}, u32[]{:S(2)}, u32[]{:S(2)}) collective-permute-start(bf16[48,128]{1,0:T(8,128)(2,1)S(1)} %get-tuple-element.67), channel_id=1, source_target_pairs={{0,1},{1,0},{2,3},{3,2},{4,5},{5,4},{6,7},{7,6},{8,9},{9,8},{10,11... | collective-permute-start | bytes 36872 | tf_op jit(solution)/shard_map/ppermute | solution.py:863
  29.9 3.8 %collective-permute-start.11 = (bf16[48,128]{1,0:T(8,128)(2,1)S(1)}, bf16[48,128]{1,0:T(8,128)(2,1)S(1)}, u32[]{:S(2)}, u32[]{:S(2)}) collective-permute-start(bf16[48,128]{1,0:T(8,128)(2,1)S(1)} %get-tuple-element.68), channel_id=1, source_target_pairs={{0,4},{1,5},{4,8},{5,9},{6,2},{7,3},{8,12},{9,13},{10,6},{11,7},{1... | collective-permute-start | bytes 36872 | tf_op jit(solution)/shard_map/ppermute | solution.py:974
  33.7 0.0 collective-permute-done.8.refs_1_
  33.7 0.0 collective-permute-done.9.refs_2_
  33.7 0.0 collective-permute-done.10.refs_3_
  33.7 0.8 %collective-permute-done.11.refs_4_ = bf16[48,128]{1,0:T(8,128)(2,1)S(1)} collective-permute-done((bf16[48,128]{1,0:T(8,128)(2,1)S(1)}, bf16[48,128]{1,0:T(8,128)(2,1)S(1)}, u32[]{:S(2)}, u32[]{:S(2)}) %collective-permute-start.11) | collective-permute-done | bytes 12320 | tf_op jit(solution)/shard_map/ppermute | solution.py:974
  34.5 0.7 %shard_map.52 = f32[50,96]{1,0:T(8,128)} custom-call(f32[48,128]{1,0:T(8,128)S(1)} %get-tuple-element.64.refs_0_, bf16[48,128]{1,0:T(8,128)(2,1)S(1)} %collective-permute-done.8.refs_1_, bf16[48,128]{1,0:T(8,128)(2,1)S(1)} %collective-permute-done.9.refs_2_, bf16[48,128]{1,0:T(8,128)(2,1)S(1)} %collective-permute-done.10.refs_3_, ...), custom_call_target="tpu_custom_call" | custom-call | tf_op jit(solution)/shard_map/pallas_call | solution.py:1010
  (2 shorter events, 0.0 us)
Async XLA Ops:
  0.0 6.8 %copy-start.2 = (s32[2048]{0:T(1024)S(1)}, s32[2048]{0:T(1024)}, u32[]{:S(2)}) copy-start(s32[2048]{0:T(1024)} %param.5) | copy-start | bytes 24580
  2.1 9.5 %copy-start = (s32[50,384]{1,0:T(8,128)S(1)}, s32[50,384]{1,0:T(8,128)}, u32[]{:S(2)}) copy-start(s32[50,384]{1,0:T(8,128)} %annot_ref.3) | copy-start | bytes 230404
  2.2 9.4 %copy-start.1 = (s32[4]{0:T(128)S(1)}, s32[4]{0:T(128)}, u32[]{:S(2)}) copy-start(s32[4]{0:T(128)} %reach_ref.5) | copy-start | bytes 52
  2.2 9.4 %collective-permute-start.1 = (bf16[1056,384]{1,0:T(8,128)(2,1)S(1)}, bf16[1056,384]{1,0:T(8,128)(2,1)S(1)}, u32[]{:S(2)}, u32[]{:S(2)}) collective-permute-start(bf16[1056,384]{1,0:T(8,128)(2,1)S(1)} %get-tuple-element.40), channel_id=1, source_target_pairs={{0,4},{4,0},{8,12},{12,8},{1,5},{5,1},{9,13},{13,9},{2,6},{6,2},{1... | collective-permute-start | bytes 2433032 | tf_op jit(solution)/shard_map/ppermute | solution.py:872
  2.3 14.4 %collective-permute-start = (bf16[1056,384]{1,0:T(8,128)(2,1)S(1)}, bf16[1056,384]{1,0:T(8,128)(2,1)S(1)}, u32[]{:S(2)}, u32[]{:S(2)}) collective-permute-start(bf16[1056,384]{1,0:T(8,128)(2,1)S(1)} %get-tuple-element.39), channel_id=1, source_target_pairs={{4,8},{8,4},{5,9},{9,5},{6,10},{10,6},{7,11},{11,7},{20,24},{24,20... | collective-permute-start | bytes 2433032 | tf_op jit(solution)/shard_map/ppermute | solution.py:872
  7.9 14.2 %collective-permute-start.5 = (s32[152,128]{1,0:T(8,128)S(1)}, s32[152,128]{1,0:T(8,128)S(1)}, u32[]{:S(2)}, u32[]{:S(2)}) collective-permute-start(s32[152,128]{1,0:T(8,128)S(1)} %get-tuple-element.50), channel_id=1, source_target_pairs={{0,2},{1,3},{2,0},{3,1},{4,6},{5,7},{6,4},{7,5},{8,10},{9,11},{10,... | collective-permute-start | bytes 233480 | tf_op jit(solution)/shard_map/ppermute | solution.py:863
  10.3 12.2 %collective-permute-start.6 = (s32[152,128]{1,0:T(8,128)S(1)}, s32[152,128]{1,0:T(8,128)S(1)}, u32[]{:S(2)}, u32[]{:S(2)}) collective-permute-start(s32[152,128]{1,0:T(8,128)S(1)} %get-tuple-element.51), channel_id=1, source_target_pairs={{0,3},{1,2},{2,1},{3,0},{4,7},{5,6},{6,5},{7,4},{8,11},{9,10},{10,... | collective-permute-start | bytes 233480 | tf_op jit(solution)/shard_map/ppermute | solution.py:863
  11.4 11.2 %collective-permute-start.7 = (s32[152,128]{1,0:T(8,128)S(1)}, s32[152,128]{1,0:T(8,128)S(1)}, u32[]{:S(2)}, u32[]{:S(2)}) collective-permute-start(s32[152,128]{1,0:T(8,128)S(1)} %get-tuple-element.52), channel_id=1, source_target_pairs={{0,1},{1,0},{2,3},{3,2},{4,5},{5,4},{6,7},{7,6},{8,9},{9,8},{10,11... | collective-permute-start | bytes 233480 | tf_op jit(solution)/shard_map/ppermute | solution.py:863
  17.8 9.8 %collective-permute-start.2 = (s32[224,128]{1,0:T(8,128)S(1)}, s32[224,128]{1,0:T(8,128)S(1)}, u32[]{:S(2)}, u32[]{:S(2)}) collective-permute-start(s32[224,128]{1,0:T(8,128)S(1)} %get-tuple-element.46), channel_id=1, source_target_pairs={{0,3},{1,2},{2,1},{3,0},{4,7},{5,6},{6,5},{7,4},{8,11},{9,10},{10,... | collective-permute-start | bytes 344072 | tf_op jit(solution)/shard_map/ppermute | solution.py:863
  22.1 5.7 %collective-permute-start.3 = (s32[224,128]{1,0:T(8,128)S(1)}, s32[224,128]{1,0:T(8,128)S(1)}, u32[]{:S(2)}, u32[]{:S(2)}) collective-permute-start(s32[224,128]{1,0:T(8,128)S(1)} %get-tuple-element.47), channel_id=1, source_target_pairs={{0,2},{1,3},{2,0},{3,1},{4,6},{5,7},{6,4},{7,5},{8,10},{9,11},{10,... | collective-permute-start | bytes 344072 | tf_op jit(solution)/shard_map/ppermute | solution.py:863
  22.1 5.6 %collective-permute-start.4 = (s32[224,128]{1,0:T(8,128)S(1)}, s32[224,128]{1,0:T(8,128)S(1)}, u32[]{:S(2)}, u32[]{:S(2)}) collective-permute-start(s32[224,128]{1,0:T(8,128)S(1)} %get-tuple-element.48), channel_id=1, source_target_pairs={{0,1},{1,0},{2,3},{3,2},{4,5},{5,4},{6,7},{7,6},{8,9},{9,8},{10,11... | collective-permute-start | bytes 344072 | tf_op jit(solution)/shard_map/ppermute | solution.py:863
  24.3 9.4 %collective-permute-start.8 = (bf16[48,128]{1,0:T(8,128)(2,1)S(1)}, bf16[48,128]{1,0:T(8,128)(2,1)S(1)}, u32[]{:S(2)}, u32[]{:S(2)}) collective-permute-start(bf16[48,128]{1,0:T(8,128)(2,1)S(1)} %get-tuple-element.65), channel_id=1, source_target_pairs={{0,3},{1,2},{2,1},{3,0},{4,7},{5,6},{6,5},{7,4},{8,11},{9,10},{10,... | collective-permute-start | bytes 36872 | tf_op jit(solution)/shard_map/ppermute | solution.py:863
  27.6 6.1 %collective-permute-start.9 = (bf16[48,128]{1,0:T(8,128)(2,1)S(1)}, bf16[48,128]{1,0:T(8,128)(2,1)S(1)}, u32[]{:S(2)}, u32[]{:S(2)}) collective-permute-start(bf16[48,128]{1,0:T(8,128)(2,1)S(1)} %get-tuple-element.66), channel_id=1, source_target_pairs={{0,2},{1,3},{2,0},{3,1},{4,6},{5,7},{6,4},{7,5},{8,10},{9,11},{10,... | collective-permute-start | bytes 36872 | tf_op jit(solution)/shard_map/ppermute | solution.py:863
  28.9 4.8 %collective-permute-start.10 = (bf16[48,128]{1,0:T(8,128)(2,1)S(1)}, bf16[48,128]{1,0:T(8,128)(2,1)S(1)}, u32[]{:S(2)}, u32[]{:S(2)}) collective-permute-start(bf16[48,128]{1,0:T(8,128)(2,1)S(1)} %get-tuple-element.67), channel_id=1, source_target_pairs={{0,1},{1,0},{2,3},{3,2},{4,5},{5,4},{6,7},{7,6},{8,9},{9,8},{10,11... | collective-permute-start | bytes 36872 | tf_op jit(solution)/shard_map/ppermute | solution.py:863
  29.9 4.7 %collective-permute-start.11 = (bf16[48,128]{1,0:T(8,128)(2,1)S(1)}, bf16[48,128]{1,0:T(8,128)(2,1)S(1)}, u32[]{:S(2)}, u32[]{:S(2)}) collective-permute-start(bf16[48,128]{1,0:T(8,128)(2,1)S(1)} %get-tuple-element.68), channel_id=1, source_target_pairs={{0,4},{1,5},{4,8},{5,9},{6,2},{7,3},{8,12},{9,13},{10,6},{11,7},{1... | collective-permute-start | bytes 36872 | tf_op jit(solution)/shard_map/ppermute | solution.py:974

commit v25 on v23

--- a/solution.py
+++ b/solution.py
@@ -13,7 +13,7 @@
 FIELD_BITS = 16
 LANES = 128
 HALF_LANES = LANES // 2
-CHUNKS = 4
+CHUNKS = (8, 5, 3)
 VMEM = pl.BlockSpec(memory_space=pltpu.VMEM)
 SMEM = pl.BlockSpec(memory_space=pltpu.SMEM)
 HBM = pl.BlockSpec(memory_space=pltpu.HBM)
@@ -84,15 +84,18 @@
 def prepare_kernel(hap_ref, annot_ref, alleles_ref, far_ref, close_ref, held, held_annots, sems):
     rows = hap_ref.shape[0]
     annot_rows = annot_ref.shape[0]
-    size = rows // (2 * CHUNKS)
-    starts = [side * (rows // 2) + chunk * size for chunk in range(CHUNKS) for side in range(2)]
+    sizes = [chunk * (rows // 32) for chunk in CHUNKS]
+    places = [sum(sizes[:number]) for number in range(len(sizes))]
+    pieces = [
+        (side * (rows // 2) + place, size) for place, size in zip(places, sizes) for side in range(2)
+    ]
     copies = [
         pltpu.make_async_copy(
             hap_ref.at[pl.ds(start, size)], held.at[pl.ds(start, size)], sems.at[number]
         )
-        for number, start in enumerate(starts)
+        for number, (start, size) in enumerate(pieces)
     ]
-    copies.append(pltpu.make_async_copy(annot_ref, held_annots, sems.at[2 * CHUNKS]))
+    copies.append(pltpu.make_async_copy(annot_ref, held_annots, sems.at[len(pieces)]))
     for copy in copies:
         copy.start()
     part = far_ref.shape[0] - rows // 2
@@ -107,16 +110,15 @@
         def _():
             store_packed(far_ref, close_ref, where, first, second)
 
-    for chunk in range(CHUNKS):
+    for chunk, (place, size) in enumerate(zip(places, sizes)):
         pair = []
-        for side in range(2):
-            number = 2 * chunk + side
+        for number in (2 * chunk, 2 * chunk + 1):
             copies[number].wait()
-            where = slice(starts[number], starts[number] + size)
+            where = slice(pieces[number][0], pieces[number][0] + size)
             values = held[where, :].astype(jnp.float32)
             alleles_ref[where, :] = values.astype(jnp.bfloat16)
             pair.append(values)
-        store(slice(chunk * size, (chunk + 1) * size), *pair)
+        store(slice(place, place + size), *pair)
     copies[-1].wait()
     annots = jnp.concatenate(
         [
@@ -895,7 +897,7 @@
         [
             pltpu.VMEM((rows, snps), i32),
             pltpu.VMEM(annotations.shape, i32),
-            pltpu.SemaphoreType.DMA((2 * CHUNKS + 1,)),
+            pltpu.SemaphoreType.DMA((2 * len(CHUNKS) + 1,)),
         ],
         moved=rows * snps * 8,
     )(haplotypes, annots_in)

time: 35.2 us -> 35.1 us (level)
  no operation moved by 1% of the time
where the time goes in v25:
time: 35.1 us; the launch traced here: 34.8 us
  starting transfers between devices  20 us (57%)
  Pallas kernels  9.87 us (28%)
  waiting for transfers between devices  4.84 us (14%)
    ppermute x9, starting transfers between devices, around(): lax.ppermute(value, 'hap', [(source, partner(source, step, groups)) for s...  11.6 us
    ppermute x2, starting transfers between devices, swapped(): return lax.ppermute(value, 'snp', pairs)  4.58 us
    ppermute x1, starting transfers between devices, to_neighbour(): return lax.ppermute(value, ('snp', 'hap'), pairs)  3.83 us
    ppermute x2, waiting for transfers between devices, swapped(): return lax.ppermute(value, 'snp', pairs)  3.58 us
    pallas_call x1, Pallas kernels, per_device(): call(prepare_kernel, [shape((rows, snps), bf16), packed, packed], [HBM, H...  2.13 us
    pallas_call x1, Pallas kernels, per_device(): call(functools.partial(own_score_kernel, groups, share), [by_snp, shape((...  1.8 us
    pallas_call x1, Pallas kernels, per_device(): call(functools.partial(close_kernel, groups), [shape(*args) for args in s...  1.79 us
    pallas_call x1, Pallas kernels, per_device(): call(functools.partial(near_score_kernel, groups, share), [packed_share,...  1.15 us
  transfers between devices with their start and end apart: 12, of which 3 were waited for; matrix products, arithmetic and copies ran while one was open for 0% of the time, Pallas kernels for 20%

profile of v25, /device:TPU:1, one launch (start us, length us, event | category | flops | bytes accessed | tf_op | source)
XLA Modules:
  0.0 34.8 jit_solution(9692456125929685304)
XLA Ops:
  0.0 0.0 copy-start.2
  0.0 2.1 %shard_map.46 = (bf16[2048,384]{1,0:T(8,128)(2,1)S(1)}, bf16[1056,384]{1,0:T(8,128)(2,1)S(1)}, bf16[1056,384]{1,0:T(8,128)(2,1)S(1)}) custom-call(s32[2048,384]{1,0:T(8,128)} %hap_ref.1, s32[50,384]{1,0:T(8,128)} %annot_ref.3), custom_call_target="tpu_custom_call" | custom-call | bytes 6291456 | tf_op jit(solution)/shard_map/pallas_call | solution.py:893
  2.1 0.0 copy-start
  2.1 0.0 copy-start.1
  2.2 0.1 collective-permute-start.1
  2.3 4.5 %collective-permute-start = (bf16[1056,384]{1,0:T(8,128)(2,1)S(1)}, bf16[1056,384]{1,0:T(8,128)(2,1)S(1)}, u32[]{:S(2)}, u32[]{:S(2)}) collective-permute-start(bf16[1056,384]{1,0:T(8,128)(2,1)S(1)} %get-tuple-element.39), channel_id=1, source_target_pairs={{4,8},{8,4},{5,9},{9,5},{6,10},{10,6},{7,11},{11,7},{20,24},{24,20... | collective-permute-start | bytes 2433032 | tf_op jit(solution)/shard_map/ppermute | solution.py:874
  6.8 0.0 copy-done.2
  6.8 1.1 %shard_map.47 = (bf16[400,2048]{1,0:T(8,128)(2,1)S(1)}, f32[8,384]{1,0:T(8,128)S(1)}, s32[152,128]{1,0:T(8,128)S(1)}, s32[152,128]{1,0:T(8,128)S(1)}, s32[152,128]{1,0:T(8,128)S(1)}, /*index=5*/s32[152,128]{1,0:T(8,128)S(1)}) custom-call(bf16[2048,384]{1,0:T(8,128)(2,1)S(1)} %get-tuple-element.37.alleles_ref, s32[1,2048]{1,0:T(1,128)S(1)} %bitcast.1), custom_call_target="tpu_custom_call" | custom-call | flops 603979776 | bytes 3145728 | tf_op jit(solution)/shard_map/pallas_call | solution.py:914
  7.9 2.4 %collective-permute-start.5 = (s32[152,128]{1,0:T(8,128)S(1)}, s32[152,128]{1,0:T(8,128)S(1)}, u32[]{:S(2)}, u32[]{:S(2)}) collective-permute-start(s32[152,128]{1,0:T(8,128)S(1)} %get-tuple-element.50), channel_id=1, source_target_pairs={{0,2},{1,3},{2,0},{3,1},{4,6},{5,7},{6,4},{7,5},{8,10},{9,11},{10,... | collective-permute-start | bytes 233480 | tf_op jit(solution)/shard_map/ppermute | solution.py:865
  10.3 1.1 %collective-permute-start.6 = (s32[152,128]{1,0:T(8,128)S(1)}, s32[152,128]{1,0:T(8,128)S(1)}, u32[]{:S(2)}, u32[]{:S(2)}) collective-permute-start(s32[152,128]{1,0:T(8,128)S(1)} %get-tuple-element.51), channel_id=1, source_target_pairs={{0,3},{1,2},{2,1},{3,0},{4,7},{5,6},{6,5},{7,4},{8,11},{9,10},{10,... | collective-permute-start | bytes 233480 | tf_op jit(solution)/shard_map/ppermute | solution.py:865
  11.4 0.2 collective-permute-start.7
  11.6 0.0 collective-permute-done.1.side_ref
  11.6 0.0 copy-done
  11.6 0.0 copy-done.1
  11.6 1.8 %shard_map.48 = (s32[96,384]{1,0:T(8,128)S(1)}, s32[112,256]{1,0:T(8,128)S(1)}, f32[8,384]{1,0:T(8,128)S(1)}, f32[384,128]{1,0:T(8,128)S(1)}, f32[2,240,128]{2,1...) custom-call(s32[4]{0:T(128)S(1)} %copy-done.1, ...), custom_call_target="tpu_custom_call" | custom-call | flops 402653184 | bytes 3145728 | tf_op jit(solution)/shard_map/pallas_call | solution.py:931
  13.4 3.6 %collective-permute-done.side_ref = bf16[1056,384]{1,0:T(8,128)(2,1)S(1)} collective-permute-done((bf16[1056,384]{1,0:T(8,128)(2,1)S(1)}, bf16[1056,384]{1,0:T(8,128)(2,1)S(1)}, u32[]{:S(2)}, u32[]{:S(2)}) %collective-permute-start) | collective-permute-done | bytes 811040 | tf_op jit(solution)/shard_map/ppermute | solution.py:874
  17.0 1.1 %shard_map.49 = (s32[224,128]{1,0:T(8,128)S(1)}, s32[224,128]{1,0:T(8,128)S(1)}, s32[224,128]{1,0:T(8,128)S(1)}, s32[224,128]{1,0:T(8,128)S(1)}) custom-call(bf16[400,2048]{1,0:T(8,128)(2,1)S(1)} %get-tuple-element.38.weighted_ref, bf16[1056,384]{1,0:T(8,128)(2,1)S(1)} %collective-permute-done.side_ref, s32[96,384]{1,0:T(8,128)S(1)} %get-tuple-element.41.close_ref, ...), custom_call_target="tpu_custom_call" | custom-call | flops 402653184 | bytes 3145728 | tf_op jit(solution)/shard_map/pallas_call | solution.py:944
  18.1 3.0 %collective-permute-start.2 = (s32[224,128]{1,0:T(8,128)S(1)}, s32[224,128]{1,0:T(8,128)S(1)}, u32[]{:S(2)}, u32[]{:S(2)}) collective-permute-start(s32[224,128]{1,0:T(8,128)S(1)} %get-tuple-element.46), channel_id=1, source_target_pairs={{0,2},{1,3},{2,0},{3,1},{4,6},{5,7},{6,4},{7,5},{8,10},{9,11},{10,... | collective-permute-start | bytes 344072 | tf_op jit(solution)/shard_map/ppermute | solution.py:865
  21.1 1.1 %collective-permute-start.3 = (s32[224,128]{1,0:T(8,128)S(1)}, s32[224,128]{1,0:T(8,128)S(1)}, u32[]{:S(2)}, u32[]{:S(2)}) collective-permute-start(s32[224,128]{1,0:T(8,128)S(1)} %get-tuple-element.47), channel_id=1, source_target_pairs={{0,3},{1,2},{2,1},{3,0},{4,7},{5,6},{6,5},{7,4},{8,11},{9,10},{10,... | collective-permute-start | bytes 344072 | tf_op jit(solution)/shard_map/ppermute | solution.py:865
  22.2 0.0 collective-permute-done.5.refs_1_
  22.2 0.3 collective-permute-start.4
  22.4 0.0 collective-permute-done.6.refs_2_
  22.5 0.0 collective-permute-done.7.refs_3_
  22.5 1.8 %shard_map.50 = (f32[384,128]{1,0:T(8,128)S(1)}, f32[96,128]{1,0:T(8,128)S(1)}, f32[6,240,128]{2,1,0:T(8,128)S(1)}, bf16[128,128]{1,0:T(8,128)(2,1)S(1)}, f32[6,...) custom-call(s32[4]{0:T(128)S(1)} %copy-done.1, ...), custom_call_target="tpu_custom_call" | custom-call | flops 8589934592 | bytes 1048576 | tf_op jit(solution)/shard_map/pallas_call | solution.py:983
  24.3 2.4 %collective-permute-start.8 = (bf16[48,128]{1,0:T(8,128)(2,1)S(1)}, bf16[48,128]{1,0:T(8,128)(2,1)S(1)}, u32[]{:S(2)}, u32[]{:S(2)}) collective-permute-start(bf16[48,128]{1,0:T(8,128)(2,1)S(1)} %get-tuple-element.65), channel_id=1, source_target_pairs={{0,3},{1,2},{2,1},{3,0},{4,7},{5,6},{6,5},{7,4},{8,11},{9,10},{10,... | collective-permute-start | bytes 36872 | tf_op jit(solution)/shard_map/ppermute | solution.py:865
  26.7 0.1 collective-permute-start.9
  26.8 0.0 collective-permute-done.2.refs_1_
  26.8 0.0 collective-permute-done.3.refs_2_
  26.8 0.4 %collective-permute-done.4.refs_3_ = s32[224,128]{1,0:T(8,128)S(1)} collective-permute-done((s32[224,128]{1,0:T(8,128)S(1)}, s32[224,128]{1,0:T(8,128)S(1)}, u32[]{:S(2)}, u32[]{:S(2)}) %collective-permute-start.4) | collective-permute-done | bytes 114720 | tf_op jit(solution)/shard_map/ppermute | solution.py:865
  27.2 1.2 %shard_map.51 = (f32[48,128]{1,0:T(8,128)S(1)}, bf16[48,128]{1,0:T(8,128)(2,1)S(1)}, bf16[48,128]{1,0:T(8,128)(2,1)S(1)}) custom-call(s32[4]{0:T(128)S(1)} %copy-done.1, s32[224,128]{1,0:T(8,128)S(1)} %get-tuple-element.45.refs_0_, s32[224,128]{1,0:T(8,128)S(1)} %collective-permute-done.2.refs_1_, s32[224,128]{1,0:T(8,128)S(1)} %collective-permute-done.3.refs_2_, ...), custom_call_target="tpu_custom_call" | custom-call | flops 67108864 | bytes 2097152 | tf_op jit(solution)/shard_map/pallas_call | solution.py:1002
  28.4 1.0 %collective-permute-start.10 = (bf16[48,128]{1,0:T(8,128)(2,1)S(1)}, bf16[48,128]{1,0:T(8,128)(2,1)S(1)}, u32[]{:S(2)}, u32[]{:S(2)}) collective-permute-start(bf16[48,128]{1,0:T(8,128)(2,1)S(1)} %get-tuple-element.67), channel_id=1, source_target_pairs={{0,1},{1,0},{2,3},{3,2},{4,5},{5,4},{6,7},{7,6},{8,9},{9,8},{10,11... | collective-permute-start | bytes 36872 | tf_op jit(solution)/shard_map/ppermute | solution.py:865
  29.4 3.8 %collective-permute-start.11 = (bf16[48,128]{1,0:T(8,128)(2,1)S(1)}, bf16[48,128]{1,0:T(8,128)(2,1)S(1)}, u32[]{:S(2)}, u32[]{:S(2)}) collective-permute-start(bf16[48,128]{1,0:T(8,128)(2,1)S(1)} %get-tuple-element.68), channel_id=1, source_target_pairs={{0,4},{1,5},{4,8},{5,9},{6,2},{7,3},{8,12},{9,13},{10,6},{11,7},{1... | collective-permute-start | bytes 36872 | tf_op jit(solution)/shard_map/ppermute | solution.py:975
  33.3 0.0 collective-permute-done.8.refs_1_
  33.3 0.0 collective-permute-done.9.refs_2_
  33.3 0.0 collective-permute-done.10.refs_3_
  33.3 0.8 %collective-permute-done.11.refs_4_ = bf16[48,128]{1,0:T(8,128)(2,1)S(1)} collective-permute-done((bf16[48,128]{1,0:T(8,128)(2,1)S(1)}, bf16[48,128]{1,0:T(8,128)(2,1)S(1)}, u32[]{:S(2)}, u32[]{:S(2)}) %collective-permute-start.11) | collective-permute-done | bytes 12320 | tf_op jit(solution)/shard_map/ppermute | solution.py:975
  34.1 0.7 %shard_map.52 = f32[50,96]{1,0:T(8,128)} custom-call(f32[48,128]{1,0:T(8,128)S(1)} %get-tuple-element.64.refs_0_, bf16[48,128]{1,0:T(8,128)(2,1)S(1)} %collective-permute-done.8.refs_1_, bf16[48,128]{1,0:T(8,128)(2,1)S(1)} %collective-permute-done.9.refs_2_, bf16[48,128]{1,0:T(8,128)(2,1)S(1)} %collective-permute-done.10.refs_3_, ...), custom_call_target="tpu_custom_call" | custom-call | tf_op jit(solution)/shard_map/pallas_call | solution.py:1011
  (2 shorter events, 0.0 us)
Async XLA Ops:
  0.0 6.8 %copy-start.2 = (s32[2048]{0:T(1024)S(1)}, s32[2048]{0:T(1024)}, u32[]{:S(2)}) copy-start(s32[2048]{0:T(1024)} %param.5) | copy-start | bytes 24580
  2.1 9.4 %copy-start = (s32[50,384]{1,0:T(8,128)S(1)}, s32[50,384]{1,0:T(8,128)}, u32[]{:S(2)}) copy-start(s32[50,384]{1,0:T(8,128)} %annot_ref.3) | copy-start | bytes 230404
  2.1 9.4 %copy-start.1 = (s32[4]{0:T(128)S(1)}, s32[4]{0:T(128)}, u32[]{:S(2)}) copy-start(s32[4]{0:T(128)} %reach_ref.5) | copy-start | bytes 52
  2.2 9.4 %collective-permute-start.1 = (bf16[1056,384]{1,0:T(8,128)(2,1)S(1)}, bf16[1056,384]{1,0:T(8,128)(2,1)S(1)}, u32[]{:S(2)}, u32[]{:S(2)}) collective-permute-start(bf16[1056,384]{1,0:T(8,128)(2,1)S(1)} %get-tuple-element.40), channel_id=1, source_target_pairs={{0,4},{4,0},{8,12},{12,8},{1,5},{5,1},{9,13},{13,9},{2,6},{6,2},{1... | collective-permute-start | bytes 2433032 | tf_op jit(solution)/shard_map/ppermute | solution.py:874
  2.3 14.7 %collective-permute-start = (bf16[1056,384]{1,0:T(8,128)(2,1)S(1)}, bf16[1056,384]{1,0:T(8,128)(2,1)S(1)}, u32[]{:S(2)}, u32[]{:S(2)}) collective-permute-start(bf16[1056,384]{1,0:T(8,128)(2,1)S(1)} %get-tuple-element.39), channel_id=1, source_target_pairs={{4,8},{8,4},{5,9},{9,5},{6,10},{10,6},{7,11},{11,7},{20,24},{24,20... | collective-permute-start | bytes 2433032 | tf_op jit(solution)/shard_map/ppermute | solution.py:874
  7.9 14.3 %collective-permute-start.5 = (s32[152,128]{1,0:T(8,128)S(1)}, s32[152,128]{1,0:T(8,128)S(1)}, u32[]{:S(2)}, u32[]{:S(2)}) collective-permute-start(s32[152,128]{1,0:T(8,128)S(1)} %get-tuple-element.50), channel_id=1, source_target_pairs={{0,2},{1,3},{2,0},{3,1},{4,6},{5,7},{6,4},{7,5},{8,10},{9,11},{10,... | collective-permute-start | bytes 233480 | tf_op jit(solution)/shard_map/ppermute | solution.py:865
  10.3 12.2 %collective-permute-start.6 = (s32[152,128]{1,0:T(8,128)S(1)}, s32[152,128]{1,0:T(8,128)S(1)}, u32[]{:S(2)}, u32[]{:S(2)}) collective-permute-start(s32[152,128]{1,0:T(8,128)S(1)} %get-tuple-element.51), channel_id=1, source_target_pairs={{0,3},{1,2},{2,1},{3,0},{4,7},{5,6},{6,5},{7,4},{8,11},{9,10},{10,... | collective-permute-start | bytes 233480 | tf_op jit(solution)/shard_map/ppermute | solution.py:865
  11.4 11.1 %collective-permute-start.7 = (s32[152,128]{1,0:T(8,128)S(1)}, s32[152,128]{1,0:T(8,128)S(1)}, u32[]{:S(2)}, u32[]{:S(2)}) collective-permute-start(s32[152,128]{1,0:T(8,128)S(1)} %get-tuple-element.52), channel_id=1, source_target_pairs={{0,1},{1,0},{2,3},{3,2},{4,5},{5,4},{6,7},{7,6},{8,9},{9,8},{10,11... | collective-permute-start | bytes 233480 | tf_op jit(solution)/shard_map/ppermute | solution.py:865
  18.1 8.7 %collective-permute-start.2 = (s32[224,128]{1,0:T(8,128)S(1)}, s32[224,128]{1,0:T(8,128)S(1)}, u32[]{:S(2)}, u32[]{:S(2)}) collective-permute-start(s32[224,128]{1,0:T(8,128)S(1)} %get-tuple-element.46), channel_id=1, source_target_pairs={{0,2},{1,3},{2,0},{3,1},{4,6},{5,7},{6,4},{7,5},{8,10},{9,11},{10,... | collective-permute-start | bytes 344072 | tf_op jit(solution)/shard_map/ppermute | solution.py:865
  21.1 5.7 %collective-permute-start.3 = (s32[224,128]{1,0:T(8,128)S(1)}, s32[224,128]{1,0:T(8,128)S(1)}, u32[]{:S(2)}, u32[]{:S(2)}) collective-permute-start(s32[224,128]{1,0:T(8,128)S(1)} %get-tuple-element.47), channel_id=1, source_target_pairs={{0,3},{1,2},{2,1},{3,0},{4,7},{5,6},{6,5},{7,4},{8,11},{9,10},{10,... | collective-permute-start | bytes 344072 | tf_op jit(solution)/shard_map/ppermute | solution.py:865
  22.2 5.1 %collective-permute-start.4 = (s32[224,128]{1,0:T(8,128)S(1)}, s32[224,128]{1,0:T(8,128)S(1)}, u32[]{:S(2)}, u32[]{:S(2)}) collective-permute-start(s32[224,128]{1,0:T(8,128)S(1)} %get-tuple-element.48), channel_id=1, source_target_pairs={{0,1},{1,0},{2,3},{3,2},{4,5},{5,4},{6,7},{7,6},{8,9},{9,8},{10,11... | collective-permute-start | bytes 344072 | tf_op jit(solution)/shard_map/ppermute | solution.py:865
  24.3 9.0 %collective-permute-start.8 = (bf16[48,128]{1,0:T(8,128)(2,1)S(1)}, bf16[48,128]{1,0:T(8,128)(2,1)S(1)}, u32[]{:S(2)}, u32[]{:S(2)}) collective-permute-start(bf16[48,128]{1,0:T(8,128)(2,1)S(1)} %get-tuple-element.65), channel_id=1, source_target_pairs={{0,3},{1,2},{2,1},{3,0},{4,7},{5,6},{6,5},{7,4},{8,11},{9,10},{10,... | collective-permute-start | bytes 36872 | tf_op jit(solution)/shard_map/ppermute | solution.py:865
  26.7 6.6 %collective-permute-start.9 = (bf16[48,128]{1,0:T(8,128)(2,1)S(1)}, bf16[48,128]{1,0:T(8,128)(2,1)S(1)}, u32[]{:S(2)}, u32[]{:S(2)}) collective-permute-start(bf16[48,128]{1,0:T(8,128)(2,1)S(1)} %get-tuple-element.66), channel_id=1, source_target_pairs={{0,2},{1,3},{2,0},{3,1},{4,6},{5,7},{6,4},{7,5},{8,10},{9,11},{10,... | collective-permute-start | bytes 36872 | tf_op jit(solution)/shard_map/ppermute | solution.py:865
  28.4 4.9 %collective-permute-start.10 = (bf16[48,128]{1,0:T(8,128)(2,1)S(1)}, bf16[48,128]{1,0:T(8,128)(2,1)S(1)}, u32[]{:S(2)}, u32[]{:S(2)}) collective-permute-start(bf16[48,128]{1,0:T(8,128)(2,1)S(1)} %get-tuple-element.67), channel_id=1, source_target_pairs={{0,1},{1,0},{2,3},{3,2},{4,5},{5,4},{6,7},{7,6},{8,9},{9,8},{10,11... | collective-permute-start | bytes 36872 | tf_op jit(solution)/shard_map/ppermute | solution.py:865
  29.4 4.6 %collective-permute-start.11 = (bf16[48,128]{1,0:T(8,128)(2,1)S(1)}, bf16[48,128]{1,0:T(8,128)(2,1)S(1)}, u32[]{:S(2)}, u32[]{:S(2)}) collective-permute-start(bf16[48,128]{1,0:T(8,128)(2,1)S(1)} %get-tuple-element.68), channel_id=1, source_target_pairs={{0,4},{1,5},{4,8},{5,9},{6,2},{7,3},{8,12},{9,13},{10,6},{11,7},{1... | collective-permute-start | bytes 36872 | tf_op jit(solution)/shard_map/ppermute | solution.py:975

commit v26 on v25

--- a/solution.py
+++ b/solution.py
@@ -920,7 +920,7 @@
         moved=rows * snps * 4,
     )(alleles, labels.reshape(1, rows))
     order = (2, 3, 1) if by_column else range(groups - 1, 0, -1)
-    own_parts = [own_parts[0]] + [around(own_parts[k], groups, k) for k in order]
+    own_parts = [own_parts[0]] + [around(own_parts[k], groups, k) for k in range(groups - 1, 0, -1)]
 
     near_shapes = [own_share_counts] + [near_share_counts if by_column else shape((share + 8, snps), i32)] * groups
     if by_column:

time: 35.1 us -> 35.1 us (level)
    ppermute x2, waiting for transfers between devices: 3.58 us -> 3.21 us  [swapped(): return lax.ppermute(value, 'snp', pairs)]
where the time goes in v26:
time: 35.1 us; the launch traced here: 34.8 us
  starting transfers between devices  20.2 us (58%)
  Pallas kernels  9.87 us (28%)
  waiting for transfers between devices  4.6 us (13%)
    ppermute x9, starting transfers between devices, around(): lax.ppermute(value, 'hap', [(source, partner(source, step, groups)) for s...  11.7 us
    ppermute x2, starting transfers between devices, swapped(): return lax.ppermute(value, 'snp', pairs)  4.58 us
    ppermute x1, starting transfers between devices, to_neighbour(): return lax.ppermute(value, ('snp', 'hap'), pairs)  3.94 us
    ppermute x2, waiting for transfers between devices, swapped(): return lax.ppermute(value, 'snp', pairs)  3.21 us
    pallas_call x1, Pallas kernels, per_device(): call(prepare_kernel, [shape((rows, snps), bf16), packed, packed], [HBM, H...  2.13 us
    pallas_call x1, Pallas kernels, per_device(): call(functools.partial(own_score_kernel, groups, share), [by_snp, shape((...  1.8 us
    pallas_call x1, Pallas kernels, per_device(): call(functools.partial(close_kernel, groups), [shape(*args) for args in s...  1.79 us
    pallas_call x1, Pallas kernels, per_device(): call(functools.partial(near_score_kernel, groups, share), [packed_share,...  1.15 us
  transfers between devices with their start and end apart: 12, of which 3 were waited for; matrix products, arithmetic and copies ran while one was open for 0% of the time, Pallas kernels for 20%

profile of v26, /device:TPU:1, one launch (start us, length us, event | category | flops | bytes accessed | tf_op | source)
XLA Modules:
  0.0 34.8 jit_solution(14876560230522451430)
XLA Ops:
  0.0 0.0 copy-start.2
  0.0 2.1 %shard_map.46 = (bf16[2048,384]{1,0:T(8,128)(2,1)S(1)}, bf16[1056,384]{1,0:T(8,128)(2,1)S(1)}, bf16[1056,384]{1,0:T(8,128)(2,1)S(1)}) custom-call(s32[2048,384]{1,0:T(8,128)} %hap_ref.1, s32[50,384]{1,0:T(8,128)} %annot_ref.3), custom_call_target="tpu_custom_call" | custom-call | bytes 6291456 | tf_op jit(solution)/shard_map/pallas_call | solution.py:893
  2.1 0.0 copy-start
  2.1 0.0 copy-start.1
  2.2 0.1 collective-permute-start.1
  2.3 4.5 %collective-permute-start = (bf16[1056,384]{1,0:T(8,128)(2,1)S(1)}, bf16[1056,384]{1,0:T(8,128)(2,1)S(1)}, u32[]{:S(2)}, u32[]{:S(2)}) collective-permute-start(bf16[1056,384]{1,0:T(8,128)(2,1)S(1)} %get-tuple-element.39), channel_id=1, source_target_pairs={{4,8},{8,4},{5,9},{9,5},{6,10},{10,6},{7,11},{11,7},{20,24},{24,20... | collective-permute-start | bytes 2433032 | tf_op jit(solution)/shard_map/ppermute | solution.py:874
  6.8 0.0 copy-done.2
  6.8 1.1 %shard_map.47 = (bf16[400,2048]{1,0:T(8,128)(2,1)S(1)}, f32[8,384]{1,0:T(8,128)S(1)}, s32[152,128]{1,0:T(8,128)S(1)}, s32[152,128]{1,0:T(8,128)S(1)}, s32[152,128]{1,0:T(8,128)S(1)}, /*index=5*/s32[152,128]{1,0:T(8,128)S(1)}) custom-call(bf16[2048,384]{1,0:T(8,128)(2,1)S(1)} %get-tuple-element.37.alleles_ref, s32[1,2048]{1,0:T(1,128)S(1)} %bitcast.1), custom_call_target="tpu_custom_call" | custom-call | flops 603979776 | bytes 3145728 | tf_op jit(solution)/shard_map/pallas_call | solution.py:914
  7.9 3.4 %collective-permute-start.5 = (s32[152,128]{1,0:T(8,128)S(1)}, s32[152,128]{1,0:T(8,128)S(1)}, u32[]{:S(2)}, u32[]{:S(2)}) collective-permute-start(s32[152,128]{1,0:T(8,128)S(1)} %get-tuple-element.50), channel_id=1, source_target_pairs={{0,3},{1,2},{2,1},{3,0},{4,7},{5,6},{6,5},{7,4},{8,11},{9,10},{10,... | collective-permute-start | bytes 233480 | tf_op jit(solution)/shard_map/ppermute | solution.py:865
  11.3 0.0 collective-permute-start.6
  11.3 0.4 %collective-permute-start.7 = (s32[152,128]{1,0:T(8,128)S(1)}, s32[152,128]{1,0:T(8,128)S(1)}, u32[]{:S(2)}, u32[]{:S(2)}) collective-permute-start(s32[152,128]{1,0:T(8,128)S(1)} %get-tuple-element.52), channel_id=1, source_target_pairs={{0,1},{1,0},{2,3},{3,2},{4,5},{5,4},{6,7},{7,6},{8,9},{9,8},{10,11... | collective-permute-start | bytes 233480 | tf_op jit(solution)/shard_map/ppermute | solution.py:865
  11.7 0.0 collective-permute-done.1.side_ref
  11.7 0.0 copy-done
  11.7 0.0 copy-done.1
  11.7 1.8 %shard_map.48 = (s32[96,384]{1,0:T(8,128)S(1)}, s32[112,256]{1,0:T(8,128)S(1)}, f32[8,384]{1,0:T(8,128)S(1)}, f32[384,128]{1,0:T(8,128)S(1)}, f32[2,240,128]{2,1...) custom-call(s32[4]{0:T(128)S(1)} %copy-done.1, ...), custom_call_target="tpu_custom_call" | custom-call | flops 402653184 | bytes 3145728 | tf_op jit(solution)/shard_map/pallas_call | solution.py:931
  13.5 3.2 %collective-permute-done.side_ref = bf16[1056,384]{1,0:T(8,128)(2,1)S(1)} collective-permute-done((bf16[1056,384]{1,0:T(8,128)(2,1)S(1)}, bf16[1056,384]{1,0:T(8,128)(2,1)S(1)}, u32[]{:S(2)}, u32[]{:S(2)}) %collective-permute-start) | collective-permute-done | bytes 811040 | tf_op jit(solution)/shard_map/ppermute | solution.py:874
  16.7 1.1 %shard_map.49 = (s32[224,128]{1,0:T(8,128)S(1)}, s32[224,128]{1,0:T(8,128)S(1)}, s32[224,128]{1,0:T(8,128)S(1)}, s32[224,128]{1,0:T(8,128)S(1)}) custom-call(bf16[400,2048]{1,0:T(8,128)(2,1)S(1)} %get-tuple-element.38.weighted_ref, bf16[1056,384]{1,0:T(8,128)(2,1)S(1)} %collective-permute-done.side_ref, s32[96,384]{1,0:T(8,128)S(1)} %get-tuple-element.41.close_ref, ...), custom_call_target="tpu_custom_call" | custom-call | flops 402653184 | bytes 3145728 | tf_op jit(solution)/shard_map/pallas_call | solution.py:944
  17.8 3.3 %collective-permute-start.2 = (s32[224,128]{1,0:T(8,128)S(1)}, s32[224,128]{1,0:T(8,128)S(1)}, u32[]{:S(2)}, u32[]{:S(2)}) collective-permute-start(s32[224,128]{1,0:T(8,128)S(1)} %get-tuple-element.46), channel_id=1, source_target_pairs={{0,2},{1,3},{2,0},{3,1},{4,6},{5,7},{6,4},{7,5},{8,10},{9,11},{10,... | collective-permute-start | bytes 344072 | tf_op jit(solution)/shard_map/ppermute | solution.py:865
  21.1 1.1 %collective-permute-start.3 = (s32[224,128]{1,0:T(8,128)S(1)}, s32[224,128]{1,0:T(8,128)S(1)}, u32[]{:S(2)}, u32[]{:S(2)}) collective-permute-start(s32[224,128]{1,0:T(8,128)S(1)} %get-tuple-element.47), channel_id=1, source_target_pairs={{0,3},{1,2},{2,1},{3,0},{4,7},{5,6},{6,5},{7,4},{8,11},{9,10},{10,... | collective-permute-start | bytes 344072 | tf_op jit(solution)/shard_map/ppermute | solution.py:865
  22.2 0.0 collective-permute-done.5.refs_1_
  22.2 0.3 collective-permute-start.4
  22.4 0.0 collective-permute-done.6.refs_2_
  22.5 0.0 collective-permute-done.7.refs_3_
  22.5 1.8 %shard_map.50 = (f32[384,128]{1,0:T(8,128)S(1)}, f32[96,128]{1,0:T(8,128)S(1)}, f32[6,240,128]{2,1,0:T(8,128)S(1)}, bf16[128,128]{1,0:T(8,128)(2,1)S(1)}, f32[6,...) custom-call(s32[4]{0:T(128)S(1)} %copy-done.1, ...), custom_call_target="tpu_custom_call" | custom-call | flops 8589934592 | bytes 1048576 | tf_op jit(solution)/shard_map/pallas_call | solution.py:983
  24.3 2.4 %collective-permute-start.8 = (bf16[48,128]{1,0:T(8,128)(2,1)S(1)}, bf16[48,128]{1,0:T(8,128)(2,1)S(1)}, u32[]{:S(2)}, u32[]{:S(2)}) collective-permute-start(bf16[48,128]{1,0:T(8,128)(2,1)S(1)} %get-tuple-element.65), channel_id=1, source_target_pairs={{0,3},{1,2},{2,1},{3,0},{4,7},{5,6},{6,5},{7,4},{8,11},{9,10},{10,... | collective-permute-start | bytes 36872 | tf_op jit(solution)/shard_map/ppermute | solution.py:865
  26.7 0.1 collective-permute-start.9
  26.8 0.0 collective-permute-done.2.refs_1_
  26.8 0.0 collective-permute-done.3.refs_2_
  26.8 0.6 %collective-permute-done.4.refs_3_ = s32[224,128]{1,0:T(8,128)S(1)} collective-permute-done((s32[224,128]{1,0:T(8,128)S(1)}, s32[224,128]{1,0:T(8,128)S(1)}, u32[]{:S(2)}, u32[]{:S(2)}) %collective-permute-start.4) | collective-permute-done | bytes 114720 | tf_op jit(solution)/shard_map/ppermute | solution.py:865
  27.4 1.2 %shard_map.51 = (f32[48,128]{1,0:T(8,128)S(1)}, bf16[48,128]{1,0:T(8,128)(2,1)S(1)}, bf16[48,128]{1,0:T(8,128)(2,1)S(1)}) custom-call(s32[4]{0:T(128)S(1)} %copy-done.1, s32[224,128]{1,0:T(8,128)S(1)} %get-tuple-element.45.refs_0_, s32[224,128]{1,0:T(8,128)S(1)} %collective-permute-done.2.refs_1_, s32[224,128]{1,0:T(8,128)S(1)} %collective-permute-done.3.refs_2_, ...), custom_call_target="tpu_custom_call" | custom-call | flops 67108864 | bytes 2097152 | tf_op jit(solution)/shard_map/pallas_call | solution.py:1002
  28.5 0.8 %collective-permute-start.10 = (bf16[48,128]{1,0:T(8,128)(2,1)S(1)}, bf16[48,128]{1,0:T(8,128)(2,1)S(1)}, u32[]{:S(2)}, u32[]{:S(2)}) collective-permute-start(bf16[48,128]{1,0:T(8,128)(2,1)S(1)} %get-tuple-element.67), channel_id=1, source_target_pairs={{0,1},{1,0},{2,3},{3,2},{4,5},{5,4},{6,7},{7,6},{8,9},{9,8},{10,11... | collective-permute-start | bytes 36872 | tf_op jit(solution)/shard_map/ppermute | solution.py:865
  29.3 3.9 %collective-permute-start.11 = (bf16[48,128]{1,0:T(8,128)(2,1)S(1)}, bf16[48,128]{1,0:T(8,128)(2,1)S(1)}, u32[]{:S(2)}, u32[]{:S(2)}) collective-permute-start(bf16[48,128]{1,0:T(8,128)(2,1)S(1)} %get-tuple-element.68), channel_id=1, source_target_pairs={{0,4},{1,5},{4,8},{5,9},{6,2},{7,3},{8,12},{9,13},{10,6},{11,7},{1... | collective-permute-start | bytes 36872 | tf_op jit(solution)/shard_map/ppermute | solution.py:975
  33.3 0.0 collective-permute-done.8.refs_1_
  33.3 0.0 collective-permute-done.9.refs_2_
  33.3 0.0 collective-permute-done.10.refs_3_
  33.3 0.8 %collective-permute-done.11.refs_4_ = bf16[48,128]{1,0:T(8,128)(2,1)S(1)} collective-permute-done((bf16[48,128]{1,0:T(8,128)(2,1)S(1)}, bf16[48,128]{1,0:T(8,128)(2,1)S(1)}, u32[]{:S(2)}, u32[]{:S(2)}) %collective-permute-start.11) | collective-permute-done | bytes 12320 | tf_op jit(solution)/shard_map/ppermute | solution.py:975
  34.1 0.7 %shard_map.52 = f32[50,96]{1,0:T(8,128)} custom-call(f32[48,128]{1,0:T(8,128)S(1)} %get-tuple-element.64.refs_0_, bf16[48,128]{1,0:T(8,128)(2,1)S(1)} %collective-permute-done.8.refs_1_, bf16[48,128]{1,0:T(8,128)(2,1)S(1)} %collective-permute-done.9.refs_2_, bf16[48,128]{1,0:T(8,128)(2,1)S(1)} %collective-permute-done.10.refs_3_, ...), custom_call_target="tpu_custom_call" | custom-call | tf_op jit(solution)/shard_map/pallas_call | solution.py:1011
  (2 shorter events, 0.0 us)
Async XLA Ops:
  0.0 6.8 %copy-start.2 = (s32[2048]{0:T(1024)S(1)}, s32[2048]{0:T(1024)}, u32[]{:S(2)}) copy-start(s32[2048]{0:T(1024)} %param.5) | copy-start | bytes 24580
  2.1 9.5 %copy-start = (s32[50,384]{1,0:T(8,128)S(1)}, s32[50,384]{1,0:T(8,128)}, u32[]{:S(2)}) copy-start(s32[50,384]{1,0:T(8,128)} %annot_ref.3) | copy-start | bytes 230404
  2.1 9.5 %copy-start.1 = (s32[4]{0:T(128)S(1)}, s32[4]{0:T(128)}, u32[]{:S(2)}) copy-start(s32[4]{0:T(128)} %reach_ref.5) | copy-start | bytes 52
  2.2 9.5 %collective-permute-start.1 = (bf16[1056,384]{1,0:T(8,128)(2,1)S(1)}, bf16[1056,384]{1,0:T(8,128)(2,1)S(1)}, u32[]{:S(2)}, u32[]{:S(2)}) collective-permute-start(bf16[1056,384]{1,0:T(8,128)(2,1)S(1)} %get-tuple-element.40), channel_id=1, source_target_pairs={{0,4},{4,0},{8,12},{12,8},{1,5},{5,1},{9,13},{13,9},{2,6},{6,2},{1... | collective-permute-start | bytes 2433032 | tf_op jit(solution)/shard_map/ppermute | solution.py:874
  2.3 14.4 %collective-permute-start = (bf16[1056,384]{1,0:T(8,128)(2,1)S(1)}, bf16[1056,384]{1,0:T(8,128)(2,1)S(1)}, u32[]{:S(2)}, u32[]{:S(2)}) collective-permute-start(bf16[1056,384]{1,0:T(8,128)(2,1)S(1)} %get-tuple-element.39), channel_id=1, source_target_pairs={{4,8},{8,4},{5,9},{9,5},{6,10},{10,6},{7,11},{11,7},{20,24},{24,20... | collective-permute-start | bytes 2433032 | tf_op jit(solution)/shard_map/ppermute | solution.py:874
  7.9 14.3 %collective-permute-start.5 = (s32[152,128]{1,0:T(8,128)S(1)}, s32[152,128]{1,0:T(8,128)S(1)}, u32[]{:S(2)}, u32[]{:S(2)}) collective-permute-start(s32[152,128]{1,0:T(8,128)S(1)} %get-tuple-element.50), channel_id=1, source_target_pairs={{0,3},{1,2},{2,1},{3,0},{4,7},{5,6},{6,5},{7,4},{8,11},{9,10},{10,... | collective-permute-start | bytes 233480 | tf_op jit(solution)/shard_map/ppermute | solution.py:865
  11.3 11.2 %collective-permute-start.6 = (s32[152,128]{1,0:T(8,128)S(1)}, s32[152,128]{1,0:T(8,128)S(1)}, u32[]{:S(2)}, u32[]{:S(2)}) collective-permute-start(s32[152,128]{1,0:T(8,128)S(1)} %get-tuple-element.51), channel_id=1, source_target_pairs={{0,2},{1,3},{2,0},{3,1},{4,6},{5,7},{6,4},{7,5},{8,10},{9,11},{10,... | collective-permute-start | bytes 233480 | tf_op jit(solution)/shard_map/ppermute | solution.py:865
  11.3 11.2 %collective-permute-start.7 = (s32[152,128]{1,0:T(8,128)S(1)}, s32[152,128]{1,0:T(8,128)S(1)}, u32[]{:S(2)}, u32[]{:S(2)}) collective-permute-start(s32[152,128]{1,0:T(8,128)S(1)} %get-tuple-element.52), channel_id=1, source_target_pairs={{0,1},{1,0},{2,3},{3,2},{4,5},{5,4},{6,7},{7,6},{8,9},{9,8},{10,11... | collective-permute-start | bytes 233480 | tf_op jit(solution)/shard_map/ppermute | solution.py:865
  17.8 9.0 %collective-permute-start.2 = (s32[224,128]{1,0:T(8,128)S(1)}, s32[224,128]{1,0:T(8,128)S(1)}, u32[]{:S(2)}, u32[]{:S(2)}) collective-permute-start(s32[224,128]{1,0:T(8,128)S(1)} %get-tuple-element.46), channel_id=1, source_target_pairs={{0,2},{1,3},{2,0},{3,1},{4,6},{5,7},{6,4},{7,5},{8,10},{9,11},{10,... | collective-permute-start | bytes 344072 | tf_op jit(solution)/shard_map/ppermute | solution.py:865
  21.1 5.7 %collective-permute-start.3 = (s32[224,128]{1,0:T(8,128)S(1)}, s32[224,128]{1,0:T(8,128)S(1)}, u32[]{:S(2)}, u32[]{:S(2)}) collective-permute-start(s32[224,128]{1,0:T(8,128)S(1)} %get-tuple-element.47), channel_id=1, source_target_pairs={{0,3},{1,2},{2,1},{3,0},{4,7},{5,6},{6,5},{7,4},{8,11},{9,10},{10,... | collective-permute-start | bytes 344072 | tf_op jit(solution)/shard_map/ppermute | solution.py:865
  22.2 5.2 %collective-permute-start.4 = (s32[224,128]{1,0:T(8,128)S(1)}, s32[224,128]{1,0:T(8,128)S(1)}, u32[]{:S(2)}, u32[]{:S(2)}) collective-permute-start(s32[224,128]{1,0:T(8,128)S(1)} %get-tuple-element.48), channel_id=1, source_target_pairs={{0,1},{1,0},{2,3},{3,2},{4,5},{5,4},{6,7},{7,6},{8,9},{9,8},{10,11... | collective-permute-start | bytes 344072 | tf_op jit(solution)/shard_map/ppermute | solution.py:865
  24.3 9.0 %collective-permute-start.8 = (bf16[48,128]{1,0:T(8,128)(2,1)S(1)}, bf16[48,128]{1,0:T(8,128)(2,1)S(1)}, u32[]{:S(2)}, u32[]{:S(2)}) collective-permute-start(bf16[48,128]{1,0:T(8,128)(2,1)S(1)} %get-tuple-element.65), channel_id=1, source_target_pairs={{0,3},{1,2},{2,1},{3,0},{4,7},{5,6},{6,5},{7,4},{8,11},{9,10},{10,... | collective-permute-start | bytes 36872 | tf_op jit(solution)/shard_map/ppermute | solution.py:865
  26.7 6.6 %collective-permute-start.9 = (bf16[48,128]{1,0:T(8,128)(2,1)S(1)}, bf16[48,128]{1,0:T(8,128)(2,1)S(1)}, u32[]{:S(2)}, u32[]{:S(2)}) collective-permute-start(bf16[48,128]{1,0:T(8,128)(2,1)S(1)} %get-tuple-element.66), channel_id=1, source_target_pairs={{0,2},{1,3},{2,0},{3,1},{4,6},{5,7},{6,4},{7,5},{8,10},{9,11},{10,... | collective-permute-start | bytes 36872 | tf_op jit(solution)/shard_map/ppermute | solution.py:865
  28.5 4.8 %collective-permute-start.10 = (bf16[48,128]{1,0:T(8,128)(2,1)S(1)}, bf16[48,128]{1,0:T(8,128)(2,1)S(1)}, u32[]{:S(2)}, u32[]{:S(2)}) collective-permute-start(bf16[48,128]{1,0:T(8,128)(2,1)S(1)} %get-tuple-element.67), channel_id=1, source_target_pairs={{0,1},{1,0},{2,3},{3,2},{4,5},{5,4},{6,7},{7,6},{8,9},{9,8},{10,11... | collective-permute-start | bytes 36872 | tf_op jit(solution)/shard_map/ppermute | solution.py:865
  29.3 4.8 %collective-permute-start.11 = (bf16[48,128]{1,0:T(8,128)(2,1)S(1)}, bf16[48,128]{1,0:T(8,128)(2,1)S(1)}, u32[]{:S(2)}, u32[]{:S(2)}) collective-permute-start(bf16[48,128]{1,0:T(8,128)(2,1)S(1)} %get-tuple-element.68), channel_id=1, source_target_pairs={{0,4},{1,5},{4,8},{5,9},{6,2},{7,3},{8,12},{9,13},{10,6},{11,7},{1... | collective-permute-start | bytes 36872 | tf_op jit(solution)/shard_map/ppermute | solution.py:975

commit v27 on v26

--- a/solution.py
+++ b/solution.py
@@ -998,7 +998,7 @@
             flops=1 << 33,
             moved=1 << 20,
         )(reach, *own_parts, own_annots, from_far[rows // 2 :], from_close[rows // 2 :])
-        parts = [around(third, groups, 3), around(second, groups, 2)]
+        parts = [around(second, groups, 2), around(third, groups, 3)]
         own_scores, send, there = call(
             functools.partial(near_score_kernel, groups, share),
             [packed_share, sent, sent],

time: 35.1 us -> 35.1 us (level)
  waiting for transfers between devices: 4.6 us -> 4.02 us
  starting transfers between devices: 20.2 us -> 20.6 us
    ppermute x9, starting transfers between devices: 11.7 us -> 12.4 us  [around(): lax.ppermute(value, 'hap', [(source, partner(source, step, groups)) for s...]
    ppermute x9, waiting for transfers between devices: 0.61 us -> 0.02 us  [around(): lax.ppermute(value, 'hap', [(source, partner(source, step, groups)) for s...]
  transfers between devices with their start and end apart: 12 -> 12, of which waited for: 3 -> 2; matrix products, arithmetic and copies ran while one was open for 0% -> 0% of each run, Pallas kernels for 20% -> 20%
where the time goes in v27:
time: 35.1 us; the launch traced here: 34.6 us
  starting transfers between devices  20.6 us (59%)
  Pallas kernels  9.88 us (28%)
  waiting for transfers between devices  4.02 us (11%)
    ppermute x9, starting transfers between devices, around(): lax.ppermute(value, 'hap', [(source, partner(source, step, groups)) for s...  12.4 us
    ppermute x2, starting transfers between devices, swapped(): return lax.ppermute(value, 'snp', pairs)  4.58 us
    ppermute x1, starting transfers between devices, to_neighbour(): return lax.ppermute(value, ('snp', 'hap'), pairs)  3.64 us
    ppermute x2, waiting for transfers between devices, swapped(): return lax.ppermute(value, 'snp', pairs)  3.21 us
    pallas_call x1, Pallas kernels, per_device(): call(prepare_kernel, [shape((rows, snps), bf16), packed, packed], [HBM, H...  2.13 us
    pallas_call x1, Pallas kernels, per_device(): call(functools.partial(own_score_kernel, groups, share), [by_snp, shape((...  1.8 us
    pallas_call x1, Pallas kernels, per_device(): call(functools.partial(close_kernel, groups), [shape(*args) for args in s...  1.79 us
    pallas_call x1, Pallas kernels, per_device(): call(functools.partial(near_score_kernel, groups, share), [packed_share,...  1.16 us
  transfers between devices with their start and end apart: 12, of which 2 were waited for; matrix products, arithmetic and copies ran while one was open for 0% of the time, Pallas kernels for 20%

profile of v27, /device:TPU:1, one launch (start us, length us, event | category | flops | bytes accessed | tf_op | source)
XLA Modules:
  0.0 34.6 jit_solution(14621949616892207095)
XLA Ops:
  0.0 0.0 copy-start.2
  0.0 2.1 %shard_map.46 = (bf16[2048,384]{1,0:T(8,128)(2,1)S(1)}, bf16[1056,384]{1,0:T(8,128)(2,1)S(1)}, bf16[1056,384]{1,0:T(8,128)(2,1)S(1)}) custom-call(s32[2048,384]{1,0:T(8,128)} %hap_ref.1, s32[50,384]{1,0:T(8,128)} %annot_ref.3), custom_call_target="tpu_custom_call" | custom-call | bytes 6291456 | tf_op jit(solution)/shard_map/pallas_call | solution.py:893
  2.1 0.0 copy-start
  2.1 0.0 copy-start.1
  2.2 0.1 collective-permute-start.1
  2.3 4.5 %collective-permute-start = (bf16[1056,384]{1,0:T(8,128)(2,1)S(1)}, bf16[1056,384]{1,0:T(8,128)(2,1)S(1)}, u32[]{:S(2)}, u32[]{:S(2)}) collective-permute-start(bf16[1056,384]{1,0:T(8,128)(2,1)S(1)} %get-tuple-element.39), channel_id=1, source_target_pairs={{4,8},{8,4},{5,9},{9,5},{6,10},{10,6},{7,11},{11,7},{20,24},{24,20... | collective-permute-start | bytes 2433032 | tf_op jit(solution)/shard_map/ppermute | solution.py:874
  6.8 0.0 copy-done.2
  6.8 1.1 %shard_map.47 = (bf16[400,2048]{1,0:T(8,128)(2,1)S(1)}, f32[8,384]{1,0:T(8,128)S(1)}, s32[152,128]{1,0:T(8,128)S(1)}, s32[152,128]{1,0:T(8,128)S(1)}, s32[152,128]{1,0:T(8,128)S(1)}, /*index=5*/s32[152,128]{1,0:T(8,128)S(1)}) custom-call(bf16[2048,384]{1,0:T(8,128)(2,1)S(1)} %get-tuple-element.37.alleles_ref, s32[1,2048]{1,0:T(1,128)S(1)} %bitcast.1), custom_call_target="tpu_custom_call" | custom-call | flops 603979776 | bytes 3145728 | tf_op jit(solution)/shard_map/pallas_call | solution.py:914
  7.9 3.4 %collective-permute-start.5 = (s32[152,128]{1,0:T(8,128)S(1)}, s32[152,128]{1,0:T(8,128)S(1)}, u32[]{:S(2)}, u32[]{:S(2)}) collective-permute-start(s32[152,128]{1,0:T(8,128)S(1)} %get-tuple-element.50), channel_id=1, source_target_pairs={{0,3},{1,2},{2,1},{3,0},{4,7},{5,6},{6,5},{7,4},{8,11},{9,10},{10,... | collective-permute-start | bytes 233480 | tf_op jit(solution)/shard_map/ppermute | solution.py:865
  11.3 0.0 collective-permute-start.6
  11.3 0.4 %collective-permute-start.7 = (s32[152,128]{1,0:T(8,128)S(1)}, s32[152,128]{1,0:T(8,128)S(1)}, u32[]{:S(2)}, u32[]{:S(2)}) collective-permute-start(s32[152,128]{1,0:T(8,128)S(1)} %get-tuple-element.52), channel_id=1, source_target_pairs={{0,1},{1,0},{2,3},{3,2},{4,5},{5,4},{6,7},{7,6},{8,9},{9,8},{10,11... | collective-permute-start | bytes 233480 | tf_op jit(solution)/shard_map/ppermute | solution.py:865
  11.7 0.0 collective-permute-done.1.side_ref
  11.7 0.0 copy-done
  11.7 0.0 copy-done.1
  11.7 1.8 %shard_map.48 = (s32[96,384]{1,0:T(8,128)S(1)}, s32[112,256]{1,0:T(8,128)S(1)}, f32[8,384]{1,0:T(8,128)S(1)}, f32[384,128]{1,0:T(8,128)S(1)}, f32[2,240,128]{2,1...) custom-call(s32[4]{0:T(128)S(1)} %copy-done.1, ...), custom_call_target="tpu_custom_call" | custom-call | flops 402653184 | bytes 3145728 | tf_op jit(solution)/shard_map/pallas_call | solution.py:931
  13.5 3.2 %collective-permute-done.side_ref = bf16[1056,384]{1,0:T(8,128)(2,1)S(1)} collective-permute-done((bf16[1056,384]{1,0:T(8,128)(2,1)S(1)}, bf16[1056,384]{1,0:T(8,128)(2,1)S(1)}, u32[]{:S(2)}, u32[]{:S(2)}) %collective-permute-start) | collective-permute-done | bytes 811040 | tf_op jit(solution)/shard_map/ppermute | solution.py:874
  16.7 1.1 %shard_map.49 = (s32[224,128]{1,0:T(8,128)S(1)}, s32[224,128]{1,0:T(8,128)S(1)}, s32[224,128]{1,0:T(8,128)S(1)}, s32[224,128]{1,0:T(8,128)S(1)}) custom-call(bf16[400,2048]{1,0:T(8,128)(2,1)S(1)} %get-tuple-element.38.weighted_ref, bf16[1056,384]{1,0:T(8,128)(2,1)S(1)} %collective-permute-done.side_ref, s32[96,384]{1,0:T(8,128)S(1)} %get-tuple-element.41.close_ref, ...), custom_call_target="tpu_custom_call" | custom-call | flops 402653184 | bytes 3145728 | tf_op jit(solution)/shard_map/pallas_call | solution.py:944
  17.8 3.3 %collective-permute-start.2 = (s32[224,128]{1,0:T(8,128)S(1)}, s32[224,128]{1,0:T(8,128)S(1)}, u32[]{:S(2)}, u32[]{:S(2)}) collective-permute-start(s32[224,128]{1,0:T(8,128)S(1)} %get-tuple-element.46), channel_id=1, source_target_pairs={{0,2},{1,3},{2,0},{3,1},{4,6},{5,7},{6,4},{7,5},{8,10},{9,11},{10,... | collective-permute-start | bytes 344072 | tf_op jit(solution)/shard_map/ppermute | solution.py:865
  21.1 1.1 %collective-permute-start.3 = (s32[224,128]{1,0:T(8,128)S(1)}, s32[224,128]{1,0:T(8,128)S(1)}, u32[]{:S(2)}, u32[]{:S(2)}) collective-permute-start(s32[224,128]{1,0:T(8,128)S(1)} %get-tuple-element.47), channel_id=1, source_target_pairs={{0,3},{1,2},{2,1},{3,0},{4,7},{5,6},{6,5},{7,4},{8,11},{9,10},{10,... | collective-permute-start | bytes 344072 | tf_op jit(solution)/shard_map/ppermute | solution.py:865
  22.2 0.0 collective-permute-done.5.refs_1_
  22.2 0.3 collective-permute-start.4
  22.4 0.0 collective-permute-done.6.refs_2_
  22.5 0.0 collective-permute-done.7.refs_3_
  22.5 1.8 %shard_map.50 = (f32[384,128]{1,0:T(8,128)S(1)}, f32[96,128]{1,0:T(8,128)S(1)}, f32[6,240,128]{2,1,0:T(8,128)S(1)}, bf16[128,128]{1,0:T(8,128)(2,1)S(1)}, f32[6,...) custom-call(s32[4]{0:T(128)S(1)} %copy-done.1, ...), custom_call_target="tpu_custom_call" | custom-call | flops 8589934592 | bytes 1048576 | tf_op jit(solution)/shard_map/pallas_call | solution.py:983
  24.3 2.3 %collective-permute-start.8 = (bf16[48,128]{1,0:T(8,128)(2,1)S(1)}, bf16[48,128]{1,0:T(8,128)(2,1)S(1)}, u32[]{:S(2)}, u32[]{:S(2)}) collective-permute-start(bf16[48,128]{1,0:T(8,128)(2,1)S(1)} %get-tuple-element.65), channel_id=1, source_target_pairs={{0,2},{1,3},{2,0},{3,1},{4,6},{5,7},{6,4},{7,5},{8,10},{9,11},{10,... | collective-permute-start | bytes 36872 | tf_op jit(solution)/shard_map/ppermute | solution.py:865
  26.6 1.1 %collective-permute-start.9 = (bf16[48,128]{1,0:T(8,128)(2,1)S(1)}, bf16[48,128]{1,0:T(8,128)(2,1)S(1)}, u32[]{:S(2)}, u32[]{:S(2)}) collective-permute-start(bf16[48,128]{1,0:T(8,128)(2,1)S(1)} %get-tuple-element.66), channel_id=1, source_target_pairs={{0,3},{1,2},{2,1},{3,0},{4,7},{5,6},{6,5},{7,4},{8,11},{9,10},{10,... | collective-permute-start | bytes 36872 | tf_op jit(solution)/shard_map/ppermute | solution.py:865
  27.7 0.0 collective-permute-done.2.refs_1_
  27.7 0.0 collective-permute-done.3.refs_2_
  27.7 0.0 collective-permute-done.4.refs_3_
  27.7 1.2 %shard_map.51 = (f32[48,128]{1,0:T(8,128)S(1)}, bf16[48,128]{1,0:T(8,128)(2,1)S(1)}, bf16[48,128]{1,0:T(8,128)(2,1)S(1)}) custom-call(s32[4]{0:T(128)S(1)} %copy-done.1, s32[224,128]{1,0:T(8,128)S(1)} %get-tuple-element.45.refs_0_, s32[224,128]{1,0:T(8,128)S(1)} %collective-permute-done.2.refs_1_, s32[224,128]{1,0:T(8,128)S(1)} %collective-permute-done.3.refs_2_, ...), custom_call_target="tpu_custom_call" | custom-call | flops 67108864 | bytes 2097152 | tf_op jit(solution)/shard_map/pallas_call | solution.py:1002
  28.9 0.6 %collective-permute-start.10 = (bf16[48,128]{1,0:T(8,128)(2,1)S(1)}, bf16[48,128]{1,0:T(8,128)(2,1)S(1)}, u32[]{:S(2)}, u32[]{:S(2)}) collective-permute-start(bf16[48,128]{1,0:T(8,128)(2,1)S(1)} %get-tuple-element.67), channel_id=1, source_target_pairs={{0,1},{1,0},{2,3},{3,2},{4,5},{5,4},{6,7},{7,6},{8,9},{9,8},{10,11... | collective-permute-start | bytes 36872 | tf_op jit(solution)/shard_map/ppermute | solution.py:865
  29.4 3.6 %collective-permute-start.11 = (bf16[48,128]{1,0:T(8,128)(2,1)S(1)}, bf16[48,128]{1,0:T(8,128)(2,1)S(1)}, u32[]{:S(2)}, u32[]{:S(2)}) collective-permute-start(bf16[48,128]{1,0:T(8,128)(2,1)S(1)} %get-tuple-element.68), channel_id=1, source_target_pairs={{0,4},{1,5},{4,8},{5,9},{6,2},{7,3},{8,12},{9,13},{10,6},{11,7},{1... | collective-permute-start | bytes 36872 | tf_op jit(solution)/shard_map/ppermute | solution.py:975
  33.1 0.0 collective-permute-done.8.refs_1_
  33.1 0.0 collective-permute-done.9.refs_2_
  33.1 0.0 collective-permute-done.10.refs_3_
  33.1 0.8 %collective-permute-done.11.refs_4_ = bf16[48,128]{1,0:T(8,128)(2,1)S(1)} collective-permute-done((bf16[48,128]{1,0:T(8,128)(2,1)S(1)}, bf16[48,128]{1,0:T(8,128)(2,1)S(1)}, u32[]{:S(2)}, u32[]{:S(2)}) %collective-permute-start.11) | collective-permute-done | bytes 12320 | tf_op jit(solution)/shard_map/ppermute | solution.py:975
  33.9 0.7 %shard_map.52 = f32[50,96]{1,0:T(8,128)} custom-call(f32[48,128]{1,0:T(8,128)S(1)} %get-tuple-element.64.refs_0_, bf16[48,128]{1,0:T(8,128)(2,1)S(1)} %collective-permute-done.8.refs_1_, bf16[48,128]{1,0:T(8,128)(2,1)S(1)} %collective-permute-done.9.refs_2_, bf16[48,128]{1,0:T(8,128)(2,1)S(1)} %collective-permute-done.10.refs_3_, ...), custom_call_target="tpu_custom_call" | custom-call | tf_op jit(solution)/shard_map/pallas_call | solution.py:1011
  (2 shorter events, 0.0 us)
Async XLA Ops:
  0.0 6.8 %copy-start.2 = (s32[2048]{0:T(1024)S(1)}, s32[2048]{0:T(1024)}, u32[]{:S(2)}) copy-start(s32[2048]{0:T(1024)} %param.5) | copy-start | bytes 24580
  2.1 9.5 %copy-start = (s32[50,384]{1,0:T(8,128)S(1)}, s32[50,384]{1,0:T(8,128)}, u32[]{:S(2)}) copy-start(s32[50,384]{1,0:T(8,128)} %annot_ref.3) | copy-start | bytes 230404
  2.1 9.5 %copy-start.1 = (s32[4]{0:T(128)S(1)}, s32[4]{0:T(128)}, u32[]{:S(2)}) copy-start(s32[4]{0:T(128)} %reach_ref.5) | copy-start | bytes 52
  2.2 9.5 %collective-permute-start.1 = (bf16[1056,384]{1,0:T(8,128)(2,1)S(1)}, bf16[1056,384]{1,0:T(8,128)(2,1)S(1)}, u32[]{:S(2)}, u32[]{:S(2)}) collective-permute-start(bf16[1056,384]{1,0:T(8,128)(2,1)S(1)} %get-tuple-element.40), channel_id=1, source_target_pairs={{0,4},{4,0},{8,12},{12,8},{1,5},{5,1},{9,13},{13,9},{2,6},{6,2},{1... | collective-permute-start | bytes 2433032 | tf_op jit(solution)/shard_map/ppermute | solution.py:874
  2.3 14.4 %collective-permute-start = (bf16[1056,384]{1,0:T(8,128)(2,1)S(1)}, bf16[1056,384]{1,0:T(8,128)(2,1)S(1)}, u32[]{:S(2)}, u32[]{:S(2)}) collective-permute-start(bf16[1056,384]{1,0:T(8,128)(2,1)S(1)} %get-tuple-element.39), channel_id=1, source_target_pairs={{4,8},{8,4},{5,9},{9,5},{6,10},{10,6},{7,11},{11,7},{20,24},{24,20... | collective-permute-start | bytes 2433032 | tf_op jit(solution)/shard_map/ppermute | solution.py:874
  7.9 14.3 %collective-permute-start.5 = (s32[152,128]{1,0:T(8,128)S(1)}, s32[152,128]{1,0:T(8,128)S(1)}, u32[]{:S(2)}, u32[]{:S(2)}) collective-permute-start(s32[152,128]{1,0:T(8,128)S(1)} %get-tuple-element.50), channel_id=1, source_target_pairs={{0,3},{1,2},{2,1},{3,0},{4,7},{5,6},{6,5},{7,4},{8,11},{9,10},{10,... | collective-permute-start | bytes 233480 | tf_op jit(solution)/shard_map/ppermute | solution.py:865
  11.3 11.2 %collective-permute-start.6 = (s32[152,128]{1,0:T(8,128)S(1)}, s32[152,128]{1,0:T(8,128)S(1)}, u32[]{:S(2)}, u32[]{:S(2)}) collective-permute-start(s32[152,128]{1,0:T(8,128)S(1)} %get-tuple-element.51), channel_id=1, source_target_pairs={{0,2},{1,3},{2,0},{3,1},{4,6},{5,7},{6,4},{7,5},{8,10},{9,11},{10,... | collective-permute-start | bytes 233480 | tf_op jit(solution)/shard_map/ppermute | solution.py:865
  11.3 11.2 %collective-permute-start.7 = (s32[152,128]{1,0:T(8,128)S(1)}, s32[152,128]{1,0:T(8,128)S(1)}, u32[]{:S(2)}, u32[]{:S(2)}) collective-permute-start(s32[152,128]{1,0:T(8,128)S(1)} %get-tuple-element.52), channel_id=1, source_target_pairs={{0,1},{1,0},{2,3},{3,2},{4,5},{5,4},{6,7},{7,6},{8,9},{9,8},{10,11... | collective-permute-start | bytes 233480 | tf_op jit(solution)/shard_map/ppermute | solution.py:865
  17.8 9.9 %collective-permute-start.2 = (s32[224,128]{1,0:T(8,128)S(1)}, s32[224,128]{1,0:T(8,128)S(1)}, u32[]{:S(2)}, u32[]{:S(2)}) collective-permute-start(s32[224,128]{1,0:T(8,128)S(1)} %get-tuple-element.46), channel_id=1, source_target_pairs={{0,2},{1,3},{2,0},{3,1},{4,6},{5,7},{6,4},{7,5},{8,10},{9,11},{10,... | collective-permute-start | bytes 344072 | tf_op jit(solution)/shard_map/ppermute | solution.py:865
  21.1 6.6 %collective-permute-start.3 = (s32[224,128]{1,0:T(8,128)S(1)}, s32[224,128]{1,0:T(8,128)S(1)}, u32[]{:S(2)}, u32[]{:S(2)}) collective-permute-start(s32[224,128]{1,0:T(8,128)S(1)} %get-tuple-element.47), channel_id=1, source_target_pairs={{0,3},{1,2},{2,1},{3,0},{4,7},{5,6},{6,5},{7,4},{8,11},{9,10},{10,... | collective-permute-start | bytes 344072 | tf_op jit(solution)/shard_map/ppermute | solution.py:865
  22.2 5.5 %collective-permute-start.4 = (s32[224,128]{1,0:T(8,128)S(1)}, s32[224,128]{1,0:T(8,128)S(1)}, u32[]{:S(2)}, u32[]{:S(2)}) collective-permute-start(s32[224,128]{1,0:T(8,128)S(1)} %get-tuple-element.48), channel_id=1, source_target_pairs={{0,1},{1,0},{2,3},{3,2},{4,5},{5,4},{6,7},{7,6},{8,9},{9,8},{10,11... | collective-permute-start | bytes 344072 | tf_op jit(solution)/shard_map/ppermute | solution.py:865
  24.3 8.8 %collective-permute-start.8 = (bf16[48,128]{1,0:T(8,128)(2,1)S(1)}, bf16[48,128]{1,0:T(8,128)(2,1)S(1)}, u32[]{:S(2)}, u32[]{:S(2)}) collective-permute-start(bf16[48,128]{1,0:T(8,128)(2,1)S(1)} %get-tuple-element.65), channel_id=1, source_target_pairs={{0,2},{1,3},{2,0},{3,1},{4,6},{5,7},{6,4},{7,5},{8,10},{9,11},{10,... | collective-permute-start | bytes 36872 | tf_op jit(solution)/shard_map/ppermute | solution.py:865
  26.6 6.5 %collective-permute-start.9 = (bf16[48,128]{1,0:T(8,128)(2,1)S(1)}, bf16[48,128]{1,0:T(8,128)(2,1)S(1)}, u32[]{:S(2)}, u32[]{:S(2)}) collective-permute-start(bf16[48,128]{1,0:T(8,128)(2,1)S(1)} %get-tuple-element.66), channel_id=1, source_target_pairs={{0,3},{1,2},{2,1},{3,0},{4,7},{5,6},{6,5},{7,4},{8,11},{9,10},{10,... | collective-permute-start | bytes 36872 | tf_op jit(solution)/shard_map/ppermute | solution.py:865
  28.9 4.2 %collective-permute-start.10 = (bf16[48,128]{1,0:T(8,128)(2,1)S(1)}, bf16[48,128]{1,0:T(8,128)(2,1)S(1)}, u32[]{:S(2)}, u32[]{:S(2)}) collective-permute-start(bf16[48,128]{1,0:T(8,128)(2,1)S(1)} %get-tuple-element.67), channel_id=1, source_target_pairs={{0,1},{1,0},{2,3},{3,2},{4,5},{5,4},{6,7},{7,6},{8,9},{9,8},{10,11... | collective-permute-start | bytes 36872 | tf_op jit(solution)/shard_map/ppermute | solution.py:865
  29.4 4.5 %collective-permute-start.11 = (bf16[48,128]{1,0:T(8,128)(2,1)S(1)}, bf16[48,128]{1,0:T(8,128)(2,1)S(1)}, u32[]{:S(2)}, u32[]{:S(2)}) collective-permute-start(bf16[48,128]{1,0:T(8,128)(2,1)S(1)} %get-tuple-element.68), channel_id=1, source_target_pairs={{0,4},{1,5},{4,8},{5,9},{6,2},{7,3},{8,12},{9,13},{10,6},{11,7},{1... | collective-permute-start | bytes 36872 | tf_op jit(solution)/shard_map/ppermute | solution.py:975
